TPU v7x, 32 devices: a whole 2x2x4 slice. The times are simulated.
32 devices in a mesh: ctx: 8 (over z, x), head: 4 (over y, core).
Axes of the slice: x: 2, y: 2, z: 4, core: 2. Of those that a mesh axis runs over, the one named last changes fastest.
Arguments:
- queries: bfloat16 [4096, 2048], P('ctx', 'head'), may hold values from -6 to 6
- keys: bfloat16 [4096, 2048], P('ctx', 'head'), may hold values from -6 to 6
- values: bfloat16 [4096, 2048], P('ctx', 'head'), may hold values from -6 to 6
- out_grad: bfloat16 [4096, 2048], P('ctx', 'head'), may hold values from -6 to 6
- inputs: bfloat16 [4096, 4096], P('ctx', 'head'), may hold values from -6 to 6
- value_weight: bfloat16 [4096, 2048], P('ctx', 'head'), may hold values from -0.125 to 0.125
Outputs:
- query_grad: bfloat16 [4096, 2048], P('ctx', 'head')
- key_grad: bfloat16 [4096, 2048], P('ctx', 'head')
- input_grad: bfloat16 [4096, 4096], P('ctx', 'head')
- weight_grad: float32 [4096, 2048], P('ctx', 'head')
All inputs are finite; a program needn't handle non-finite values.
Results may differ from a plain program's by a relative error of at most 0.0049.
Values may be sent and summed in bfloat16 or wider, within the bound.
No kernel may reach another device: no remote copies, remote signals or barrier semaphores. Data moves between devices by JAX's collectives and lax.ppermute only.
A program may use at most 128 MiB of HBM per device.

v0:
```python
import math

import jax
import jax.numpy as jnp
from jax import lax
from jax.sharding import PartitionSpec as P

DH = 128


def entering(shard, axis, combine, identity, reverse):
    size, here = (lax.axis_size(axis), lax.axis_index(axis))
    everything = lax.all_gather(shard, axis)
    start = jnp.broadcast_to(jnp.asarray(identity, shard.dtype), shard.shape)

    def lap(k, before):
        at = size - 1 - k if reverse else k
        reached = at > here if reverse else at < here
        new = combine(before, everything[at])
        return jnp.where(reached, new, before)

    return lax.fori_loop(0, size, lap, start)


def add_states(earlier, later_part):
    return earlier + later_part


def local(queries, keys, values, out_grad, inputs, value_weight):
    length = queries.shape[0]
    heads = queries.shape[1] // DH
    factor = 1.0 / math.sqrt(DH * length * lax.axis_size("ctx"))
    highest = lax.Precision.HIGHEST
    query_heads = queries.reshape(length, heads, DH)
    key_heads = keys.reshape(length, heads, DH)
    value_heads = values.reshape(length, heads, DH)
    grad_heads = out_grad.reshape(length, heads, DH)
    local_kv = jnp.einsum(
        "thd,the->hde", key_heads, value_heads, preferred_element_type=jnp.float32
    )
    local_qg = jnp.einsum(
        "thd,the->hde", query_heads, grad_heads, preferred_element_type=jnp.float32
    )
    zeros = jnp.zeros((heads, DH, DH), jnp.float32)
    prior = entering(local_kv, "ctx", add_states, zeros, False)
    later = entering(local_qg, "ctx", add_states, zeros, True)
    rows = lax.broadcasted_iota(jnp.int32, (length, length), 0)
    cols = lax.broadcasted_iota(jnp.int32, (length, length), 1)
    causal = (rows >= cols)[None]
    grad_scores = jnp.where(
        causal,
        jnp.einsum("the,she->hts", grad_heads, value_heads, preferred_element_type=jnp.float32),
        0.0,
    ).astype(jnp.bfloat16)
    key_scores = jnp.where(
        causal,
        jnp.einsum("thd,shd->hts", query_heads, key_heads, preferred_element_type=jnp.float32),
        0.0,
    ).astype(jnp.bfloat16)
    query_out = factor * (
        jnp.einsum("the,hde->thd", grad_heads.astype(jnp.float32), prior, precision=highest)
        + jnp.einsum("hts,shd->thd", grad_scores, key_heads, preferred_element_type=jnp.float32)
    )
    key_out = factor * (
        jnp.einsum("hts,thd->shd", grad_scores, query_heads, preferred_element_type=jnp.float32)
        + jnp.einsum("she,hde->shd", value_heads.astype(jnp.float32), later, precision=highest)
    )
    value_out = factor * (
        jnp.einsum("hts,the->she", key_scores, grad_heads, preferred_element_type=jnp.float32)
        + jnp.einsum("shd,hde->she", key_heads.astype(jnp.float32), later, precision=highest)
    )
    query_grad = query_out.astype(jnp.bfloat16).reshape(length, heads * DH)
    key_grad = key_out.astype(jnp.bfloat16).reshape(length, heads * DH)
    value_grad = value_out.astype(jnp.bfloat16).reshape(length, heads * DH)
    features = lax.all_gather(inputs, "head", axis=1, tiled=True)
    summed = lax.psum_scatter(
        lax.dot_general(
            features, value_grad, (((0,), (0,)), ((), ())), preferred_element_type=jnp.float32
        ),
        "ctx",
        scatter_dimension=0,
        tiled=True,
    )
    weight_grad = summed * (1.0 / math.sqrt(length * lax.axis_size("ctx")))
    weight_all = lax.all_gather(value_weight, "ctx", axis=0, tiled=True)
    weight_full = lax.all_to_all(weight_all, "head", split_axis=0, concat_axis=1, tiled=True)
    value_all = lax.all_gather(value_grad, "head", axis=1, tiled=True)
    input_grad = lax.dot_general(
        value_all, weight_full, (((1,), (1,)), ((), ())), preferred_element_type=jnp.float32
    ).astype(jnp.bfloat16)
    return (query_grad, key_grad, input_grad, weight_grad)


def solution(mesh):
    return jax.shard_map(
        local,
        mesh=mesh,
        in_specs=(
            P("ctx", "head"),
            P("ctx", "head"),
            P("ctx", "head"),
            P("ctx", "head"),
            P("ctx", "head"),
            P("ctx", "head"),
        ),
        out_specs=(P("ctx", "head"), P("ctx", "head"), P("ctx", "head"), P("ctx", "head")),
        check_vma=False,
    )
```

profile of v0, /device:TPU:0, one launch (start us, length us, event | category | flops | bytes accessed | tf_op | source)
XLA Modules:
  0.0 408.2 jit_solution(14388880740991191847)
XLA Ops:
  7.2 1.3 copy.81
  8.6 2.3 fusion.11
  12.4 1.1 fusion.18
  14.4 48.7 %all-gather.16.cloned.1.call-done = f32[32,128,128]{2,1,0:T(8,128)} async-done(((f32[4,128,128]{2,1,0:T(8,128)}), f32[32,128,128]{2,1,0:T(8,128)}) %all-gather.16.cloned.1.call-update) | async-done | bytes 2097168 | tf_op jit(solution)/shard_map/all_gather | solution.py:13
  63.0 8.7 %while.31 = (s32[]{:T(128)}, f32[4,128,128]{2,1,0:T(8,128)S(1)}, s32[]{:T(128)}, f32[8,4,128,128]{3,2,1,0:T(8,128)}, s32[]{:T(128)}, /*index=5*/s32[]{:T(128)}, s32[]{:T(128)}, s32[]{:T(128)}) while((s32[]{:T(128)}, f32[4,128,128]{2,1,0:T(8,128)S(1)}, s32[]{:T(128)}, f32[8,4,128,128]{3,2,1,0:T(8,128)}, s32[]{:T(128)}, ...), condition=%wide.region_3.4_spmd.clone, body=%wide.region_2.3_spmd.clone.sunk | while | flops 196616 | bytes 786587 | solution.py:22
  63.0 1.1 add_select_fusion.5
  64.2 1.0 add_select_fusion.5
  66.3 1.0 add_select_fusion.5
  68.4 1.1 add_select_fusion.5
  69.5 1.1 add_select_fusion.5
  70.6 1.1 add_select_fusion.5
  72.3 2.8 fusion.10
  75.3 22.3 %all-gather.12.cloned.1.call-done = bf16[512,4096]{1,0:T(8,128)(2,1)} async-done(((bf16[512,1024]{1,0:T(8,128)(2,1)}), bf16[512,4096]{1,0:T(8,128)(2,1)}) %all-gather.12.cloned.1.call-update) | async-done | bytes 4194320 | tf_op jit(solution)/shard_map/all_gather | solution.py:75
  97.6 8.0 %convolution_bitcast_fusion = f32[4096,512]{0,1:T(8,128)} fusion(bf16[512,512]{0,1:T(8,128)(2,1)} %bitcast.129, bf16[512,4096]{1,0:T(8,128)(2,1)} %all-gather.12.cloned.1.call-done), kind=kOutput, calls=%fused_computation.2 | convolution fusion | flops 2147483648 | bytes 13107200 | tf_op jit(solution)/shard_map/dot_general | solution.py:77
  105.6 67.6 %all-gather.10.cloned.1.call-done = bf16[4096,512]{1,0:T(8,128)(2,1)} async-done(((bf16[512,512]{1,0:T(8,128)(2,1)}), bf16[4096,512]{1,0:T(8,128)(2,1)}) %all-gather.10.cloned.1.call-update) | async-done | bytes 4194320 | tf_op jit(solution)/shard_map/all_gather | solution.py:85
  173.2 5.0 %all-to-all-start = ((bf16[4,1024,512]{2,1,0:T(8,128)(2,1)}), bf16[4,1024,512]{2,1,0:T(8,128)(2,1)}, u32[]{:S(2)}, u32[]{:S(2)}) async-start(bf16[4,1024,512]{2,1,0:T(8,128)(2,1)} %bitcast.126), calls=%async_computation | async-start | bytes 8388608 | tf_op jit(solution)/shard_map/all_to_all | solution.py:86
  178.2 1.9 select_convert_fusion.1
  180.1 1.6 convolution_bitcast_fusion.1
  181.7 1.8 convolution_bitcast_fusion.2
  185.2 37.5 %all-gather.14.cloned.1.call-done = f32[32,128,128]{2,1,0:T(8,128)} async-done(((f32[4,128,128]{2,1,0:T(8,128)}), f32[32,128,128]{2,1,0:T(8,128)}) %all-gather.14.cloned.1.call-update) | async-done | bytes 2097168 | tf_op jit(solution)/shard_map/all_gather | solution.py:13
  222.7 8.5 %while.30 = (s32[]{:T(128)}, f32[4,128,128]{2,1,0:T(8,128)S(1)}, s32[]{:T(128)}, f32[8,4,128,128]{3,2,1,0:T(8,128)}, s32[]{:T(128)}, /*index=5*/s32[]{:T(128)}) while((s32[]{:T(128)}, f32[4,128,128]{2,1,0:T(8,128)S(1)}, s32[]{:T(128)}, f32[8,4,128,128]{3,2,1,0:T(8,128)}, s32[]{:T(128)}, /*index=5*/s32[]{:T(128)}) %tuple.93), condition=%wide.region_1.2_spmd.clone, body=%wide.region_0.1_spmd.clone.sunk | while | flops 196612 | bytes 786525 | solution.py:22
  223.8 1.0 add_select_fusion.4
  225.9 1.0 add_select_fusion.4
  228.0 1.1 add_select_fusion.4
  229.1 1.1 add_select_fusion.4
  230.2 1.0 add_select_fusion.4
  232.9 6.3 %copy.76 = bf16[1024,4,512]{0,2,1:T(8,128)(2,1)} copy(bf16[1024,4,512]{2,0,1:T(8,128)(2,1)} %bitcast.12) | data formatting | bytes 8388608 | tf_op jit(solution)/shard_map/all_to_all | solution.py:86
  239.2 6.6 %all-gather.8.cloned.1.call-done = bf16[512,2048]{0,1:T(8,128)(2,1)} async-done(((bf16[512,512]{0,1:T(8,128)(2,1)}), bf16[512,2048]{0,1:T(8,128)(2,1)}) %all-gather.8.cloned.1.call-update) | async-done | bytes 2097168 | tf_op jit(solution)/shard_map/all_gather | solution.py:87
  245.8 6.1 %convolution_convert_fusion = bf16[512,1024]{1,0:T(8,128)(2,1)} fusion(bf16[512,2048]{0,1:T(8,128)(2,1)} %all-gather.8.cloned.1.call-done, bf16[1024,2048]{0,1:T(8,128)(2,1)} %bitcast.127), kind=kOutput, calls=%fused_computation.6 | convolution fusion | flops 2148007936 | bytes 7340032 | tf_op jit(solution)/shard_map/dot_general | solution.py:88
  252.0 146.8 %reduce-scatter.2.cloned.1.call-done = f32[512,512]{0,1:T(8,128)} async-done(((f32[4096,512]{0,1:T(8,128)}), f32[512,512]{0,1:T(8,128)}) %reduce-scatter.2.cloned.1.call-update) | async-done | bytes 1048592 | tf_op jit(solution)/shard_map/reduce_scatter | solution.py:76
  398.7 1.3 broadcast_multiply_fusion
  400.0 1.3 copy.79
  (42 shorter events, 11.6 us)
Async XLA Ops:
  7.2 5.3 %copy-start = (bf16[512,512]{1,0:T(8,128)(2,1)S(1)}, bf16[512,512]{1,0:T(8,128)(2,1)}, u32[]{:S(2)}) copy-start(bf16[512,512]{1,0:T(8,128)(2,1)} %param.12) | copy-start | bytes 1572868
  7.2 5.3 %copy-start.4 = (bf16[512,512]{1,0:T(8,128)(2,1)S(1)}, bf16[512,512]{1,0:T(8,128)(2,1)}, u32[]{:S(2)}) copy-start(bf16[512,512]{1,0:T(8,128)(2,1)} %param.11) | copy-start | bytes 1572868
  7.2 55.8 %all-gather.16.cloned.1.call-start = ((), (), s32[]{:S(2)}) async-start(), calls=%async_computation.7 | async-start | bytes 2359296 | tf_op jit(solution)/shard_map/all_gather | solution.py:13
  8.6 63.8 %copy-start.1 = (bf16[512,512]{0,1:T(8,128)(2,1)}, bf16[512,512]{0,1:T(8,128)(2,1)S(1)}, u32[]{:S(2)}) copy-start(bf16[512,512]{0,1:T(8,128)(2,1)S(1)} %copy.81) | copy-start | bytes 1572868
  10.9 86.7 %all-gather.12.cloned.1.call-start = ((), (), s32[]{:S(2)}) async-start(), calls=%async_computation.4 | async-start | bytes 5242880 | tf_op jit(solution)/shard_map/all_gather | solution.py:75
  11.6 161.5 %all-gather.10.cloned.1.call-start = ((), (), s32[]{:S(2)}) async-start(), calls=%async_computation.3 | async-start | bytes 4718592 | tf_op jit(solution)/shard_map/all_gather | solution.py:85
  12.4 210.3 %all-gather.14.cloned.1.call-start = ((), (), s32[]{:S(2)}) async-start(), calls=%async_computation.6 | async-start | bytes 2359296 | tf_op jit(solution)/shard_map/all_gather | solution.py:13
  13.5 232.3 %all-gather.8.cloned.1.call-start = ((), (), s32[]{:S(2)}) async-start(), calls=%async_computation.2 | async-start | bytes 2621440 | tf_op jit(solution)/shard_map/all_gather | solution.py:87
  63.0 9.3 %copy-start.6 = (bf16[512,512]{1,0:T(8,128)(2,1)S(1)}, bf16[512,512]{1,0:T(8,128)(2,1)}, u32[]{:S(2)}) copy-start(bf16[512,512]{1,0:T(8,128)(2,1)} %param.10) | copy-start | bytes 1572868
  75.2 323.5 %reduce-scatter.2.cloned.1.call-start = ((), (), s32[]{:S(2)}) async-start(), calls=%async_computation.5 | async-start | bytes 9437184 | tf_op jit(solution)/shard_map/reduce_scatter | solution.py:76
  173.2 5.0 %copy-start.7 = (pred[512,512]{1,0:T(8,128)(4,1)S(1)}, pred[512,512]{1,0:T(8,128)(4,1)}, u32[]{:S(2)}) copy-start(pred[512,512]{1,0:T(8,128)(4,1)} %iota_compare_fusion) | copy-start | bytes 786436
  173.2 59.7 %all-to-all-start = ((bf16[4,1024,512]{2,1,0:T(8,128)(2,1)}), bf16[4,1024,512]{2,1,0:T(8,128)(2,1)}, u32[]{:S(2)}, u32[]{:S(2)}) async-start(bf16[4,1024,512]{2,1,0:T(8,128)(2,1)} %bitcast.126), calls=%async_computation | async-start | bytes 8388608 | tf_op jit(solution)/shard_map/all_to_all | solution.py:86
  180.1 1.6 copy-start.5
  184.2 47.1 %copy-start.3 = (f32[512,4,128]{0,2,1:T(8,128)S(1)}, f32[512,4,128]{0,2,1:T(8,128)}, u32[]{:S(2)}) copy-start(f32[512,4,128]{0,2,1:T(8,128)} %convolution_bitcast_fusion.2) | copy-start | bytes 3145732
  185.2 46.1 %copy-start.2 = (bf16[512,512]{0,1:T(8,128)(2,1)S(1)}, bf16[512,512]{0,1:T(8,128)(2,1)}, u32[]{:S(2)}) copy-start(bf16[512,512]{0,1:T(8,128)(2,1)} %copy-done.1) | copy-start | bytes 1572868
Sparse Core Ops, SparseCore 0:
  11.0 51.9 all-gather.15
  64.6 32.9 all-gather.11
  99.7 73.3 all-gather.9
  175.1 47.5 all-gather.13
  224.7 21.0 all-gather.7
  249.3 149.3 reduce-scatter.1
where the time goes:
time: 409 us; the launch traced here: 408 us
  waiting for transfers between devices  331 us (81%)
  matrix products  27.4 us (7%)
  other arithmetic  18.9 us (5%)
  between operations  14.3 us (3%)
  local copies, waits for them, and re-layouts  11 us (3%)
  starting transfers between devices  5.27 us (1%)
    reduce_scatter x1, waiting for transfers between devices, local(): lax.psum_scatter(lax.dot_general(features, value_grad, (((0,), (0,)), (()...  147 us
    all_gather x2, waiting for transfers between devices, entering(): everything = lax.all_gather(shard, axis)  86.2 us
    all_gather x1, waiting for transfers between devices, local(): weight_all = lax.all_gather(value_weight, 'ctx', axis=0, tiled=True)  67.6 us
    all_gather x1, waiting for transfers between devices, local(): features = lax.all_gather(inputs, 'head', axis=1, tiled=True)  22.3 us
    select_n x16, other arithmetic, lap(): return jnp.where(reached, new, before)  16.8 us
  transfers between devices with their start and end apart: 7, of which 6 were waited for; matrix products, arithmetic and copies ran while one was open for 13% of the time, Pallas kernels for 0%

commit v1 on v0

v1 whole, which is shorter than its diff:
```python
import math

import jax
import jax.numpy as jnp
from jax import lax
from jax.sharding import PartitionSpec as P

DH = 128


def local(queries, keys, values, out_grad, inputs, value_weight):
    f32, bf16 = jnp.float32, jnp.bfloat16
    length, cols = queries.shape
    heads = cols // DH
    n_ctx, n_head = lax.axis_size("ctx"), lax.axis_size("head")
    pairs = n_ctx // 2
    ctx, head = lax.axis_index("ctx"), lax.axis_index("head")
    parity, pair = ctx % 2, ctx // 2
    factor = 1.0 / math.sqrt(DH * length * n_ctx)
    lines = [[2 * i + k for i in range(pairs)] for k in range(2)]

    def partner(x):
        return lax.ppermute(x, "ctx", [(i, i ^ 1) for i in range(n_ctx)])

    def across(x, bit):
        return lax.ppermute(x, "head", [(i, i ^ bit) for i in range(n_head)])

    def over_lines(x):
        return lax.all_gather(x, "ctx", axis_index_groups=lines)

    weight = lax.all_gather(
        value_weight, "ctx", axis=0, tiled=True, axis_index_groups=lines
    )

    query_heads = queries.reshape(length, heads, DH)
    key_heads = keys.reshape(length, heads, DH)
    value_heads = values.reshape(length, heads, DH)
    grad_heads = out_grad.reshape(length, heads, DH)

    def outside(state, reverse):
        mine = state.astype(bf16)
        theirs = partner(mine)
        both = (mine.astype(f32) + theirs.astype(f32)).astype(bf16)
        every = over_lines(both)
        at = lax.broadcasted_iota(jnp.int32, (pairs, 1, 1, 1), 0)
        reached = at > pair if reverse else at < pair
        total = jnp.sum(jnp.where(reached, every.astype(f32), 0.0), axis=0)
        near = parity == (0 if reverse else 1)
        return total + jnp.where(near, theirs.astype(f32), 0.0)

    qg = jnp.einsum("thd,the->hde", query_heads, grad_heads, preferred_element_type=f32)
    later = outside(qg, True)
    kv = jnp.einsum("thd,the->hde", key_heads, value_heads, preferred_element_type=f32)
    prior = outside(kv, False)

    per = n_ctx // n_head // 2
    width = inputs.shape[1] // (2 * per)
    block = per * width
    split = inputs.reshape(length, per, 2, width)
    even, odd = (split[:, :, k].reshape(length, block) for k in range(2))
    own = jnp.where(parity == 0, even, odd)
    theirs = partner(jnp.where(parity == 0, odd, even))
    rows = [jnp.concatenate([own, theirs], axis=0)]
    bit = n_head // 2
    bits = []
    while bit:
        bits.append(bit)
        rows = rows + [across(r, bit) for r in rows]
        bit //= 2
    offsets = [0]
    for b in bits:
        offsets = offsets + [o ^ b for o in offsets]

    idx_r = lax.broadcasted_iota(jnp.int32, (length, length), 0)
    idx_c = lax.broadcasted_iota(jnp.int32, (length, length), 1)
    causal = (idx_r >= idx_c)[None]

    def scores(a, b):
        s = jnp.einsum("the,she->hts", a, b, preferred_element_type=f32)
        return jnp.where(causal, s, 0.0).astype(bf16)

    def inter(x, state, spec):
        hi = state.astype(bf16)
        lo = (state - hi.astype(f32)).astype(bf16)
        return jnp.einsum(spec, x, hi, preferred_element_type=f32) + jnp.einsum(
            spec, x, lo, preferred_element_type=f32
        )

    key_scores = scores(query_heads, key_heads)
    value_out = factor * (
        jnp.einsum("hts,the->she", key_scores, grad_heads, preferred_element_type=f32)
        + inter(key_heads, later, "shd,hde->she")
    )
    value_grad = value_out.astype(bf16).reshape(length, cols)
    value_both = jnp.concatenate([value_grad, partner(value_grad)], axis=0)

    grad_scores = scores(grad_heads, value_heads)
    query_out = factor * (
        inter(grad_heads, prior, "the,hde->thd")
        + jnp.einsum("hts,shd->thd", grad_scores, key_heads, preferred_element_type=f32)
    )
    key_out = factor * (
        jnp.einsum("hts,thd->shd", grad_scores, query_heads, preferred_element_type=f32)
        + inter(value_heads, later, "she,hde->shd")
    )
    query_grad = query_out.astype(bf16).reshape(length, cols)
    key_grad = key_out.astype(bf16).reshape(length, cols)

    partial = jnp.zeros((n_head * block, cols), bf16)
    for off, r in zip(offsets, rows):
        piece = lax.dot_general(
            r, value_both, (((0,), (0,)), ((), ())), preferred_element_type=f32
        )
        partial = lax.dynamic_update_slice(
            partial, piece.astype(bf16), ((head ^ off) * block, 0)
        )
    summed = lax.psum_scatter(
        partial, "ctx", scatter_dimension=0, tiled=True, axis_index_groups=lines
    )
    weight_grad = summed.astype(f32) * (1.0 / math.sqrt(length * n_ctx))

    def part(off):
        w = lax.dynamic_slice_in_dim(weight, (head ^ off) * block, block, 0)
        return lax.dot_general(
            value_both, w, (((1,), (1,)), ((), ())), preferred_element_type=f32
        )

    pieces = {off: part(off) for off in range(n_head)}
    bit = 1
    while bit < n_head:
        for off in sorted(pieces):
            if off & bit:
                got = across(pieces.pop(off).astype(bf16), bit)
                pieces[off ^ bit] = pieces[off ^ bit] + got.astype(f32)
        bit *= 2
    total = pieces[0].astype(bf16)
    mine = total[:length].reshape(length, per, width)
    other = partner(total[length:]).reshape(length, per, width)
    first = jnp.where(parity == 0, mine, other)
    second = jnp.where(parity == 0, other, mine)
    input_grad = jnp.stack([first, second], axis=2).reshape(length, 2 * block)
    return (query_grad, key_grad, input_grad, weight_grad)


def solution(mesh):
    spec = P("ctx", "head")
    return jax.shard_map(
        local, mesh=mesh, in_specs=(spec,) * 6, out_specs=(spec,) * 4, check_vma=False
    )
```

time: 409 us -> 146 us (0.36)
  waiting for transfers between devices: 331 us -> 25 us
  blocking collectives: 0 us -> 44.6 us
  other arithmetic: 18.9 us -> 7.68 us
  matrix products: 27.4 us -> 33.6 us
  starting transfers between devices: 5.27 us -> 10.6 us
    all_gather x5 -> x1, waiting for transfers between devices: 183 us -> 0.02 us  [local(): lax.all_gather(value_weight, 'ctx', axis=0, tiled=True, axis_index_groups...]
    reduce_scatter x1, waiting for transfers between devices: 147 us -> 0.01 us  [local(): lax.psum_scatter(partial, 'ctx', scatter_dimension=0, tiled=True, axis_in...]
    all_gather x0 -> x2, blocking collectives: none -> 44.6 us  [over_lines(): return lax.all_gather(x, 'ctx', axis_index_groups=lines)]
    ppermute x0 -> x11, waiting for transfers between devices: none -> 24.9 us  [the longest x6 14 us: across(): return lax.ppermute(x, 'head', [(i, i ^ bit) for i in range(n_head)])]
    select_n x16 -> x1, other arithmetic: 16.8 us -> 0.07 us  [local(): own = jnp.where(parity == 0, even, odd)]
    ppermute x0 -> x11, starting transfers between devices: none -> 10.5 us  [the longest x5 6.73 us: partner(): return lax.ppermute(x, 'ctx', [(i, i ^ 1) for i in range(n_ctx)])]
    dot_general x6 -> x15, matrix products: 17.8 us -> 25.1 us  [the longest x4 11.4 us: part(): lax.dot_general(value_both, w, (((1,), (1,)), ((), ())), preferred_elemen...]
    all_to_all x1 -> x0, local copies, waits for them, and re-layouts: 6.3 us -> none  [local(): lax.all_to_all(weight_all, 'head', split_axis=0, concat_axis=1, tiled=True)]
  transfers between devices with their start and end apart: 7 -> 13, of which waited for: 6 -> 3; matrix products, arithmetic and copies ran while one was open for 13% -> 29% of each run, Pallas kernels for 0% -> 0%
where the time goes in v1:
time: 146 us; the launch traced here: 145 us
  blocking collectives  44.6 us (31%)
  matrix products  33.6 us (23%)
  waiting for transfers between devices  25 us (17%)
  between operations  14.4 us (10%)
  starting transfers between devices  10.6 us (7%)
  local copies, waits for them, and re-layouts  9.05 us (6%)
  other arithmetic  7.68 us (5%)
    all_gather x2, blocking collectives, over_lines(): return lax.all_gather(x, 'ctx', axis_index_groups=lines)  44.6 us
    ppermute x6, waiting for transfers between devices, across(): return lax.ppermute(x, 'head', [(i, i ^ bit) for i in range(n_head)])  14 us
    dot_general x4, matrix products, part(): lax.dot_general(value_both, w, (((1,), (1,)), ((), ())), preferred_elemen...  11.4 us
    ppermute x5, waiting for transfers between devices, partner(): return lax.ppermute(x, 'ctx', [(i, i ^ 1) for i in range(n_ctx)])  10.9 us
    dot_general x4, matrix products, local(): lax.dot_general(r, value_both, (((0,), (0,)), ((), ())), preferred_elemen...  8.25 us
    unnamed x34, local copies, waits for them, and re-layouts  7.57 us
    ppermute x5, starting transfers between devices, partner(): return lax.ppermute(x, 'ctx', [(i, i ^ 1) for i in range(n_ctx)])  6.73 us
    ppermute x6, starting transfers between devices, across(): return lax.ppermute(x, 'head', [(i, i ^ bit) for i in range(n_head)])  3.78 us
  transfers between devices with their start and end apart: 13, of which 3 were waited for; matrix products, arithmetic and copies ran while one was open for 29% of the time, Pallas kernels for 0%

profile of v1, /device:TPU:0, one launch (start us, length us, event | category | flops | bytes accessed | tf_op | source)
XLA Modules:
  0.0 144.9 jit_solution(7316406777389315604)
XLA Ops:
  7.2 1.3 copy.122
  8.5 1.4 convolution_convert_fusion.6
  9.9 3.0 %collective-permute-start.1 = (bf16[4,128,128]{2,1,0:T(8,128)(2,1)S(1)}, bf16[4,128,128]{2,1,0:T(8,128)(2,1)S(1)}, u32[]{:S(2)}, u32[]{:S(2)}) collective-permute-start(bf16[4,128,128]{2,1,0:T(8,128)(2,1)S(1)} %convolution_convert_fusion.6), channel_id=1, source_target_pairs={{0,4},{4,0},{8,12},{12,8},{16,20},{20,16},{24,28},{28,24},{1,5},{5... | collective-permute-start | bytes 393224 | tf_op jit(solution)/shard_map/ppermute | solution.py:23
  13.0 1.5 %copy.110 = bf16[512,1024]{0,1:T(8,128)(2,1)S(1)} copy(bf16[512,1024]{1,0:T(8,128)(2,1)} %param.10) | data formatting | bytes 2097152 | tf_op args[4]
  15.5 1.3 collective-permute-done.1
  16.8 22.4 %all-gather.1 = bf16[16,128,128]{2,1,0:T(8,128)(2,1)S(1)} all-gather(bf16[4,128,128]{2,1,0:T(8,128)(2,1)S(1)} %fusion.57), channel_id=3, replica_groups={{0,8,16,24},{4,12,20,28},{1,9,17,25},{5,13,21,29},{2,10,18,26},{6,14,22..., dimensions={0}, use_global_device_ids=true | all-gather | bytes 655360 | tf_op jit(solution)/shard_map/all_gather | solution.py:29
  39.4 1.1 pad_maximum_fusion.2
  40.5 1.5 %collective-permute-start.8 = (bf16[1024,512]{0,1:T(8,128)(2,1)}, bf16[1024,512]{0,1:T(8,128)(2,1)}, u32[]{:S(2)}, u32[]{:S(2)}) collective-permute-start(bf16[1024,512]{0,1:T(8,128)(2,1)} %pad_maximum_fusion.2), channel_id=1, source_target_pairs={{0,2},{1,3},{2,0},{3,1},{4,6},{5,7},{6,4},{7,5},{8,10},{9,11},{10,... | collective-permute-start | bytes 3145736 | tf_op jit(solution)/shard_map/ppermute | solution.py:26
  43.2 2.8 %fusion.13 = bf16[512,4,128]{0,2,1:T(8,128)(2,1)} fusion(f32[512,4,128]{0,2,1:T(8,128)S(1)} %fusion.4, bf16[512,4,128]{0,2,1:T(8,128)(2,1)S(1)} %bitcast.131, pred[512,512]{1,0:T(8,128)(4,1)} %iota_compare_fusion, bf16[512,512]{1,0:T(8,128)(2,1)S(1)} %copy-done.6, bf16[512,512]{1,0:T(8,128)(2,1)S(1)} %copy-done.2), kind=kOutput, calls=%fused_computation.24 | convolution fusion | flops 539754496 | bytes 3407872 | tf_op jit(solution)/shard_map/hts,the->she/dot_general | solution.py:91
  46.0 1.9 %collective-permute-start.2 = (bf16[512,512]{0,1:T(8,128)(2,1)}, bf16[512,512]{0,1:T(8,128)(2,1)}, u32[]{:S(2)}, u32[]{:S(2)}) collective-permute-start(bf16[512,512]{0,1:T(8,128)(2,1)} %bitcast.141), channel_id=1, source_target_pairs={{0,4},{4,0},{8,12},{12,8},{16,20},{20,16},{24,28},{28,24},{1,5},{5... | collective-permute-start | bytes 1572872 | tf_op jit(solution)/shard_map/ppermute | solution.py:23
  47.9 14.0 %collective-permute-done.8 = bf16[1024,512]{0,1:T(8,128)(2,1)} collective-permute-done((bf16[1024,512]{0,1:T(8,128)(2,1)}, bf16[1024,512]{0,1:T(8,128)(2,1)}, u32[]{:S(2)}, u32[]{:S(2)}) %collective-permute-start.8) | collective-permute-done | bytes 1048608 | tf_op jit(solution)/shard_map/ppermute | solution.py:26
  64.4 1.9 %fusion.17 = bf16[2048,512]{1,0:T(8,128)(2,1)S(1)} fusion(bf16[2048,512]{1,0:T(8,128)(2,1)S(1)} %broadcast_in_dim.51, s32[]{:T(128)S(6)} %select_n.98, bf16[512,512]{0,1:T(8,128)(2,1)S(1)} %copy-done.14, bf16[512,512]{0,1:T(8,128)(2,1)} %copy-done.8, bf16[512,512]{0,1:T(8,128)(2,1)} %collective-permute-done.2, bf16[512,512]{0,1:T(8,128)(2,1)S(1)} %bitcast.144), kind=kOutput, calls=%fused_computation.32 | convolution fusion | flops 541327360 | bytes 2621444 | tf_op jit(solution)/shard_map/dot_general | solution.py:111
  66.4 2.1 %fusion.16 = bf16[2048,512]{1,0:T(8,128)(2,1)S(1)} fusion(bf16[2048,512]{1,0:T(8,128)(2,1)S(1)} %fusion.17, s32[]{:T(128)S(6)} %select_n.100, bf16[1024,512]{0,1:T(8,128)(2,1)} %collective-permute-done.8, bf16[512,512]{0,1:T(8,128)(2,1)} %collective-permute-done.2, bf16[512,512]{0,1:T(8,128)(2,1)S(1)} %bitcast.145), kind=kOutput, calls=%fused_computation.30 | convolution fusion | flops 539230208 | bytes 2621444 | tf_op jit(solution)/shard_map/dot_general | solution.py:111
  68.5 2.1 %fusion.15 = bf16[2048,512]{1,0:T(8,128)(2,1)S(1)} fusion(bf16[2048,512]{1,0:T(8,128)(2,1)S(1)} %fusion.16, s32[]{:T(128)S(6)} %select_n.99, bf16[1024,512]{0,1:T(8,128)(2,1)} %collective-permute-done.9, bf16[512,512]{0,1:T(8,128)(2,1)} %collective-permute-done.2, bf16[512,512]{0,1:T(8,128)(2,1)S(1)} %bitcast.146), kind=kOutput, calls=%fused_computation.28 | convolution fusion | flops 539230208 | bytes 2621444 | tf_op jit(solution)/shard_map/dot_general | solution.py:111
  70.6 2.1 %fusion.14 = bf16[2048,512]{1,0:T(8,128)(2,1)S(1)} fusion(bf16[2048,512]{1,0:T(8,128)(2,1)S(1)} %fusion.15, s32[]{:T(128)S(6)} %select_n.101, bf16[1024,512]{0,1:T(8,128)(2,1)} %collective-permute-done.10, bf16[512,512]{0,1:T(8,128)(2,1)} %collective-permute-done.2, bf16[512,512]{0,1:T(8,128)(2,1)S(1)} %bitcast.147), kind=kOutput, calls=%fused_computation.26 | convolution fusion | flops 539230208 | bytes 2621444 | tf_op jit(solution)/shard_map/dot_general | solution.py:111
  72.7 1.4 copy-done.1
  74.1 1.8 %select_convert_fusion.1 = bf16[4,512,512]{2,1,0:T(8,128)(2,1)S(1)} fusion(bf16[512,4,128]{0,2,1:T(8,128)(2,1)S(1)} %bitcast.132, pred[512,512]{1,0:T(8,128)(4,1)} %iota_compare_fusion, bf16[512,512]{1,0:T(8,128)(2,1)S(1)} %copy-done), kind=kOutput, calls=%fused_computation.1 | convolution fusion | flops 270532608 | bytes 3407872 | tf_op jit(solution)/shard_map/the,she->hts/dot_general | solution.py:79
  75.9 3.1 %convolution_convert_fusion = bf16[1024,512]{0,1:T(8,128)(2,1)} fusion(bf16[2048,512]{1,0:T(8,128)(2,1)} %all-gather.4.cloned.1.call-done, s32[]{:T(128)S(6)} %select_n.101, bf16[512,512]{0,1:T(8,128)(2,1)} %collective-permute-done.2, bf16[512,512]{0,1:T(8,128)(2,1)} %bitcast.142), kind=kOutput, calls=%fused_computation.5 | convolution fusion | flops 539492352 | bytes 2621444 | tf_op jit(solution)/shard_map/dot_general | solution.py:124
  79.3 1.8 %convolution_bitcast_fusion.1 = f32[512,4,128]{0,2,1:T(8,128)} fusion(bf16[4,512,512]{2,1,0:T(8,128)(2,1)S(1)} %select_convert_fusion.1, bf16[512,512]{1,0:T(8,128)(2,1)S(1)} %copy-done.3), kind=kOutput, calls=%fused_computation.8 | convolution fusion | flops 268435456 | bytes 3670016 | tf_op jit(solution)/shard_map/hts,shd->thd/dot_general | solution.py:100
  81.1 1.5 %convolution_bitcast_fusion = f32[512,4,128]{0,2,1:T(8,128)} fusion(bf16[4,512,512]{2,1,0:T(8,128)(2,1)S(1)} %select_convert_fusion.1, bf16[512,512]{1,0:T(8,128)(2,1)S(1)} %copy-done.7), kind=kOutput, calls=%fused_computation.7 | convolution fusion | flops 268435456 | bytes 3670016 | tf_op jit(solution)/shard_map/hts,thd->shd/dot_general | solution.py:103
  83.6 3.1 %convolution_convert_fusion.1 = bf16[1024,512]{0,1:T(8,128)(2,1)} fusion(bf16[2048,512]{1,0:T(8,128)(2,1)} %all-gather.4.cloned.1.call-done, s32[]{:T(128)S(6)} %select_n.99, bf16[512,512]{0,1:T(8,128)(2,1)} %collective-permute-done.2, bf16[512,512]{0,1:T(8,128)(2,1)} %bitcast.143), kind=kOutput, calls=%fused_computation.6 | convolution fusion | flops 539492352 | bytes 2621444 | tf_op jit(solution)/shard_map/dot_general | solution.py:124
  87.0 3.3 %add_convert_fusion.1 = bf16[1024,512]{0,1:T(8,128)(2,1)} fusion(bf16[1024,512]{0,1:T(8,128)(2,1)} %collective-permute-done.4, bf16[2048,512]{1,0:T(8,128)(2,1)} %all-gather.4.cloned.1.call-done, s32[]{:T(128)S(6)} %select_n.100, bf16[512,512]{0,1:T(8,128)(2,1)} %collective-permute-done.2, bf16[512,512]{0,1:T(8,128)(2,1)S(1)} %bitcast.148), kind=kOutput, calls=%fused_computation.3 | convolution fusion | flops 540540928 | bytes 3670020 | tf_op jit(solution)/shard_map/dot_general | solution.py:124
  90.3 1.7 %collective-permute-start.5 = (bf16[1024,512]{0,1:T(8,128)(2,1)}, bf16[1024,512]{0,1:T(8,128)(2,1)}, u32[]{:S(2)}, u32[]{:S(2)}) collective-permute-start(bf16[1024,512]{0,1:T(8,128)(2,1)} %add_convert_fusion.1), channel_id=1, source_target_pairs={{0,2},{1,3},{2,0},{3,1},{4,6},{5,7},{6,4},{7,5},{8,10},{9,11},{10,... | collective-permute-start | bytes 3145736 | tf_op jit(solution)/shard_map/ppermute | solution.py:26
  92.0 22.2 %all-gather = bf16[16,128,128]{2,1,0:T(8,128)(2,1)S(1)} all-gather(bf16[4,128,128]{2,1,0:T(8,128)(2,1)S(1)} %fusion.55), channel_id=2, replica_groups={{0,8,16,24},{4,12,20,28},{1,9,17,25},{5,13,21,29},{2,10,18,26},{6,14,22..., dimensions={0}, use_global_device_ids=true | all-gather | bytes 655360 | tf_op jit(solution)/shard_map/all_gather | solution.py:29
  114.4 1.2 fusion.62
  115.6 1.2 fusion.11
  117.8 1.9 %fusion.39 = f32[1024,512]{0,1:T(8,128)S(1)} fusion(bf16[2048,512]{1,0:T(8,128)(2,1)} %all-gather.4.cloned.1.call-done, s32[]{:T(128)S(6)} %select_n.98, bf16[512,512]{0,1:T(8,128)(2,1)} %collective-permute-done.2, bf16[512,512]{0,1:T(8,128)(2,1)S(1)} %bitcast.149), kind=kOutput, calls=%fused_computation.65 | convolution fusion | flops 538968064 | bytes 3670020 | tf_op jit(solution)/shard_map/dot_general | solution.py:124
  119.7 1.9 %add_convert_fusion = bf16[1024,512]{0,1:T(8,128)(2,1)S(1)} fusion(bf16[1024,512]{0,1:T(8,128)(2,1)} %collective-permute-done.5, f32[1024,512]{0,1:T(8,128)S(1)} %fusion.39, bf16[1024,512]{0,1:T(8,128)(2,1)S(1)} %collective-permute-done.3), kind=kLoop, calls=%fused_computation.2 | loop fusion | flops 2621440 | bytes 5242880 | tf_op jit(solution)/shard_map/convert_element_type | solution.py:136
  121.6 1.5 %collective-permute-start.6 = (bf16[512,512]{0,1:T(8,128)(2,1)S(1)}, bf16[512,512]{0,1:T(8,128)(2,1)S(1)}, u32[]{:S(2)}, u32[]{:S(2)}) collective-permute-start(bf16[512,512]{0,1:T(8,128)(2,1)S(1)} %slice.17), channel_id=1, source_target_pairs={{0,4},{4,0},{8,12},{12,8},{16,20},{20,16},{24,28},{28,24},{1,5},{5... | collective-permute-start | bytes 1572872 | tf_op jit(solution)/shard_map/ppermute | solution.py:23
  124.8 9.6 %collective-permute-done.6 = bf16[512,512]{0,1:T(8,128)(2,1)S(1)} collective-permute-done((bf16[512,512]{0,1:T(8,128)(2,1)S(1)}, bf16[512,512]{0,1:T(8,128)(2,1)S(1)}, u32[]{:S(2)}, u32[]{:S(2)}) %collective-permute-start.6) | collective-permute-done | bytes 524320 | tf_op jit(solution)/shard_map/ppermute | solution.py:23
  134.5 1.3 copy.115
  135.9 2.2 %convert_multiply_fusion = f32[512,512]{1,0:T(8,128)} fusion(bf16[512,512]{1,0:T(8,128)(2,1)} %reduce-scatter.2.cloned.1.call-done), kind=kLoop, calls=%fused_computation.42 | loop fusion | flops 524288 | bytes 1572864 | tf_op jit(solution)/shard_map/mul | solution.py:120
  (69 shorter events, 9.5 us)
Async XLA Ops:
  7.2 54.8 %copy-start = (bf16[512,512]{1,0:T(8,128)(2,1)S(1)}, bf16[512,512]{1,0:T(8,128)(2,1)}, u32[]{:S(2)}) copy-start(bf16[512,512]{1,0:T(8,128)(2,1)} %param.8) | copy-start | bytes 1572868
  7.2 68.7 %all-gather.4.cloned.1.call-start = ((), (), s32[]{:S(2)}) async-start(), calls=%async_computation.1 | async-start | bytes 2621440 | tf_op jit(solution)/shard_map/all_gather | solution.py:31
  9.9 6.9 %collective-permute-start.1 = (bf16[4,128,128]{2,1,0:T(8,128)(2,1)S(1)}, bf16[4,128,128]{2,1,0:T(8,128)(2,1)S(1)}, u32[]{:S(2)}, u32[]{:S(2)}) collective-permute-start(bf16[4,128,128]{2,1,0:T(8,128)(2,1)S(1)} %convolution_convert_fusion.6), channel_id=1, source_target_pairs={{0,4},{4,0},{8,12},{12,8},{16,20},{20,16},{24,28},{28,24},{1,5},{5... | collective-permute-start | bytes 393224 | tf_op jit(solution)/shard_map/ppermute | solution.py:23
  13.0 122.9 %reduce-scatter.2.cloned.1.call-start = ((), (), s32[]{:S(2)}) async-start(), calls=%async_computation.2 | async-start | bytes 2621440 | tf_op jit(solution)/shard_map/reduce_scatter | solution.py:117
  14.6 25.9 %copy-start.8 = (bf16[512,512]{0,1:T(8,128)(2,1)}, bf16[512,512]{0,1:T(8,128)(2,1)S(1)}, u32[]{:S(2)}) copy-start(bf16[512,512]{0,1:T(8,128)(2,1)S(1)} %get-tuple-element.22) | copy-start | bytes 1572868
  14.6 24.8 %collective-permute-start.7 = (bf16[512,512]{0,1:T(8,128)(2,1)S(1)}, bf16[512,512]{0,1:T(8,128)(2,1)S(1)}, u32[]{:S(2)}, u32[]{:S(2)}) collective-permute-start(bf16[512,512]{0,1:T(8,128)(2,1)S(1)} %get-tuple-element.23), channel_id=1, source_target_pairs={{0,4},{4,0},{8,12},{12,8},{16,20},{20,16},{24,28},{28,24},{1,5},{5... | collective-permute-start | bytes 1572872 | tf_op jit(solution)/shard_map/ppermute | solution.py:23
  16.8 25.3 %copy-start.2 = (bf16[512,512]{1,0:T(8,128)(2,1)S(1)}, bf16[512,512]{1,0:T(8,128)(2,1)}, u32[]{:S(2)}) copy-start(bf16[512,512]{1,0:T(8,128)(2,1)} %param.7) | copy-start | bytes 1572868
  39.4 2.7 %copy-start.13 = (bf16[512,512]{0,1:T(8,128)(2,1)}, bf16[512,512]{0,1:T(8,128)(2,1)S(1)}, u32[]{:S(2)}) copy-start(bf16[512,512]{0,1:T(8,128)(2,1)S(1)} %collective-permute-done.7) | copy-start | bytes 1572868
  40.5 21.4 %collective-permute-start.8 = (bf16[1024,512]{0,1:T(8,128)(2,1)}, bf16[1024,512]{0,1:T(8,128)(2,1)}, u32[]{:S(2)}, u32[]{:S(2)}) collective-permute-start(bf16[1024,512]{0,1:T(8,128)(2,1)} %pad_maximum_fusion.2), channel_id=1, source_target_pairs={{0,2},{1,3},{2,0},{3,1},{4,6},{5,7},{6,4},{7,5},{8,10},{9,11},{10,... | collective-permute-start | bytes 3145736 | tf_op jit(solution)/shard_map/ppermute | solution.py:26
  42.1 0.7 copy-start.9
  42.1 1.1 copy-start.6
  42.9 25.6 %collective-permute-start.9 = (bf16[1024,512]{0,1:T(8,128)(2,1)}, bf16[1024,512]{0,1:T(8,128)(2,1)}, u32[]{:S(2)}, u32[]{:S(2)}) collective-permute-start(bf16[1024,512]{0,1:T(8,128)(2,1)} %pad_maximum_fusion.2), channel_id=1, source_target_pairs={{0,1},{1,0},{2,3},{3,2},{4,5},{5,4},{6,7},{7,6},{8,9},{9,8},{10,11... | collective-permute-start | bytes 3145736 | tf_op jit(solution)/shard_map/ppermute | solution.py:26
  46.0 17.2 %collective-permute-start.2 = (bf16[512,512]{0,1:T(8,128)(2,1)}, bf16[512,512]{0,1:T(8,128)(2,1)}, u32[]{:S(2)}, u32[]{:S(2)}) collective-permute-start(bf16[512,512]{0,1:T(8,128)(2,1)} %bitcast.141), channel_id=1, source_target_pairs={{0,4},{4,0},{8,12},{12,8},{16,20},{20,16},{24,28},{28,24},{1,5},{5... | collective-permute-start | bytes 1572872 | tf_op jit(solution)/shard_map/ppermute | solution.py:23
  62.0 8.6 %collective-permute-start.10 = (bf16[1024,512]{0,1:T(8,128)(2,1)}, bf16[1024,512]{0,1:T(8,128)(2,1)}, u32[]{:S(2)}, u32[]{:S(2)}) collective-permute-start(bf16[1024,512]{0,1:T(8,128)(2,1)} %collective-permute-done.8), channel_id=1, source_target_pairs={{0,1},{1,0},{2,3},{3,2},{4,5},{5,4},{6,7},{7,6},{8,9},{9,8},{10,11... | collective-permute-start | bytes 3145736 | tf_op jit(solution)/shard_map/ppermute | solution.py:26
  63.0 19.6 %collective-permute-start = (bf16[4,128,128]{2,1,0:T(8,128)(2,1)}, bf16[4,128,128]{2,1,0:T(8,128)(2,1)}, u32[]{:S(2)}, u32[]{:S(2)}) collective-permute-start(bf16[4,128,128]{2,1,0:T(8,128)(2,1)} %convolution_convert_fusion.7), channel_id=1, source_target_pairs={{0,4},{4,0},{8,12},{12,8},{16,20},{20,16},{24,28},{28,24},{1,5},{5... | collective-permute-start | bytes 393224 | tf_op jit(solution)/shard_map/ppermute | solution.py:23
  63.2 1.0 copy-start.11
  63.2 1.2 copy-start.14
  72.7 1.4 copy-start.1
  75.9 3.4 %copy-start.3 = (bf16[512,512]{1,0:T(8,128)(2,1)S(1)}, bf16[512,512]{1,0:T(8,128)(2,1)}, u32[]{:S(2)}) copy-start(bf16[512,512]{1,0:T(8,128)(2,1)} %param.7) | copy-start | bytes 1572868
  79.0 2.0 %copy-start.7 = (bf16[512,512]{1,0:T(8,128)(2,1)S(1)}, bf16[512,512]{1,0:T(8,128)(2,1)}, u32[]{:S(2)}) copy-start(bf16[512,512]{1,0:T(8,128)(2,1)} %param.6) | copy-start | bytes 1572868
  79.0 7.9 %collective-permute-start.4 = (bf16[1024,512]{0,1:T(8,128)(2,1)}, bf16[1024,512]{0,1:T(8,128)(2,1)}, u32[]{:S(2)}, u32[]{:S(2)}) collective-permute-start(bf16[1024,512]{0,1:T(8,128)(2,1)} %convolution_convert_fusion), channel_id=1, source_target_pairs={{0,1},{1,0},{2,3},{3,2},{4,5},{5,4},{6,7},{7,6},{8,9},{9,8},{10,11... | collective-permute-start | bytes 3145736 | tf_op jit(solution)/shard_map/ppermute | solution.py:26
  82.6 4.4 %copy-start.12 = (bf16[512,4,128]{0,2,1:T(8,128)(2,1)S(1)}, bf16[512,4,128]{0,2,1:T(8,128)(2,1)}, u32[]{:S(2)}) copy-start(bf16[512,4,128]{0,2,1:T(8,128)(2,1)} %fusion.13) | copy-start | bytes 1572868
  86.7 33.0 %collective-permute-start.3 = (bf16[1024,512]{0,1:T(8,128)(2,1)}, bf16[1024,512]{0,1:T(8,128)(2,1)S(1)}, u32[]{:S(2)}, u32[]{:S(2)}) collective-permute-start(bf16[1024,512]{0,1:T(8,128)(2,1)} %convolution_convert_fusion.1), channel_id=1, source_target_pairs={{0,1},{1,0},{2,3},{3,2},{4,5},{5,4},{6,7},{7,6},{8,9},{9,8},{10,11... | collective-permute-start | bytes 3145736 | tf_op jit(solution)/shard_map/ppermute | solution.py:26
  90.3 25.3 %copy-start.5 = (f32[512,4,128]{0,2,1:T(8,128)S(1)}, f32[512,4,128]{0,2,1:T(8,128)}, u32[]{:S(2)}) copy-start(f32[512,4,128]{0,2,1:T(8,128)} %convolution_bitcast_fusion.1) | copy-start | bytes 3145732
  90.3 29.4 %collective-permute-start.5 = (bf16[1024,512]{0,1:T(8,128)(2,1)}, bf16[1024,512]{0,1:T(8,128)(2,1)}, u32[]{:S(2)}, u32[]{:S(2)}) collective-permute-start(bf16[1024,512]{0,1:T(8,128)(2,1)} %add_convert_fusion.1), channel_id=1, source_target_pairs={{0,2},{1,3},{2,0},{3,1},{4,6},{5,7},{6,4},{7,5},{8,10},{9,11},{10,... | collective-permute-start | bytes 3145736 | tf_op jit(solution)/shard_map/ppermute | solution.py:26
  119.7 3.4 %copy-start.10 = (bf16[4,128,128]{2,1,0:T(8,128)(2,1)S(1)}, bf16[4,128,128]{2,1,0:T(8,128)(2,1)}, u32[]{:S(2)}) copy-start(bf16[4,128,128]{2,1,0:T(8,128)(2,1)} %copy-done.9) | copy-start | bytes 393220
  121.6 1.9 %copy-start.4 = (f32[512,4,128]{0,2,1:T(8,128)S(1)}, f32[512,4,128]{0,2,1:T(8,128)}, u32[]{:S(2)}) copy-start(f32[512,4,128]{0,2,1:T(8,128)} %convolution_bitcast_fusion) | copy-start | bytes 3145732
  121.6 12.7 %collective-permute-start.6 = (bf16[512,512]{0,1:T(8,128)(2,1)S(1)}, bf16[512,512]{0,1:T(8,128)(2,1)S(1)}, u32[]{:S(2)}, u32[]{:S(2)}) collective-permute-start(bf16[512,512]{0,1:T(8,128)(2,1)S(1)} %slice.17), channel_id=1, source_target_pairs={{0,4},{4,0},{8,12},{12,8},{16,20},{20,16},{24,28},{28,24},{1,5},{5... | collective-permute-start | bytes 1572872 | tf_op jit(solution)/shard_map/ppermute | solution.py:23
Sparse Core Ops, SparseCore 0:
  13.1 50.7 all-gather.3
  74.2 51.3 reduce-scatter.1

commit v2 on v1

v2 whole, which is shorter than its diff:
```python
import math

import jax
import jax.numpy as jnp
from jax import lax
from jax.sharding import PartitionSpec as P

DH = 128


def local(queries, keys, values, out_grad, inputs, value_weight):
    f32, bf16 = jnp.float32, jnp.bfloat16
    length, cols = queries.shape
    heads = cols // DH
    n_ctx, n_head = lax.axis_size("ctx"), lax.axis_size("head")
    pairs = n_ctx // 2
    ctx, head = lax.axis_index("ctx"), lax.axis_index("head")
    parity, pair = ctx % 2, ctx // 2
    factor = 1.0 / math.sqrt(DH * length * n_ctx)
    lines = [[2 * i + k for i in range(pairs)] for k in range(2)]

    def partner(x):
        return lax.ppermute(x, "ctx", [(i, i ^ 1) for i in range(n_ctx)])

    def across(x, bit):
        return lax.ppermute(x, "head", [(i, i ^ bit) for i in range(n_head)])

    weight = lax.all_gather(value_weight, "ctx", axis_index_groups=lines)

    query_heads = queries.reshape(length, heads, DH)
    key_heads = keys.reshape(length, heads, DH)
    value_heads = values.reshape(length, heads, DH)
    grad_heads = out_grad.reshape(length, heads, DH)

    def state(a, b):
        s = jnp.einsum("thd,the->hde", a, b, preferred_element_type=f32).astype(bf16)
        return s.reshape(2, heads // 2, DH, DH)

    def pick(x, k):
        return jnp.where(k == 0, x[:, 0], x[:, 1])

    states = jnp.stack([state(query_heads, grad_heads), state(key_heads, value_heads)])
    their_half = partner(pick(states, 1 - parity))
    both = (pick(states, parity).astype(f32) + their_half.astype(f32)).astype(bf16)
    every = lax.all_gather(both, "ctx", axis_index_groups=lines)
    at = lax.broadcasted_iota(jnp.int32, (pairs, 1, 1, 1), 0)
    zero = jnp.zeros((), f32)
    after = jnp.sum(jnp.where(at > pair, every[:, 0].astype(f32), zero), axis=0)
    before = jnp.sum(jnp.where(at < pair, every[:, 1].astype(f32), zero), axis=0)
    far = jnp.stack([after, before]).astype(bf16)
    got = partner(jnp.stack([far, pick(states, parity)]))

    def whole(mine, theirs):
        a, b = mine.astype(f32), theirs.astype(f32)
        first = jnp.where(parity == 0, a, b)
        second = jnp.where(parity == 0, b, a)
        return jnp.concatenate([first, second], axis=0)

    near_later = jnp.where(parity == 0, whole(their_half[0], got[1, 0]), zero)
    near_prior = jnp.where(parity == 1, whole(their_half[1], got[1, 1]), zero)
    later = whole(far[0], got[0, 0]) + near_later
    prior = whole(far[1], got[0, 1]) + near_prior

    per = n_ctx // n_head // 2
    width = inputs.shape[1] // (2 * per)
    split = inputs.reshape(length, per, 2, width).transpose(1, 2, 0, 3)
    own = jnp.where(parity == 0, split[:, 0], split[:, 1])
    theirs = partner(jnp.where(parity == 0, split[:, 1], split[:, 0]))
    rows = [jnp.concatenate([own, theirs], axis=1)]
    offsets = [0]
    bit = n_head // 2
    while bit:
        rows = rows + [across(r, bit) for r in rows]
        offsets = offsets + [o ^ bit for o in offsets]
        bit //= 2
    features = jnp.zeros((pairs, 2 * length, width), bf16)
    for off, r in zip(offsets, rows):
        features = lax.dynamic_update_slice(features, r, ((head ^ off) * per, 0, 0))

    idx_r = lax.broadcasted_iota(jnp.int32, (length, length), 0)
    idx_c = lax.broadcasted_iota(jnp.int32, (length, length), 1)
    causal = (idx_r >= idx_c)[None]

    def scores(a, b):
        s = jnp.einsum("the,she->hts", a, b, preferred_element_type=f32)
        return jnp.where(causal, s, 0.0).astype(bf16)

    def inter(x, state, spec):
        hi = state.astype(bf16)
        lo = (state - hi.astype(f32)).astype(bf16)
        return jnp.einsum(spec, x, hi, preferred_element_type=f32) + jnp.einsum(
            spec, x, lo, preferred_element_type=f32
        )

    key_scores = scores(query_heads, key_heads)
    value_out = factor * (
        jnp.einsum("hts,the->she", key_scores, grad_heads, preferred_element_type=f32)
        + inter(key_heads, later, "shd,hde->she")
    )
    value_grad = value_out.astype(bf16).reshape(length, cols)
    value_both = jnp.concatenate([value_grad, partner(value_grad)], axis=0)

    grad_scores = scores(grad_heads, value_heads)
    query_out = factor * (
        inter(grad_heads, prior, "the,hde->thd")
        + jnp.einsum("hts,shd->thd", grad_scores, key_heads, preferred_element_type=f32)
    )
    key_out = factor * (
        jnp.einsum("hts,thd->shd", grad_scores, query_heads, preferred_element_type=f32)
        + inter(value_heads, later, "she,hde->shd")
    )
    query_grad = query_out.astype(bf16).reshape(length, cols)
    key_grad = key_out.astype(bf16).reshape(length, cols)

    order = list(range(0, pairs, 2)) + list(range(1, pairs, 2))[::-1]
    place = [order.index(i) for i in range(pairs)]
    ring = [
        (2 * order[i] + k, 2 * order[(i + 1) % pairs] + k)
        for i in range(pairs)
        for k in range(2)
    ]
    spot = jnp.asarray(place, jnp.int32)[pair]
    chains = 2
    span = cols // chains

    def piece(step, chain):
        which = jnp.asarray(order, jnp.int32)[(spot - 1 - step) % pairs]
        block = lax.dynamic_index_in_dim(features, which, 0, keepdims=False)
        return lax.dot_general(
            block,
            value_both[:, chain * span : (chain + 1) * span],
            (((0,), (0,)), ((), ())),
            preferred_element_type=f32,
        )

    sums = [piece(0, chain) for chain in range(chains)]
    for step in range(1, pairs):
        for chain in range(chains):
            moved = lax.ppermute(sums[chain].astype(bf16), "ctx", ring)
            sums[chain] = moved.astype(f32) + piece(step, chain)
    weight_grad = jnp.concatenate(sums, axis=1) * (1.0 / math.sqrt(length * n_ctx))

    def part(off, positions):
        w = lax.dynamic_slice_in_dim(weight, (head ^ off) * per, per, 0)
        return lax.dot_general(
            positions,
            w.reshape(per * width, cols),
            (((1,), (1,)), ((), ())),
            preferred_element_type=f32,
        )

    def over_heads(positions):
        pieces = {off: part(off, positions) for off in range(n_head)}
        bit = 1
        while bit < n_head:
            out = [off for off in sorted(pieces) if off & bit]
            got = across(jnp.stack([pieces.pop(o).astype(bf16) for o in out]), bit)
            for i, off in enumerate(out):
                pieces[off ^ bit] = pieces[off ^ bit] + got[i].astype(f32)
            bit *= 2
        return pieces[0].astype(bf16)

    other = partner(over_heads(value_both[length:])).reshape(length, per, width)
    mine = over_heads(value_both[:length]).reshape(length, per, width)
    first = jnp.where(parity == 0, mine, other)
    second = jnp.where(parity == 0, other, mine)
    input_grad = jnp.stack([first, second], axis=2).reshape(length, 2 * per * width)
    return (query_grad, key_grad, input_grad, weight_grad)


def solution(mesh):
    spec = P("ctx", "head")
    return jax.shard_map(
        local, mesh=mesh, in_specs=(spec,) * 6, out_specs=(spec,) * 4, check_vma=False
    )
```

time: 146 us -> 175 us (1.20)
  blocking collectives: 44.6 us -> 23.1 us
  waiting for transfers between devices: 25 us -> 39.3 us
  starting transfers between devices: 10.6 us -> 20.9 us
  local copies, waits for them, and re-layouts: 9.05 us -> 19.2 us
  between operations: 14.4 us -> 24.1 us
  matrix products: 33.6 us -> 37.2 us
  other arithmetic: 7.68 us -> 10.3 us
    all_gather x2 -> x1, blocking collectives: 44.6 us -> 23.1 us  [local(): every = lax.all_gather(both, 'ctx', axis_index_groups=lines)]
    ppermute x6 -> x7, waiting for transfers between devices: 14 us -> 25 us  [across(): return lax.ppermute(x, 'head', [(i, i ^ bit) for i in range(n_head)])]
    ppermute x0 -> x6, starting transfers between devices: none -> 10.1 us  [local(): moved = lax.ppermute(sums[chain].astype(bf16), 'ctx', ring)]
    dynamic_update_slice x0 -> x3, local copies, waits for them, and re-layouts: none -> 6.84 us  [local(): features = lax.dynamic_update_slice(features, r, ((head ^ off) * per, 0, 0))]
    ppermute x0 -> x6, waiting for transfers between devices: none -> 5.01 us  [local(): moved = lax.ppermute(sums[chain].astype(bf16), 'ctx', ring)]
    select_n x1 -> x3, other arithmetic: 0.07 us -> 3.6 us  [the longest x1 1.84 us: whole(): first = jnp.where(parity == 0, a, b)]
    dot_general x3, matrix products: 1.83 us -> 4.94 us  [inter(): jnp.einsum(spec, x, lo, preferred_element_type=f32)]
    convert_element_type x3 -> x1, other arithmetic: 2.95 us -> 0.06 us  [local(): (pick(states, parity).astype(f32) + their_half.astype(f32)).astype(bf16)]
  transfers between devices with their start and end apart: 13 -> 19, of which waited for: 3 -> 9; matrix products, arithmetic and copies ran while one was open for 29% -> 35% of each run, Pallas kernels for 0% -> 0%
where the time goes in v2:
time: 175 us; the launch traced here: 174 us
  waiting for transfers between devices  39.3 us (22%)
  matrix products  37.2 us (21%)
  between operations  24.1 us (14%)
  blocking collectives  23.1 us (13%)
  starting transfers between devices  20.9 us (12%)
  local copies, waits for them, and re-layouts  19.2 us (11%)
  other arithmetic  10.3 us (6%)
    ppermute x7, waiting for transfers between devices, across(): return lax.ppermute(x, 'head', [(i, i ^ bit) for i in range(n_head)])  25 us
    all_gather x1, blocking collectives, local(): every = lax.all_gather(both, 'ctx', axis_index_groups=lines)  23.1 us
    dot_general x8, matrix products, piece(): lax.dot_general(block, value_both[:, chain * span:(chain + 1) * span], ((...  14.3 us
    ppermute x6, starting transfers between devices, local(): moved = lax.ppermute(sums[chain].astype(bf16), 'ctx', ring)  10.1 us
    ppermute x5, waiting for transfers between devices, partner(): return lax.ppermute(x, 'ctx', [(i, i ^ 1) for i in range(n_ctx)])  9.27 us
    unnamed x34, local copies, waits for them, and re-layouts  7.33 us
    dynamic_update_slice x3, local copies, waits for them, and re-layouts, local(): features = lax.dynamic_update_slice(features, r, ((head ^ off) * per, 0, 0))  6.84 us
    dot_general x8, matrix products, part(): lax.dot_general(positions, w.reshape(per * width, cols), (((1,), (1,)), (...  5.74 us
  transfers between devices with their start and end apart: 19, of which 9 were waited for; matrix products, arithmetic and copies ran while one was open for 35% of the time, Pallas kernels for 0%

profile of v2, /device:TPU:0, one launch (start us, length us, event | category | flops | bytes accessed | tf_op | source)
XLA Modules:
  0.0 174.0 jit_solution(17777477328606567861)
XLA Ops:
  7.3 1.6 copy.159
  9.9 2.9 %collective-permute-start.8 = (bf16[1,512,512]{1,2,0:T(8,128)(2,1)}, bf16[1,512,512]{1,2,0:T(8,128)(2,1)}, u32[]{:S(2)}, u32[]{:S(2)}) collective-permute-start(bf16[1,512,512]{1,2,0:T(8,128)(2,1)} %get-tuple-element.31), channel_id=1, source_target_pairs={{0,4},{4,0},{8,12},{12,8},{16,20},{20,16},{24,28},{28,24},{1,5},{5... | collective-permute-start | bytes 1572872 | tf_op jit(solution)/shard_map/ppermute | solution.py:23
  17.3 2.5 %convolution_bitcast_fusion = f32[512,4,128]{0,2,1:T(8,128)} fusion(bf16[4,512,512]{2,1,0:T(8,128)(2,1)S(1)} %select_convert_fusion.1, bf16[512,512]{1,0:T(8,128)(2,1)} %param.15), kind=kOutput, calls=%fused_computation.3 | convolution fusion | flops 268435456 | bytes 3670016 | tf_op jit(solution)/shard_map/hts,thd->shd/dot_general | solution.py:109
  19.8 8.0 %collective-permute-done = bf16[2,2,128,128]{3,2,1,0:T(8,128)(2,1)S(1)} collective-permute-done((bf16[2,2,128,128]{3,2,1,0:T(8,128)(2,1)}, bf16[2,2,128,128]{3,2,1,0:T(8,128)(2,1)S(1)}, u32[]{:S(2)}, u32[]{:S(2)}) %collective-permute-start) | collective-permute-done | bytes 131104 | tf_op jit(solution)/shard_map/ppermute | solution.py:23
  27.9 23.1 %all-gather = bf16[8,2,128,128]{3,2,1,0:T(8,128)(2,1)S(1)} all-gather(bf16[2,2,128,128]{3,2,1,0:T(8,128)(2,1)S(1)} %fusion.114), channel_id=2, replica_groups={{0,8,16,24},{4,12,20,28},{1,9,17,25},{5,13,21,29},{2,10,18,26},{6,14,22..., dimensions={0}, use_global_device_ids=true | all-gather | bytes 655360 | tf_op jit(solution)/shard_map/all_gather | solution.py:45
  51.7 1.6 pad_maximum_fusion.5
  54.9 2.8 %convolution_bitcast_fusion.1 = f32[512,4,128]{0,2,1:T(8,128)} fusion(bf16[4,512,512]{2,1,0:T(8,128)(2,1)S(1)} %select_convert_fusion.1, bf16[512,512]{1,0:T(8,128)(2,1)} %param.16), kind=kOutput, calls=%fused_computation.4 | convolution fusion | flops 268435456 | bytes 3670016 | tf_op jit(solution)/shard_map/hts,shd->thd/dot_general | solution.py:106
  68.6 1.8 %convert_select_fusion.5 = (f32[2,128,128]{2,1,0:T(8,128)S(1)}, f32[2,128,128]{2,1,0:T(8,128)S(1)}, f32[2,128,128]{2,1,0:T(8,128)S(1)}, f32[2,128,128]{2,1,0:T(8...) fusion(pred[]{:T(512)S(6)} %eq.16, ...), kind=kLoop, calls=%fused_computation.156 | loop fusion | flops 524288 | bytes 1572865 | tf_op jit(solution)/shard_map/jit(_where)/select_n | solution.py:55
  70.5 2.5 %broadcast_in_dim.51 = bf16[4,1024,512]{1,2,0:T(8,128)(2,1)} broadcast(bf16[]{:T(256)} %constant.105.clone.1), dimensions={} | broadcast | bytes 4194306 | tf_op jit(solution)/shard_map/broadcast_in_dim | solution.py:76
  73.0 2.7 %pad_maximum_fusion.3 = (bf16[1,1024,512]{1,2,0:T(8,128)(2,1)}, bf16[4,1024,512]{1,2,0:T(8,128)(2,1)}) fusion(bf16[1,512,512]{1,2,0:T(8,128)(2,1)} %collective-permute-done.8, bf16[1,512,512]{1,2,0:T(8,128)(2,1)S(1)} %copy-done.6, bf16[4,1024,512]{1,2,0:T(8,128)(2,1)} %broadcast_in_dim.51, s32[]{:T(128)S(6)} %select_n.267), kind=kLoop, calls=%fused_computation.47 | loop fusion | flops 2097152 | bytes 3145732 | tf_op jit(solution)/shard_map/concatenate | solution.py:69
  79.0 2.6 %fusion.16 = bf16[512,4,128]{0,2,1:T(8,128)(2,1)S(1)} fusion(f32[512,4,128]{0,2,1:T(8,128)} %fusion.5, bf16[512,4,128]{0,2,1:T(8,128)(2,1)S(1)} %bitcast.320, pred[512,512]{1,0:T(8,128)(4,1)} %copy-done.12, bf16[512,512]{1,0:T(8,128)(2,1)S(1)} %copy-done.2, bf16[512,512]{1,0:T(8,128)(2,1)} %param.15), kind=kOutput, calls=%fused_computation.29 | convolution fusion | flops 539754496 | bytes 3407872 | tf_op jit(solution)/shard_map/hts,the->she/dot_general | solution.py:97
  83.5 15.1 %collective-permute-done.9 = bf16[1,1024,512]{1,2,0:T(8,128)(2,1)} collective-permute-done((bf16[1,1024,512]{1,2,0:T(8,128)(2,1)}, bf16[1,1024,512]{1,2,0:T(8,128)(2,1)}, u32[]{:S(2)}, u32[]{:S(2)}) %collective-permute-start.9) | collective-permute-done | bytes 1048608 | tf_op jit(solution)/shard_map/ppermute | solution.py:26
  98.6 2.0 %fusion.14 = bf16[512,4,128]{0,2,1:T(8,128)(2,1)} fusion(f32[512,4,128]{0,2,1:T(8,128)S(1)} %copy-done.3, f32[4,128,512]{2,1,0:T(8,128)S(1)} %fusion.63, bf16[4,128,128]{2,1,0:T(8,128)(2,1)} %copy-done.7, bf16[512,512]{1,0:T(8,128)(2,1)S(1)} %copy-done), kind=kOutput, calls=%fused_computation.27 | convolution fusion | flops 68157440 | bytes 3276800 | tf_op jit(solution)/shard_map/she,hde->shd/dot_general | solution.py:91
  100.6 2.0 %copy.165 = bf16[512,512]{1,0:T(8,128)(2,1)} copy(bf16[512,512]{0,1:T(8,128)(2,1)} %bitcast.340) | data formatting | bytes 1048576
  106.6 2.3 %constant_dynamic-update-slice_fusion.2 = bf16[4,1024,512]{1,2,0:T(8,128)(2,1)} fusion(bf16[4,1024,512]{1,2,0:T(8,128)(2,1)} %get-tuple-element.29, bf16[1,1024,512]{1,2,0:T(8,128)(2,1)} %collective-permute-done.9, s32[]{:T(128)S(6)} %select_n.270), kind=kLoop, calls=%fused_computation.190 | loop fusion | bytes 2097156 | tf_op jit(solution)/shard_map/dynamic_update_slice | solution.py:78
  108.9 2.3 %constant_dynamic-update-slice_fusion.1 = bf16[4,1024,512]{1,2,0:T(8,128)(2,1)} fusion(bf16[4,1024,512]{1,2,0:T(8,128)(2,1)} %constant_dynamic-update-slice_fusion.2, bf16[1,1024,512]{1,2,0:T(8,128)(2,1)} %collective-permute-done.10, s32[]{:T(128)S(6)} %select_n.268), kind=kLoop, calls=%fused_computation.189 | loop fusion | bytes 2097156 | tf_op jit(solution)/shard_map/dynamic_update_slice | solution.py:78
  111.2 2.3 %constant_dynamic-update-slice_fusion = bf16[4,1024,512]{1,2,0:T(8,128)(2,1)} fusion(bf16[4,1024,512]{1,2,0:T(8,128)(2,1)} %constant_dynamic-update-slice_fusion.1, bf16[1,1024,512]{1,2,0:T(8,128)(2,1)} %collective-permute-done.11, s32[]{:T(128)S(6)} %select_n.269), kind=kLoop, calls=%fused_computation.188 | loop fusion | bytes 2097156 | tf_op jit(solution)/shard_map/dynamic_update_slice | solution.py:78
  113.5 2.4 %convolution_convert_fusion.5 = bf16[512,256]{1,0:T(8,128)(2,1)} fusion(bf16[1024,256]{0,1:T(8,128)(2,1)S(1)} %get-tuple-element.26, bf16[4,1024,512]{1,2,0:T(8,128)(2,1)} %constant_dynamic-update-slice_fusion, s32[]{:T(128)S(6)} %select_n.281), kind=kOutput, calls=%fused_computation.41 | convolution fusion | flops 268566528 | bytes 1835012 | tf_op jit(solution)/shard_map/dot_general | solution.py:129
  116.4 1.7 convolution_convert_fusion.4
  118.1 3.2 %collective-permute-start.15 = (bf16[512,256]{1,0:T(8,128)(2,1)S(1)}, bf16[512,256]{1,0:T(8,128)(2,1)S(1)}, u32[]{:S(2)}, u32[]{:S(2)}) collective-permute-start(bf16[512,256]{1,0:T(8,128)(2,1)S(1)} %convolution_convert_fusion.4), channel_id=1, source_target_pairs={{0,16},{4,20},{16,24},{20,28},{24,8},{28,12},{8,0},{12,4},{1,17},{... | collective-permute-start | bytes 786440 | tf_op jit(solution)/shard_map/ppermute | solution.py:139
  121.3 1.6 fusion.20
  125.2 1.7 fusion.22
  130.8 1.7 fusion.47
  132.5 1.7 collective-permute-start.16
  134.2 2.2 %collective-permute-done.13 = bf16[512,256]{1,0:T(8,128)(2,1)S(1)} collective-permute-done((bf16[512,256]{1,0:T(8,128)(2,1)S(1)}, bf16[512,256]{1,0:T(8,128)(2,1)S(1)}, u32[]{:S(2)}, u32[]{:S(2)}) %collective-permute-start.13) | collective-permute-done | bytes 262176 | tf_op jit(solution)/shard_map/ppermute | solution.py:139
  136.4 1.7 fusion.23
  142.3 1.7 fusion.38
  144.0 2.0 %collective-permute-start.17 = (bf16[512,256]{1,0:T(8,128)(2,1)S(1)}, bf16[512,256]{1,0:T(8,128)(2,1)S(1)}, u32[]{:S(2)}, u32[]{:S(2)}) collective-permute-start(bf16[512,256]{1,0:T(8,128)(2,1)S(1)} %fusion.38), channel_id=1, source_target_pairs={{0,16},{4,20},{16,24},{20,28},{24,8},{28,12},{8,0},{12,4},{1,17},{... | collective-permute-start | bytes 786440 | tf_op jit(solution)/shard_map/ppermute | solution.py:139
  148.4 6.3 %collective-permute-done.6 = bf16[1,512,512]{1,2,0:T(8,128)(2,1)S(1)} collective-permute-done((bf16[1,512,512]{1,2,0:T(8,128)(2,1)S(1)}, bf16[1,512,512]{1,2,0:T(8,128)(2,1)S(1)}, u32[]{:S(2)}, u32[]{:S(2)}) %collective-permute-start.6) | collective-permute-done | bytes 524320 | tf_op jit(solution)/shard_map/ppermute | solution.py:26
  155.9 1.7 convolution_add_fusion.5
  157.6 1.7 fusion.29
  160.5 3.5 %collective-permute-done.3 = bf16[1,512,512]{1,2,0:T(8,128)(2,1)S(1)} collective-permute-done((bf16[1,512,512]{1,2,0:T(8,128)(2,1)S(1)}, bf16[1,512,512]{1,2,0:T(8,128)(2,1)S(1)}, u32[]{:S(2)}, u32[]{:S(2)}) %collective-permute-start.3) | collective-permute-done | bytes 524320 | tf_op jit(solution)/shard_map/ppermute | solution.py:26
  (94 shorter events, 36.8 us)
Async XLA Ops:
  7.2 7.3 %copy-start = (bf16[512,512]{1,0:T(8,128)(2,1)S(1)}, bf16[512,512]{1,0:T(8,128)(2,1)}, u32[]{:S(2)}) copy-start(bf16[512,512]{1,0:T(8,128)(2,1)} %param.17) | copy-start | bytes 1572868
  7.2 6.9 %copy-start.5 = (bf16[512,512]{1,0:T(8,128)(2,1)S(1)}, bf16[512,512]{1,0:T(8,128)(2,1)}, u32[]{:S(2)}) copy-start(bf16[512,512]{1,0:T(8,128)(2,1)} %param.15) | copy-start | bytes 1572868
  7.2 7.3 %copy-start.1 = (bf16[512,512]{1,0:T(8,128)(2,1)S(1)}, bf16[512,512]{1,0:T(8,128)(2,1)}, u32[]{:S(2)}) copy-start(bf16[512,512]{1,0:T(8,128)(2,1)} %param.16) | copy-start | bytes 1572868
  7.2 114.1 %all-gather.4.cloned.1.call-start = ((), (), s32[]{:S(2)}) async-start(), calls=%async_computation | async-start | bytes 2621440 | tf_op jit(solution)/shard_map/all_gather | solution.py:28
  9.9 60.6 %collective-permute-start.8 = (bf16[1,512,512]{1,2,0:T(8,128)(2,1)}, bf16[1,512,512]{1,2,0:T(8,128)(2,1)}, u32[]{:S(2)}, u32[]{:S(2)}) collective-permute-start(bf16[1,512,512]{1,2,0:T(8,128)(2,1)} %get-tuple-element.31), channel_id=1, source_target_pairs={{0,4},{4,0},{8,12},{12,8},{16,20},{20,16},{24,28},{28,24},{1,5},{5... | collective-permute-start | bytes 1572872 | tf_op jit(solution)/shard_map/ppermute | solution.py:23
  15.6 12.2 %collective-permute-start = (bf16[2,2,128,128]{3,2,1,0:T(8,128)(2,1)}, bf16[2,2,128,128]{3,2,1,0:T(8,128)(2,1)S(1)}, u32[]{:S(2)}, u32[]{:S(2)}) collective-permute-start(bf16[2,2,128,128]{3,2,1,0:T(8,128)(2,1)} %get-tuple-element.46), channel_id=1, source_target_pairs={{0,4},{4,0},{8,12},{12,8},{16,20},{20,16},{24,28},{28,24},{1,5},{5... | collective-permute-start | bytes 393224 | tf_op jit(solution)/shard_map/ppermute | solution.py:23
  17.3 40.4 %copy-start.14 = (s32[4]{0:T(128)S(1)}, s32[4]{0:T(128)}, u32[]{:S(2)}) copy-start(s32[4]{0:T(128)} %constant.111.clone) | copy-start | bytes 52
  17.3 43.3 %copy-start.13 = (s32[4]{0:T(128)S(1)}, s32[4]{0:T(128)}, u32[]{:S(2)}) copy-start(s32[4]{0:T(128)} %constant.112.clone) | copy-start | bytes 52
  27.8 40.8 %copy-start.11 = (bf16[2,2,128,128]{3,2,1,0:T(8,128)(2,1)}, bf16[2,2,128,128]{3,2,1,0:T(8,128)(2,1)S(1)}, u32[]{:S(2)}) copy-start(bf16[2,2,128,128]{3,2,1,0:T(8,128)(2,1)S(1)} %collective-permute-done) | copy-start | bytes 393220
  51.1 2.2 %copy-start.10 = (bf16[2,128,128]{2,1,0:T(8,128)(2,1)}, bf16[2,128,128]{2,1,0:T(8,128)(2,1)S(1)}, u32[]{:S(2)}) copy-start(bf16[2,128,128]{2,1,0:T(8,128)(2,1)S(1)} %get-tuple-element.21) | copy-start | bytes 196612
  53.4 15.2 %collective-permute-start.1 = (bf16[2,2,2,128,128]{4,3,2,1,0:T(8,128)(2,1)}, bf16[2,2,2,128,128]{4,3,2,1,0:T(8,128)(2,1)}, u32[]{:S(2)}, u32[]{:S(2)}) collective-permute-start(bf16[2,2,2,128,128]{4,3,2,1,0:T(8,128)(2,1)} %pad_maximum_fusion.5), channel_id=1, source_target_pairs={{0,4},{4,0},{8,12},{12,8},{16,20},{20,16},{24,28},{28,24},{1,5},{5... | collective-permute-start | bytes 786440 | tf_op jit(solution)/shard_map/ppermute | solution.py:23
  57.7 15.3 %copy-start.6 = (bf16[1,512,512]{1,2,0:T(8,128)(2,1)S(1)}, bf16[1,512,512]{1,2,0:T(8,128)(2,1)}, u32[]{:S(2)}) copy-start(bf16[1,512,512]{1,2,0:T(8,128)(2,1)} %get-tuple-element.30) | copy-start | bytes 1572868
  70.4 6.9 %copy-start.2 = (bf16[512,512]{1,0:T(8,128)(2,1)S(1)}, bf16[512,512]{1,0:T(8,128)(2,1)}, u32[]{:S(2)}) copy-start(bf16[512,512]{1,0:T(8,128)(2,1)} %param.16) | copy-start | bytes 1572868
  70.5 7.2 %copy-start.8 = (bf16[4,128,128]{2,1,0:T(8,128)(2,1)}, bf16[4,128,128]{2,1,0:T(8,128)(2,1)S(1)}, u32[]{:S(2)}) copy-start(bf16[4,128,128]{2,1,0:T(8,128)(2,1)S(1)} %get-tuple-element.25) | copy-start | bytes 393220
  70.5 7.2 %copy-start.7 = (bf16[4,128,128]{2,1,0:T(8,128)(2,1)}, bf16[4,128,128]{2,1,0:T(8,128)(2,1)S(1)}, u32[]{:S(2)}) copy-start(bf16[4,128,128]{2,1,0:T(8,128)(2,1)S(1)} %get-tuple-element.24) | copy-start | bytes 393220
  75.7 22.9 %collective-permute-start.9 = (bf16[1,1024,512]{1,2,0:T(8,128)(2,1)}, bf16[1,1024,512]{1,2,0:T(8,128)(2,1)}, u32[]{:S(2)}, u32[]{:S(2)}) collective-permute-start(bf16[1,1024,512]{1,2,0:T(8,128)(2,1)} %get-tuple-element.28), channel_id=1, source_target_pairs={{0,2},{1,3},{2,0},{3,1},{4,6},{5,7},{6,4},{7,5},{8,10},{9,11},{10,... | collective-permute-start | bytes 3145736 | tf_op jit(solution)/shard_map/ppermute | solution.py:26
  79.0 19.6 %copy-start.3 = (f32[512,4,128]{0,2,1:T(8,128)S(1)}, f32[512,4,128]{0,2,1:T(8,128)}, u32[]{:S(2)}) copy-start(f32[512,4,128]{0,2,1:T(8,128)} %convolution_bitcast_fusion) | copy-start | bytes 3145732
  81.6 24.8 %collective-permute-start.4 = (bf16[512,512]{0,1:T(8,128)(2,1)S(1)}, bf16[512,512]{0,1:T(8,128)(2,1)S(1)}, u32[]{:S(2)}, u32[]{:S(2)}) collective-permute-start(bf16[512,512]{0,1:T(8,128)(2,1)S(1)} %bitcast.323), channel_id=1, source_target_pairs={{0,4},{4,0},{8,12},{12,8},{16,20},{20,16},{24,28},{28,24},{1,5},{5... | collective-permute-start | bytes 1572872 | tf_op jit(solution)/shard_map/ppermute | solution.py:23
  83.5 25.5 %collective-permute-start.10 = (bf16[1,1024,512]{1,2,0:T(8,128)(2,1)}, bf16[1,1024,512]{1,2,0:T(8,128)(2,1)}, u32[]{:S(2)}, u32[]{:S(2)}) collective-permute-start(bf16[1,1024,512]{1,2,0:T(8,128)(2,1)} %get-tuple-element.28), channel_id=1, source_target_pairs={{0,1},{1,0},{2,3},{3,2},{4,5},{5,4},{6,7},{7,6},{8,9},{9,8},{10,11... | collective-permute-start | bytes 3145736 | tf_op jit(solution)/shard_map/ppermute | solution.py:26
  98.6 12.5 %collective-permute-start.11 = (bf16[1,1024,512]{1,2,0:T(8,128)(2,1)}, bf16[1,1024,512]{1,2,0:T(8,128)(2,1)}, u32[]{:S(2)}, u32[]{:S(2)}) collective-permute-start(bf16[1,1024,512]{1,2,0:T(8,128)(2,1)} %collective-permute-done.9), channel_id=1, source_target_pairs={{0,1},{1,0},{2,3},{3,2},{4,5},{5,4},{6,7},{7,6},{8,9},{9,8},{10,11... | collective-permute-start | bytes 3145736 | tf_op jit(solution)/shard_map/ppermute | solution.py:26
  115.9 9.3 %collective-permute-start.12 = (bf16[512,256]{1,0:T(8,128)(2,1)}, bf16[512,256]{1,0:T(8,128)(2,1)S(1)}, u32[]{:S(2)}, u32[]{:S(2)}) collective-permute-start(bf16[512,256]{1,0:T(8,128)(2,1)} %convolution_convert_fusion.5), channel_id=1, source_target_pairs={{0,16},{4,20},{16,24},{20,28},{24,8},{28,12},{8,0},{12,4},{1,17},{... | collective-permute-start | bytes 786440 | tf_op jit(solution)/shard_map/ppermute | solution.py:139
  118.1 12.7 %collective-permute-start.15 = (bf16[512,256]{1,0:T(8,128)(2,1)S(1)}, bf16[512,256]{1,0:T(8,128)(2,1)S(1)}, u32[]{:S(2)}, u32[]{:S(2)}) collective-permute-start(bf16[512,256]{1,0:T(8,128)(2,1)S(1)} %convolution_convert_fusion.4), channel_id=1, source_target_pairs={{0,16},{4,20},{16,24},{20,28},{24,8},{28,12},{8,0},{12,4},{1,17},{... | collective-permute-start | bytes 786440 | tf_op jit(solution)/shard_map/ppermute | solution.py:139
  121.3 7.1 %copy-start.4 = (bf16[2048,512]{1,0:T(8,128)(2,1)S(1)}, bf16[2048,512]{1,0:T(8,128)(2,1)}, u32[]{:S(2)}) copy-start(bf16[2048,512]{1,0:T(8,128)(2,1)} %all-gather.4.cloned.1.call-done) | copy-start | bytes 6291460
  124.5 14.8 %collective-permute-start.5 = (bf16[2,512,512]{1,2,0:T(8,128)(2,1)S(1)}, bf16[2,512,512]{1,2,0:T(8,128)(2,1)S(1)}, u32[]{:S(2)}, u32[]{:S(2)}) collective-permute-start(bf16[2,512,512]{1,2,0:T(8,128)(2,1)S(1)} %pad_maximum_fusion.1), channel_id=1, source_target_pairs={{0,1},{1,0},{2,3},{3,2},{4,5},{5,4},{6,7},{7,6},{8,9},{9,8},{10,11... | collective-permute-start | bytes 3145736 | tf_op jit(solution)/shard_map/ppermute | solution.py:26
  126.9 9.5 %collective-permute-start.13 = (bf16[512,256]{1,0:T(8,128)(2,1)S(1)}, bf16[512,256]{1,0:T(8,128)(2,1)S(1)}, u32[]{:S(2)}, u32[]{:S(2)}) collective-permute-start(bf16[512,256]{1,0:T(8,128)(2,1)S(1)} %fusion.22), channel_id=1, source_target_pairs={{0,16},{4,20},{16,24},{20,28},{24,8},{28,12},{8,0},{12,4},{1,17},{... | collective-permute-start | bytes 786440 | tf_op jit(solution)/shard_map/ppermute | solution.py:139
  129.4 17.0 %collective-permute-start.2 = (bf16[2,512,512]{1,2,0:T(8,128)(2,1)S(1)}, bf16[2,512,512]{1,2,0:T(8,128)(2,1)S(1)}, u32[]{:S(2)}, u32[]{:S(2)}) collective-permute-start(bf16[2,512,512]{1,2,0:T(8,128)(2,1)S(1)} %pad_maximum_fusion), channel_id=1, source_target_pairs={{0,1},{1,0},{2,3},{3,2},{4,5},{5,4},{6,7},{7,6},{8,9},{9,8},{10,11... | collective-permute-start | bytes 3145736 | tf_op jit(solution)/shard_map/ppermute | solution.py:26
  132.5 9.7 %collective-permute-start.16 = (bf16[512,256]{1,0:T(8,128)(2,1)S(1)}, bf16[512,256]{1,0:T(8,128)(2,1)S(1)}, u32[]{:S(2)}, u32[]{:S(2)}) collective-permute-start(bf16[512,256]{1,0:T(8,128)(2,1)S(1)} %fusion.47), channel_id=1, source_target_pairs={{0,16},{4,20},{16,24},{20,28},{24,8},{28,12},{8,0},{12,4},{1,17},{... | collective-permute-start | bytes 786440 | tf_op jit(solution)/shard_map/ppermute | solution.py:139
  138.1 17.8 %collective-permute-start.14 = (bf16[512,256]{1,0:T(8,128)(2,1)S(1)}, bf16[512,256]{1,0:T(8,128)(2,1)S(1)}, u32[]{:S(2)}, u32[]{:S(2)}) collective-permute-start(bf16[512,256]{1,0:T(8,128)(2,1)S(1)} %fusion.23), channel_id=1, source_target_pairs={{0,16},{4,20},{16,24},{20,28},{24,8},{28,12},{8,0},{12,4},{1,17},{... | collective-permute-start | bytes 786440 | tf_op jit(solution)/shard_map/ppermute | solution.py:139
  139.8 14.9 %collective-permute-start.6 = (bf16[1,512,512]{1,2,0:T(8,128)(2,1)S(1)}, bf16[1,512,512]{1,2,0:T(8,128)(2,1)S(1)}, u32[]{:S(2)}, u32[]{:S(2)}) collective-permute-start(bf16[1,512,512]{1,2,0:T(8,128)(2,1)S(1)} %fusion.17), channel_id=1, source_target_pairs={{0,2},{1,3},{2,0},{3,1},{4,6},{5,7},{6,4},{7,5},{8,10},{9,11},{10,... | collective-permute-start | bytes 1572872 | tf_op jit(solution)/shard_map/ppermute | solution.py:26
  144.0 13.6 %collective-permute-start.17 = (bf16[512,256]{1,0:T(8,128)(2,1)S(1)}, bf16[512,256]{1,0:T(8,128)(2,1)S(1)}, u32[]{:S(2)}, u32[]{:S(2)}) collective-permute-start(bf16[512,256]{1,0:T(8,128)(2,1)S(1)} %fusion.38), channel_id=1, source_target_pairs={{0,16},{4,20},{16,24},{20,28},{24,8},{28,12},{8,0},{12,4},{1,17},{... | collective-permute-start | bytes 786440 | tf_op jit(solution)/shard_map/ppermute | solution.py:139
  146.9 17.1 %collective-permute-start.3 = (bf16[1,512,512]{1,2,0:T(8,128)(2,1)S(1)}, bf16[1,512,512]{1,2,0:T(8,128)(2,1)S(1)}, u32[]{:S(2)}, u32[]{:S(2)}) collective-permute-start(bf16[1,512,512]{1,2,0:T(8,128)(2,1)S(1)} %fusion.60), channel_id=1, source_target_pairs={{0,2},{1,3},{2,0},{3,1},{4,6},{5,7},{6,4},{7,5},{8,10},{9,11},{10,... | collective-permute-start | bytes 1572872 | tf_op jit(solution)/shard_map/ppermute | solution.py:26
  155.2 10.1 %collective-permute-start.7 = (bf16[512,512]{0,1:T(8,128)(2,1)S(1)}, bf16[512,512]{0,1:T(8,128)(2,1)S(1)}, u32[]{:S(2)}, u32[]{:S(2)}) collective-permute-start(bf16[512,512]{0,1:T(8,128)(2,1)S(1)} %fusion.12), channel_id=1, source_target_pairs={{0,4},{4,0},{8,12},{12,8},{16,20},{20,16},{24,28},{28,24},{1,5},{5... | collective-permute-start | bytes 1572872 | tf_op jit(solution)/shard_map/ppermute | solution.py:23
  (2 other events, 1.3 us)
Sparse Core Ops, SparseCore 0:
  15.7 56.0 all-gather.3

commit v3 on v2

v3 whole, which is shorter than its diff:
```python
import functools
import math

import jax
import jax.numpy as jnp
from jax import lax
from jax.experimental import pallas as pl
from jax.experimental.pallas import tpu as pltpu
from jax.sharding import PartitionSpec as P

DH = 128
F32, BF16 = jnp.float32, jnp.bfloat16
VMEM = pl.BlockSpec(memory_space=pltpu.VMEM)
SMEM = pl.BlockSpec(memory_space=pltpu.SMEM)
ANY = pl.BlockSpec(memory_space=pl.ANY)
PARAMS = pltpu.CompilerParams(vmem_limit_bytes=48 * 2**20)


def dot(a, b, ca, cb):
    return lax.dot_general(a, b, (((ca,), (cb,)), ((), ())), preferred_element_type=F32)


def cost(flops, moved):
    return pl.CostEstimate(flops=flops, bytes_accessed=moved, transcendentals=0)


def states_kernel(par_ref, q_ref, k_ref, v_ref, g_ref, keep_ref, send_ref, near_ref):
    heads = q_ref.shape[1] // DH
    half = heads // 2
    for hd in range(heads):
        at = slice(hd * DH, (hd + 1) * DH)
        for kind, (a, b) in enumerate(((q_ref, g_ref), (k_ref, v_ref))):
            s = dot(a[:, at], b[:, at], 0, 0)
            own = par_ref[0] == hd // half

            @pl.when(own)
            def _():
                keep_ref[kind, hd % half] = s
                near_ref[kind, hd % half] = s.astype(BF16)

            @pl.when(jnp.logical_not(own))
            def _():
                send_ref[kind, hd % half] = s


def states(par, q, k, v, g):
    half = q.shape[1] // DH // 2
    shape = (2, half, DH, DH)
    return pl.pallas_call(
        states_kernel,
        in_specs=[SMEM] + [VMEM] * 4,
        out_specs=[VMEM] * 3,
        out_shape=[
            jax.ShapeDtypeStruct(shape, F32),
            jax.ShapeDtypeStruct(shape, F32),
            jax.ShapeDtypeStruct(shape, BF16),
        ],
        compiler_params=PARAMS,
        cost_estimate=cost(8 * 512 * 512 * DH, 4 * q.size * 2),
        name="states",
    )(par, q, k, v, g)


def split_kernel(per, par_ref, x_ref, _, own_ref, theirs_ref):
    width = x_ref.shape[1] // (2 * per)
    for k in range(2):
        for i in range(per):
            block = x_ref[:, (2 * i + k) * width : (2 * i + k + 1) * width]

            @pl.when(par_ref[0] == k)
            def _():
                own_ref[i] = block

            @pl.when(par_ref[0] != k)
            def _():
                theirs_ref[i] = block


def split(par, x, per, after):
    width = x.shape[1] // (2 * per)
    out = jax.ShapeDtypeStruct((per, x.shape[0], width), x.dtype)
    return pl.pallas_call(
        functools.partial(split_kernel, per),
        in_specs=[SMEM, VMEM, ANY],
        out_specs=[VMEM] * 2,
        out_shape=[out, out],
        compiler_params=PARAMS,
        cost_estimate=cost(0, x.size * 4),
        name="split",
    )(par, x, after)


def inside_kernel(q_ref, k_ref, v_ref, g_ref, _, vo_ref, qo_ref, ko_ref):
    q, k, v, g = q_ref[...], k_ref[...], v_ref[...], g_ref[...]
    n = q.shape[0]
    rows = lax.broadcasted_iota(jnp.int32, (n, n), 0)
    cols = lax.broadcasted_iota(jnp.int32, (n, n), 1)
    causal = rows >= cols
    ks = jnp.where(causal, dot(q, k, 1, 1), 0.0).astype(BF16)
    vo_ref[...] = dot(ks, g, 0, 0)
    gs = jnp.where(causal, dot(g, v, 1, 1), 0.0).astype(BF16)
    qo_ref[...] = dot(gs, k, 1, 0)
    ko_ref[...] = dot(gs, q, 0, 0)


def inside(q, k, v, g, after):
    n, cols = q.shape
    spec = pl.BlockSpec((n, DH), lambda h: (0, h))
    out = jax.ShapeDtypeStruct((n, cols), F32)
    return pl.pallas_call(
        inside_kernel,
        grid=(cols // DH,),
        in_specs=[spec] * 4 + [ANY],
        out_specs=[spec] * 3,
        out_shape=[out] * 3,
        compiler_params=PARAMS,
        cost_estimate=cost(10 * n * n * cols, 20 * n * cols),
        name="inside",
    )(q, k, v, g, after)


def far_kernel(pair_ref, every_ref, out_ref):
    for kind in range(2):
        total = jnp.zeros(out_ref.shape[1:], F32)
        for p in range(every_ref.shape[0]):
            reached = p > pair_ref[0] if kind == 0 else p < pair_ref[0]
            total = total + jnp.where(reached, every_ref[p, kind].astype(F32), 0.0)
        out_ref[kind] = total


def far_states(pair, every):
    return pl.pallas_call(
        far_kernel,
        in_specs=[SMEM, VMEM],
        out_specs=VMEM,
        out_shape=jax.ShapeDtypeStruct(every.shape[1:], F32),
        compiler_params=PARAMS,
        cost_estimate=cost(0, every.size * 2),
        name="far",
    )(pair, every)


def entering(par, hd, half, kind, far, got_far, near, got_near):
    mine = par == hd // half
    i = hd % half
    outer = jnp.where(mine, far[kind, i], got_far[kind, i])
    close = jnp.where(mine, near[kind, i], got_near[kind, i].astype(F32))
    total = outer + jnp.where(par == kind, close, 0.0)
    hi = total.astype(BF16)
    return hi, (total - hi.astype(F32)).astype(BF16)


def value_kernel(factor, par_ref, k_ref, vi_ref, far, got_far, near, got_near, *outs):
    heads = k_ref.shape[1] // DH
    span = outs[0].shape[1] // DH
    for hd in range(heads):
        at = slice(hd * DH, (hd + 1) * DH)
        hi, lo = entering(
            par_ref[0], hd, heads // 2, 0, far, got_far, near, got_near
        )
        k = k_ref[:, at]
        total = vi_ref[:, at] + (dot(k, hi, 1, 0) + dot(k, lo, 1, 0))
        to = (hd % span) * DH
        outs[hd // span][:, to : to + DH] = (factor * total).astype(BF16)


def finish_value(factor, par, k, vi, ends, chains):
    n, cols = k.shape
    out = jax.ShapeDtypeStruct((n, cols // chains), BF16)
    return pl.pallas_call(
        functools.partial(value_kernel, factor),
        in_specs=[SMEM] + [VMEM] * 6,
        out_specs=[VMEM] * chains,
        out_shape=[out] * chains,
        compiler_params=PARAMS,
        cost_estimate=cost(4 * n * cols * DH, 8 * n * cols),
        name="finish_value",
    )(par, k, vi, *ends)


def others_kernel(
    factor, par_ref, g_ref, v_ref, qi_ref, ki_ref, far, got_far, near, got_near, *outs
):
    heads = g_ref.shape[1] // DH
    for hd in range(heads):
        at = slice(hd * DH, (hd + 1) * DH)
        for kind, x_ref, i_ref in ((1, g_ref, qi_ref), (0, v_ref, ki_ref)):
            hi, lo = entering(
                par_ref[0], hd, heads // 2, kind, far, got_far, near, got_near
            )
            x = x_ref[:, at]
            total = i_ref[:, at] + (dot(x, hi, 1, 1) + dot(x, lo, 1, 1))
            outs[1 - kind][:, at] = (factor * total).astype(BF16)


def finish_others(factor, par, g, v, qi, ki, ends):
    out = jax.ShapeDtypeStruct(g.shape, BF16)
    return pl.pallas_call(
        functools.partial(others_kernel, factor),
        in_specs=[SMEM] + [VMEM] * 8,
        out_specs=[VMEM] * 2,
        out_shape=[out] * 2,
        compiler_params=PARAMS,
        cost_estimate=cost(8 * g.size * DH, 16 * g.size),
        name="finish_others",
    )(par, g, v, qi, ki, *ends)


def piece_kernel(count, dtype, offs_ref, subs_ref, a_ref, b_ref, *refs):
    own, theirs = refs[:count], refs[count : 2 * count]
    out_ref, x, y, sems = refs[2 * count :]
    step = pl.program_id(0)
    for i in range(count):

        @pl.when(offs_ref[step] == i)
        def _():
            one = pltpu.make_async_copy(own[i].at[subs_ref[step]], x, sems.at[0])
            two = pltpu.make_async_copy(theirs[i].at[subs_ref[step]], y, sems.at[1])
            one.start()
            two.start()
            one.wait()
            two.wait()

    total = dot(x[...], a_ref[...], 0, 0) + dot(y[...], b_ref[...], 0, 0)
    out_ref[0] = total.astype(dtype)


def pieces(dtype, offs, subs, a, b, own, theirs):
    steps = offs.shape[0]
    count = len(own)
    _, n, width = own[0].shape
    span = a.shape[1]
    return pl.pallas_call(
        functools.partial(piece_kernel, count, dtype),
        grid=(steps,),
        in_specs=[SMEM] * 2 + [VMEM] * 2 + [ANY] * (2 * count),
        out_specs=pl.BlockSpec((1, width, span), lambda s: (s, 0, 0)),
        out_shape=jax.ShapeDtypeStruct((steps, width, span), dtype),
        scratch_shapes=[
            pltpu.VMEM((n, width), BF16),
            pltpu.VMEM((n, width), BF16),
            pltpu.SemaphoreType.DMA((2,)),
        ],
        compiler_params=PARAMS,
        cost_estimate=cost(4 * n * width * span * steps, 4 * n * (width + span) * steps),
        name="pieces",
    )(offs, subs, a, b, *own, *theirs)


def local(queries, keys, values, out_grad, inputs, value_weight):
    length, cols = queries.shape
    n_ctx, n_head = lax.axis_size("ctx"), lax.axis_size("head")
    pairs = n_ctx // 2
    ctx, head = lax.axis_index("ctx"), lax.axis_index("head")
    parity, pair = ctx % 2, ctx // 2
    par = parity.astype(jnp.int32).reshape(1)
    factor = 1.0 / math.sqrt(DH * length * n_ctx)
    lines = [[2 * i + k for i in range(pairs)] for k in range(2)]
    chains = 2
    span = cols // chains

    def partner(x):
        return lax.ppermute(x, "ctx", [(i, i ^ 1) for i in range(n_ctx)])

    def across(x, bit):
        return lax.ppermute(x, "head", [(i, i ^ bit) for i in range(n_head)])

    part_rows = value_weight.shape[0] // 2
    weights = [
        lax.all_gather(
            value_weight[i * part_rows : (i + 1) * part_rows],
            "ctx",
            axis_index_groups=lines,
        )
        for i in range(2)
    ]

    keep, send, near16 = states(par, queries, keys, values, out_grad)
    their_half = partner(send)
    got_near = partner(near16)
    both = (keep + their_half).astype(BF16)

    per = n_ctx // n_head // 2
    own, theirs = split(par, inputs, per, send)
    own, theirs = [own], [partner(theirs)]
    offsets = [0]
    bit = n_head // 2
    while bit:
        own = own + [across(r, bit) for r in own]
        theirs = theirs + [across(r, bit) for r in theirs]
        offsets = offsets + [o ^ bit for o in offsets]
        bit //= 2
    own = [own[offsets.index(i)] for i in range(n_head)]
    theirs = [theirs[offsets.index(i)] for i in range(n_head)]

    vi, qi, ki = inside(queries, keys, values, out_grad, send)

    every = lax.all_gather(both, "ctx", axis_index_groups=lines)
    far = far_states(pair.astype(jnp.int32).reshape(1), every)
    ends = (far, partner(far), their_half, got_near)

    value_mine = finish_value(factor, par, keys, vi, ends, chains)
    value_theirs = [partner(x) for x in value_mine]
    query_grad, key_grad = finish_others(factor, par, out_grad, values, qi, ki, ends)

    order = list(range(0, pairs, 2)) + list(range(1, pairs, 2))[::-1]
    place = [order.index(i) for i in range(pairs)]
    ring = [
        (2 * order[i] + k, 2 * order[(i + 1) % pairs] + k)
        for i in range(pairs)
        for k in range(2)
    ]
    spot = jnp.asarray(place, jnp.int32)[pair]
    which = jnp.asarray(order, jnp.int32)[
        (spot - 1 - jnp.arange(pairs, dtype=jnp.int32)) % pairs
    ]
    offs, subs = (which // per) ^ head, which % per

    sums, rest = [], []
    for a, b in zip(value_mine, value_theirs):
        sums.append(pieces(BF16, offs[:1], subs[:1], a, b, own, theirs)[0])
        rest.append(pieces(F32, offs[1:], subs[1:], a, b, own, theirs))
    for step in range(1, pairs):
        for i in range(chains):
            moved = lax.ppermute(sums[i].astype(BF16), "ctx", ring)
            sums[i] = moved.astype(F32) + rest[i][step - 1]
    weight_grad = jnp.concatenate(sums, axis=1) * (1.0 / math.sqrt(length * n_ctx))

    value_both = jnp.concatenate(
        [jnp.concatenate(x, axis=1) for x in (value_theirs, value_mine)], axis=0
    )
    block = per * part_rows

    def over_heads(weight):
        found = {}
        for off in range(n_head):
            w = lax.dynamic_slice_in_dim(weight, (head ^ off) * per, per, 0)
            found[off] = dot(value_both, w.reshape(block, cols), 1, 1)
        bit = 1
        while bit < n_head:
            out = [off for off in sorted(found) if off & bit]
            got = across(jnp.stack([found.pop(o).astype(BF16) for o in out]), bit)
            for i, off in enumerate(out):
                found[off ^ bit] = found[off ^ bit] + got[i].astype(F32)
            bit *= 2
        return found[0].astype(BF16)

    mine, other = [], []
    for weight in weights:
        total = over_heads(weight)
        other.append(partner(total[:length]).reshape(length, per, part_rows))
        mine.append(total[length:].reshape(length, per, part_rows))
    mine, other = jnp.concatenate(mine, axis=2), jnp.concatenate(other, axis=2)
    first = jnp.where(parity == 0, mine, other)
    second = jnp.where(parity == 0, other, mine)
    input_grad = jnp.stack([first, second], axis=2).reshape(length, -1)
    return (query_grad, key_grad, input_grad, weight_grad)


def solution(mesh):
    spec = P("ctx", "head")
    return jax.shard_map(
        local, mesh=mesh, in_specs=(spec,) * 6, out_specs=(spec,) * 4, check_vma=False
    )
```

time: 175 us -> 162 us (0.926)
  Pallas kernels: 0 us -> 27.8 us
  matrix products: 37.2 us -> 13.2 us
  between operations: 24.1 us -> 15.1 us
  starting transfers between devices: 20.9 us -> 28.6 us
  other arithmetic: 10.3 us -> 4.05 us
  blocking collectives: 23.1 us -> 17.4 us
  waiting for transfers between devices: 39.3 us -> 36.4 us
    pallas_call x0 -> x10, Pallas kernels: none -> 27.8 us  [the longest x4 14.6 us: pieces(): pl.pallas_call(functools.partial(piece_kernel, count, dtype), grid=(steps...]
    dot_general x28 -> x8, matrix products: 37.2 us -> 13.2 us  [dot(): lax.dot_general(a, b, (((ca,), (cb,)), ((), ())), preferred_element_type=...]
    ppermute x7 -> x10, waiting for transfers between devices: 25 us -> 11.4 us  [across(): return lax.ppermute(x, 'head', [(i, i ^ bit) for i in range(n_head)])]
    ppermute x5 -> x8, waiting for transfers between devices: 9.27 us -> 17.8 us  [partner(): return lax.ppermute(x, 'ctx', [(i, i ^ 1) for i in range(n_ctx)])]
    unnamed x34 -> x55, local copies, waits for them, and re-layouts: 7.33 us -> 14.8 us
    dynamic_update_slice x3 -> x0, local copies, waits for them, and re-layouts: 6.84 us -> none  [local(): features = lax.dynamic_update_slice(features, r, ((head ^ off) * per, 0, 0))]
    all_gather x1, blocking collectives: 23.1 us -> 17.4 us  [local(): every = lax.all_gather(both, 'ctx', axis_index_groups=lines)]
    ppermute x7 -> x10, starting transfers between devices: 4.95 us -> 8.78 us  [across(): return lax.ppermute(x, 'head', [(i, i ^ bit) for i in range(n_head)])]
  transfers between devices with their start and end apart: 19 -> 26, of which waited for: 9 -> 8; matrix products, arithmetic and copies ran while one was open for 35% -> 11% of each run, Pallas kernels for 0% -> 17%
where the time goes in v3:
time: 162 us; the launch traced here: 161 us
  waiting for transfers between devices  36.4 us (22%)
  starting transfers between devices  28.6 us (18%)
  Pallas kernels  27.8 us (17%)
  local copies, waits for them, and re-layouts  18.1 us (11%)
  blocking collectives  17.4 us (11%)
  between operations  15.1 us (9%)
  matrix products  13.2 us (8%)
  other arithmetic  4.05 us (2%)
    ppermute x8, waiting for transfers between devices, partner(): return lax.ppermute(x, 'ctx', [(i, i ^ 1) for i in range(n_ctx)])  17.8 us
    all_gather x1, blocking collectives, local(): every = lax.all_gather(both, 'ctx', axis_index_groups=lines)  17.4 us
    unnamed x55, local copies, waits for them, and re-layouts  14.8 us
    pallas_call x4, Pallas kernels, pieces(): pl.pallas_call(functools.partial(piece_kernel, count, dtype), grid=(steps...  14.6 us
    dot_general x8, matrix products, dot(): lax.dot_general(a, b, (((ca,), (cb,)), ((), ())), preferred_element_type=...  13.2 us
    ppermute x10, waiting for transfers between devices, across(): return lax.ppermute(x, 'head', [(i, i ^ bit) for i in range(n_head)])  11.4 us
    ppermute x6, starting transfers between devices, local(): moved = lax.ppermute(sums[i].astype(BF16), 'ctx', ring)  10.4 us
    ppermute x8, starting transfers between devices, partner(): return lax.ppermute(x, 'ctx', [(i, i ^ 1) for i in range(n_ctx)])  9.29 us
  transfers between devices with their start and end apart: 26, of which 8 were waited for; matrix products, arithmetic and copies ran while one was open for 11% of the time, Pallas kernels for 17%

profile of v3, /device:TPU:0, one launch (start us, length us, event | category | flops | bytes accessed | tf_op | source)
XLA Modules:
  0.0 160.6 jit_solution(4758765075850087603)
XLA Ops:
  7.2 1.9 %fusion.48 = (bf16[256,512]{1,0:T(8,128)(2,1)}, bf16[256,512]{1,0:T(8,128)(2,1)}) fusion(bf16[512,512]{1,0:T(8,128)(2,1)} %param.13), kind=kLoop, calls=%fused_computation.85 | loop fusion | bytes 1048576 | tf_op jit(solution)/shard_map/slice | solution.py:271
  11.4 2.5 %states.1 = (f32[2,2,128,128]{3,2,1,0:T(8,128)S(1)}, f32[2,2,128,128]{3,2,1,0:T(8,128)S(1)}, bf16[2,2,128,128]{3,2,1,0:T(8,128)(2,1)}) custom-call(s32[1]{0:T(128)} %bitcast.par_ref, bf16[512,512]{1,0:T(8,128)(2,1)S(1)} %copy-done.17, bf16[512,512]{1,0:T(8,128)(2,1)S(1)} %copy-done.6, bf16[512,512]{1,0:T(8,128)(2,1)S(1)} %copy-done.3, ...), custom_call_target="tpu_custom_call" | custom-call | flops 268435456 | bytes 2097152 | tf_op jit(solution)/shard_map/states/pallas_call | solution.py:49
  14.0 3.0 %collective-permute-start.14 = (bf16[1,512,512]{2,1,0:T(8,128)(2,1)S(1)}, bf16[1,512,512]{2,1,0:T(8,128)(2,1)S(1)}, u32[]{:S(2)}, u32[]{:S(2)}) collective-permute-start(bf16[1,512,512]{2,1,0:T(8,128)(2,1)S(1)} %get-tuple-element.27), channel_id=1, source_target_pairs={{0,4},{4,0},{8,12},{12,8},{16,20},{20,16},{24,28},{28,24},{1,5},{5... | collective-permute-start | bytes 1572872 | tf_op jit(solution)/shard_map/ppermute | solution.py:263
  17.1 2.0 %collective-permute-start.12 = (bf16[1,512,512]{2,1,0:T(8,128)(2,1)S(1)}, bf16[1,512,512]{2,1,0:T(8,128)(2,1)S(1)}, u32[]{:S(2)}, u32[]{:S(2)}) collective-permute-start(bf16[1,512,512]{2,1,0:T(8,128)(2,1)S(1)} %get-tuple-element.26.refs_0_), channel_id=1, source_target_pairs={{0,2},{1,3},{2,0},{3,1},{4,6},{5,7},{6,4},{7,5},{8,10},{9,11},{10,... | collective-permute-start | bytes 1572872 | tf_op jit(solution)/shard_map/ppermute | solution.py:266
  19.1 10.7 %collective-permute-done.14.refs_4_ = bf16[1,512,512]{2,1,0:T(8,128)(2,1)S(1)} collective-permute-done((bf16[1,512,512]{2,1,0:T(8,128)(2,1)S(1)}, bf16[1,512,512]{2,1,0:T(8,128)(2,1)S(1)}, u32[]{:S(2)}, u32[]{:S(2)}) %collective-permute-start.14) | collective-permute-done | bytes 524320 | tf_op jit(solution)/shard_map/ppermute | solution.py:263
  29.8 2.1 %collective-permute-start.16 = (bf16[1,512,512]{2,1,0:T(8,128)(2,1)S(1)}, bf16[1,512,512]{2,1,0:T(8,128)(2,1)S(1)}, u32[]{:S(2)}, u32[]{:S(2)}) collective-permute-start(bf16[1,512,512]{2,1,0:T(8,128)(2,1)S(1)} %collective-permute-done.14.refs_4_), channel_id=1, source_target_pairs={{0,2},{1,3},{2,0},{3,1},{4,6},{5,7},{6,4},{7,5},{8,10},{9,11},{10,... | collective-permute-start | bytes 1572872 | tf_op jit(solution)/shard_map/ppermute | solution.py:266
  34.6 17.4 %all-gather = bf16[8,2,128,128]{3,2,1,0:T(8,128)(2,1)S(1)} all-gather(bf16[2,2,128,128]{3,2,1,0:T(8,128)(2,1)S(1)} %add_convert_fusion), channel_id=2, replica_groups={{0,8,16,24},{4,12,20,28},{1,9,17,25},{5,13,21,29},{2,10,18,26},{6,14,22..., dimensions={0}, use_global_device_ids=true | all-gather | bytes 655360 | tf_op jit(solution)/shard_map/all_gather | solution.py:298
  61.3 4.4 %inside.1 = (f32[512,512]{1,0:T(8,128)S(1)}, f32[512,512]{1,0:T(8,128)S(1)}, f32[512,512]{1,0:T(8,128)S(1)}) custom-call(bf16[512,512]{1,0:T(8,128)(2,1)S(1)} %copy-done.18, bf16[512,512]{1,0:T(8,128)(2,1)S(1)} %copy-done.7, bf16[512,512]{1,0:T(8,128)(2,1)S(1)} %copy-done.4, bf16[512,512]{1,0:T(8,128)(2,1)S(1)} %copy-done.1, f32[2,2,128,128]{3,2,1,0:T(8,128)S(1)} %copy-done.20), custom_call_target="tpu_custom_call" | custom-call | flops 1342177280 | bytes 5242880 | tf_op jit(solution)/shard_map/inside/pallas_call | solution.py:110
  66.8 2.6 %finish_value.1 = (bf16[512,256]{1,0:T(8,128)(2,1)S(1)}, bf16[512,256]{1,0:T(8,128)(2,1)}) custom-call(s32[1]{0:T(128)} %bitcast.par_ref, bf16[512,512]{1,0:T(8,128)(2,1)S(1)} %copy-done.8, f32[512,512]{1,0:T(8,128)S(1)} %get-tuple-element.23.vi_ref, f32[2,2,128,128]{3,2,1,0:T(8,128)} %far.1, f32[2,2,128,128]{3,2,1,0:T(8,128)} %collective-permute-done.1.got_far, ...), custom_call_target="tpu_custom_call" | custom-call | flops 134217728 | bytes 2097152 | tf_op jit(solution)/shard_map/finish_value/pallas_call | solution.py:170
  77.4 2.8 %finish_others.1 = (bf16[512,512]{1,0:T(8,128)(2,1)}, bf16[512,512]{1,0:T(8,128)(2,1)}) custom-call(s32[1]{0:T(128)} %bitcast.par_ref, bf16[512,512]{1,0:T(8,128)(2,1)S(1)} %copy-done.2, bf16[512,512]{1,0:T(8,128)(2,1)S(1)} %copy-done.5, f32[512,512]{1,0:T(8,128)S(1)} %copy-done.11, f32[512,512]{1,0:T(8,128)S(1)} %copy-done.13, f32[2,2,128,128]{3,2,1,0:T(8,128)} %far.1, ...), custom_call_target="tpu_custom_call" | custom-call | flops 268435456 | bytes 4194304 | tf_op jit(solution)/shard_map/finish_others/pallas_call | solution.py:198
  80.2 2.4 %pieces.6 = bf16[1,512,256]{2,1,0:T(8,128)(2,1)} custom-call(s32[1]{0:T(128)S(1)} %bitcast.113, s32[1]{0:T(128)} %constant.79.clone.1.subs_ref, bf16[512,256]{1,0:T(8,128)(2,1)} %get-tuple-element.25.a_ref, bf16[512,256]{1,0:T(8,128)(2,1)} %collective-permute-done.4.b_ref, bf16[1,512,512]{2,1,0:T(8,128)(2,1)S(1)} %get-tuple-element.26.refs_0_, ...), custom_call_target="tpu_custom_call" | custom-call | flops 268435456 | bytes 1572864 | tf_op jit(solution)/shard_map/pieces/pallas_call | solution.py:233
  84.6 2.3 %pieces.4 = bf16[1,512,256]{2,1,0:T(8,128)(2,1)} custom-call(s32[1]{0:T(128)S(1)} %bitcast.114, s32[1]{0:T(128)} %constant.79.clone.1.subs_ref, bf16[512,256]{1,0:T(8,128)(2,1)S(1)} %copy-done.15, bf16[512,256]{1,0:T(8,128)(2,1)} %collective-permute-done.3.b_ref, bf16[1,512,512]{2,1,0:T(8,128)(2,1)S(1)} %get-tuple-element.26.refs_0_, ...), custom_call_target="tpu_custom_call" | custom-call | flops 268435456 | bytes 1572864 | tf_op jit(solution)/shard_map/pieces/pallas_call | solution.py:233
  87.7 5.0 %pieces.7 = f32[3,512,256]{2,1,0:T(8,128)} custom-call(s32[3]{0:T(128)S(1)} %slice.73.offs_ref, s32[3]{0:T(128)S(1)} %slice.74.subs_ref, bf16[512,256]{1,0:T(8,128)(2,1)} %get-tuple-element.25.a_ref, bf16[512,256]{1,0:T(8,128)(2,1)} %collective-permute-done.4.b_ref, bf16[1,512,512]{2,1,0:T(8,128)(2,1)S(1)} %get-tuple-element.26.refs_0_, ...), custom_call_target="tpu_custom_call" | custom-call | flops 805306368 | bytes 4718592 | tf_op jit(solution)/shard_map/pieces/pallas_call | solution.py:233
  92.7 4.9 %pieces.5 = f32[3,512,256]{2,1,0:T(8,128)} custom-call(s32[3]{0:T(128)S(1)} %slice.73.offs_ref, s32[3]{0:T(128)S(1)} %slice.74.subs_ref, bf16[512,256]{1,0:T(8,128)(2,1)S(1)} %copy-done.15, bf16[512,256]{1,0:T(8,128)(2,1)} %collective-permute-done.3.b_ref, bf16[1,512,512]{2,1,0:T(8,128)(2,1)S(1)} %get-tuple-element.26.refs_0_, ...), custom_call_target="tpu_custom_call" | custom-call | flops 805306368 | bytes 4718592 | tf_op jit(solution)/shard_map/pieces/pallas_call | solution.py:233
  97.7 1.8 %fusion.11 = bf16[1,1024,256]{1,2,0:T(8,128)(2,1)S(1)} fusion(bf16[4,256,512]{2,1,0:T(8,128)(2,1)} %bitcast.118, s32[]{:T(128)S(6)} %select_n.94, bf16[512,256]{1,0:T(8,128)(2,1)} %get-tuple-element.25.a_ref, bf16[512,256]{1,0:T(8,128)(2,1)} %copy-done.14, bf16[512,256]{1,0:T(8,128)(2,1)} %collective-permute-done.4.b_ref, ...), kind=kOutput, calls=%fused_computation.20 | convolution fusion | flops 272891904 | bytes 1835012 | tf_op jit(solution)/shard_map/dot_general | solution.py:20
  99.6 1.6 fusion.10
  101.8 1.7 %fusion.9 = bf16[1,1024,256]{1,2,0:T(8,128)(2,1)S(1)} fusion(bf16[4,256,512]{2,1,0:T(8,128)(2,1)} %bitcast.122, s32[]{:T(128)S(6)} %select_n.94, bf16[512,256]{1,0:T(8,128)(2,1)} %get-tuple-element.25.a_ref, bf16[512,256]{1,0:T(8,128)(2,1)S(1)} %copy-done.16, bf16[512,256]{1,0:T(8,128)(2,1)} %collective-permute-done.4.b_ref, ...), kind=kOutput, calls=%fused_computation.18 | convolution fusion | flops 272891904 | bytes 1835012 | tf_op jit(solution)/shard_map/dot_general | solution.py:20
  103.5 1.7 %fusion.8 = bf16[1,1024,256]{1,2,0:T(8,128)(2,1)S(1)} fusion(bf16[4,256,512]{2,1,0:T(8,128)(2,1)S(1)} %bitcast.123, s32[]{:T(128)S(6)} %select_n.93, bf16[512,256]{1,0:T(8,128)(2,1)} %get-tuple-element.25.a_ref, bf16[512,256]{1,0:T(8,128)(2,1)S(1)} %copy-done.16, bf16[512,256]{1,0:T(8,128)(2,1)} %collective-permute-done.4.b_ref, ...), kind=kOutput, calls=%fused_computation.17 | convolution fusion | flops 272891904 | bytes 1835012 | tf_op jit(solution)/shard_map/dot_general | solution.py:20
  106.4 2.1 %collective-permute-start.22 = (bf16[512,256]{1,0:T(8,128)(2,1)S(1)}, bf16[512,256]{1,0:T(8,128)(2,1)S(1)}, u32[]{:S(2)}, u32[]{:S(2)}) collective-permute-start(bf16[512,256]{1,0:T(8,128)(2,1)S(1)} %fusion.16), channel_id=1, source_target_pairs={{0,16},{4,20},{16,24},{20,28},{24,8},{28,12},{8,0},{12,4},{1,17},{... | collective-permute-start | bytes 786440 | tf_op jit(solution)/shard_map/ppermute | solution.py:325
  111.0 4.6 %collective-permute-done.22 = bf16[512,256]{1,0:T(8,128)(2,1)S(1)} collective-permute-done((bf16[512,256]{1,0:T(8,128)(2,1)S(1)}, bf16[512,256]{1,0:T(8,128)(2,1)S(1)}, u32[]{:S(2)}, u32[]{:S(2)}) %collective-permute-start.22) | collective-permute-done | bytes 262176 | tf_op jit(solution)/shard_map/ppermute | solution.py:325
  115.7 3.0 %collective-permute-start.23 = (bf16[512,256]{1,0:T(8,128)(2,1)S(1)}, bf16[512,256]{1,0:T(8,128)(2,1)S(1)}, u32[]{:S(2)}, u32[]{:S(2)}) collective-permute-start(bf16[512,256]{1,0:T(8,128)(2,1)S(1)} %fusion.14), channel_id=1, source_target_pairs={{0,16},{4,20},{16,24},{20,28},{24,8},{28,12},{8,0},{12,4},{1,17},{... | collective-permute-start | bytes 786440 | tf_op jit(solution)/shard_map/ppermute | solution.py:325
  118.7 1.6 fusion.6
  120.3 1.5 collective-permute-start.8
  121.9 2.4 %collective-permute-start.20 = (bf16[512,256]{1,0:T(8,128)(2,1)S(1)}, bf16[512,256]{1,0:T(8,128)(2,1)S(1)}, u32[]{:S(2)}, u32[]{:S(2)}) collective-permute-start(bf16[512,256]{1,0:T(8,128)(2,1)S(1)} %fusion.19), channel_id=1, source_target_pairs={{0,16},{4,20},{16,24},{20,28},{24,8},{28,12},{8,0},{12,4},{1,17},{... | collective-permute-start | bytes 786440 | tf_op jit(solution)/shard_map/ppermute | solution.py:325
  124.3 2.6 %collective-permute-done.23 = bf16[512,256]{1,0:T(8,128)(2,1)S(1)} collective-permute-done((bf16[512,256]{1,0:T(8,128)(2,1)S(1)}, bf16[512,256]{1,0:T(8,128)(2,1)S(1)}, u32[]{:S(2)}, u32[]{:S(2)}) %collective-permute-start.23) | collective-permute-done | bytes 262176 | tf_op jit(solution)/shard_map/ppermute | solution.py:325
  126.9 1.6 fusion.7
  128.5 2.0 %collective-permute-start.6 = (bf16[1,1024,256]{1,2,0:T(8,128)(2,1)S(1)}, bf16[1,1024,256]{1,2,0:T(8,128)(2,1)S(1)}, u32[]{:S(2)}, u32[]{:S(2)}) collective-permute-start(bf16[1,1024,256]{1,2,0:T(8,128)(2,1)S(1)} %fusion.7), channel_id=1, source_target_pairs={{0,2},{1,3},{2,0},{3,1},{4,6},{5,7},{6,4},{7,5},{8,10},{9,11},{10,... | collective-permute-start | bytes 1572872 | tf_op jit(solution)/shard_map/ppermute | solution.py:266
  130.5 4.7 %collective-permute-done.8 = bf16[1,1024,256]{1,2,0:T(8,128)(2,1)S(1)} collective-permute-done((bf16[1,1024,256]{1,2,0:T(8,128)(2,1)S(1)}, bf16[1,1024,256]{1,2,0:T(8,128)(2,1)S(1)}, u32[]{:S(2)}, u32[]{:S(2)}) %collective-permute-start.8) | collective-permute-done | bytes 524320 | tf_op jit(solution)/shard_map/ppermute | solution.py:266
  135.2 1.6 fusion.4
  137.4 6.7 %collective-permute-done.6 = bf16[1,1024,256]{1,2,0:T(8,128)(2,1)S(1)} collective-permute-done((bf16[1,1024,256]{1,2,0:T(8,128)(2,1)S(1)}, bf16[1,1024,256]{1,2,0:T(8,128)(2,1)S(1)}, u32[]{:S(2)}, u32[]{:S(2)}) %collective-permute-start.6) | collective-permute-done | bytes 524320 | tf_op jit(solution)/shard_map/ppermute | solution.py:266
  144.1 1.6 fusion.2
  147.5 4.7 %collective-permute-done.9 = bf16[512,256]{0,1:T(8,128)(2,1)S(1)} collective-permute-done((bf16[512,256]{0,1:T(8,128)(2,1)S(1)}, bf16[512,256]{0,1:T(8,128)(2,1)S(1)}, u32[]{:S(2)}, u32[]{:S(2)}) %collective-permute-start.9) | collective-permute-done | bytes 262176 | tf_op jit(solution)/shard_map/ppermute | solution.py:263
  (118 shorter events, 34.1 us)
Async XLA Ops:
  7.2 90.5 %all-gather.8.cloned.1.call-start = ((), (), s32[]{:S(2)}) async-start(), calls=%async_computation.1 | async-start | bytes 1310720 | tf_op jit(solution)/shard_map/all_gather | solution.py:270
  9.2 92.6 %all-gather.6.cloned.1.call-start = ((), (), s32[]{:S(2)}) async-start(), calls=%async_computation | async-start | bytes 1310720 | tf_op jit(solution)/shard_map/all_gather | solution.py:270
  13.9 38.9 %copy-start.19 = (f32[2,2,128,128]{3,2,1,0:T(8,128)}, f32[2,2,128,128]{3,2,1,0:T(8,128)S(1)}, u32[]{:S(2)}) copy-start(f32[2,2,128,128]{3,2,1,0:T(8,128)S(1)} %get-tuple-element.16._) | copy-start | bytes 786436
  13.9 40.4 %copy-start.26 = (s32[4]{0:T(128)S(1)}, s32[4]{0:T(128)}, u32[]{:S(2)}) copy-start(s32[4]{0:T(128)} %constant.81.clone) | copy-start | bytes 52
  14.0 15.8 %collective-permute-start.14 = (bf16[1,512,512]{2,1,0:T(8,128)(2,1)S(1)}, bf16[1,512,512]{2,1,0:T(8,128)(2,1)S(1)}, u32[]{:S(2)}, u32[]{:S(2)}) collective-permute-start(bf16[1,512,512]{2,1,0:T(8,128)(2,1)S(1)} %get-tuple-element.27), channel_id=1, source_target_pairs={{0,4},{4,0},{8,12},{12,8},{16,20},{20,16},{24,28},{28,24},{1,5},{5... | collective-permute-start | bytes 1572872 | tf_op jit(solution)/shard_map/ppermute | solution.py:263
  17.0 17.5 %collective-permute-start = (f32[2,2,128,128]{3,2,1,0:T(8,128)S(1)}, f32[2,2,128,128]{3,2,1,0:T(8,128)S(1)}, u32[]{:S(2)}, u32[]{:S(2)}) collective-permute-start(f32[2,2,128,128]{3,2,1,0:T(8,128)S(1)} %get-tuple-element.16._), channel_id=1, source_target_pairs={{0,4},{4,0},{8,12},{12,8},{16,20},{20,16},{24,28},{28,24},{1,5},{5... | collective-permute-start | bytes 786440 | tf_op jit(solution)/shard_map/ppermute | solution.py:263
  17.1 38.5 %collective-permute-start.12 = (bf16[1,512,512]{2,1,0:T(8,128)(2,1)S(1)}, bf16[1,512,512]{2,1,0:T(8,128)(2,1)S(1)}, u32[]{:S(2)}, u32[]{:S(2)}) collective-permute-start(bf16[1,512,512]{2,1,0:T(8,128)(2,1)S(1)} %get-tuple-element.26.refs_0_), channel_id=1, source_target_pairs={{0,2},{1,3},{2,0},{3,1},{4,6},{5,7},{6,4},{7,5},{8,10},{9,11},{10,... | collective-permute-start | bytes 1572872 | tf_op jit(solution)/shard_map/ppermute | solution.py:266
  29.8 26.3 %collective-permute-start.16 = (bf16[1,512,512]{2,1,0:T(8,128)(2,1)S(1)}, bf16[1,512,512]{2,1,0:T(8,128)(2,1)S(1)}, u32[]{:S(2)}, u32[]{:S(2)}) collective-permute-start(bf16[1,512,512]{2,1,0:T(8,128)(2,1)S(1)} %collective-permute-done.14.refs_4_), channel_id=1, source_target_pairs={{0,2},{1,3},{2,0},{3,1},{4,6},{5,7},{6,4},{7,5},{8,10},{9,11},{10,... | collective-permute-start | bytes 1572872 | tf_op jit(solution)/shard_map/ppermute | solution.py:266
  31.9 39.4 %collective-permute-start.11 = (bf16[1,512,512]{2,1,0:T(8,128)(2,1)S(1)}, bf16[1,512,512]{2,1,0:T(8,128)(2,1)S(1)}, u32[]{:S(2)}, u32[]{:S(2)}) collective-permute-start(bf16[1,512,512]{2,1,0:T(8,128)(2,1)S(1)} %get-tuple-element.26.refs_0_), channel_id=1, source_target_pairs={{0,1},{1,0},{2,3},{3,2},{4,5},{5,4},{6,7},{7,6},{8,9},{9,8},{10,11... | collective-permute-start | bytes 1572872 | tf_op jit(solution)/shard_map/ppermute | solution.py:266
  31.9 23.7 %collective-permute-start.2 = (bf16[2,2,128,128]{3,2,1,0:T(8,128)(2,1)}, bf16[2,2,128,128]{3,2,1,0:T(8,128)(2,1)S(1)}, u32[]{:S(2)}, u32[]{:S(2)}) collective-permute-start(bf16[2,2,128,128]{3,2,1,0:T(8,128)(2,1)} %get-tuple-element.20), channel_id=1, source_target_pairs={{0,4},{4,0},{8,12},{12,8},{16,20},{20,16},{24,28},{28,24},{1,5},{5... | collective-permute-start | bytes 393224 | tf_op jit(solution)/shard_map/ppermute | solution.py:263
  52.8 14.0 %collective-permute-start.1 = (f32[2,2,128,128]{3,2,1,0:T(8,128)}, f32[2,2,128,128]{3,2,1,0:T(8,128)}, u32[]{:S(2)}, u32[]{:S(2)}) collective-permute-start(f32[2,2,128,128]{3,2,1,0:T(8,128)} %far.1), channel_id=1, source_target_pairs={{0,4},{4,0},{8,12},{12,8},{16,20},{20,16},{24,28},{28,24},{1,5},{5... | collective-permute-start | bytes 786440 | tf_op jit(solution)/shard_map/ppermute | solution.py:263
  55.5 24.6 %collective-permute-start.15 = (bf16[1,512,512]{2,1,0:T(8,128)(2,1)S(1)}, bf16[1,512,512]{2,1,0:T(8,128)(2,1)S(1)}, u32[]{:S(2)}, u32[]{:S(2)}) collective-permute-start(bf16[1,512,512]{2,1,0:T(8,128)(2,1)S(1)} %collective-permute-done.14.refs_4_), channel_id=1, source_target_pairs={{0,1},{1,0},{2,3},{3,2},{4,5},{5,4},{6,7},{7,6},{8,9},{9,8},{10,11... | collective-permute-start | bytes 1572872 | tf_op jit(solution)/shard_map/ppermute | solution.py:266
  55.6 24.6 %collective-permute-start.13 = (bf16[1,512,512]{2,1,0:T(8,128)(2,1)S(1)}, bf16[1,512,512]{2,1,0:T(8,128)(2,1)}, u32[]{:S(2)}, u32[]{:S(2)}) collective-permute-start(bf16[1,512,512]{2,1,0:T(8,128)(2,1)S(1)} %collective-permute-done.12.refs_2_), channel_id=1, source_target_pairs={{0,1},{1,0},{2,3},{3,2},{4,5},{5,4},{6,7},{7,6},{8,9},{9,8},{10,11... | collective-permute-start | bytes 1572872 | tf_op jit(solution)/shard_map/ppermute | solution.py:266
  56.1 24.1 %collective-permute-start.17 = (bf16[1,512,512]{2,1,0:T(8,128)(2,1)S(1)}, bf16[1,512,512]{2,1,0:T(8,128)(2,1)}, u32[]{:S(2)}, u32[]{:S(2)}) collective-permute-start(bf16[1,512,512]{2,1,0:T(8,128)(2,1)S(1)} %collective-permute-done.16.refs_6_), channel_id=1, source_target_pairs={{0,1},{1,0},{2,3},{3,2},{4,5},{5,4},{6,7},{7,6},{8,9},{9,8},{10,11... | collective-permute-start | bytes 1572872 | tf_op jit(solution)/shard_map/ppermute | solution.py:266
  61.3 5.4 %copy-start.8 = (bf16[512,512]{1,0:T(8,128)(2,1)S(1)}, bf16[512,512]{1,0:T(8,128)(2,1)}, u32[]{:S(2)}) copy-start(bf16[512,512]{1,0:T(8,128)(2,1)} %k_ref.5) | copy-start | bytes 1572868
  66.8 3.8 %copy-start.21 = (s32[4]{0:T(128)S(1)}, s32[4]{0:T(128)}, u32[]{:S(2)}) copy-start(s32[4]{0:T(128)} %constant.82.clone) | copy-start | bytes 52
  70.0 10.1 %collective-permute-start.4 = (bf16[512,256]{1,0:T(8,128)(2,1)}, bf16[512,256]{1,0:T(8,128)(2,1)}, u32[]{:S(2)}, u32[]{:S(2)}) collective-permute-start(bf16[512,256]{1,0:T(8,128)(2,1)} %get-tuple-element.25.a_ref), channel_id=1, source_target_pairs={{0,4},{4,0},{8,12},{12,8},{16,20},{20,16},{24,28},{28,24},{1,5},{5... | collective-permute-start | bytes 786440 | tf_op jit(solution)/shard_map/ppermute | solution.py:263
  71.3 13.4 %collective-permute-start.3 = (bf16[512,256]{1,0:T(8,128)(2,1)}, bf16[512,256]{1,0:T(8,128)(2,1)}, u32[]{:S(2)}, u32[]{:S(2)}) collective-permute-start(bf16[512,256]{1,0:T(8,128)(2,1)} %copy-done.14), channel_id=1, source_target_pairs={{0,4},{4,0},{8,12},{12,8},{16,20},{20,16},{24,28},{28,24},{1,5},{5... | collective-permute-start | bytes 786440 | tf_op jit(solution)/shard_map/ppermute | solution.py:263
  80.2 4.5 %copy-start.15 = (bf16[512,256]{1,0:T(8,128)(2,1)S(1)}, bf16[512,256]{1,0:T(8,128)(2,1)}, u32[]{:S(2)}) copy-start(bf16[512,256]{1,0:T(8,128)(2,1)} %copy-done.14) | copy-start | bytes 786436
  82.6 22.7 %collective-permute-start.21 = (bf16[512,256]{1,0:T(8,128)(2,1)}, bf16[512,256]{1,0:T(8,128)(2,1)}, u32[]{:S(2)}, u32[]{:S(2)}) collective-permute-start(bf16[512,256]{1,0:T(8,128)(2,1)} %bitcast.36), channel_id=1, source_target_pairs={{0,16},{4,20},{16,24},{20,28},{24,8},{28,12},{8,0},{12,4},{1,17},{... | collective-permute-start | bytes 786440 | tf_op jit(solution)/shard_map/ppermute | solution.py:325
  86.9 21.8 %collective-permute-start.18 = (bf16[512,256]{1,0:T(8,128)(2,1)}, bf16[512,256]{1,0:T(8,128)(2,1)}, u32[]{:S(2)}, u32[]{:S(2)}) collective-permute-start(bf16[512,256]{1,0:T(8,128)(2,1)} %bitcast.32), channel_id=1, source_target_pairs={{0,16},{4,20},{16,24},{20,28},{24,8},{28,12},{8,0},{12,4},{1,17},{... | collective-permute-start | bytes 786440 | tf_op jit(solution)/shard_map/ppermute | solution.py:325
  101.3 17.4 %collective-permute-start.7 = (bf16[2,1024,256]{1,2,0:T(8,128)(2,1)S(1)}, bf16[2,1024,256]{1,2,0:T(8,128)(2,1)S(1)}, u32[]{:S(2)}, u32[]{:S(2)}) collective-permute-start(bf16[2,1024,256]{1,2,0:T(8,128)(2,1)S(1)} %pad_maximum_fusion.1), channel_id=1, source_target_pairs={{0,1},{1,0},{2,3},{3,2},{4,5},{5,4},{6,7},{7,6},{8,9},{9,8},{10,11... | collective-permute-start | bytes 3145736 | tf_op jit(solution)/shard_map/ppermute | solution.py:266
  105.2 3.5 %copy-start.22 = (f32[3,512,256]{2,1,0:T(8,128)S(1)}, f32[3,512,256]{2,1,0:T(8,128)}, u32[]{:S(2)}) copy-start(f32[3,512,256]{2,1,0:T(8,128)} %pieces.5) | copy-start | bytes 4718596
  106.4 9.2 %collective-permute-start.22 = (bf16[512,256]{1,0:T(8,128)(2,1)S(1)}, bf16[512,256]{1,0:T(8,128)(2,1)S(1)}, u32[]{:S(2)}, u32[]{:S(2)}) collective-permute-start(bf16[512,256]{1,0:T(8,128)(2,1)S(1)} %fusion.16), channel_id=1, source_target_pairs={{0,16},{4,20},{16,24},{20,28},{24,8},{28,12},{8,0},{12,4},{1,17},{... | collective-permute-start | bytes 786440 | tf_op jit(solution)/shard_map/ppermute | solution.py:325
  108.6 18.3 %collective-permute-start.5 = (bf16[2,1024,256]{1,2,0:T(8,128)(2,1)S(1)}, bf16[2,1024,256]{1,2,0:T(8,128)(2,1)S(1)}, u32[]{:S(2)}, u32[]{:S(2)}) collective-permute-start(bf16[2,1024,256]{1,2,0:T(8,128)(2,1)S(1)} %pad_maximum_fusion), channel_id=1, source_target_pairs={{0,1},{1,0},{2,3},{3,2},{4,5},{5,4},{6,7},{7,6},{8,9},{9,8},{10,11... | collective-permute-start | bytes 3145736 | tf_op jit(solution)/shard_map/ppermute | solution.py:266
  109.7 12.1 %collective-permute-start.19 = (bf16[512,256]{1,0:T(8,128)(2,1)S(1)}, bf16[512,256]{1,0:T(8,128)(2,1)S(1)}, u32[]{:S(2)}, u32[]{:S(2)}) collective-permute-start(bf16[512,256]{1,0:T(8,128)(2,1)S(1)} %fusion.21), channel_id=1, source_target_pairs={{0,16},{4,20},{16,24},{20,28},{24,8},{28,12},{8,0},{12,4},{1,17},{... | collective-permute-start | bytes 786440 | tf_op jit(solution)/shard_map/ppermute | solution.py:325
  115.7 11.2 %collective-permute-start.23 = (bf16[512,256]{1,0:T(8,128)(2,1)S(1)}, bf16[512,256]{1,0:T(8,128)(2,1)S(1)}, u32[]{:S(2)}, u32[]{:S(2)}) collective-permute-start(bf16[512,256]{1,0:T(8,128)(2,1)S(1)} %fusion.14), channel_id=1, source_target_pairs={{0,16},{4,20},{16,24},{20,28},{24,8},{28,12},{8,0},{12,4},{1,17},{... | collective-permute-start | bytes 786440 | tf_op jit(solution)/shard_map/ppermute | solution.py:325
  120.3 14.9 %collective-permute-start.8 = (bf16[1,1024,256]{1,2,0:T(8,128)(2,1)S(1)}, bf16[1,1024,256]{1,2,0:T(8,128)(2,1)S(1)}, u32[]{:S(2)}, u32[]{:S(2)}) collective-permute-start(bf16[1,1024,256]{1,2,0:T(8,128)(2,1)S(1)} %fusion.6), channel_id=1, source_target_pairs={{0,2},{1,3},{2,0},{3,1},{4,6},{5,7},{6,4},{7,5},{8,10},{9,11},{10,... | collective-permute-start | bytes 1572872 | tf_op jit(solution)/shard_map/ppermute | solution.py:266
  121.9 24.5 %collective-permute-start.20 = (bf16[512,256]{1,0:T(8,128)(2,1)S(1)}, bf16[512,256]{1,0:T(8,128)(2,1)S(1)}, u32[]{:S(2)}, u32[]{:S(2)}) collective-permute-start(bf16[512,256]{1,0:T(8,128)(2,1)S(1)} %fusion.19), channel_id=1, source_target_pairs={{0,16},{4,20},{16,24},{20,28},{24,8},{28,12},{8,0},{12,4},{1,17},{... | collective-permute-start | bytes 786440 | tf_op jit(solution)/shard_map/ppermute | solution.py:325
  128.5 15.6 %collective-permute-start.6 = (bf16[1,1024,256]{1,2,0:T(8,128)(2,1)S(1)}, bf16[1,1024,256]{1,2,0:T(8,128)(2,1)S(1)}, u32[]{:S(2)}, u32[]{:S(2)}) collective-permute-start(bf16[1,1024,256]{1,2,0:T(8,128)(2,1)S(1)} %fusion.7), channel_id=1, source_target_pairs={{0,2},{1,3},{2,0},{3,1},{4,6},{5,7},{6,4},{7,5},{8,10},{9,11},{10,... | collective-permute-start | bytes 1572872 | tf_op jit(solution)/shard_map/ppermute | solution.py:266
  136.8 10.7 %collective-permute-start.10 = (bf16[512,256]{0,1:T(8,128)(2,1)S(1)}, bf16[512,256]{0,1:T(8,128)(2,1)S(1)}, u32[]{:S(2)}, u32[]{:S(2)}) collective-permute-start(bf16[512,256]{0,1:T(8,128)(2,1)S(1)} %get-tuple-element.45), channel_id=1, source_target_pairs={{0,4},{4,0},{8,12},{12,8},{16,20},{20,16},{24,28},{28,24},{1,5},{5... | collective-permute-start | bytes 786440 | tf_op jit(solution)/shard_map/ppermute | solution.py:263
  145.7 6.4 %collective-permute-start.9 = (bf16[512,256]{0,1:T(8,128)(2,1)S(1)}, bf16[512,256]{0,1:T(8,128)(2,1)S(1)}, u32[]{:S(2)}, u32[]{:S(2)}) collective-permute-start(bf16[512,256]{0,1:T(8,128)(2,1)S(1)} %get-tuple-element.43), channel_id=1, source_target_pairs={{0,4},{4,0},{8,12},{12,8},{16,20},{20,16},{24,28},{28,24},{1,5},{5... | collective-permute-start | bytes 786440 | tf_op jit(solution)/shard_map/ppermute | solution.py:263
  (21 other events, 29.9 us)
Sparse Core Ops, SparseCore 0:
  9.6 31.6 all-gather.7
  42.9 27.7 all-gather.5

commit v4 on v3

v4 whole, which is shorter than its diff:
```python
import functools
import math

import jax
import jax.numpy as jnp
from jax import lax
from jax.experimental import pallas as pl
from jax.experimental.pallas import tpu as pltpu
from jax.sharding import PartitionSpec as P

DH = 128
F32, BF16 = jnp.float32, jnp.bfloat16
VMEM = pl.BlockSpec(memory_space=pltpu.VMEM)
SMEM = pl.BlockSpec(memory_space=pltpu.SMEM)
ANY = pl.BlockSpec(memory_space=pl.ANY)


def dot(a, b, ca, cb):
    return lax.dot_general(a, b, (((ca,), (cb,)), ((), ())), preferred_element_type=F32)


def cost(flops, moved):
    return pl.CostEstimate(flops=flops, bytes_accessed=moved, transcendentals=0)


def states_kernel(a_ref, b_ref, out_ref):
    for hd in range(a_ref.shape[1] // DH):
        at = slice(hd * DH, (hd + 1) * DH)
        out_ref[hd] = dot(a_ref[:, at], b_ref[:, at], 0, 0).astype(BF16)


def states(a, b):
    heads = a.shape[1] // DH
    return pl.pallas_call(
        states_kernel,
        in_specs=[VMEM] * 2,
        out_specs=VMEM,
        out_shape=jax.ShapeDtypeStruct((heads, DH, DH), BF16),
        cost_estimate=cost(2 * a.size * DH, 4 * a.size),
        name="states",
    )(a, b)


def split_kernel(per, par_ref, x_ref, own_ref, theirs_ref):
    width = x_ref.shape[1] // (2 * per)
    for k in range(2):
        for i in range(per):
            block = x_ref[:, (2 * i + k) * width : (2 * i + k + 1) * width]

            @pl.when(par_ref[0] == k)
            def _():
                own_ref[i] = block

            @pl.when(par_ref[0] != k)
            def _():
                theirs_ref[i] = block


def split(par, x, per):
    width = x.shape[1] // (2 * per)
    out = jax.ShapeDtypeStruct((per, x.shape[0], width), x.dtype)
    return pl.pallas_call(
        functools.partial(split_kernel, per),
        in_specs=[SMEM, VMEM],
        out_specs=[VMEM] * 2,
        out_shape=[out, out],
        cost_estimate=cost(0, x.size * 4),
        name="split",
    )(par, x)


def inside_kernel(q_ref, k_ref, v_ref, g_ref, vo_ref, qo_ref, ko_ref):
    q, k, v, g = q_ref[...], k_ref[...], v_ref[...], g_ref[...]
    n = q.shape[0]
    rows = lax.broadcasted_iota(jnp.int32, (n, n), 0)
    cols = lax.broadcasted_iota(jnp.int32, (n, n), 1)
    causal = rows >= cols
    ks = jnp.where(causal, dot(q, k, 1, 1), 0.0).astype(BF16)
    vo_ref[...] = dot(ks, g, 0, 0)
    gs = jnp.where(causal, dot(g, v, 1, 1), 0.0).astype(BF16)
    qo_ref[...] = dot(gs, k, 1, 0)
    ko_ref[...] = dot(gs, q, 0, 0)


def inside(q, k, v, g):
    n, cols = q.shape
    spec = pl.BlockSpec((n, DH), lambda h: (0, h))
    out = jax.ShapeDtypeStruct((n, cols), F32)
    return pl.pallas_call(
        inside_kernel,
        grid=(cols // DH,),
        in_specs=[spec] * 4,
        out_specs=[spec] * 3,
        out_shape=[out] * 3,
        cost_estimate=cost(10 * n * n * cols, 20 * n * cols),
        name="inside",
    )(q, k, v, g)


def far_kernel(count_ref, *refs):
    got, (out_ref, send_ref) = refs[:-2], refs[-2:]
    total = jnp.zeros(out_ref.shape, F32)
    for i, x in enumerate(got):
        total = total + jnp.where(i < count_ref[0], x[...].astype(F32), 0.0)
    out_ref[...] = total
    send_ref[...] = total.astype(BF16)


def far_states(count, got):
    shape = got[0].shape
    return pl.pallas_call(
        far_kernel,
        in_specs=[SMEM] + [VMEM] * len(got),
        out_specs=[VMEM] * 2,
        out_shape=[
            jax.ShapeDtypeStruct(shape, F32),
            jax.ShapeDtypeStruct(shape, BF16),
        ],
        cost_estimate=cost(0, got[0].size * (2 * len(got) + 6)),
        name="far",
    )(count, *got)


def entering(par, kind, hd, far, got_far, near):
    close = jnp.where(par == kind, near[hd].astype(F32), 0.0)
    total = far[hd] + got_far[hd].astype(F32) + close
    hi = total.astype(BF16)
    return hi, (total - hi.astype(F32)).astype(BF16)


def value_kernel(factor, par_ref, k_ref, vi_ref, far, got_far, near, *outs):
    heads = k_ref.shape[1] // DH
    span = outs[0].shape[1] // DH
    for hd in range(heads):
        at = slice(hd * DH, (hd + 1) * DH)
        hi, lo = entering(par_ref[0], 0, hd, far, got_far, near)
        k = k_ref[:, at]
        total = vi_ref[:, at] + (dot(k, hi, 1, 0) + dot(k, lo, 1, 0))
        to = (hd % span) * DH
        outs[hd // span][:, to : to + DH] = (factor * total).astype(BF16)


def finish_value(factor, par, k, vi, later, chains):
    n, cols = k.shape
    out = jax.ShapeDtypeStruct((n, cols // chains), BF16)
    return pl.pallas_call(
        functools.partial(value_kernel, factor),
        in_specs=[SMEM] + [VMEM] * 5,
        out_specs=[VMEM] * chains,
        out_shape=[out] * chains,
        cost_estimate=cost(4 * n * cols * DH, 8 * n * cols),
        name="finish_value",
    )(par, k, vi, *later)


def others_kernel(factor, par_ref, g_ref, v_ref, qi_ref, ki_ref, *refs):
    heads = g_ref.shape[1] // DH
    later, prior, outs = refs[:3], refs[3:6], refs[6:]
    for hd in range(heads):
        at = slice(hd * DH, (hd + 1) * DH)
        for kind, x_ref, i_ref, ends in (
            (1, g_ref, qi_ref, prior),
            (0, v_ref, ki_ref, later),
        ):
            hi, lo = entering(par_ref[0], kind, hd, *ends)
            x = x_ref[:, at]
            total = i_ref[:, at] + (dot(x, hi, 1, 1) + dot(x, lo, 1, 1))
            outs[1 - kind][:, at] = (factor * total).astype(BF16)


def finish_others(factor, par, g, v, qi, ki, later, prior):
    out = jax.ShapeDtypeStruct(g.shape, BF16)
    return pl.pallas_call(
        functools.partial(others_kernel, factor),
        in_specs=[SMEM] + [VMEM] * 10,
        out_specs=[VMEM] * 2,
        out_shape=[out] * 2,
        cost_estimate=cost(8 * g.size * DH, 16 * g.size),
        name="finish_others",
    )(par, g, v, qi, ki, *later, *prior)


def piece_kernel(count, offs_ref, subs_ref, a_ref, b_ref, *refs):
    own, theirs = refs[:count], refs[count : 2 * count]
    out_ref, x, y, at, bt, sems = refs[2 * count :]
    step = pl.program_id(0)
    for i in range(count):

        @pl.when(offs_ref[step] == i)
        def _():
            pltpu.make_async_copy(own[i].at[subs_ref[step]], x, sems.at[0]).start()
            pltpu.make_async_copy(theirs[i].at[subs_ref[step]], y, sems.at[1]).start()

    @pl.when(step == 0)
    def _():
        at[...] = a_ref[...].T
        bt[...] = b_ref[...].T

    pltpu.make_async_copy(own[0].at[0], x, sems.at[0]).wait()
    pltpu.make_async_copy(theirs[0].at[0], y, sems.at[1]).wait()
    total = dot(at[...], x[...], 1, 0) + dot(bt[...], y[...], 1, 0)
    out_ref[0] = total.astype(out_ref.dtype)


def pieces(dtype, offs, subs, a, b, own, theirs):
    steps = offs.shape[0]
    count = len(own)
    _, n, width = own[0].shape
    span = a.shape[1]
    return pl.pallas_call(
        functools.partial(piece_kernel, count),
        grid=(steps,),
        in_specs=[SMEM] * 2 + [VMEM] * 2 + [ANY] * (2 * count),
        out_specs=pl.BlockSpec((1, span, width), lambda s: (s, 0, 0)),
        out_shape=jax.ShapeDtypeStruct((steps, span, width), dtype),
        scratch_shapes=[
            pltpu.VMEM((n, width), BF16),
            pltpu.VMEM((n, width), BF16),
            pltpu.VMEM((span, n), BF16),
            pltpu.VMEM((span, n), BF16),
            pltpu.SemaphoreType.DMA((2,)),
        ],
        cost_estimate=cost(4 * n * width * span * steps, 4 * n * (width + span) * steps),
        name="pieces",
    )(offs, subs, a, b, *own, *theirs)


def weight_kernel(scale, *refs):
    chains = (len(refs) - 1) // 2
    out_ref = refs[-1]
    for i in range(chains):
        total = refs[i][...].astype(F32) + refs[chains + i][...]
        span = total.shape[0]
        out_ref[:, i * span : (i + 1) * span] = total.T * scale


def finish_weight(scale, moved, rest):
    span, width = moved[0].shape
    count = len(moved)
    return pl.pallas_call(
        functools.partial(weight_kernel, scale),
        in_specs=[VMEM] * (2 * count),
        out_specs=VMEM,
        out_shape=jax.ShapeDtypeStruct((width, count * span), F32),
        cost_estimate=cost(0, 10 * count * span * width),
        name="finish_weight",
    )(*moved, *rest)


def inputs_kernel(offs, per, chains, got, head_ref, w_ref, *refs):
    vals, refs = refs[: 2 * chains], refs[2 * chains :]
    got_ref, outs = (refs[0], refs[1:]) if got else (None, refs)
    n, span = vals[0].shape
    rows, cols = w_ref.shape[1:]
    for at, off in enumerate(offs):
        first = (head_ref[0] ^ off) * per
        w = w_ref[pl.ds(first, per)].reshape(per * rows, cols)
        for side in range(2):
            total = 0.0
            for c in range(chains):
                part = w[:, c * span : (c + 1) * span]
                total = total + dot(vals[side * chains + c][...], part, 1, 1)
            to = slice(side * n, (side + 1) * n)
            if got:
                total = total + got_ref[at, to].astype(F32)
            outs[at][to] = total.astype(outs[at].dtype)


def inputs_part(offs, dtypes, per, head, w, theirs, mine, got=None):
    chains = len(mine)
    n = mine[0].shape[0]
    block = per * w.shape[1]
    extra = [] if got is None else [got]
    return pl.pallas_call(
        functools.partial(inputs_kernel, offs, per, chains, got is not None),
        in_specs=[SMEM] + [VMEM] * (1 + 2 * chains + len(extra)),
        out_specs=[VMEM] * len(offs),
        out_shape=[jax.ShapeDtypeStruct((2 * n, block), d) for d in dtypes],
        cost_estimate=cost(4 * n * block * w.shape[2] * len(offs), 8 * w.size),
        name="inputs_part",
    )(head, w, *theirs, *mine, *extra)


def after(x, *earlier):
    return lax.optimization_barrier((x, *earlier))[0]


def local(queries, keys, values, out_grad, inputs, value_weight):
    length, cols = queries.shape
    n_ctx, n_head = lax.axis_size("ctx"), lax.axis_size("head")
    pairs = n_ctx // 2
    ctx, head = lax.axis_index("ctx"), lax.axis_index("head")
    parity, pair = ctx % 2, ctx // 2
    par = parity.astype(jnp.int32).reshape(1)
    factor = 1.0 / math.sqrt(DH * length * n_ctx)
    lines = [[2 * i + k for i in range(pairs)] for k in range(2)]
    chains = 2
    span = cols // chains

    def partner(x):
        return lax.ppermute(x, "ctx", [(i, i ^ 1) for i in range(n_ctx)])

    def across(x, bit):
        return lax.ppermute(x, "head", [(i, i ^ bit) for i in range(n_head)])

    part_rows = value_weight.shape[0] // 2
    weights = [
        lax.all_gather(
            value_weight[i * part_rows : (i + 1) * part_rows],
            "ctx",
            axis_index_groups=lines,
        )
        for i in range(2)
    ]

    per = n_ctx // n_head // 2
    own, theirs = split(par, inputs, per)

    def line_move(x, by):
        moves = [
            (i, i + 2 * by) for i in range(n_ctx) if 0 <= i + 2 * by < n_ctx
        ]
        return lax.ppermute(x, "ctx", moves)

    def far_of(x, sign):
        got = [line_move(x, sign * d) for d in range(1, pairs)]
        count = pairs - 1 - pair if sign < 0 else pair
        return far_states(count.astype(jnp.int32).reshape(1), got)

    qg = states(queries, out_grad)
    far_qg, send_qg = far_of(qg, -1)
    kv = states(keys, values)
    near = partner(jnp.stack([qg, kv]))
    theirs = partner(theirs)
    later = (far_qg, partner(send_qg), near[0])

    own, theirs = [own], [theirs]
    offsets = [0]
    bit = n_head // 2
    while bit:
        own = own + [across(r, bit) for r in own]
        theirs = theirs + [across(r, bit) for r in theirs]
        offsets = offsets + [o ^ bit for o in offsets]
        bit //= 2
    own = [own[offsets.index(i)] for i in range(n_head)]
    theirs = [theirs[offsets.index(i)] for i in range(n_head)]

    vi, qi, ki = inside(queries, keys, values, out_grad)
    mine = finish_value(factor, par, keys, vi, later, chains)
    other = []
    for x in mine:
        other.append(partner(after(x, *other)))
    far_kv, send_kv = far_of(after(kv, far_qg), 1)
    prior = (far_kv, partner(after(send_kv, *other)), near[1])

    order = list(range(0, pairs, 2)) + list(range(1, pairs, 2))[::-1]
    place = [order.index(i) for i in range(pairs)]
    ring = [
        (2 * order[i] + k, 2 * order[(i + 1) % pairs] + k)
        for i in range(pairs)
        for k in range(2)
    ]
    spot = jnp.asarray(place, jnp.int32)[pair]
    which = jnp.asarray(order, jnp.int32)[
        (spot - 1 - jnp.arange(pairs, dtype=jnp.int32)) % pairs
    ]
    offs, subs = (which // per) ^ head, which % per

    sums = []
    for a, b in zip(mine, other):
        sums.append(pieces(BF16, offs[:1], subs[:1], a, b, own, theirs)[0])
    token = sums[-1]
    rest = []
    for a, b in zip(mine, other):
        rest.append(
            pieces(F32, offs[1:], subs[1:], after(a, token), b, own, theirs)
        )
        token = rest[-1]

    hd = head.astype(jnp.int32).reshape(1)
    odd = [o for o in range(n_head) if o & 1]
    even = [o for o in range(n_head) if not o & 1]
    state = [{} for _ in weights]

    def first_part(i, token):
        vals = (after(other[0], token), *other[1:])
        out = inputs_part(odd, [BF16] * len(odd), per, hd, weights[i], vals, mine)
        state[i]["got"] = across(jnp.stack(out), 1)
        return out[0]

    def second_part(i, token):
        vals = (after(other[0], token), *other[1:])
        kinds = [BF16 if o & 2 else F32 for o in even]
        out = inputs_part(
            even, kinds, per, hd, weights[i], vals, mine, state[i]["got"]
        )
        state[i]["found"] = found = dict(zip(even, out))
        if n_head > 2:
            gone = [o for o in even if o & 2]
            state[i]["got"] = across(jnp.stack([found.pop(o) for o in gone]), 2)
        return out[0]

    def third_part(i, token):
        found, bit = state[i]["found"], 2
        while bit < n_head:
            for j, o in enumerate(sorted(found)):
                moved = after(state[i]["got"][j], token).astype(F32)
                found[o] = found[o] + moved
            bit *= 2
            if bit < n_head:
                gone = [o for o in sorted(found) if o & bit]
                moved = jnp.stack([found.pop(o).astype(BF16) for o in gone])
                state[i]["got"] = across(moved, bit)
        total = found[0].astype(BF16)
        state[i]["mine"] = total[length:]
        state[i]["other"] = partner(total[:length])
        return total

    moved = [None] * chains

    def ring_step(step, i, token):
        moved[i] = lax.ppermute(sums[i], "ctx", ring)
        if step < pairs - 1:
            local_part = after(rest[i], token)[step - 1]
            sums[i] = (moved[i].astype(F32) + local_part).astype(BF16)
            return sums[i]
        return token

    plan = [
        lambda t: first_part(0, t),
        lambda t: ring_step(1, 0, t),
        lambda t: second_part(0, t),
        lambda t: ring_step(1, 1, t),
        lambda t: first_part(1, t),
        lambda t: ring_step(2, 0, t),
        lambda t: second_part(1, t),
        lambda t: ring_step(2, 1, t),
    ]
    for act in plan:
        token = act(token)
    token = third_part(0, token)
    query_grad, key_grad = finish_others(
        factor, par, after(out_grad, token), values, qi, ki, later, prior
    )
    for step in range(3, pairs):
        for i in range(chains):
            token = ring_step(step, i, token)
    weight_grad = finish_weight(
        1.0 / math.sqrt(length * n_ctx), moved, [r[-1] for r in rest]
    )
    third_part(1, token)

    mine, other = (
        jnp.concatenate(
            [s[k].reshape(length, per, part_rows) for s in state], axis=2
        )
        for k in ("mine", "other")
    )
    first = jnp.where(parity == 0, mine, other)
    second = jnp.where(parity == 0, other, mine)
    input_grad = jnp.stack([first, second], axis=2).reshape(length, -1)
    return (query_grad, key_grad, input_grad, weight_grad)


def solution(mesh):
    spec = P("ctx", "head")
    return jax.shard_map(
        local, mesh=mesh, in_specs=(spec,) * 6, out_specs=(spec,) * 4, check_vma=False
    )
```

time: 162 us -> 196 us (1.21)
  Pallas kernels: 27.8 us -> 61.6 us
  blocking collectives: 17.4 us -> 0 us
  starting transfers between devices: 28.6 us -> 44.3 us
  matrix products: 13.2 us -> 0 us
  waiting for transfers between devices: 36.4 us -> 47.5 us
  other arithmetic: 4.05 us -> 11.8 us
  local copies, waits for them, and re-layouts: 18.1 us -> 13.4 us
    pallas_call x7 -> x14, Pallas kernels: 22.4 us -> 52.8 us  [the longest x4 22.7 us: pieces(): pl.pallas_call(functools.partial(piece_kernel, count), grid=(steps,), in_...]
    ppermute x6 -> x12, waiting for transfers between devices: 7.19 us -> 25.3 us  [the longest x6 15.3 us: line_move(): return lax.ppermute(x, 'ctx', moves)]
    all_gather x1 -> x0, blocking collectives: 17.4 us -> none  [local(): every = lax.all_gather(both, 'ctx', axis_index_groups=lines)]
    ppermute x6 -> x12, starting transfers between devices: 10.4 us -> 27.6 us  [the longest x6 16 us: ring_step(): moved[i] = lax.ppermute(sums[i], 'ctx', ring)]
    dot_general x8 -> x0, matrix products: 13.2 us -> none  [dot(): lax.dot_general(a, b, (((ca,), (cb,)), ((), ())), preferred_element_type=...]
    unnamed x55 -> x47, local copies, waits for them, and re-layouts: 14.8 us -> 4.79 us
    another operation x2 -> x3, other arithmetic: 0.2 us -> 5.57 us  [the longest x2 4.57 us: first_part(): state[i]['got'] = across(jnp.stack(out), 1)]
    ppermute x10, waiting for transfers between devices: 11.4 us -> 7.65 us  [across(): return lax.ppermute(x, 'head', [(i, i ^ bit) for i in range(n_head)])]
  transfers between devices with their start and end apart: 26 -> 32, of which waited for: 8 -> 10; matrix products, arithmetic and copies ran while one was open for 11% -> 8% of each run, Pallas kernels for 17% -> 30%
where the time goes in v4:
time: 196 us; the launch traced here: 194 us
  Pallas kernels  61.6 us (31%)
  waiting for transfers between devices  47.5 us (24%)
  starting transfers between devices  44.3 us (23%)
  between operations  15 us (8%)
  local copies, waits for them, and re-layouts  13.4 us (7%)
  other arithmetic  11.8 us (6%)
    pallas_call x4, Pallas kernels, pieces(): pl.pallas_call(functools.partial(piece_kernel, count), grid=(steps,), in_...  22.7 us
    ppermute x6, starting transfers between devices, ring_step(): moved[i] = lax.ppermute(sums[i], 'ctx', ring)  16 us
    ppermute x6, waiting for transfers between devices, line_move(): return lax.ppermute(x, 'ctx', moves)  15.3 us
    ppermute x8, waiting for transfers between devices, partner(): return lax.ppermute(x, 'ctx', [(i, i ^ 1) for i in range(n_ctx)])  14.6 us
    pallas_call x4, Pallas kernels, inputs_part(): pl.pallas_call(functools.partial(inputs_kernel, offs, per, chains, got is...  13.2 us
    ppermute x6, starting transfers between devices, line_move(): return lax.ppermute(x, 'ctx', moves)  11.6 us
    ppermute x6, waiting for transfers between devices, ring_step(): moved[i] = lax.ppermute(sums[i], 'ctx', ring)  10 us
    ppermute x8, starting transfers between devices, partner(): return lax.ppermute(x, 'ctx', [(i, i ^ 1) for i in range(n_ctx)])  9.49 us
  transfers between devices with their start and end apart: 32, of which 10 were waited for; matrix products, arithmetic and copies ran while one was open for 8% of the time, Pallas kernels for 30%

profile of v4, /device:TPU:0, one launch (start us, length us, event | category | flops | bytes accessed | tf_op | source)
XLA Modules:
  0.0 193.6 jit_solution(321291776954815020)
XLA Ops:
  9.2 2.3 %split.1 = (bf16[1,512,512]{2,1,0:T(8,128)(2,1)}, bf16[1,512,512]{2,1,0:T(8,128)(2,1)}) custom-call(s32[1]{0:T(128)} %bitcast.par_ref, bf16[512,1024]{1,0:T(8,128)(2,1)} %x_ref.1), custom_call_target="tpu_custom_call" | custom-call | bytes 2097152 | tf_op jit(solution)/shard_map/split/pallas_call | solution.py:62
  11.5 2.9 %collective-permute-start.9 = (bf16[1,512,512]{2,1,0:T(8,128)(2,1)}, bf16[1,512,512]{2,1,0:T(8,128)(2,1)S(1)}, u32[]{:S(2)}, u32[]{:S(2)}) collective-permute-start(bf16[1,512,512]{2,1,0:T(8,128)(2,1)} %get-tuple-element.46), channel_id=1, source_target_pairs={{0,4},{4,0},{8,12},{12,8},{16,20},{20,16},{24,28},{28,24},{1,5},{5... | collective-permute-start | bytes 1572872 | tf_op jit(solution)/shard_map/ppermute | solution.py:301
  14.4 2.2 %states.2 = bf16[4,128,128]{2,1,0:T(8,128)(2,1)} custom-call(bf16[512,512]{1,0:T(8,128)(2,1)} %a_ref.2, bf16[512,512]{1,0:T(8,128)(2,1)} %g_ref.2), custom_call_target="tpu_custom_call" | custom-call | flops 67108864 | bytes 1048576 | tf_op jit(solution)/shard_map/states/pallas_call | solution.py:34
  18.0 2.2 %states.3 = bf16[4,128,128]{2,1,0:T(8,128)(2,1)} custom-call(bf16[512,512]{1,0:T(8,128)(2,1)} %k_ref.3, bf16[512,512]{1,0:T(8,128)(2,1)} %v_ref.3), custom_call_target="tpu_custom_call" | custom-call | flops 67108864 | bytes 1048576 | tf_op jit(solution)/shard_map/states/pallas_call | solution.py:34
  21.4 2.0 %collective-permute-start.7 = (bf16[1,512,512]{2,1,0:T(8,128)(2,1)S(1)}, bf16[1,512,512]{2,1,0:T(8,128)(2,1)S(1)}, u32[]{:S(2)}, u32[]{:S(2)}) collective-permute-start(bf16[1,512,512]{2,1,0:T(8,128)(2,1)S(1)} %copy-done.3), channel_id=1, source_target_pairs={{0,2},{1,3},{2,0},{3,1},{4,6},{5,7},{6,4},{7,5},{8,10},{9,11},{10,... | collective-permute-start | bytes 1572872 | tf_op jit(solution)/shard_map/ppermute | solution.py:304
  23.4 4.0 %collective-permute-done.9.refs_4_ = bf16[1,512,512]{2,1,0:T(8,128)(2,1)S(1)} collective-permute-done((bf16[1,512,512]{2,1,0:T(8,128)(2,1)}, bf16[1,512,512]{2,1,0:T(8,128)(2,1)S(1)}, u32[]{:S(2)}, u32[]{:S(2)}) %collective-permute-start.9) | collective-permute-done | bytes 524320 | tf_op jit(solution)/shard_map/ppermute | solution.py:301
  27.4 2.1 %collective-permute-start.11 = (bf16[1,512,512]{2,1,0:T(8,128)(2,1)S(1)}, bf16[1,512,512]{2,1,0:T(8,128)(2,1)S(1)}, u32[]{:S(2)}, u32[]{:S(2)}) collective-permute-start(bf16[1,512,512]{2,1,0:T(8,128)(2,1)S(1)} %collective-permute-done.9.refs_4_), channel_id=1, source_target_pairs={{0,2},{1,3},{2,0},{3,1},{4,6},{5,7},{6,4},{7,5},{8,10},{9,11},{10,... | collective-permute-start | bytes 1572872 | tf_op jit(solution)/shard_map/ppermute | solution.py:304
  32.1 6.1 %inside.1 = (f32[512,512]{1,0:T(8,128)}, f32[512,512]{1,0:T(8,128)}, f32[512,512]{1,0:T(8,128)}) custom-call(bf16[512,512]{1,0:T(8,128)(2,1)} %a_ref.2, bf16[512,512]{1,0:T(8,128)(2,1)} %k_ref.3, bf16[512,512]{1,0:T(8,128)(2,1)} %v_ref.3, bf16[512,512]{1,0:T(8,128)(2,1)} %g_ref.2), custom_call_target="tpu_custom_call" | custom-call | flops 1342177280 | bytes 5242880 | tf_op jit(solution)/shard_map/inside/pallas_call | solution.py:89
  38.2 11.1 %collective-permute-done.1.refs_1_ = bf16[4,128,128]{2,1,0:T(8,128)(2,1)S(1)} collective-permute-done((bf16[4,128,128]{2,1,0:T(8,128)(2,1)S(1)}, bf16[4,128,128]{2,1,0:T(8,128)(2,1)S(1)}, u32[]{:S(2)}, u32[]{:S(2)}) %collective-permute-start.1) | collective-permute-done | bytes 131104 | tf_op jit(solution)/shard_map/ppermute | solution.py:323
  53.8 3.3 %collective-permute-done.3.got_far.refs_1_ = bf16[4,128,128]{2,1,0:T(8,128)(2,1)S(1)} collective-permute-done((bf16[4,128,128]{2,1,0:T(8,128)(2,1)}, bf16[4,128,128]{2,1,0:T(8,128)(2,1)S(1)}, u32[]{:S(2)}, u32[]{:S(2)}) %collective-permute-start.3) | collective-permute-done | bytes 131104 | tf_op jit(solution)/shard_map/ppermute | solution.py:301
  57.8 2.7 %finish_value.1 = (bf16[512,256]{1,0:T(8,128)(2,1)}, bf16[512,256]{1,0:T(8,128)(2,1)}) custom-call(s32[1]{0:T(128)} %bitcast.par_ref, bf16[512,512]{1,0:T(8,128)(2,1)} %k_ref.3, f32[512,512]{1,0:T(8,128)} %get-tuple-element.41.vi_ref, f32[4,128,128]{2,1,0:T(8,128)} %get-tuple-element.42.far.refs_0_, bf16[4,128,128]{2,1,0:T(8,128)(2,1)} %copy-done.12, ...), custom_call_target="tpu_custom_call" | custom-call | flops 134217728 | bytes 2097152 | tf_op jit(solution)/shard_map/finish_value/pallas_call | solution.py:146
  63.9 3.2 %collective-permute-done.5.b_ref.refs_0_ = bf16[512,256]{1,0:T(8,128)(2,1)S(1)} collective-permute-done((bf16[512,256]{1,0:T(8,128)(2,1)}, bf16[512,256]{1,0:T(8,128)(2,1)S(1)}, u32[]{:S(2)}, u32[]{:S(2)}) %collective-permute-start.5) | collective-permute-done | bytes 262176 | tf_op jit(solution)/shard_map/ppermute | solution.py:301
  69.7 4.0 %collective-permute-done.14.b_ref.refs_1_ = bf16[512,256]{1,0:T(8,128)(2,1)S(1)} collective-permute-done((bf16[512,256]{1,0:T(8,128)(2,1)}, bf16[512,256]{1,0:T(8,128)(2,1)S(1)}, u32[]{:S(2)}, u32[]{:S(2)}) %collective-permute-start.14) | collective-permute-done | bytes 262176 | tf_op jit(solution)/shard_map/ppermute | solution.py:301
  74.4 4.0 %pieces.5 = bf16[1,256,512]{2,1,0:T(8,128)(2,1)} custom-call(s32[1]{0:T(128)} %bitcast.69, s32[1]{0:T(128)} %constant.78.clone.1.subs_ref, bf16[512,256]{1,0:T(8,128)(2,1)} %get-tuple-element.50.a_ref.refs_3_, bf16[512,256]{1,0:T(8,128)(2,1)} %copy-done.2, bf16[1,512,512]{2,1,0:T(8,128)(2,1)} %get-tuple-element.45.refs_0_, bf16[1,512,512]{2,1,0:T(8,128)(2,1)} %copy-done.7, ...), custom_call_target="tpu_custom_call" | custom-call | flops 268435456 | bytes 1572864 | tf_op jit(solution)/shard_map/pieces/pallas_call | solution.py:210
  79.0 7.2 %pieces.6 = f32[3,256,512]{2,1,0:T(8,128)} custom-call(s32[3]{0:T(128)} %slice.59.offs_ref, s32[3]{0:T(128)} %slice.60.subs_ref, bf16[512,256]{1,0:T(8,128)(2,1)} %get-tuple-element.49.a_ref.refs_2_, bf16[512,256]{1,0:T(8,128)(2,1)} %copy-done.1, bf16[1,512,512]{2,1,0:T(8,128)(2,1)} %get-tuple-element.45.refs_0_, bf16[1,512,512]{2,1,0:T(8,128)(2,1)} %copy-done.7, ...), custom_call_target="tpu_custom_call" | custom-call | flops 805306368 | bytes 4718592 | tf_op jit(solution)/shard_map/pieces/pallas_call | solution.py:210
  86.2 7.3 %pieces.7 = f32[3,256,512]{2,1,0:T(8,128)} custom-call(s32[3]{0:T(128)} %slice.59.offs_ref, s32[3]{0:T(128)} %slice.60.subs_ref, bf16[512,256]{1,0:T(8,128)(2,1)} %get-tuple-element.50.a_ref.refs_3_, bf16[512,256]{1,0:T(8,128)(2,1)} %copy-done.2, bf16[1,512,512]{2,1,0:T(8,128)(2,1)} %get-tuple-element.45.refs_0_, bf16[1,512,512]{2,1,0:T(8,128)(2,1)} %copy-done.7, ...), custom_call_target="tpu_custom_call" | custom-call | flops 805306368 | bytes 4718592 | tf_op jit(solution)/shard_map/pieces/pallas_call | solution.py:210
  93.5 3.0 %inputs_part.4 = (bf16[1024,256]{1,0:T(8,128)(2,1)}, bf16[1024,256]{1,0:T(8,128)(2,1)}) custom-call(s32[1]{0:T(128)} %bitcast.1.head_ref, bf16[4,256,512]{2,1,0:T(8,128)(2,1)} %bitcast.53, bf16[512,256]{1,0:T(8,128)(2,1)} %copy-done.1, bf16[512,256]{1,0:T(8,128)(2,1)} %copy-done.2, bf16[512,256]{1,0:T(8,128)(2,1)} %get-tuple-element.49.a_ref.refs_2_, ...), custom_call_target="tpu_custom_call" | custom-call | flops 536870912 | bytes 4194304 | tf_op jit(solution)/shard_map/inputs_part/pallas_call | solution.py:274
  96.6 2.3 %pad_maximum_fusion = bf16[2,1024,256]{2,1,0:T(8,128)(2,1)} fusion(bf16[1,1024,256]{2,1,0:T(8,128)(2,1)} %bitcast.62, bf16[1,1024,256]{2,1,0:T(8,128)(2,1)} %bitcast.61), kind=kLoop, calls=%fused_computation.1 | loop fusion | flops 524288 | bytes 2097152 | tf_op jit(solution)/shard_map/stack | solution.py:388
  98.8 4.2 %pieces.4 = bf16[1,256,512]{2,1,0:T(8,128)(2,1)} custom-call(s32[1]{0:T(128)} %bitcast.70, s32[1]{0:T(128)} %constant.78.clone.1.subs_ref, bf16[512,256]{1,0:T(8,128)(2,1)} %get-tuple-element.49.a_ref.refs_2_, bf16[512,256]{1,0:T(8,128)(2,1)} %copy-done.1, bf16[1,512,512]{2,1,0:T(8,128)(2,1)} %get-tuple-element.45.refs_0_, bf16[1,512,512]{2,1,0:T(8,128)(2,1)} %copy-done.7, ...), custom_call_target="tpu_custom_call" | custom-call | flops 268435456 | bytes 1572864 | tf_op jit(solution)/shard_map/pieces/pallas_call | solution.py:210
  103.1 9.3 %collective-permute-done.13 = bf16[256,512]{1,0:T(8,128)(2,1)S(1)} collective-permute-done((bf16[256,512]{1,0:T(8,128)(2,1)}, bf16[256,512]{1,0:T(8,128)(2,1)S(1)}, u32[]{:S(2)}, u32[]{:S(2)}) %collective-permute-start.13) | collective-permute-done | bytes 262176 | tf_op jit(solution)/shard_map/ppermute | solution.py:422
  113.2 3.6 %inputs_part.5 = (f32[1024,256]{1,0:T(8,128)}, bf16[1024,256]{1,0:T(8,128)(2,1)}) custom-call(s32[1]{0:T(128)} %bitcast.1.head_ref, bf16[4,256,512]{2,1,0:T(8,128)(2,1)} %bitcast.54, bf16[512,256]{1,0:T(8,128)(2,1)} %copy-done.1, bf16[512,256]{1,0:T(8,128)(2,1)} %copy-done.2, bf16[512,256]{1,0:T(8,128)(2,1)} %get-tuple-element.49.a_ref.refs_2_, ...), custom_call_target="tpu_custom_call" | custom-call | flops 536870912 | bytes 4194304 | tf_op jit(solution)/shard_map/inputs_part/pallas_call | solution.py:274
  118.6 3.0 %inputs_part.6 = (bf16[1024,256]{1,0:T(8,128)(2,1)}, bf16[1024,256]{1,0:T(8,128)(2,1)}) custom-call(s32[1]{0:T(128)} %bitcast.1.head_ref, bf16[4,256,512]{2,1,0:T(8,128)(2,1)} %bitcast.55, bf16[512,256]{1,0:T(8,128)(2,1)} %copy-done.1, bf16[512,256]{1,0:T(8,128)(2,1)} %copy-done.2, bf16[512,256]{1,0:T(8,128)(2,1)} %get-tuple-element.49.a_ref.refs_2_, ...), custom_call_target="tpu_custom_call" | custom-call | flops 536870912 | bytes 4194304 | tf_op jit(solution)/shard_map/inputs_part/pallas_call | solution.py:274
  121.7 2.3 %pad_maximum_fusion.1 = bf16[2,1024,256]{2,1,0:T(8,128)(2,1)} fusion(bf16[1,1024,256]{2,1,0:T(8,128)(2,1)} %bitcast.64, bf16[1,1024,256]{2,1,0:T(8,128)(2,1)} %bitcast.63), kind=kLoop, calls=%fused_computation.2 | loop fusion | flops 524288 | bytes 2097152 | tf_op jit(solution)/shard_map/stack | solution.py:388
  124.0 2.0 %collective-permute-start.21 = (bf16[4,128,128]{2,1,0:T(8,128)(2,1)S(1)}, bf16[4,128,128]{2,1,0:T(8,128)(2,1)}, u32[]{:S(2)}, u32[]{:S(2)}) collective-permute-start(bf16[4,128,128]{2,1,0:T(8,128)(2,1)S(1)} %copy-done.13), channel_id=1, source_target_pairs={{0,8},{4,12},{8,16},{12,20},{16,24},{20,28},{1,9},{5,13},{9,17},{1... | collective-permute-start | bytes 393224 | tf_op jit(solution)/shard_map/ppermute | solution.py:323
  126.0 3.7 %collective-permute-start.22 = (bf16[4,128,128]{2,1,0:T(8,128)(2,1)S(1)}, bf16[4,128,128]{2,1,0:T(8,128)(2,1)}, u32[]{:S(2)}, u32[]{:S(2)}) collective-permute-start(bf16[4,128,128]{2,1,0:T(8,128)(2,1)S(1)} %copy-done.13), channel_id=1, source_target_pairs={{0,16},{4,20},{8,24},{12,28},{1,17},{5,21},{9,25},{13,29},{2,18},{... | collective-permute-start | bytes 393224 | tf_op jit(solution)/shard_map/ppermute | solution.py:323
  132.8 2.9 %collective-permute-done.23.refs_2_ = bf16[4,128,128]{2,1,0:T(8,128)(2,1)} collective-permute-done((bf16[4,128,128]{2,1,0:T(8,128)(2,1)S(1)}, bf16[4,128,128]{2,1,0:T(8,128)(2,1)}, u32[]{:S(2)}, u32[]{:S(2)}) %collective-permute-start.23) | collective-permute-done | bytes 131104 | tf_op jit(solution)/shard_map/ppermute | solution.py:323
  139.7 11.9 %collective-permute-start.18 = (bf16[256,512]{1,0:T(8,128)(2,1)S(1)}, bf16[256,512]{1,0:T(8,128)(2,1)}, u32[]{:S(2)}, u32[]{:S(2)}) collective-permute-start(bf16[256,512]{1,0:T(8,128)(2,1)S(1)} %fusion.2), channel_id=1, source_target_pairs={{0,16},{4,20},{16,24},{20,28},{24,8},{28,12},{8,0},{12,4},{1,17},{... | collective-permute-start | bytes 786440 | tf_op jit(solution)/shard_map/ppermute | solution.py:422
  154.2 3.9 %collective-permute-start.28 = (bf16[256,512]{1,0:T(8,128)(2,1)}, bf16[256,512]{1,0:T(8,128)(2,1)S(1)}, u32[]{:S(2)}, u32[]{:S(2)}) collective-permute-start(bf16[256,512]{1,0:T(8,128)(2,1)} %fusion.1), channel_id=1, source_target_pairs={{0,16},{4,20},{16,24},{20,28},{24,8},{28,12},{8,0},{12,4},{1,17},{... | collective-permute-start | bytes 786440 | tf_op jit(solution)/shard_map/ppermute | solution.py:422
  158.0 3.5 %inputs_part.7 = (f32[1024,256]{1,0:T(8,128)}, bf16[1024,256]{1,0:T(8,128)(2,1)}) custom-call(s32[1]{0:T(128)} %bitcast.1.head_ref, bf16[4,256,512]{2,1,0:T(8,128)(2,1)} %bitcast.56, bf16[512,256]{1,0:T(8,128)(2,1)} %copy-done.1, bf16[512,256]{1,0:T(8,128)(2,1)} %copy-done.2, bf16[512,256]{1,0:T(8,128)(2,1)} %get-tuple-element.49.a_ref.refs_2_, ...), custom_call_target="tpu_custom_call" | custom-call | flops 536870912 | bytes 4194304 | tf_op jit(solution)/shard_map/inputs_part/pallas_call | solution.py:274
  166.5 7.6 %collective-permute-done.25 = bf16[1,1024,256]{2,1,0:T(8,128)(2,1)S(1)} collective-permute-done((bf16[1,1024,256]{2,1,0:T(8,128)(2,1)}, bf16[1,1024,256]{2,1,0:T(8,128)(2,1)S(1)}, u32[]{:S(2)}, u32[]{:S(2)}) %collective-permute-start.25) | collective-permute-done | bytes 524320 | tf_op jit(solution)/shard_map/ppermute | solution.py:304
  176.7 3.9 %finish_others.1 = (bf16[512,512]{1,0:T(8,128)(2,1)}, bf16[512,512]{1,0:T(8,128)(2,1)}) custom-call(s32[1]{0:T(128)} %bitcast.par_ref, bf16[512,512]{1,0:T(8,128)(2,1)} %g_ref.2, bf16[512,512]{1,0:T(8,128)(2,1)} %v_ref.3, f32[512,512]{1,0:T(8,128)} %get-tuple-element.68.qi_ref, f32[512,512]{1,0:T(8,128)} %get-tuple-element.69.ki_ref, ...), custom_call_target="tpu_custom_call" | custom-call | flops 268435456 | bytes 4194304 | tf_op jit(solution)/shard_map/finish_others/pallas_call | solution.py:173
  182.0 2.7 %finish_weight.1 = f32[512,512]{1,0:T(8,128)} custom-call(bf16[256,512]{1,0:T(8,128)(2,1)} %copy-done.15, bf16[256,512]{1,0:T(8,128)(2,1)} %copy-done.16, f32[256,512]{1,0:T(8,128)} %slice_bitcast_fusion.1.refs_2_, f32[256,512]{1,0:T(8,128)} %slice_bitcast_fusion.refs_3_), custom_call_target="tpu_custom_call" | custom-call | bytes 2621440 | tf_op jit(solution)/shard_map/finish_weight/pallas_call | solution.py:240
  (123 shorter events, 42.3 us)
Async XLA Ops:
  7.2 86.3 %all-gather.5.cloned.1.call-start = ((), (), s32[]{:S(2)}) async-start(), calls=%async_computation | async-start | bytes 1310720 | tf_op jit(solution)/shard_map/all_gather | solution.py:308
  9.1 109.5 %all-gather.7.cloned.1.call-start = ((), (), s32[]{:S(2)}) async-start(), calls=%async_computation.1 | async-start | bytes 1310720 | tf_op jit(solution)/shard_map/all_gather | solution.py:308
  11.5 15.9 %collective-permute-start.9 = (bf16[1,512,512]{2,1,0:T(8,128)(2,1)}, bf16[1,512,512]{2,1,0:T(8,128)(2,1)S(1)}, u32[]{:S(2)}, u32[]{:S(2)}) collective-permute-start(bf16[1,512,512]{2,1,0:T(8,128)(2,1)} %get-tuple-element.46), channel_id=1, source_target_pairs={{0,4},{4,0},{8,12},{12,8},{16,20},{20,16},{24,28},{28,24},{1,5},{5... | collective-permute-start | bytes 1572872 | tf_op jit(solution)/shard_map/ppermute | solution.py:301
  16.6 14.1 %collective-permute-start = (bf16[4,128,128]{2,1,0:T(8,128)(2,1)}, bf16[4,128,128]{2,1,0:T(8,128)(2,1)S(1)}, u32[]{:S(2)}, u32[]{:S(2)}) collective-permute-start(bf16[4,128,128]{2,1,0:T(8,128)(2,1)} %states.2), channel_id=1, source_target_pairs={{8,0},{12,4},{16,8},{20,12},{24,16},{28,20},{9,1},{13,5},{17,9},{2... | collective-permute-start | bytes 393224 | tf_op jit(solution)/shard_map/ppermute | solution.py:323
  21.3 31.8 %collective-permute-start.4 = (bf16[2,4,128,128]{3,2,1,0:T(8,128)(2,1)S(1)}, bf16[2,4,128,128]{3,2,1,0:T(8,128)(2,1)S(1)}, u32[]{:S(2)}, u32[]{:S(2)}) collective-permute-start(bf16[2,4,128,128]{3,2,1,0:T(8,128)(2,1)S(1)} %pad_maximum_fusion.5), channel_id=1, source_target_pairs={{0,4},{4,0},{8,12},{12,8},{16,20},{20,16},{24,28},{28,24},{1,5},{5... | collective-permute-start | bytes 786440 | tf_op jit(solution)/shard_map/ppermute | solution.py:301
  21.4 40.7 %collective-permute-start.7 = (bf16[1,512,512]{2,1,0:T(8,128)(2,1)S(1)}, bf16[1,512,512]{2,1,0:T(8,128)(2,1)S(1)}, u32[]{:S(2)}, u32[]{:S(2)}) collective-permute-start(bf16[1,512,512]{2,1,0:T(8,128)(2,1)S(1)} %copy-done.3), channel_id=1, source_target_pairs={{0,2},{1,3},{2,0},{3,1},{4,6},{5,7},{6,4},{7,5},{8,10},{9,11},{10,... | collective-permute-start | bytes 1572872 | tf_op jit(solution)/shard_map/ppermute | solution.py:304
  27.4 34.8 %collective-permute-start.11 = (bf16[1,512,512]{2,1,0:T(8,128)(2,1)S(1)}, bf16[1,512,512]{2,1,0:T(8,128)(2,1)S(1)}, u32[]{:S(2)}, u32[]{:S(2)}) collective-permute-start(bf16[1,512,512]{2,1,0:T(8,128)(2,1)S(1)} %collective-permute-done.9.refs_4_), channel_id=1, source_target_pairs={{0,2},{1,3},{2,0},{3,1},{4,6},{5,7},{6,4},{7,5},{8,10},{9,11},{10,... | collective-permute-start | bytes 1572872 | tf_op jit(solution)/shard_map/ppermute | solution.py:304
  29.5 19.9 %collective-permute-start.1 = (bf16[4,128,128]{2,1,0:T(8,128)(2,1)S(1)}, bf16[4,128,128]{2,1,0:T(8,128)(2,1)S(1)}, u32[]{:S(2)}, u32[]{:S(2)}) collective-permute-start(bf16[4,128,128]{2,1,0:T(8,128)(2,1)S(1)} %copy-done.14), channel_id=1, source_target_pairs={{16,0},{20,4},{24,8},{28,12},{17,1},{21,5},{25,9},{29,13},{18,2},{... | collective-permute-start | bytes 393224 | tf_op jit(solution)/shard_map/ppermute | solution.py:323
  30.8 18.6 %collective-permute-start.2 = (bf16[4,128,128]{2,1,0:T(8,128)(2,1)S(1)}, bf16[4,128,128]{2,1,0:T(8,128)(2,1)S(1)}, u32[]{:S(2)}, u32[]{:S(2)}) collective-permute-start(bf16[4,128,128]{2,1,0:T(8,128)(2,1)S(1)} %copy-done.14), channel_id=1, source_target_pairs={{24,0},{28,4},{25,1},{29,5},{26,2},{30,6},{27,3},{31,7}} | collective-permute-start | bytes 393224 | tf_op jit(solution)/shard_map/ppermute | solution.py:323
  52.0 5.2 %collective-permute-start.3 = (bf16[4,128,128]{2,1,0:T(8,128)(2,1)}, bf16[4,128,128]{2,1,0:T(8,128)(2,1)S(1)}, u32[]{:S(2)}, u32[]{:S(2)}) collective-permute-start(bf16[4,128,128]{2,1,0:T(8,128)(2,1)} %get-tuple-element.43), channel_id=1, source_target_pairs={{0,4},{4,0},{8,12},{12,8},{16,20},{20,16},{24,28},{28,24},{1,5},{5... | collective-permute-start | bytes 393224 | tf_op jit(solution)/shard_map/ppermute | solution.py:301
  60.5 6.7 %collective-permute-start.5 = (bf16[512,256]{1,0:T(8,128)(2,1)}, bf16[512,256]{1,0:T(8,128)(2,1)S(1)}, u32[]{:S(2)}, u32[]{:S(2)}) collective-permute-start(bf16[512,256]{1,0:T(8,128)(2,1)} %get-tuple-element.49.a_ref.refs_2_), channel_id=1, source_target_pairs={{0,4},{4,0},{8,12},{12,8},{16,20},{20,16},{24,28},{28,24},{1,5},{5... | collective-permute-start | bytes 786440 | tf_op jit(solution)/shard_map/ppermute | solution.py:301
  61.6 8.1 %collective-permute-start.6 = (bf16[1,512,512]{2,1,0:T(8,128)(2,1)S(1)}, bf16[1,512,512]{2,1,0:T(8,128)(2,1)S(1)}, u32[]{:S(2)}, u32[]{:S(2)}) collective-permute-start(bf16[1,512,512]{2,1,0:T(8,128)(2,1)S(1)} %copy-done.3), channel_id=1, source_target_pairs={{0,1},{1,0},{2,3},{3,2},{4,5},{5,4},{6,7},{7,6},{8,9},{9,8},{10,11... | collective-permute-start | bytes 1572872 | tf_op jit(solution)/shard_map/ppermute | solution.py:304
  61.6 12.1 %collective-permute-start.10 = (bf16[1,512,512]{2,1,0:T(8,128)(2,1)S(1)}, bf16[1,512,512]{2,1,0:T(8,128)(2,1)}, u32[]{:S(2)}, u32[]{:S(2)}) collective-permute-start(bf16[1,512,512]{2,1,0:T(8,128)(2,1)S(1)} %collective-permute-done.9.refs_4_), channel_id=1, source_target_pairs={{0,1},{1,0},{2,3},{3,2},{4,5},{5,4},{6,7},{7,6},{8,9},{9,8},{10,11... | collective-permute-start | bytes 1572872 | tf_op jit(solution)/shard_map/ppermute | solution.py:304
  62.1 11.6 %collective-permute-start.8 = (bf16[1,512,512]{2,1,0:T(8,128)(2,1)S(1)}, bf16[1,512,512]{2,1,0:T(8,128)(2,1)}, u32[]{:S(2)}, u32[]{:S(2)}) collective-permute-start(bf16[1,512,512]{2,1,0:T(8,128)(2,1)S(1)} %collective-permute-done.7.refs_2_), channel_id=1, source_target_pairs={{0,1},{1,0},{2,3},{3,2},{4,5},{5,4},{6,7},{7,6},{8,9},{9,8},{10,11... | collective-permute-start | bytes 1572872 | tf_op jit(solution)/shard_map/ppermute | solution.py:304
  62.2 11.5 %collective-permute-start.12 = (bf16[1,512,512]{2,1,0:T(8,128)(2,1)S(1)}, bf16[1,512,512]{2,1,0:T(8,128)(2,1)}, u32[]{:S(2)}, u32[]{:S(2)}) collective-permute-start(bf16[1,512,512]{2,1,0:T(8,128)(2,1)S(1)} %collective-permute-done.11.refs_6_), channel_id=1, source_target_pairs={{0,1},{1,0},{2,3},{3,2},{4,5},{5,4},{6,7},{7,6},{8,9},{9,8},{10,11... | collective-permute-start | bytes 1572872 | tf_op jit(solution)/shard_map/ppermute | solution.py:304
  67.1 6.6 %collective-permute-start.14 = (bf16[512,256]{1,0:T(8,128)(2,1)}, bf16[512,256]{1,0:T(8,128)(2,1)S(1)}, u32[]{:S(2)}, u32[]{:S(2)}) collective-permute-start(bf16[512,256]{1,0:T(8,128)(2,1)} %get-tuple-element.50.a_ref.refs_3_), channel_id=1, source_target_pairs={{0,4},{4,0},{8,12},{12,8},{16,20},{20,16},{24,28},{28,24},{1,5},{5... | collective-permute-start | bytes 786440 | tf_op jit(solution)/shard_map/ppermute | solution.py:301
  98.8 14.4 %collective-permute-start.15 = (bf16[2,1024,256]{2,1,0:T(8,128)(2,1)}, bf16[2,1024,256]{2,1,0:T(8,128)(2,1)}, u32[]{:S(2)}, u32[]{:S(2)}) collective-permute-start(bf16[2,1024,256]{2,1,0:T(8,128)(2,1)} %pad_maximum_fusion), channel_id=1, source_target_pairs={{0,1},{1,0},{2,3},{3,2},{4,5},{5,4},{6,7},{7,6},{8,9},{9,8},{10,11... | collective-permute-start | bytes 3145736 | tf_op jit(solution)/shard_map/ppermute | solution.py:304
  103.0 9.4 %collective-permute-start.13 = (bf16[256,512]{1,0:T(8,128)(2,1)}, bf16[256,512]{1,0:T(8,128)(2,1)S(1)}, u32[]{:S(2)}, u32[]{:S(2)}) collective-permute-start(bf16[256,512]{1,0:T(8,128)(2,1)} %bitcast.68), channel_id=1, source_target_pairs={{0,16},{4,20},{16,24},{20,28},{24,8},{28,12},{8,0},{12,4},{1,17},{... | collective-permute-start | bytes 786440 | tf_op jit(solution)/shard_map/ppermute | solution.py:422
  103.1 14.5 %collective-permute-start.17 = (bf16[256,512]{1,0:T(8,128)(2,1)S(1)}, bf16[256,512]{1,0:T(8,128)(2,1)}, u32[]{:S(2)}, u32[]{:S(2)}) collective-permute-start(bf16[256,512]{1,0:T(8,128)(2,1)S(1)} %bitcast.67), channel_id=1, source_target_pairs={{0,16},{4,20},{16,24},{20,28},{24,8},{28,12},{8,0},{12,4},{1,17},{... | collective-permute-start | bytes 786440 | tf_op jit(solution)/shard_map/ppermute | solution.py:422
  124.0 34.1 %collective-permute-start.20 = (bf16[2,1024,256]{2,1,0:T(8,128)(2,1)}, bf16[2,1024,256]{2,1,0:T(8,128)(2,1)}, u32[]{:S(2)}, u32[]{:S(2)}) collective-permute-start(bf16[2,1024,256]{2,1,0:T(8,128)(2,1)} %pad_maximum_fusion.1), channel_id=1, source_target_pairs={{0,1},{1,0},{2,3},{3,2},{4,5},{5,4},{6,7},{7,6},{8,9},{9,8},{10,11... | collective-permute-start | bytes 3145736 | tf_op jit(solution)/shard_map/ppermute | solution.py:304
  124.0 7.6 %collective-permute-start.21 = (bf16[4,128,128]{2,1,0:T(8,128)(2,1)S(1)}, bf16[4,128,128]{2,1,0:T(8,128)(2,1)}, u32[]{:S(2)}, u32[]{:S(2)}) collective-permute-start(bf16[4,128,128]{2,1,0:T(8,128)(2,1)S(1)} %copy-done.13), channel_id=1, source_target_pairs={{0,8},{4,12},{8,16},{12,20},{16,24},{20,28},{1,9},{5,13},{9,17},{1... | collective-permute-start | bytes 393224 | tf_op jit(solution)/shard_map/ppermute | solution.py:323
  126.0 6.9 %collective-permute-start.22 = (bf16[4,128,128]{2,1,0:T(8,128)(2,1)S(1)}, bf16[4,128,128]{2,1,0:T(8,128)(2,1)}, u32[]{:S(2)}, u32[]{:S(2)}) collective-permute-start(bf16[4,128,128]{2,1,0:T(8,128)(2,1)S(1)} %copy-done.13), channel_id=1, source_target_pairs={{0,16},{4,20},{8,24},{12,28},{1,17},{5,21},{9,25},{13,29},{2,18},{... | collective-permute-start | bytes 393224 | tf_op jit(solution)/shard_map/ppermute | solution.py:323
  129.6 6.0 %collective-permute-start.23 = (bf16[4,128,128]{2,1,0:T(8,128)(2,1)S(1)}, bf16[4,128,128]{2,1,0:T(8,128)(2,1)}, u32[]{:S(2)}, u32[]{:S(2)}) collective-permute-start(bf16[4,128,128]{2,1,0:T(8,128)(2,1)S(1)} %copy-done.13), channel_id=1, source_target_pairs={{0,24},{4,28},{1,25},{5,29},{2,26},{6,30},{3,27},{7,31}} | collective-permute-start | bytes 393224 | tf_op jit(solution)/shard_map/ppermute | solution.py:323
  131.6 20.9 %collective-permute-start.19 = (bf16[256,512]{1,0:T(8,128)(2,1)}, bf16[256,512]{1,0:T(8,128)(2,1)}, u32[]{:S(2)}, u32[]{:S(2)}) collective-permute-start(bf16[256,512]{1,0:T(8,128)(2,1)} %fusion.3), channel_id=1, source_target_pairs={{0,16},{4,20},{16,24},{20,28},{24,8},{28,12},{8,0},{12,4},{1,17},{... | collective-permute-start | bytes 786440 | tf_op jit(solution)/shard_map/ppermute | solution.py:422
  137.5 39.2 %collective-permute-start.24 = (bf16[4,128,128]{2,1,0:T(8,128)(2,1)}, bf16[4,128,128]{2,1,0:T(8,128)(2,1)}, u32[]{:S(2)}, u32[]{:S(2)}) collective-permute-start(bf16[4,128,128]{2,1,0:T(8,128)(2,1)} %get-tuple-element.73), channel_id=1, source_target_pairs={{0,4},{4,0},{8,12},{12,8},{16,20},{20,16},{24,28},{28,24},{1,5},{5... | collective-permute-start | bytes 393224 | tf_op jit(solution)/shard_map/ppermute | solution.py:301
  139.7 23.0 %collective-permute-start.18 = (bf16[256,512]{1,0:T(8,128)(2,1)S(1)}, bf16[256,512]{1,0:T(8,128)(2,1)}, u32[]{:S(2)}, u32[]{:S(2)}) collective-permute-start(bf16[256,512]{1,0:T(8,128)(2,1)S(1)} %fusion.2), channel_id=1, source_target_pairs={{0,16},{4,20},{16,24},{20,28},{24,8},{28,12},{8,0},{12,4},{1,17},{... | collective-permute-start | bytes 786440 | tf_op jit(solution)/shard_map/ppermute | solution.py:422
  151.6 12.3 %collective-permute-start.16 = (bf16[1,1024,256]{2,1,0:T(8,128)(2,1)}, bf16[1,1024,256]{2,1,0:T(8,128)(2,1)}, u32[]{:S(2)}, u32[]{:S(2)}) collective-permute-start(bf16[1,1024,256]{2,1,0:T(8,128)(2,1)} %bitcast.71), channel_id=1, source_target_pairs={{0,2},{1,3},{2,0},{3,1},{4,6},{5,7},{6,4},{7,5},{8,10},{9,11},{10,... | collective-permute-start | bytes 1572872 | tf_op jit(solution)/shard_map/ppermute | solution.py:304
  154.2 26.4 %collective-permute-start.28 = (bf16[256,512]{1,0:T(8,128)(2,1)}, bf16[256,512]{1,0:T(8,128)(2,1)S(1)}, u32[]{:S(2)}, u32[]{:S(2)}) collective-permute-start(bf16[256,512]{1,0:T(8,128)(2,1)} %fusion.1), channel_id=1, source_target_pairs={{0,16},{4,20},{16,24},{20,28},{24,8},{28,12},{8,0},{12,4},{1,17},{... | collective-permute-start | bytes 786440 | tf_op jit(solution)/shard_map/ppermute | solution.py:422
  161.5 12.7 %collective-permute-start.25 = (bf16[1,1024,256]{2,1,0:T(8,128)(2,1)}, bf16[1,1024,256]{2,1,0:T(8,128)(2,1)S(1)}, u32[]{:S(2)}, u32[]{:S(2)}) collective-permute-start(bf16[1,1024,256]{2,1,0:T(8,128)(2,1)} %bitcast.72), channel_id=1, source_target_pairs={{0,2},{1,3},{2,0},{3,1},{4,6},{5,7},{6,4},{7,5},{8,10},{9,11},{10,... | collective-permute-start | bytes 1572872 | tf_op jit(solution)/shard_map/ppermute | solution.py:304
  163.7 16.8 %collective-permute-start.29 = (bf16[256,512]{1,0:T(8,128)(2,1)S(1)}, bf16[256,512]{1,0:T(8,128)(2,1)S(1)}, u32[]{:S(2)}, u32[]{:S(2)}) collective-permute-start(bf16[256,512]{1,0:T(8,128)(2,1)S(1)} %fusion), channel_id=1, source_target_pairs={{0,16},{4,20},{16,24},{20,28},{24,8},{28,12},{8,0},{12,4},{1,17},{... | collective-permute-start | bytes 786440 | tf_op jit(solution)/shard_map/ppermute | solution.py:422
  165.9 18.8 %collective-permute-start.26 = (bf16[512,256]{1,0:T(8,128)(2,1)}, bf16[512,256]{1,0:T(8,128)(2,1)S(1)}, u32[]{:S(2)}, u32[]{:S(2)}) collective-permute-start(bf16[512,256]{1,0:T(8,128)(2,1)} %get-tuple-element.85), channel_id=1, source_target_pairs={{0,4},{4,0},{8,12},{12,8},{16,20},{20,16},{24,28},{28,24},{1,5},{5... | collective-permute-start | bytes 786440 | tf_op jit(solution)/shard_map/ppermute | solution.py:301
  175.0 9.6 %collective-permute-start.27 = (bf16[512,256]{1,0:T(8,128)(2,1)}, bf16[512,256]{1,0:T(8,128)(2,1)S(1)}, u32[]{:S(2)}, u32[]{:S(2)}) collective-permute-start(bf16[512,256]{1,0:T(8,128)(2,1)} %get-tuple-element.87), channel_id=1, source_target_pairs={{0,4},{4,0},{8,12},{12,8},{16,20},{20,16},{24,28},{28,24},{1,5},{5... | collective-permute-start | bytes 786440 | tf_op jit(solution)/shard_map/ppermute | solution.py:301
  (23 other events, 187.3 us)
Sparse Core Ops, SparseCore 0:
  10.1 40.3 all-gather.4
  62.8 25.0 all-gather.6

commit v5 on v4

v5 whole, which is shorter than its diff:
```python
import functools
import math

import jax
import jax.numpy as jnp
from jax import lax
from jax.experimental import pallas as pl
from jax.experimental.pallas import tpu as pltpu
from jax.sharding import PartitionSpec as P

DH = 128
F32, BF16 = jnp.float32, jnp.bfloat16
VMEM = pl.BlockSpec(memory_space=pltpu.VMEM)
SMEM = pl.BlockSpec(memory_space=pltpu.SMEM)
ANY = pl.BlockSpec(memory_space=pl.ANY)


def dot(a, b, ca, cb):
    return lax.dot_general(a, b, (((ca,), (cb,)), ((), ())), preferred_element_type=F32)


def call(kernel, **kw):
    hint = pl.CostEstimate(flops=1, bytes_accessed=1, transcendentals=0)
    return pl.pallas_call(kernel, cost_estimate=hint, **kw)


def states_kernel(a_ref, b_ref, out_ref):
    for hd in range(a_ref.shape[1] // DH):
        at = slice(hd * DH, (hd + 1) * DH)
        out_ref[hd] = dot(a_ref[:, at], b_ref[:, at], 0, 0).astype(BF16)


def states(a, b):
    heads = a.shape[1] // DH
    return call(
        states_kernel,
        in_specs=[VMEM] * 2,
        out_specs=VMEM,
        out_shape=jax.ShapeDtypeStruct((heads, DH, DH), BF16),
        name="states",
    )(a, b)


def split_kernel(per, par_ref, x_ref, own_ref, theirs_ref):
    width = x_ref.shape[1] // (2 * per)
    for k in range(2):
        for i in range(per):
            block = x_ref[:, (2 * i + k) * width : (2 * i + k + 1) * width]

            @pl.when(par_ref[0] == k)
            def _():
                own_ref[i] = block

            @pl.when(par_ref[0] != k)
            def _():
                theirs_ref[i] = block


def split(par, x, per):
    width = x.shape[1] // (2 * per)
    out = jax.ShapeDtypeStruct((per, x.shape[0], width), x.dtype)
    return call(
        functools.partial(split_kernel, per),
        in_specs=[SMEM, VMEM],
        out_specs=[VMEM] * 2,
        out_shape=[out, out],
        name="split",
    )(par, x)


def inside_kernel(q_ref, k_ref, v_ref, g_ref, vo_ref, qo_ref, ko_ref):
    q, k, v, g = q_ref[...], k_ref[...], v_ref[...], g_ref[...]
    n = q.shape[0]
    rows = lax.broadcasted_iota(jnp.int32, (n, n), 0)
    cols = lax.broadcasted_iota(jnp.int32, (n, n), 1)
    causal = rows >= cols
    ks = jnp.where(causal, dot(q, k, 1, 1), 0.0).astype(BF16)
    vo_ref[...] = dot(ks, g, 0, 0)
    gs = jnp.where(causal, dot(g, v, 1, 1), 0.0).astype(BF16)
    qo_ref[...] = dot(gs, k, 1, 0)
    ko_ref[...] = dot(gs, q, 0, 0)


def inside(q, k, v, g):
    n, cols = q.shape
    spec = pl.BlockSpec((n, DH), lambda h: (0, h))
    out = jax.ShapeDtypeStruct((n, cols), F32)
    return call(
        inside_kernel,
        grid=(cols // DH,),
        in_specs=[spec] * 4,
        out_specs=[spec] * 3,
        out_shape=[out] * 3,
        name="inside",
    )(q, k, v, g)


def added(count, got, hd):
    total = jnp.zeros(got[0].shape[1:], F32)
    for i, x in enumerate(got):
        total = total + jnp.where(i < count, x[hd].astype(F32), 0.0)
    return total


def far_kernel(count_ref, *refs):
    got, out_ref = refs[:-1], refs[-1]
    for hd in range(out_ref.shape[0]):
        out_ref[hd] = added(count_ref[0], got, hd).astype(BF16)


def far_states(count, got):
    return call(
        far_kernel,
        in_specs=[SMEM] + [VMEM] * len(got),
        out_specs=VMEM,
        out_shape=jax.ShapeDtypeStruct(got[0].shape, BF16),
        name="far",
    )(count, *got)


def entering(par, kind, hd, count, near, got_far, *got):
    close = jnp.where(par == kind, near[hd].astype(F32), 0.0)
    total = added(count, got, hd) + got_far[hd].astype(F32) + close
    hi = total.astype(BF16)
    return hi, (total - hi.astype(F32)).astype(BF16)


def value_kernel(factor, par_ref, count_ref, k_ref, vi_ref, *refs):
    ends, out_ref = refs[:-1], refs[-1]
    for hd in range(k_ref.shape[1] // DH):
        at = slice(hd * DH, (hd + 1) * DH)
        hi, lo = entering(par_ref[0], 0, hd, count_ref[0], *ends)
        k = k_ref[:, at]
        total = vi_ref[:, at] + (dot(k, hi, 1, 0) + dot(k, lo, 1, 0))
        out_ref[:, at] = (factor * total).astype(BF16)


def finish_value(factor, par, count, k, vi, later):
    return call(
        functools.partial(value_kernel, factor),
        in_specs=[SMEM] * 2 + [VMEM] * (2 + len(later)),
        out_specs=VMEM,
        out_shape=jax.ShapeDtypeStruct(k.shape, BF16),
        name="finish_value",
    )(par, count, k, vi, *later)


def others_kernel(factor, par_ref, counts_ref, g_ref, v_ref, qi_ref, ki_ref, *refs):
    half = (len(refs) - 2) // 2
    later, prior, outs = refs[:half], refs[half : 2 * half], refs[2 * half :]
    for hd in range(g_ref.shape[1] // DH):
        at = slice(hd * DH, (hd + 1) * DH)
        for kind, x_ref, i_ref, ends in (
            (1, g_ref, qi_ref, prior),
            (0, v_ref, ki_ref, later),
        ):
            hi, lo = entering(par_ref[0], kind, hd, counts_ref[kind], *ends)
            x = x_ref[:, at]
            total = i_ref[:, at] + (dot(x, hi, 1, 1) + dot(x, lo, 1, 1))
            outs[1 - kind][:, at] = (factor * total).astype(BF16)


def finish_others(factor, par, counts, g, v, qi, ki, later, prior):
    out = jax.ShapeDtypeStruct(g.shape, BF16)
    return call(
        functools.partial(others_kernel, factor),
        in_specs=[SMEM] * 2 + [VMEM] * (4 + len(later) + len(prior)),
        out_specs=[VMEM] * 2,
        out_shape=[out] * 2,
        name="finish_others",
    )(par, counts, g, v, qi, ki, *later, *prior)


def piece_kernel(count, offs_ref, subs_ref, a_ref, b_ref, *refs):
    own, theirs = refs[:count], refs[count : 2 * count]
    out_ref, x, y, at, bt, sems = refs[2 * count :]
    step, steps = pl.program_id(0), pl.num_programs(0)
    slot = lax.rem(step, 2)

    def fetch(k, to):
        for i in range(count):

            @pl.when(offs_ref[k] == i)
            def _():
                for j, (src, dst) in enumerate(((own, x), (theirs, y))):
                    pltpu.make_async_copy(
                        src[i].at[subs_ref[k]], dst.at[to], sems.at[j, to]
                    ).start()

    @pl.when(step == 0)
    def _():
        fetch(0, 0)

    @pl.when(step + 1 < steps)
    def _():
        fetch(step + 1, 1 - slot)

    @pl.when(step == 0)
    def _():
        at[...] = a_ref[...].T
        bt[...] = b_ref[...].T

    for j, (src, dst) in enumerate(((own, x), (theirs, y))):
        pltpu.make_async_copy(src[0].at[0], dst.at[slot], sems.at[j, slot]).wait()
    total = dot(at[...], x[slot], 1, 0) + dot(bt[...], y[slot], 1, 0)
    out_ref[0] = total.astype(out_ref.dtype)


def pieces(offs, subs, a, b, own, theirs):
    steps = offs.shape[0]
    count = len(own)
    _, n, width = own[0].shape
    cols = a.shape[1]
    return call(
        functools.partial(piece_kernel, count),
        grid=(steps,),
        in_specs=[SMEM] * 2 + [VMEM] * 2 + [ANY] * (2 * count),
        out_specs=pl.BlockSpec((1, cols, width), lambda s: (s, 0, 0)),
        out_shape=jax.ShapeDtypeStruct((steps, cols, width), BF16),
        scratch_shapes=[
            pltpu.VMEM((2, n, width), BF16),
            pltpu.VMEM((2, n, width), BF16),
            pltpu.VMEM((cols, n), BF16),
            pltpu.VMEM((cols, n), BF16),
            pltpu.SemaphoreType.DMA((2, 2)),
        ],
        name="pieces",
    )(offs, subs, a, b, *own, *theirs)


def weight_kernel(scale, x_ref, out_ref):
    out_ref[...] = x_ref[...].astype(F32).T * scale


def finish_weight(scale, x):
    return call(
        functools.partial(weight_kernel, scale),
        in_specs=[VMEM],
        out_specs=VMEM,
        out_shape=jax.ShapeDtypeStruct(x.shape[::-1], F32),
        name="finish_weight",
    )(x)


def odd_kernel(at_ref, w_ref, theirs_ref, mine_ref, out_ref):
    n = mine_ref.shape[0]
    w = w_ref[...].reshape(-1, w_ref.shape[2])
    out_ref[0, :n] = dot(theirs_ref[...], w, 1, 1).astype(BF16)
    out_ref[0, n:] = dot(mine_ref[...], w, 1, 1).astype(BF16)


def odd_parts(at, per, w, theirs, mine):
    _, rows, cols = w.shape
    n = mine.shape[0]
    steps = at.shape[0]
    whole = pl.BlockSpec((n, cols), lambda s, a: (0, 0))
    return call(
        odd_kernel,
        grid_spec=pltpu.PrefetchScalarGridSpec(
            num_scalar_prefetch=1,
            grid=(steps,),
            in_specs=[
                pl.BlockSpec((per, rows, cols), lambda s, a: (a[s], 0, 0)),
                whole,
                whole,
            ],
            out_specs=pl.BlockSpec((1, 2 * n, per * rows), lambda s, a: (s, 0, 0)),
        ),
        out_shape=jax.ShapeDtypeStruct((steps, 2 * n, per * rows), BF16),
        name="odd_parts",
    )(at, w, theirs, mine)


def even_kernel(go, at_ref, w_ref, theirs_ref, mine_ref, got_ref, send_ref, keep_ref):
    step = pl.program_id(0)
    n = mine_ref.shape[0]
    half = got_ref.shape[2]
    part = go[1]
    w = w_ref[...].reshape(-1, w_ref.shape[2])[part * half : (part + 1) * half]
    for side, x_ref in enumerate((theirs_ref, mine_ref)):
        to = slice(side * n, (side + 1) * n)
        total = dot(x_ref[...], w, 1, 1) + got_ref[0, to].astype(F32)

        @pl.when(step < go[0])
        def _():
            send_ref[0, to] = total.astype(BF16)

        @pl.when(step >= go[0])
        def _():
            keep_ref[0, to] = total


def even_parts(part, at, per, w, theirs, mine, got):
    _, rows, cols = w.shape
    n = mine.shape[0]
    steps = at.shape[0]
    go = steps // 2
    half = per * rows // 2
    whole = pl.BlockSpec((n, cols), lambda s, a: (0, 0))
    block = (1, 2 * n, half)
    return call(
        functools.partial(even_kernel, (go, part)),
        grid_spec=pltpu.PrefetchScalarGridSpec(
            num_scalar_prefetch=1,
            grid=(steps,),
            in_specs=[
                pl.BlockSpec((per, rows, cols), lambda s, a: (a[s], 0, 0)),
                whole,
                whole,
                pl.BlockSpec(block, lambda s, a: (s, 0, part)),
            ],
            out_specs=[
                pl.BlockSpec(block, lambda s, a: (jnp.minimum(s, go - 1), 0, 0)),
                pl.BlockSpec(block, lambda s, a: (jnp.maximum(s - go, 0), 0, 0)),
            ],
        ),
        out_shape=[
            jax.ShapeDtypeStruct((go, 2 * n, half), BF16),
            jax.ShapeDtypeStruct((steps - go, 2 * n, half), F32),
        ],
        name="even_parts",
    )(at, w, theirs, mine, got)


def swap_kernel(keep_ref, got_ref, out_ref):
    out_ref[...] = (keep_ref[...] + got_ref[...].astype(F32)).astype(BF16)


def for_partner(keep, got):
    n, half = keep.shape[0] // 2, keep.shape[1]
    spec = pl.BlockSpec((n, half), lambda s: (0, 0))
    return call(
        swap_kernel,
        grid=(1,),
        in_specs=[spec] * 2,
        out_specs=spec,
        out_shape=jax.ShapeDtypeStruct((n, half), BF16),
        name="for_partner",
    )(keep, got)


def join_kernel(rows, par_ref, *refs):
    *refs, out_ref = refs
    count = len(refs) // 3
    half = refs[0].shape[1]
    for part in range(count):
        keep, got, other = refs[part], refs[count + part], refs[2 * count + part]
        mine = (keep[...] + got[...].astype(F32)).astype(BF16)
        both = (mine, other[...])
        for f in range(0, half, min(rows, half)):
            size = min(rows, half)
            block, at = divmod(part * half + f, rows)
            for k in range(2):
                for flip in range(2):

                    @pl.when(par_ref[0] == (k ^ flip))
                    def _():
                        to = (2 * block + k) * rows + at
                        out_ref[:, to : to + size] = both[flip][:, f : f + size]


def join(par, rows, keep, got, other):
    n, half = other[0].shape
    lower = pl.BlockSpec((n, half), lambda s: (1, 0))
    whole = pl.BlockSpec((n, half), lambda s: (0, 0))
    count = len(keep)
    out = (n, 2 * count * half)
    return call(
        functools.partial(join_kernel, rows),
        grid=(1,),
        in_specs=[SMEM] + [lower] * (2 * count) + [whole] * count,
        out_specs=pl.BlockSpec(out, lambda s: (0, 0)),
        out_shape=jax.ShapeDtypeStruct(out, BF16),
        name="join",
    )(par, *keep, *got, *other)


def after(x, *earlier):
    return lax.optimization_barrier((x, *earlier))[0]


def local(queries, keys, values, out_grad, inputs, value_weight):
    length, cols = queries.shape
    n_ctx, n_head = lax.axis_size("ctx"), lax.axis_size("head")
    pairs = n_ctx // 2
    ctx, head = lax.axis_index("ctx"), lax.axis_index("head")
    parity, pair = ctx % 2, ctx // 2
    par = parity.astype(jnp.int32).reshape(1)
    factor = 1.0 / math.sqrt(DH * length * n_ctx)
    lines = [[2 * i + k for i in range(pairs)] for k in range(2)]
    def partner(x):
        return lax.ppermute(x, "ctx", [(i, i ^ 1) for i in range(n_ctx)])

    def across(x, bit):
        return lax.ppermute(x, "head", [(i, i ^ bit) for i in range(n_head)])

    weight = lax.all_gather(value_weight, "ctx", axis_index_groups=lines)

    per = n_ctx // n_head // 2
    own, theirs = split(par, inputs, per)

    def line_move(x, by):
        moves = [
            (i, i + 2 * by) for i in range(n_ctx) if 0 <= i + 2 * by < n_ctx
        ]
        return lax.ppermute(x, "ctx", moves)

    def far_of(x, sign):
        got = [line_move(x, sign * d) for d in range(1, pairs)]
        count = pairs - 1 - pair if sign < 0 else pair
        count = count.astype(jnp.int32).reshape(1)
        return count, got, far_states(count, got)

    qg = states(queries, out_grad)
    count_qg, got_qg, far_qg = far_of(qg, -1)
    kv = states(keys, values)
    near = partner(jnp.stack([qg, kv]))
    theirs = partner(theirs)
    later = (near[0], partner(far_qg), *got_qg)

    own, theirs = [own], [theirs]
    offsets = [0]
    bit = n_head // 2
    while bit:
        own = own + [across(r, bit) for r in own]
        theirs = theirs + [across(r, bit) for r in theirs]
        offsets = offsets + [o ^ bit for o in offsets]
        bit //= 2
    own = [own[offsets.index(i)] for i in range(n_head)]
    theirs = [theirs[offsets.index(i)] for i in range(n_head)]

    vi, qi, ki = inside(queries, keys, values, out_grad)
    mine = finish_value(factor, par, count_qg, keys, vi, later)
    other = partner(mine)
    count_kv, got_kv, far_kv = far_of(after(kv, far_qg), 1)
    prior = (near[1], partner(after(far_kv, other)), *got_kv)

    which = jnp.arange(pairs, dtype=jnp.int32)
    found = pieces((which // per) ^ head, which % per, mine, other, own, theirs)
    summed = lax.psum_scatter(found, "ctx", axis_index_groups=lines)
    weight_grad = finish_weight(1.0 / math.sqrt(length * n_ctx), summed)

    odd = jnp.asarray([o for o in range(1, n_head, 2)][::-1], jnp.int32) ^ head
    even = jnp.asarray([o for o in range(0, n_head, 2)][::-1], jnp.int32) ^ head
    got = across(odd_parts(odd, per, weight, after(other, found), mine), 1)
    keep, back = [], []
    token = got
    for part in range(2):
        vals = after(other, token)
        send, kept = even_parts(part, even, per, weight, vals, mine, got)
        token = send
        keep.append(kept[0])
        back.append(across(send[0], 2))
    query_grad, key_grad = finish_others(
        factor,
        par,
        jnp.concatenate([count_qg, count_kv]),
        after(out_grad, token),
        values,
        qi,
        ki,
        later,
        prior,
    )
    swapped = [partner(for_partner(k, b)) for k, b in zip(keep, back)]
    input_grad = join(par, value_weight.shape[0], keep, back, swapped)
    return (query_grad, key_grad, input_grad, weight_grad)


def solution(mesh):
    spec = P("ctx", "head")
    return jax.shard_map(
        local, mesh=mesh, in_specs=(spec,) * 6, out_specs=(spec,) * 4, check_vma=False
    )
```

time: 196 us -> 165 us (0.84)
  the two profiles are of different devices: /device:TPU:0 before, /device:TPU:10 now
where the time goes in v5:
time: 165 us; the launch traced here: 164 us
  waiting for transfers between devices  60.7 us (37%)
  Pallas kernels  54.5 us (33%)
  starting transfers between devices  22.1 us (13%)
  between operations  14.2 us (9%)
  local copies, waits for them, and re-layouts  9.16 us (6%)
  other arithmetic  3.26 us (2%)
    ppermute x7, waiting for transfers between devices, partner(): return lax.ppermute(x, 'ctx', [(i, i ^ 1) for i in range(n_ctx)])  23.4 us
    ppermute x9, waiting for transfers between devices, across(): return lax.ppermute(x, 'head', [(i, i ^ bit) for i in range(n_head)])  20.2 us
    ppermute x6, waiting for transfers between devices, line_move(): return lax.ppermute(x, 'ctx', moves)  16.3 us
    pallas_call x2, Pallas kernels, even_parts(): call(functools.partial(even_kernel, (go, part)), grid_spec=pltpu.Prefetch...  11 us
    ppermute x6, starting transfers between devices, line_move(): return lax.ppermute(x, 'ctx', moves)  8.3 us
    ppermute x7, starting transfers between devices, partner(): return lax.ppermute(x, 'ctx', [(i, i ^ 1) for i in range(n_ctx)])  7.97 us
    unnamed x46, local copies, waits for them, and re-layouts  7.87 us
    pallas_call x1, Pallas kernels, pieces(): call(functools.partial(piece_kernel, count), grid=(steps,), in_specs=[SME...  6.93 us
  transfers between devices with their start and end apart: 24, of which 9 were waited for; matrix products, arithmetic and copies ran while one was open for 3% of the time, Pallas kernels for 32%

profile of v5, /device:TPU:10, one launch (start us, length us, event | category | flops | bytes accessed | tf_op | source)
XLA Modules:
  0.0 163.9 jit_solution(10581842303016558877)
XLA Ops:
  8.0 2.3 %split.1 = (bf16[1,512,512]{2,1,0:T(8,128)(2,1)}, bf16[1,512,512]{2,1,0:T(8,128)(2,1)}) custom-call(s32[1]{0:T(128)} %bitcast.par_ref, bf16[512,1024]{1,0:T(8,128)(2,1)} %x_ref.1), custom_call_target="tpu_custom_call" | custom-call | flops 1 | bytes 1 | tf_op jit(solution)/shard_map/split/pallas_call | solution.py:62
  10.8 2.2 %states.2 = bf16[4,128,128]{2,1,0:T(8,128)(2,1)} custom-call(bf16[512,512]{1,0:T(8,128)(2,1)} %a_ref.2, bf16[512,512]{1,0:T(8,128)(2,1)} %g_ref.2), custom_call_target="tpu_custom_call" | custom-call | flops 1 | bytes 1 | tf_op jit(solution)/shard_map/states/pallas_call | solution.py:35
  13.8 1.6 collective-permute-start.7
  15.4 2.2 %states.3 = bf16[4,128,128]{2,1,0:T(8,128)(2,1)} custom-call(bf16[512,512]{1,0:T(8,128)(2,1)} %k_ref.3, bf16[512,512]{1,0:T(8,128)(2,1)} %v_ref.3), custom_call_target="tpu_custom_call" | custom-call | flops 1 | bytes 1 | tf_op jit(solution)/shard_map/states/pallas_call | solution.py:35
  17.6 6.6 %collective-permute-done.9.refs_4_ = bf16[1,512,512]{2,1,0:T(8,128)(2,1)S(1)} collective-permute-done((bf16[1,512,512]{2,1,0:T(8,128)(2,1)}, bf16[1,512,512]{2,1,0:T(8,128)(2,1)S(1)}, u32[]{:S(2)}, u32[]{:S(2)}) %collective-permute-start.9) | collective-permute-done | bytes 524320 | tf_op jit(solution)/shard_map/ppermute | solution.py:392
  28.6 2.4 %collective-permute-start.1 = (bf16[4,128,128]{2,1,0:T(8,128)(2,1)}, bf16[4,128,128]{2,1,0:T(8,128)(2,1)S(1)}, u32[]{:S(2)}, u32[]{:S(2)}) collective-permute-start(bf16[4,128,128]{2,1,0:T(8,128)(2,1)} %states.2), channel_id=1, source_target_pairs={{8,0},{12,4},{16,8},{20,12},{24,16},{28,20},{9,1},{13,5},{17,9},{2... | collective-permute-start | bytes 393224 | tf_op jit(solution)/shard_map/ppermute | solution.py:406
  31.0 6.1 %inside.1 = (f32[512,512]{1,0:T(8,128)}, f32[512,512]{1,0:T(8,128)}, f32[512,512]{1,0:T(8,128)}) custom-call(bf16[512,512]{1,0:T(8,128)(2,1)} %a_ref.2, bf16[512,512]{1,0:T(8,128)(2,1)} %k_ref.3, bf16[512,512]{1,0:T(8,128)(2,1)} %v_ref.3, bf16[512,512]{1,0:T(8,128)(2,1)} %g_ref.2), custom_call_target="tpu_custom_call" | custom-call | flops 1 | bytes 1 | tf_op jit(solution)/shard_map/inside/pallas_call | solution.py:88
  37.1 2.3 %collective-permute-done.2.refs_1_.refs_3_ = bf16[4,128,128]{2,1,0:T(8,128)(2,1)S(1)} collective-permute-done((bf16[4,128,128]{2,1,0:T(8,128)(2,1)}, bf16[4,128,128]{2,1,0:T(8,128)(2,1)S(1)}, u32[]{:S(2)}, u32[]{:S(2)}) %collective-permute-start.2) | collective-permute-done | bytes 131104 | tf_op jit(solution)/shard_map/ppermute | solution.py:406
  39.4 14.0 %collective-permute-done.1.refs_0_.refs_2_ = bf16[4,128,128]{2,1,0:T(8,128)(2,1)S(1)} collective-permute-done((bf16[4,128,128]{2,1,0:T(8,128)(2,1)}, bf16[4,128,128]{2,1,0:T(8,128)(2,1)S(1)}, u32[]{:S(2)}, u32[]{:S(2)}) %collective-permute-start.1) | collective-permute-done | bytes 131104 | tf_op jit(solution)/shard_map/ppermute | solution.py:406
  54.0 1.8 %far.2 = bf16[4,128,128]{2,1,0:T(8,128)(2,1)} custom-call(s32[1]{0:T(128)} %bitcast.1.count_ref, bf16[4,128,128]{2,1,0:T(8,128)(2,1)} %copy-done.6, bf16[4,128,128]{2,1,0:T(8,128)(2,1)} %copy-done.5, bf16[4,128,128]{2,1,0:T(8,128)(2,1)} %copy-done.4), custom_call_target="tpu_custom_call" | custom-call | flops 1 | bytes 1 | tf_op jit(solution)/shard_map/far/pallas_call | solution.py:112
  55.8 2.3 %collective-permute-start.4 = (bf16[4,128,128]{2,1,0:T(8,128)(2,1)}, bf16[4,128,128]{2,1,0:T(8,128)(2,1)S(1)}, u32[]{:S(2)}, u32[]{:S(2)}) collective-permute-start(bf16[4,128,128]{2,1,0:T(8,128)(2,1)} %far.2), channel_id=1, source_target_pairs={{0,4},{4,0},{8,12},{12,8},{16,20},{20,16},{24,28},{28,24},{1,5},{5... | collective-permute-start | bytes 393224 | tf_op jit(solution)/shard_map/ppermute | solution.py:392
  58.9 2.4 %collective-permute-done.4.refs_1_ = bf16[4,128,128]{2,1,0:T(8,128)(2,1)S(1)} collective-permute-done((bf16[4,128,128]{2,1,0:T(8,128)(2,1)}, bf16[4,128,128]{2,1,0:T(8,128)(2,1)S(1)}, u32[]{:S(2)}, u32[]{:S(2)}) %collective-permute-start.4) | collective-permute-done | bytes 131104 | tf_op jit(solution)/shard_map/ppermute | solution.py:392
  61.9 2.8 %finish_value.1.a_ref.mine_ref = bf16[512,512]{1,0:T(8,128)(2,1)} custom-call(s32[1]{0:T(128)} %bitcast.par_ref, s32[1]{0:T(128)} %bitcast.1.count_ref, bf16[512,512]{1,0:T(8,128)(2,1)} %k_ref.3, f32[512,512]{1,0:T(8,128)} %get-tuple-element.21.vi_ref, bf16[4,128,128]{2,1,0:T(8,128)(2,1)} %get-tuple-element.39.refs_0_, bf16[4,128,128]{2,1,0:T(8,128)(2,1)} %copy-done.7, ...), custom_call_target="tpu_custom_call" | custom-call | flops 1 | bytes 1 | tf_op jit(solution)/shard_map/finish_value/pallas_call | solution.py:139
  64.8 2.0 %collective-permute-start.5 = (bf16[512,512]{1,0:T(8,128)(2,1)}, bf16[512,512]{1,0:T(8,128)(2,1)S(1)}, u32[]{:S(2)}, u32[]{:S(2)}) collective-permute-start(bf16[512,512]{1,0:T(8,128)(2,1)} %finish_value.1.a_ref.mine_ref), channel_id=1, source_target_pairs={{0,4},{4,0},{8,12},{12,8},{16,20},{20,16},{24,28},{28,24},{1,5},{5... | collective-permute-start | bytes 1572872 | tf_op jit(solution)/shard_map/ppermute | solution.py:392
  68.0 9.1 %collective-permute-done.5.b_ref.theirs_ref = bf16[512,512]{1,0:T(8,128)(2,1)S(1)} collective-permute-done((bf16[512,512]{1,0:T(8,128)(2,1)}, bf16[512,512]{1,0:T(8,128)(2,1)S(1)}, u32[]{:S(2)}, u32[]{:S(2)}) %collective-permute-start.5) | collective-permute-done | bytes 524320 | tf_op jit(solution)/shard_map/ppermute | solution.py:392
  77.9 6.9 %pieces.1 = bf16[4,512,512]{2,1,0:T(8,128)(2,1)} custom-call(s32[4]{0:T(128)} %iota_xor_fusion.offs_ref, s32[4]{0:T(128)} %rem.32.subs_ref, bf16[512,512]{1,0:T(8,128)(2,1)} %finish_value.1.a_ref.mine_ref, bf16[512,512]{1,0:T(8,128)(2,1)} %copy-done.1, bf16[1,512,512]{2,1,0:T(8,128)(2,1)} %get-tuple-element.22.refs_0_, bf16[1,512,512]{2,1,0:T(8,128)(2,1)} %copy-done.16, ...), custom_call_target="tpu_custom_call" | custom-call | flops 1 | bytes 1 | tf_op jit(solution)/shard_map/pieces/pallas_call | solution.py:214
  86.0 4.7 %odd_parts.1 = bf16[2,1024,512]{2,1,0:T(8,128)(2,1)} custom-call(s32[2]{0:T(128)} %broadcast_xor_fusion.at_ref, bf16[4,512,512]{2,1,0:T(8,128)(2,1)} %bitcast.15, bf16[512,512]{1,0:T(8,128)(2,1)} %copy-done.1, bf16[512,512]{1,0:T(8,128)(2,1)} %finish_value.1.a_ref.mine_ref), custom_call_target="tpu_custom_call" | custom-call | flops 1 | bytes 1 | tf_op jit(solution)/shard_map/odd_parts/pallas_call | solution.py:257
  91.2 3.9 %collective-permute-done.13.got_ref = bf16[2,1024,512]{2,1,0:T(8,128)(2,1)S(1)} collective-permute-done((bf16[2,1024,512]{2,1,0:T(8,128)(2,1)}, bf16[2,1024,512]{2,1,0:T(8,128)(2,1)S(1)}, u32[]{:S(2)}, u32[]{:S(2)}) %collective-permute-start.13) | collective-permute-done | bytes 2097184 | tf_op jit(solution)/shard_map/ppermute | solution.py:395
  96.4 5.4 %even_parts.2 = (bf16[1,1024,256]{2,1,0:T(8,128)(2,1)}, f32[1,1024,256]{2,1,0:T(8,128)}) custom-call(s32[2]{0:T(128)} %broadcast_xor_fusion.1.at_ref, bf16[4,512,512]{2,1,0:T(8,128)(2,1)} %bitcast.16, bf16[512,512]{1,0:T(8,128)(2,1)} %copy-done.1, bf16[512,512]{1,0:T(8,128)(2,1)} %finish_value.1.a_ref.mine_ref, bf16[2,1024,512]{2,1,0:T(8,128)(2,1)} %copy-done), custom_call_target="tpu_custom_call" | custom-call | flops 1 | bytes 1 | tf_op jit(solution)/shard_map/even_parts/pallas_call | solution.py:301
  101.8 5.5 %even_parts.3 = (bf16[1,1024,256]{2,1,0:T(8,128)(2,1)}, f32[1,1024,256]{2,1,0:T(8,128)}) custom-call(s32[2]{0:T(128)} %broadcast_xor_fusion.1.at_ref, bf16[4,512,512]{2,1,0:T(8,128)(2,1)} %bitcast.17, bf16[512,512]{1,0:T(8,128)(2,1)} %copy-done.1, bf16[512,512]{1,0:T(8,128)(2,1)} %finish_value.1.a_ref.mine_ref, bf16[2,1024,512]{2,1,0:T(8,128)(2,1)} %copy-done), custom_call_target="tpu_custom_call" | custom-call | flops 1 | bytes 1 | tf_op jit(solution)/shard_map/even_parts/pallas_call | solution.py:301
  107.5 1.9 %collective-permute-start.18 = (bf16[1024,256]{1,0:T(8,128)(2,1)S(1)}, bf16[1024,256]{1,0:T(8,128)(2,1)S(1)}, u32[]{:S(2)}, u32[]{:S(2)}) collective-permute-start(bf16[1024,256]{1,0:T(8,128)(2,1)S(1)} %bitcast.25), channel_id=1, source_target_pairs={{0,2},{1,3},{2,0},{3,1},{4,6},{5,7},{6,4},{7,5},{8,10},{9,11},{10,... | collective-permute-start | bytes 1572872 | tf_op jit(solution)/shard_map/ppermute | solution.py:395
  111.3 1.9 %collective-permute-start.14 = (bf16[4,128,128]{2,1,0:T(8,128)(2,1)S(1)}, bf16[4,128,128]{2,1,0:T(8,128)(2,1)S(1)}, u32[]{:S(2)}, u32[]{:S(2)}) collective-permute-start(bf16[4,128,128]{2,1,0:T(8,128)(2,1)S(1)} %copy-done.11), channel_id=1, source_target_pairs={{0,8},{4,12},{8,16},{12,20},{16,24},{20,28},{1,9},{5,13},{9,17},{1... | collective-permute-start | bytes 393224 | tf_op jit(solution)/shard_map/ppermute | solution.py:406
  113.3 9.0 %collective-permute-done.19.got_ref.refs_3_ = bf16[1024,256]{1,0:T(8,128)(2,1)S(1)} collective-permute-done((bf16[1024,256]{1,0:T(8,128)(2,1)}, bf16[1024,256]{1,0:T(8,128)(2,1)S(1)}, u32[]{:S(2)}, u32[]{:S(2)}) %collective-permute-start.19) | collective-permute-done | bytes 524320 | tf_op jit(solution)/shard_map/ppermute | solution.py:395
  123.1 1.9 %for_partner.3 = bf16[512,256]{1,0:T(8,128)(2,1)} custom-call(f32[1024,256]{1,0:T(8,128)} %bitcast.20, bf16[1024,256]{1,0:T(8,128)(2,1)} %copy-done.2), custom_call_target="tpu_custom_call" | custom-call | flops 1 | bytes 1 | tf_op jit(solution)/shard_map/for_partner/pallas_call | solution.py:332
  125.4 7.3 %collective-permute-done.18.got_ref.refs_2_ = bf16[1024,256]{1,0:T(8,128)(2,1)S(1)} collective-permute-done((bf16[1024,256]{1,0:T(8,128)(2,1)S(1)}, bf16[1024,256]{1,0:T(8,128)(2,1)S(1)}, u32[]{:S(2)}, u32[]{:S(2)}) %collective-permute-start.18) | collective-permute-done | bytes 524320 | tf_op jit(solution)/shard_map/ppermute | solution.py:395
  133.6 1.8 %for_partner.2 = bf16[512,256]{1,0:T(8,128)(2,1)} custom-call(f32[1024,256]{1,0:T(8,128)} %bitcast.18, bf16[1024,256]{1,0:T(8,128)(2,1)} %copy-done.3), custom_call_target="tpu_custom_call" | custom-call | flops 1 | bytes 1 | tf_op jit(solution)/shard_map/for_partner/pallas_call | solution.py:332
  136.6 1.8 %far.3 = bf16[4,128,128]{2,1,0:T(8,128)(2,1)} custom-call(s32[1]{0:T(128)} %bitcast.2.count_ref, bf16[4,128,128]{2,1,0:T(8,128)(2,1)} %copy-done.10, bf16[4,128,128]{2,1,0:T(8,128)(2,1)} %copy-done.9, bf16[4,128,128]{2,1,0:T(8,128)(2,1)} %copy-done.8), custom_call_target="tpu_custom_call" | custom-call | flops 1 | bytes 1 | tf_op jit(solution)/shard_map/far/pallas_call | solution.py:112
  138.4 1.5 collective-permute-start.17
  140.6 5.4 %collective-permute-done.17.refs_6_ = bf16[4,128,128]{2,1,0:T(8,128)(2,1)S(1)} collective-permute-done((bf16[4,128,128]{2,1,0:T(8,128)(2,1)}, bf16[4,128,128]{2,1,0:T(8,128)(2,1)S(1)}, u32[]{:S(2)}, u32[]{:S(2)}) %collective-permute-start.17) | collective-permute-done | bytes 131104 | tf_op jit(solution)/shard_map/ppermute | solution.py:392
  146.6 4.0 %finish_others.1 = (bf16[512,512]{1,0:T(8,128)(2,1)}, bf16[512,512]{1,0:T(8,128)(2,1)}) custom-call(s32[1]{0:T(128)} %bitcast.par_ref, s32[2]{0:T(128)} %pad_add_fusion.counts_ref, bf16[512,512]{1,0:T(8,128)(2,1)} %g_ref.2, bf16[512,512]{1,0:T(8,128)(2,1)} %v_ref.3, f32[512,512]{1,0:T(8,128)} %get-tuple-element.30.qi_ref, ...), custom_call_target="tpu_custom_call" | custom-call | flops 1 | bytes 1 | tf_op jit(solution)/shard_map/finish_others/pallas_call | solution.py:165
  150.6 2.2 %finish_weight.1 = f32[512,512]{1,0:T(8,128)} custom-call(bf16[512,512]{1,0:T(8,128)(2,1)} %bitcast.22), custom_call_target="tpu_custom_call" | custom-call | flops 1 | bytes 1 | tf_op jit(solution)/shard_map/finish_weight/pallas_call | solution.py:236
  154.3 2.8 %join.1 = bf16[512,1024]{1,0:T(8,128)(2,1)} custom-call(s32[1]{0:T(128)} %bitcast.par_ref, f32[1024,256]{1,0:T(8,128)} %bitcast.19, f32[1024,256]{1,0:T(8,128)} %bitcast.21, bf16[1024,256]{1,0:T(8,128)(2,1)} %copy-done.3, bf16[1024,256]{1,0:T(8,128)(2,1)} %copy-done.2, bf16[512,256]{1,0:T(8,128)(2,1)} %copy-done.18, bf16[512,256]{1,0:T(8,128)(2,1)} %copy-done.17), custom_call_target="tpu_custom_call" | custom-call | flops 1 | bytes 1 | tf_op jit(solution)/shard_map/join/pallas_call | solution.py:368
  (87 shorter events, 21.6 us)
Async XLA Ops:
  7.2 78.8 %all-gather.3.cloned.1.call-start = ((), (), s32[]{:S(2)}) async-start(), calls=%async_computation.2 | async-start | bytes 2621440 | tf_op jit(solution)/shard_map/all_gather | solution.py:397
  7.9 142.7 %reduce-scatter.2.cloned.1.call-start = ((), (), s32[]{:S(2)}) async-start(), calls=%async_computation.1 | async-start | bytes 2621440 | tf_op jit(solution)/shard_map/reduce_scatter | solution.py:440
  10.3 13.9 %collective-permute-start.9 = (bf16[1,512,512]{2,1,0:T(8,128)(2,1)}, bf16[1,512,512]{2,1,0:T(8,128)(2,1)S(1)}, u32[]{:S(2)}, u32[]{:S(2)}) collective-permute-start(bf16[1,512,512]{2,1,0:T(8,128)(2,1)} %get-tuple-element.23), channel_id=1, source_target_pairs={{0,4},{4,0},{8,12},{12,8},{16,20},{20,16},{24,28},{28,24},{1,5},{5... | collective-permute-start | bytes 1572872 | tf_op jit(solution)/shard_map/ppermute | solution.py:392
  13.0 26.4 %copy-start.12 = (bf16[1,512,512]{2,1,0:T(8,128)(2,1)S(1)}, bf16[1,512,512]{2,1,0:T(8,128)(2,1)}, u32[]{:S(2)}) copy-start(bf16[1,512,512]{2,1,0:T(8,128)(2,1)} %get-tuple-element.22.refs_0_) | copy-start | bytes 1572868
  13.0 15.5 %collective-permute-start.3 = (bf16[4,128,128]{2,1,0:T(8,128)(2,1)}, bf16[4,128,128]{2,1,0:T(8,128)(2,1)S(1)}, u32[]{:S(2)}, u32[]{:S(2)}) collective-permute-start(bf16[4,128,128]{2,1,0:T(8,128)(2,1)} %states.2), channel_id=1, source_target_pairs={{24,0},{28,4},{25,1},{29,5},{26,2},{30,6},{27,3},{31,7}} | collective-permute-start | bytes 393224 | tf_op jit(solution)/shard_map/ppermute | solution.py:406
  13.8 53.0 %collective-permute-start.7 = (bf16[1,512,512]{2,1,0:T(8,128)(2,1)}, bf16[1,512,512]{2,1,0:T(8,128)(2,1)S(1)}, u32[]{:S(2)}, u32[]{:S(2)}) collective-permute-start(bf16[1,512,512]{2,1,0:T(8,128)(2,1)} %get-tuple-element.22.refs_0_), channel_id=1, source_target_pairs={{0,2},{1,3},{2,0},{3,1},{4,6},{5,7},{6,4},{7,5},{8,10},{9,11},{10,... | collective-permute-start | bytes 1572872 | tf_op jit(solution)/shard_map/ppermute | solution.py:395
  24.2 42.6 %copy-start.13 = (bf16[1,512,512]{2,1,0:T(8,128)(2,1)}, bf16[1,512,512]{2,1,0:T(8,128)(2,1)S(1)}, u32[]{:S(2)}) copy-start(bf16[1,512,512]{2,1,0:T(8,128)(2,1)S(1)} %collective-permute-done.9.refs_4_) | copy-start | bytes 1572868
  24.2 43.1 %collective-permute-start.11 = (bf16[1,512,512]{2,1,0:T(8,128)(2,1)S(1)}, bf16[1,512,512]{2,1,0:T(8,128)(2,1)S(1)}, u32[]{:S(2)}, u32[]{:S(2)}) collective-permute-start(bf16[1,512,512]{2,1,0:T(8,128)(2,1)S(1)} %collective-permute-done.9.refs_4_), channel_id=1, source_target_pairs={{0,2},{1,3},{2,0},{3,1},{4,6},{5,7},{6,4},{7,5},{8,10},{9,11},{10,... | collective-permute-start | bytes 1572872 | tf_op jit(solution)/shard_map/ppermute | solution.py:395
  26.7 31.5 %collective-permute-start = (bf16[2,4,128,128]{3,2,1,0:T(8,128)(2,1)S(1)}, bf16[2,4,128,128]{3,2,1,0:T(8,128)(2,1)S(1)}, u32[]{:S(2)}, u32[]{:S(2)}) collective-permute-start(bf16[2,4,128,128]{3,2,1,0:T(8,128)(2,1)S(1)} %pad_maximum_fusion), channel_id=1, source_target_pairs={{0,4},{4,0},{8,12},{12,8},{16,20},{20,16},{24,28},{28,24},{1,5},{5... | collective-permute-start | bytes 786440 | tf_op jit(solution)/shard_map/ppermute | solution.py:392
  27.3 12.1 %collective-permute-start.2 = (bf16[4,128,128]{2,1,0:T(8,128)(2,1)}, bf16[4,128,128]{2,1,0:T(8,128)(2,1)S(1)}, u32[]{:S(2)}, u32[]{:S(2)}) collective-permute-start(bf16[4,128,128]{2,1,0:T(8,128)(2,1)} %states.2), channel_id=1, source_target_pairs={{16,0},{20,4},{24,8},{28,12},{17,1},{21,5},{25,9},{29,13},{18,2},{... | collective-permute-start | bytes 393224 | tf_op jit(solution)/shard_map/ppermute | solution.py:406
  28.6 24.8 %copy-start.4 = (bf16[4,128,128]{2,1,0:T(8,128)(2,1)}, bf16[4,128,128]{2,1,0:T(8,128)(2,1)S(1)}, u32[]{:S(2)}) copy-start(bf16[4,128,128]{2,1,0:T(8,128)(2,1)S(1)} %collective-permute-done.3.refs_2_.refs_4_) | copy-start | bytes 393220
  28.6 24.8 %collective-permute-start.1 = (bf16[4,128,128]{2,1,0:T(8,128)(2,1)}, bf16[4,128,128]{2,1,0:T(8,128)(2,1)S(1)}, u32[]{:S(2)}, u32[]{:S(2)}) collective-permute-start(bf16[4,128,128]{2,1,0:T(8,128)(2,1)} %states.2), channel_id=1, source_target_pairs={{8,0},{12,4},{16,8},{20,12},{24,16},{28,20},{9,1},{13,5},{17,9},{2... | collective-permute-start | bytes 393224 | tf_op jit(solution)/shard_map/ppermute | solution.py:406
  39.4 14.0 %copy-start.5 = (bf16[4,128,128]{2,1,0:T(8,128)(2,1)}, bf16[4,128,128]{2,1,0:T(8,128)(2,1)S(1)}, u32[]{:S(2)}) copy-start(bf16[4,128,128]{2,1,0:T(8,128)(2,1)S(1)} %collective-permute-done.2.refs_1_.refs_3_) | copy-start | bytes 393220
  39.4 28.6 %collective-permute-start.6 = (bf16[1,512,512]{2,1,0:T(8,128)(2,1)S(1)}, bf16[1,512,512]{2,1,0:T(8,128)(2,1)S(1)}, u32[]{:S(2)}, u32[]{:S(2)}) collective-permute-start(bf16[1,512,512]{2,1,0:T(8,128)(2,1)S(1)} %copy-done.12), channel_id=1, source_target_pairs={{0,1},{1,0},{2,3},{3,2},{4,5},{5,4},{6,7},{7,6},{8,9},{9,8},{10,11... | collective-permute-start | bytes 1572872 | tf_op jit(solution)/shard_map/ppermute | solution.py:395
  55.8 5.5 %collective-permute-start.4 = (bf16[4,128,128]{2,1,0:T(8,128)(2,1)}, bf16[4,128,128]{2,1,0:T(8,128)(2,1)S(1)}, u32[]{:S(2)}, u32[]{:S(2)}) collective-permute-start(bf16[4,128,128]{2,1,0:T(8,128)(2,1)} %far.2), channel_id=1, source_target_pairs={{0,4},{4,0},{8,12},{12,8},{16,20},{20,16},{24,28},{28,24},{1,5},{5... | collective-permute-start | bytes 393224 | tf_op jit(solution)/shard_map/ppermute | solution.py:392
  64.8 12.3 %collective-permute-start.5 = (bf16[512,512]{1,0:T(8,128)(2,1)}, bf16[512,512]{1,0:T(8,128)(2,1)S(1)}, u32[]{:S(2)}, u32[]{:S(2)}) collective-permute-start(bf16[512,512]{1,0:T(8,128)(2,1)} %finish_value.1.a_ref.mine_ref), channel_id=1, source_target_pairs={{0,4},{4,0},{8,12},{12,8},{16,20},{20,16},{24,28},{28,24},{1,5},{5... | collective-permute-start | bytes 1572872 | tf_op jit(solution)/shard_map/ppermute | solution.py:392
  66.8 10.3 %collective-permute-start.10 = (bf16[1,512,512]{2,1,0:T(8,128)(2,1)S(1)}, bf16[1,512,512]{2,1,0:T(8,128)(2,1)}, u32[]{:S(2)}, u32[]{:S(2)}) collective-permute-start(bf16[1,512,512]{2,1,0:T(8,128)(2,1)S(1)} %collective-permute-done.9.refs_4_), channel_id=1, source_target_pairs={{0,1},{1,0},{2,3},{3,2},{4,5},{5,4},{6,7},{7,6},{8,9},{9,8},{10,11... | collective-permute-start | bytes 1572872 | tf_op jit(solution)/shard_map/ppermute | solution.py:395
  66.8 10.9 %copy-start.14 = (bf16[1,512,512]{2,1,0:T(8,128)(2,1)}, bf16[1,512,512]{2,1,0:T(8,128)(2,1)S(1)}, u32[]{:S(2)}) copy-start(bf16[1,512,512]{2,1,0:T(8,128)(2,1)S(1)} %collective-permute-done.7.refs_2_) | copy-start | bytes 1572868
  66.8 10.3 %collective-permute-start.8 = (bf16[1,512,512]{2,1,0:T(8,128)(2,1)S(1)}, bf16[1,512,512]{2,1,0:T(8,128)(2,1)}, u32[]{:S(2)}, u32[]{:S(2)}) collective-permute-start(bf16[1,512,512]{2,1,0:T(8,128)(2,1)S(1)} %collective-permute-done.7.refs_2_), channel_id=1, source_target_pairs={{0,1},{1,0},{2,3},{3,2},{4,5},{5,4},{6,7},{7,6},{8,9},{9,8},{10,11... | collective-permute-start | bytes 1572872 | tf_op jit(solution)/shard_map/ppermute | solution.py:395
  67.3 10.4 %copy-start.15 = (bf16[1,512,512]{2,1,0:T(8,128)(2,1)}, bf16[1,512,512]{2,1,0:T(8,128)(2,1)S(1)}, u32[]{:S(2)}) copy-start(bf16[1,512,512]{2,1,0:T(8,128)(2,1)S(1)} %collective-permute-done.11.refs_6_) | copy-start | bytes 1572868
  67.3 9.8 %collective-permute-start.12 = (bf16[1,512,512]{2,1,0:T(8,128)(2,1)S(1)}, bf16[1,512,512]{2,1,0:T(8,128)(2,1)}, u32[]{:S(2)}, u32[]{:S(2)}) collective-permute-start(bf16[1,512,512]{2,1,0:T(8,128)(2,1)S(1)} %collective-permute-done.11.refs_6_), channel_id=1, source_target_pairs={{0,1},{1,0},{2,3},{3,2},{4,5},{5,4},{6,7},{7,6},{8,9},{9,8},{10,11... | collective-permute-start | bytes 1572872 | tf_op jit(solution)/shard_map/ppermute | solution.py:395
  68.0 9.7 %copy-start.16 = (bf16[1,512,512]{2,1,0:T(8,128)(2,1)}, bf16[1,512,512]{2,1,0:T(8,128)(2,1)S(1)}, u32[]{:S(2)}) copy-start(bf16[1,512,512]{2,1,0:T(8,128)(2,1)S(1)} %collective-permute-done.6.refs_1_) | copy-start | bytes 1572868
  90.7 4.4 %collective-permute-start.13 = (bf16[2,1024,512]{2,1,0:T(8,128)(2,1)}, bf16[2,1024,512]{2,1,0:T(8,128)(2,1)S(1)}, u32[]{:S(2)}, u32[]{:S(2)}) collective-permute-start(bf16[2,1024,512]{2,1,0:T(8,128)(2,1)} %odd_parts.1), channel_id=1, source_target_pairs={{0,1},{1,0},{2,3},{3,2},{4,5},{5,4},{6,7},{7,6},{8,9},{9,8},{10,11... | collective-permute-start | bytes 6291464 | tf_op jit(solution)/shard_map/ppermute | solution.py:395
  101.8 7.5 %copy-start.11 = (bf16[4,128,128]{2,1,0:T(8,128)(2,1)S(1)}, bf16[4,128,128]{2,1,0:T(8,128)(2,1)}, u32[]{:S(2)}) copy-start(bf16[4,128,128]{2,1,0:T(8,128)(2,1)} %states.3) | copy-start | bytes 393220
  107.3 15.0 %collective-permute-start.19 = (bf16[1024,256]{1,0:T(8,128)(2,1)}, bf16[1024,256]{1,0:T(8,128)(2,1)S(1)}, u32[]{:S(2)}, u32[]{:S(2)}) collective-permute-start(bf16[1024,256]{1,0:T(8,128)(2,1)} %bitcast.26), channel_id=1, source_target_pairs={{0,2},{1,3},{2,0},{3,1},{4,6},{5,7},{6,4},{7,5},{8,10},{9,11},{10,... | collective-permute-start | bytes 1572872 | tf_op jit(solution)/shard_map/ppermute | solution.py:395
  107.5 25.3 %collective-permute-start.18 = (bf16[1024,256]{1,0:T(8,128)(2,1)S(1)}, bf16[1024,256]{1,0:T(8,128)(2,1)S(1)}, u32[]{:S(2)}, u32[]{:S(2)}) collective-permute-start(bf16[1024,256]{1,0:T(8,128)(2,1)S(1)} %bitcast.25), channel_id=1, source_target_pairs={{0,2},{1,3},{2,0},{3,1},{4,6},{5,7},{6,4},{7,5},{8,10},{9,11},{10,... | collective-permute-start | bytes 1572872 | tf_op jit(solution)/shard_map/ppermute | solution.py:395
  109.4 26.5 %collective-permute-start.16 = (bf16[4,128,128]{2,1,0:T(8,128)(2,1)S(1)}, bf16[4,128,128]{2,1,0:T(8,128)(2,1)S(1)}, u32[]{:S(2)}, u32[]{:S(2)}) collective-permute-start(bf16[4,128,128]{2,1,0:T(8,128)(2,1)S(1)} %copy-done.11), channel_id=1, source_target_pairs={{0,24},{4,28},{1,25},{5,29},{2,26},{6,30},{3,27},{7,31}} | collective-permute-start | bytes 393224 | tf_op jit(solution)/shard_map/ppermute | solution.py:406
  110.0 25.9 %collective-permute-start.15 = (bf16[4,128,128]{2,1,0:T(8,128)(2,1)S(1)}, bf16[4,128,128]{2,1,0:T(8,128)(2,1)S(1)}, u32[]{:S(2)}, u32[]{:S(2)}) collective-permute-start(bf16[4,128,128]{2,1,0:T(8,128)(2,1)S(1)} %copy-done.11), channel_id=1, source_target_pairs={{0,16},{4,20},{8,24},{12,28},{1,17},{5,21},{9,25},{13,29},{2,18},{... | collective-permute-start | bytes 393224 | tf_op jit(solution)/shard_map/ppermute | solution.py:406
  111.3 24.6 %collective-permute-start.14 = (bf16[4,128,128]{2,1,0:T(8,128)(2,1)S(1)}, bf16[4,128,128]{2,1,0:T(8,128)(2,1)S(1)}, u32[]{:S(2)}, u32[]{:S(2)}) collective-permute-start(bf16[4,128,128]{2,1,0:T(8,128)(2,1)S(1)} %copy-done.11), channel_id=1, source_target_pairs={{0,8},{4,12},{8,16},{12,20},{16,24},{20,28},{1,9},{5,13},{9,17},{1... | collective-permute-start | bytes 393224 | tf_op jit(solution)/shard_map/ppermute | solution.py:406
  125.0 27.9 %collective-permute-start.21 = (bf16[512,256]{1,0:T(8,128)(2,1)}, bf16[512,256]{1,0:T(8,128)(2,1)S(1)}, u32[]{:S(2)}, u32[]{:S(2)}) collective-permute-start(bf16[512,256]{1,0:T(8,128)(2,1)} %for_partner.3), channel_id=1, source_target_pairs={{0,4},{4,0},{8,12},{12,8},{16,20},{20,16},{24,28},{28,24},{1,5},{5... | collective-permute-start | bytes 786440 | tf_op jit(solution)/shard_map/ppermute | solution.py:392
  135.4 17.5 %collective-permute-start.20 = (bf16[512,256]{1,0:T(8,128)(2,1)}, bf16[512,256]{1,0:T(8,128)(2,1)S(1)}, u32[]{:S(2)}, u32[]{:S(2)}) collective-permute-start(bf16[512,256]{1,0:T(8,128)(2,1)} %for_partner.2), channel_id=1, source_target_pairs={{0,4},{4,0},{8,12},{12,8},{16,20},{20,16},{24,28},{28,24},{1,5},{5... | collective-permute-start | bytes 786440 | tf_op jit(solution)/shard_map/ppermute | solution.py:392
  138.4 7.6 %collective-permute-start.17 = (bf16[4,128,128]{2,1,0:T(8,128)(2,1)}, bf16[4,128,128]{2,1,0:T(8,128)(2,1)S(1)}, u32[]{:S(2)}, u32[]{:S(2)}) collective-permute-start(bf16[4,128,128]{2,1,0:T(8,128)(2,1)} %far.3), channel_id=1, source_target_pairs={{0,4},{4,0},{8,12},{12,8},{16,20},{20,16},{24,28},{28,24},{1,5},{5... | collective-permute-start | bytes 393224 | tf_op jit(solution)/shard_map/ppermute | solution.py:392
  (15 other events, 20.2 us)
Sparse Core Ops, SparseCore 0:
  9.6 51.2 all-gather.2
  84.9 50.2 reduce-scatter.1

commit v6 on v3

v6 whole, which is shorter than its diff:
```python
import functools
import math

import jax
import jax.numpy as jnp
from jax import lax
from jax.experimental import pallas as pl
from jax.experimental.pallas import tpu as pltpu
from jax.sharding import PartitionSpec as P

DH = 128
F32, BF16 = jnp.float32, jnp.bfloat16
VMEM = pl.BlockSpec(memory_space=pltpu.VMEM)
SMEM = pl.BlockSpec(memory_space=pltpu.SMEM)
ANY = pl.BlockSpec(memory_space=pl.ANY)


def dot(a, b, ca, cb):
    return lax.dot_general(a, b, (((ca,), (cb,)), ((), ())), preferred_element_type=F32)


def call(kernel, **kw):
    hint = pl.CostEstimate(flops=1, bytes_accessed=1, transcendentals=0)
    params = pltpu.CompilerParams(vmem_limit_bytes=16 * 2**20)
    return pl.pallas_call(kernel, cost_estimate=hint, compiler_params=params, **kw)


def states_kernel(par_ref, q_ref, k_ref, v_ref, g_ref, keep_ref, send_ref, near_ref):
    heads = q_ref.shape[1] // DH
    half = heads // 2
    for hd in range(heads):
        at = slice(hd * DH, (hd + 1) * DH)
        for kind, (a, b) in enumerate(((q_ref, g_ref), (k_ref, v_ref))):
            s = dot(a[:, at], b[:, at], 0, 0)
            own = par_ref[0] == hd // half

            @pl.when(own)
            def _():
                keep_ref[kind, hd % half] = s
                near_ref[kind, hd % half] = s.astype(BF16)

            @pl.when(jnp.logical_not(own))
            def _():
                send_ref[kind, hd % half] = s.astype(BF16)


def states(par, q, k, v, g):
    shape = (2, q.shape[1] // DH // 2, DH, DH)
    return call(
        states_kernel,
        in_specs=[SMEM] + [VMEM] * 4,
        out_specs=[VMEM] * 3,
        out_shape=[jax.ShapeDtypeStruct(shape, d) for d in (F32, BF16, BF16)],
        name="states",
    )(par, q, k, v, g)


def split_kernel(per, par_ref, x_ref, own_ref, theirs_ref):
    width = x_ref.shape[1] // (2 * per)
    for k in range(2):
        for i in range(per):
            block = x_ref[:, (2 * i + k) * width : (2 * i + k + 1) * width]

            @pl.when(par_ref[0] == k)
            def _():
                own_ref[i] = block

            @pl.when(par_ref[0] != k)
            def _():
                theirs_ref[i] = block


def split(par, x, per):
    width = x.shape[1] // (2 * per)
    out = jax.ShapeDtypeStruct((per, x.shape[0], width), x.dtype)
    return call(
        functools.partial(split_kernel, per),
        in_specs=[SMEM, VMEM],
        out_specs=[VMEM] * 2,
        out_shape=[out, out],
        name="split",
    )(par, x)


def inside_kernel(q_ref, k_ref, g_ref, out_ref):
    n = q_ref.shape[0]
    rows = lax.broadcasted_iota(jnp.int32, (n, n), 0)
    cols = lax.broadcasted_iota(jnp.int32, (n, n), 1)
    scores = dot(q_ref[...], k_ref[...], 1, 1)
    scores = jnp.where(rows >= cols, scores, 0.0).astype(BF16)
    out_ref[...] = dot(scores, g_ref[...], 0, 0)


def inside(q, k, g):
    n, cols = q.shape
    spec = pl.BlockSpec((n, DH), lambda h: (0, h))
    return call(
        inside_kernel,
        grid=(cols // DH,),
        in_specs=[spec] * 3,
        out_specs=spec,
        out_shape=jax.ShapeDtypeStruct((n, cols), F32),
        name="inside",
    )(q, k, g)


def far_kernel(pair_ref, every_ref, out_ref, send_ref):
    for kind in range(2):
        total = jnp.zeros(out_ref.shape[1:], F32)
        for p in range(every_ref.shape[0]):
            reached = p > pair_ref[0] if kind == 0 else p < pair_ref[0]
            total = total + jnp.where(reached, every_ref[p, kind].astype(F32), 0.0)
        out_ref[kind] = total
        send_ref[kind] = total.astype(BF16)


def far_states(pair, every):
    shape = every.shape[1:]
    return call(
        far_kernel,
        in_specs=[SMEM, VMEM],
        out_specs=[VMEM] * 2,
        out_shape=[jax.ShapeDtypeStruct(shape, d) for d in (F32, BF16)],
        name="far",
    )(pair, every)


def entering(par, kind, hd, half, far, got_far, near, got_near):
    mine = par == hd // half
    i = hd % half
    outer = jnp.where(mine, far[kind, i], got_far[kind, i].astype(F32))
    close = jnp.where(mine, near[kind, i].astype(F32), got_near[kind, i].astype(F32))
    total = outer + jnp.where(par == kind, close, 0.0)
    hi = total.astype(BF16)
    return hi, (total - hi.astype(F32)).astype(BF16)


def value_kernel(factor, half, par_ref, k_ref, vi_ref, *refs):
    ends, out_ref = refs[:-1], refs[-1]
    for hd in range(2 * half):
        at = slice(hd * DH, (hd + 1) * DH)
        hi, lo = entering(par_ref[0], 0, hd, half, *ends)
        k = k_ref[:, at]
        total = vi_ref[:, at] + (dot(k, hi, 1, 0) + dot(k, lo, 1, 0))
        out_ref[:, at] = (factor * total).astype(BF16)


def finish_value(factor, par, k, vi, ends):
    return call(
        functools.partial(value_kernel, factor, k.shape[1] // DH // 2),
        in_specs=[SMEM] + [VMEM] * (2 + len(ends)),
        out_specs=VMEM,
        out_shape=jax.ShapeDtypeStruct(k.shape, BF16),
        name="finish_value",
    )(par, k, vi, *ends)


def others_kernel(factor, half, par_ref, q_ref, k_ref, v_ref, g_ref, *refs):
    ends, (qo_ref, ko_ref) = refs[:-2], refs[-2:]
    hd = pl.program_id(0)
    q, k, v, g = q_ref[...], k_ref[...], v_ref[...], g_ref[...]
    n = q.shape[0]
    rows = lax.broadcasted_iota(jnp.int32, (n, n), 0)
    cols = lax.broadcasted_iota(jnp.int32, (n, n), 1)
    scores = jnp.where(rows >= cols, dot(g, v, 1, 1), 0.0).astype(BF16)
    hi, lo = entering(par_ref[0], 1, hd, half, *ends)
    total = dot(scores, k, 1, 0) + (dot(g, hi, 1, 1) + dot(g, lo, 1, 1))
    qo_ref[...] = (factor * total).astype(BF16)
    hi, lo = entering(par_ref[0], 0, hd, half, *ends)
    total = dot(scores, q, 0, 0) + (dot(v, hi, 1, 1) + dot(v, lo, 1, 1))
    ko_ref[...] = (factor * total).astype(BF16)


def others(factor, par, q, k, v, g, ends):
    n, cols = q.shape
    spec = pl.BlockSpec((n, DH), lambda h: (0, h))
    shape = ends[0].shape
    state = pl.BlockSpec(shape, lambda h: (0, 0, 0, 0))
    out = jax.ShapeDtypeStruct(q.shape, BF16)
    return call(
        functools.partial(others_kernel, factor, cols // DH // 2),
        grid=(cols // DH,),
        in_specs=[SMEM] + [spec] * 4 + [state] * len(ends),
        out_specs=[spec] * 2,
        out_shape=[out] * 2,
        name="others",
    )(par, q, k, v, g, *ends)


def piece_kernel(count, offs_ref, subs_ref, a_ref, b_ref, *refs):
    own, theirs = refs[:count], refs[count : 2 * count]
    out_ref, x, y, at, bt, sems = refs[2 * count :]
    step, steps = pl.program_id(0), pl.num_programs(0)
    slot = lax.rem(step, 2)

    def fetch(k, to):
        for i in range(count):

            @pl.when(offs_ref[k] == i)
            def _():
                for j, (src, dst) in enumerate(((own, x), (theirs, y))):
                    pltpu.make_async_copy(
                        src[i].at[subs_ref[k]], dst.at[to], sems.at[j, to]
                    ).start()

    @pl.when(step == 0)
    def _():
        fetch(0, 0)

    @pl.when(step + 1 < steps)
    def _():
        fetch(step + 1, 1 - slot)

    @pl.when(step == 0)
    def _():
        at[...] = a_ref[...].T
        bt[...] = b_ref[...].T

    for j, (src, dst) in enumerate(((own, x), (theirs, y))):
        pltpu.make_async_copy(src[0].at[0], dst.at[slot], sems.at[j, slot]).wait()
    total = dot(at[...], x[slot], 1, 0) + dot(bt[...], y[slot], 1, 0)
    out_ref[0] = total.astype(out_ref.dtype)


def pieces(offs, subs, a, b, own, theirs):
    steps = offs.shape[0]
    count = len(own)
    _, n, width = own[0].shape
    cols = a.shape[1]
    return call(
        functools.partial(piece_kernel, count),
        grid=(steps,),
        in_specs=[SMEM] * 2 + [VMEM] * 2 + [ANY] * (2 * count),
        out_specs=pl.BlockSpec((1, cols, width), lambda s: (s, 0, 0)),
        out_shape=jax.ShapeDtypeStruct((steps, cols, width), BF16),
        scratch_shapes=[
            pltpu.VMEM((2, n, width), BF16),
            pltpu.VMEM((2, n, width), BF16),
            pltpu.VMEM((cols, n), BF16),
            pltpu.VMEM((cols, n), BF16),
            pltpu.SemaphoreType.DMA((2, 2)),
        ],
        name="pieces",
    )(offs, subs, a, b, *own, *theirs)


def weight_kernel(scale, x_ref, out_ref):
    out_ref[...] = x_ref[...].astype(F32).T * scale


def finish_weight(scale, x):
    return call(
        functools.partial(weight_kernel, scale),
        in_specs=[VMEM],
        out_specs=VMEM,
        out_shape=jax.ShapeDtypeStruct(x.shape[::-1], F32),
        name="finish_weight",
    )(x)


def block_product(per, at_ref, x_ref, y_ref, w_ref, wy_ref):
    w = w_ref[pl.ds(at_ref[0] * per, per)].reshape(-1, w_ref.shape[2])
    wy = wy_ref[at_ref[0] // 2]
    return dot(x_ref[...], w, 1, 1) + dot(y_ref[...], wy, 1, 1)


def part_kernel(per, count, at_ref, x_ref, y_ref, w_ref, wy_ref, *refs):
    total = block_product(per, at_ref, x_ref, y_ref, w_ref, wy_ref)
    for got in refs[:count]:
        total = total + got[...].astype(F32)
    refs[-1][...] = total.astype(BF16)


def head_part(at, per, x, y, w, wy, got=()):
    return call(
        functools.partial(part_kernel, per, len(got)),
        in_specs=[SMEM] + [VMEM] * (4 + len(got)),
        out_specs=VMEM,
        out_shape=jax.ShapeDtypeStruct((x.shape[0], per * w.shape[1]), BF16),
        name="head_part",
    )(at, x, y, w, wy, *got)


def join_kernel(per, count, par_ref, at_ref, x_ref, y_ref, w_ref, wy_ref, *refs):
    total = block_product(per, at_ref, x_ref, y_ref, w_ref, wy_ref)
    for got in refs[:count]:
        total = total + got[...].astype(F32)
    other_ref, out_ref = refs[count:]
    rows = w_ref.shape[1]
    both = (total.astype(BF16), other_ref[...])
    for k in range(2):

        @pl.when(par_ref[0] == k)
        def _():
            for i in range(per):
                at = slice(i * rows, (i + 1) * rows)
                for j in range(2):
                    to = (2 * i + j) * rows
                    out_ref[:, to : to + rows] = both[j ^ k][:, at]


def join(par, at, per, x, y, w, wy, got, other):
    return call(
        functools.partial(join_kernel, per, len(got)),
        in_specs=[SMEM] * 2 + [VMEM] * (5 + len(got)),
        out_specs=VMEM,
        out_shape=jax.ShapeDtypeStruct((x.shape[0], 2 * other.shape[1]), BF16),
        name="join",
    )(par, at, x, y, w, wy, *got, other)


def after(x, *earlier):
    return lax.optimization_barrier((x, *earlier))[0]


def local(queries, keys, values, out_grad, inputs, value_weight):
    length, cols = queries.shape
    n_ctx, n_head = lax.axis_size("ctx"), lax.axis_size("head")
    pairs = n_ctx // 2
    ctx, head = lax.axis_index("ctx"), lax.axis_index("head")
    parity, pair = ctx % 2, ctx // 2
    par = parity.astype(jnp.int32).reshape(1)
    factor = 1.0 / math.sqrt(DH * length * n_ctx)
    lines = [[2 * i + k for i in range(pairs)] for k in range(2)]
    def partner(x):
        return lax.ppermute(x, "ctx", [(i, i ^ 1) for i in range(n_ctx)])

    def across(x, bit):
        return lax.ppermute(x, "head", [(i, i ^ bit) for i in range(n_head)])

    weight = lax.all_gather(value_weight, "ctx", axis_index_groups=lines)

    keep, send, near16 = states(par, queries, keys, values, out_grad)
    their_half = partner(send)
    both = (keep + their_half.astype(F32)).astype(BF16)

    per = n_ctx // n_head // 2
    own, theirs = split(after(par, send), inputs, per)
    got_near = partner(after(near16, their_half))
    own, theirs = [own], [partner(after(theirs, their_half))]

    every = lax.all_gather(both, "ctx", axis_index_groups=lines)
    far, send_far = far_states(pair.astype(jnp.int32).reshape(1), every)
    ends = (far, partner(send_far), their_half, got_near)
    vi = inside(queries, after(keys, send_far), out_grad)
    mine = finish_value(factor, par, keys, vi, ends)
    other = partner(mine)

    offsets = [0]
    bit = n_head // 2
    while bit:
        own = own + [across(r, bit) for r in own]
        theirs = theirs + [across(r, bit) for r in theirs]
        offsets = offsets + [o ^ bit for o in offsets]
        bit //= 2
    own = [own[offsets.index(i)] for i in range(n_head)]
    theirs = [theirs[offsets.index(i)] for i in range(n_head)]

    query_grad, key_grad = others(
        factor, par, queries, keys, after(values, mine), out_grad, ends
    )

    which = jnp.arange(pairs, dtype=jnp.int32)
    found = pieces(
        (which // per) ^ head,
        which % per,
        after(mine, query_grad),
        other,
        own,
        theirs,
    )
    summed = lax.psum_scatter(found, "ctx", axis_index_groups=lines)
    weight_grad = finish_weight(1.0 / math.sqrt(length * n_ctx), summed)

    weight = after(weight, found)
    split_heads = weight.reshape(n_head // 2, 2, -1, cols)
    lent = across(jnp.where(head % 2 == 0, split_heads[:, 1], split_heads[:, 0]), 1)
    mine_too, other_too = across(mine, 1), across(other, 1)
    here = head.astype(jnp.int32).reshape(1)

    def summed_parts(x, y):
        return [
            across(head_part(here ^ off, per, x, y, weight, lent), off)
            for off in range(2, n_head, 2)
        ]

    got_other = summed_parts(other, other_too)
    got_mine = summed_parts(mine, mine_too)
    swapped = partner(
        head_part(here, per, other, other_too, weight, lent, got_other)
    )
    input_grad = join(
        par, here, per, mine, mine_too, weight, lent, got_mine, swapped
    )
    return (query_grad, key_grad, input_grad, weight_grad)


def solution(mesh):
    spec = P("ctx", "head")
    return jax.shard_map(
        local, mesh=mesh, in_specs=(spec,) * 6, out_specs=(spec,) * 4, check_vma=False
    )
```

time: 162 us -> 138 us (0.85)
  waiting for transfers between devices: 36.4 us -> 51.7 us
  matrix products: 13.2 us -> 0 us
  starting transfers between devices: 28.6 us -> 16.1 us
  local copies, waits for them, and re-layouts: 18.1 us -> 8.9 us
  Pallas kernels: 27.8 us -> 21.9 us
  blocking collectives: 17.4 us -> 22.8 us
  other arithmetic: 4.05 us -> 1.84 us
    dot_general x8 -> x0, matrix products: 13.2 us -> none  [dot(): lax.dot_general(a, b, (((ca,), (cb,)), ((), ())), preferred_element_type=...]
    ppermute x10 -> x11, waiting for transfers between devices: 11.4 us -> 22.9 us  [across(): return lax.ppermute(x, 'head', [(i, i ^ bit) for i in range(n_head)])]
    ppermute x6 -> x0, starting transfers between devices: 10.4 us -> none  [local(): moved = lax.ppermute(sums[i].astype(BF16), 'ctx', ring)]
    reduce_scatter x0 -> x1, waiting for transfers between devices: none -> 7.3 us  [local(): summed = lax.psum_scatter(found, 'ctx', axis_index_groups=lines)]
    ppermute x6 -> x0, waiting for transfers between devices: 7.19 us -> none  [local(): moved = lax.ppermute(sums[i].astype(BF16), 'ctx', ring)]
    pallas_call x10 -> x12, Pallas kernels: 27.8 us -> 21.9 us  [the longest x1 6.32 us: pieces(): call(functools.partial(piece_kernel, count), grid=(steps,), in_specs=[SME...]
    unnamed x55 -> x30, local copies, waits for them, and re-layouts: 14.8 us -> 8.9 us
    all_gather x1, blocking collectives: 17.4 us -> 22.8 us  [local(): every = lax.all_gather(both, 'ctx', axis_index_groups=lines)]
  transfers between devices with their start and end apart: 26 -> 19, of which waited for: 8 -> 9; matrix products, arithmetic and copies ran while one was open for 11% -> 1% of each run, Pallas kernels for 17% -> 15%
where the time goes in v6:
time: 138 us
  waiting for transfers between devices  51.7 us (37%)
  blocking collectives  22.8 us (17%)
  Pallas kernels  21.9 us (16%)
  starting transfers between devices  16.1 us (12%)
  between operations  14.3 us (10%)
  local copies, waits for them, and re-layouts  8.9 us (6%)
  other arithmetic  1.84 us (1%)
    ppermute x11, waiting for transfers between devices, across(): return lax.ppermute(x, 'head', [(i, i ^ bit) for i in range(n_head)])  22.9 us
    all_gather x1, blocking collectives, local(): every = lax.all_gather(both, 'ctx', axis_index_groups=lines)  22.8 us
    ppermute x6, waiting for transfers between devices, partner(): return lax.ppermute(x, 'ctx', [(i, i ^ 1) for i in range(n_ctx)])  20.8 us
    ppermute x6, starting transfers between devices, partner(): return lax.ppermute(x, 'ctx', [(i, i ^ 1) for i in range(n_ctx)])  9.78 us
    unnamed x30, local copies, waits for them, and re-layouts  8.9 us
    reduce_scatter x1, waiting for transfers between devices, local(): summed = lax.psum_scatter(found, 'ctx', axis_index_groups=lines)  7.3 us
    pallas_call x1, Pallas kernels, pieces(): call(functools.partial(piece_kernel, count), grid=(steps,), in_specs=[SME...  6.32 us
    ppermute x11, starting transfers between devices, across(): return lax.ppermute(x, 'head', [(i, i ^ bit) for i in range(n_head)])  6.28 us
  transfers between devices with their start and end apart: 19, of which 9 were waited for; matrix products, arithmetic and copies ran while one was open for 1% of the time, Pallas kernels for 15%

profile of v6, /device:TPU:0, one launch (start us, length us, event | category | flops | bytes accessed | tf_op | source)
XLA Modules:
  0.0 137.5 jit_solution(15696888842184955381)
XLA Ops:
  8.0 1.0 copy-done.1
  9.0 1.0 copy-done.3
  10.0 1.0 copy-done.5
  11.1 1.0 copy-done.7
  12.1 1.8 %states.1 = (f32[2,2,128,128]{3,2,1,0:T(8,128)S(1)}, bf16[2,2,128,128]{3,2,1,0:T(8,128)(2,1)S(1)}, bf16[2,2,128,128]{3,2,1,0:T(8,128)(2,1)S(1)}) custom-call(s32[1]{0:T(128)} %bitcast.par_ref, bf16[512,512]{1,0:T(8,128)(2,1)S(1)} %copy-done.3, bf16[512,512]{1,0:T(8,128)(2,1)S(1)} %copy-done.1, bf16[512,512]{1,0:T(8,128)(2,1)S(1)} %copy-done.7, ...), custom_call_target="tpu_custom_call" | custom-call | flops 1 | bytes 1 | tf_op jit(solution)/shard_map/states/pallas_call | solution.py:49
  14.0 3.0 %collective-permute-start = (bf16[2,2,128,128]{3,2,1,0:T(8,128)(2,1)S(1)}, bf16[2,2,128,128]{3,2,1,0:T(8,128)(2,1)S(1)}, u32[]{:S(2)}, u32[]{:S(2)}) collective-permute-start(bf16[2,2,128,128]{3,2,1,0:T(8,128)(2,1)S(1)} %get-tuple-element.21), channel_id=1, source_target_pairs={{0,4},{4,0},{8,12},{12,8},{16,20},{20,16},{24,28},{28,24},{1,5},{5... | collective-permute-start | bytes 393224 | tf_op jit(solution)/shard_map/ppermute | solution.py:326
  17.0 1.2 copy-done.9
  18.2 0.9 split.1
  19.2 1.3 collective-permute-done.refs_2_
  20.5 1.7 %collective-permute-start.8 = (bf16[1,512,512]{2,1,0:T(8,128)(2,1)S(1)}, bf16[1,512,512]{2,1,0:T(8,128)(2,1)}, u32[]{:S(2)}, u32[]{:S(2)}) collective-permute-start(bf16[1,512,512]{2,1,0:T(8,128)(2,1)S(1)} %get-tuple-element.34), channel_id=1, source_target_pairs={{0,4},{4,0},{8,12},{12,8},{16,20},{20,16},{24,28},{28,24},{1,5},{5... | collective-permute-start | bytes 1572872 | tf_op jit(solution)/shard_map/ppermute | solution.py:326
  22.2 1.5 %collective-permute-start.6 = (bf16[1,512,512]{2,1,0:T(8,128)(2,1)}, bf16[1,512,512]{2,1,0:T(8,128)(2,1)}, u32[]{:S(2)}, u32[]{:S(2)}) collective-permute-start(bf16[1,512,512]{2,1,0:T(8,128)(2,1)} %get-tuple-element.32.refs_0_), channel_id=1, source_target_pairs={{0,2},{1,3},{2,0},{3,1},{4,6},{5,7},{6,4},{7,5},{8,10},{9,11},{10,... | collective-permute-start | bytes 1572872 | tf_op jit(solution)/shard_map/ppermute | solution.py:329
  23.8 10.0 %collective-permute-done.8.refs_4_ = bf16[1,512,512]{2,1,0:T(8,128)(2,1)} collective-permute-done((bf16[1,512,512]{2,1,0:T(8,128)(2,1)S(1)}, bf16[1,512,512]{2,1,0:T(8,128)(2,1)}, u32[]{:S(2)}, u32[]{:S(2)}) %collective-permute-start.8) | collective-permute-done | bytes 524320 | tf_op jit(solution)/shard_map/ppermute | solution.py:326
  33.7 1.4 %collective-permute-start.10 = (bf16[1,512,512]{2,1,0:T(8,128)(2,1)}, bf16[1,512,512]{2,1,0:T(8,128)(2,1)}, u32[]{:S(2)}, u32[]{:S(2)}) collective-permute-start(bf16[1,512,512]{2,1,0:T(8,128)(2,1)} %collective-permute-done.8.refs_4_), channel_id=1, source_target_pairs={{0,2},{1,3},{2,0},{3,1},{4,6},{5,7},{6,4},{7,5},{8,10},{9,11},{10,... | collective-permute-start | bytes 1572872 | tf_op jit(solution)/shard_map/ppermute | solution.py:329
  35.2 22.8 %all-gather = bf16[8,2,128,128]{3,2,1,0:T(8,128)(2,1)S(1)} all-gather(bf16[2,2,128,128]{3,2,1,0:T(8,128)(2,1)S(1)} %add_convert_fusion), channel_id=2, replica_groups={{0,8,16,24},{4,12,20,28},{1,9,17,25},{5,13,21,29},{2,10,18,26},{6,14,22..., dimensions={0}, use_global_device_ids=true | all-gather | bytes 655360 | tf_op jit(solution)/shard_map/all_gather | solution.py:342
  58.1 1.6 %collective-permute-start.1 = (bf16[2,2,128,128]{3,2,1,0:T(8,128)(2,1)S(1)}, bf16[2,2,128,128]{3,2,1,0:T(8,128)(2,1)S(1)}, u32[]{:S(2)}, u32[]{:S(2)}) collective-permute-start(bf16[2,2,128,128]{3,2,1,0:T(8,128)(2,1)S(1)} %get-tuple-element.22), channel_id=1, source_target_pairs={{0,4},{4,0},{8,12},{12,8},{16,20},{20,16},{24,28},{28,24},{1,5},{5... | collective-permute-start | bytes 393224 | tf_op jit(solution)/shard_map/ppermute | solution.py:326
  60.3 2.9 %inside.1.vi_ref = f32[512,512]{1,0:T(8,128)S(1)} custom-call(bf16[512,512]{1,0:T(8,128)(2,1)S(1)} %copy-done.4, bf16[512,512]{1,0:T(8,128)(2,1)S(1)} %copy-done.2, bf16[512,512]{1,0:T(8,128)(2,1)S(1)} %copy-done.6), custom_call_target="tpu_custom_call" | custom-call | flops 1 | bytes 1 | tf_op jit(solution)/shard_map/inside/pallas_call | solution.py:97
  63.2 1.4 %collective-permute-done.2.refs_3_ = bf16[2,2,128,128]{3,2,1,0:T(8,128)(2,1)S(1)} collective-permute-done((bf16[2,2,128,128]{3,2,1,0:T(8,128)(2,1)S(1)}, bf16[2,2,128,128]{3,2,1,0:T(8,128)(2,1)S(1)}, u32[]{:S(2)}, u32[]{:S(2)}) %collective-permute-start.2) | collective-permute-done | bytes 131104 | tf_op jit(solution)/shard_map/ppermute | solution.py:326
  65.8 1.4 %collective-permute-start.4 = (bf16[512,512]{1,0:T(8,128)(2,1)S(1)}, bf16[512,512]{1,0:T(8,128)(2,1)S(1)}, u32[]{:S(2)}, u32[]{:S(2)}) collective-permute-start(bf16[512,512]{1,0:T(8,128)(2,1)S(1)} %finish_value.1.a_ref.x_ref), channel_id=1, source_target_pairs={{0,4},{4,0},{8,12},{12,8},{16,20},{20,16},{24,28},{28,24},{1,5},{5... | collective-permute-start | bytes 1572872 | tf_op jit(solution)/shard_map/ppermute | solution.py:326
  69.6 4.1 %others.1 = (bf16[512,512]{1,0:T(8,128)(2,1)}, bf16[512,512]{1,0:T(8,128)(2,1)}) custom-call(s32[1]{0:T(128)} %bitcast.par_ref, bf16[512,512]{1,0:T(8,128)(2,1)S(1)} %copy-done.4, bf16[512,512]{1,0:T(8,128)(2,1)S(1)} %copy-done.2, bf16[512,512]{1,0:T(8,128)(2,1)S(1)} %copy-done.8, bf16[512,512]{1,0:T(8,128)(2,1)S(1)} %copy-done.6, ...), custom_call_target="tpu_custom_call" | custom-call | flops 1 | bytes 1 | tf_op jit(solution)/shard_map/others/pallas_call | solution.py:180
  73.6 5.2 %collective-permute-done.4.b_ref.x_ref = bf16[512,512]{1,0:T(8,128)(2,1)S(1)} collective-permute-done((bf16[512,512]{1,0:T(8,128)(2,1)S(1)}, bf16[512,512]{1,0:T(8,128)(2,1)S(1)}, u32[]{:S(2)}, u32[]{:S(2)}) %collective-permute-start.4) | collective-permute-done | bytes 524320 | tf_op jit(solution)/shard_map/ppermute | solution.py:326
  78.9 6.3 %pieces.1 = bf16[4,512,512]{2,1,0:T(8,128)(2,1)} custom-call(s32[4]{0:T(128)S(1)} %iota_xor_fusion.offs_ref, s32[4]{0:T(128)S(1)} %rem.45.subs_ref, bf16[512,512]{1,0:T(8,128)(2,1)S(1)} %finish_value.1.a_ref.x_ref, bf16[512,512]{1,0:T(8,128)(2,1)S(1)} %collective-permute-done.4.b_ref.x_ref, bf16[1,512,512]{2,1,0:T(8,128)(2,1)} %get-tuple-element.32.refs_0_, ...), custom_call_target="tpu_custom_call" | custom-call | flops 1 | bytes 1 | tf_op jit(solution)/shard_map/pieces/pallas_call | solution.py:230
  85.3 1.8 %fusion.1 = bf16[2,512,512]{2,1,0:T(8,128)(2,1)S(1)} fusion(bf16[2,2,512,512]{3,2,1,0:T(8,128)(2,1)} %bitcast.19, pred[]{:T(512)S(6)} %eq.8), kind=kLoop, calls=%fused_computation.2 | loop fusion | flops 524288 | bytes 3145729 | tf_op jit(solution)/shard_map/jit(_where)/select_n | solution.py:377
  87.7 2.8 %collective-permute-done.14.y_ref = bf16[512,512]{1,0:T(8,128)(2,1)S(1)} collective-permute-done((bf16[512,512]{1,0:T(8,128)(2,1)S(1)}, bf16[512,512]{1,0:T(8,128)(2,1)S(1)}, u32[]{:S(2)}, u32[]{:S(2)}) %collective-permute-start.14) | collective-permute-done | bytes 524320 | tf_op jit(solution)/shard_map/ppermute | solution.py:329
  92.6 1.6 %collective-permute-start.13 = (bf16[512,512]{1,0:T(8,128)(2,1)S(1)}, bf16[512,512]{1,0:T(8,128)(2,1)S(1)}, u32[]{:S(2)}, u32[]{:S(2)}) collective-permute-start(bf16[512,512]{1,0:T(8,128)(2,1)S(1)} %head_part.3), channel_id=1, source_target_pairs={{0,2},{1,3},{2,0},{3,1},{4,6},{5,7},{6,4},{7,5},{8,10},{9,11},{10,... | collective-permute-start | bytes 1572872 | tf_op jit(solution)/shard_map/ppermute | solution.py:329
  94.2 11.9 %collective-permute-done.15.refs_0_ = bf16[512,512]{1,0:T(8,128)(2,1)S(1)} collective-permute-done((bf16[512,512]{1,0:T(8,128)(2,1)S(1)}, bf16[512,512]{1,0:T(8,128)(2,1)S(1)}, u32[]{:S(2)}, u32[]{:S(2)}) %collective-permute-start.15) | collective-permute-done | bytes 524320 | tf_op jit(solution)/shard_map/ppermute | solution.py:329
  106.9 1.5 %collective-permute-start.16 = (bf16[512,512]{1,0:T(8,128)(2,1)S(1)}, bf16[512,512]{1,0:T(8,128)(2,1)S(1)}, u32[]{:S(2)}, u32[]{:S(2)}) collective-permute-start(bf16[512,512]{1,0:T(8,128)(2,1)S(1)} %head_part.5), channel_id=1, source_target_pairs={{0,4},{4,0},{8,12},{12,8},{16,20},{20,16},{24,28},{28,24},{1,5},{5... | collective-permute-start | bytes 1572872 | tf_op jit(solution)/shard_map/ppermute | solution.py:326
  108.4 8.1 %collective-permute-done.13.refs_0_ = bf16[512,512]{1,0:T(8,128)(2,1)S(1)} collective-permute-done((bf16[512,512]{1,0:T(8,128)(2,1)S(1)}, bf16[512,512]{1,0:T(8,128)(2,1)S(1)}, u32[]{:S(2)}, u32[]{:S(2)}) %collective-permute-start.13) | collective-permute-done | bytes 524320 | tf_op jit(solution)/shard_map/ppermute | solution.py:329
  116.6 2.8 %collective-permute-done.16.refs_1_ = bf16[512,512]{1,0:T(8,128)(2,1)S(1)} collective-permute-done((bf16[512,512]{1,0:T(8,128)(2,1)S(1)}, bf16[512,512]{1,0:T(8,128)(2,1)S(1)}, u32[]{:S(2)}, u32[]{:S(2)}) %collective-permute-start.16) | collective-permute-done | bytes 524320 | tf_op jit(solution)/shard_map/ppermute | solution.py:326
  119.4 1.8 %join.1 = bf16[512,1024]{1,0:T(8,128)(2,1)} custom-call(s32[1]{0:T(128)} %bitcast.par_ref, s32[1]{0:T(128)} %bitcast.3.at_ref, bf16[512,512]{1,0:T(8,128)(2,1)S(1)} %finish_value.1.a_ref.x_ref, bf16[512,512]{1,0:T(8,128)(2,1)S(1)} %collective-permute-done.3.y_ref, bf16[4,512,512]{2,1,0:T(8,128)(2,1)S(1)} %bitcast.23, ...), custom_call_target="tpu_custom_call" | custom-call | flops 1 | bytes 1 | tf_op jit(solution)/shard_map/join/pallas_call | solution.py:303
  121.2 7.3 %reduce-scatter.2.cloned.1.call-done = bf16[1,512,512]{2,1,0:T(8,128)(2,1)} async-done(((bf16[4,512,512]{2,1,0:T(8,128)(2,1)}), bf16[1,512,512]{2,1,0:T(8,128)(2,1)}) %reduce-scatter.2.cloned.1.call-update) | async-done | bytes 524304 | tf_op jit(solution)/shard_map/reduce_scatter | solution.py:372
  128.5 1.0 copy-done.10
  129.5 1.2 finish_weight.1
  (55 shorter events, 8.4 us)
Async XLA Ops:
  7.2 78.1 %all-gather.4.cloned.1.call-start = ((), (), s32[]{:S(2)}) async-start(), calls=%async_computation.2 | async-start | bytes 2621440 | tf_op jit(solution)/shard_map/all_gather | solution.py:331
  7.9 120.6 %reduce-scatter.2.cloned.1.call-start = ((), (), s32[]{:S(2)}) async-start(), calls=%async_computation.1 | async-start | bytes 2621440 | tf_op jit(solution)/shard_map/reduce_scatter | solution.py:372
  8.0 1.0 copy-start.1
  9.0 1.0 copy-start.3
  10.0 1.0 copy-start.5
  11.1 1.0 copy-start.7
  12.1 48.1 %copy-start.2 = (bf16[512,512]{1,0:T(8,128)(2,1)S(1)}, bf16[512,512]{1,0:T(8,128)(2,1)}, u32[]{:S(2)}) copy-start(bf16[512,512]{1,0:T(8,128)(2,1)} %k_ref.6) | copy-start | bytes 1572868
  12.1 48.1 %copy-start.4 = (bf16[512,512]{1,0:T(8,128)(2,1)S(1)}, bf16[512,512]{1,0:T(8,128)(2,1)}, u32[]{:S(2)}) copy-start(bf16[512,512]{1,0:T(8,128)(2,1)} %q_ref.5) | copy-start | bytes 1572868
  12.1 48.1 %copy-start.6 = (bf16[512,512]{1,0:T(8,128)(2,1)S(1)}, bf16[512,512]{1,0:T(8,128)(2,1)}, u32[]{:S(2)}) copy-start(bf16[512,512]{1,0:T(8,128)(2,1)} %g_ref.5) | copy-start | bytes 1572868
  14.0 6.5 %collective-permute-start = (bf16[2,2,128,128]{3,2,1,0:T(8,128)(2,1)S(1)}, bf16[2,2,128,128]{3,2,1,0:T(8,128)(2,1)S(1)}, u32[]{:S(2)}, u32[]{:S(2)}) collective-permute-start(bf16[2,2,128,128]{3,2,1,0:T(8,128)(2,1)S(1)} %get-tuple-element.21), channel_id=1, source_target_pairs={{0,4},{4,0},{8,12},{12,8},{16,20},{20,16},{24,28},{28,24},{1,5},{5... | collective-permute-start | bytes 393224 | tf_op jit(solution)/shard_map/ppermute | solution.py:326
  17.0 1.2 copy-start.9
  20.5 13.2 %collective-permute-start.8 = (bf16[1,512,512]{2,1,0:T(8,128)(2,1)S(1)}, bf16[1,512,512]{2,1,0:T(8,128)(2,1)}, u32[]{:S(2)}, u32[]{:S(2)}) collective-permute-start(bf16[1,512,512]{2,1,0:T(8,128)(2,1)S(1)} %get-tuple-element.34), channel_id=1, source_target_pairs={{0,4},{4,0},{8,12},{12,8},{16,20},{20,16},{24,28},{28,24},{1,5},{5... | collective-permute-start | bytes 1572872 | tf_op jit(solution)/shard_map/ppermute | solution.py:326
  22.2 45.0 %collective-permute-start.6 = (bf16[1,512,512]{2,1,0:T(8,128)(2,1)}, bf16[1,512,512]{2,1,0:T(8,128)(2,1)}, u32[]{:S(2)}, u32[]{:S(2)}) collective-permute-start(bf16[1,512,512]{2,1,0:T(8,128)(2,1)} %get-tuple-element.32.refs_0_), channel_id=1, source_target_pairs={{0,2},{1,3},{2,0},{3,1},{4,6},{5,7},{6,4},{7,5},{8,10},{9,11},{10,... | collective-permute-start | bytes 1572872 | tf_op jit(solution)/shard_map/ppermute | solution.py:329
  33.7 34.0 %collective-permute-start.10 = (bf16[1,512,512]{2,1,0:T(8,128)(2,1)}, bf16[1,512,512]{2,1,0:T(8,128)(2,1)}, u32[]{:S(2)}, u32[]{:S(2)}) collective-permute-start(bf16[1,512,512]{2,1,0:T(8,128)(2,1)} %collective-permute-done.8.refs_4_), channel_id=1, source_target_pairs={{0,2},{1,3},{2,0},{3,1},{4,6},{5,7},{6,4},{7,5},{8,10},{9,11},{10,... | collective-permute-start | bytes 1572872 | tf_op jit(solution)/shard_map/ppermute | solution.py:329
  58.1 5.1 %collective-permute-start.1 = (bf16[2,2,128,128]{3,2,1,0:T(8,128)(2,1)S(1)}, bf16[2,2,128,128]{3,2,1,0:T(8,128)(2,1)S(1)}, u32[]{:S(2)}, u32[]{:S(2)}) collective-permute-start(bf16[2,2,128,128]{3,2,1,0:T(8,128)(2,1)S(1)} %get-tuple-element.22), channel_id=1, source_target_pairs={{0,4},{4,0},{8,12},{12,8},{16,20},{20,16},{24,28},{28,24},{1,5},{5... | collective-permute-start | bytes 393224 | tf_op jit(solution)/shard_map/ppermute | solution.py:326
  59.7 8.0 %copy-start.8 = (bf16[512,512]{1,0:T(8,128)(2,1)S(1)}, bf16[512,512]{1,0:T(8,128)(2,1)}, u32[]{:S(2)}) copy-start(bf16[512,512]{1,0:T(8,128)(2,1)} %v_ref.2) | copy-start | bytes 1572868
  59.7 5.0 %collective-permute-start.2 = (bf16[2,2,128,128]{3,2,1,0:T(8,128)(2,1)S(1)}, bf16[2,2,128,128]{3,2,1,0:T(8,128)(2,1)S(1)}, u32[]{:S(2)}, u32[]{:S(2)}) collective-permute-start(bf16[2,2,128,128]{3,2,1,0:T(8,128)(2,1)S(1)} %get-tuple-element.26), channel_id=1, source_target_pairs={{0,4},{4,0},{8,12},{12,8},{16,20},{20,16},{24,28},{28,24},{1,5},{5... | collective-permute-start | bytes 393224 | tf_op jit(solution)/shard_map/ppermute | solution.py:326
  60.2 13.4 %collective-permute-start.5 = (bf16[1,512,512]{2,1,0:T(8,128)(2,1)}, bf16[1,512,512]{2,1,0:T(8,128)(2,1)}, u32[]{:S(2)}, u32[]{:S(2)}) collective-permute-start(bf16[1,512,512]{2,1,0:T(8,128)(2,1)} %get-tuple-element.32.refs_0_), channel_id=1, source_target_pairs={{0,1},{1,0},{2,3},{3,2},{4,5},{5,4},{6,7},{7,6},{8,9},{9,8},{10,11... | collective-permute-start | bytes 1572872 | tf_op jit(solution)/shard_map/ppermute | solution.py:329
  63.2 1.9 %copy-start.11 = (bf16[2,2,128,128]{3,2,1,0:T(8,128)(2,1)}, bf16[2,2,128,128]{3,2,1,0:T(8,128)(2,1)S(1)}, u32[]{:S(2)}) copy-start(bf16[2,2,128,128]{3,2,1,0:T(8,128)(2,1)S(1)} %collective-permute-done.1.refs_1_) | copy-start | bytes 393220
  65.8 13.0 %collective-permute-start.4 = (bf16[512,512]{1,0:T(8,128)(2,1)S(1)}, bf16[512,512]{1,0:T(8,128)(2,1)S(1)}, u32[]{:S(2)}, u32[]{:S(2)}) collective-permute-start(bf16[512,512]{1,0:T(8,128)(2,1)S(1)} %finish_value.1.a_ref.x_ref), channel_id=1, source_target_pairs={{0,4},{4,0},{8,12},{12,8},{16,20},{20,16},{24,28},{28,24},{1,5},{5... | collective-permute-start | bytes 1572872 | tf_op jit(solution)/shard_map/ppermute | solution.py:326
  67.2 11.6 %collective-permute-start.7 = (bf16[1,512,512]{2,1,0:T(8,128)(2,1)}, bf16[1,512,512]{2,1,0:T(8,128)(2,1)}, u32[]{:S(2)}, u32[]{:S(2)}) collective-permute-start(bf16[1,512,512]{2,1,0:T(8,128)(2,1)} %collective-permute-done.6.refs_2_), channel_id=1, source_target_pairs={{0,1},{1,0},{2,3},{3,2},{4,5},{5,4},{6,7},{7,6},{8,9},{9,8},{10,11... | collective-permute-start | bytes 1572872 | tf_op jit(solution)/shard_map/ppermute | solution.py:329
  67.2 11.6 %collective-permute-start.9 = (bf16[1,512,512]{2,1,0:T(8,128)(2,1)}, bf16[1,512,512]{2,1,0:T(8,128)(2,1)}, u32[]{:S(2)}, u32[]{:S(2)}) collective-permute-start(bf16[1,512,512]{2,1,0:T(8,128)(2,1)} %collective-permute-done.8.refs_4_), channel_id=1, source_target_pairs={{0,1},{1,0},{2,3},{3,2},{4,5},{5,4},{6,7},{7,6},{8,9},{9,8},{10,11... | collective-permute-start | bytes 1572872 | tf_op jit(solution)/shard_map/ppermute | solution.py:329
  67.7 11.1 %collective-permute-start.11 = (bf16[1,512,512]{2,1,0:T(8,128)(2,1)}, bf16[1,512,512]{2,1,0:T(8,128)(2,1)}, u32[]{:S(2)}, u32[]{:S(2)}) collective-permute-start(bf16[1,512,512]{2,1,0:T(8,128)(2,1)} %collective-permute-done.10.refs_6_), channel_id=1, source_target_pairs={{0,1},{1,0},{2,3},{3,2},{4,5},{5,4},{6,7},{7,6},{8,9},{9,8},{10,11... | collective-permute-start | bytes 1572872 | tf_op jit(solution)/shard_map/ppermute | solution.py:329
  67.7 0.9 copy-start.12
  85.3 5.3 %copy-start = (bf16[2048,512]{1,0:T(8,128)(2,1)S(1)}, bf16[2048,512]{1,0:T(8,128)(2,1)}, u32[]{:S(2)}) copy-start(bf16[2048,512]{1,0:T(8,128)(2,1)} %all-gather.4.cloned.1.call-done) | copy-start | bytes 6291460
  87.1 3.5 %collective-permute-start.12 = (bf16[2,512,512]{2,1,0:T(8,128)(2,1)S(1)}, bf16[2,512,512]{2,1,0:T(8,128)(2,1)S(1)}, u32[]{:S(2)}, u32[]{:S(2)}) collective-permute-start(bf16[2,512,512]{2,1,0:T(8,128)(2,1)S(1)} %fusion.1), channel_id=1, source_target_pairs={{0,1},{1,0},{2,3},{3,2},{4,5},{5,4},{6,7},{7,6},{8,9},{9,8},{10,11... | collective-permute-start | bytes 3145736 | tf_op jit(solution)/shard_map/ppermute | solution.py:329
  87.2 3.4 %collective-permute-start.14 = (bf16[512,512]{1,0:T(8,128)(2,1)S(1)}, bf16[512,512]{1,0:T(8,128)(2,1)S(1)}, u32[]{:S(2)}, u32[]{:S(2)}) collective-permute-start(bf16[512,512]{1,0:T(8,128)(2,1)S(1)} %collective-permute-done.4.b_ref.x_ref), channel_id=1, source_target_pairs={{0,1},{1,0},{2,3},{3,2},{4,5},{5,4},{6,7},{7,6},{8,9},{9,8},{10,11... | collective-permute-start | bytes 1572872 | tf_op jit(solution)/shard_map/ppermute | solution.py:329
  87.7 4.2 %collective-permute-start.3 = (bf16[512,512]{1,0:T(8,128)(2,1)S(1)}, bf16[512,512]{1,0:T(8,128)(2,1)S(1)}, u32[]{:S(2)}, u32[]{:S(2)}) collective-permute-start(bf16[512,512]{1,0:T(8,128)(2,1)S(1)} %finish_value.1.a_ref.x_ref), channel_id=1, source_target_pairs={{0,1},{1,0},{2,3},{3,2},{4,5},{5,4},{6,7},{7,6},{8,9},{9,8},{10,11... | collective-permute-start | bytes 1572872 | tf_op jit(solution)/shard_map/ppermute | solution.py:329
  91.3 14.8 %collective-permute-start.15 = (bf16[512,512]{1,0:T(8,128)(2,1)S(1)}, bf16[512,512]{1,0:T(8,128)(2,1)S(1)}, u32[]{:S(2)}, u32[]{:S(2)}) collective-permute-start(bf16[512,512]{1,0:T(8,128)(2,1)S(1)} %head_part.4), channel_id=1, source_target_pairs={{0,2},{1,3},{2,0},{3,1},{4,6},{5,7},{6,4},{7,5},{8,10},{9,11},{10,... | collective-permute-start | bytes 1572872 | tf_op jit(solution)/shard_map/ppermute | solution.py:329
  92.6 23.9 %collective-permute-start.13 = (bf16[512,512]{1,0:T(8,128)(2,1)S(1)}, bf16[512,512]{1,0:T(8,128)(2,1)S(1)}, u32[]{:S(2)}, u32[]{:S(2)}) collective-permute-start(bf16[512,512]{1,0:T(8,128)(2,1)S(1)} %head_part.3), channel_id=1, source_target_pairs={{0,2},{1,3},{2,0},{3,1},{4,6},{5,7},{6,4},{7,5},{8,10},{9,11},{10,... | collective-permute-start | bytes 1572872 | tf_op jit(solution)/shard_map/ppermute | solution.py:329
  106.9 12.5 %collective-permute-start.16 = (bf16[512,512]{1,0:T(8,128)(2,1)S(1)}, bf16[512,512]{1,0:T(8,128)(2,1)S(1)}, u32[]{:S(2)}, u32[]{:S(2)}) collective-permute-start(bf16[512,512]{1,0:T(8,128)(2,1)S(1)} %head_part.5), channel_id=1, source_target_pairs={{0,4},{4,0},{8,12},{12,8},{16,20},{20,16},{24,28},{28,24},{1,5},{5... | collective-permute-start | bytes 1572872 | tf_op jit(solution)/shard_map/ppermute | solution.py:326
  128.5 1.0 copy-start.10
  (2 other events, 1.6 us)
Sparse Core Ops, SparseCore 0:
  9.6 56.9 all-gather.3
  85.3 43.0 reduce-scatter.1

commit v7 on v6

--- a/solution.py
+++ b/solution.py
@@ -19,9 +19,9 @@
     return lax.dot_general(a, b, (((ca,), (cb,)), ((), ())), preferred_element_type=F32)
 
 
-def call(kernel, **kw):
+def call(kernel, vmem=16, **kw):
     hint = pl.CostEstimate(flops=1, bytes_accessed=1, transcendentals=0)
-    params = pltpu.CompilerParams(vmem_limit_bytes=16 * 2**20)
+    params = pltpu.CompilerParams(vmem_limit_bytes=vmem * 2**20)
     return pl.pallas_call(kernel, cost_estimate=hint, compiler_params=params, **kw)
 
 
@@ -48,6 +48,7 @@
     shape = (2, q.shape[1] // DH // 2, DH, DH)
     return call(
         states_kernel,
+        vmem=60,
         in_specs=[SMEM] + [VMEM] * 4,
         out_specs=[VMEM] * 3,
         out_shape=[jax.ShapeDtypeStruct(shape, d) for d in (F32, BF16, BF16)],
@@ -104,18 +105,34 @@
     )(q, k, g)
 
 
+def offer_kernel(pair_ref, keep_ref, got_ref, out_ref):
+    sums = [(keep_ref[k] + got_ref[k].astype(F32)).astype(BF16) for k in range(2)]
+    for p in range(out_ref.shape[0]):
+        out_ref[p] = jnp.where(p < pair_ref[0], sums[0], sums[1])
+
+
+def offer(pair, keep, got, pairs):
+    return call(
+        offer_kernel,
+        in_specs=[SMEM, VMEM, VMEM],
+        out_specs=VMEM,
+        out_shape=jax.ShapeDtypeStruct((pairs, *keep.shape[1:]), BF16),
+        name="offer",
+    )(pair, keep, got)
+
+
 def far_kernel(pair_ref, every_ref, out_ref, send_ref):
     for kind in range(2):
         total = jnp.zeros(out_ref.shape[1:], F32)
         for p in range(every_ref.shape[0]):
             reached = p > pair_ref[0] if kind == 0 else p < pair_ref[0]
-            total = total + jnp.where(reached, every_ref[p, kind].astype(F32), 0.0)
+            total = total + jnp.where(reached, every_ref[p].astype(F32), 0.0)
         out_ref[kind] = total
         send_ref[kind] = total.astype(BF16)
 
 
 def far_states(pair, every):
-    shape = every.shape[1:]
+    shape = (2, *every.shape[1:])
     return call(
         far_kernel,
         in_specs=[SMEM, VMEM],
@@ -332,15 +349,19 @@
 
     keep, send, near16 = states(par, queries, keys, values, out_grad)
     their_half = partner(send)
-    both = (keep + their_half.astype(F32)).astype(BF16)
+    line = pair.astype(jnp.int32).reshape(1)
+    offered = offer(line, keep, their_half, pairs)
 
     per = n_ctx // n_head // 2
     own, theirs = split(after(par, send), inputs, per)
     got_near = partner(after(near16, their_half))
     own, theirs = [own], [partner(after(theirs, their_half))]
 
-    every = lax.all_gather(both, "ctx", axis_index_groups=lines)
-    far, send_far = far_states(pair.astype(jnp.int32).reshape(1), every)
+    every = lax.all_to_all(
+        offered, "ctx", split_axis=0, concat_axis=0, axis_index_groups=lines
+    )
+    far, send_far = far_states(line, every)
+    theirs = [after(theirs[0], send_far)]
     ends = (far, partner(send_far), their_half, got_near)
     vi = inside(queries, after(keys, send_far), out_grad)
     mine = finish_value(factor, par, keys, vi, ends)

time: 138 us -> 124 us (0.90)
  blocking collectives: 22.8 us -> 0 us
  waiting for transfers between devices: 51.7 us -> 58.6 us
  local copies, waits for them, and re-layouts: 8.9 us -> 4.68 us
  starting transfers between devices: 16.1 us -> 19.6 us
  Pallas kernels: 21.9 us -> 25 us
    all_gather x1 -> x0, blocking collectives: 22.8 us -> none  [local(): every = lax.all_gather(both, 'ctx', axis_index_groups=lines)]
    all_to_all x0 -> x1, waiting for transfers between devices: none -> 13.9 us  [local(): lax.all_to_all(offered, 'ctx', split_axis=0, concat_axis=0, axis_index_gr...]
    ppermute x6, waiting for transfers between devices: 20.8 us -> 11.3 us  [partner(): return lax.ppermute(x, 'ctx', [(i, i ^ 1) for i in range(n_ctx)])]
    all_to_all x0 -> x1, starting transfers between devices: none -> 4.87 us  [local(): lax.all_to_all(offered, 'ctx', split_axis=0, concat_axis=0, axis_index_gr...]
    unnamed x30 -> x24, local copies, waits for them, and re-layouts: 8.9 us -> 4.68 us
    pallas_call x1 -> x2, Pallas kernels: 1.85 us -> 5.03 us  [the longest x1 4.27 us: states(): call(states_kernel, vmem=60, in_specs=[SMEM] + [VMEM] * 4, out_specs=[VME...]
    ppermute x11, waiting for transfers between devices: 22.9 us -> 26 us  [across(): return lax.ppermute(x, 'head', [(i, i ^ bit) for i in range(n_head)])]
    ppermute x6, starting transfers between devices: 9.78 us -> 8.29 us  [partner(): return lax.ppermute(x, 'ctx', [(i, i ^ 1) for i in range(n_ctx)])]
  transfers between devices with their start and end apart: 19 -> 20, of which waited for: 9 -> 11; matrix products, arithmetic and copies ran while one was open for 1% -> 1% of each run, Pallas kernels for 15% -> 19%
where the time goes in v7:
time: 124 us
  waiting for transfers between devices  58.6 us (47%)
  Pallas kernels  25 us (20%)
  starting transfers between devices  19.6 us (16%)
  between operations  14.2 us (11%)
  local copies, waits for them, and re-layouts  4.68 us (4%)
  other arithmetic  1.81 us (1%)
    ppermute x11, waiting for transfers between devices, across(): return lax.ppermute(x, 'head', [(i, i ^ bit) for i in range(n_head)])  26 us
    all_to_all x1, waiting for transfers between devices, local(): lax.all_to_all(offered, 'ctx', split_axis=0, concat_axis=0, axis_index_gr...  13.9 us
    ppermute x6, waiting for transfers between devices, partner(): return lax.ppermute(x, 'ctx', [(i, i ^ 1) for i in range(n_ctx)])  11.3 us
    ppermute x6, starting transfers between devices, partner(): return lax.ppermute(x, 'ctx', [(i, i ^ 1) for i in range(n_ctx)])  8.29 us
    reduce_scatter x1, waiting for transfers between devices, local(): summed = lax.psum_scatter(found, 'ctx', axis_index_groups=lines)  6.76 us
    ppermute x11, starting transfers between devices, across(): return lax.ppermute(x, 'head', [(i, i ^ bit) for i in range(n_head)])  6.45 us
    pallas_call x1, Pallas kernels, pieces(): call(functools.partial(piece_kernel, count), grid=(steps,), in_specs=[SME...  6.3 us
    all_to_all x1, starting transfers between devices, local(): lax.all_to_all(offered, 'ctx', split_axis=0, concat_axis=0, axis_index_gr...  4.87 us
  transfers between devices with their start and end apart: 20, of which 11 were waited for; matrix products, arithmetic and copies ran while one was open for 1% of the time, Pallas kernels for 19%

profile of v7, /device:TPU:0, one launch (start us, length us, event | category | flops | bytes accessed | tf_op | source)
XLA Modules:
  0.0 124.0 jit_solution(15922929668091735692)
XLA Ops:
  8.0 4.3 %states.1 = (f32[2,2,128,128]{3,2,1,0:T(8,128)}, bf16[2,2,128,128]{3,2,1,0:T(8,128)(2,1)}, bf16[2,2,128,128]{3,2,1,0:T(8,128)(2,1)}) custom-call(s32[1]{0:T(128)} %bitcast.par_ref, bf16[512,512]{1,0:T(8,128)(2,1)} %q_ref.5, bf16[512,512]{1,0:T(8,128)(2,1)} %k_ref.6, bf16[512,512]{1,0:T(8,128)(2,1)} %v_ref.2, bf16[512,512]{1,0:T(8,128)(2,1)} %g_ref.5), custom_call_target="tpu_custom_call" | custom-call | flops 1 | bytes 1 | tf_op jit(solution)/shard_map/states/pallas_call | solution.py:49
  12.2 2.9 %collective-permute-start = (bf16[2,2,128,128]{3,2,1,0:T(8,128)(2,1)}, bf16[2,2,128,128]{3,2,1,0:T(8,128)(2,1)S(1)}, u32[]{:S(2)}, u32[]{:S(2)}) collective-permute-start(bf16[2,2,128,128]{3,2,1,0:T(8,128)(2,1)} %get-tuple-element.22), channel_id=1, source_target_pairs={{0,4},{4,0},{8,12},{12,8},{16,20},{20,16},{24,28},{28,24},{1,5},{5... | collective-permute-start | bytes 393224 | tf_op jit(solution)/shard_map/ppermute | solution.py:343
  15.2 0.9 split.1
  16.1 2.8 %collective-permute-done.got_ref.refs_2_ = bf16[2,2,128,128]{3,2,1,0:T(8,128)(2,1)S(1)} collective-permute-done((bf16[2,2,128,128]{3,2,1,0:T(8,128)(2,1)}, bf16[2,2,128,128]{3,2,1,0:T(8,128)(2,1)S(1)}, u32[]{:S(2)}, u32[]{:S(2)}) %collective-permute-start) | collective-permute-done | bytes 131104 | tf_op jit(solution)/shard_map/ppermute | solution.py:343
  18.9 1.7 %collective-permute-start.8 = (bf16[1,512,512]{2,1,0:T(8,128)(2,1)S(1)}, bf16[1,512,512]{2,1,0:T(8,128)(2,1)}, u32[]{:S(2)}, u32[]{:S(2)}) collective-permute-start(bf16[1,512,512]{2,1,0:T(8,128)(2,1)S(1)} %get-tuple-element.35), channel_id=1, source_target_pairs={{0,4},{4,0},{8,12},{12,8},{16,20},{20,16},{24,28},{28,24},{1,5},{5... | collective-permute-start | bytes 1572872 | tf_op jit(solution)/shard_map/ppermute | solution.py:343
  20.6 1.0 copy-done.11
  21.6 0.8 offer.1
  22.3 4.9 %all-to-all-start = ((bf16[4,2,128,128]{3,2,1,0:T(8,128)(2,1)}), bf16[4,2,128,128]{3,2,1,0:T(8,128)(2,1)S(1)}, u32[]{:S(2)}, u32[]{:S(2)}) async-start(bf16[4,2,128,128]{3,2,1,0:T(8,128)(2,1)} %offer.1), calls=%async_computation | async-start | bytes 524288 | tf_op jit(solution)/shard_map/all_to_all | solution.py:360
  27.2 1.5 %collective-permute-start.6 = (bf16[1,512,512]{2,1,0:T(8,128)(2,1)}, bf16[1,512,512]{2,1,0:T(8,128)(2,1)}, u32[]{:S(2)}, u32[]{:S(2)}) collective-permute-start(bf16[1,512,512]{2,1,0:T(8,128)(2,1)} %get-tuple-element.33.refs_0_), channel_id=1, source_target_pairs={{0,2},{1,3},{2,0},{3,1},{4,6},{5,7},{6,4},{7,5},{8,10},{9,11},{10,... | collective-permute-start | bytes 1572872 | tf_op jit(solution)/shard_map/ppermute | solution.py:346
  28.7 13.9 %all-to-all-done.every_ref = bf16[4,2,128,128]{3,2,1,0:T(8,128)(2,1)S(1)} async-done(((bf16[4,2,128,128]{3,2,1,0:T(8,128)(2,1)}), bf16[4,2,128,128]{3,2,1,0:T(8,128)(2,1)S(1)}, u32[]{:S(2)}, u32[]{:S(2)}) %all-to-all-start) | async-done | bytes 262176 | tf_op jit(solution)/shard_map/all_to_all | solution.py:360
  42.8 1.6 %collective-permute-start.10 = (bf16[1,512,512]{2,1,0:T(8,128)(2,1)}, bf16[1,512,512]{2,1,0:T(8,128)(2,1)}, u32[]{:S(2)}, u32[]{:S(2)}) collective-permute-start(bf16[1,512,512]{2,1,0:T(8,128)(2,1)} %collective-permute-done.8.refs_4_), channel_id=1, source_target_pairs={{0,2},{1,3},{2,0},{3,1},{4,6},{5,7},{6,4},{7,5},{8,10},{9,11},{10,... | collective-permute-start | bytes 1572872 | tf_op jit(solution)/shard_map/ppermute | solution.py:346
  44.3 1.3 %collective-permute-start.2 = (bf16[2,2,128,128]{3,2,1,0:T(8,128)(2,1)}, bf16[2,2,128,128]{3,2,1,0:T(8,128)(2,1)S(1)}, u32[]{:S(2)}, u32[]{:S(2)}) collective-permute-start(bf16[2,2,128,128]{3,2,1,0:T(8,128)(2,1)} %get-tuple-element.27), channel_id=1, source_target_pairs={{0,4},{4,0},{8,12},{12,8},{16,20},{20,16},{24,28},{28,24},{1,5},{5... | collective-permute-start | bytes 393224 | tf_op jit(solution)/shard_map/ppermute | solution.py:343
  45.6 0.7 collective-permute-start.1
  46.4 2.9 %inside.1.vi_ref = f32[512,512]{1,0:T(8,128)S(1)} custom-call(bf16[512,512]{1,0:T(8,128)(2,1)S(1)} %copy-done.2, bf16[512,512]{1,0:T(8,128)(2,1)S(1)} %copy-done.1, bf16[512,512]{1,0:T(8,128)(2,1)S(1)} %copy-done.3), custom_call_target="tpu_custom_call" | custom-call | flops 1 | bytes 1 | tf_op jit(solution)/shard_map/inside/pallas_call | solution.py:98
  50.2 1.4 %collective-permute-done.1.refs_1_ = bf16[2,2,128,128]{3,2,1,0:T(8,128)(2,1)S(1)} collective-permute-done((bf16[2,2,128,128]{3,2,1,0:T(8,128)(2,1)S(1)}, bf16[2,2,128,128]{3,2,1,0:T(8,128)(2,1)S(1)}, u32[]{:S(2)}, u32[]{:S(2)}) %collective-permute-start.1) | collective-permute-done | bytes 131104 | tf_op jit(solution)/shard_map/ppermute | solution.py:343
  53.5 2.5 %collective-permute-done.10.refs_6_ = bf16[1,512,512]{2,1,0:T(8,128)(2,1)} collective-permute-done((bf16[1,512,512]{2,1,0:T(8,128)(2,1)}, bf16[1,512,512]{2,1,0:T(8,128)(2,1)}, u32[]{:S(2)}, u32[]{:S(2)}) %collective-permute-start.10) | collective-permute-done | bytes 524320 | tf_op jit(solution)/shard_map/ppermute | solution.py:346
  56.0 0.9 copy-done.8
  56.9 0.9 copy-done.10
  57.8 4.1 %others.1 = (bf16[512,512]{1,0:T(8,128)(2,1)}, bf16[512,512]{1,0:T(8,128)(2,1)}) custom-call(s32[1]{0:T(128)} %bitcast.par_ref, bf16[512,512]{1,0:T(8,128)(2,1)S(1)} %copy-done.2, bf16[512,512]{1,0:T(8,128)(2,1)S(1)} %copy-done.1, bf16[512,512]{1,0:T(8,128)(2,1)S(1)} %copy-done.4, bf16[512,512]{1,0:T(8,128)(2,1)S(1)} %copy-done.3, ...), custom_call_target="tpu_custom_call" | custom-call | flops 1 | bytes 1 | tf_op jit(solution)/shard_map/others/pallas_call | solution.py:197
  61.9 3.9 %collective-permute-done.4.b_ref.x_ref = bf16[512,512]{1,0:T(8,128)(2,1)S(1)} collective-permute-done((bf16[512,512]{1,0:T(8,128)(2,1)S(1)}, bf16[512,512]{1,0:T(8,128)(2,1)S(1)}, u32[]{:S(2)}, u32[]{:S(2)}) %collective-permute-start.4) | collective-permute-done | bytes 524320 | tf_op jit(solution)/shard_map/ppermute | solution.py:343
  65.9 6.3 %pieces.1 = bf16[4,512,512]{2,1,0:T(8,128)(2,1)} custom-call(s32[4]{0:T(128)S(1)} %iota_xor_fusion.offs_ref, s32[4]{0:T(128)S(1)} %rem.45.subs_ref, bf16[512,512]{1,0:T(8,128)(2,1)S(1)} %finish_value.1.a_ref.x_ref, bf16[512,512]{1,0:T(8,128)(2,1)S(1)} %collective-permute-done.4.b_ref.x_ref, bf16[1,512,512]{2,1,0:T(8,128)(2,1)} %get-tuple-element.33.refs_0_, ...), custom_call_target="tpu_custom_call" | custom-call | flops 1 | bytes 1 | tf_op jit(solution)/shard_map/pieces/pallas_call | solution.py:247
  72.3 1.8 %fusion.1 = bf16[2,512,512]{2,1,0:T(8,128)(2,1)S(1)} fusion(bf16[2,2,512,512]{3,2,1,0:T(8,128)(2,1)} %bitcast.18, pred[]{:T(512)S(6)} %eq.8), kind=kLoop, calls=%fused_computation.2 | loop fusion | flops 524288 | bytes 3145729 | tf_op jit(solution)/shard_map/jit(_where)/select_n | solution.py:398
  74.7 2.8 %collective-permute-done.14.y_ref = bf16[512,512]{1,0:T(8,128)(2,1)S(1)} collective-permute-done((bf16[512,512]{1,0:T(8,128)(2,1)S(1)}, bf16[512,512]{1,0:T(8,128)(2,1)S(1)}, u32[]{:S(2)}, u32[]{:S(2)}) %collective-permute-start.14) | collective-permute-done | bytes 524320 | tf_op jit(solution)/shard_map/ppermute | solution.py:346
  79.5 1.7 %collective-permute-start.13 = (bf16[512,512]{1,0:T(8,128)(2,1)S(1)}, bf16[512,512]{1,0:T(8,128)(2,1)S(1)}, u32[]{:S(2)}, u32[]{:S(2)}) collective-permute-start(bf16[512,512]{1,0:T(8,128)(2,1)S(1)} %head_part.3), channel_id=1, source_target_pairs={{0,2},{1,3},{2,0},{3,1},{4,6},{5,7},{6,4},{7,5},{8,10},{9,11},{10,... | collective-permute-start | bytes 1572872 | tf_op jit(solution)/shard_map/ppermute | solution.py:346
  81.2 11.9 %collective-permute-done.15.refs_0_ = bf16[512,512]{1,0:T(8,128)(2,1)S(1)} collective-permute-done((bf16[512,512]{1,0:T(8,128)(2,1)S(1)}, bf16[512,512]{1,0:T(8,128)(2,1)S(1)}, u32[]{:S(2)}, u32[]{:S(2)}) %collective-permute-start.15) | collective-permute-done | bytes 524320 | tf_op jit(solution)/shard_map/ppermute | solution.py:346
  93.9 1.0 collective-permute-start.16
  94.9 8.7 %collective-permute-done.13.refs_0_ = bf16[512,512]{1,0:T(8,128)(2,1)S(1)} collective-permute-done((bf16[512,512]{1,0:T(8,128)(2,1)S(1)}, bf16[512,512]{1,0:T(8,128)(2,1)S(1)}, u32[]{:S(2)}, u32[]{:S(2)}) %collective-permute-start.13) | collective-permute-done | bytes 524320 | tf_op jit(solution)/shard_map/ppermute | solution.py:346
  103.6 2.8 %collective-permute-done.16.refs_1_ = bf16[512,512]{1,0:T(8,128)(2,1)S(1)} collective-permute-done((bf16[512,512]{1,0:T(8,128)(2,1)S(1)}, bf16[512,512]{1,0:T(8,128)(2,1)S(1)}, u32[]{:S(2)}, u32[]{:S(2)}) %collective-permute-start.16) | collective-permute-done | bytes 524320 | tf_op jit(solution)/shard_map/ppermute | solution.py:343
  106.4 1.8 %join.1 = bf16[512,1024]{1,0:T(8,128)(2,1)} custom-call(s32[1]{0:T(128)} %bitcast.par_ref, s32[1]{0:T(128)} %bitcast.2.at_ref, bf16[512,512]{1,0:T(8,128)(2,1)S(1)} %finish_value.1.a_ref.x_ref, bf16[512,512]{1,0:T(8,128)(2,1)S(1)} %collective-permute-done.3.y_ref, bf16[4,512,512]{2,1,0:T(8,128)(2,1)S(1)} %bitcast.22, ...), custom_call_target="tpu_custom_call" | custom-call | flops 1 | bytes 1 | tf_op jit(solution)/shard_map/join/pallas_call | solution.py:320
  108.2 6.8 %reduce-scatter.2.cloned.1.call-done = bf16[1,512,512]{2,1,0:T(8,128)(2,1)} async-done(((bf16[4,512,512]{2,1,0:T(8,128)(2,1)}), bf16[1,512,512]{2,1,0:T(8,128)(2,1)}) %reduce-scatter.2.cloned.1.call-update) | async-done | bytes 524304 | tf_op jit(solution)/shard_map/reduce_scatter | solution.py:393
  114.9 1.0 copy-done.6
  116.0 1.2 finish_weight.1
  (50 shorter events, 7.0 us)
Async XLA Ops:
  7.2 8.0 %copy-start.5 = (bf16[512,1024]{1,0:T(8,128)(2,1)S(1)}, bf16[512,1024]{1,0:T(8,128)(2,1)}, u32[]{:S(2)}) copy-start(bf16[512,1024]{1,0:T(8,128)(2,1)} %x_ref.1) | copy-start | bytes 3145732
  7.2 65.1 %all-gather.3.cloned.1.call-start = ((), (), s32[]{:S(2)}) async-start(), calls=%async_computation.3 | async-start | bytes 2621440 | tf_op jit(solution)/shard_map/all_gather | solution.py:348
  7.9 38.4 %copy-start.1 = (bf16[512,512]{1,0:T(8,128)(2,1)S(1)}, bf16[512,512]{1,0:T(8,128)(2,1)}, u32[]{:S(2)}) copy-start(bf16[512,512]{1,0:T(8,128)(2,1)} %k_ref.6) | copy-start | bytes 1572868
  7.9 38.4 %copy-start.2 = (bf16[512,512]{1,0:T(8,128)(2,1)S(1)}, bf16[512,512]{1,0:T(8,128)(2,1)}, u32[]{:S(2)}) copy-start(bf16[512,512]{1,0:T(8,128)(2,1)} %q_ref.5) | copy-start | bytes 1572868
  7.9 38.4 %copy-start.3 = (bf16[512,512]{1,0:T(8,128)(2,1)S(1)}, bf16[512,512]{1,0:T(8,128)(2,1)}, u32[]{:S(2)}) copy-start(bf16[512,512]{1,0:T(8,128)(2,1)} %g_ref.5) | copy-start | bytes 1572868
  12.2 6.6 %collective-permute-start = (bf16[2,2,128,128]{3,2,1,0:T(8,128)(2,1)}, bf16[2,2,128,128]{3,2,1,0:T(8,128)(2,1)S(1)}, u32[]{:S(2)}, u32[]{:S(2)}) collective-permute-start(bf16[2,2,128,128]{3,2,1,0:T(8,128)(2,1)} %get-tuple-element.22), channel_id=1, source_target_pairs={{0,4},{4,0},{8,12},{12,8},{16,20},{20,16},{24,28},{28,24},{1,5},{5... | collective-permute-start | bytes 393224 | tf_op jit(solution)/shard_map/ppermute | solution.py:343
  18.9 23.9 %collective-permute-start.8 = (bf16[1,512,512]{2,1,0:T(8,128)(2,1)S(1)}, bf16[1,512,512]{2,1,0:T(8,128)(2,1)}, u32[]{:S(2)}, u32[]{:S(2)}) collective-permute-start(bf16[1,512,512]{2,1,0:T(8,128)(2,1)S(1)} %get-tuple-element.35), channel_id=1, source_target_pairs={{0,4},{4,0},{8,12},{12,8},{16,20},{20,16},{24,28},{28,24},{1,5},{5... | collective-permute-start | bytes 1572872 | tf_op jit(solution)/shard_map/ppermute | solution.py:343
  20.6 1.0 copy-start.11
  22.3 20.3 %all-to-all-start = ((bf16[4,2,128,128]{3,2,1,0:T(8,128)(2,1)}), bf16[4,2,128,128]{3,2,1,0:T(8,128)(2,1)S(1)}, u32[]{:S(2)}, u32[]{:S(2)}) async-start(bf16[4,2,128,128]{3,2,1,0:T(8,128)(2,1)} %offer.1), calls=%async_computation | async-start | bytes 524288 | tf_op jit(solution)/shard_map/all_to_all | solution.py:360
  27.2 87.7 %reduce-scatter.2.cloned.1.call-start = ((), (), s32[]{:S(2)}) async-start(), calls=%async_computation.2 | async-start | bytes 2621440 | tf_op jit(solution)/shard_map/reduce_scatter | solution.py:393
  27.2 22.1 %collective-permute-start.6 = (bf16[1,512,512]{2,1,0:T(8,128)(2,1)}, bf16[1,512,512]{2,1,0:T(8,128)(2,1)}, u32[]{:S(2)}, u32[]{:S(2)}) collective-permute-start(bf16[1,512,512]{2,1,0:T(8,128)(2,1)} %get-tuple-element.33.refs_0_), channel_id=1, source_target_pairs={{0,2},{1,3},{2,0},{3,1},{4,6},{5,7},{6,4},{7,5},{8,10},{9,11},{10,... | collective-permute-start | bytes 1572872 | tf_op jit(solution)/shard_map/ppermute | solution.py:346
  42.8 13.3 %collective-permute-start.10 = (bf16[1,512,512]{2,1,0:T(8,128)(2,1)}, bf16[1,512,512]{2,1,0:T(8,128)(2,1)}, u32[]{:S(2)}, u32[]{:S(2)}) collective-permute-start(bf16[1,512,512]{2,1,0:T(8,128)(2,1)} %collective-permute-done.8.refs_4_), channel_id=1, source_target_pairs={{0,2},{1,3},{2,0},{3,1},{4,6},{5,7},{6,4},{7,5},{8,10},{9,11},{10,... | collective-permute-start | bytes 1572872 | tf_op jit(solution)/shard_map/ppermute | solution.py:346
  44.3 11.7 %copy-start.4 = (bf16[512,512]{1,0:T(8,128)(2,1)S(1)}, bf16[512,512]{1,0:T(8,128)(2,1)}, u32[]{:S(2)}) copy-start(bf16[512,512]{1,0:T(8,128)(2,1)} %v_ref.2) | copy-start | bytes 1572868
  44.3 5.9 %collective-permute-start.2 = (bf16[2,2,128,128]{3,2,1,0:T(8,128)(2,1)}, bf16[2,2,128,128]{3,2,1,0:T(8,128)(2,1)S(1)}, u32[]{:S(2)}, u32[]{:S(2)}) collective-permute-start(bf16[2,2,128,128]{3,2,1,0:T(8,128)(2,1)} %get-tuple-element.27), channel_id=1, source_target_pairs={{0,4},{4,0},{8,12},{12,8},{16,20},{20,16},{24,28},{28,24},{1,5},{5... | collective-permute-start | bytes 393224 | tf_op jit(solution)/shard_map/ppermute | solution.py:343
  45.6 6.0 %collective-permute-start.1 = (bf16[2,2,128,128]{3,2,1,0:T(8,128)(2,1)S(1)}, bf16[2,2,128,128]{3,2,1,0:T(8,128)(2,1)S(1)}, u32[]{:S(2)}, u32[]{:S(2)}) collective-permute-start(bf16[2,2,128,128]{3,2,1,0:T(8,128)(2,1)S(1)} %get-tuple-element.23), channel_id=1, source_target_pairs={{0,4},{4,0},{8,12},{12,8},{16,20},{20,16},{24,28},{28,24},{1,5},{5... | collective-permute-start | bytes 393224 | tf_op jit(solution)/shard_map/ppermute | solution.py:343
  46.3 15.6 %collective-permute-start.5 = (bf16[1,512,512]{2,1,0:T(8,128)(2,1)}, bf16[1,512,512]{2,1,0:T(8,128)(2,1)}, u32[]{:S(2)}, u32[]{:S(2)}) collective-permute-start(bf16[1,512,512]{2,1,0:T(8,128)(2,1)} %get-tuple-element.33.refs_0_), channel_id=1, source_target_pairs={{0,1},{1,0},{2,3},{3,2},{4,5},{5,4},{6,7},{7,6},{8,9},{9,8},{10,11... | collective-permute-start | bytes 1572872 | tf_op jit(solution)/shard_map/ppermute | solution.py:346
  49.3 12.6 %collective-permute-start.7 = (bf16[1,512,512]{2,1,0:T(8,128)(2,1)}, bf16[1,512,512]{2,1,0:T(8,128)(2,1)}, u32[]{:S(2)}, u32[]{:S(2)}) collective-permute-start(bf16[1,512,512]{2,1,0:T(8,128)(2,1)} %collective-permute-done.6.refs_2_), channel_id=1, source_target_pairs={{0,1},{1,0},{2,3},{3,2},{4,5},{5,4},{6,7},{7,6},{8,9},{9,8},{10,11... | collective-permute-start | bytes 1572872 | tf_op jit(solution)/shard_map/ppermute | solution.py:346
  50.2 11.7 %collective-permute-start.9 = (bf16[1,512,512]{2,1,0:T(8,128)(2,1)}, bf16[1,512,512]{2,1,0:T(8,128)(2,1)}, u32[]{:S(2)}, u32[]{:S(2)}) collective-permute-start(bf16[1,512,512]{2,1,0:T(8,128)(2,1)} %collective-permute-done.8.refs_4_), channel_id=1, source_target_pairs={{0,1},{1,0},{2,3},{3,2},{4,5},{5,4},{6,7},{7,6},{8,9},{9,8},{10,11... | collective-permute-start | bytes 1572872 | tf_op jit(solution)/shard_map/ppermute | solution.py:346
  51.6 0.7 copy-start.9
  52.3 0.7 copy-start.7
  52.9 12.9 %collective-permute-start.4 = (bf16[512,512]{1,0:T(8,128)(2,1)S(1)}, bf16[512,512]{1,0:T(8,128)(2,1)S(1)}, u32[]{:S(2)}, u32[]{:S(2)}) collective-permute-start(bf16[512,512]{1,0:T(8,128)(2,1)S(1)} %finish_value.1.a_ref.x_ref), channel_id=1, source_target_pairs={{0,4},{4,0},{8,12},{12,8},{16,20},{20,16},{24,28},{28,24},{1,5},{5... | collective-permute-start | bytes 1572872 | tf_op jit(solution)/shard_map/ppermute | solution.py:343
  56.0 9.8 %collective-permute-start.11 = (bf16[1,512,512]{2,1,0:T(8,128)(2,1)}, bf16[1,512,512]{2,1,0:T(8,128)(2,1)}, u32[]{:S(2)}, u32[]{:S(2)}) collective-permute-start(bf16[1,512,512]{2,1,0:T(8,128)(2,1)} %collective-permute-done.10.refs_6_), channel_id=1, source_target_pairs={{0,1},{1,0},{2,3},{3,2},{4,5},{5,4},{6,7},{7,6},{8,9},{9,8},{10,11... | collective-permute-start | bytes 1572872 | tf_op jit(solution)/shard_map/ppermute | solution.py:346
  56.0 0.9 copy-start.8
  56.9 0.9 copy-start.10
  72.2 5.3 %copy-start = (bf16[2048,512]{1,0:T(8,128)(2,1)S(1)}, bf16[2048,512]{1,0:T(8,128)(2,1)}, u32[]{:S(2)}) copy-start(bf16[2048,512]{1,0:T(8,128)(2,1)} %all-gather.3.cloned.1.call-done) | copy-start | bytes 6291460
  74.1 3.5 %collective-permute-start.12 = (bf16[2,512,512]{2,1,0:T(8,128)(2,1)S(1)}, bf16[2,512,512]{2,1,0:T(8,128)(2,1)S(1)}, u32[]{:S(2)}, u32[]{:S(2)}) collective-permute-start(bf16[2,512,512]{2,1,0:T(8,128)(2,1)S(1)} %fusion.1), channel_id=1, source_target_pairs={{0,1},{1,0},{2,3},{3,2},{4,5},{5,4},{6,7},{7,6},{8,9},{9,8},{10,11... | collective-permute-start | bytes 3145736 | tf_op jit(solution)/shard_map/ppermute | solution.py:346
  74.1 3.4 %collective-permute-start.14 = (bf16[512,512]{1,0:T(8,128)(2,1)S(1)}, bf16[512,512]{1,0:T(8,128)(2,1)S(1)}, u32[]{:S(2)}, u32[]{:S(2)}) collective-permute-start(bf16[512,512]{1,0:T(8,128)(2,1)S(1)} %collective-permute-done.4.b_ref.x_ref), channel_id=1, source_target_pairs={{0,1},{1,0},{2,3},{3,2},{4,5},{5,4},{6,7},{7,6},{8,9},{9,8},{10,11... | collective-permute-start | bytes 1572872 | tf_op jit(solution)/shard_map/ppermute | solution.py:346
  74.6 4.2 %collective-permute-start.3 = (bf16[512,512]{1,0:T(8,128)(2,1)S(1)}, bf16[512,512]{1,0:T(8,128)(2,1)S(1)}, u32[]{:S(2)}, u32[]{:S(2)}) collective-permute-start(bf16[512,512]{1,0:T(8,128)(2,1)S(1)} %finish_value.1.a_ref.x_ref), channel_id=1, source_target_pairs={{0,1},{1,0},{2,3},{3,2},{4,5},{5,4},{6,7},{7,6},{8,9},{9,8},{10,11... | collective-permute-start | bytes 1572872 | tf_op jit(solution)/shard_map/ppermute | solution.py:346
  78.3 14.8 %collective-permute-start.15 = (bf16[512,512]{1,0:T(8,128)(2,1)S(1)}, bf16[512,512]{1,0:T(8,128)(2,1)S(1)}, u32[]{:S(2)}, u32[]{:S(2)}) collective-permute-start(bf16[512,512]{1,0:T(8,128)(2,1)S(1)} %head_part.4), channel_id=1, source_target_pairs={{0,2},{1,3},{2,0},{3,1},{4,6},{5,7},{6,4},{7,5},{8,10},{9,11},{10,... | collective-permute-start | bytes 1572872 | tf_op jit(solution)/shard_map/ppermute | solution.py:346
  79.5 24.0 %collective-permute-start.13 = (bf16[512,512]{1,0:T(8,128)(2,1)S(1)}, bf16[512,512]{1,0:T(8,128)(2,1)S(1)}, u32[]{:S(2)}, u32[]{:S(2)}) collective-permute-start(bf16[512,512]{1,0:T(8,128)(2,1)S(1)} %head_part.3), channel_id=1, source_target_pairs={{0,2},{1,3},{2,0},{3,1},{4,6},{5,7},{6,4},{7,5},{8,10},{9,11},{10,... | collective-permute-start | bytes 1572872 | tf_op jit(solution)/shard_map/ppermute | solution.py:346
  93.9 12.5 %collective-permute-start.16 = (bf16[512,512]{1,0:T(8,128)(2,1)S(1)}, bf16[512,512]{1,0:T(8,128)(2,1)S(1)}, u32[]{:S(2)}, u32[]{:S(2)}) collective-permute-start(bf16[512,512]{1,0:T(8,128)(2,1)S(1)} %head_part.5), channel_id=1, source_target_pairs={{0,4},{4,0},{8,12},{12,8},{16,20},{20,16},{24,28},{28,24},{1,5},{5... | collective-permute-start | bytes 1572872 | tf_op jit(solution)/shard_map/ppermute | solution.py:343
  114.9 1.0 copy-start.6
Sparse Core Ops, SparseCore 0:
  9.6 54.1 all-gather.2
  72.3 42.5 reduce-scatter.1

commit v8 on v7

--- a/solution.py
+++ b/solution.py
@@ -25,13 +25,31 @@
     return pl.pallas_call(kernel, cost_estimate=hint, compiler_params=params, **kw)
 
 
-def states_kernel(par_ref, q_ref, k_ref, v_ref, g_ref, keep_ref, send_ref, near_ref):
-    heads = q_ref.shape[1] // DH
+def states_kernel(par_ref, *refs):
+    arrays, (keep_ref, send_ref, near_ref), bufs, sems = (
+        refs[:4],
+        refs[4:7],
+        refs[7:11],
+        refs[11],
+    )
+    heads = arrays[0].shape[1] // DH
     half = heads // 2
+
+    def copy(j, hd):
+        at = pl.ds(hd * DH, DH)
+        return pltpu.make_async_copy(
+            arrays[j].at[:, at], bufs[j].at[:, at], sems.at[j, hd]
+        )
+
+    for hd in range(heads):
+        for j in range(4):
+            copy(j, hd).start()
     for hd in range(heads):
         at = slice(hd * DH, (hd + 1) * DH)
-        for kind, (a, b) in enumerate(((q_ref, g_ref), (k_ref, v_ref))):
-            s = dot(a[:, at], b[:, at], 0, 0)
+        for j in range(4):
+            copy(j, hd).wait()
+        for kind, (a, b) in enumerate(((0, 3), (1, 2))):
+            s = dot(bufs[a][:, at], bufs[b][:, at], 0, 0)
             own = par_ref[0] == hd // half
 
             @pl.when(own)
@@ -44,16 +62,19 @@
                 send_ref[kind, hd % half] = s.astype(BF16)
 
 
-def states(par, q, k, v, g):
-    shape = (2, q.shape[1] // DH // 2, DH, DH)
+def states(par, *arrays):
+    n, cols = arrays[0].shape
+    heads = cols // DH
+    shape = (2, heads // 2, DH, DH)
     return call(
         states_kernel,
-        vmem=60,
-        in_specs=[SMEM] + [VMEM] * 4,
+        in_specs=[SMEM] + [pl.BlockSpec(memory_space=pltpu.HBM)] * 4,
         out_specs=[VMEM] * 3,
         out_shape=[jax.ShapeDtypeStruct(shape, d) for d in (F32, BF16, BF16)],
+        scratch_shapes=[pltpu.VMEM((n, cols), BF16)] * 4
+        + [pltpu.SemaphoreType.DMA((4, heads))],
         name="states",
-    )(par, q, k, v, g)
+    )(par, *arrays)
 
 
 def split_kernel(per, par_ref, x_ref, own_ref, theirs_ref):
@@ -153,21 +174,22 @@
 
 
 def value_kernel(factor, half, par_ref, k_ref, vi_ref, *refs):
-    ends, out_ref = refs[:-1], refs[-1]
+    ends, outs = refs[:-2], refs[-2:]
     for hd in range(2 * half):
         at = slice(hd * DH, (hd + 1) * DH)
         hi, lo = entering(par_ref[0], 0, hd, half, *ends)
         k = k_ref[:, at]
         total = vi_ref[:, at] + (dot(k, hi, 1, 0) + dot(k, lo, 1, 0))
-        out_ref[:, at] = (factor * total).astype(BF16)
+        to = (hd % half) * DH
+        outs[hd // half][:, to : to + DH] = (factor * total).astype(BF16)
 
 
 def finish_value(factor, par, k, vi, ends):
     return call(
         functools.partial(value_kernel, factor, k.shape[1] // DH // 2),
         in_specs=[SMEM] + [VMEM] * (2 + len(ends)),
-        out_specs=VMEM,
-        out_shape=jax.ShapeDtypeStruct(k.shape, BF16),
+        out_specs=[VMEM] * 2,
+        out_shape=[jax.ShapeDtypeStruct((k.shape[0], k.shape[1] // 2), BF16)] * 2,
         name="finish_value",
     )(par, k, vi, *ends)
 
@@ -206,37 +228,21 @@
 
 def piece_kernel(count, offs_ref, subs_ref, a_ref, b_ref, *refs):
     own, theirs = refs[:count], refs[count : 2 * count]
-    out_ref, x, y, at, bt, sems = refs[2 * count :]
-    step, steps = pl.program_id(0), pl.num_programs(0)
-    slot = lax.rem(step, 2)
-
-    def fetch(k, to):
-        for i in range(count):
-
-            @pl.when(offs_ref[k] == i)
-            def _():
-                for j, (src, dst) in enumerate(((own, x), (theirs, y))):
-                    pltpu.make_async_copy(
-                        src[i].at[subs_ref[k]], dst.at[to], sems.at[j, to]
-                    ).start()
-
-    @pl.when(step == 0)
-    def _():
-        fetch(0, 0)
-
-    @pl.when(step + 1 < steps)
-    def _():
-        fetch(step + 1, 1 - slot)
+    out_ref, at, bt = refs[2 * count :]
+    step = pl.program_id(0)
 
     @pl.when(step == 0)
     def _():
         at[...] = a_ref[...].T
         bt[...] = b_ref[...].T
 
-    for j, (src, dst) in enumerate(((own, x), (theirs, y))):
-        pltpu.make_async_copy(src[0].at[0], dst.at[slot], sems.at[j, slot]).wait()
-    total = dot(at[...], x[slot], 1, 0) + dot(bt[...], y[slot], 1, 0)
-    out_ref[0] = total.astype(out_ref.dtype)
+    sub = subs_ref[step]
+    for i in range(count):
+
+        @pl.when(offs_ref[step] == i)
+        def _():
+            total = dot(at[...], own[i][sub], 1, 0) + dot(bt[...], theirs[i][sub], 1, 0)
+            out_ref[0] = total.astype(out_ref.dtype)
 
 
 def pieces(offs, subs, a, b, own, theirs):
@@ -246,63 +252,68 @@
     cols = a.shape[1]
     return call(
         functools.partial(piece_kernel, count),
+        vmem=20,
         grid=(steps,),
-        in_specs=[SMEM] * 2 + [VMEM] * 2 + [ANY] * (2 * count),
+        in_specs=[SMEM] * 2 + [VMEM] * (2 + 2 * count),
         out_specs=pl.BlockSpec((1, cols, width), lambda s: (s, 0, 0)),
         out_shape=jax.ShapeDtypeStruct((steps, cols, width), BF16),
-        scratch_shapes=[
-            pltpu.VMEM((2, n, width), BF16),
-            pltpu.VMEM((2, n, width), BF16),
-            pltpu.VMEM((cols, n), BF16),
-            pltpu.VMEM((cols, n), BF16),
-            pltpu.SemaphoreType.DMA((2, 2)),
-        ],
+        scratch_shapes=[pltpu.VMEM((cols, n), BF16)] * 2,
         name="pieces",
     )(offs, subs, a, b, *own, *theirs)
 
 
-def weight_kernel(scale, x_ref, out_ref):
-    out_ref[...] = x_ref[...].astype(F32).T * scale
-
-
-def finish_weight(scale, x):
+def weight_kernel(scale, *refs):
+    span = refs[0].shape[0]
+    for i, x_ref in enumerate(refs[:-1]):
+        refs[-1][:, i * span : (i + 1) * span] = x_ref[...].astype(F32).T * scale
+
+
+def finish_weight(scale, parts):
+    span, width = parts[0].shape
     return call(
         functools.partial(weight_kernel, scale),
-        in_specs=[VMEM],
+        in_specs=[VMEM] * len(parts),
         out_specs=VMEM,
-        out_shape=jax.ShapeDtypeStruct(x.shape[::-1], F32),
+        out_shape=jax.ShapeDtypeStruct((width, span * len(parts)), F32),
         name="finish_weight",
-    )(x)
-
-
-def block_product(per, at_ref, x_ref, y_ref, w_ref, wy_ref):
+    )(*parts)
+
+
+def block_product(per, at_ref, vals, w_ref, wy_ref):
     w = w_ref[pl.ds(at_ref[0] * per, per)].reshape(-1, w_ref.shape[2])
     wy = wy_ref[at_ref[0] // 2]
-    return dot(x_ref[...], w, 1, 1) + dot(y_ref[...], wy, 1, 1)
-
-
-def part_kernel(per, count, at_ref, x_ref, y_ref, w_ref, wy_ref, *refs):
-    total = block_product(per, at_ref, x_ref, y_ref, w_ref, wy_ref)
-    for got in refs[:count]:
+    span = vals[0].shape[1]
+    half = len(vals) // 2
+    total = 0.0
+    for i, x in enumerate(vals):
+        part = (w, wy)[i // half]
+        at = (i % half) * span
+        total = total + dot(x[...], part[:, at : at + span], 1, 1)
+    return total
+
+
+def part_kernel(per, count, at_ref, w_ref, wy_ref, *refs):
+    total = block_product(per, at_ref, refs[:count], w_ref, wy_ref)
+    for got in refs[count:-1]:
         total = total + got[...].astype(F32)
     refs[-1][...] = total.astype(BF16)
 
 
-def head_part(at, per, x, y, w, wy, got=()):
-    return call(
-        functools.partial(part_kernel, per, len(got)),
-        in_specs=[SMEM] + [VMEM] * (4 + len(got)),
+def head_part(at, per, w, wy, vals, got=()):
+    return call(
+        functools.partial(part_kernel, per, len(vals)),
+        in_specs=[SMEM] + [VMEM] * (2 + len(vals) + len(got)),
         out_specs=VMEM,
-        out_shape=jax.ShapeDtypeStruct((x.shape[0], per * w.shape[1]), BF16),
+        out_shape=jax.ShapeDtypeStruct((vals[0].shape[0], per * w.shape[1]), BF16),
         name="head_part",
-    )(at, x, y, w, wy, *got)
-
-
-def join_kernel(per, count, par_ref, at_ref, x_ref, y_ref, w_ref, wy_ref, *refs):
-    total = block_product(per, at_ref, x_ref, y_ref, w_ref, wy_ref)
-    for got in refs[:count]:
+    )(at, w, wy, *vals, *got)
+
+
+def join_kernel(per, count, par_ref, at_ref, w_ref, wy_ref, *refs):
+    total = block_product(per, at_ref, refs[:count], w_ref, wy_ref)
+    for got in refs[count:-2]:
         total = total + got[...].astype(F32)
-    other_ref, out_ref = refs[count:]
+    other_ref, out_ref = refs[-2:]
     rows = w_ref.shape[1]
     both = (total.astype(BF16), other_ref[...])
     for k in range(2):
@@ -316,14 +327,14 @@
                     out_ref[:, to : to + rows] = both[j ^ k][:, at]
 
 
-def join(par, at, per, x, y, w, wy, got, other):
-    return call(
-        functools.partial(join_kernel, per, len(got)),
-        in_specs=[SMEM] * 2 + [VMEM] * (5 + len(got)),
+def join(par, at, per, w, wy, vals, got, other):
+    return call(
+        functools.partial(join_kernel, per, len(vals)),
+        in_specs=[SMEM] * 2 + [VMEM] * (3 + len(vals) + len(got)),
         out_specs=VMEM,
-        out_shape=jax.ShapeDtypeStruct((x.shape[0], 2 * other.shape[1]), BF16),
+        out_shape=jax.ShapeDtypeStruct((other.shape[0], 2 * other.shape[1]), BF16),
         name="join",
-    )(par, at, x, y, w, wy, *got, other)
+    )(par, at, w, wy, *vals, *got, other)
 
 
 def after(x, *earlier):
@@ -361,11 +372,11 @@
         offered, "ctx", split_axis=0, concat_axis=0, axis_index_groups=lines
     )
     far, send_far = far_states(line, every)
-    theirs = [after(theirs[0], send_far)]
     ends = (far, partner(send_far), their_half, got_near)
-    vi = inside(queries, after(keys, send_far), out_grad)
+    vi = inside(queries, after(keys, offered), out_grad)
+    theirs = [after(theirs[0], vi)]
     mine = finish_value(factor, par, keys, vi, ends)
-    other = partner(mine)
+    other = [partner(x) for x in mine]
 
     offsets = [0]
     bit = n_head // 2
@@ -378,41 +389,38 @@
     theirs = [theirs[offsets.index(i)] for i in range(n_head)]
 
     query_grad, key_grad = others(
-        factor, par, queries, keys, after(values, mine), out_grad, ends
+        factor, par, queries, keys, after(values, mine[0]), out_grad, ends
     )
 
     which = jnp.arange(pairs, dtype=jnp.int32)
-    found = pieces(
-        (which // per) ^ head,
-        which % per,
-        after(mine, query_grad),
-        other,
-        own,
-        theirs,
-    )
-    summed = lax.psum_scatter(found, "ctx", axis_index_groups=lines)
-    weight_grad = finish_weight(1.0 / math.sqrt(length * n_ctx), summed)
-
-    weight = after(weight, found)
+    offs, subs = (which // per) ^ head, which % per
+    mine_too = [across(x, 1) for x in mine]
+    first = pieces(offs, subs, after(mine[0], query_grad), other[0], own, theirs)
+    weight = after(weight, first)
     split_heads = weight.reshape(n_head // 2, 2, -1, cols)
-    lent = across(jnp.where(head % 2 == 0, split_heads[:, 1], split_heads[:, 0]), 1)
-    mine_too, other_too = across(mine, 1), across(other, 1)
+    lend = jnp.where(head % 2 == 0, split_heads[:, 1], split_heads[:, 0])
+    lent = across(lend, 1)
+    other_too = [across(x, 1) for x in other]
+    second = pieces(offs, subs, after(mine[1], lend), other[1], own, theirs)
+    sums = [
+        lax.psum_scatter(x, "ctx", axis_index_groups=lines) for x in (first, second)
+    ]
+    weight_grad = finish_weight(1.0 / math.sqrt(length * n_ctx), sums)
+
     here = head.astype(jnp.int32).reshape(1)
-
-    def summed_parts(x, y):
+    mine_vals = (after(mine[0], second), mine[1], *mine_too)
+    other_vals = (after(other[0], second), other[1], *other_too)
+
+    def summed_parts(vals):
         return [
-            across(head_part(here ^ off, per, x, y, weight, lent), off)
+            across(head_part(here ^ off, per, weight, lent, vals), off)
             for off in range(2, n_head, 2)
         ]
 
-    got_other = summed_parts(other, other_too)
-    got_mine = summed_parts(mine, mine_too)
-    swapped = partner(
-        head_part(here, per, other, other_too, weight, lent, got_other)
-    )
-    input_grad = join(
-        par, here, per, mine, mine_too, weight, lent, got_mine, swapped
-    )
+    got_other = summed_parts(other_vals)
+    got_mine = summed_parts(mine_vals)
+    swapped = partner(head_part(here, per, weight, lent, other_vals, got_other))
+    input_grad = join(par, here, per, weight, lent, mine_vals, got_mine, swapped)
     return (query_grad, key_grad, input_grad, weight_grad)
 
 

time: 124 us -> 143 us (1.15)
  Pallas kernels: 25 us -> 32.5 us
  local copies, waits for them, and re-layouts: 4.68 us -> 12 us
  starting transfers between devices: 19.6 us -> 22.1 us
    ppermute x6 -> x7, waiting for transfers between devices: 11.3 us -> 19.7 us  [partner(): return lax.ppermute(x, 'ctx', [(i, i ^ 1) for i in range(n_ctx)])]
    unnamed x24 -> x46, local copies, waits for them, and re-layouts: 4.68 us -> 12 us
    pallas_call x7 -> x8, Pallas kernels: 15.8 us -> 20.9 us  [the longest x2 9.42 us: pieces(): call(functools.partial(piece_kernel, count), vmem=20, grid=(steps,), in_s...]
    all_to_all x1, waiting for transfers between devices: 13.9 us -> 9.62 us  [local(): lax.all_to_all(offered, 'ctx', split_axis=0, concat_axis=0, axis_index_gr...]
    reduce_scatter x1 -> x2, waiting for transfers between devices: 6.76 us -> 4.34 us  [local(): lax.psum_scatter(x, 'ctx', axis_index_groups=lines)]
    ppermute x6 -> x7, starting transfers between devices: 8.29 us -> 10.5 us  [partner(): return lax.ppermute(x, 'ctx', [(i, i ^ 1) for i in range(n_ctx)])]
    pallas_call x1, Pallas kernels: 0.46 us -> 2.11 us  [finish_value(): call(functools.partial(value_kernel, factor, k.shape[1] // DH // 2), in_s...]
    ppermute x11 -> x13, waiting for transfers between devices: 26 us -> 24.4 us  [across(): return lax.ppermute(x, 'head', [(i, i ^ bit) for i in range(n_head)])]
  transfers between devices with their start and end apart: 20 -> 24, of which waited for: 11 -> 14; matrix products, arithmetic and copies ran while one was open for 1% -> 2% of each run, Pallas kernels for 19% -> 22%
where the time goes in v8:
time: 143 us; the launch traced here: 142 us
  waiting for transfers between devices  58.8 us (41%)
  Pallas kernels  32.5 us (23%)
  starting transfers between devices  22.1 us (15%)
  between operations  14 us (10%)
  local copies, waits for them, and re-layouts  12 us (8%)
  other arithmetic  2.63 us (2%)
    ppermute x13, waiting for transfers between devices, across(): return lax.ppermute(x, 'head', [(i, i ^ bit) for i in range(n_head)])  24.4 us
    ppermute x7, waiting for transfers between devices, partner(): return lax.ppermute(x, 'ctx', [(i, i ^ 1) for i in range(n_ctx)])  19.7 us
    unnamed x46, local copies, waits for them, and re-layouts  12 us
    ppermute x7, starting transfers between devices, partner(): return lax.ppermute(x, 'ctx', [(i, i ^ 1) for i in range(n_ctx)])  10.5 us
    all_to_all x1, waiting for transfers between devices, local(): lax.all_to_all(offered, 'ctx', split_axis=0, concat_axis=0, axis_index_gr...  9.62 us
    pallas_call x2, Pallas kernels, pieces(): call(functools.partial(piece_kernel, count), vmem=20, grid=(steps,), in_s...  9.42 us
    ppermute x13, starting transfers between devices, across(): return lax.ppermute(x, 'head', [(i, i ^ bit) for i in range(n_head)])  6.72 us
    pallas_call x3, Pallas kernels, head_part(): call(functools.partial(part_kernel, per, len(vals)), in_specs=[SMEM] + [V...  5.07 us
  transfers between devices with their start and end apart: 24, of which 14 were waited for; matrix products, arithmetic and copies ran while one was open for 2% of the time, Pallas kernels for 22%

profile of v8, /device:TPU:0, one launch (start us, length us, event | category | flops | bytes accessed | tf_op | source)
XLA Modules:
  0.0 142.0 jit_solution(2742885241758694826)
XLA Ops:
  12.1 2.4 %states.1 = (f32[2,2,128,128]{3,2,1,0:T(8,128)S(1)}, bf16[2,2,128,128]{3,2,1,0:T(8,128)(2,1)S(1)}, bf16[2,2,128,128]{3,2,1,0:T(8,128)(2,1)S(1)}) custom-call(s32[1]{0:T(128)} %bitcast.par_ref, bf16[512,512]{1,0:T(8,128)(2,1)S(1)} %copy-done.3, bf16[512,512]{1,0:T(8,128)(2,1)S(1)} %copy-done.1, bf16[512,512]{1,0:T(8,128)(2,1)S(1)} %copy-done.13, ...), custom_call_target="tpu_custom_call" | custom-call | flops 1 | bytes 1 | tf_op jit(solution)/shard_map/states/pallas_call | solution.py:69
  14.5 3.0 %collective-permute-start = (bf16[2,2,128,128]{3,2,1,0:T(8,128)(2,1)S(1)}, bf16[2,2,128,128]{3,2,1,0:T(8,128)(2,1)S(1)}, u32[]{:S(2)}, u32[]{:S(2)}) collective-permute-start(bf16[2,2,128,128]{3,2,1,0:T(8,128)(2,1)S(1)} %get-tuple-element.27), channel_id=1, source_target_pairs={{0,4},{4,0},{8,12},{12,8},{16,20},{20,16},{24,28},{28,24},{1,5},{5... | collective-permute-start | bytes 393224 | tf_op jit(solution)/shard_map/ppermute | solution.py:354
  18.4 2.6 %collective-permute-done.got_ref.refs_2_ = bf16[2,2,128,128]{3,2,1,0:T(8,128)(2,1)S(1)} collective-permute-done((bf16[2,2,128,128]{3,2,1,0:T(8,128)(2,1)S(1)}, bf16[2,2,128,128]{3,2,1,0:T(8,128)(2,1)S(1)}, u32[]{:S(2)}, u32[]{:S(2)}) %collective-permute-start) | collective-permute-done | bytes 131104 | tf_op jit(solution)/shard_map/ppermute | solution.py:354
  21.0 1.7 %collective-permute-start.7 = (bf16[1,512,512]{2,1,0:T(8,128)(2,1)}, bf16[1,512,512]{2,1,0:T(8,128)(2,1)}, u32[]{:S(2)}, u32[]{:S(2)}) collective-permute-start(bf16[1,512,512]{2,1,0:T(8,128)(2,1)} %get-tuple-element.41), channel_id=1, source_target_pairs={{0,4},{4,0},{8,12},{12,8},{16,20},{20,16},{24,28},{28,24},{1,5},{5... | collective-permute-start | bytes 1572872 | tf_op jit(solution)/shard_map/ppermute | solution.py:354
  22.8 1.5 %collective-permute-start.5 = (bf16[1,512,512]{2,1,0:T(8,128)(2,1)S(1)}, bf16[1,512,512]{2,1,0:T(8,128)(2,1)}, u32[]{:S(2)}, u32[]{:S(2)}) collective-permute-start(bf16[1,512,512]{2,1,0:T(8,128)(2,1)S(1)} %get-tuple-element.39.refs_0_), channel_id=1, source_target_pairs={{0,2},{1,3},{2,0},{3,1},{4,6},{5,7},{6,4},{7,5},{8,10},{9,11},{10,... | collective-permute-start | bytes 1572872 | tf_op jit(solution)/shard_map/ppermute | solution.py:357
  25.0 2.9 %inside.1.vi_ref = f32[512,512]{1,0:T(8,128)S(1)} custom-call(bf16[512,512]{1,0:T(8,128)(2,1)S(1)} %copy-done.4, bf16[512,512]{1,0:T(8,128)(2,1)S(1)} %copy-done.2, bf16[512,512]{1,0:T(8,128)(2,1)S(1)} %copy-done.6), custom_call_target="tpu_custom_call" | custom-call | flops 1 | bytes 1 | tf_op jit(solution)/shard_map/inside/pallas_call | solution.py:119
  28.0 6.5 %collective-permute-done.7.refs_4_ = bf16[1,512,512]{2,1,0:T(8,128)(2,1)} collective-permute-done((bf16[1,512,512]{2,1,0:T(8,128)(2,1)}, bf16[1,512,512]{2,1,0:T(8,128)(2,1)}, u32[]{:S(2)}, u32[]{:S(2)}) %collective-permute-start.7) | collective-permute-done | bytes 524320 | tf_op jit(solution)/shard_map/ppermute | solution.py:354
  34.4 1.5 %collective-permute-start.9 = (bf16[1,512,512]{2,1,0:T(8,128)(2,1)}, bf16[1,512,512]{2,1,0:T(8,128)(2,1)}, u32[]{:S(2)}, u32[]{:S(2)}) collective-permute-start(bf16[1,512,512]{2,1,0:T(8,128)(2,1)} %collective-permute-done.7.refs_4_), channel_id=1, source_target_pairs={{0,2},{1,3},{2,0},{3,1},{4,6},{5,7},{6,4},{7,5},{8,10},{9,11},{10,... | collective-permute-start | bytes 1572872 | tf_op jit(solution)/shard_map/ppermute | solution.py:357
  35.9 4.9 %all-to-all-start = ((bf16[4,2,128,128]{3,2,1,0:T(8,128)(2,1)}), bf16[4,2,128,128]{3,2,1,0:T(8,128)(2,1)S(1)}, u32[]{:S(2)}, u32[]{:S(2)}) async-start(bf16[4,2,128,128]{3,2,1,0:T(8,128)(2,1)} %offer.1), calls=%async_computation | async-start | bytes 524288 | tf_op jit(solution)/shard_map/all_to_all | solution.py:371
  40.8 1.5 %collective-permute-start.2 = (bf16[2,2,128,128]{3,2,1,0:T(8,128)(2,1)}, bf16[2,2,128,128]{3,2,1,0:T(8,128)(2,1)}, u32[]{:S(2)}, u32[]{:S(2)}) collective-permute-start(bf16[2,2,128,128]{3,2,1,0:T(8,128)(2,1)} %copy-done.22), channel_id=1, source_target_pairs={{0,4},{4,0},{8,12},{12,8},{16,20},{20,16},{24,28},{28,24},{1,5},{5... | collective-permute-start | bytes 393224 | tf_op jit(solution)/shard_map/ppermute | solution.py:354
  42.8 4.2 %collective-permute-done.9.refs_6_ = bf16[1,512,512]{2,1,0:T(8,128)(2,1)} collective-permute-done((bf16[1,512,512]{2,1,0:T(8,128)(2,1)}, bf16[1,512,512]{2,1,0:T(8,128)(2,1)}, u32[]{:S(2)}, u32[]{:S(2)}) %collective-permute-start.9) | collective-permute-done | bytes 524320 | tf_op jit(solution)/shard_map/ppermute | solution.py:357
  46.9 9.6 %all-to-all-done.every_ref = bf16[4,2,128,128]{3,2,1,0:T(8,128)(2,1)S(1)} async-done(((bf16[4,2,128,128]{3,2,1,0:T(8,128)(2,1)}), bf16[4,2,128,128]{3,2,1,0:T(8,128)(2,1)S(1)}, u32[]{:S(2)}, u32[]{:S(2)}) %all-to-all-start) | async-done | bytes 262176 | tf_op jit(solution)/shard_map/all_to_all | solution.py:371
  56.7 1.5 %collective-permute-start.1 = (bf16[2,2,128,128]{3,2,1,0:T(8,128)(2,1)S(1)}, bf16[2,2,128,128]{3,2,1,0:T(8,128)(2,1)S(1)}, u32[]{:S(2)}, u32[]{:S(2)}) collective-permute-start(bf16[2,2,128,128]{3,2,1,0:T(8,128)(2,1)S(1)} %get-tuple-element.30), channel_id=1, source_target_pairs={{0,4},{4,0},{8,12},{12,8},{16,20},{20,16},{24,28},{28,24},{1,5},{5... | collective-permute-start | bytes 393224 | tf_op jit(solution)/shard_map/ppermute | solution.py:354
  58.2 3.5 %collective-permute-done.1.refs_1_ = bf16[2,2,128,128]{3,2,1,0:T(8,128)(2,1)S(1)} collective-permute-done((bf16[2,2,128,128]{3,2,1,0:T(8,128)(2,1)S(1)}, bf16[2,2,128,128]{3,2,1,0:T(8,128)(2,1)S(1)}, u32[]{:S(2)}, u32[]{:S(2)}) %collective-permute-start.1) | collective-permute-done | bytes 131104 | tf_op jit(solution)/shard_map/ppermute | solution.py:354
  61.7 2.1 %finish_value.1 = (bf16[512,256]{1,0:T(8,128)(2,1)S(1)}, bf16[512,256]{1,0:T(8,128)(2,1)}) custom-call(s32[1]{0:T(128)} %bitcast.par_ref, bf16[512,512]{1,0:T(8,128)(2,1)S(1)} %copy-done.2, f32[512,512]{1,0:T(8,128)S(1)} %inside.1.vi_ref, f32[2,2,128,128]{3,2,1,0:T(8,128)S(1)} %get-tuple-element.29.refs_0_, ...), custom_call_target="tpu_custom_call" | custom-call | flops 1 | bytes 1 | tf_op jit(solution)/shard_map/finish_value/pallas_call | solution.py:188
  63.8 1.5 %collective-permute-start.3 = (bf16[512,256]{1,0:T(8,128)(2,1)S(1)}, bf16[512,256]{1,0:T(8,128)(2,1)S(1)}, u32[]{:S(2)}, u32[]{:S(2)}) collective-permute-start(bf16[512,256]{1,0:T(8,128)(2,1)S(1)} %get-tuple-element.46.a_ref.refs_0_), channel_id=1, source_target_pairs={{0,4},{4,0},{8,12},{12,8},{16,20},{20,16},{24,28},{28,24},{1,5},{5... | collective-permute-start | bytes 786440 | tf_op jit(solution)/shard_map/ppermute | solution.py:354
  68.2 4.9 %others.1 = (bf16[512,512]{1,0:T(8,128)(2,1)}, bf16[512,512]{1,0:T(8,128)(2,1)}) custom-call(s32[1]{0:T(128)} %bitcast.par_ref, bf16[512,512]{1,0:T(8,128)(2,1)S(1)} %copy-done.4, bf16[512,512]{1,0:T(8,128)(2,1)S(1)} %copy-done.2, bf16[512,512]{1,0:T(8,128)(2,1)S(1)} %copy-done.14, bf16[512,512]{1,0:T(8,128)(2,1)S(1)} %copy-done.6, ...), custom_call_target="tpu_custom_call" | custom-call | flops 1 | bytes 1 | tf_op jit(solution)/shard_map/others/pallas_call | solution.py:219
  73.1 5.1 %pieces.2 = bf16[4,256,512]{2,1,0:T(8,128)(2,1)} custom-call(s32[4]{0:T(128)S(1)} %iota_xor_fusion.offs_ref, s32[4]{0:T(128)S(1)} %rem.45.subs_ref, bf16[512,256]{1,0:T(8,128)(2,1)S(1)} %get-tuple-element.46.a_ref.refs_0_, bf16[512,256]{1,0:T(8,128)(2,1)S(1)} %collective-permute-done.3.b_ref.refs_0_, bf16[1,512,512]{2,1,0:T(8,128)(2,1)S(1)} %get-tuple-element.39.refs_0_, ...), custom_call_target="tpu_custom_call" | custom-call | flops 1 | bytes 1 | tf_op jit(solution)/shard_map/pieces/pallas_call | solution.py:253
  78.9 2.6 %fusion.1 = bf16[2,512,512]{2,1,0:T(8,128)(2,1)} fusion(bf16[2,2,512,512]{3,2,1,0:T(8,128)(2,1)} %bitcast.19, pred[]{:T(512)S(6)} %eq.8), kind=kLoop, calls=%fused_computation.2 | loop fusion | flops 524288 | bytes 3145729 | tf_op jit(solution)/shard_map/jit(_where)/select_n | solution.py:401
  81.6 3.5 %collective-permute-done.12.b_ref.refs_1_ = bf16[512,256]{1,0:T(8,128)(2,1)} collective-permute-done((bf16[512,256]{1,0:T(8,128)(2,1)}, bf16[512,256]{1,0:T(8,128)(2,1)}, u32[]{:S(2)}, u32[]{:S(2)}) %collective-permute-start.12) | collective-permute-done | bytes 262176 | tf_op jit(solution)/shard_map/ppermute | solution.py:354
  86.1 4.3 %pieces.3 = bf16[4,256,512]{2,1,0:T(8,128)(2,1)S(1)} custom-call(s32[4]{0:T(128)S(1)} %iota_xor_fusion.offs_ref, s32[4]{0:T(128)S(1)} %rem.45.subs_ref, bf16[512,256]{1,0:T(8,128)(2,1)} %get-tuple-element.45.a_ref.refs_1_, bf16[512,256]{1,0:T(8,128)(2,1)} %collective-permute-done.12.b_ref.refs_1_, bf16[1,512,512]{2,1,0:T(8,128)(2,1)S(1)} %copy-done.12, ...), custom_call_target="tpu_custom_call" | custom-call | flops 1 | bytes 1 | tf_op jit(solution)/shard_map/pieces/pallas_call | solution.py:253
  92.0 1.2 collective-permute-done.16.refs_2_
  94.6 1.7 %head_part.4 = bf16[512,512]{1,0:T(8,128)(2,1)S(1)} custom-call(s32[1]{0:T(128)S(6)} %xor.12.at_ref, bf16[4,512,512]{2,1,0:T(8,128)(2,1)S(1)} %bitcast.20, bf16[2,512,512]{2,1,0:T(8,128)(2,1)S(1)} %collective-permute-done.11.wy_ref, bf16[512,256]{1,0:T(8,128)(2,1)S(1)} %copy-done.9, bf16[512,256]{1,0:T(8,128)(2,1)} %collective-permute-done.12.b_ref.refs_1_, ...), custom_call_target="tpu_custom_call" | custom-call | flops 1 | bytes 1 | tf_op jit(solution)/shard_map/head_part/pallas_call | solution.py:303
  97.8 1.4 collective-permute-done.13.refs_2_
  99.4 1.7 %head_part.3 = bf16[512,512]{1,0:T(8,128)(2,1)S(1)} custom-call(s32[1]{0:T(128)S(6)} %xor.12.at_ref, bf16[4,512,512]{2,1,0:T(8,128)(2,1)S(1)} %bitcast.21, bf16[2,512,512]{2,1,0:T(8,128)(2,1)S(1)} %collective-permute-done.11.wy_ref, bf16[512,256]{1,0:T(8,128)(2,1)S(1)} %get-tuple-element.46.a_ref.refs_0_, bf16[512,256]{1,0:T(8,128)(2,1)} %get-tuple-element.45.a_ref.refs_1_, ...), custom_call_target="tpu_custom_call" | custom-call | flops 1 | bytes 1 | tf_op jit(solution)/shard_map/head_part/pallas_call | solution.py:303
  102.3 8.9 %collective-permute-done.18.refs_4_ = bf16[512,512]{1,0:T(8,128)(2,1)S(1)} collective-permute-done((bf16[512,512]{1,0:T(8,128)(2,1)S(1)}, bf16[512,512]{1,0:T(8,128)(2,1)S(1)}, u32[]{:S(2)}, u32[]{:S(2)}) %collective-permute-start.18) | collective-permute-done | bytes 524320 | tf_op jit(solution)/shard_map/ppermute | solution.py:357
  111.2 1.7 %head_part.5 = bf16[512,512]{1,0:T(8,128)(2,1)S(1)} custom-call(s32[1]{0:T(128)} %bitcast.2.at_ref, bf16[4,512,512]{2,1,0:T(8,128)(2,1)S(1)} %bitcast.22, bf16[2,512,512]{2,1,0:T(8,128)(2,1)S(1)} %collective-permute-done.11.wy_ref, bf16[512,256]{1,0:T(8,128)(2,1)S(1)} %copy-done.10, bf16[512,256]{1,0:T(8,128)(2,1)} %collective-permute-done.12.b_ref.refs_1_, ...), custom_call_target="tpu_custom_call" | custom-call | flops 1 | bytes 1 | tf_op jit(solution)/shard_map/head_part/pallas_call | solution.py:303
  113.5 8.1 %collective-permute-done.15.refs_4_ = bf16[512,512]{1,0:T(8,128)(2,1)S(1)} collective-permute-done((bf16[512,512]{1,0:T(8,128)(2,1)S(1)}, bf16[512,512]{1,0:T(8,128)(2,1)S(1)}, u32[]{:S(2)}, u32[]{:S(2)}) %collective-permute-start.15) | collective-permute-done | bytes 524320 | tf_op jit(solution)/shard_map/ppermute | solution.py:357
  121.6 3.7 %collective-permute-done.19.refs_5_ = bf16[512,512]{1,0:T(8,128)(2,1)S(1)} collective-permute-done((bf16[512,512]{1,0:T(8,128)(2,1)S(1)}, bf16[512,512]{1,0:T(8,128)(2,1)S(1)}, u32[]{:S(2)}, u32[]{:S(2)}) %collective-permute-start.19) | collective-permute-done | bytes 524320 | tf_op jit(solution)/shard_map/ppermute | solution.py:354
  125.3 2.8 %join.1 = bf16[512,1024]{1,0:T(8,128)(2,1)} custom-call(s32[1]{0:T(128)} %bitcast.par_ref, s32[1]{0:T(128)} %bitcast.2.at_ref, bf16[4,512,512]{2,1,0:T(8,128)(2,1)S(1)} %bitcast.23, bf16[2,512,512]{2,1,0:T(8,128)(2,1)S(1)} %collective-permute-done.11.wy_ref, bf16[512,256]{1,0:T(8,128)(2,1)S(1)} %get-tuple-element.46.a_ref.refs_0_, ...), custom_call_target="tpu_custom_call" | custom-call | flops 1 | bytes 1 | tf_op jit(solution)/shard_map/join/pallas_call | solution.py:331
  128.0 4.3 %reduce-scatter.5.cloned.1.call-done = bf16[1,256,512]{2,1,0:T(8,128)(2,1)} async-done(((bf16[4,256,512]{2,1,0:T(8,128)(2,1)}), bf16[1,256,512]{2,1,0:T(8,128)(2,1)}) %reduce-scatter.5.cloned.1.call-update) | async-done | bytes 262160 | tf_op jit(solution)/shard_map/reduce_scatter | solution.py:406
  134.3 1.2 finish_weight.1
  (82 shorter events, 20.2 us)
Async XLA Ops:
  7.2 17.9 %copy-start.2 = (bf16[512,512]{1,0:T(8,128)(2,1)S(1)}, bf16[512,512]{1,0:T(8,128)(2,1)}, u32[]{:S(2)}) copy-start(bf16[512,512]{1,0:T(8,128)(2,1)} %k_ref.4) | copy-start | bytes 1572868
  7.2 71.8 %all-gather.3.cloned.1.call-start = ((), (), s32[]{:S(2)}) async-start(), calls=%async_computation.5 | async-start | bytes 2621440 | tf_op jit(solution)/shard_map/all_gather | solution.py:359
  12.1 12.9 %copy-start.4 = (bf16[512,512]{1,0:T(8,128)(2,1)S(1)}, bf16[512,512]{1,0:T(8,128)(2,1)}, u32[]{:S(2)}) copy-start(bf16[512,512]{1,0:T(8,128)(2,1)} %q_ref.3) | copy-start | bytes 1572868
  12.1 12.9 %copy-start.6 = (bf16[512,512]{1,0:T(8,128)(2,1)S(1)}, bf16[512,512]{1,0:T(8,128)(2,1)}, u32[]{:S(2)}) copy-start(bf16[512,512]{1,0:T(8,128)(2,1)} %g_ref.3) | copy-start | bytes 1572868
  14.5 8.3 %copy-start.22 = (bf16[2,2,128,128]{3,2,1,0:T(8,128)(2,1)}, bf16[2,2,128,128]{3,2,1,0:T(8,128)(2,1)S(1)}, u32[]{:S(2)}) copy-start(bf16[2,2,128,128]{3,2,1,0:T(8,128)(2,1)S(1)} %get-tuple-element.32) | copy-start | bytes 393220
  14.5 6.5 %collective-permute-start = (bf16[2,2,128,128]{3,2,1,0:T(8,128)(2,1)S(1)}, bf16[2,2,128,128]{3,2,1,0:T(8,128)(2,1)S(1)}, u32[]{:S(2)}, u32[]{:S(2)}) collective-permute-start(bf16[2,2,128,128]{3,2,1,0:T(8,128)(2,1)S(1)} %get-tuple-element.27), channel_id=1, source_target_pairs={{0,4},{4,0},{8,12},{12,8},{16,20},{20,16},{24,28},{28,24},{1,5},{5... | collective-permute-start | bytes 393224 | tf_op jit(solution)/shard_map/ppermute | solution.py:354
  18.4 54.7 %copy-start.11 = (bf16[1,512,512]{2,1,0:T(8,128)(2,1)}, bf16[1,512,512]{2,1,0:T(8,128)(2,1)S(1)}, u32[]{:S(2)}) copy-start(bf16[1,512,512]{2,1,0:T(8,128)(2,1)S(1)} %get-tuple-element.39.refs_0_) | copy-start | bytes 1572868
  21.0 13.4 %collective-permute-start.7 = (bf16[1,512,512]{2,1,0:T(8,128)(2,1)}, bf16[1,512,512]{2,1,0:T(8,128)(2,1)}, u32[]{:S(2)}, u32[]{:S(2)}) collective-permute-start(bf16[1,512,512]{2,1,0:T(8,128)(2,1)} %get-tuple-element.41), channel_id=1, source_target_pairs={{0,4},{4,0},{8,12},{12,8},{16,20},{20,16},{24,28},{28,24},{1,5},{5... | collective-permute-start | bytes 1572872 | tf_op jit(solution)/shard_map/ppermute | solution.py:354
  22.8 19.5 %collective-permute-start.5 = (bf16[1,512,512]{2,1,0:T(8,128)(2,1)S(1)}, bf16[1,512,512]{2,1,0:T(8,128)(2,1)}, u32[]{:S(2)}, u32[]{:S(2)}) collective-permute-start(bf16[1,512,512]{2,1,0:T(8,128)(2,1)S(1)} %get-tuple-element.39.refs_0_), channel_id=1, source_target_pairs={{0,2},{1,3},{2,0},{3,1},{4,6},{5,7},{6,4},{7,5},{8,10},{9,11},{10,... | collective-permute-start | bytes 1572872 | tf_op jit(solution)/shard_map/ppermute | solution.py:357
  34.4 12.5 %collective-permute-start.9 = (bf16[1,512,512]{2,1,0:T(8,128)(2,1)}, bf16[1,512,512]{2,1,0:T(8,128)(2,1)}, u32[]{:S(2)}, u32[]{:S(2)}) collective-permute-start(bf16[1,512,512]{2,1,0:T(8,128)(2,1)} %collective-permute-done.7.refs_4_), channel_id=1, source_target_pairs={{0,2},{1,3},{2,0},{3,1},{4,6},{5,7},{6,4},{7,5},{8,10},{9,11},{10,... | collective-permute-start | bytes 1572872 | tf_op jit(solution)/shard_map/ppermute | solution.py:357
  35.9 20.7 %all-to-all-start = ((bf16[4,2,128,128]{3,2,1,0:T(8,128)(2,1)}), bf16[4,2,128,128]{3,2,1,0:T(8,128)(2,1)S(1)}, u32[]{:S(2)}, u32[]{:S(2)}) async-start(bf16[4,2,128,128]{3,2,1,0:T(8,128)(2,1)} %offer.1), calls=%async_computation | async-start | bytes 524288 | tf_op jit(solution)/shard_map/all_to_all | solution.py:371
  40.8 87.3 %reduce-scatter.3.cloned.1.call-start = ((), (), s32[]{:S(2)}) async-start(), calls=%async_computation.3 | async-start | bytes 1310720 | tf_op jit(solution)/shard_map/reduce_scatter | solution.py:406
  40.8 15.9 %collective-permute-start.2 = (bf16[2,2,128,128]{3,2,1,0:T(8,128)(2,1)}, bf16[2,2,128,128]{3,2,1,0:T(8,128)(2,1)}, u32[]{:S(2)}, u32[]{:S(2)}) collective-permute-start(bf16[2,2,128,128]{3,2,1,0:T(8,128)(2,1)} %copy-done.22), channel_id=1, source_target_pairs={{0,4},{4,0},{8,12},{12,8},{16,20},{20,16},{24,28},{28,24},{1,5},{5... | collective-permute-start | bytes 393224 | tf_op jit(solution)/shard_map/ppermute | solution.py:354
  42.3 30.8 %collective-permute-start.4 = (bf16[1,512,512]{2,1,0:T(8,128)(2,1)S(1)}, bf16[1,512,512]{2,1,0:T(8,128)(2,1)}, u32[]{:S(2)}, u32[]{:S(2)}) collective-permute-start(bf16[1,512,512]{2,1,0:T(8,128)(2,1)S(1)} %get-tuple-element.39.refs_0_), channel_id=1, source_target_pairs={{0,1},{1,0},{2,3},{3,2},{4,5},{5,4},{6,7},{7,6},{8,9},{9,8},{10,11... | collective-permute-start | bytes 1572872 | tf_op jit(solution)/shard_map/ppermute | solution.py:357
  42.3 30.8 %collective-permute-start.6 = (bf16[1,512,512]{2,1,0:T(8,128)(2,1)}, bf16[1,512,512]{2,1,0:T(8,128)(2,1)}, u32[]{:S(2)}, u32[]{:S(2)}) collective-permute-start(bf16[1,512,512]{2,1,0:T(8,128)(2,1)} %collective-permute-done.5.refs_2_), channel_id=1, source_target_pairs={{0,1},{1,0},{2,3},{3,2},{4,5},{5,4},{6,7},{7,6},{8,9},{9,8},{10,11... | collective-permute-start | bytes 1572872 | tf_op jit(solution)/shard_map/ppermute | solution.py:357
  42.8 30.3 %collective-permute-start.8 = (bf16[1,512,512]{2,1,0:T(8,128)(2,1)}, bf16[1,512,512]{2,1,0:T(8,128)(2,1)}, u32[]{:S(2)}, u32[]{:S(2)}) collective-permute-start(bf16[1,512,512]{2,1,0:T(8,128)(2,1)} %collective-permute-done.7.refs_4_), channel_id=1, source_target_pairs={{0,1},{1,0},{2,3},{3,2},{4,5},{5,4},{6,7},{7,6},{8,9},{9,8},{10,11... | collective-permute-start | bytes 1572872 | tf_op jit(solution)/shard_map/ppermute | solution.py:357
  46.9 26.2 %collective-permute-start.10 = (bf16[1,512,512]{2,1,0:T(8,128)(2,1)}, bf16[1,512,512]{2,1,0:T(8,128)(2,1)}, u32[]{:S(2)}, u32[]{:S(2)}) collective-permute-start(bf16[1,512,512]{2,1,0:T(8,128)(2,1)} %collective-permute-done.9.refs_6_), channel_id=1, source_target_pairs={{0,1},{1,0},{2,3},{3,2},{4,5},{5,4},{6,7},{7,6},{8,9},{9,8},{10,11... | collective-permute-start | bytes 1572872 | tf_op jit(solution)/shard_map/ppermute | solution.py:357
  56.7 7.2 %copy-start.15 = (f32[2,2,128,128]{3,2,1,0:T(8,128)}, f32[2,2,128,128]{3,2,1,0:T(8,128)S(1)}, u32[]{:S(2)}) copy-start(f32[2,2,128,128]{3,2,1,0:T(8,128)S(1)} %get-tuple-element.29.refs_0_) | copy-start | bytes 786436
  56.7 5.0 %collective-permute-start.1 = (bf16[2,2,128,128]{3,2,1,0:T(8,128)(2,1)S(1)}, bf16[2,2,128,128]{3,2,1,0:T(8,128)(2,1)S(1)}, u32[]{:S(2)}, u32[]{:S(2)}) collective-permute-start(bf16[2,2,128,128]{3,2,1,0:T(8,128)(2,1)S(1)} %get-tuple-element.30), channel_id=1, source_target_pairs={{0,4},{4,0},{8,12},{12,8},{16,20},{20,16},{24,28},{28,24},{1,5},{5... | collective-permute-start | bytes 393224 | tf_op jit(solution)/shard_map/ppermute | solution.py:354
  63.8 9.2 %collective-permute-start.3 = (bf16[512,256]{1,0:T(8,128)(2,1)S(1)}, bf16[512,256]{1,0:T(8,128)(2,1)S(1)}, u32[]{:S(2)}, u32[]{:S(2)}) collective-permute-start(bf16[512,256]{1,0:T(8,128)(2,1)S(1)} %get-tuple-element.46.a_ref.refs_0_), channel_id=1, source_target_pairs={{0,4},{4,0},{8,12},{12,8},{16,20},{20,16},{24,28},{28,24},{1,5},{5... | collective-permute-start | bytes 786440 | tf_op jit(solution)/shard_map/ppermute | solution.py:354
  78.2 54.1 %reduce-scatter.5.cloned.1.call-start = ((), (), s32[]{:S(2)}) async-start(), calls=%async_computation.4 | async-start | bytes 1310720 | tf_op jit(solution)/shard_map/reduce_scatter | solution.py:406
  78.3 6.8 %collective-permute-start.12 = (bf16[512,256]{1,0:T(8,128)(2,1)}, bf16[512,256]{1,0:T(8,128)(2,1)}, u32[]{:S(2)}, u32[]{:S(2)}) collective-permute-start(bf16[512,256]{1,0:T(8,128)(2,1)} %get-tuple-element.45.a_ref.refs_1_), channel_id=1, source_target_pairs={{0,4},{4,0},{8,12},{12,8},{16,20},{20,16},{24,28},{28,24},{1,5},{5... | collective-permute-start | bytes 786440 | tf_op jit(solution)/shard_map/ppermute | solution.py:354
  81.6 12.1 %copy-start = (bf16[2048,512]{1,0:T(8,128)(2,1)S(1)}, bf16[2048,512]{1,0:T(8,128)(2,1)}, u32[]{:S(2)}) copy-start(bf16[2048,512]{1,0:T(8,128)(2,1)} %all-gather.3.cloned.1.call-done) | copy-start | bytes 6291460
  81.6 12.1 %collective-permute-start.11 = (bf16[2,512,512]{2,1,0:T(8,128)(2,1)}, bf16[2,512,512]{2,1,0:T(8,128)(2,1)S(1)}, u32[]{:S(2)}, u32[]{:S(2)}) collective-permute-start(bf16[2,512,512]{2,1,0:T(8,128)(2,1)} %fusion.1), channel_id=1, source_target_pairs={{0,1},{1,0},{2,3},{3,2},{4,5},{5,4},{6,7},{7,6},{8,9},{9,8},{10,11... | collective-permute-start | bytes 3145736 | tf_op jit(solution)/shard_map/ppermute | solution.py:357
  91.5 1.8 %collective-permute-start.16 = (bf16[512,256]{1,0:T(8,128)(2,1)}, bf16[512,256]{1,0:T(8,128)(2,1)S(1)}, u32[]{:S(2)}, u32[]{:S(2)}) collective-permute-start(bf16[512,256]{1,0:T(8,128)(2,1)} %copy-done.8), channel_id=1, source_target_pairs={{0,1},{1,0},{2,3},{3,2},{4,5},{5,4},{6,7},{7,6},{8,9},{9,8},{10,11... | collective-permute-start | bytes 786440 | tf_op jit(solution)/shard_map/ppermute | solution.py:357
  91.5 2.1 %collective-permute-start.17 = (bf16[512,256]{1,0:T(8,128)(2,1)}, bf16[512,256]{1,0:T(8,128)(2,1)S(1)}, u32[]{:S(2)}, u32[]{:S(2)}) collective-permute-start(bf16[512,256]{1,0:T(8,128)(2,1)} %collective-permute-done.12.b_ref.refs_1_), channel_id=1, source_target_pairs={{0,1},{1,0},{2,3},{3,2},{4,5},{5,4},{6,7},{7,6},{8,9},{9,8},{10,11... | collective-permute-start | bytes 786440 | tf_op jit(solution)/shard_map/ppermute | solution.py:357
  96.3 14.8 %copy-start.10 = (bf16[512,256]{1,0:T(8,128)(2,1)S(1)}, bf16[512,256]{1,0:T(8,128)(2,1)}, u32[]{:S(2)}) copy-start(bf16[512,256]{1,0:T(8,128)(2,1)} %copy-done.8) | copy-start | bytes 786436
  96.3 14.8 %collective-permute-start.18 = (bf16[512,512]{1,0:T(8,128)(2,1)S(1)}, bf16[512,512]{1,0:T(8,128)(2,1)S(1)}, u32[]{:S(2)}, u32[]{:S(2)}) collective-permute-start(bf16[512,512]{1,0:T(8,128)(2,1)S(1)} %head_part.4), channel_id=1, source_target_pairs={{0,2},{1,3},{2,0},{3,1},{4,6},{5,7},{6,4},{7,5},{8,10},{9,11},{10,... | collective-permute-start | bytes 1572872 | tf_op jit(solution)/shard_map/ppermute | solution.py:357
  97.3 1.9 %collective-permute-start.13 = (bf16[512,256]{1,0:T(8,128)(2,1)S(1)}, bf16[512,256]{1,0:T(8,128)(2,1)S(1)}, u32[]{:S(2)}, u32[]{:S(2)}) collective-permute-start(bf16[512,256]{1,0:T(8,128)(2,1)S(1)} %get-tuple-element.46.a_ref.refs_0_), channel_id=1, source_target_pairs={{0,1},{1,0},{2,3},{3,2},{4,5},{5,4},{6,7},{7,6},{8,9},{9,8},{10,11... | collective-permute-start | bytes 786440 | tf_op jit(solution)/shard_map/ppermute | solution.py:357
  97.3 2.1 %collective-permute-start.14 = (bf16[512,256]{1,0:T(8,128)(2,1)}, bf16[512,256]{1,0:T(8,128)(2,1)S(1)}, u32[]{:S(2)}, u32[]{:S(2)}) collective-permute-start(bf16[512,256]{1,0:T(8,128)(2,1)} %get-tuple-element.45.a_ref.refs_1_), channel_id=1, source_target_pairs={{0,1},{1,0},{2,3},{3,2},{4,5},{5,4},{6,7},{7,6},{8,9},{9,8},{10,11... | collective-permute-start | bytes 786440 | tf_op jit(solution)/shard_map/ppermute | solution.py:357
  101.1 20.5 %collective-permute-start.15 = (bf16[512,512]{1,0:T(8,128)(2,1)S(1)}, bf16[512,512]{1,0:T(8,128)(2,1)S(1)}, u32[]{:S(2)}, u32[]{:S(2)}) collective-permute-start(bf16[512,512]{1,0:T(8,128)(2,1)S(1)} %head_part.3), channel_id=1, source_target_pairs={{0,2},{1,3},{2,0},{3,1},{4,6},{5,7},{6,4},{7,5},{8,10},{9,11},{10,... | collective-permute-start | bytes 1572872 | tf_op jit(solution)/shard_map/ppermute | solution.py:357
  112.9 12.4 %collective-permute-start.19 = (bf16[512,512]{1,0:T(8,128)(2,1)S(1)}, bf16[512,512]{1,0:T(8,128)(2,1)S(1)}, u32[]{:S(2)}, u32[]{:S(2)}) collective-permute-start(bf16[512,512]{1,0:T(8,128)(2,1)S(1)} %head_part.5), channel_id=1, source_target_pairs={{0,4},{4,0},{8,12},{12,8},{16,20},{20,16},{24,28},{28,24},{1,5},{5... | collective-permute-start | bytes 1572872 | tf_op jit(solution)/shard_map/ppermute | solution.py:354
  (15 other events, 25.3 us)
Sparse Core Ops, SparseCore 0:
  9.6 54.1 all-gather.2
  78.4 25.7 reduce-scatter.2
  106.5 25.7 reduce-scatter.4

commit v9 on v7

--- a/solution.py
+++ b/solution.py
@@ -25,13 +25,31 @@
     return pl.pallas_call(kernel, cost_estimate=hint, compiler_params=params, **kw)
 
 
-def states_kernel(par_ref, q_ref, k_ref, v_ref, g_ref, keep_ref, send_ref, near_ref):
-    heads = q_ref.shape[1] // DH
+def states_kernel(par_ref, *refs):
+    arrays, (keep_ref, send_ref, near_ref), bufs, sems = (
+        refs[:4],
+        refs[4:7],
+        refs[7:11],
+        refs[11],
+    )
+    heads = arrays[0].shape[1] // DH
     half = heads // 2
+
+    def copy(j, hd):
+        at = pl.ds(hd * DH, DH)
+        return pltpu.make_async_copy(
+            arrays[j].at[:, at], bufs[j].at[:, at], sems.at[j, hd]
+        )
+
+    for hd in range(heads):
+        for j in range(4):
+            copy(j, hd).start()
     for hd in range(heads):
         at = slice(hd * DH, (hd + 1) * DH)
-        for kind, (a, b) in enumerate(((q_ref, g_ref), (k_ref, v_ref))):
-            s = dot(a[:, at], b[:, at], 0, 0)
+        for j in range(4):
+            copy(j, hd).wait()
+        for kind, (a, b) in enumerate(((0, 3), (1, 2))):
+            s = dot(bufs[a][:, at], bufs[b][:, at], 0, 0)
             own = par_ref[0] == hd // half
 
             @pl.when(own)
@@ -44,16 +62,20 @@
                 send_ref[kind, hd % half] = s.astype(BF16)
 
 
-def states(par, q, k, v, g):
-    shape = (2, q.shape[1] // DH // 2, DH, DH)
+def states(par, *arrays):
+    n, cols = arrays[0].shape
+    heads = cols // DH
+    shape = (2, heads // 2, DH, DH)
     return call(
         states_kernel,
         vmem=60,
-        in_specs=[SMEM] + [VMEM] * 4,
+        in_specs=[SMEM] + [pl.BlockSpec(memory_space=pltpu.HBM)] * 4,
         out_specs=[VMEM] * 3,
         out_shape=[jax.ShapeDtypeStruct(shape, d) for d in (F32, BF16, BF16)],
+        scratch_shapes=[pltpu.VMEM((n, cols), BF16)] * 4
+        + [pltpu.SemaphoreType.DMA((4, heads))],
         name="states",
-    )(par, q, k, v, g)
+    )(par, *arrays)
 
 
 def split_kernel(per, par_ref, x_ref, own_ref, theirs_ref):
@@ -83,26 +105,42 @@
     )(par, x)
 
 
-def inside_kernel(q_ref, k_ref, g_ref, out_ref):
-    n = q_ref.shape[0]
+def inside_kernel(*refs):
+    arrays, out_ref, bufs, sems = refs[:3], refs[3], refs[4:7], refs[7]
+    n, cols = out_ref.shape
+    heads = cols // DH
+
+    def copy(j, hd):
+        at = pl.ds(hd * DH, DH)
+        return pltpu.make_async_copy(
+            arrays[j].at[:, at], bufs[j].at[:, at], sems.at[j, hd]
+        )
+
+    for hd in range(heads):
+        for j in range(3):
+            copy(j, hd).start()
     rows = lax.broadcasted_iota(jnp.int32, (n, n), 0)
-    cols = lax.broadcasted_iota(jnp.int32, (n, n), 1)
-    scores = dot(q_ref[...], k_ref[...], 1, 1)
-    scores = jnp.where(rows >= cols, scores, 0.0).astype(BF16)
-    out_ref[...] = dot(scores, g_ref[...], 0, 0)
-
-
-def inside(q, k, g):
-    n, cols = q.shape
-    spec = pl.BlockSpec((n, DH), lambda h: (0, h))
+    causal = rows >= lax.broadcasted_iota(jnp.int32, (n, n), 1)
+    for hd in range(heads):
+        at = slice(hd * DH, (hd + 1) * DH)
+        for j in range(3):
+            copy(j, hd).wait()
+        q, k, g = (x[:, at] for x in bufs)
+        scores = jnp.where(causal, dot(q, k, 1, 1), 0.0).astype(BF16)
+        out_ref[:, at] = dot(scores, g, 0, 0)
+
+
+def inside(*arrays):
+    n, cols = arrays[0].shape
     return call(
         inside_kernel,
-        grid=(cols // DH,),
-        in_specs=[spec] * 3,
-        out_specs=spec,
+        in_specs=[pl.BlockSpec(memory_space=pltpu.HBM)] * 3,
+        out_specs=VMEM,
         out_shape=jax.ShapeDtypeStruct((n, cols), F32),
+        scratch_shapes=[pltpu.VMEM((n, cols), BF16)] * 3
+        + [pltpu.SemaphoreType.DMA((3, cols // DH))],
         name="inside",
-    )(q, k, g)
+    )(*arrays)
 
 
 def offer_kernel(pair_ref, keep_ref, got_ref, out_ref):
@@ -206,7 +244,7 @@
 
 def piece_kernel(count, offs_ref, subs_ref, a_ref, b_ref, *refs):
     own, theirs = refs[:count], refs[count : 2 * count]
-    out_ref, x, y, at, bt, sems = refs[2 * count :]
+    outs, (x, y, at, bt, sems) = refs[2 * count : -5], refs[-5:]
     step, steps = pl.program_id(0), pl.num_programs(0)
     slot = lax.rem(step, 2)
 
@@ -236,10 +274,14 @@
     for j, (src, dst) in enumerate(((own, x), (theirs, y))):
         pltpu.make_async_copy(src[0].at[0], dst.at[slot], sems.at[j, slot]).wait()
     total = dot(at[...], x[slot], 1, 0) + dot(bt[...], y[slot], 1, 0)
-    out_ref[0] = total.astype(out_ref.dtype)
-
-
-def pieces(offs, subs, a, b, own, theirs):
+    for i, out_ref in enumerate(outs):
+
+        @pl.when(step == i)
+        def _():
+            out_ref[...] = total.astype(out_ref.dtype)
+
+
+def pieces(dtype, offs, subs, a, b, own, theirs):
     steps = offs.shape[0]
     count = len(own)
     _, n, width = own[0].shape
@@ -248,8 +290,8 @@
         functools.partial(piece_kernel, count),
         grid=(steps,),
         in_specs=[SMEM] * 2 + [VMEM] * 2 + [ANY] * (2 * count),
-        out_specs=pl.BlockSpec((1, cols, width), lambda s: (s, 0, 0)),
-        out_shape=jax.ShapeDtypeStruct((steps, cols, width), BF16),
+        out_specs=[VMEM] * steps,
+        out_shape=[jax.ShapeDtypeStruct((cols, width), dtype)] * steps,
         scratch_shapes=[
             pltpu.VMEM((2, n, width), BF16),
             pltpu.VMEM((2, n, width), BF16),
@@ -261,18 +303,70 @@
     )(offs, subs, a, b, *own, *theirs)
 
 
-def weight_kernel(scale, x_ref, out_ref):
-    out_ref[...] = x_ref[...].astype(F32).T * scale
-
-
-def finish_weight(scale, x):
+def weight_kernel(scale, moved_ref, own_ref, out_ref):
+    out_ref[...] = (moved_ref[...].astype(F32) + own_ref[...]).T * scale
+
+
+def finish_weight(scale, moved, own):
     return call(
         functools.partial(weight_kernel, scale),
-        in_specs=[VMEM],
-        out_specs=VMEM,
-        out_shape=jax.ShapeDtypeStruct(x.shape[::-1], F32),
+        in_specs=[VMEM] * 2,
+        out_specs=VMEM,
+        out_shape=jax.ShapeDtypeStruct(moved.shape[::-1], F32),
         name="finish_weight",
-    )(x)
+    )(moved, own)
+
+
+def add_kernel(moved_ref, own_ref, out_ref):
+    out_ref[...] = (moved_ref[...].astype(F32) + own_ref[...]).astype(BF16)
+
+
+def add_own(moved, own):
+    return call(
+        add_kernel,
+        in_specs=[VMEM] * 2,
+        out_specs=VMEM,
+        out_shape=jax.ShapeDtypeStruct(moved.shape, BF16),
+        name="add_own",
+    )(moved, own)
+
+
+def arrange_kernel(per, head_ref, which_ref, *refs):
+    count = which_ref.shape[0]
+    blocks, out_ref, lend_ref, sems = refs[:count], refs[-3], refs[-2], refs[-1]
+    rows = blocks[0].shape[0]
+
+    def copies(s):
+        p = which_ref[s]
+        to = lend_ref.at[p // per // 2, pl.ds((p % per) * rows, rows)]
+        keep = pltpu.make_async_copy(blocks[s], out_ref.at[p], sems.at[0, s])
+        lend = pltpu.make_async_copy(blocks[s], to, sems.at[1, s])
+        return keep, lend, (p // per) % 2 != head_ref[0] % 2
+
+    for s in range(count):
+        keep, lend, needed = copies(s)
+        keep.start()
+        pl.when(needed)(lend.start)
+    for s in range(count):
+        keep, lend, needed = copies(s)
+        keep.wait()
+        pl.when(needed)(lend.wait)
+
+
+def arrange(per, n_head, head, which, blocks):
+    rows, cols = blocks[0].shape
+    count = len(blocks)
+    return call(
+        functools.partial(arrange_kernel, per),
+        in_specs=[SMEM] * 2 + [ANY] * count,
+        out_specs=[VMEM] * 2,
+        out_shape=[
+            jax.ShapeDtypeStruct((count, rows, cols), BF16),
+            jax.ShapeDtypeStruct((n_head // 2, per * rows, cols), BF16),
+        ],
+        scratch_shapes=[pltpu.SemaphoreType.DMA((2, count))],
+        name="arrange",
+    )(head, which, *blocks)
 
 
 def block_product(per, at_ref, x_ref, y_ref, w_ref, wy_ref):
@@ -345,27 +439,46 @@
     def across(x, bit):
         return lax.ppermute(x, "head", [(i, i ^ bit) for i in range(n_head)])
 
-    weight = lax.all_gather(value_weight, "ctx", axis_index_groups=lines)
+    order = list(range(0, pairs, 2)) + list(range(1, pairs, 2))[::-1]
+    place = [order.index(i) for i in range(pairs)]
+    moves = [
+        (2 * order[i] + k, 2 * order[(i + 1) % pairs] + k)
+        for i in range(pairs)
+        for k in range(2)
+    ]
+    spot = jnp.asarray(place, jnp.int32)[pair]
+    steps = jnp.arange(pairs, dtype=jnp.int32)
+
+    def ring(x):
+        return lax.ppermute(x, "ctx", moves)
 
     keep, send, near16 = states(par, queries, keys, values, out_grad)
     their_half = partner(send)
     line = pair.astype(jnp.int32).reshape(1)
-    offered = offer(line, keep, their_half, pairs)
 
     per = n_ctx // n_head // 2
     own, theirs = split(after(par, send), inputs, per)
+    vi = inside(after(queries, own), keys, out_grad)
+    blocks = [value_weight, ring(after(value_weight, send))]
     got_near = partner(after(near16, their_half))
     own, theirs = [own], [partner(after(theirs, their_half))]
 
+    offered = offer(line, after(keep, vi), their_half, pairs)
     every = lax.all_to_all(
         offered, "ctx", split_axis=0, concat_axis=0, axis_index_groups=lines
     )
     far, send_far = far_states(line, every)
+    ends = (far, partner(send_far), their_half, got_near)
     theirs = [after(theirs[0], send_far)]
-    ends = (far, partner(send_far), their_half, got_near)
-    vi = inside(queries, after(keys, send_far), out_grad)
+    token = send_far
     mine = finish_value(factor, par, keys, vi, ends)
     other = partner(mine)
+    query_grad, key_grad = others(
+        factor, par, queries, keys, after(values, mine), out_grad, ends
+    )
+    for _ in range(2, pairs):
+        blocks.append(ring(after(blocks[-1], token)))
+        token = mine
 
     offsets = [0]
     bit = n_head // 2
@@ -377,41 +490,43 @@
     own = [own[offsets.index(i)] for i in range(n_head)]
     theirs = [theirs[offsets.index(i)] for i in range(n_head)]
 
-    query_grad, key_grad = others(
-        factor, par, queries, keys, after(values, mine), out_grad, ends
-    )
-
-    which = jnp.arange(pairs, dtype=jnp.int32)
-    found = pieces(
-        (which // per) ^ head,
-        which % per,
-        after(mine, query_grad),
-        other,
-        own,
-        theirs,
-    )
-    summed = lax.psum_scatter(found, "ctx", axis_index_groups=lines)
-    weight_grad = finish_weight(1.0 / math.sqrt(length * n_ctx), summed)
-
-    weight = after(weight, found)
-    split_heads = weight.reshape(n_head // 2, 2, -1, cols)
-    lent = across(jnp.where(head % 2 == 0, split_heads[:, 1], split_heads[:, 0]), 1)
-    mine_too, other_too = across(mine, 1), across(other, 1)
+    which = jnp.asarray(order, jnp.int32)[(spot - 1 - steps) % pairs]
+    offs, subs = (which // per) ^ head, which % per
+    vals = (after(mine, query_grad), other, own, theirs)
+    (total,) = pieces(BF16, offs[:1], subs[:1], *vals)
+    moved = ring(total)
+    vals = (after(mine, total), other, own, theirs)
+    rest = pieces(F32, offs[1:], subs[1:], *vals)
+
     here = head.astype(jnp.int32).reshape(1)
+    held = jnp.asarray(order, jnp.int32)[(spot - steps) % pairs]
+    weight, lend = arrange(per, n_head, here, held, [after(blocks[0], rest[0])] + blocks[1:])
+    lent = across(lend, 1)
+    mine_too, other_too = across(after(mine, total), 1), across(other, 1)
 
     def summed_parts(x, y):
-        return [
-            across(head_part(here ^ off, per, x, y, weight, lent), off)
+        sent = [
+            head_part(here ^ off, per, x, y, weight, lent)
             for off in range(2, n_head, 2)
         ]
-
-    got_other = summed_parts(other, other_too)
-    got_mine = summed_parts(mine, mine_too)
-    swapped = partner(
-        head_part(here, per, other, other_too, weight, lent, got_other)
+        return sent[-1], [across(x, 2 * i + 2) for i, x in enumerate(sent)]
+
+    token, got_other = summed_parts(other, other_too)
+    total = add_own(moved, after(rest[0], token))
+    moved = ring(total)
+    token, got_mine = summed_parts(after(mine, total), mine_too)
+    for i in range(1, pairs - 2):
+        total = add_own(moved, after(rest[i], token))
+        moved = ring(total)
+    part = head_part(
+        here, per, after(other, total), other_too, weight, lent, got_other
+    )
+    swapped = partner(part)
+    weight_grad = finish_weight(
+        1.0 / math.sqrt(length * n_ctx), moved, after(rest[-1], part)
     )
     input_grad = join(
-        par, here, per, mine, mine_too, weight, lent, got_mine, swapped
+        par, here, per, after(mine, weight_grad), mine_too, weight, lent, got_mine, swapped
     )
     return (query_grad, key_grad, input_grad, weight_grad)
 

time: 124 us -> 115 us (0.927)
  between operations: 14.2 us -> 1.58 us
  waiting for transfers between devices: 58.6 us -> 48.9 us
  starting transfers between devices: 19.6 us -> 27.5 us
  Pallas kernels: 25 us -> 28 us
  local copies, waits for them, and re-layouts: 4.68 us -> 7.4 us
    ppermute x0 -> x6, waiting for transfers between devices: none -> 27.5 us  [ring(): return lax.ppermute(x, 'ctx', moves)]
    ppermute x11, waiting for transfers between devices: 26 us -> 2.02 us  [across(): return lax.ppermute(x, 'head', [(i, i ^ bit) for i in range(n_head)])]
    ppermute x0 -> x6, starting transfers between devices: none -> 11 us  [ring(): return lax.ppermute(x, 'ctx', moves)]
    all_to_all x1, waiting for transfers between devices: 13.9 us -> 6.61 us  [local(): lax.all_to_all(offered, 'ctx', split_axis=0, concat_axis=0, axis_index_gr...]
    reduce_scatter x1 -> x0, waiting for transfers between devices: 6.76 us -> none  [local(): summed = lax.psum_scatter(found, 'ctx', axis_index_groups=lines)]
    ppermute x6, starting transfers between devices: 8.29 us -> 5.67 us  [partner(): return lax.ppermute(x, 'ctx', [(i, i ^ 1) for i in range(n_ctx)])]
    pallas_call x3 -> x6, Pallas kernels: 8.4 us -> 10.9 us  [the longest x1 4.03 us: states(): call(states_kernel, vmem=60, in_specs=[SMEM] + [pl.BlockSpec(memory_space...]
    ppermute x6, waiting for transfers between devices: 11.3 us -> 12.7 us  [partner(): return lax.ppermute(x, 'ctx', [(i, i ^ 1) for i in range(n_ctx)])]
  transfers between devices with their start and end apart: 20 -> 24, of which waited for: 11 -> 10; matrix products, arithmetic and copies ran while one was open for 1% -> 3% of each run, Pallas kernels for 19% -> 17%
where the time goes in v9:
time: 115 us
  waiting for transfers between devices  48.9 us (43%)
  Pallas kernels  28 us (24%)
  starting transfers between devices  27.5 us (24%)
  local copies, waits for them, and re-layouts  7.4 us (6%)
  between operations  1.58 us (1%)
  other arithmetic  1.27 us (1%)
    ppermute x6, waiting for transfers between devices, ring(): return lax.ppermute(x, 'ctx', moves)  27.5 us
    ppermute x6, waiting for transfers between devices, partner(): return lax.ppermute(x, 'ctx', [(i, i ^ 1) for i in range(n_ctx)])  12.7 us
    ppermute x6, starting transfers between devices, ring(): return lax.ppermute(x, 'ctx', moves)  11 us
    all_to_all x1, waiting for transfers between devices, local(): lax.all_to_all(offered, 'ctx', split_axis=0, concat_axis=0, axis_index_gr...  6.61 us
    pallas_call x2, Pallas kernels, pieces(): call(functools.partial(piece_kernel, count), grid=(steps,), in_specs=[SME...  6.6 us
    ppermute x11, starting transfers between devices, across(): return lax.ppermute(x, 'head', [(i, i ^ bit) for i in range(n_head)])  5.92 us
    ppermute x6, starting transfers between devices, partner(): return lax.ppermute(x, 'ctx', [(i, i ^ 1) for i in range(n_ctx)])  5.67 us
    unnamed x32, local copies, waits for them, and re-layouts  5.32 us
  transfers between devices with their start and end apart: 24, of which 10 were waited for; matrix products, arithmetic and copies ran while one was open for 3% of the time, Pallas kernels for 17%

profile of v9, /device:TPU:0, one launch (start us, length us, event | category | flops | bytes accessed | tf_op | source)
XLA Modules:
  0.0 114.6 jit_solution(10334702889313392511)
XLA Ops:
  0.7 4.0 %states.1 = (f32[2,2,128,128]{3,2,1,0:T(8,128)}, bf16[2,2,128,128]{3,2,1,0:T(8,128)(2,1)}, bf16[2,2,128,128]{3,2,1,0:T(8,128)(2,1)}) custom-call(s32[1]{0:T(128)} %bitcast.par_ref, bf16[512,512]{1,0:T(8,128)(2,1)} %q_ref.1, bf16[512,512]{1,0:T(8,128)(2,1)} %k_ref.3, bf16[512,512]{1,0:T(8,128)(2,1)} %v_ref, bf16[512,512]{1,0:T(8,128)(2,1)} %g_ref.1), custom_call_target="tpu_custom_call" | custom-call | flops 1 | bytes 1 | tf_op jit(solution)/shard_map/states/pallas_call | solution.py:69
  4.7 3.0 %collective-permute-start = (bf16[2,2,128,128]{3,2,1,0:T(8,128)(2,1)}, bf16[2,2,128,128]{3,2,1,0:T(8,128)(2,1)S(1)}, u32[]{:S(2)}, u32[]{:S(2)}) collective-permute-start(bf16[2,2,128,128]{3,2,1,0:T(8,128)(2,1)} %get-tuple-element.37), channel_id=1, source_target_pairs={{0,4},{4,0},{8,12},{12,8},{16,20},{20,16},{24,28},{28,24},{1,5},{5... | collective-permute-start | bytes 393224 | tf_op jit(solution)/shard_map/ppermute | solution.py:437
  7.7 2.6 %collective-permute-start.13 = (bf16[512,512]{1,0:T(8,128)(2,1)S(1)}, bf16[512,512]{1,0:T(8,128)(2,1)}, u32[]{:S(2)}, u32[]{:S(2)}) collective-permute-start(bf16[512,512]{1,0:T(8,128)(2,1)S(1)} %copy-done.11), channel_id=1, source_target_pairs={{0,16},{4,20},{16,24},{20,28},{24,8},{28,12},{8,0},{12,4},{1,17},{... | collective-permute-start | bytes 1572872 | tf_op jit(solution)/shard_map/ppermute | solution.py:453
  10.3 1.2 %copy-done.6 = bf16[512,1024]{1,0:T(8,128)(2,1)S(1)} copy-done((bf16[512,1024]{1,0:T(8,128)(2,1)S(1)}, bf16[512,1024]{1,0:T(8,128)(2,1)}, u32[]{:S(2)}) %copy-start.6) | copy-done | bytes 1048600
  11.5 1.1 split.1
  13.2 3.0 %inside.1.vi_ref = f32[512,512]{1,0:T(8,128)S(1)} custom-call(bf16[512,512]{1,0:T(8,128)(2,1)S(1)} %copy-done.1, bf16[512,512]{1,0:T(8,128)(2,1)S(1)} %copy-done, bf16[512,512]{1,0:T(8,128)(2,1)S(1)} %copy-done.2), custom_call_target="tpu_custom_call" | custom-call | flops 1 | bytes 1 | tf_op jit(solution)/shard_map/inside/pallas_call | solution.py:135
  16.2 1.0 copy-done.3
  17.9 5.0 %all-to-all-start = ((bf16[4,2,128,128]{3,2,1,0:T(8,128)(2,1)}), bf16[4,2,128,128]{3,2,1,0:T(8,128)(2,1)S(1)}, u32[]{:S(2)}, u32[]{:S(2)}) async-start(bf16[4,2,128,128]{3,2,1,0:T(8,128)(2,1)} %offer.1), calls=%async_computation | async-start | bytes 524288 | tf_op jit(solution)/shard_map/all_to_all | solution.py:467
  22.9 1.5 %collective-permute-start.5 = (bf16[1,512,512]{2,1,0:T(8,128)(2,1)}, bf16[1,512,512]{2,1,0:T(8,128)(2,1)}, u32[]{:S(2)}, u32[]{:S(2)}) collective-permute-start(bf16[1,512,512]{2,1,0:T(8,128)(2,1)} %get-tuple-element.39.refs_0_), channel_id=1, source_target_pairs={{0,2},{1,3},{2,0},{3,1},{4,6},{5,7},{6,4},{7,5},{8,10},{9,11},{10,... | collective-permute-start | bytes 1572872 | tf_op jit(solution)/shard_map/ppermute | solution.py:440
  24.5 6.6 %all-to-all-done.every_ref = bf16[4,2,128,128]{3,2,1,0:T(8,128)(2,1)S(1)} async-done(((bf16[4,2,128,128]{3,2,1,0:T(8,128)(2,1)}), bf16[4,2,128,128]{3,2,1,0:T(8,128)(2,1)S(1)}, u32[]{:S(2)}, u32[]{:S(2)}) %all-to-all-start) | async-done | bytes 262176 | tf_op jit(solution)/shard_map/all_to_all | solution.py:467
  31.3 1.6 %collective-permute-start.9 = (bf16[1,512,512]{2,1,0:T(8,128)(2,1)}, bf16[1,512,512]{2,1,0:T(8,128)(2,1)}, u32[]{:S(2)}, u32[]{:S(2)}) collective-permute-start(bf16[1,512,512]{2,1,0:T(8,128)(2,1)} %collective-permute-done.7.refs_4_), channel_id=1, source_target_pairs={{0,2},{1,3},{2,0},{3,1},{4,6},{5,7},{6,4},{7,5},{8,10},{9,11},{10,... | collective-permute-start | bytes 1572872 | tf_op jit(solution)/shard_map/ppermute | solution.py:440
  33.4 5.3 %collective-permute-done.2.refs_3_ = bf16[2,2,128,128]{3,2,1,0:T(8,128)(2,1)S(1)} collective-permute-done((bf16[2,2,128,128]{3,2,1,0:T(8,128)(2,1)}, bf16[2,2,128,128]{3,2,1,0:T(8,128)(2,1)S(1)}, u32[]{:S(2)}, u32[]{:S(2)}) %collective-permute-start.2) | collective-permute-done | bytes 131104 | tf_op jit(solution)/shard_map/ppermute | solution.py:437
  40.6 3.1 %collective-permute-done.1.refs_1_ = bf16[2,2,128,128]{3,2,1,0:T(8,128)(2,1)S(1)} collective-permute-done((bf16[2,2,128,128]{3,2,1,0:T(8,128)(2,1)S(1)}, bf16[2,2,128,128]{3,2,1,0:T(8,128)(2,1)S(1)}, u32[]{:S(2)}, u32[]{:S(2)}) %collective-permute-start.1) | collective-permute-done | bytes 131104 | tf_op jit(solution)/shard_map/ppermute | solution.py:437
  43.7 1.3 %copy-done.4 = f32[512,512]{1,0:T(8,128)S(1)} copy-done((f32[512,512]{1,0:T(8,128)S(1)}, f32[512,512]{1,0:T(8,128)}, u32[]{:S(2)}) %copy-start.4) | copy-done | bytes 1048600
  46.0 1.6 %collective-permute-start.15 = (bf16[512,512]{1,0:T(8,128)(2,1)}, bf16[512,512]{1,0:T(8,128)(2,1)}, u32[]{:S(2)}, u32[]{:S(2)}) collective-permute-start(bf16[512,512]{1,0:T(8,128)(2,1)} %collective-permute-done.14.refs_2_), channel_id=1, source_target_pairs={{0,16},{4,20},{16,24},{20,28},{24,8},{28,12},{8,0},{12,4},{1,17},{... | collective-permute-start | bytes 1572872 | tf_op jit(solution)/shard_map/ppermute | solution.py:453
  50.4 0.9 copy-done.8
  51.3 0.9 copy-done.10
  52.2 4.1 %others.1 = (bf16[512,512]{1,0:T(8,128)(2,1)}, bf16[512,512]{1,0:T(8,128)(2,1)}) custom-call(s32[1]{0:T(128)} %bitcast.par_ref, bf16[512,512]{1,0:T(8,128)(2,1)S(1)} %copy-done.1, bf16[512,512]{1,0:T(8,128)(2,1)S(1)} %copy-done, bf16[512,512]{1,0:T(8,128)(2,1)S(1)} %copy-done.5, bf16[512,512]{1,0:T(8,128)(2,1)S(1)} %copy-done.2, ...), custom_call_target="tpu_custom_call" | custom-call | flops 1 | bytes 1 | tf_op jit(solution)/shard_map/others/pallas_call | solution.py:235
  56.3 3.5 %collective-permute-done.3.b_ref.x_ref = bf16[512,512]{1,0:T(8,128)(2,1)S(1)} collective-permute-done((bf16[512,512]{1,0:T(8,128)(2,1)S(1)}, bf16[512,512]{1,0:T(8,128)(2,1)S(1)}, u32[]{:S(2)}, u32[]{:S(2)}) %collective-permute-start.3) | collective-permute-done | bytes 524320 | tf_op jit(solution)/shard_map/ppermute | solution.py:437
  59.8 2.0 %pieces.2 = bf16[512,512]{1,0:T(8,128)(2,1)S(1)} custom-call(s32[1]{0:T(128)S(1)} %bitcast.9, s32[1]{0:T(128)} %constant.81.clone.1.subs_ref, bf16[512,512]{1,0:T(8,128)(2,1)S(1)} %finish_value.1.a_ref.x_ref, bf16[512,512]{1,0:T(8,128)(2,1)S(1)} %collective-permute-done.3.b_ref.x_ref, bf16[1,512,512]{2,1,0:T(8,128)(2,1)} %get-tuple-element.39.refs_0_, ...), custom_call_target="tpu_custom_call" | custom-call | flops 1 | bytes 1 | tf_op jit(solution)/shard_map/pieces/pallas_call | solution.py:289
  61.8 4.6 %pieces.3 = (f32[512,512]{1,0:T(8,128)S(1)}, f32[512,512]{1,0:T(8,128)S(1)}, f32[512,512]{1,0:T(8,128)S(1)}) custom-call(s32[3]{0:T(128)S(1)} %slice.11.offs_ref, s32[3]{0:T(128)S(1)} %slice.12.subs_ref, bf16[512,512]{1,0:T(8,128)(2,1)S(1)} %finish_value.1.a_ref.x_ref, bf16[512,512]{1,0:T(8,128)(2,1)S(1)} %collective-permute-done.3.b_ref.x_ref, ...), custom_call_target="tpu_custom_call" | custom-call | flops 1 | bytes 1 | tf_op jit(solution)/shard_map/pieces/pallas_call | solution.py:289
  66.5 2.4 %arrange.1 = (bf16[4,512,512]{2,1,0:T(8,128)(2,1)S(1)}, bf16[2,512,512]{2,1,0:T(8,128)(2,1)S(1)}) custom-call(s32[1]{0:T(128)} %bitcast.2.head_ref.at_ref, s32[4]{0:T(128)S(1)} %gather_fusion.1, bf16[512,512]{1,0:T(8,128)(2,1)S(1)} %copy-done.12, bf16[512,512]{1,0:T(8,128)(2,1)} %collective-permute-done.13.refs_1_, ...), custom_call_target="tpu_custom_call" | custom-call | flops 1 | bytes 1 | tf_op jit(solution)/shard_map/arrange/pallas_call | solution.py:359
  69.4 1.7 %collective-permute-start.11 = (bf16[512,512]{1,0:T(8,128)(2,1)S(1)}, bf16[512,512]{1,0:T(8,128)(2,1)S(1)}, u32[]{:S(2)}, u32[]{:S(2)}) collective-permute-start(bf16[512,512]{1,0:T(8,128)(2,1)S(1)} %pieces.2), channel_id=1, source_target_pairs={{0,16},{4,20},{16,24},{20,28},{24,8},{28,12},{8,0},{12,4},{1,17},{... | collective-permute-start | bytes 1572872 | tf_op jit(solution)/shard_map/ppermute | solution.py:453
  71.1 1.2 %collective-permute-done.12.y_ref = bf16[512,512]{1,0:T(8,128)(2,1)S(1)} collective-permute-done((bf16[512,512]{1,0:T(8,128)(2,1)S(1)}, bf16[512,512]{1,0:T(8,128)(2,1)S(1)}, u32[]{:S(2)}, u32[]{:S(2)}) %collective-permute-start.12) | collective-permute-done | bytes 524320 | tf_op jit(solution)/shard_map/ppermute | solution.py:440
  73.1 10.3 %collective-permute-done.11.moved_ref = bf16[512,512]{1,0:T(8,128)(2,1)S(1)} collective-permute-done((bf16[512,512]{1,0:T(8,128)(2,1)S(1)}, bf16[512,512]{1,0:T(8,128)(2,1)S(1)}, u32[]{:S(2)}, u32[]{:S(2)}) %collective-permute-start.11) | collective-permute-done | bytes 524320 | tf_op jit(solution)/shard_map/ppermute | solution.py:453
  83.5 2.5 %collective-permute-start.17 = (bf16[512,512]{1,0:T(8,128)(2,1)S(1)}, bf16[512,512]{1,0:T(8,128)(2,1)S(1)}, u32[]{:S(2)}, u32[]{:S(2)}) collective-permute-start(bf16[512,512]{1,0:T(8,128)(2,1)S(1)} %add_own.2), channel_id=1, source_target_pairs={{0,16},{4,20},{16,24},{20,28},{24,8},{28,12},{8,0},{12,4},{1,17},{... | collective-permute-start | bytes 1572872 | tf_op jit(solution)/shard_map/ppermute | solution.py:453
  87.3 1.6 %collective-permute-start.21 = (bf16[512,512]{1,0:T(8,128)(2,1)S(1)}, bf16[512,512]{1,0:T(8,128)(2,1)S(1)}, u32[]{:S(2)}, u32[]{:S(2)}) collective-permute-start(bf16[512,512]{1,0:T(8,128)(2,1)S(1)} %head_part.4), channel_id=1, source_target_pairs={{0,2},{1,3},{2,0},{3,1},{4,6},{5,7},{6,4},{7,5},{8,10},{9,11},{10,... | collective-permute-start | bytes 1572872 | tf_op jit(solution)/shard_map/ppermute | solution.py:440
  88.9 8.7 %collective-permute-done.17.moved_ref = bf16[512,512]{1,0:T(8,128)(2,1)S(1)} collective-permute-done((bf16[512,512]{1,0:T(8,128)(2,1)S(1)}, bf16[512,512]{1,0:T(8,128)(2,1)S(1)}, u32[]{:S(2)}, u32[]{:S(2)}) %collective-permute-start.17) | collective-permute-done | bytes 524320 | tf_op jit(solution)/shard_map/ppermute | solution.py:453
  97.6 2.5 %collective-permute-start.19 = (bf16[512,512]{1,0:T(8,128)(2,1)S(1)}, bf16[512,512]{1,0:T(8,128)(2,1)S(1)}, u32[]{:S(2)}, u32[]{:S(2)}) collective-permute-start(bf16[512,512]{1,0:T(8,128)(2,1)S(1)} %add_own.3), channel_id=1, source_target_pairs={{0,16},{4,20},{16,24},{20,28},{24,8},{28,12},{8,0},{12,4},{1,17},{... | collective-permute-start | bytes 1572872 | tf_op jit(solution)/shard_map/ppermute | solution.py:453
  102.2 8.5 %collective-permute-done.19.moved_ref = bf16[512,512]{1,0:T(8,128)(2,1)S(1)} collective-permute-done((bf16[512,512]{1,0:T(8,128)(2,1)S(1)}, bf16[512,512]{1,0:T(8,128)(2,1)S(1)}, u32[]{:S(2)}, u32[]{:S(2)}) %collective-permute-start.19) | collective-permute-done | bytes 524320 | tf_op jit(solution)/shard_map/ppermute | solution.py:453
  110.7 1.3 %finish_weight.1 = f32[512,512]{1,0:T(8,128)} custom-call(bf16[512,512]{1,0:T(8,128)(2,1)S(1)} %collective-permute-done.19.moved_ref, f32[512,512]{1,0:T(8,128)S(1)} %get-tuple-element.68.own_ref), custom_call_target="tpu_custom_call" | custom-call | flops 1 | bytes 1 | tf_op jit(solution)/shard_map/finish_weight/pallas_call | solution.py:311
  112.8 1.8 %join.1 = bf16[512,1024]{1,0:T(8,128)(2,1)} custom-call(s32[1]{0:T(128)} %bitcast.par_ref, s32[1]{0:T(128)} %bitcast.2.head_ref.at_ref, bf16[512,512]{1,0:T(8,128)(2,1)S(1)} %finish_value.1.a_ref.x_ref, bf16[512,512]{1,0:T(8,128)(2,1)S(1)} %collective-permute-done.18.y_ref, bf16[4,512,512]{2,1,0:T(8,128)(2,1)S(1)} %get-tuple-element.60.w_ref, ...), custom_call_target="tpu_custom_call" | custom-call | flops 1 | bytes 1 | tf_op jit(solution)/shard_map/join/pallas_call | solution.py:414
  (75 shorter events, 12.7 us)
Async XLA Ops:
  0.6 12.6 %copy-start = (bf16[512,512]{1,0:T(8,128)(2,1)S(1)}, bf16[512,512]{1,0:T(8,128)(2,1)}, u32[]{:S(2)}) copy-start(bf16[512,512]{1,0:T(8,128)(2,1)} %k_ref.3) | copy-start | bytes 1572868
  0.6 12.6 %copy-start.2 = (bf16[512,512]{1,0:T(8,128)(2,1)S(1)}, bf16[512,512]{1,0:T(8,128)(2,1)}, u32[]{:S(2)}) copy-start(bf16[512,512]{1,0:T(8,128)(2,1)} %g_ref.1) | copy-start | bytes 1572868
  0.7 12.5 %copy-start.1 = (bf16[512,512]{1,0:T(8,128)(2,1)S(1)}, bf16[512,512]{1,0:T(8,128)(2,1)}, u32[]{:S(2)}) copy-start(bf16[512,512]{1,0:T(8,128)(2,1)} %q_ref.1) | copy-start | bytes 1572868
  0.7 7.1 %copy-start.11 = (bf16[512,512]{1,0:T(8,128)(2,1)S(1)}, bf16[512,512]{1,0:T(8,128)(2,1)}, u32[]{:S(2)}) copy-start(bf16[512,512]{1,0:T(8,128)(2,1)} %refs_0_.3) | copy-start | bytes 1572868
  4.7 7.9 %collective-permute-start = (bf16[2,2,128,128]{3,2,1,0:T(8,128)(2,1)}, bf16[2,2,128,128]{3,2,1,0:T(8,128)(2,1)S(1)}, u32[]{:S(2)}, u32[]{:S(2)}) collective-permute-start(bf16[2,2,128,128]{3,2,1,0:T(8,128)(2,1)} %get-tuple-element.37), channel_id=1, source_target_pairs={{0,4},{4,0},{8,12},{12,8},{16,20},{20,16},{24,28},{28,24},{1,5},{5... | collective-permute-start | bytes 393224 | tf_op jit(solution)/shard_map/ppermute | solution.py:437
  7.7 23.4 %collective-permute-start.13 = (bf16[512,512]{1,0:T(8,128)(2,1)S(1)}, bf16[512,512]{1,0:T(8,128)(2,1)}, u32[]{:S(2)}, u32[]{:S(2)}) collective-permute-start(bf16[512,512]{1,0:T(8,128)(2,1)S(1)} %copy-done.11), channel_id=1, source_target_pairs={{0,16},{4,20},{16,24},{20,28},{24,8},{28,12},{8,0},{12,4},{1,17},{... | collective-permute-start | bytes 1572872 | tf_op jit(solution)/shard_map/ppermute | solution.py:453
  12.6 26.6 %copy-start.15 = (s32[4]{0:T(128)S(1)}, s32[4]{0:T(128)}, u32[]{:S(2)}) copy-start(s32[4]{0:T(128)} %constant.83.clone) | copy-start | bytes 52
  12.7 18.7 %collective-permute-start.7 = (bf16[1,512,512]{2,1,0:T(8,128)(2,1)}, bf16[1,512,512]{2,1,0:T(8,128)(2,1)}, u32[]{:S(2)}, u32[]{:S(2)}) collective-permute-start(bf16[1,512,512]{2,1,0:T(8,128)(2,1)} %get-tuple-element.52), channel_id=1, source_target_pairs={{0,4},{4,0},{8,12},{12,8},{16,20},{20,16},{24,28},{28,24},{1,5},{5... | collective-permute-start | bytes 1572872 | tf_op jit(solution)/shard_map/ppermute | solution.py:437
  17.2 30.5 %copy-start.14 = (s32[4]{0:T(128)S(1)}, s32[4]{0:T(128)}, u32[]{:S(2)}) copy-start(s32[4]{0:T(128)} %constant.84.clone) | copy-start | bytes 52
  17.9 32.5 %copy-start.5 = (bf16[512,512]{1,0:T(8,128)(2,1)S(1)}, bf16[512,512]{1,0:T(8,128)(2,1)}, u32[]{:S(2)}) copy-start(bf16[512,512]{1,0:T(8,128)(2,1)} %v_ref) | copy-start | bytes 1572868
  17.9 13.1 %all-to-all-start = ((bf16[4,2,128,128]{3,2,1,0:T(8,128)(2,1)}), bf16[4,2,128,128]{3,2,1,0:T(8,128)(2,1)S(1)}, u32[]{:S(2)}, u32[]{:S(2)}) async-start(bf16[4,2,128,128]{3,2,1,0:T(8,128)(2,1)} %offer.1), calls=%async_computation | async-start | bytes 524288 | tf_op jit(solution)/shard_map/all_to_all | solution.py:467
  22.9 17.5 %collective-permute-start.5 = (bf16[1,512,512]{2,1,0:T(8,128)(2,1)}, bf16[1,512,512]{2,1,0:T(8,128)(2,1)}, u32[]{:S(2)}, u32[]{:S(2)}) collective-permute-start(bf16[1,512,512]{2,1,0:T(8,128)(2,1)} %get-tuple-element.39.refs_0_), channel_id=1, source_target_pairs={{0,2},{1,3},{2,0},{3,1},{4,6},{5,7},{6,4},{7,5},{8,10},{9,11},{10,... | collective-permute-start | bytes 1572872 | tf_op jit(solution)/shard_map/ppermute | solution.py:440
  31.2 14.3 %collective-permute-start.14 = (bf16[512,512]{1,0:T(8,128)(2,1)}, bf16[512,512]{1,0:T(8,128)(2,1)}, u32[]{:S(2)}, u32[]{:S(2)}) collective-permute-start(bf16[512,512]{1,0:T(8,128)(2,1)} %collective-permute-done.13.refs_1_), channel_id=1, source_target_pairs={{0,16},{4,20},{16,24},{20,28},{24,8},{28,12},{8,0},{12,4},{1,17},{... | collective-permute-start | bytes 1572872 | tf_op jit(solution)/shard_map/ppermute | solution.py:453
  31.2 14.8 %collective-permute-start.4 = (bf16[1,512,512]{2,1,0:T(8,128)(2,1)}, bf16[1,512,512]{2,1,0:T(8,128)(2,1)}, u32[]{:S(2)}, u32[]{:S(2)}) collective-permute-start(bf16[1,512,512]{2,1,0:T(8,128)(2,1)} %get-tuple-element.39.refs_0_), channel_id=1, source_target_pairs={{0,1},{1,0},{2,3},{3,2},{4,5},{5,4},{6,7},{7,6},{8,9},{9,8},{10,11... | collective-permute-start | bytes 1572872 | tf_op jit(solution)/shard_map/ppermute | solution.py:440
  31.3 16.3 %collective-permute-start.9 = (bf16[1,512,512]{2,1,0:T(8,128)(2,1)}, bf16[1,512,512]{2,1,0:T(8,128)(2,1)}, u32[]{:S(2)}, u32[]{:S(2)}) collective-permute-start(bf16[1,512,512]{2,1,0:T(8,128)(2,1)} %collective-permute-done.7.refs_4_), channel_id=1, source_target_pairs={{0,2},{1,3},{2,0},{3,1},{4,6},{5,7},{6,4},{7,5},{8,10},{9,11},{10,... | collective-permute-start | bytes 1572872 | tf_op jit(solution)/shard_map/ppermute | solution.py:440
  32.9 5.8 %collective-permute-start.2 = (bf16[2,2,128,128]{3,2,1,0:T(8,128)(2,1)}, bf16[2,2,128,128]{3,2,1,0:T(8,128)(2,1)S(1)}, u32[]{:S(2)}, u32[]{:S(2)}) collective-permute-start(bf16[2,2,128,128]{3,2,1,0:T(8,128)(2,1)} %get-tuple-element.46), channel_id=1, source_target_pairs={{0,4},{4,0},{8,12},{12,8},{16,20},{20,16},{24,28},{28,24},{1,5},{5... | collective-permute-start | bytes 393224 | tf_op jit(solution)/shard_map/ppermute | solution.py:437
  38.7 6.7 %copy-start.7 = (bf16[2,2,128,128]{3,2,1,0:T(8,128)(2,1)}, bf16[2,2,128,128]{3,2,1,0:T(8,128)(2,1)S(1)}, u32[]{:S(2)}) copy-start(bf16[2,2,128,128]{3,2,1,0:T(8,128)(2,1)S(1)} %collective-permute-done.2.refs_3_) | copy-start | bytes 393220
  38.7 5.0 %collective-permute-start.1 = (bf16[2,2,128,128]{3,2,1,0:T(8,128)(2,1)S(1)}, bf16[2,2,128,128]{3,2,1,0:T(8,128)(2,1)S(1)}, u32[]{:S(2)}, u32[]{:S(2)}) collective-permute-start(bf16[2,2,128,128]{3,2,1,0:T(8,128)(2,1)S(1)} %get-tuple-element.44), channel_id=1, source_target_pairs={{0,4},{4,0},{8,12},{12,8},{16,20},{20,16},{24,28},{28,24},{1,5},{5... | collective-permute-start | bytes 393224 | tf_op jit(solution)/shard_map/ppermute | solution.py:437
  40.5 15.8 %collective-permute-start.6 = (bf16[1,512,512]{2,1,0:T(8,128)(2,1)}, bf16[1,512,512]{2,1,0:T(8,128)(2,1)}, u32[]{:S(2)}, u32[]{:S(2)}) collective-permute-start(bf16[1,512,512]{2,1,0:T(8,128)(2,1)} %collective-permute-done.5.refs_2_), channel_id=1, source_target_pairs={{0,1},{1,0},{2,3},{3,2},{4,5},{5,4},{6,7},{7,6},{8,9},{9,8},{10,11... | collective-permute-start | bytes 1572872 | tf_op jit(solution)/shard_map/ppermute | solution.py:440
  43.7 12.6 %collective-permute-start.8 = (bf16[1,512,512]{2,1,0:T(8,128)(2,1)}, bf16[1,512,512]{2,1,0:T(8,128)(2,1)}, u32[]{:S(2)}, u32[]{:S(2)}) collective-permute-start(bf16[1,512,512]{2,1,0:T(8,128)(2,1)} %collective-permute-done.7.refs_4_), channel_id=1, source_target_pairs={{0,1},{1,0},{2,3},{3,2},{4,5},{5,4},{6,7},{7,6},{8,9},{9,8},{10,11... | collective-permute-start | bytes 1572872 | tf_op jit(solution)/shard_map/ppermute | solution.py:440
  45.5 14.4 %collective-permute-start.3 = (bf16[512,512]{1,0:T(8,128)(2,1)S(1)}, bf16[512,512]{1,0:T(8,128)(2,1)S(1)}, u32[]{:S(2)}, u32[]{:S(2)}) collective-permute-start(bf16[512,512]{1,0:T(8,128)(2,1)S(1)} %finish_value.1.a_ref.x_ref), channel_id=1, source_target_pairs={{0,4},{4,0},{8,12},{12,8},{16,20},{20,16},{24,28},{28,24},{1,5},{5... | collective-permute-start | bytes 1572872 | tf_op jit(solution)/shard_map/ppermute | solution.py:437
  46.0 20.4 %collective-permute-start.15 = (bf16[512,512]{1,0:T(8,128)(2,1)}, bf16[512,512]{1,0:T(8,128)(2,1)}, u32[]{:S(2)}, u32[]{:S(2)}) collective-permute-start(bf16[512,512]{1,0:T(8,128)(2,1)} %collective-permute-done.14.refs_2_), channel_id=1, source_target_pairs={{0,16},{4,20},{16,24},{20,28},{24,8},{28,12},{8,0},{12,4},{1,17},{... | collective-permute-start | bytes 1572872 | tf_op jit(solution)/shard_map/ppermute | solution.py:453
  47.7 12.2 %collective-permute-start.10 = (bf16[1,512,512]{2,1,0:T(8,128)(2,1)}, bf16[1,512,512]{2,1,0:T(8,128)(2,1)}, u32[]{:S(2)}, u32[]{:S(2)}) collective-permute-start(bf16[1,512,512]{2,1,0:T(8,128)(2,1)} %collective-permute-done.9.refs_6_), channel_id=1, source_target_pairs={{0,1},{1,0},{2,3},{3,2},{4,5},{5,4},{6,7},{7,6},{8,9},{9,8},{10,11... | collective-permute-start | bytes 1572872 | tf_op jit(solution)/shard_map/ppermute | solution.py:440
  68.9 3.5 %collective-permute-start.16 = (bf16[2,512,512]{2,1,0:T(8,128)(2,1)S(1)}, bf16[2,512,512]{2,1,0:T(8,128)(2,1)S(1)}, u32[]{:S(2)}, u32[]{:S(2)}) collective-permute-start(bf16[2,512,512]{2,1,0:T(8,128)(2,1)S(1)} %get-tuple-element.61), channel_id=1, source_target_pairs={{0,1},{1,0},{2,3},{3,2},{4,5},{5,4},{6,7},{7,6},{8,9},{9,8},{10,11... | collective-permute-start | bytes 3145736 | tf_op jit(solution)/shard_map/ppermute | solution.py:440
  68.9 3.4 %collective-permute-start.12 = (bf16[512,512]{1,0:T(8,128)(2,1)S(1)}, bf16[512,512]{1,0:T(8,128)(2,1)S(1)}, u32[]{:S(2)}, u32[]{:S(2)}) collective-permute-start(bf16[512,512]{1,0:T(8,128)(2,1)S(1)} %collective-permute-done.3.b_ref.x_ref), channel_id=1, source_target_pairs={{0,1},{1,0},{2,3},{3,2},{4,5},{5,4},{6,7},{7,6},{8,9},{9,8},{10,11... | collective-permute-start | bytes 1572872 | tf_op jit(solution)/shard_map/ppermute | solution.py:440
  69.4 14.0 %collective-permute-start.11 = (bf16[512,512]{1,0:T(8,128)(2,1)S(1)}, bf16[512,512]{1,0:T(8,128)(2,1)S(1)}, u32[]{:S(2)}, u32[]{:S(2)}) collective-permute-start(bf16[512,512]{1,0:T(8,128)(2,1)S(1)} %pieces.2), channel_id=1, source_target_pairs={{0,16},{4,20},{16,24},{20,28},{24,8},{28,12},{8,0},{12,4},{1,17},{... | collective-permute-start | bytes 1572872 | tf_op jit(solution)/shard_map/ppermute | solution.py:453
  71.1 15.5 %collective-permute-start.18 = (bf16[512,512]{1,0:T(8,128)(2,1)S(1)}, bf16[512,512]{1,0:T(8,128)(2,1)S(1)}, u32[]{:S(2)}, u32[]{:S(2)}) collective-permute-start(bf16[512,512]{1,0:T(8,128)(2,1)S(1)} %finish_value.1.a_ref.x_ref), channel_id=1, source_target_pairs={{0,1},{1,0},{2,3},{3,2},{4,5},{5,4},{6,7},{7,6},{8,9},{9,8},{10,11... | collective-permute-start | bytes 1572872 | tf_op jit(solution)/shard_map/ppermute | solution.py:440
  83.5 14.0 %collective-permute-start.17 = (bf16[512,512]{1,0:T(8,128)(2,1)S(1)}, bf16[512,512]{1,0:T(8,128)(2,1)S(1)}, u32[]{:S(2)}, u32[]{:S(2)}) collective-permute-start(bf16[512,512]{1,0:T(8,128)(2,1)S(1)} %add_own.2), channel_id=1, source_target_pairs={{0,16},{4,20},{16,24},{20,28},{24,8},{28,12},{8,0},{12,4},{1,17},{... | collective-permute-start | bytes 1572872 | tf_op jit(solution)/shard_map/ppermute | solution.py:453
  86.0 14.9 %collective-permute-start.20 = (bf16[512,512]{1,0:T(8,128)(2,1)S(1)}, bf16[512,512]{1,0:T(8,128)(2,1)S(1)}, u32[]{:S(2)}, u32[]{:S(2)}) collective-permute-start(bf16[512,512]{1,0:T(8,128)(2,1)S(1)} %head_part.3), channel_id=1, source_target_pairs={{0,2},{1,3},{2,0},{3,1},{4,6},{5,7},{6,4},{7,5},{8,10},{9,11},{10,... | collective-permute-start | bytes 1572872 | tf_op jit(solution)/shard_map/ppermute | solution.py:440
  87.3 24.8 %collective-permute-start.21 = (bf16[512,512]{1,0:T(8,128)(2,1)S(1)}, bf16[512,512]{1,0:T(8,128)(2,1)S(1)}, u32[]{:S(2)}, u32[]{:S(2)}) collective-permute-start(bf16[512,512]{1,0:T(8,128)(2,1)S(1)} %head_part.4), channel_id=1, source_target_pairs={{0,2},{1,3},{2,0},{3,1},{4,6},{5,7},{6,4},{7,5},{8,10},{9,11},{10,... | collective-permute-start | bytes 1572872 | tf_op jit(solution)/shard_map/ppermute | solution.py:440
  97.6 13.1 %collective-permute-start.19 = (bf16[512,512]{1,0:T(8,128)(2,1)S(1)}, bf16[512,512]{1,0:T(8,128)(2,1)S(1)}, u32[]{:S(2)}, u32[]{:S(2)}) collective-permute-start(bf16[512,512]{1,0:T(8,128)(2,1)S(1)} %add_own.3), channel_id=1, source_target_pairs={{0,16},{4,20},{16,24},{20,28},{24,8},{28,12},{8,0},{12,4},{1,17},{... | collective-permute-start | bytes 1572872 | tf_op jit(solution)/shard_map/ppermute | solution.py:453
  101.6 11.2 %collective-permute-start.22 = (bf16[512,512]{1,0:T(8,128)(2,1)S(1)}, bf16[512,512]{1,0:T(8,128)(2,1)S(1)}, u32[]{:S(2)}, u32[]{:S(2)}) collective-permute-start(bf16[512,512]{1,0:T(8,128)(2,1)S(1)} %head_part.5), channel_id=1, source_target_pairs={{0,4},{4,0},{8,12},{12,8},{16,20},{20,16},{24,28},{28,24},{1,5},{5... | collective-permute-start | bytes 1572872 | tf_op jit(solution)/shard_map/ppermute | solution.py:437
  (8 other events, 17.3 us)

commit v10 on v9

--- a/solution.py
+++ b/solution.py
@@ -78,35 +78,45 @@
     )(par, *arrays)
 
 
-def split_kernel(per, par_ref, x_ref, own_ref, theirs_ref):
-    width = x_ref.shape[1] // (2 * per)
+def split_kernel(per, par_ref, x_ref, own_ref, theirs_ref, sems):
+    width = own_ref.shape[2]
     for k in range(2):
-        for i in range(per):
-            block = x_ref[:, (2 * i + k) * width : (2 * i + k + 1) * width]
-
-            @pl.when(par_ref[0] == k)
-            def _():
-                own_ref[i] = block
-
-            @pl.when(par_ref[0] != k)
-            def _():
-                theirs_ref[i] = block
+
+        @pl.when(par_ref[0] == k)
+        def _():
+            copies = []
+            for i in range(per):
+                for j, out_ref in enumerate((own_ref, theirs_ref)):
+                    at = (2 * i + (k ^ j)) * width
+                    if width % 128:
+                        out_ref[i] = x_ref[:, at : at + width]
+                    else:
+                        src = x_ref.at[:, pl.ds(at, width)]
+                        copies.append(
+                            pltpu.make_async_copy(src, out_ref.at[i], sems.at[j, i])
+                        )
+            for c in copies:
+                c.start()
+            for c in copies:
+                c.wait()
 
 
 def split(par, x, per):
     width = x.shape[1] // (2 * per)
     out = jax.ShapeDtypeStruct((per, x.shape[0], width), x.dtype)
+    place = VMEM if width % 128 else pl.BlockSpec(memory_space=pltpu.HBM)
     return call(
         functools.partial(split_kernel, per),
-        in_specs=[SMEM, VMEM],
+        in_specs=[SMEM, place],
         out_specs=[VMEM] * 2,
         out_shape=[out, out],
+        scratch_shapes=[pltpu.SemaphoreType.DMA((2, per))],
         name="split",
     )(par, x)
 
 
 def inside_kernel(*refs):
-    arrays, out_ref, bufs, sems = refs[:3], refs[3], refs[4:7], refs[7]
+    arrays, (out_ref, k_ref), bufs, sems = refs[:3], refs[3:5], refs[5:8], refs[8]
     n, cols = out_ref.shape
     heads = cols // DH
 
@@ -128,6 +138,7 @@
         q, k, g = (x[:, at] for x in bufs)
         scores = jnp.where(causal, dot(q, k, 1, 1), 0.0).astype(BF16)
         out_ref[:, at] = dot(scores, g, 0, 0)
+        k_ref[:, at] = k
 
 
 def inside(*arrays):
@@ -135,8 +146,8 @@
     return call(
         inside_kernel,
         in_specs=[pl.BlockSpec(memory_space=pltpu.HBM)] * 3,
-        out_specs=VMEM,
-        out_shape=jax.ShapeDtypeStruct((n, cols), F32),
+        out_specs=[VMEM] * 2,
+        out_shape=[jax.ShapeDtypeStruct((n, cols), d) for d in (F32, BF16)],
         scratch_shapes=[pltpu.VMEM((n, cols), BF16)] * 3
         + [pltpu.SemaphoreType.DMA((3, cols // DH))],
         name="inside",
@@ -159,32 +170,36 @@
     )(pair, keep, got)
 
 
-def far_kernel(pair_ref, every_ref, out_ref, send_ref):
+def far_kernel(pair_ref, every_ref, near_ref, out_ref, send_ref):
     for kind in range(2):
         total = jnp.zeros(out_ref.shape[1:], F32)
         for p in range(every_ref.shape[0]):
             reached = p > pair_ref[0] if kind == 0 else p < pair_ref[0]
             total = total + jnp.where(reached, every_ref[p].astype(F32), 0.0)
         out_ref[kind] = total
-        send_ref[kind] = total.astype(BF16)
-
-
-def far_states(pair, every):
+        send_ref[0, kind] = total.astype(BF16)
+        send_ref[1, kind] = near_ref[kind]
+
+
+def far_states(pair, every, near):
     shape = (2, *every.shape[1:])
     return call(
         far_kernel,
-        in_specs=[SMEM, VMEM],
+        in_specs=[SMEM, VMEM, VMEM],
         out_specs=[VMEM] * 2,
-        out_shape=[jax.ShapeDtypeStruct(shape, d) for d in (F32, BF16)],
+        out_shape=[
+            jax.ShapeDtypeStruct(shape, F32),
+            jax.ShapeDtypeStruct((2, *shape), BF16),
+        ],
         name="far",
-    )(pair, every)
-
-
-def entering(par, kind, hd, half, far, got_far, near, got_near):
+    )(pair, every, near)
+
+
+def entering(par, kind, hd, half, far, got, near):
     mine = par == hd // half
     i = hd % half
-    outer = jnp.where(mine, far[kind, i], got_far[kind, i].astype(F32))
-    close = jnp.where(mine, near[kind, i].astype(F32), got_near[kind, i].astype(F32))
+    outer = jnp.where(mine, far[kind, i], got[0, kind, i].astype(F32))
+    close = jnp.where(mine, near[kind, i].astype(F32), got[1, kind, i].astype(F32))
     total = outer + jnp.where(par == kind, close, 0.0)
     hi = total.astype(BF16)
     return hi, (total - hi.astype(F32)).astype(BF16)
@@ -229,13 +244,12 @@
 def others(factor, par, q, k, v, g, ends):
     n, cols = q.shape
     spec = pl.BlockSpec((n, DH), lambda h: (0, h))
-    shape = ends[0].shape
-    state = pl.BlockSpec(shape, lambda h: (0, 0, 0, 0))
+    held = [pl.BlockSpec(x.shape, lambda h, d=x.ndim: (0,) * d) for x in ends]
     out = jax.ShapeDtypeStruct(q.shape, BF16)
     return call(
         functools.partial(others_kernel, factor, cols // DH // 2),
         grid=(cols // DH,),
-        in_specs=[SMEM] + [spec] * 4 + [state] * len(ends),
+        in_specs=[SMEM] + [spec] * 4 + held,
         out_specs=[spec] * 2,
         out_shape=[out] * 2,
         name="others",
@@ -333,71 +347,70 @@
 
 def arrange_kernel(per, head_ref, which_ref, *refs):
     count = which_ref.shape[0]
-    blocks, out_ref, lend_ref, sems = refs[:count], refs[-3], refs[-2], refs[-1]
-    rows = blocks[0].shape[0]
+    outs, sems = refs[-3:-1], refs[-1]
+    rows = refs[0].shape[0]
 
     def copies(s):
         p = which_ref[s]
-        to = lend_ref.at[p // per // 2, pl.ds((p % per) * rows, rows)]
-        keep = pltpu.make_async_copy(blocks[s], out_ref.at[p], sems.at[0, s])
-        lend = pltpu.make_async_copy(blocks[s], to, sems.at[1, s])
-        return keep, lend, (p // per) % 2 != head_ref[0] % 2
-
-    for s in range(count):
-        keep, lend, needed = copies(s)
-        keep.start()
-        pl.when(needed)(lend.start)
-    for s in range(count):
-        keep, lend, needed = copies(s)
-        keep.wait()
-        pl.when(needed)(lend.wait)
-
-
-def arrange(per, n_head, head, which, blocks):
+        at = (p // per // 2, pl.ds((p % per) * rows, rows))
+        pair = [
+            pltpu.make_async_copy(refs[j * count + s], outs[j].at[at], sems.at[j, s])
+            for j in range(2)
+        ]
+        return pair, (p // per) % 2 == head_ref[0] % 2
+
+    for act in ("start", "wait"):
+        for s in range(count):
+            pair, needed = copies(s)
+
+            @pl.when(needed)
+            def _():
+                for c in pair:
+                    getattr(c, act)()
+
+
+def arrange(per, n_head, head, which, blocks, lent):
     rows, cols = blocks[0].shape
     count = len(blocks)
+    out = jax.ShapeDtypeStruct((n_head // 2, per * rows, cols), BF16)
     return call(
         functools.partial(arrange_kernel, per),
-        in_specs=[SMEM] * 2 + [ANY] * count,
+        in_specs=[SMEM] * 2 + [ANY] * (2 * count),
         out_specs=[VMEM] * 2,
-        out_shape=[
-            jax.ShapeDtypeStruct((count, rows, cols), BF16),
-            jax.ShapeDtypeStruct((n_head // 2, per * rows, cols), BF16),
-        ],
+        out_shape=[out] * 2,
         scratch_shapes=[pltpu.SemaphoreType.DMA((2, count))],
         name="arrange",
-    )(head, which, *blocks)
-
-
-def block_product(per, at_ref, x_ref, y_ref, w_ref, wy_ref):
-    w = w_ref[pl.ds(at_ref[0] * per, per)].reshape(-1, w_ref.shape[2])
-    wy = wy_ref[at_ref[0] // 2]
-    return dot(x_ref[...], w, 1, 1) + dot(y_ref[...], wy, 1, 1)
-
-
-def part_kernel(per, count, at_ref, x_ref, y_ref, w_ref, wy_ref, *refs):
-    total = block_product(per, at_ref, x_ref, y_ref, w_ref, wy_ref)
-    for got in refs[:count]:
+    )(head, which, *blocks, *lent)
+
+
+def block_product(at_ref, x_ref, y_ref, w_ref, wy_ref):
+    at = at_ref[0] // 2
+    return dot(x_ref[...], w_ref[at], 1, 1) + dot(y_ref[...], wy_ref[at], 1, 1)
+
+
+def part_kernel(at_ref, x_ref, y_ref, w_ref, wy_ref, *refs):
+    total = block_product(at_ref, x_ref, y_ref, w_ref, wy_ref)
+    for got in refs[:-1]:
         total = total + got[...].astype(F32)
     refs[-1][...] = total.astype(BF16)
 
 
-def head_part(at, per, x, y, w, wy, got=()):
-    return call(
-        functools.partial(part_kernel, per, len(got)),
+def head_part(at, x, y, w, wy, got=()):
+    return call(
+        part_kernel,
         in_specs=[SMEM] + [VMEM] * (4 + len(got)),
         out_specs=VMEM,
-        out_shape=jax.ShapeDtypeStruct((x.shape[0], per * w.shape[1]), BF16),
+        out_shape=jax.ShapeDtypeStruct((x.shape[0], w.shape[1]), BF16),
         name="head_part",
     )(at, x, y, w, wy, *got)
 
 
-def join_kernel(per, count, par_ref, at_ref, x_ref, y_ref, w_ref, wy_ref, *refs):
-    total = block_product(per, at_ref, x_ref, y_ref, w_ref, wy_ref)
-    for got in refs[:count]:
+def join_kernel(per, par_ref, at_ref, x_ref, y_ref, w_ref, wy_ref, *refs):
+    total = block_product(at_ref, x_ref, y_ref, w_ref, wy_ref)
+    for got in refs[:-2]:
         total = total + got[...].astype(F32)
-    other_ref, out_ref = refs[count:]
-    rows = w_ref.shape[1]
+    other_ref, out_ref = refs[-2:]
+    rows = other_ref.shape[1] // per
     both = (total.astype(BF16), other_ref[...])
     for k in range(2):
 
@@ -412,7 +425,7 @@
 
 def join(par, at, per, x, y, w, wy, got, other):
     return call(
-        functools.partial(join_kernel, per, len(got)),
+        functools.partial(join_kernel, per),
         in_specs=[SMEM] * 2 + [VMEM] * (5 + len(got)),
         out_specs=VMEM,
         out_shape=jax.ShapeDtypeStruct((x.shape[0], 2 * other.shape[1]), BF16),
@@ -458,27 +471,26 @@
 
     per = n_ctx // n_head // 2
     own, theirs = split(after(par, send), inputs, per)
-    vi = inside(after(queries, own), keys, out_grad)
+    vi, keys_too = inside(after(queries, own), keys, out_grad)
     blocks = [value_weight, ring(after(value_weight, send))]
-    got_near = partner(after(near16, their_half))
     own, theirs = [own], [partner(after(theirs, their_half))]
 
     offered = offer(line, after(keep, vi), their_half, pairs)
     every = lax.all_to_all(
         offered, "ctx", split_axis=0, concat_axis=0, axis_index_groups=lines
     )
-    far, send_far = far_states(line, every)
-    ends = (far, partner(send_far), their_half, got_near)
-    theirs = [after(theirs[0], send_far)]
-    token = send_far
-    mine = finish_value(factor, par, keys, vi, ends)
+    far, send_far = far_states(line, every, near16)
+    ends = (far, partner(send_far), their_half)
+    mine = finish_value(factor, par, keys_too, vi, ends)
     other = partner(mine)
+    theirs = [after(theirs[0], mine)]
     query_grad, key_grad = others(
         factor, par, queries, keys, after(values, mine), out_grad, ends
     )
     for _ in range(2, pairs):
-        blocks.append(ring(after(blocks[-1], token)))
-        token = mine
+        blocks.append(ring(after(blocks[-1], mine)))
+    lent = [across(after(x, mine), 1) for x in blocks[:-1]]
+    mine_too = across(mine, 1)
 
     offsets = [0]
     bit = n_head // 2
@@ -495,38 +507,39 @@
     vals = (after(mine, query_grad), other, own, theirs)
     (total,) = pieces(BF16, offs[:1], subs[:1], *vals)
     moved = ring(total)
-    vals = (after(mine, total), other, own, theirs)
+    other_too = across(after(other, total), 1)
+    vals = (after(mine, other_too), other, own, theirs)
     rest = pieces(F32, offs[1:], subs[1:], *vals)
+    lent.append(across(after(blocks[-1], rest[0]), 1))
 
     here = head.astype(jnp.int32).reshape(1)
     held = jnp.asarray(order, jnp.int32)[(spot - steps) % pairs]
-    weight, lend = arrange(per, n_head, here, held, [after(blocks[0], rest[0])] + blocks[1:])
-    lent = across(lend, 1)
-    mine_too, other_too = across(after(mine, total), 1), across(other, 1)
 
     def summed_parts(x, y):
         sent = [
-            head_part(here ^ off, per, x, y, weight, lent)
+            head_part(here ^ off, x, y, weight, borrowed)
             for off in range(2, n_head, 2)
         ]
         return sent[-1], [across(x, 2 * i + 2) for i, x in enumerate(sent)]
 
+    total = add_own(moved, rest[0])
+    moved = ring(total)
+    weight, borrowed = arrange(
+        per, n_head, here, held, [after(blocks[0], total)] + blocks[1:], lent
+    )
     token, got_other = summed_parts(other, other_too)
-    total = add_own(moved, after(rest[0], token))
-    moved = ring(total)
-    token, got_mine = summed_parts(after(mine, total), mine_too)
+    token, got_mine = summed_parts(after(mine, token), mine_too)
     for i in range(1, pairs - 2):
         total = add_own(moved, after(rest[i], token))
         moved = ring(total)
-    part = head_part(
-        here, per, after(other, total), other_too, weight, lent, got_other
-    )
+    part = head_part(here, after(other, total), other_too, weight, borrowed, got_other)
     swapped = partner(part)
     weight_grad = finish_weight(
         1.0 / math.sqrt(length * n_ctx), moved, after(rest[-1], part)
     )
+    mine = after(mine, weight_grad)
     input_grad = join(
-        par, here, per, after(mine, weight_grad), mine_too, weight, lent, got_mine, swapped
+        par, here, per, mine, mine_too, weight, borrowed, got_mine, swapped
     )
     return (query_grad, key_grad, input_grad, weight_grad)
 

time: 115 us -> 135 us (1.17)
  waiting for transfers between devices: 48.9 us -> 61.5 us
  local copies, waits for them, and re-layouts: 7.4 us -> 11.1 us
  starting transfers between devices: 27.5 us -> 30 us
    ppermute x11 -> x14, waiting for transfers between devices: 2.02 us -> 12.9 us  [across(): return lax.ppermute(x, 'head', [(i, i ^ bit) for i in range(n_head)])]
    unnamed x32 -> x48, local copies, waits for them, and re-layouts: 5.32 us -> 9.19 us
    ppermute x6, starting transfers between devices: 11 us -> 13.1 us  [ring(): return lax.ppermute(x, 'ctx', moves)]
    ppermute x6, waiting for transfers between devices: 27.5 us -> 29.6 us  [ring(): return lax.ppermute(x, 'ctx', moves)]
    ppermute x6 -> x5, waiting for transfers between devices: 12.7 us -> 11.1 us  [partner(): return lax.ppermute(x, 'ctx', [(i, i ^ 1) for i in range(n_ctx)])]
    all_to_all x1, waiting for transfers between devices: 6.61 us -> 8.06 us  [local(): lax.all_to_all(offered, 'ctx', split_axis=0, concat_axis=0, axis_index_gr...]
    ppermute x11 -> x14, starting transfers between devices: 5.92 us -> 6.72 us  [across(): return lax.ppermute(x, 'head', [(i, i ^ bit) for i in range(n_head)])]
    ppermute x6 -> x5, starting transfers between devices: 5.67 us -> 5.25 us  [partner(): return lax.ppermute(x, 'ctx', [(i, i ^ 1) for i in range(n_ctx)])]
  transfers between devices with their start and end apart: 24 -> 26, of which waited for: 10 -> 11; matrix products, arithmetic and copies ran while one was open for 3% -> 2% of each run, Pallas kernels for 17% -> 17%
where the time goes in v10:
time: 135 us; the launch traced here: 134 us
  waiting for transfers between devices  61.5 us (46%)
  starting transfers between devices  30 us (22%)
  Pallas kernels  29.2 us (22%)
  local copies, waits for them, and re-layouts  11.1 us (8%)
  between operations  1.53 us (1%)
    ppermute x6, waiting for transfers between devices, ring(): return lax.ppermute(x, 'ctx', moves)  29.6 us
    ppermute x6, starting transfers between devices, ring(): return lax.ppermute(x, 'ctx', moves)  13.1 us
    ppermute x14, waiting for transfers between devices, across(): return lax.ppermute(x, 'head', [(i, i ^ bit) for i in range(n_head)])  12.9 us
    ppermute x5, waiting for transfers between devices, partner(): return lax.ppermute(x, 'ctx', [(i, i ^ 1) for i in range(n_ctx)])  11.1 us
    unnamed x48, local copies, waits for them, and re-layouts  9.19 us
    all_to_all x1, waiting for transfers between devices, local(): lax.all_to_all(offered, 'ctx', split_axis=0, concat_axis=0, axis_index_gr...  8.06 us
    pallas_call x2, Pallas kernels, pieces(): call(functools.partial(piece_kernel, count), grid=(steps,), in_specs=[SME...  7.29 us
    ppermute x14, starting transfers between devices, across(): return lax.ppermute(x, 'head', [(i, i ^ bit) for i in range(n_head)])  6.72 us
  transfers between devices with their start and end apart: 26, of which 11 were waited for; matrix products, arithmetic and copies ran while one was open for 2% of the time, Pallas kernels for 17%

profile of v10, /device:TPU:0, one launch (start us, length us, event | category | flops | bytes accessed | tf_op | source)
XLA Modules:
  0.0 134.0 jit_solution(17584298721933522558)
XLA Ops:
  0.7 4.0 %states.1 = (f32[2,2,128,128]{3,2,1,0:T(8,128)}, bf16[2,2,128,128]{3,2,1,0:T(8,128)(2,1)}, bf16[2,2,128,128]{3,2,1,0:T(8,128)(2,1)}) custom-call(s32[1]{0:T(128)} %bitcast.par_ref, bf16[512,512]{1,0:T(8,128)(2,1)} %q_ref.1, bf16[512,512]{1,0:T(8,128)(2,1)} %k_ref.1, bf16[512,512]{1,0:T(8,128)(2,1)} %v_ref, bf16[512,512]{1,0:T(8,128)(2,1)} %g_ref.1), custom_call_target="tpu_custom_call" | custom-call | flops 1 | bytes 1 | tf_op jit(solution)/shard_map/states/pallas_call | solution.py:69
  4.7 3.0 %collective-permute-start = (bf16[2,2,128,128]{3,2,1,0:T(8,128)(2,1)}, bf16[2,2,128,128]{3,2,1,0:T(8,128)(2,1)S(1)}, u32[]{:S(2)}, u32[]{:S(2)}) collective-permute-start(bf16[2,2,128,128]{3,2,1,0:T(8,128)(2,1)} %get-tuple-element.40), channel_id=1, source_target_pairs={{0,4},{4,0},{8,12},{12,8},{16,20},{20,16},{24,28},{28,24},{1,5},{5... | collective-permute-start | bytes 393224 | tf_op jit(solution)/shard_map/ppermute | solution.py:450
  9.5 3.0 %inside.1 = (f32[512,512]{1,0:T(8,128)S(1)}, bf16[512,512]{1,0:T(8,128)(2,1)S(1)}) custom-call(bf16[512,512]{1,0:T(8,128)(2,1)S(1)} %copy-done, bf16[512,512]{1,0:T(8,128)(2,1)S(1)} %copy-done.1, bf16[512,512]{1,0:T(8,128)(2,1)S(1)} %copy-done.2), custom_call_target="tpu_custom_call" | custom-call | flops 1 | bytes 1 | tf_op jit(solution)/shard_map/inside/pallas_call | solution.py:146
  14.4 5.0 %all-to-all-start = ((bf16[4,2,128,128]{3,2,1,0:T(8,128)(2,1)}), bf16[4,2,128,128]{3,2,1,0:T(8,128)(2,1)S(1)}, u32[]{:S(2)}, u32[]{:S(2)}) async-start(bf16[4,2,128,128]{3,2,1,0:T(8,128)(2,1)} %offer.1), calls=%async_computation | async-start | bytes 524288 | tf_op jit(solution)/shard_map/all_to_all | solution.py:479
  19.9 8.1 %all-to-all-done.every_ref = bf16[4,2,128,128]{3,2,1,0:T(8,128)(2,1)S(1)} async-done(((bf16[4,2,128,128]{3,2,1,0:T(8,128)(2,1)}), bf16[4,2,128,128]{3,2,1,0:T(8,128)(2,1)S(1)}, u32[]{:S(2)}, u32[]{:S(2)}) %all-to-all-start) | async-done | bytes 262176 | tf_op jit(solution)/shard_map/all_to_all | solution.py:479
  28.7 1.5 %collective-permute-start.4 = (bf16[1,512,512]{2,1,0:T(8,128)(2,1)}, bf16[1,512,512]{2,1,0:T(8,128)(2,1)}, u32[]{:S(2)}, u32[]{:S(2)}) collective-permute-start(bf16[1,512,512]{2,1,0:T(8,128)(2,1)} %get-tuple-element.42.refs_0_), channel_id=1, source_target_pairs={{0,2},{1,3},{2,0},{3,1},{4,6},{5,7},{6,4},{7,5},{8,10},{9,11},{10,... | collective-permute-start | bytes 1572872 | tf_op jit(solution)/shard_map/ppermute | solution.py:453
  30.2 8.1 %collective-permute-done.1.refs_1_ = bf16[2,2,2,128,128]{4,3,2,1,0:T(8,128)(2,1)S(1)} collective-permute-done((bf16[2,2,2,128,128]{4,3,2,1,0:T(8,128)(2,1)S(1)}, bf16[2,2,2,128,128]{4,3,2,1,0:T(8,128)(2,1)S(1)}, u32[]{:S(2)}, u32[]{:S(2)}) %collective-permute-start.1) | collective-permute-done | bytes 262176 | tf_op jit(solution)/shard_map/ppermute | solution.py:450
  38.3 1.3 copy-done.12
  39.7 1.0 copy-done.18
  41.2 1.6 %collective-permute-start.8 = (bf16[1,512,512]{2,1,0:T(8,128)(2,1)}, bf16[1,512,512]{2,1,0:T(8,128)(2,1)}, u32[]{:S(2)}, u32[]{:S(2)}) collective-permute-start(bf16[1,512,512]{2,1,0:T(8,128)(2,1)} %collective-permute-done.6.refs_4_), channel_id=1, source_target_pairs={{0,2},{1,3},{2,0},{3,1},{4,6},{5,7},{6,4},{7,5},{8,10},{9,11},{10,... | collective-permute-start | bytes 1572872 | tf_op jit(solution)/shard_map/ppermute | solution.py:453
  43.8 10.0 %collective-permute-done.8.refs_6_ = bf16[1,512,512]{2,1,0:T(8,128)(2,1)} collective-permute-done((bf16[1,512,512]{2,1,0:T(8,128)(2,1)}, bf16[1,512,512]{2,1,0:T(8,128)(2,1)}, u32[]{:S(2)}, u32[]{:S(2)}) %collective-permute-start.8) | collective-permute-done | bytes 524320 | tf_op jit(solution)/shard_map/ppermute | solution.py:453
  54.7 2.4 %collective-permute-start.14 = (bf16[512,512]{1,0:T(8,128)(2,1)}, bf16[512,512]{1,0:T(8,128)(2,1)}, u32[]{:S(2)}, u32[]{:S(2)}) collective-permute-start(bf16[512,512]{1,0:T(8,128)(2,1)} %collective-permute-done.13.refs_1_), channel_id=1, source_target_pairs={{0,16},{4,20},{16,24},{20,28},{24,8},{28,12},{8,0},{12,4},{1,17},{... | collective-permute-start | bytes 1572872 | tf_op jit(solution)/shard_map/ppermute | solution.py:466
  59.8 4.0 %others.1 = (bf16[512,512]{1,0:T(8,128)(2,1)}, bf16[512,512]{1,0:T(8,128)(2,1)}) custom-call(s32[1]{0:T(128)} %bitcast.par_ref, bf16[512,512]{1,0:T(8,128)(2,1)S(1)} %copy-done, bf16[512,512]{1,0:T(8,128)(2,1)S(1)} %copy-done.1, bf16[512,512]{1,0:T(8,128)(2,1)S(1)} %copy-done.3, bf16[512,512]{1,0:T(8,128)(2,1)S(1)} %copy-done.2, ...), custom_call_target="tpu_custom_call" | custom-call | flops 1 | bytes 1 | tf_op jit(solution)/shard_map/others/pallas_call | solution.py:249
  63.9 2.7 %pieces.2 = bf16[512,512]{1,0:T(8,128)(2,1)} custom-call(s32[1]{0:T(128)S(1)} %bitcast.9, s32[1]{0:T(128)} %constant.81.clone.1.subs_ref, bf16[512,512]{1,0:T(8,128)(2,1)S(1)} %finish_value.1.a_ref.x_ref, bf16[512,512]{1,0:T(8,128)(2,1)S(1)} %collective-permute-done.2.b_ref.x_ref, bf16[1,512,512]{2,1,0:T(8,128)(2,1)} %get-tuple-element.42.refs_0_, ...), custom_call_target="tpu_custom_call" | custom-call | flops 1 | bytes 1 | tf_op jit(solution)/shard_map/pieces/pallas_call | solution.py:303
  67.0 2.3 %collective-permute-done.14.refs_2_ = bf16[512,512]{1,0:T(8,128)(2,1)} collective-permute-done((bf16[512,512]{1,0:T(8,128)(2,1)}, bf16[512,512]{1,0:T(8,128)(2,1)}, u32[]{:S(2)}, u32[]{:S(2)}) %collective-permute-start.14) | collective-permute-done | bytes 524320 | tf_op jit(solution)/shard_map/ppermute | solution.py:466
  69.3 3.3 %collective-permute-start.15 = (bf16[512,512]{1,0:T(8,128)(2,1)}, bf16[512,512]{1,0:T(8,128)(2,1)}, u32[]{:S(2)}, u32[]{:S(2)}) collective-permute-start(bf16[512,512]{1,0:T(8,128)(2,1)} %collective-permute-done.14.refs_2_), channel_id=1, source_target_pairs={{0,16},{4,20},{16,24},{20,28},{24,8},{28,12},{8,0},{12,4},{1,17},{... | collective-permute-start | bytes 1572872 | tf_op jit(solution)/shard_map/ppermute | solution.py:466
  73.7 4.6 %pieces.3 = (f32[512,512]{1,0:T(8,128)S(1)}, f32[512,512]{1,0:T(8,128)S(1)}, f32[512,512]{1,0:T(8,128)S(1)}) custom-call(s32[3]{0:T(128)S(1)} %slice.11.offs_ref, s32[3]{0:T(128)S(1)} %slice.12.subs_ref, bf16[512,512]{1,0:T(8,128)(2,1)S(1)} %finish_value.1.a_ref.x_ref, bf16[512,512]{1,0:T(8,128)(2,1)S(1)} %collective-permute-done.2.b_ref.x_ref, ...), custom_call_target="tpu_custom_call" | custom-call | flops 1 | bytes 1 | tf_op jit(solution)/shard_map/pieces/pallas_call | solution.py:303
  79.3 1.0 copy-done.13
  80.3 5.0 %collective-permute-done.15.refs_3_ = bf16[512,512]{1,0:T(8,128)(2,1)} collective-permute-done((bf16[512,512]{1,0:T(8,128)(2,1)}, bf16[512,512]{1,0:T(8,128)(2,1)}, u32[]{:S(2)}, u32[]{:S(2)}) %collective-permute-start.15) | collective-permute-done | bytes 524320 | tf_op jit(solution)/shard_map/ppermute | solution.py:466
  86.5 8.7 %collective-permute-done.10.moved_ref = bf16[512,512]{1,0:T(8,128)(2,1)} collective-permute-done((bf16[512,512]{1,0:T(8,128)(2,1)}, bf16[512,512]{1,0:T(8,128)(2,1)}, u32[]{:S(2)}, u32[]{:S(2)}) %collective-permute-start.10) | collective-permute-done | bytes 524320 | tf_op jit(solution)/shard_map/ppermute | solution.py:466
  95.2 1.2 copy-done.14
  96.4 1.1 add_own.2
  97.6 3.4 %collective-permute-start.12 = (bf16[512,512]{1,0:T(8,128)(2,1)S(1)}, bf16[512,512]{1,0:T(8,128)(2,1)S(1)}, u32[]{:S(2)}, u32[]{:S(2)}) collective-permute-start(bf16[512,512]{1,0:T(8,128)(2,1)S(1)} %add_own.2), channel_id=1, source_target_pairs={{0,16},{4,20},{16,24},{20,28},{24,8},{28,12},{8,0},{12,4},{1,17},{... | collective-permute-start | bytes 1572872 | tf_op jit(solution)/shard_map/ppermute | solution.py:466
  101.0 2.0 %arrange.1 = (bf16[2,512,512]{2,1,0:T(8,128)(2,1)S(1)}, bf16[2,512,512]{2,1,0:T(8,128)(2,1)S(1)}) custom-call(s32[1]{0:T(128)} %bitcast.2.head_ref.at_ref, s32[4]{0:T(128)S(1)} %gather_fusion.1, bf16[512,512]{1,0:T(8,128)(2,1)S(1)} %copy-done.16, bf16[512,512]{1,0:T(8,128)(2,1)} %collective-permute-done.13.refs_1_, ...), custom_call_target="tpu_custom_call" | custom-call | flops 1 | bytes 1 | tf_op jit(solution)/shard_map/arrange/pallas_call | solution.py:376
  103.8 1.6 %collective-permute-start.22 = (bf16[512,512]{1,0:T(8,128)(2,1)S(1)}, bf16[512,512]{1,0:T(8,128)(2,1)S(1)}, u32[]{:S(2)}, u32[]{:S(2)}) collective-permute-start(bf16[512,512]{1,0:T(8,128)(2,1)S(1)} %head_part.3), channel_id=1, source_target_pairs={{0,2},{1,3},{2,0},{3,1},{4,6},{5,7},{6,4},{7,5},{8,10},{9,11},{10,... | collective-permute-start | bytes 1572872 | tf_op jit(solution)/shard_map/ppermute | solution.py:453
  106.7 6.1 %collective-permute-done.12.moved_ref = bf16[512,512]{1,0:T(8,128)(2,1)S(1)} collective-permute-done((bf16[512,512]{1,0:T(8,128)(2,1)S(1)}, bf16[512,512]{1,0:T(8,128)(2,1)S(1)}, u32[]{:S(2)}, u32[]{:S(2)}) %collective-permute-start.12) | collective-permute-done | bytes 524320 | tf_op jit(solution)/shard_map/ppermute | solution.py:466
  113.0 3.4 %collective-permute-start.21 = (bf16[512,512]{1,0:T(8,128)(2,1)S(1)}, bf16[512,512]{1,0:T(8,128)(2,1)S(1)}, u32[]{:S(2)}, u32[]{:S(2)}) collective-permute-start(bf16[512,512]{1,0:T(8,128)(2,1)S(1)} %add_own.3), channel_id=1, source_target_pairs={{0,16},{4,20},{16,24},{20,28},{24,8},{28,12},{8,0},{12,4},{1,17},{... | collective-permute-start | bytes 1572872 | tf_op jit(solution)/shard_map/ppermute | solution.py:466
  116.4 2.3 %collective-permute-done.22.refs_0_ = bf16[512,512]{1,0:T(8,128)(2,1)S(1)} collective-permute-done((bf16[512,512]{1,0:T(8,128)(2,1)S(1)}, bf16[512,512]{1,0:T(8,128)(2,1)S(1)}, u32[]{:S(2)}, u32[]{:S(2)}) %collective-permute-start.22) | collective-permute-done | bytes 524320 | tf_op jit(solution)/shard_map/ppermute | solution.py:453
  120.0 7.5 %collective-permute-done.21.moved_ref = bf16[512,512]{1,0:T(8,128)(2,1)S(1)} collective-permute-done((bf16[512,512]{1,0:T(8,128)(2,1)S(1)}, bf16[512,512]{1,0:T(8,128)(2,1)S(1)}, u32[]{:S(2)}, u32[]{:S(2)}) %collective-permute-start.21) | collective-permute-done | bytes 524320 | tf_op jit(solution)/shard_map/ppermute | solution.py:466
  127.5 1.3 finish_weight.1
  129.3 2.9 %collective-permute-done.24.refs_1_ = bf16[512,512]{1,0:T(8,128)(2,1)S(1)} collective-permute-done((bf16[512,512]{1,0:T(8,128)(2,1)S(1)}, bf16[512,512]{1,0:T(8,128)(2,1)S(1)}, u32[]{:S(2)}, u32[]{:S(2)}) %collective-permute-start.24) | collective-permute-done | bytes 524320 | tf_op jit(solution)/shard_map/ppermute | solution.py:450
  132.3 1.8 %join.1 = bf16[512,1024]{1,0:T(8,128)(2,1)} custom-call(s32[1]{0:T(128)} %bitcast.par_ref, s32[1]{0:T(128)} %bitcast.2.head_ref.at_ref, bf16[512,512]{1,0:T(8,128)(2,1)S(1)} %finish_value.1.a_ref.x_ref, bf16[512,512]{1,0:T(8,128)(2,1)S(1)} %collective-permute-done.20.y_ref, bf16[2,512,512]{2,1,0:T(8,128)(2,1)S(1)} %get-tuple-element.68.w_ref, ...), custom_call_target="tpu_custom_call" | custom-call | flops 1 | bytes 1 | tf_op jit(solution)/shard_map/join/pallas_call | solution.py:427
  (95 shorter events, 17.2 us)
Async XLA Ops:
  4.7 8.8 %collective-permute-start = (bf16[2,2,128,128]{3,2,1,0:T(8,128)(2,1)}, bf16[2,2,128,128]{3,2,1,0:T(8,128)(2,1)S(1)}, u32[]{:S(2)}, u32[]{:S(2)}) collective-permute-start(bf16[2,2,128,128]{3,2,1,0:T(8,128)(2,1)} %get-tuple-element.40), channel_id=1, source_target_pairs={{0,4},{4,0},{8,12},{12,8},{16,20},{20,16},{24,28},{28,24},{1,5},{5... | collective-permute-start | bytes 393224 | tf_op jit(solution)/shard_map/ppermute | solution.py:450
  13.5 14.5 %copy-start.20 = (bf16[2,2,128,128]{3,2,1,0:T(8,128)(2,1)S(1)}, bf16[2,2,128,128]{3,2,1,0:T(8,128)(2,1)}, u32[]{:S(2)}) copy-start(bf16[2,2,128,128]{3,2,1,0:T(8,128)(2,1)} %get-tuple-element.48.near_ref) | copy-start | bytes 393220
  14.3 15.9 %copy-start.15 = (bf16[512,512]{1,0:T(8,128)(2,1)S(1)}, bf16[512,512]{1,0:T(8,128)(2,1)}, u32[]{:S(2)}) copy-start(bf16[512,512]{1,0:T(8,128)(2,1)} %refs_0_.3) | copy-start | bytes 1572868
  14.4 13.6 %all-to-all-start = ((bf16[4,2,128,128]{3,2,1,0:T(8,128)(2,1)}), bf16[4,2,128,128]{3,2,1,0:T(8,128)(2,1)S(1)}, u32[]{:S(2)}, u32[]{:S(2)}) async-start(bf16[4,2,128,128]{3,2,1,0:T(8,128)(2,1)} %offer.1), calls=%async_computation | async-start | bytes 524288 | tf_op jit(solution)/shard_map/all_to_all | solution.py:479
  19.4 21.8 %collective-permute-start.6 = (bf16[1,512,512]{2,1,0:T(8,128)(2,1)}, bf16[1,512,512]{2,1,0:T(8,128)(2,1)}, u32[]{:S(2)}, u32[]{:S(2)}) collective-permute-start(bf16[1,512,512]{2,1,0:T(8,128)(2,1)} %copy-done.21), channel_id=1, source_target_pairs={{0,4},{4,0},{8,12},{12,8},{16,20},{20,16},{24,28},{28,24},{1,5},{5... | collective-permute-start | bytes 1572872 | tf_op jit(solution)/shard_map/ppermute | solution.py:450
  28.1 10.2 %collective-permute-start.1 = (bf16[2,2,2,128,128]{4,3,2,1,0:T(8,128)(2,1)S(1)}, bf16[2,2,2,128,128]{4,3,2,1,0:T(8,128)(2,1)S(1)}, u32[]{:S(2)}, u32[]{:S(2)}) collective-permute-start(bf16[2,2,2,128,128]{4,3,2,1,0:T(8,128)(2,1)S(1)} %get-tuple-element.50), channel_id=1, source_target_pairs={{0,4},{4,0},{8,12},{12,8},{16,20},{20,16},{24,28},{28,24},{1,5},{5... | collective-permute-start | bytes 786440 | tf_op jit(solution)/shard_map/ppermute | solution.py:450
  28.7 14.1 %collective-permute-start.4 = (bf16[1,512,512]{2,1,0:T(8,128)(2,1)}, bf16[1,512,512]{2,1,0:T(8,128)(2,1)}, u32[]{:S(2)}, u32[]{:S(2)}) collective-permute-start(bf16[1,512,512]{2,1,0:T(8,128)(2,1)} %get-tuple-element.42.refs_0_), channel_id=1, source_target_pairs={{0,2},{1,3},{2,0},{3,1},{4,6},{5,7},{6,4},{7,5},{8,10},{9,11},{10,... | collective-permute-start | bytes 1572872 | tf_op jit(solution)/shard_map/ppermute | solution.py:453
  30.2 13.1 %collective-permute-start.13 = (bf16[512,512]{1,0:T(8,128)(2,1)S(1)}, bf16[512,512]{1,0:T(8,128)(2,1)}, u32[]{:S(2)}, u32[]{:S(2)}) collective-permute-start(bf16[512,512]{1,0:T(8,128)(2,1)S(1)} %copy-done.15), channel_id=1, source_target_pairs={{0,16},{4,20},{16,24},{20,28},{24,8},{28,12},{8,0},{12,4},{1,17},{... | collective-permute-start | bytes 1572872 | tf_op jit(solution)/shard_map/ppermute | solution.py:466
  40.7 16.3 %copy-start.23 = (s32[4]{0:T(128)S(1)}, s32[4]{0:T(128)}, u32[]{:S(2)}) copy-start(s32[4]{0:T(128)} %constant.83.clone) | copy-start | bytes 52
  40.7 17.5 %copy-start.22 = (s32[4]{0:T(128)S(1)}, s32[4]{0:T(128)}, u32[]{:S(2)}) copy-start(s32[4]{0:T(128)} %constant.84.clone) | copy-start | bytes 52
  41.2 17.7 %copy-start.3 = (bf16[512,512]{1,0:T(8,128)(2,1)S(1)}, bf16[512,512]{1,0:T(8,128)(2,1)}, u32[]{:S(2)}) copy-start(bf16[512,512]{1,0:T(8,128)(2,1)} %v_ref) | copy-start | bytes 1572868
  41.2 12.7 %collective-permute-start.8 = (bf16[1,512,512]{2,1,0:T(8,128)(2,1)}, bf16[1,512,512]{2,1,0:T(8,128)(2,1)}, u32[]{:S(2)}, u32[]{:S(2)}) collective-permute-start(bf16[1,512,512]{2,1,0:T(8,128)(2,1)} %collective-permute-done.6.refs_4_), channel_id=1, source_target_pairs={{0,2},{1,3},{2,0},{3,1},{4,6},{5,7},{6,4},{7,5},{8,10},{9,11},{10,... | collective-permute-start | bytes 1572872 | tf_op jit(solution)/shard_map/ppermute | solution.py:453
  42.8 11.1 %collective-permute-start.3 = (bf16[1,512,512]{2,1,0:T(8,128)(2,1)}, bf16[1,512,512]{2,1,0:T(8,128)(2,1)S(1)}, u32[]{:S(2)}, u32[]{:S(2)}) collective-permute-start(bf16[1,512,512]{2,1,0:T(8,128)(2,1)} %get-tuple-element.42.refs_0_), channel_id=1, source_target_pairs={{0,1},{1,0},{2,3},{3,2},{4,5},{5,4},{6,7},{7,6},{8,9},{9,8},{10,11... | collective-permute-start | bytes 1572872 | tf_op jit(solution)/shard_map/ppermute | solution.py:453
  42.8 21.1 %collective-permute-start.5 = (bf16[1,512,512]{2,1,0:T(8,128)(2,1)}, bf16[1,512,512]{2,1,0:T(8,128)(2,1)}, u32[]{:S(2)}, u32[]{:S(2)}) collective-permute-start(bf16[1,512,512]{2,1,0:T(8,128)(2,1)} %collective-permute-done.4.refs_2_), channel_id=1, source_target_pairs={{0,1},{1,0},{2,3},{3,2},{4,5},{5,4},{6,7},{7,6},{8,9},{9,8},{10,11... | collective-permute-start | bytes 1572872 | tf_op jit(solution)/shard_map/ppermute | solution.py:453
  43.3 20.6 %collective-permute-start.7 = (bf16[1,512,512]{2,1,0:T(8,128)(2,1)}, bf16[1,512,512]{2,1,0:T(8,128)(2,1)}, u32[]{:S(2)}, u32[]{:S(2)}) collective-permute-start(bf16[1,512,512]{2,1,0:T(8,128)(2,1)} %collective-permute-done.6.refs_4_), channel_id=1, source_target_pairs={{0,1},{1,0},{2,3},{3,2},{4,5},{5,4},{6,7},{7,6},{8,9},{9,8},{10,11... | collective-permute-start | bytes 1572872 | tf_op jit(solution)/shard_map/ppermute | solution.py:453
  43.3 20.6 %collective-permute-start.2 = (bf16[512,512]{1,0:T(8,128)(2,1)S(1)}, bf16[512,512]{1,0:T(8,128)(2,1)S(1)}, u32[]{:S(2)}, u32[]{:S(2)}) collective-permute-start(bf16[512,512]{1,0:T(8,128)(2,1)S(1)} %finish_value.1.a_ref.x_ref), channel_id=1, source_target_pairs={{0,4},{4,0},{8,12},{12,8},{16,20},{20,16},{24,28},{28,24},{1,5},{5... | collective-permute-start | bytes 1572872 | tf_op jit(solution)/shard_map/ppermute | solution.py:450
  53.9 10.0 %collective-permute-start.9 = (bf16[1,512,512]{2,1,0:T(8,128)(2,1)}, bf16[1,512,512]{2,1,0:T(8,128)(2,1)}, u32[]{:S(2)}, u32[]{:S(2)}) collective-permute-start(bf16[1,512,512]{2,1,0:T(8,128)(2,1)} %collective-permute-done.8.refs_6_), channel_id=1, source_target_pairs={{0,1},{1,0},{2,3},{3,2},{4,5},{5,4},{6,7},{7,6},{8,9},{9,8},{10,11... | collective-permute-start | bytes 1572872 | tf_op jit(solution)/shard_map/ppermute | solution.py:453
  54.7 14.7 %collective-permute-start.14 = (bf16[512,512]{1,0:T(8,128)(2,1)}, bf16[512,512]{1,0:T(8,128)(2,1)}, u32[]{:S(2)}, u32[]{:S(2)}) collective-permute-start(bf16[512,512]{1,0:T(8,128)(2,1)} %collective-permute-done.13.refs_1_), channel_id=1, source_target_pairs={{0,16},{4,20},{16,24},{20,28},{24,8},{28,12},{8,0},{12,4},{1,17},{... | collective-permute-start | bytes 1572872 | tf_op jit(solution)/shard_map/ppermute | solution.py:466
  66.6 6.5 %collective-permute-start.11 = (bf16[512,512]{1,0:T(8,128)(2,1)S(1)}, bf16[512,512]{1,0:T(8,128)(2,1)S(1)}, u32[]{:S(2)}, u32[]{:S(2)}) collective-permute-start(bf16[512,512]{1,0:T(8,128)(2,1)S(1)} %collective-permute-done.2.b_ref.x_ref), channel_id=1, source_target_pairs={{0,1},{1,0},{2,3},{3,2},{4,5},{5,4},{6,7},{7,6},{8,9},{9,8},{10,11... | collective-permute-start | bytes 1572872 | tf_op jit(solution)/shard_map/ppermute | solution.py:453
  69.3 15.9 %collective-permute-start.15 = (bf16[512,512]{1,0:T(8,128)(2,1)}, bf16[512,512]{1,0:T(8,128)(2,1)}, u32[]{:S(2)}, u32[]{:S(2)}) collective-permute-start(bf16[512,512]{1,0:T(8,128)(2,1)} %collective-permute-done.14.refs_2_), channel_id=1, source_target_pairs={{0,16},{4,20},{16,24},{20,28},{24,8},{28,12},{8,0},{12,4},{1,17},{... | collective-permute-start | bytes 1572872 | tf_op jit(solution)/shard_map/ppermute | solution.py:466
  72.7 24.9 %collective-permute-start.17 = (bf16[512,512]{1,0:T(8,128)(2,1)}, bf16[512,512]{1,0:T(8,128)(2,1)}, u32[]{:S(2)}, u32[]{:S(2)}) collective-permute-start(bf16[512,512]{1,0:T(8,128)(2,1)} %collective-permute-done.13.refs_1_), channel_id=1, source_target_pairs={{0,1},{1,0},{2,3},{3,2},{4,5},{5,4},{6,7},{7,6},{8,9},{9,8},{10,11... | collective-permute-start | bytes 1572872 | tf_op jit(solution)/shard_map/ppermute | solution.py:453
  72.7 28.4 %collective-permute-start.16 = (bf16[512,512]{1,0:T(8,128)(2,1)S(1)}, bf16[512,512]{1,0:T(8,128)(2,1)}, u32[]{:S(2)}, u32[]{:S(2)}) collective-permute-start(bf16[512,512]{1,0:T(8,128)(2,1)S(1)} %copy-done.16), channel_id=1, source_target_pairs={{0,1},{1,0},{2,3},{3,2},{4,5},{5,4},{6,7},{7,6},{8,9},{9,8},{10,11... | collective-permute-start | bytes 1572872 | tf_op jit(solution)/shard_map/ppermute | solution.py:453
  73.2 27.8 %collective-permute-start.18 = (bf16[512,512]{1,0:T(8,128)(2,1)}, bf16[512,512]{1,0:T(8,128)(2,1)}, u32[]{:S(2)}, u32[]{:S(2)}) collective-permute-start(bf16[512,512]{1,0:T(8,128)(2,1)} %collective-permute-done.14.refs_2_), channel_id=1, source_target_pairs={{0,1},{1,0},{2,3},{3,2},{4,5},{5,4},{6,7},{7,6},{8,9},{9,8},{10,11... | collective-permute-start | bytes 1572872 | tf_op jit(solution)/shard_map/ppermute | solution.py:453
  73.2 22.0 %collective-permute-start.10 = (bf16[512,512]{1,0:T(8,128)(2,1)}, bf16[512,512]{1,0:T(8,128)(2,1)}, u32[]{:S(2)}, u32[]{:S(2)}) collective-permute-start(bf16[512,512]{1,0:T(8,128)(2,1)} %pieces.2), channel_id=1, source_target_pairs={{0,16},{4,20},{16,24},{20,28},{24,8},{28,12},{8,0},{12,4},{1,17},{... | collective-permute-start | bytes 1572872 | tf_op jit(solution)/shard_map/ppermute | solution.py:466
  85.2 15.8 %collective-permute-start.19 = (bf16[512,512]{1,0:T(8,128)(2,1)}, bf16[512,512]{1,0:T(8,128)(2,1)}, u32[]{:S(2)}, u32[]{:S(2)}) collective-permute-start(bf16[512,512]{1,0:T(8,128)(2,1)} %collective-permute-done.15.refs_3_), channel_id=1, source_target_pairs={{0,1},{1,0},{2,3},{3,2},{4,5},{5,4},{6,7},{7,6},{8,9},{9,8},{10,11... | collective-permute-start | bytes 1572872 | tf_op jit(solution)/shard_map/ppermute | solution.py:453
  95.2 10.2 %collective-permute-start.20 = (bf16[512,512]{1,0:T(8,128)(2,1)S(1)}, bf16[512,512]{1,0:T(8,128)(2,1)S(1)}, u32[]{:S(2)}, u32[]{:S(2)}) collective-permute-start(bf16[512,512]{1,0:T(8,128)(2,1)S(1)} %finish_value.1.a_ref.x_ref), channel_id=1, source_target_pairs={{0,1},{1,0},{2,3},{3,2},{4,5},{5,4},{6,7},{7,6},{8,9},{9,8},{10,11... | collective-permute-start | bytes 1572872 | tf_op jit(solution)/shard_map/ppermute | solution.py:453
  97.6 15.3 %collective-permute-start.12 = (bf16[512,512]{1,0:T(8,128)(2,1)S(1)}, bf16[512,512]{1,0:T(8,128)(2,1)S(1)}, u32[]{:S(2)}, u32[]{:S(2)}) collective-permute-start(bf16[512,512]{1,0:T(8,128)(2,1)S(1)} %add_own.2), channel_id=1, source_target_pairs={{0,16},{4,20},{16,24},{20,28},{24,8},{28,12},{8,0},{12,4},{1,17},{... | collective-permute-start | bytes 1572872 | tf_op jit(solution)/shard_map/ppermute | solution.py:466
  103.8 9.1 %copy-start.10 = (f32[512,512]{1,0:T(8,128)S(1)}, f32[512,512]{1,0:T(8,128)}, u32[]{:S(2)}) copy-start(f32[512,512]{1,0:T(8,128)} %copy-done.9) | copy-start | bytes 3145732
  103.8 14.8 %collective-permute-start.22 = (bf16[512,512]{1,0:T(8,128)(2,1)S(1)}, bf16[512,512]{1,0:T(8,128)(2,1)S(1)}, u32[]{:S(2)}, u32[]{:S(2)}) collective-permute-start(bf16[512,512]{1,0:T(8,128)(2,1)S(1)} %head_part.3), channel_id=1, source_target_pairs={{0,2},{1,3},{2,0},{3,1},{4,6},{5,7},{6,4},{7,5},{8,10},{9,11},{10,... | collective-permute-start | bytes 1572872 | tf_op jit(solution)/shard_map/ppermute | solution.py:453
  106.2 23.1 %collective-permute-start.23 = (bf16[512,512]{1,0:T(8,128)(2,1)S(1)}, bf16[512,512]{1,0:T(8,128)(2,1)S(1)}, u32[]{:S(2)}, u32[]{:S(2)}) collective-permute-start(bf16[512,512]{1,0:T(8,128)(2,1)S(1)} %head_part.4), channel_id=1, source_target_pairs={{0,2},{1,3},{2,0},{3,1},{4,6},{5,7},{6,4},{7,5},{8,10},{9,11},{10,... | collective-permute-start | bytes 1572872 | tf_op jit(solution)/shard_map/ppermute | solution.py:453
  113.0 14.5 %collective-permute-start.21 = (bf16[512,512]{1,0:T(8,128)(2,1)S(1)}, bf16[512,512]{1,0:T(8,128)(2,1)S(1)}, u32[]{:S(2)}, u32[]{:S(2)}) collective-permute-start(bf16[512,512]{1,0:T(8,128)(2,1)S(1)} %add_own.3), channel_id=1, source_target_pairs={{0,16},{4,20},{16,24},{20,28},{24,8},{28,12},{8,0},{12,4},{1,17},{... | collective-permute-start | bytes 1572872 | tf_op jit(solution)/shard_map/ppermute | solution.py:466
  119.4 12.9 %collective-permute-start.24 = (bf16[512,512]{1,0:T(8,128)(2,1)S(1)}, bf16[512,512]{1,0:T(8,128)(2,1)S(1)}, u32[]{:S(2)}, u32[]{:S(2)}) collective-permute-start(bf16[512,512]{1,0:T(8,128)(2,1)S(1)} %head_part.5), channel_id=1, source_target_pairs={{0,4},{4,0},{8,12},{12,8},{16,20},{20,16},{24,28},{28,24},{1,5},{5... | collective-permute-start | bytes 1572872 | tf_op jit(solution)/shard_map/ppermute | solution.py:450
  (18 other events, 55.1 us)

commit v11 on v10

--- a/solution.py
+++ b/solution.py
@@ -471,24 +471,26 @@
 
     per = n_ctx // n_head // 2
     own, theirs = split(after(par, send), inputs, per)
-    vi, keys_too = inside(after(queries, own), keys, out_grad)
     blocks = [value_weight, ring(after(value_weight, send))]
     own, theirs = [own], [partner(after(theirs, their_half))]
 
-    offered = offer(line, after(keep, vi), their_half, pairs)
+    offered = offer(line, keep, their_half, pairs)
     every = lax.all_to_all(
         offered, "ctx", split_axis=0, concat_axis=0, axis_index_groups=lines
     )
     far, send_far = far_states(line, every, near16)
     ends = (far, partner(send_far), their_half)
+    vi, keys_too = inside(after(queries, send_far), keys, out_grad)
+    theirs = [after(theirs[0], send_far)]
     mine = finish_value(factor, par, keys_too, vi, ends)
     other = partner(mine)
-    theirs = [after(theirs[0], mine)]
     query_grad, key_grad = others(
         factor, par, queries, keys, after(values, mine), out_grad, ends
     )
+    token = send_far
     for _ in range(2, pairs):
-        blocks.append(ring(after(blocks[-1], mine)))
+        blocks.append(ring(after(blocks[-1], token)))
+        token = mine
     lent = [across(after(x, mine), 1) for x in blocks[:-1]]
     mine_too = across(mine, 1)
 
@@ -504,13 +506,16 @@
 
     which = jnp.asarray(order, jnp.int32)[(spot - 1 - steps) % pairs]
     offs, subs = (which // per) ^ head, which % per
-    vals = (after(mine, query_grad), other, own, theirs)
-    (total,) = pieces(BF16, offs[:1], subs[:1], *vals)
+
+    def piece(dtype, step, token):
+        at = (offs[step : step + 1], subs[step : step + 1])
+        return pieces(dtype, *at, after(mine, token), other, own, theirs)[0]
+
+    total = piece(BF16, 0, query_grad)
     moved = ring(total)
     other_too = across(after(other, total), 1)
-    vals = (after(mine, other_too), other, own, theirs)
-    rest = pieces(F32, offs[1:], subs[1:], *vals)
-    lent.append(across(after(blocks[-1], rest[0]), 1))
+    local_part = piece(F32, 1, other_too)
+    lent.append(across(after(blocks[-1], local_part), 1))
 
     here = head.astype(jnp.int32).reshape(1)
     held = jnp.asarray(order, jnp.int32)[(spot - steps) % pairs]
@@ -522,20 +527,24 @@
         ]
         return sent[-1], [across(x, 2 * i + 2) for i, x in enumerate(sent)]
 
-    total = add_own(moved, rest[0])
+    total = add_own(moved, local_part)
     moved = ring(total)
     weight, borrowed = arrange(
         per, n_head, here, held, [after(blocks[0], total)] + blocks[1:], lent
     )
     token, got_other = summed_parts(other, other_too)
     token, got_mine = summed_parts(after(mine, token), mine_too)
-    for i in range(1, pairs - 2):
-        total = add_own(moved, after(rest[i], token))
+    for step in range(2, pairs - 1):
+        total = add_own(moved, piece(F32, step, token))
         moved = ring(total)
-    part = head_part(here, after(other, total), other_too, weight, borrowed, got_other)
+        token = total
+    local_part = piece(F32, pairs - 1, token)
+    part = head_part(
+        here, after(other, local_part), other_too, weight, borrowed, got_other
+    )
     swapped = partner(part)
     weight_grad = finish_weight(
-        1.0 / math.sqrt(length * n_ctx), moved, after(rest[-1], part)
+        1.0 / math.sqrt(length * n_ctx), moved, after(local_part, part)
     )
     mine = after(mine, weight_grad)
     input_grad = join(

time: 135 us -> 136 us (level)
  waiting for transfers between devices: 61.5 us -> 54 us
  Pallas kernels: 29.2 us -> 35 us
  local copies, waits for them, and re-layouts: 11.1 us -> 15.8 us
  starting transfers between devices: 30 us -> 28.5 us
    ppermute x14, waiting for transfers between devices: 12.9 us -> 0.04 us  [across(): return lax.ppermute(x, 'head', [(i, i ^ bit) for i in range(n_head)])]
    all_to_all x1, waiting for transfers between devices: 8.06 us -> 14.7 us  [local(): lax.all_to_all(offered, 'ctx', split_axis=0, concat_axis=0, axis_index_gr...]
    ppermute x6, starting transfers between devices: 13.1 us -> 8.64 us  [ring(): return lax.ppermute(x, 'ctx', moves)]
    unnamed x48 -> x40, local copies, waits for them, and re-layouts: 9.19 us -> 13.3 us
    ppermute x5, starting transfers between devices: 5.25 us -> 8.39 us  [partner(): return lax.ppermute(x, 'ctx', [(i, i ^ 1) for i in range(n_ctx)])]
    ppermute x5, waiting for transfers between devices: 11.1 us -> 8.35 us  [partner(): return lax.ppermute(x, 'ctx', [(i, i ^ 1) for i in range(n_ctx)])]
    pallas_call x2 -> x4, Pallas kernels: 7.29 us -> 9.39 us  [pieces(): call(functools.partial(piece_kernel, count), grid=(steps,), in_specs=[SME...]
  transfers between devices with their start and end apart: 26 -> 26, of which waited for: 11 -> 9; matrix products, arithmetic and copies ran while one was open for 2% -> 2% of each run, Pallas kernels for 17% -> 21%
where the time goes in v11:
time: 136 us; the launch traced here: 135 us
  waiting for transfers between devices  54 us (40%)
  Pallas kernels  35 us (26%)
  starting transfers between devices  28.5 us (21%)
  local copies, waits for them, and re-layouts  15.8 us (12%)
  between operations  1.5 us (1%)
    ppermute x6, waiting for transfers between devices, ring(): return lax.ppermute(x, 'ctx', moves)  30.9 us
    all_to_all x1, waiting for transfers between devices, local(): lax.all_to_all(offered, 'ctx', split_axis=0, concat_axis=0, axis_index_gr...  14.7 us
    unnamed x40, local copies, waits for them, and re-layouts  13.3 us
    pallas_call x4, Pallas kernels, pieces(): call(functools.partial(piece_kernel, count), grid=(steps,), in_specs=[SME...  9.39 us
    ppermute x6, starting transfers between devices, ring(): return lax.ppermute(x, 'ctx', moves)  8.64 us
    ppermute x5, starting transfers between devices, partner(): return lax.ppermute(x, 'ctx', [(i, i ^ 1) for i in range(n_ctx)])  8.39 us
    ppermute x5, waiting for transfers between devices, partner(): return lax.ppermute(x, 'ctx', [(i, i ^ 1) for i in range(n_ctx)])  8.35 us
    ppermute x14, starting transfers between devices, across(): return lax.ppermute(x, 'head', [(i, i ^ bit) for i in range(n_head)])  6.48 us
  transfers between devices with their start and end apart: 26, of which 9 were waited for; matrix products, arithmetic and copies ran while one was open for 2% of the time, Pallas kernels for 21%

profile of v11, /device:TPU:0, one launch (start us, length us, event | category | flops | bytes accessed | tf_op | source)
XLA Modules:
  0.0 135.4 jit_solution(16178170282043731302)
XLA Ops:
  0.7 4.0 %states.1 = (f32[2,2,128,128]{3,2,1,0:T(8,128)}, bf16[2,2,128,128]{3,2,1,0:T(8,128)(2,1)}, bf16[2,2,128,128]{3,2,1,0:T(8,128)(2,1)}) custom-call(s32[1]{0:T(128)} %bitcast.par_ref, bf16[512,512]{1,0:T(8,128)(2,1)} %q_ref.1, bf16[512,512]{1,0:T(8,128)(2,1)} %k_ref.1, bf16[512,512]{1,0:T(8,128)(2,1)} %v_ref, bf16[512,512]{1,0:T(8,128)(2,1)} %g_ref.1), custom_call_target="tpu_custom_call" | custom-call | flops 1 | bytes 1 | tf_op jit(solution)/shard_map/states/pallas_call | solution.py:69
  4.7 3.0 %collective-permute-start = (bf16[2,2,128,128]{3,2,1,0:T(8,128)(2,1)}, bf16[2,2,128,128]{3,2,1,0:T(8,128)(2,1)S(1)}, u32[]{:S(2)}, u32[]{:S(2)}) collective-permute-start(bf16[2,2,128,128]{3,2,1,0:T(8,128)(2,1)} %get-tuple-element.39), channel_id=1, source_target_pairs={{0,4},{4,0},{8,12},{12,8},{16,20},{20,16},{24,28},{28,24},{1,5},{5... | collective-permute-start | bytes 393224 | tf_op jit(solution)/shard_map/ppermute | solution.py:450
  8.6 2.7 %collective-permute-done.got_ref.refs_2_ = bf16[2,2,128,128]{3,2,1,0:T(8,128)(2,1)S(1)} collective-permute-done((bf16[2,2,128,128]{3,2,1,0:T(8,128)(2,1)}, bf16[2,2,128,128]{3,2,1,0:T(8,128)(2,1)S(1)}, u32[]{:S(2)}, u32[]{:S(2)}) %collective-permute-start) | collective-permute-done | bytes 131104 | tf_op jit(solution)/shard_map/ppermute | solution.py:450
  11.4 1.7 %collective-permute-start.6 = (bf16[1,512,512]{2,1,0:T(8,128)(2,1)}, bf16[1,512,512]{2,1,0:T(8,128)(2,1)S(1)}, u32[]{:S(2)}, u32[]{:S(2)}) collective-permute-start(bf16[1,512,512]{2,1,0:T(8,128)(2,1)} %get-tuple-element.53), channel_id=1, source_target_pairs={{0,4},{4,0},{8,12},{12,8},{16,20},{20,16},{24,28},{28,24},{1,5},{5... | collective-permute-start | bytes 1572872 | tf_op jit(solution)/shard_map/ppermute | solution.py:450
  13.9 5.0 %all-to-all-start = ((bf16[4,2,128,128]{3,2,1,0:T(8,128)(2,1)}), bf16[4,2,128,128]{3,2,1,0:T(8,128)(2,1)S(1)}, u32[]{:S(2)}, u32[]{:S(2)}) async-start(bf16[4,2,128,128]{3,2,1,0:T(8,128)(2,1)} %offer.1), calls=%async_computation | async-start | bytes 524288 | tf_op jit(solution)/shard_map/all_to_all | solution.py:478
  18.9 2.9 %collective-permute-start.13 = (bf16[512,512]{1,0:T(8,128)(2,1)}, bf16[512,512]{1,0:T(8,128)(2,1)}, u32[]{:S(2)}, u32[]{:S(2)}) collective-permute-start(bf16[512,512]{1,0:T(8,128)(2,1)} %refs_0_.3), channel_id=1, source_target_pairs={{0,16},{4,20},{16,24},{20,28},{24,8},{28,12},{8,0},{12,4},{1,17},{... | collective-permute-start | bytes 1572872 | tf_op jit(solution)/shard_map/ppermute | solution.py:466
  21.8 1.5 %collective-permute-start.4 = (bf16[1,512,512]{2,1,0:T(8,128)(2,1)S(1)}, bf16[1,512,512]{2,1,0:T(8,128)(2,1)S(1)}, u32[]{:S(2)}, u32[]{:S(2)}) collective-permute-start(bf16[1,512,512]{2,1,0:T(8,128)(2,1)S(1)} %get-tuple-element.51.refs_0_), channel_id=1, source_target_pairs={{0,2},{1,3},{2,0},{3,1},{4,6},{5,7},{6,4},{7,5},{8,10},{9,11},{10,... | collective-permute-start | bytes 1572872 | tf_op jit(solution)/shard_map/ppermute | solution.py:453
  23.3 14.7 %all-to-all-done.every_ref = bf16[4,2,128,128]{3,2,1,0:T(8,128)(2,1)S(1)} async-done(((bf16[4,2,128,128]{3,2,1,0:T(8,128)(2,1)}), bf16[4,2,128,128]{3,2,1,0:T(8,128)(2,1)S(1)}, u32[]{:S(2)}, u32[]{:S(2)}) %all-to-all-start) | async-done | bytes 262176 | tf_op jit(solution)/shard_map/all_to_all | solution.py:478
  41.4 1.5 %collective-permute-start.8 = (bf16[1,512,512]{2,1,0:T(8,128)(2,1)S(1)}, bf16[1,512,512]{2,1,0:T(8,128)(2,1)}, u32[]{:S(2)}, u32[]{:S(2)}) collective-permute-start(bf16[1,512,512]{2,1,0:T(8,128)(2,1)S(1)} %collective-permute-done.6.refs_4_), channel_id=1, source_target_pairs={{0,2},{1,3},{2,0},{3,1},{4,6},{5,7},{6,4},{7,5},{8,10},{9,11},{10,... | collective-permute-start | bytes 1572872 | tf_op jit(solution)/shard_map/ppermute | solution.py:453
  46.3 3.0 %inside.1 = (f32[512,512]{1,0:T(8,128)S(1)}, bf16[512,512]{1,0:T(8,128)(2,1)S(1)}) custom-call(bf16[512,512]{1,0:T(8,128)(2,1)S(1)} %copy-done, bf16[512,512]{1,0:T(8,128)(2,1)S(1)} %copy-done.2, bf16[512,512]{1,0:T(8,128)(2,1)S(1)} %copy-done.4), custom_call_target="tpu_custom_call" | custom-call | flops 1 | bytes 1 | tf_op jit(solution)/shard_map/inside/pallas_call | solution.py:146
  50.0 1.4 %finish_value.1.a_ref.x_ref = bf16[512,512]{1,0:T(8,128)(2,1)S(1)} custom-call(s32[1]{0:T(128)} %bitcast.par_ref, bf16[512,512]{1,0:T(8,128)(2,1)S(1)} %get-tuple-element.43.k_ref, f32[512,512]{1,0:T(8,128)S(1)} %get-tuple-element.44.vi_ref, f32[2,2,128,128]{3,2,1,0:T(8,128)S(1)} %get-tuple-element.45.refs_0_, ...), custom_call_target="tpu_custom_call" | custom-call | flops 1 | bytes 1 | tf_op jit(solution)/shard_map/finish_value/pallas_call | solution.py:219
  51.4 1.6 %collective-permute-start.2 = (bf16[512,512]{1,0:T(8,128)(2,1)S(1)}, bf16[512,512]{1,0:T(8,128)(2,1)S(1)}, u32[]{:S(2)}, u32[]{:S(2)}) collective-permute-start(bf16[512,512]{1,0:T(8,128)(2,1)S(1)} %finish_value.1.a_ref.x_ref), channel_id=1, source_target_pairs={{0,4},{4,0},{8,12},{12,8},{16,20},{20,16},{24,28},{28,24},{1,5},{5... | collective-permute-start | bytes 1572872 | tf_op jit(solution)/shard_map/ppermute | solution.py:450
  58.5 4.9 %others.1 = (bf16[512,512]{1,0:T(8,128)(2,1)}, bf16[512,512]{1,0:T(8,128)(2,1)}) custom-call(s32[1]{0:T(128)} %bitcast.par_ref, bf16[512,512]{1,0:T(8,128)(2,1)S(1)} %copy-done.1, bf16[512,512]{1,0:T(8,128)(2,1)S(1)} %copy-done.3, bf16[512,512]{1,0:T(8,128)(2,1)S(1)} %copy-done.8, bf16[512,512]{1,0:T(8,128)(2,1)S(1)} %copy-done.5, ...), custom_call_target="tpu_custom_call" | custom-call | flops 1 | bytes 1 | tf_op jit(solution)/shard_map/others/pallas_call | solution.py:249
  63.4 2.1 %collective-permute-done.2.b_ref.x_ref = bf16[512,512]{1,0:T(8,128)(2,1)S(1)} collective-permute-done((bf16[512,512]{1,0:T(8,128)(2,1)S(1)}, bf16[512,512]{1,0:T(8,128)(2,1)S(1)}, u32[]{:S(2)}, u32[]{:S(2)}) %collective-permute-start.2) | collective-permute-done | bytes 524320 | tf_op jit(solution)/shard_map/ppermute | solution.py:450
  65.5 2.5 %pieces.4 = bf16[512,512]{1,0:T(8,128)(2,1)S(1)} custom-call(s32[1]{0:T(128)} %get-tuple-element.75.offs_ref, s32[1]{0:T(128)} %constant.84.clone.1.subs_ref, bf16[512,512]{1,0:T(8,128)(2,1)S(1)} %finish_value.1.a_ref.x_ref, bf16[512,512]{1,0:T(8,128)(2,1)S(1)} %collective-permute-done.2.b_ref.x_ref, bf16[1,512,512]{2,1,0:T(8,128)(2,1)S(1)} %get-tuple-element.51.refs_0_, ...), custom_call_target="tpu_custom_call" | custom-call | flops 1 | bytes 1 | tf_op jit(solution)/shard_map/pieces/pallas_call | solution.py:303
  69.1 1.2 collective-permute-start.10
  71.7 2.6 %pieces.5.own_ref = f32[512,512]{1,0:T(8,128)S(1)} custom-call(s32[1]{0:T(128)} %get-tuple-element.74.offs_ref, s32[1]{0:T(128)} %constant.84.clone.1.subs_ref, bf16[512,512]{1,0:T(8,128)(2,1)S(1)} %finish_value.1.a_ref.x_ref, bf16[512,512]{1,0:T(8,128)(2,1)S(1)} %collective-permute-done.2.b_ref.x_ref, bf16[1,512,512]{2,1,0:T(8,128)(2,1)S(1)} %get-tuple-element.51.refs_0_, ...), custom_call_target="tpu_custom_call" | custom-call | flops 1 | bytes 1 | tf_op jit(solution)/shard_map/pieces/pallas_call | solution.py:303
  75.3 8.0 %collective-permute-done.15.refs_3_ = bf16[512,512]{1,0:T(8,128)(2,1)} collective-permute-done((bf16[512,512]{1,0:T(8,128)(2,1)}, bf16[512,512]{1,0:T(8,128)(2,1)}, u32[]{:S(2)}, u32[]{:S(2)}) %collective-permute-start.15) | collective-permute-done | bytes 524320 | tf_op jit(solution)/shard_map/ppermute | solution.py:466
  83.8 10.3 %collective-permute-done.10.moved_ref = bf16[512,512]{1,0:T(8,128)(2,1)S(1)} collective-permute-done((bf16[512,512]{1,0:T(8,128)(2,1)S(1)}, bf16[512,512]{1,0:T(8,128)(2,1)S(1)}, u32[]{:S(2)}, u32[]{:S(2)}) %collective-permute-start.10) | collective-permute-done | bytes 524320 | tf_op jit(solution)/shard_map/ppermute | solution.py:466
  97.9 1.7 %collective-permute-start.12 = (bf16[512,512]{1,0:T(8,128)(2,1)S(1)}, bf16[512,512]{1,0:T(8,128)(2,1)S(1)}, u32[]{:S(2)}, u32[]{:S(2)}) collective-permute-start(bf16[512,512]{1,0:T(8,128)(2,1)S(1)} %add_own.2), channel_id=1, source_target_pairs={{0,16},{4,20},{16,24},{20,28},{24,8},{28,12},{8,0},{12,4},{1,17},{... | collective-permute-start | bytes 1572872 | tf_op jit(solution)/shard_map/ppermute | solution.py:466
  99.6 2.1 %arrange.1 = (bf16[2,512,512]{2,1,0:T(8,128)(2,1)S(1)}, bf16[2,512,512]{2,1,0:T(8,128)(2,1)S(1)}) custom-call(s32[1]{0:T(128)} %bitcast.2.head_ref.at_ref, s32[4]{0:T(128)S(1)} %gather_fusion.1, bf16[512,512]{1,0:T(8,128)(2,1)} %refs_0_.3, bf16[512,512]{1,0:T(8,128)(2,1)} %collective-permute-done.13.refs_1_, ...), custom_call_target="tpu_custom_call" | custom-call | flops 1 | bytes 1 | tf_op jit(solution)/shard_map/arrange/pallas_call | solution.py:376
  102.5 1.2 collective-permute-start.22
  103.8 1.8 %head_part.4 = bf16[512,512]{1,0:T(8,128)(2,1)S(1)} custom-call(s32[1]{0:T(128)S(6)} %xor.12.at_ref, bf16[512,512]{1,0:T(8,128)(2,1)S(1)} %finish_value.1.a_ref.x_ref, bf16[512,512]{1,0:T(8,128)(2,1)} %collective-permute-done.20.y_ref, bf16[2,512,512]{2,1,0:T(8,128)(2,1)S(1)} %get-tuple-element.64.w_ref, bf16[2,512,512]{2,1,0:T(8,128)(2,1)S(1)} %get-tuple-element.65.wy_ref), custom_call_target="tpu_custom_call" | custom-call | flops 1 | bytes 1 | tf_op jit(solution)/shard_map/head_part/pallas_call | solution.py:399
  105.6 2.4 %pieces.6.own_ref = f32[512,512]{1,0:T(8,128)S(1)} custom-call(s32[1]{0:T(128)} %get-tuple-element.73.offs_ref, s32[1]{0:T(128)} %constant.84.clone.1.subs_ref, bf16[512,512]{1,0:T(8,128)(2,1)S(1)} %finish_value.1.a_ref.x_ref, bf16[512,512]{1,0:T(8,128)(2,1)S(1)} %collective-permute-done.2.b_ref.x_ref, bf16[1,512,512]{2,1,0:T(8,128)(2,1)S(1)} %get-tuple-element.51.refs_0_, ...), custom_call_target="tpu_custom_call" | custom-call | flops 1 | bytes 1 | tf_op jit(solution)/shard_map/pieces/pallas_call | solution.py:303
  108.0 5.2 %collective-permute-done.12.moved_ref = bf16[512,512]{1,0:T(8,128)(2,1)S(1)} collective-permute-done((bf16[512,512]{1,0:T(8,128)(2,1)S(1)}, bf16[512,512]{1,0:T(8,128)(2,1)S(1)}, u32[]{:S(2)}, u32[]{:S(2)}) %collective-permute-start.12) | collective-permute-done | bytes 524320 | tf_op jit(solution)/shard_map/ppermute | solution.py:466
  113.3 1.7 %collective-permute-start.21 = (bf16[512,512]{1,0:T(8,128)(2,1)S(1)}, bf16[512,512]{1,0:T(8,128)(2,1)S(1)}, u32[]{:S(2)}, u32[]{:S(2)}) collective-permute-start(bf16[512,512]{1,0:T(8,128)(2,1)S(1)} %add_own.3), channel_id=1, source_target_pairs={{0,16},{4,20},{16,24},{20,28},{24,8},{28,12},{8,0},{12,4},{1,17},{... | collective-permute-start | bytes 1572872 | tf_op jit(solution)/shard_map/ppermute | solution.py:466
  116.2 1.8 %pieces.7.own_ref = f32[512,512]{1,0:T(8,128)S(1)} custom-call(s32[1]{0:T(128)} %get-tuple-element.72.offs_ref, s32[1]{0:T(128)} %constant.84.clone.1.subs_ref, bf16[512,512]{1,0:T(8,128)(2,1)S(1)} %finish_value.1.a_ref.x_ref, bf16[512,512]{1,0:T(8,128)(2,1)S(1)} %collective-permute-done.2.b_ref.x_ref, bf16[1,512,512]{2,1,0:T(8,128)(2,1)S(1)} %get-tuple-element.51.refs_0_, ...), custom_call_target="tpu_custom_call" | custom-call | flops 1 | bytes 1 | tf_op jit(solution)/shard_map/pieces/pallas_call | solution.py:303
  118.8 1.6 %collective-permute-start.24 = (bf16[512,512]{1,0:T(8,128)(2,1)S(1)}, bf16[512,512]{1,0:T(8,128)(2,1)S(1)}, u32[]{:S(2)}, u32[]{:S(2)}) collective-permute-start(bf16[512,512]{1,0:T(8,128)(2,1)S(1)} %head_part.5), channel_id=1, source_target_pairs={{0,4},{4,0},{8,12},{12,8},{16,20},{20,16},{24,28},{28,24},{1,5},{5... | collective-permute-start | bytes 1572872 | tf_op jit(solution)/shard_map/ppermute | solution.py:450
  120.4 7.5 %collective-permute-done.21.moved_ref = bf16[512,512]{1,0:T(8,128)(2,1)S(1)} collective-permute-done((bf16[512,512]{1,0:T(8,128)(2,1)S(1)}, bf16[512,512]{1,0:T(8,128)(2,1)S(1)}, u32[]{:S(2)}, u32[]{:S(2)}) %collective-permute-start.21) | collective-permute-done | bytes 524320 | tf_op jit(solution)/shard_map/ppermute | solution.py:466
  127.8 1.3 finish_weight.1
  129.1 3.4 %collective-permute-done.24.refs_1_ = bf16[512,512]{1,0:T(8,128)(2,1)S(1)} collective-permute-done((bf16[512,512]{1,0:T(8,128)(2,1)S(1)}, bf16[512,512]{1,0:T(8,128)(2,1)S(1)}, u32[]{:S(2)}, u32[]{:S(2)}) %collective-permute-start.24) | collective-permute-done | bytes 524320 | tf_op jit(solution)/shard_map/ppermute | solution.py:450
  132.5 2.9 %join.1 = bf16[512,1024]{1,0:T(8,128)(2,1)} custom-call(s32[1]{0:T(128)} %bitcast.par_ref, s32[1]{0:T(128)} %bitcast.2.head_ref.at_ref, bf16[512,512]{1,0:T(8,128)(2,1)S(1)} %finish_value.1.a_ref.x_ref, bf16[512,512]{1,0:T(8,128)(2,1)} %collective-permute-done.20.y_ref, bf16[2,512,512]{2,1,0:T(8,128)(2,1)S(1)} %get-tuple-element.64.w_ref, ...), custom_call_target="tpu_custom_call" | custom-call | flops 1 | bytes 1 | tf_op jit(solution)/shard_map/join/pallas_call | solution.py:427
  (88 shorter events, 24.6 us)
Async XLA Ops:
  0.6 7.0 %copy-start.11 = (bf16[512,1024]{1,0:T(8,128)(2,1)S(1)}, bf16[512,1024]{1,0:T(8,128)(2,1)}, u32[]{:S(2)}) copy-start(bf16[512,1024]{1,0:T(8,128)(2,1)} %x_ref.1) | copy-start | bytes 3145732
  4.7 8.5 %copy-start.16 = (f32[2,2,128,128]{3,2,1,0:T(8,128)S(1)}, f32[2,2,128,128]{3,2,1,0:T(8,128)}, u32[]{:S(2)}) copy-start(f32[2,2,128,128]{3,2,1,0:T(8,128)} %get-tuple-element.38.keep_ref) | copy-start | bytes 786436
  4.7 6.7 %collective-permute-start = (bf16[2,2,128,128]{3,2,1,0:T(8,128)(2,1)}, bf16[2,2,128,128]{3,2,1,0:T(8,128)(2,1)S(1)}, u32[]{:S(2)}, u32[]{:S(2)}) collective-permute-start(bf16[2,2,128,128]{3,2,1,0:T(8,128)(2,1)} %get-tuple-element.39), channel_id=1, source_target_pairs={{0,4},{4,0},{8,12},{12,8},{16,20},{20,16},{24,28},{28,24},{1,5},{5... | collective-permute-start | bytes 393224 | tf_op jit(solution)/shard_map/ppermute | solution.py:450
  11.4 30.0 %collective-permute-start.6 = (bf16[1,512,512]{2,1,0:T(8,128)(2,1)}, bf16[1,512,512]{2,1,0:T(8,128)(2,1)S(1)}, u32[]{:S(2)}, u32[]{:S(2)}) collective-permute-start(bf16[1,512,512]{2,1,0:T(8,128)(2,1)} %get-tuple-element.53), channel_id=1, source_target_pairs={{0,4},{4,0},{8,12},{12,8},{16,20},{20,16},{24,28},{28,24},{1,5},{5... | collective-permute-start | bytes 1572872 | tf_op jit(solution)/shard_map/ppermute | solution.py:450
  13.1 32.1 %copy-start.2 = (bf16[512,512]{1,0:T(8,128)(2,1)S(1)}, bf16[512,512]{1,0:T(8,128)(2,1)}, u32[]{:S(2)}) copy-start(bf16[512,512]{1,0:T(8,128)(2,1)} %k_ref.1) | copy-start | bytes 1572868
  13.9 31.4 %copy-start = (bf16[512,512]{1,0:T(8,128)(2,1)S(1)}, bf16[512,512]{1,0:T(8,128)(2,1)}, u32[]{:S(2)}) copy-start(bf16[512,512]{1,0:T(8,128)(2,1)} %q_ref.1) | copy-start | bytes 1572868
  13.9 24.2 %all-to-all-start = ((bf16[4,2,128,128]{3,2,1,0:T(8,128)(2,1)}), bf16[4,2,128,128]{3,2,1,0:T(8,128)(2,1)S(1)}, u32[]{:S(2)}, u32[]{:S(2)}) async-start(bf16[4,2,128,128]{3,2,1,0:T(8,128)(2,1)} %offer.1), calls=%async_computation | async-start | bytes 524288 | tf_op jit(solution)/shard_map/all_to_all | solution.py:478
  18.9 30.4 %collective-permute-start.13 = (bf16[512,512]{1,0:T(8,128)(2,1)}, bf16[512,512]{1,0:T(8,128)(2,1)}, u32[]{:S(2)}, u32[]{:S(2)}) collective-permute-start(bf16[512,512]{1,0:T(8,128)(2,1)} %refs_0_.3), channel_id=1, source_target_pairs={{0,16},{4,20},{16,24},{20,28},{24,8},{28,12},{8,0},{12,4},{1,17},{... | collective-permute-start | bytes 1572872 | tf_op jit(solution)/shard_map/ppermute | solution.py:466
  21.8 27.6 %collective-permute-start.4 = (bf16[1,512,512]{2,1,0:T(8,128)(2,1)S(1)}, bf16[1,512,512]{2,1,0:T(8,128)(2,1)S(1)}, u32[]{:S(2)}, u32[]{:S(2)}) collective-permute-start(bf16[1,512,512]{2,1,0:T(8,128)(2,1)S(1)} %get-tuple-element.51.refs_0_), channel_id=1, source_target_pairs={{0,2},{1,3},{2,0},{3,1},{4,6},{5,7},{6,4},{7,5},{8,10},{9,11},{10,... | collective-permute-start | bytes 1572872 | tf_op jit(solution)/shard_map/ppermute | solution.py:453
  23.3 28.1 %collective-permute-start.3 = (bf16[1,512,512]{2,1,0:T(8,128)(2,1)S(1)}, bf16[1,512,512]{2,1,0:T(8,128)(2,1)S(1)}, u32[]{:S(2)}, u32[]{:S(2)}) collective-permute-start(bf16[1,512,512]{2,1,0:T(8,128)(2,1)S(1)} %get-tuple-element.51.refs_0_), channel_id=1, source_target_pairs={{0,1},{1,0},{2,3},{3,2},{4,5},{5,4},{6,7},{7,6},{8,9},{9,8},{10,11... | collective-permute-start | bytes 1572872 | tf_op jit(solution)/shard_map/ppermute | solution.py:453
  41.4 11.6 %collective-permute-start.8 = (bf16[1,512,512]{2,1,0:T(8,128)(2,1)S(1)}, bf16[1,512,512]{2,1,0:T(8,128)(2,1)}, u32[]{:S(2)}, u32[]{:S(2)}) collective-permute-start(bf16[1,512,512]{2,1,0:T(8,128)(2,1)S(1)} %collective-permute-done.6.refs_4_), channel_id=1, source_target_pairs={{0,2},{1,3},{2,0},{3,1},{4,6},{5,7},{6,4},{7,5},{8,10},{9,11},{10,... | collective-permute-start | bytes 1572872 | tf_op jit(solution)/shard_map/ppermute | solution.py:453
  42.9 6.7 %collective-permute-start.1 = (bf16[2,2,2,128,128]{4,3,2,1,0:T(8,128)(2,1)}, bf16[2,2,2,128,128]{4,3,2,1,0:T(8,128)(2,1)}, u32[]{:S(2)}, u32[]{:S(2)}) collective-permute-start(bf16[2,2,2,128,128]{4,3,2,1,0:T(8,128)(2,1)} %get-tuple-element.41), channel_id=1, source_target_pairs={{0,4},{4,0},{8,12},{12,8},{16,20},{20,16},{24,28},{28,24},{1,5},{5... | collective-permute-start | bytes 786440 | tf_op jit(solution)/shard_map/ppermute | solution.py:450
  49.3 18.7 %collective-permute-start.14 = (bf16[512,512]{1,0:T(8,128)(2,1)}, bf16[512,512]{1,0:T(8,128)(2,1)}, u32[]{:S(2)}, u32[]{:S(2)}) collective-permute-start(bf16[512,512]{1,0:T(8,128)(2,1)} %collective-permute-done.13.refs_1_), channel_id=1, source_target_pairs={{0,16},{4,20},{16,24},{20,28},{24,8},{28,12},{8,0},{12,4},{1,17},{... | collective-permute-start | bytes 1572872 | tf_op jit(solution)/shard_map/ppermute | solution.py:466
  49.4 14.0 %collective-permute-start.5 = (bf16[1,512,512]{2,1,0:T(8,128)(2,1)S(1)}, bf16[1,512,512]{2,1,0:T(8,128)(2,1)}, u32[]{:S(2)}, u32[]{:S(2)}) collective-permute-start(bf16[1,512,512]{2,1,0:T(8,128)(2,1)S(1)} %collective-permute-done.4.refs_2_), channel_id=1, source_target_pairs={{0,1},{1,0},{2,3},{3,2},{4,5},{5,4},{6,7},{7,6},{8,9},{9,8},{10,11... | collective-permute-start | bytes 1572872 | tf_op jit(solution)/shard_map/ppermute | solution.py:453
  49.6 13.8 %collective-permute-start.7 = (bf16[1,512,512]{2,1,0:T(8,128)(2,1)S(1)}, bf16[1,512,512]{2,1,0:T(8,128)(2,1)}, u32[]{:S(2)}, u32[]{:S(2)}) collective-permute-start(bf16[1,512,512]{2,1,0:T(8,128)(2,1)S(1)} %collective-permute-done.6.refs_4_), channel_id=1, source_target_pairs={{0,1},{1,0},{2,3},{3,2},{4,5},{5,4},{6,7},{7,6},{8,9},{9,8},{10,11... | collective-permute-start | bytes 1572872 | tf_op jit(solution)/shard_map/ppermute | solution.py:453
  50.0 3.1 %copy-start.18 = (s32[4]{0:T(128)S(1)}, s32[4]{0:T(128)}, u32[]{:S(2)}) copy-start(s32[4]{0:T(128)} %constant.87.clone) | copy-start | bytes 52
  51.4 14.1 %collective-permute-start.2 = (bf16[512,512]{1,0:T(8,128)(2,1)S(1)}, bf16[512,512]{1,0:T(8,128)(2,1)S(1)}, u32[]{:S(2)}, u32[]{:S(2)}) collective-permute-start(bf16[512,512]{1,0:T(8,128)(2,1)S(1)} %finish_value.1.a_ref.x_ref), channel_id=1, source_target_pairs={{0,4},{4,0},{8,12},{12,8},{16,20},{20,16},{24,28},{28,24},{1,5},{5... | collective-permute-start | bytes 1572872 | tf_op jit(solution)/shard_map/ppermute | solution.py:450
  53.0 12.5 %collective-permute-start.9 = (bf16[1,512,512]{2,1,0:T(8,128)(2,1)}, bf16[1,512,512]{2,1,0:T(8,128)(2,1)}, u32[]{:S(2)}, u32[]{:S(2)}) collective-permute-start(bf16[1,512,512]{2,1,0:T(8,128)(2,1)} %collective-permute-done.8.refs_6_), channel_id=1, source_target_pairs={{0,1},{1,0},{2,3},{3,2},{4,5},{5,4},{6,7},{7,6},{8,9},{9,8},{10,11... | collective-permute-start | bytes 1572872 | tf_op jit(solution)/shard_map/ppermute | solution.py:453
  68.0 2.9 %collective-permute-start.11 = (bf16[512,512]{1,0:T(8,128)(2,1)S(1)}, bf16[512,512]{1,0:T(8,128)(2,1)S(1)}, u32[]{:S(2)}, u32[]{:S(2)}) collective-permute-start(bf16[512,512]{1,0:T(8,128)(2,1)S(1)} %collective-permute-done.2.b_ref.x_ref), channel_id=1, source_target_pairs={{0,1},{1,0},{2,3},{3,2},{4,5},{5,4},{6,7},{7,6},{8,9},{9,8},{10,11... | collective-permute-start | bytes 1572872 | tf_op jit(solution)/shard_map/ppermute | solution.py:453
  68.1 15.2 %collective-permute-start.15 = (bf16[512,512]{1,0:T(8,128)(2,1)}, bf16[512,512]{1,0:T(8,128)(2,1)}, u32[]{:S(2)}, u32[]{:S(2)}) collective-permute-start(bf16[512,512]{1,0:T(8,128)(2,1)} %collective-permute-done.14.refs_2_), channel_id=1, source_target_pairs={{0,16},{4,20},{16,24},{20,28},{24,8},{28,12},{8,0},{12,4},{1,17},{... | collective-permute-start | bytes 1572872 | tf_op jit(solution)/shard_map/ppermute | solution.py:466
  69.1 25.0 %collective-permute-start.10 = (bf16[512,512]{1,0:T(8,128)(2,1)S(1)}, bf16[512,512]{1,0:T(8,128)(2,1)S(1)}, u32[]{:S(2)}, u32[]{:S(2)}) collective-permute-start(bf16[512,512]{1,0:T(8,128)(2,1)S(1)} %pieces.4), channel_id=1, source_target_pairs={{0,16},{4,20},{16,24},{20,28},{24,8},{28,12},{8,0},{12,4},{1,17},{... | collective-permute-start | bytes 1572872 | tf_op jit(solution)/shard_map/ppermute | solution.py:466
  70.3 27.6 %collective-permute-start.17 = (bf16[512,512]{1,0:T(8,128)(2,1)}, bf16[512,512]{1,0:T(8,128)(2,1)}, u32[]{:S(2)}, u32[]{:S(2)}) collective-permute-start(bf16[512,512]{1,0:T(8,128)(2,1)} %collective-permute-done.13.refs_1_), channel_id=1, source_target_pairs={{0,1},{1,0},{2,3},{3,2},{4,5},{5,4},{6,7},{7,6},{8,9},{9,8},{10,11... | collective-permute-start | bytes 1572872 | tf_op jit(solution)/shard_map/ppermute | solution.py:453
  70.3 29.3 %collective-permute-start.16 = (bf16[512,512]{1,0:T(8,128)(2,1)}, bf16[512,512]{1,0:T(8,128)(2,1)}, u32[]{:S(2)}, u32[]{:S(2)}) collective-permute-start(bf16[512,512]{1,0:T(8,128)(2,1)} %refs_0_.3), channel_id=1, source_target_pairs={{0,1},{1,0},{2,3},{3,2},{4,5},{5,4},{6,7},{7,6},{8,9},{9,8},{10,11... | collective-permute-start | bytes 1572872 | tf_op jit(solution)/shard_map/ppermute | solution.py:453
  71.7 28.0 %collective-permute-start.18 = (bf16[512,512]{1,0:T(8,128)(2,1)}, bf16[512,512]{1,0:T(8,128)(2,1)}, u32[]{:S(2)}, u32[]{:S(2)}) collective-permute-start(bf16[512,512]{1,0:T(8,128)(2,1)} %collective-permute-done.14.refs_2_), channel_id=1, source_target_pairs={{0,1},{1,0},{2,3},{3,2},{4,5},{5,4},{6,7},{7,6},{8,9},{9,8},{10,11... | collective-permute-start | bytes 1572872 | tf_op jit(solution)/shard_map/ppermute | solution.py:453
  83.2 16.4 %collective-permute-start.19 = (bf16[512,512]{1,0:T(8,128)(2,1)}, bf16[512,512]{1,0:T(8,128)(2,1)}, u32[]{:S(2)}, u32[]{:S(2)}) collective-permute-start(bf16[512,512]{1,0:T(8,128)(2,1)} %collective-permute-done.15.refs_3_), channel_id=1, source_target_pairs={{0,1},{1,0},{2,3},{3,2},{4,5},{5,4},{6,7},{7,6},{8,9},{9,8},{10,11... | collective-permute-start | bytes 1572872 | tf_op jit(solution)/shard_map/ppermute | solution.py:453
  94.9 8.9 %collective-permute-start.20 = (bf16[512,512]{1,0:T(8,128)(2,1)S(1)}, bf16[512,512]{1,0:T(8,128)(2,1)}, u32[]{:S(2)}, u32[]{:S(2)}) collective-permute-start(bf16[512,512]{1,0:T(8,128)(2,1)S(1)} %finish_value.1.a_ref.x_ref), channel_id=1, source_target_pairs={{0,1},{1,0},{2,3},{3,2},{4,5},{5,4},{6,7},{7,6},{8,9},{9,8},{10,11... | collective-permute-start | bytes 1572872 | tf_op jit(solution)/shard_map/ppermute | solution.py:453
  97.9 3.9 %copy-start.10 = (bf16[512,512]{1,0:T(8,128)(2,1)S(1)}, bf16[512,512]{1,0:T(8,128)(2,1)}, u32[]{:S(2)}) copy-start(bf16[512,512]{1,0:T(8,128)(2,1)} %copy-done.9) | copy-start | bytes 1572868
  97.9 15.3 %collective-permute-start.12 = (bf16[512,512]{1,0:T(8,128)(2,1)S(1)}, bf16[512,512]{1,0:T(8,128)(2,1)S(1)}, u32[]{:S(2)}, u32[]{:S(2)}) collective-permute-start(bf16[512,512]{1,0:T(8,128)(2,1)S(1)} %add_own.2), channel_id=1, source_target_pairs={{0,16},{4,20},{16,24},{20,28},{24,8},{28,12},{8,0},{12,4},{1,17},{... | collective-permute-start | bytes 1572872 | tf_op jit(solution)/shard_map/ppermute | solution.py:466
  102.5 15.5 %collective-permute-start.22 = (bf16[512,512]{1,0:T(8,128)(2,1)S(1)}, bf16[512,512]{1,0:T(8,128)(2,1)S(1)}, u32[]{:S(2)}, u32[]{:S(2)}) collective-permute-start(bf16[512,512]{1,0:T(8,128)(2,1)S(1)} %head_part.3), channel_id=1, source_target_pairs={{0,2},{1,3},{2,0},{3,1},{4,6},{5,7},{6,4},{7,5},{8,10},{9,11},{10,... | collective-permute-start | bytes 1572872 | tf_op jit(solution)/shard_map/ppermute | solution.py:453
  113.3 14.5 %collective-permute-start.21 = (bf16[512,512]{1,0:T(8,128)(2,1)S(1)}, bf16[512,512]{1,0:T(8,128)(2,1)S(1)}, u32[]{:S(2)}, u32[]{:S(2)}) collective-permute-start(bf16[512,512]{1,0:T(8,128)(2,1)S(1)} %add_own.3), channel_id=1, source_target_pairs={{0,16},{4,20},{16,24},{20,28},{24,8},{28,12},{8,0},{12,4},{1,17},{... | collective-permute-start | bytes 1572872 | tf_op jit(solution)/shard_map/ppermute | solution.py:466
  115.0 14.1 %collective-permute-start.23 = (bf16[512,512]{1,0:T(8,128)(2,1)S(1)}, bf16[512,512]{1,0:T(8,128)(2,1)S(1)}, u32[]{:S(2)}, u32[]{:S(2)}) collective-permute-start(bf16[512,512]{1,0:T(8,128)(2,1)S(1)} %head_part.4), channel_id=1, source_target_pairs={{0,2},{1,3},{2,0},{3,1},{4,6},{5,7},{6,4},{7,5},{8,10},{9,11},{10,... | collective-permute-start | bytes 1572872 | tf_op jit(solution)/shard_map/ppermute | solution.py:453
  118.8 13.7 %collective-permute-start.24 = (bf16[512,512]{1,0:T(8,128)(2,1)S(1)}, bf16[512,512]{1,0:T(8,128)(2,1)S(1)}, u32[]{:S(2)}, u32[]{:S(2)}) collective-permute-start(bf16[512,512]{1,0:T(8,128)(2,1)S(1)} %head_part.5), channel_id=1, source_target_pairs={{0,4},{4,0},{8,12},{12,8},{16,20},{20,16},{24,28},{28,24},{1,5},{5... | collective-permute-start | bytes 1572872 | tf_op jit(solution)/shard_map/ppermute | solution.py:450
  (14 other events, 13.3 us)

commit v12 on v11

--- a/solution.py
+++ b/solution.py
@@ -116,14 +116,21 @@
 
 
 def inside_kernel(*refs):
-    arrays, (out_ref, k_ref), bufs, sems = refs[:3], refs[3:5], refs[5:8], refs[8]
+    arrays, out_ref, bufs, (made, sems, done) = refs[:3], refs[3], refs[4:7], refs[7:]
     n, cols = out_ref.shape
     heads = cols // DH
 
+    def at(hd):
+        return pl.ds(hd * DH, DH)
+
     def copy(j, hd):
-        at = pl.ds(hd * DH, DH)
         return pltpu.make_async_copy(
-            arrays[j].at[:, at], bufs[j].at[:, at], sems.at[j, hd]
+            arrays[j].at[:, at(hd)], bufs[j].at[:, at(hd)], sems.at[j, hd]
+        )
+
+    def give(hd):
+        return pltpu.make_async_copy(
+            made.at[:, at(hd)], out_ref.at[:, at(hd)], done.at[hd]
         )
 
     for hd in range(heads):
@@ -132,24 +139,31 @@
     rows = lax.broadcasted_iota(jnp.int32, (n, n), 0)
     causal = rows >= lax.broadcasted_iota(jnp.int32, (n, n), 1)
     for hd in range(heads):
-        at = slice(hd * DH, (hd + 1) * DH)
         for j in range(3):
             copy(j, hd).wait()
-        q, k, g = (x[:, at] for x in bufs)
+        q, k, g = (x[:, at(hd)] for x in bufs)
         scores = jnp.where(causal, dot(q, k, 1, 1), 0.0).astype(BF16)
-        out_ref[:, at] = dot(scores, g, 0, 0)
-        k_ref[:, at] = k
+        made[:, at(hd)] = dot(scores, g, 0, 0)
+        give(hd).start()
+    for hd in range(heads):
+        give(hd).wait()
 
 
 def inside(*arrays):
     n, cols = arrays[0].shape
+    heads = cols // DH
+    hbm = pl.BlockSpec(memory_space=pltpu.HBM)
     return call(
         inside_kernel,
-        in_specs=[pl.BlockSpec(memory_space=pltpu.HBM)] * 3,
-        out_specs=[VMEM] * 2,
-        out_shape=[jax.ShapeDtypeStruct((n, cols), d) for d in (F32, BF16)],
+        in_specs=[hbm] * 3,
+        out_specs=hbm,
+        out_shape=jax.ShapeDtypeStruct((n, cols), F32),
         scratch_shapes=[pltpu.VMEM((n, cols), BF16)] * 3
-        + [pltpu.SemaphoreType.DMA((3, cols // DH))],
+        + [
+            pltpu.VMEM((n, cols), F32),
+            pltpu.SemaphoreType.DMA((3, heads)),
+            pltpu.SemaphoreType.DMA((heads,)),
+        ],
         name="inside",
     )(*arrays)
 
@@ -205,22 +219,43 @@
     return hi, (total - hi.astype(F32)).astype(BF16)
 
 
-def value_kernel(factor, half, par_ref, k_ref, vi_ref, *refs):
-    ends, out_ref = refs[:-1], refs[-1]
+def value_kernel(factor, half, par_ref, k_any, vi_any, *refs):
+    ends, out_ref, k_ref, vi_ref, sems = refs[:-4], *refs[-4:]
+
+    def copies(hd):
+        at = pl.ds(hd * DH, DH)
+        return [
+            pltpu.make_async_copy(src.at[:, at], dst.at[:, at], sems.at[j, hd])
+            for j, (src, dst) in enumerate(((k_any, k_ref), (vi_any, vi_ref)))
+        ]
+
+    for hd in range(2 * half):
+        for c in copies(hd):
+            c.start()
     for hd in range(2 * half):
         at = slice(hd * DH, (hd + 1) * DH)
         hi, lo = entering(par_ref[0], 0, hd, half, *ends)
+        for c in copies(hd):
+            c.wait()
         k = k_ref[:, at]
         total = vi_ref[:, at] + (dot(k, hi, 1, 0) + dot(k, lo, 1, 0))
         out_ref[:, at] = (factor * total).astype(BF16)
 
 
 def finish_value(factor, par, k, vi, ends):
-    return call(
-        functools.partial(value_kernel, factor, k.shape[1] // DH // 2),
-        in_specs=[SMEM] + [VMEM] * (2 + len(ends)),
+    heads = k.shape[1] // DH
+    return call(
+        functools.partial(value_kernel, factor, heads // 2),
+        in_specs=[SMEM]
+        + [pl.BlockSpec(memory_space=pltpu.HBM)] * 2
+        + [VMEM] * len(ends),
         out_specs=VMEM,
         out_shape=jax.ShapeDtypeStruct(k.shape, BF16),
+        scratch_shapes=[
+            pltpu.VMEM(k.shape, BF16),
+            pltpu.VMEM(k.shape, F32),
+            pltpu.SemaphoreType.DMA((2, heads)),
+        ],
         name="finish_value",
     )(par, k, vi, *ends)
 
@@ -474,15 +509,15 @@
     blocks = [value_weight, ring(after(value_weight, send))]
     own, theirs = [own], [partner(after(theirs, their_half))]
 
-    offered = offer(line, keep, their_half, pairs)
+    vi = inside(after(queries, own[0]), keys, out_grad)
+    offered = offer(line, after(keep, vi), their_half, pairs)
     every = lax.all_to_all(
         offered, "ctx", split_axis=0, concat_axis=0, axis_index_groups=lines
     )
     far, send_far = far_states(line, every, near16)
     ends = (far, partner(send_far), their_half)
-    vi, keys_too = inside(after(queries, send_far), keys, out_grad)
     theirs = [after(theirs[0], send_far)]
-    mine = finish_value(factor, par, keys_too, vi, ends)
+    mine = finish_value(factor, par, keys, vi, ends)
     other = partner(mine)
     query_grad, key_grad = others(
         factor, par, queries, keys, after(values, mine), out_grad, ends
@@ -513,9 +548,9 @@
 
     total = piece(BF16, 0, query_grad)
     moved = ring(total)
-    other_too = across(after(other, total), 1)
+    other_too = across(after(other, total, blocks[-1]), 1)
+    lent.append(across(after(blocks[-1], total), 1))
     local_part = piece(F32, 1, other_too)
-    lent.append(across(after(blocks[-1], local_part), 1))
 
     here = head.astype(jnp.int32).reshape(1)
     held = jnp.asarray(order, jnp.int32)[(spot - steps) % pairs]

time: 136 us -> 116 us (0.85)
  waiting for transfers between devices: 54 us -> 44.3 us
  local copies, waits for them, and re-layouts: 15.8 us -> 9.56 us
  starting transfers between devices: 28.5 us -> 25.7 us
  Pallas kernels: 35 us -> 33.5 us
    all_to_all x1, waiting for transfers between devices: 14.7 us -> 6.5 us  [local(): lax.all_to_all(offered, 'ctx', split_axis=0, concat_axis=0, axis_index_gr...]
    unnamed x40 -> x30, local copies, waits for them, and re-layouts: 13.3 us -> 7.05 us
    ppermute x6, waiting for transfers between devices: 30.9 us -> 26.2 us  [ring(): return lax.ppermute(x, 'ctx', moves)]
    ppermute x14, waiting for transfers between devices: 0.04 us -> 2.48 us  [across(): return lax.ppermute(x, 'head', [(i, i ^ bit) for i in range(n_head)])]
    ppermute x5, starting transfers between devices: 8.39 us -> 6.48 us  [partner(): return lax.ppermute(x, 'ctx', [(i, i ^ 1) for i in range(n_ctx)])]
  transfers between devices with their start and end apart: 26 -> 26, of which waited for: 9 -> 11; matrix products, arithmetic and copies ran while one was open for 2% -> 3% of each run, Pallas kernels for 21% -> 24%
where the time goes in v12:
time: 116 us; the launch traced here: 115 us
  waiting for transfers between devices  44.3 us (38%)
  Pallas kernels  33.5 us (29%)
  starting transfers between devices  25.7 us (22%)
  local copies, waits for them, and re-layouts  9.56 us (8%)
  between operations  1.59 us (1%)
    ppermute x6, waiting for transfers between devices, ring(): return lax.ppermute(x, 'ctx', moves)  26.2 us
    pallas_call x4, Pallas kernels, pieces(): call(functools.partial(piece_kernel, count), grid=(steps,), in_specs=[SME...  10.3 us
    ppermute x5, waiting for transfers between devices, partner(): return lax.ppermute(x, 'ctx', [(i, i ^ 1) for i in range(n_ctx)])  9.09 us
    ppermute x6, starting transfers between devices, ring(): return lax.ppermute(x, 'ctx', moves)  7.81 us
    unnamed x30, local copies, waits for them, and re-layouts  7.05 us
    all_to_all x1, waiting for transfers between devices, local(): lax.all_to_all(offered, 'ctx', split_axis=0, concat_axis=0, axis_index_gr...  6.5 us
    ppermute x5, starting transfers between devices, partner(): return lax.ppermute(x, 'ctx', [(i, i ^ 1) for i in range(n_ctx)])  6.48 us
    ppermute x14, starting transfers between devices, across(): return lax.ppermute(x, 'head', [(i, i ^ bit) for i in range(n_head)])  6.42 us
  transfers between devices with their start and end apart: 26, of which 11 were waited for; matrix products, arithmetic and copies ran while one was open for 3% of the time, Pallas kernels for 24%

profile of v12, /device:TPU:0, one launch (start us, length us, event | category | flops | bytes accessed | tf_op | source)
XLA Modules:
  0.0 115.3 jit_solution(14754553028330583979)
XLA Ops:
  0.7 4.0 %states.1 = (f32[2,2,128,128]{3,2,1,0:T(8,128)}, bf16[2,2,128,128]{3,2,1,0:T(8,128)(2,1)}, bf16[2,2,128,128]{3,2,1,0:T(8,128)(2,1)}) custom-call(s32[1]{0:T(128)} %bitcast.par_ref, bf16[512,512]{1,0:T(8,128)(2,1)} %q_ref.1, bf16[512,512]{1,0:T(8,128)(2,1)} %k_ref.1, bf16[512,512]{1,0:T(8,128)(2,1)} %v_ref, bf16[512,512]{1,0:T(8,128)(2,1)} %g_ref.1), custom_call_target="tpu_custom_call" | custom-call | flops 1 | bytes 1 | tf_op jit(solution)/shard_map/states/pallas_call | solution.py:69
  4.7 3.0 %collective-permute-start = (bf16[2,2,128,128]{3,2,1,0:T(8,128)(2,1)}, bf16[2,2,128,128]{3,2,1,0:T(8,128)(2,1)S(1)}, u32[]{:S(2)}, u32[]{:S(2)}) collective-permute-start(bf16[2,2,128,128]{3,2,1,0:T(8,128)(2,1)} %get-tuple-element.37), channel_id=1, source_target_pairs={{0,4},{4,0},{8,12},{12,8},{16,20},{20,16},{24,28},{28,24},{1,5},{5... | collective-permute-start | bytes 393224 | tf_op jit(solution)/shard_map/ppermute | solution.py:485
  7.7 2.6 %collective-permute-start.11 = (bf16[512,512]{1,0:T(8,128)(2,1)}, bf16[512,512]{1,0:T(8,128)(2,1)}, u32[]{:S(2)}, u32[]{:S(2)}) collective-permute-start(bf16[512,512]{1,0:T(8,128)(2,1)} %refs_0_.3), channel_id=1, source_target_pairs={{0,16},{4,20},{16,24},{20,28},{24,8},{28,12},{8,0},{12,4},{1,17},{... | collective-permute-start | bytes 1572872 | tf_op jit(solution)/shard_map/ppermute | solution.py:501
  11.4 1.7 %collective-permute-start.6 = (bf16[1,512,512]{2,1,0:T(8,128)(2,1)}, bf16[1,512,512]{2,1,0:T(8,128)(2,1)S(1)}, u32[]{:S(2)}, u32[]{:S(2)}) collective-permute-start(bf16[1,512,512]{2,1,0:T(8,128)(2,1)} %get-tuple-element.51), channel_id=1, source_target_pairs={{0,4},{4,0},{8,12},{12,8},{16,20},{20,16},{24,28},{28,24},{1,5},{5... | collective-permute-start | bytes 1572872 | tf_op jit(solution)/shard_map/ppermute | solution.py:485
  13.2 3.2 %inside.1.vi_any = f32[512,512]{1,0:T(8,128)S(1)} custom-call(bf16[512,512]{1,0:T(8,128)(2,1)S(1)} %copy-done.1, bf16[512,512]{1,0:T(8,128)(2,1)S(1)} %copy-done, bf16[512,512]{1,0:T(8,128)(2,1)S(1)} %copy-done.3), custom_call_target="tpu_custom_call" | custom-call | flops 1 | bytes 1 | tf_op jit(solution)/shard_map/inside/pallas_call | solution.py:156
  18.1 5.0 %all-to-all-start = ((bf16[4,2,128,128]{3,2,1,0:T(8,128)(2,1)}), bf16[4,2,128,128]{3,2,1,0:T(8,128)(2,1)S(1)}, u32[]{:S(2)}, u32[]{:S(2)}) async-start(bf16[4,2,128,128]{3,2,1,0:T(8,128)(2,1)} %offer.1), calls=%async_computation | async-start | bytes 524288 | tf_op jit(solution)/shard_map/all_to_all | solution.py:514
  23.1 1.5 %collective-permute-start.4 = (bf16[1,512,512]{2,1,0:T(8,128)(2,1)S(1)}, bf16[1,512,512]{2,1,0:T(8,128)(2,1)S(1)}, u32[]{:S(2)}, u32[]{:S(2)}) collective-permute-start(bf16[1,512,512]{2,1,0:T(8,128)(2,1)S(1)} %get-tuple-element.39.refs_0_), channel_id=1, source_target_pairs={{0,2},{1,3},{2,0},{3,1},{4,6},{5,7},{6,4},{7,5},{8,10},{9,11},{10,... | collective-permute-start | bytes 1572872 | tf_op jit(solution)/shard_map/ppermute | solution.py:488
  24.6 6.5 %all-to-all-done.every_ref = bf16[4,2,128,128]{3,2,1,0:T(8,128)(2,1)S(1)} async-done(((bf16[4,2,128,128]{3,2,1,0:T(8,128)(2,1)}), bf16[4,2,128,128]{3,2,1,0:T(8,128)(2,1)S(1)}, u32[]{:S(2)}, u32[]{:S(2)}) %all-to-all-start) | async-done | bytes 262176 | tf_op jit(solution)/shard_map/all_to_all | solution.py:514
  31.4 1.6 %collective-permute-start.8 = (bf16[1,512,512]{2,1,0:T(8,128)(2,1)S(1)}, bf16[1,512,512]{2,1,0:T(8,128)(2,1)}, u32[]{:S(2)}, u32[]{:S(2)}) collective-permute-start(bf16[1,512,512]{2,1,0:T(8,128)(2,1)S(1)} %collective-permute-done.6.refs_4_), channel_id=1, source_target_pairs={{0,2},{1,3},{2,0},{3,1},{4,6},{5,7},{6,4},{7,5},{8,10},{9,11},{10,... | collective-permute-start | bytes 1572872 | tf_op jit(solution)/shard_map/ppermute | solution.py:488
  36.1 5.3 %collective-permute-done.1.refs_1_ = bf16[2,2,2,128,128]{4,3,2,1,0:T(8,128)(2,1)S(1)} collective-permute-done((bf16[2,2,2,128,128]{4,3,2,1,0:T(8,128)(2,1)S(1)}, bf16[2,2,2,128,128]{4,3,2,1,0:T(8,128)(2,1)S(1)}, u32[]{:S(2)}, u32[]{:S(2)}) %collective-permute-start.1) | collective-permute-done | bytes 262176 | tf_op jit(solution)/shard_map/ppermute | solution.py:485
  41.4 1.3 %copy-done.6 = f32[512,512]{1,0:T(8,128)S(1)} copy-done((f32[512,512]{1,0:T(8,128)S(1)}, f32[512,512]{1,0:T(8,128)}, u32[]{:S(2)}) %copy-start.6) | copy-done | bytes 1048600
  42.7 1.4 %finish_value.1.a_ref.x_ref = bf16[512,512]{1,0:T(8,128)(2,1)S(1)} custom-call(s32[1]{0:T(128)} %bitcast.par_ref, bf16[512,512]{1,0:T(8,128)(2,1)S(1)} %copy-done, f32[512,512]{1,0:T(8,128)S(1)} %copy-done.6, f32[2,2,128,128]{3,2,1,0:T(8,128)S(1)} %get-tuple-element.44.refs_0_, bf16[2,2,2,128,128]{4,3,2,1,0:T(8,128)(2,1)S(1)} %collective-permute-done.1.refs_1_, ...), custom_call_target="tpu_custom_call" | custom-call | flops 1 | bytes 1 | tf_op jit(solution)/shard_map/finish_value/pallas_call | solution.py:247
  44.7 1.6 %collective-permute-start.13 = (bf16[512,512]{1,0:T(8,128)(2,1)}, bf16[512,512]{1,0:T(8,128)(2,1)}, u32[]{:S(2)}, u32[]{:S(2)}) collective-permute-start(bf16[512,512]{1,0:T(8,128)(2,1)} %collective-permute-done.12.refs_2_), channel_id=1, source_target_pairs={{0,16},{4,20},{16,24},{20,28},{24,8},{28,12},{8,0},{12,4},{1,17},{... | collective-permute-start | bytes 1572872 | tf_op jit(solution)/shard_map/ppermute | solution.py:501
  48.0 1.0 copy-done.2
  52.1 4.0 %others.1 = (bf16[512,512]{1,0:T(8,128)(2,1)}, bf16[512,512]{1,0:T(8,128)(2,1)}) custom-call(s32[1]{0:T(128)} %bitcast.par_ref, bf16[512,512]{1,0:T(8,128)(2,1)S(1)} %copy-done.2, bf16[512,512]{1,0:T(8,128)(2,1)S(1)} %copy-done, bf16[512,512]{1,0:T(8,128)(2,1)S(1)} %copy-done.7, bf16[512,512]{1,0:T(8,128)(2,1)S(1)} %copy-done.4, ...), custom_call_target="tpu_custom_call" | custom-call | flops 1 | bytes 1 | tf_op jit(solution)/shard_map/others/pallas_call | solution.py:284
  56.1 2.3 %collective-permute-done.2.b_ref.x_ref = bf16[512,512]{1,0:T(8,128)(2,1)S(1)} collective-permute-done((bf16[512,512]{1,0:T(8,128)(2,1)S(1)}, bf16[512,512]{1,0:T(8,128)(2,1)S(1)}, u32[]{:S(2)}, u32[]{:S(2)}) %collective-permute-start.2) | collective-permute-done | bytes 524320 | tf_op jit(solution)/shard_map/ppermute | solution.py:485
  58.5 3.4 %pieces.4 = bf16[512,512]{1,0:T(8,128)(2,1)} custom-call(s32[1]{0:T(128)} %get-tuple-element.73.offs_ref, s32[1]{0:T(128)} %constant.84.clone.1.subs_ref, bf16[512,512]{1,0:T(8,128)(2,1)S(1)} %finish_value.1.a_ref.x_ref, bf16[512,512]{1,0:T(8,128)(2,1)S(1)} %collective-permute-done.2.b_ref.x_ref, bf16[1,512,512]{2,1,0:T(8,128)(2,1)S(1)} %get-tuple-element.39.refs_0_, ...), custom_call_target="tpu_custom_call" | custom-call | flops 1 | bytes 1 | tf_op jit(solution)/shard_map/pieces/pallas_call | solution.py:338
  61.9 1.4 %collective-permute-start.10 = (bf16[512,512]{1,0:T(8,128)(2,1)}, bf16[512,512]{1,0:T(8,128)(2,1)}, u32[]{:S(2)}, u32[]{:S(2)}) collective-permute-start(bf16[512,512]{1,0:T(8,128)(2,1)} %pieces.4), channel_id=1, source_target_pairs={{0,16},{4,20},{16,24},{20,28},{24,8},{28,12},{8,0},{12,4},{1,17},{... | collective-permute-start | bytes 1572872 | tf_op jit(solution)/shard_map/ppermute | solution.py:501
  65.6 11.3 %collective-permute-done.10.moved_ref = bf16[512,512]{1,0:T(8,128)(2,1)} collective-permute-done((bf16[512,512]{1,0:T(8,128)(2,1)}, bf16[512,512]{1,0:T(8,128)(2,1)}, u32[]{:S(2)}, u32[]{:S(2)}) %collective-permute-start.10) | collective-permute-done | bytes 524320 | tf_op jit(solution)/shard_map/ppermute | solution.py:501
  76.9 2.7 %pieces.5.own_ref = f32[512,512]{1,0:T(8,128)S(1)} custom-call(s32[1]{0:T(128)} %get-tuple-element.72.offs_ref, s32[1]{0:T(128)} %constant.84.clone.1.subs_ref, bf16[512,512]{1,0:T(8,128)(2,1)S(1)} %finish_value.1.a_ref.x_ref, bf16[512,512]{1,0:T(8,128)(2,1)S(1)} %collective-permute-done.2.b_ref.x_ref, bf16[1,512,512]{2,1,0:T(8,128)(2,1)S(1)} %get-tuple-element.39.refs_0_, ...), custom_call_target="tpu_custom_call" | custom-call | flops 1 | bytes 1 | tf_op jit(solution)/shard_map/pieces/pallas_call | solution.py:338
  79.6 1.1 add_own.2
  80.7 1.4 %collective-permute-start.15 = (bf16[512,512]{1,0:T(8,128)(2,1)S(1)}, bf16[512,512]{1,0:T(8,128)(2,1)S(1)}, u32[]{:S(2)}, u32[]{:S(2)}) collective-permute-start(bf16[512,512]{1,0:T(8,128)(2,1)S(1)} %add_own.2), channel_id=1, source_target_pairs={{0,16},{4,20},{16,24},{20,28},{24,8},{28,12},{8,0},{12,4},{1,17},{... | collective-permute-start | bytes 1572872 | tf_op jit(solution)/shard_map/ppermute | solution.py:501
  82.2 2.1 %arrange.1 = (bf16[2,512,512]{2,1,0:T(8,128)(2,1)S(1)}, bf16[2,512,512]{2,1,0:T(8,128)(2,1)S(1)}) custom-call(s32[1]{0:T(128)} %bitcast.2.head_ref.at_ref, s32[4]{0:T(128)S(1)} %gather_fusion.1, bf16[512,512]{1,0:T(8,128)(2,1)} %refs_0_.3, bf16[512,512]{1,0:T(8,128)(2,1)} %collective-permute-done.11.refs_1_, ...), custom_call_target="tpu_custom_call" | custom-call | flops 1 | bytes 1 | tf_op jit(solution)/shard_map/arrange/pallas_call | solution.py:411
  85.1 1.3 %collective-permute-start.22 = (bf16[512,512]{1,0:T(8,128)(2,1)S(1)}, bf16[512,512]{1,0:T(8,128)(2,1)S(1)}, u32[]{:S(2)}, u32[]{:S(2)}) collective-permute-start(bf16[512,512]{1,0:T(8,128)(2,1)S(1)} %head_part.3), channel_id=1, source_target_pairs={{0,2},{1,3},{2,0},{3,1},{4,6},{5,7},{6,4},{7,5},{8,10},{9,11},{10,... | collective-permute-start | bytes 1572872 | tf_op jit(solution)/shard_map/ppermute | solution.py:488
  88.0 2.4 %pieces.6.own_ref = f32[512,512]{1,0:T(8,128)S(1)} custom-call(s32[1]{0:T(128)} %get-tuple-element.71.offs_ref, s32[1]{0:T(128)} %constant.84.clone.1.subs_ref, bf16[512,512]{1,0:T(8,128)(2,1)S(1)} %finish_value.1.a_ref.x_ref, bf16[512,512]{1,0:T(8,128)(2,1)S(1)} %collective-permute-done.2.b_ref.x_ref, bf16[1,512,512]{2,1,0:T(8,128)(2,1)S(1)} %get-tuple-element.39.refs_0_, ...), custom_call_target="tpu_custom_call" | custom-call | flops 1 | bytes 1 | tf_op jit(solution)/shard_map/pieces/pallas_call | solution.py:338
  90.4 5.5 %collective-permute-done.15.moved_ref = bf16[512,512]{1,0:T(8,128)(2,1)S(1)} collective-permute-done((bf16[512,512]{1,0:T(8,128)(2,1)S(1)}, bf16[512,512]{1,0:T(8,128)(2,1)S(1)}, u32[]{:S(2)}, u32[]{:S(2)}) %collective-permute-start.15) | collective-permute-done | bytes 524320 | tf_op jit(solution)/shard_map/ppermute | solution.py:501
  96.8 1.8 %pieces.7.own_ref = f32[512,512]{1,0:T(8,128)S(1)} custom-call(s32[1]{0:T(128)} %get-tuple-element.70.offs_ref, s32[1]{0:T(128)} %constant.84.clone.1.subs_ref, bf16[512,512]{1,0:T(8,128)(2,1)S(1)} %finish_value.1.a_ref.x_ref, bf16[512,512]{1,0:T(8,128)(2,1)S(1)} %collective-permute-done.2.b_ref.x_ref, bf16[1,512,512]{2,1,0:T(8,128)(2,1)S(1)} %get-tuple-element.39.refs_0_, ...), custom_call_target="tpu_custom_call" | custom-call | flops 1 | bytes 1 | tf_op jit(solution)/shard_map/pieces/pallas_call | solution.py:338
  98.6 1.4 %collective-permute-done.22.refs_0_ = bf16[512,512]{1,0:T(8,128)(2,1)S(1)} collective-permute-done((bf16[512,512]{1,0:T(8,128)(2,1)S(1)}, bf16[512,512]{1,0:T(8,128)(2,1)S(1)}, u32[]{:S(2)}, u32[]{:S(2)}) %collective-permute-start.22) | collective-permute-done | bytes 524320 | tf_op jit(solution)/shard_map/ppermute | solution.py:488
  101.4 9.5 %collective-permute-done.21.moved_ref = bf16[512,512]{1,0:T(8,128)(2,1)S(1)} collective-permute-done((bf16[512,512]{1,0:T(8,128)(2,1)S(1)}, bf16[512,512]{1,0:T(8,128)(2,1)S(1)}, u32[]{:S(2)}, u32[]{:S(2)}) %collective-permute-start.21) | collective-permute-done | bytes 524320 | tf_op jit(solution)/shard_map/ppermute | solution.py:501
  110.8 1.3 %finish_weight.1 = f32[512,512]{1,0:T(8,128)} custom-call(bf16[512,512]{1,0:T(8,128)(2,1)S(1)} %collective-permute-done.21.moved_ref, f32[512,512]{1,0:T(8,128)S(1)} %pieces.7.own_ref), custom_call_target="tpu_custom_call" | custom-call | flops 1 | bytes 1 | tf_op jit(solution)/shard_map/finish_weight/pallas_call | solution.py:360
  112.2 1.4 %collective-permute-done.24.refs_1_ = bf16[512,512]{1,0:T(8,128)(2,1)S(1)} collective-permute-done((bf16[512,512]{1,0:T(8,128)(2,1)S(1)}, bf16[512,512]{1,0:T(8,128)(2,1)S(1)}, u32[]{:S(2)}, u32[]{:S(2)}) %collective-permute-start.24) | collective-permute-done | bytes 524320 | tf_op jit(solution)/shard_map/ppermute | solution.py:485
  113.5 1.8 %join.1 = bf16[512,1024]{1,0:T(8,128)(2,1)} custom-call(s32[1]{0:T(128)} %bitcast.par_ref, s32[1]{0:T(128)} %bitcast.2.head_ref.at_ref, bf16[512,512]{1,0:T(8,128)(2,1)S(1)} %finish_value.1.a_ref.x_ref, bf16[512,512]{1,0:T(8,128)(2,1)S(1)} %collective-permute-done.20.y_ref, bf16[2,512,512]{2,1,0:T(8,128)(2,1)S(1)} %get-tuple-element.62.w_ref, ...), custom_call_target="tpu_custom_call" | custom-call | flops 1 | bytes 1 | tf_op jit(solution)/shard_map/join/pallas_call | solution.py:462
  (78 shorter events, 17.8 us)
Async XLA Ops:
  0.6 9.7 %copy-start.10 = (bf16[512,1024]{1,0:T(8,128)(2,1)S(1)}, bf16[512,1024]{1,0:T(8,128)(2,1)}, u32[]{:S(2)}) copy-start(bf16[512,1024]{1,0:T(8,128)(2,1)} %x_ref.1) | copy-start | bytes 3145732
  0.7 12.5 %copy-start.3 = (bf16[512,512]{1,0:T(8,128)(2,1)S(1)}, bf16[512,512]{1,0:T(8,128)(2,1)}, u32[]{:S(2)}) copy-start(bf16[512,512]{1,0:T(8,128)(2,1)} %g_ref.1) | copy-start | bytes 1572868
  4.7 8.5 %copy-start = (bf16[512,512]{1,0:T(8,128)(2,1)S(1)}, bf16[512,512]{1,0:T(8,128)(2,1)}, u32[]{:S(2)}) copy-start(bf16[512,512]{1,0:T(8,128)(2,1)} %k_ref.1) | copy-start | bytes 1572868
  4.7 8.5 %copy-start.1 = (bf16[512,512]{1,0:T(8,128)(2,1)S(1)}, bf16[512,512]{1,0:T(8,128)(2,1)}, u32[]{:S(2)}) copy-start(bf16[512,512]{1,0:T(8,128)(2,1)} %q_ref.1) | copy-start | bytes 1572868
  4.7 6.7 %collective-permute-start = (bf16[2,2,128,128]{3,2,1,0:T(8,128)(2,1)}, bf16[2,2,128,128]{3,2,1,0:T(8,128)(2,1)S(1)}, u32[]{:S(2)}, u32[]{:S(2)}) collective-permute-start(bf16[2,2,128,128]{3,2,1,0:T(8,128)(2,1)} %get-tuple-element.37), channel_id=1, source_target_pairs={{0,4},{4,0},{8,12},{12,8},{16,20},{20,16},{24,28},{28,24},{1,5},{5... | collective-permute-start | bytes 393224 | tf_op jit(solution)/shard_map/ppermute | solution.py:485
  7.7 23.5 %collective-permute-start.11 = (bf16[512,512]{1,0:T(8,128)(2,1)}, bf16[512,512]{1,0:T(8,128)(2,1)}, u32[]{:S(2)}, u32[]{:S(2)}) collective-permute-start(bf16[512,512]{1,0:T(8,128)(2,1)} %refs_0_.3), channel_id=1, source_target_pairs={{0,16},{4,20},{16,24},{20,28},{24,8},{28,12},{8,0},{12,4},{1,17},{... | collective-permute-start | bytes 1572872 | tf_op jit(solution)/shard_map/ppermute | solution.py:501
  11.4 20.0 %collective-permute-start.6 = (bf16[1,512,512]{2,1,0:T(8,128)(2,1)}, bf16[1,512,512]{2,1,0:T(8,128)(2,1)S(1)}, u32[]{:S(2)}, u32[]{:S(2)}) collective-permute-start(bf16[1,512,512]{2,1,0:T(8,128)(2,1)} %get-tuple-element.51), channel_id=1, source_target_pairs={{0,4},{4,0},{8,12},{12,8},{16,20},{20,16},{24,28},{28,24},{1,5},{5... | collective-permute-start | bytes 1572872 | tf_op jit(solution)/shard_map/ppermute | solution.py:485
  13.2 4.2 %copy-start.11 = (f32[2,2,128,128]{3,2,1,0:T(8,128)S(1)}, f32[2,2,128,128]{3,2,1,0:T(8,128)}, u32[]{:S(2)}) copy-start(f32[2,2,128,128]{3,2,1,0:T(8,128)} %get-tuple-element.42.keep_ref) | copy-start | bytes 786436
  18.1 13.0 %copy-start.12 = (bf16[2,2,128,128]{3,2,1,0:T(8,128)(2,1)S(1)}, bf16[2,2,128,128]{3,2,1,0:T(8,128)(2,1)}, u32[]{:S(2)}) copy-start(bf16[2,2,128,128]{3,2,1,0:T(8,128)(2,1)} %get-tuple-element.43.near_ref) | copy-start | bytes 393220
  18.1 13.0 %all-to-all-start = ((bf16[4,2,128,128]{3,2,1,0:T(8,128)(2,1)}), bf16[4,2,128,128]{3,2,1,0:T(8,128)(2,1)S(1)}, u32[]{:S(2)}, u32[]{:S(2)}) async-start(bf16[4,2,128,128]{3,2,1,0:T(8,128)(2,1)} %offer.1), calls=%async_computation | async-start | bytes 524288 | tf_op jit(solution)/shard_map/all_to_all | solution.py:514
  23.1 13.0 %collective-permute-start.4 = (bf16[1,512,512]{2,1,0:T(8,128)(2,1)S(1)}, bf16[1,512,512]{2,1,0:T(8,128)(2,1)S(1)}, u32[]{:S(2)}, u32[]{:S(2)}) collective-permute-start(bf16[1,512,512]{2,1,0:T(8,128)(2,1)S(1)} %get-tuple-element.39.refs_0_), channel_id=1, source_target_pairs={{0,2},{1,3},{2,0},{3,1},{4,6},{5,7},{6,4},{7,5},{8,10},{9,11},{10,... | collective-permute-start | bytes 1572872 | tf_op jit(solution)/shard_map/ppermute | solution.py:488
  31.3 12.9 %collective-permute-start.12 = (bf16[512,512]{1,0:T(8,128)(2,1)}, bf16[512,512]{1,0:T(8,128)(2,1)}, u32[]{:S(2)}, u32[]{:S(2)}) collective-permute-start(bf16[512,512]{1,0:T(8,128)(2,1)} %collective-permute-done.11.refs_1_), channel_id=1, source_target_pairs={{0,16},{4,20},{16,24},{20,28},{24,8},{28,12},{8,0},{12,4},{1,17},{... | collective-permute-start | bytes 1572872 | tf_op jit(solution)/shard_map/ppermute | solution.py:501
  31.3 13.4 %collective-permute-start.3 = (bf16[1,512,512]{2,1,0:T(8,128)(2,1)S(1)}, bf16[1,512,512]{2,1,0:T(8,128)(2,1)}, u32[]{:S(2)}, u32[]{:S(2)}) collective-permute-start(bf16[1,512,512]{2,1,0:T(8,128)(2,1)S(1)} %get-tuple-element.39.refs_0_), channel_id=1, source_target_pairs={{0,1},{1,0},{2,3},{3,2},{4,5},{5,4},{6,7},{7,6},{8,9},{9,8},{10,11... | collective-permute-start | bytes 1572872 | tf_op jit(solution)/shard_map/ppermute | solution.py:488
  31.4 15.3 %collective-permute-start.8 = (bf16[1,512,512]{2,1,0:T(8,128)(2,1)S(1)}, bf16[1,512,512]{2,1,0:T(8,128)(2,1)}, u32[]{:S(2)}, u32[]{:S(2)}) collective-permute-start(bf16[1,512,512]{2,1,0:T(8,128)(2,1)S(1)} %collective-permute-done.6.refs_4_), channel_id=1, source_target_pairs={{0,2},{1,3},{2,0},{3,1},{4,6},{5,7},{6,4},{7,5},{8,10},{9,11},{10,... | collective-permute-start | bytes 1572872 | tf_op jit(solution)/shard_map/ppermute | solution.py:488
  33.0 8.4 %collective-permute-start.1 = (bf16[2,2,2,128,128]{4,3,2,1,0:T(8,128)(2,1)S(1)}, bf16[2,2,2,128,128]{4,3,2,1,0:T(8,128)(2,1)S(1)}, u32[]{:S(2)}, u32[]{:S(2)}) collective-permute-start(bf16[2,2,2,128,128]{4,3,2,1,0:T(8,128)(2,1)S(1)} %get-tuple-element.45), channel_id=1, source_target_pairs={{0,4},{4,0},{8,12},{12,8},{16,20},{20,16},{24,28},{28,24},{1,5},{5... | collective-permute-start | bytes 786440 | tf_op jit(solution)/shard_map/ppermute | solution.py:485
  36.1 20.0 %collective-permute-start.5 = (bf16[1,512,512]{2,1,0:T(8,128)(2,1)S(1)}, bf16[1,512,512]{2,1,0:T(8,128)(2,1)}, u32[]{:S(2)}, u32[]{:S(2)}) collective-permute-start(bf16[1,512,512]{2,1,0:T(8,128)(2,1)S(1)} %collective-permute-done.4.refs_2_), channel_id=1, source_target_pairs={{0,1},{1,0},{2,3},{3,2},{4,5},{5,4},{6,7},{7,6},{8,9},{9,8},{10,11... | collective-permute-start | bytes 1572872 | tf_op jit(solution)/shard_map/ppermute | solution.py:488
  41.4 14.8 %collective-permute-start.7 = (bf16[1,512,512]{2,1,0:T(8,128)(2,1)S(1)}, bf16[1,512,512]{2,1,0:T(8,128)(2,1)}, u32[]{:S(2)}, u32[]{:S(2)}) collective-permute-start(bf16[1,512,512]{2,1,0:T(8,128)(2,1)S(1)} %collective-permute-done.6.refs_4_), channel_id=1, source_target_pairs={{0,1},{1,0},{2,3},{3,2},{4,5},{5,4},{6,7},{7,6},{8,9},{9,8},{10,11... | collective-permute-start | bytes 1572872 | tf_op jit(solution)/shard_map/ppermute | solution.py:488
  44.1 14.3 %collective-permute-start.2 = (bf16[512,512]{1,0:T(8,128)(2,1)S(1)}, bf16[512,512]{1,0:T(8,128)(2,1)S(1)}, u32[]{:S(2)}, u32[]{:S(2)}) collective-permute-start(bf16[512,512]{1,0:T(8,128)(2,1)S(1)} %finish_value.1.a_ref.x_ref), channel_id=1, source_target_pairs={{0,4},{4,0},{8,12},{12,8},{16,20},{20,16},{24,28},{28,24},{1,5},{5... | collective-permute-start | bytes 1572872 | tf_op jit(solution)/shard_map/ppermute | solution.py:485
  44.7 17.1 %collective-permute-start.13 = (bf16[512,512]{1,0:T(8,128)(2,1)}, bf16[512,512]{1,0:T(8,128)(2,1)}, u32[]{:S(2)}, u32[]{:S(2)}) collective-permute-start(bf16[512,512]{1,0:T(8,128)(2,1)} %collective-permute-done.12.refs_2_), channel_id=1, source_target_pairs={{0,16},{4,20},{16,24},{20,28},{24,8},{28,12},{8,0},{12,4},{1,17},{... | collective-permute-start | bytes 1572872 | tf_op jit(solution)/shard_map/ppermute | solution.py:501
  46.7 11.8 %collective-permute-start.9 = (bf16[1,512,512]{2,1,0:T(8,128)(2,1)}, bf16[1,512,512]{2,1,0:T(8,128)(2,1)}, u32[]{:S(2)}, u32[]{:S(2)}) collective-permute-start(bf16[1,512,512]{2,1,0:T(8,128)(2,1)} %collective-permute-done.8.refs_6_), channel_id=1, source_target_pairs={{0,1},{1,0},{2,3},{3,2},{4,5},{5,4},{6,7},{7,6},{8,9},{9,8},{10,11... | collective-permute-start | bytes 1572872 | tf_op jit(solution)/shard_map/ppermute | solution.py:488
  61.8 2.0 %collective-permute-start.14 = (bf16[512,512]{1,0:T(8,128)(2,1)S(1)}, bf16[512,512]{1,0:T(8,128)(2,1)S(1)}, u32[]{:S(2)}, u32[]{:S(2)}) collective-permute-start(bf16[512,512]{1,0:T(8,128)(2,1)S(1)} %collective-permute-done.2.b_ref.x_ref), channel_id=1, source_target_pairs={{0,1},{1,0},{2,3},{3,2},{4,5},{5,4},{6,7},{7,6},{8,9},{9,8},{10,11... | collective-permute-start | bytes 1572872 | tf_op jit(solution)/shard_map/ppermute | solution.py:488
  61.9 15.0 %collective-permute-start.10 = (bf16[512,512]{1,0:T(8,128)(2,1)}, bf16[512,512]{1,0:T(8,128)(2,1)}, u32[]{:S(2)}, u32[]{:S(2)}) collective-permute-start(bf16[512,512]{1,0:T(8,128)(2,1)} %pieces.4), channel_id=1, source_target_pairs={{0,16},{4,20},{16,24},{20,28},{24,8},{28,12},{8,0},{12,4},{1,17},{... | collective-permute-start | bytes 1572872 | tf_op jit(solution)/shard_map/ppermute | solution.py:501
  63.3 17.5 %collective-permute-start.17 = (bf16[512,512]{1,0:T(8,128)(2,1)}, bf16[512,512]{1,0:T(8,128)(2,1)}, u32[]{:S(2)}, u32[]{:S(2)}) collective-permute-start(bf16[512,512]{1,0:T(8,128)(2,1)} %collective-permute-done.11.refs_1_), channel_id=1, source_target_pairs={{0,1},{1,0},{2,3},{3,2},{4,5},{5,4},{6,7},{7,6},{8,9},{9,8},{10,11... | collective-permute-start | bytes 1572872 | tf_op jit(solution)/shard_map/ppermute | solution.py:488
  63.3 18.9 %collective-permute-start.16 = (bf16[512,512]{1,0:T(8,128)(2,1)}, bf16[512,512]{1,0:T(8,128)(2,1)}, u32[]{:S(2)}, u32[]{:S(2)}) collective-permute-start(bf16[512,512]{1,0:T(8,128)(2,1)} %refs_0_.3), channel_id=1, source_target_pairs={{0,1},{1,0},{2,3},{3,2},{4,5},{5,4},{6,7},{7,6},{8,9},{9,8},{10,11... | collective-permute-start | bytes 1572872 | tf_op jit(solution)/shard_map/ppermute | solution.py:488
  63.8 18.4 %collective-permute-start.18 = (bf16[512,512]{1,0:T(8,128)(2,1)}, bf16[512,512]{1,0:T(8,128)(2,1)}, u32[]{:S(2)}, u32[]{:S(2)}) collective-permute-start(bf16[512,512]{1,0:T(8,128)(2,1)} %collective-permute-done.12.refs_2_), channel_id=1, source_target_pairs={{0,1},{1,0},{2,3},{3,2},{4,5},{5,4},{6,7},{7,6},{8,9},{9,8},{10,11... | collective-permute-start | bytes 1572872 | tf_op jit(solution)/shard_map/ppermute | solution.py:488
  63.8 18.4 %collective-permute-start.19 = (bf16[512,512]{1,0:T(8,128)(2,1)}, bf16[512,512]{1,0:T(8,128)(2,1)}, u32[]{:S(2)}, u32[]{:S(2)}) collective-permute-start(bf16[512,512]{1,0:T(8,128)(2,1)} %collective-permute-done.13.refs_3_), channel_id=1, source_target_pairs={{0,1},{1,0},{2,3},{3,2},{4,5},{5,4},{6,7},{7,6},{8,9},{9,8},{10,11... | collective-permute-start | bytes 1572872 | tf_op jit(solution)/shard_map/ppermute | solution.py:488
  76.9 9.5 %collective-permute-start.20 = (bf16[512,512]{1,0:T(8,128)(2,1)S(1)}, bf16[512,512]{1,0:T(8,128)(2,1)S(1)}, u32[]{:S(2)}, u32[]{:S(2)}) collective-permute-start(bf16[512,512]{1,0:T(8,128)(2,1)S(1)} %finish_value.1.a_ref.x_ref), channel_id=1, source_target_pairs={{0,1},{1,0},{2,3},{3,2},{4,5},{5,4},{6,7},{7,6},{8,9},{9,8},{10,11... | collective-permute-start | bytes 1572872 | tf_op jit(solution)/shard_map/ppermute | solution.py:488
  80.7 15.2 %collective-permute-start.15 = (bf16[512,512]{1,0:T(8,128)(2,1)S(1)}, bf16[512,512]{1,0:T(8,128)(2,1)S(1)}, u32[]{:S(2)}, u32[]{:S(2)}) collective-permute-start(bf16[512,512]{1,0:T(8,128)(2,1)S(1)} %add_own.2), channel_id=1, source_target_pairs={{0,16},{4,20},{16,24},{20,28},{24,8},{28,12},{8,0},{12,4},{1,17},{... | collective-permute-start | bytes 1572872 | tf_op jit(solution)/shard_map/ppermute | solution.py:501
  85.1 14.9 %collective-permute-start.22 = (bf16[512,512]{1,0:T(8,128)(2,1)S(1)}, bf16[512,512]{1,0:T(8,128)(2,1)S(1)}, u32[]{:S(2)}, u32[]{:S(2)}) collective-permute-start(bf16[512,512]{1,0:T(8,128)(2,1)S(1)} %head_part.3), channel_id=1, source_target_pairs={{0,2},{1,3},{2,0},{3,1},{4,6},{5,7},{6,4},{7,5},{8,10},{9,11},{10,... | collective-permute-start | bytes 1572872 | tf_op jit(solution)/shard_map/ppermute | solution.py:488
  87.2 25.0 %collective-permute-start.23 = (bf16[512,512]{1,0:T(8,128)(2,1)S(1)}, bf16[512,512]{1,0:T(8,128)(2,1)S(1)}, u32[]{:S(2)}, u32[]{:S(2)}) collective-permute-start(bf16[512,512]{1,0:T(8,128)(2,1)S(1)} %head_part.4), channel_id=1, source_target_pairs={{0,2},{1,3},{2,0},{3,1},{4,6},{5,7},{6,4},{7,5},{8,10},{9,11},{10,... | collective-permute-start | bytes 1572872 | tf_op jit(solution)/shard_map/ppermute | solution.py:488
  96.0 14.8 %collective-permute-start.21 = (bf16[512,512]{1,0:T(8,128)(2,1)S(1)}, bf16[512,512]{1,0:T(8,128)(2,1)S(1)}, u32[]{:S(2)}, u32[]{:S(2)}) collective-permute-start(bf16[512,512]{1,0:T(8,128)(2,1)S(1)} %add_own.3), channel_id=1, source_target_pairs={{0,16},{4,20},{16,24},{20,28},{24,8},{28,12},{8,0},{12,4},{1,17},{... | collective-permute-start | bytes 1572872 | tf_op jit(solution)/shard_map/ppermute | solution.py:501
  100.8 12.8 %collective-permute-start.24 = (bf16[512,512]{1,0:T(8,128)(2,1)S(1)}, bf16[512,512]{1,0:T(8,128)(2,1)S(1)}, u32[]{:S(2)}, u32[]{:S(2)}) collective-permute-start(bf16[512,512]{1,0:T(8,128)(2,1)S(1)} %head_part.5), channel_id=1, source_target_pairs={{0,4},{4,0},{8,12},{12,8},{16,20},{20,16},{24,28},{28,24},{1,5},{5... | collective-permute-start | bytes 1572872 | tf_op jit(solution)/shard_map/ppermute | solution.py:485
  (9 other events, 13.8 us)

commit v13 on v11

--- a/solution.py
+++ b/solution.py
@@ -19,19 +19,14 @@
     return lax.dot_general(a, b, (((ca,), (cb,)), ((), ())), preferred_element_type=F32)
 
 
-def call(kernel, vmem=16, **kw):
-    hint = pl.CostEstimate(flops=1, bytes_accessed=1, transcendentals=0)
+def call(kernel, vmem=16, flops=1, **kw):
+    hint = pl.CostEstimate(flops=flops, bytes_accessed=1, transcendentals=0)
     params = pltpu.CompilerParams(vmem_limit_bytes=vmem * 2**20)
     return pl.pallas_call(kernel, cost_estimate=hint, compiler_params=params, **kw)
 
 
 def states_kernel(par_ref, *refs):
-    arrays, (keep_ref, send_ref, near_ref), bufs, sems = (
-        refs[:4],
-        refs[4:7],
-        refs[7:11],
-        refs[11],
-    )
+    arrays, (keep_ref, send_ref), bufs, sems = refs[:4], refs[4:6], refs[6:10], refs[10]
     heads = arrays[0].shape[1] // DH
     half = heads // 2
 
@@ -55,11 +50,11 @@
             @pl.when(own)
             def _():
                 keep_ref[kind, hd % half] = s
-                near_ref[kind, hd % half] = s.astype(BF16)
+                send_ref[1, kind, hd % half] = s.astype(BF16)
 
             @pl.when(jnp.logical_not(own))
             def _():
-                send_ref[kind, hd % half] = s.astype(BF16)
+                send_ref[0, kind, hd % half] = s.astype(BF16)
 
 
 def states(par, *arrays):
@@ -70,8 +65,11 @@
         states_kernel,
         vmem=60,
         in_specs=[SMEM] + [pl.BlockSpec(memory_space=pltpu.HBM)] * 4,
-        out_specs=[VMEM] * 3,
-        out_shape=[jax.ShapeDtypeStruct(shape, d) for d in (F32, BF16, BF16)],
+        out_specs=[VMEM] * 2,
+        out_shape=[
+            jax.ShapeDtypeStruct(shape, F32),
+            jax.ShapeDtypeStruct((2, *shape), BF16),
+        ],
         scratch_shapes=[pltpu.VMEM((n, cols), BF16)] * 4
         + [pltpu.SemaphoreType.DMA((4, heads))],
         name="states",
@@ -155,7 +153,7 @@
 
 
 def offer_kernel(pair_ref, keep_ref, got_ref, out_ref):
-    sums = [(keep_ref[k] + got_ref[k].astype(F32)).astype(BF16) for k in range(2)]
+    sums = [(keep_ref[k] + got_ref[0, k].astype(F32)).astype(BF16) for k in range(2)]
     for p in range(out_ref.shape[0]):
         out_ref[p] = jnp.where(p < pair_ref[0], sums[0], sums[1])
 
@@ -170,36 +168,32 @@
     )(pair, keep, got)
 
 
-def far_kernel(pair_ref, every_ref, near_ref, out_ref, send_ref):
+def far_kernel(pair_ref, every_ref, out_ref, send_ref):
     for kind in range(2):
         total = jnp.zeros(out_ref.shape[1:], F32)
         for p in range(every_ref.shape[0]):
             reached = p > pair_ref[0] if kind == 0 else p < pair_ref[0]
             total = total + jnp.where(reached, every_ref[p].astype(F32), 0.0)
         out_ref[kind] = total
-        send_ref[0, kind] = total.astype(BF16)
-        send_ref[1, kind] = near_ref[kind]
-
-
-def far_states(pair, every, near):
+        send_ref[kind] = total.astype(BF16)
+
+
+def far_states(pair, every):
     shape = (2, *every.shape[1:])
     return call(
         far_kernel,
-        in_specs=[SMEM, VMEM, VMEM],
+        in_specs=[SMEM, VMEM],
         out_specs=[VMEM] * 2,
-        out_shape=[
-            jax.ShapeDtypeStruct(shape, F32),
-            jax.ShapeDtypeStruct((2, *shape), BF16),
-        ],
+        out_shape=[jax.ShapeDtypeStruct(shape, d) for d in (F32, BF16)],
         name="far",
-    )(pair, every, near)
+    )(pair, every)
 
 
 def entering(par, kind, hd, half, far, got, near):
     mine = par == hd // half
     i = hd % half
-    outer = jnp.where(mine, far[kind, i], got[0, kind, i].astype(F32))
-    close = jnp.where(mine, near[kind, i].astype(F32), got[1, kind, i].astype(F32))
+    outer = jnp.where(mine, far[kind, i], got[kind, i].astype(F32))
+    close = jnp.where(mine, near[0, kind, i], near[1, kind, i]).astype(F32)
     total = outer + jnp.where(par == kind, close, 0.0)
     hi = total.astype(BF16)
     return hi, (total - hi.astype(F32)).astype(BF16)
@@ -288,14 +282,12 @@
     for j, (src, dst) in enumerate(((own, x), (theirs, y))):
         pltpu.make_async_copy(src[0].at[0], dst.at[slot], sems.at[j, slot]).wait()
     total = dot(at[...], x[slot], 1, 0) + dot(bt[...], y[slot], 1, 0)
+    span = outs[0].shape[0]
     for i, out_ref in enumerate(outs):
-
-        @pl.when(step == i)
-        def _():
-            out_ref[...] = total.astype(out_ref.dtype)
-
-
-def pieces(dtype, offs, subs, a, b, own, theirs):
+        out_ref[...] = total[i * span : (i + 1) * span].astype(out_ref.dtype)
+
+
+def pieces(dtype, chains, flops, offs, subs, a, b, own, theirs):
     steps = offs.shape[0]
     count = len(own)
     _, n, width = own[0].shape
@@ -304,8 +296,9 @@
         functools.partial(piece_kernel, count),
         grid=(steps,),
         in_specs=[SMEM] * 2 + [VMEM] * 2 + [ANY] * (2 * count),
-        out_specs=[VMEM] * steps,
-        out_shape=[jax.ShapeDtypeStruct((cols, width), dtype)] * steps,
+        flops=flops,
+        out_specs=[VMEM] * chains,
+        out_shape=[jax.ShapeDtypeStruct((cols // chains, width), dtype)] * chains,
         scratch_shapes=[
             pltpu.VMEM((2, n, width), BF16),
             pltpu.VMEM((2, n, width), BF16),
@@ -317,18 +310,24 @@
     )(offs, subs, a, b, *own, *theirs)
 
 
-def weight_kernel(scale, moved_ref, own_ref, out_ref):
-    out_ref[...] = (moved_ref[...].astype(F32) + own_ref[...]).T * scale
+def weight_kernel(scale, *refs):
+    count, out_ref = len(refs) // 2, refs[-1]
+    span = refs[0].shape[0]
+    for i in range(count):
+        total = refs[i][...].astype(F32) + refs[count + i][...]
+        out_ref[:, i * span : (i + 1) * span] = total.T * scale
 
 
 def finish_weight(scale, moved, own):
+    span, width = moved[0].shape
+    count = len(moved)
     return call(
         functools.partial(weight_kernel, scale),
-        in_specs=[VMEM] * 2,
+        in_specs=[VMEM] * (2 * count),
         out_specs=VMEM,
-        out_shape=jax.ShapeDtypeStruct(moved.shape[::-1], F32),
+        out_shape=jax.ShapeDtypeStruct((width, span * count), F32),
         name="finish_weight",
-    )(moved, own)
+    )(*moved, *own)
 
 
 def add_kernel(moved_ref, own_ref, out_ref):
@@ -465,21 +464,22 @@
     def ring(x):
         return lax.ppermute(x, "ctx", moves)
 
-    keep, send, near16 = states(par, queries, keys, values, out_grad)
-    their_half = partner(send)
+    keep, send = states(par, queries, keys, values, out_grad)
+    near = partner(send)
     line = pair.astype(jnp.int32).reshape(1)
 
     per = n_ctx // n_head // 2
+    width = value_weight.shape[0]
     own, theirs = split(after(par, send), inputs, per)
     blocks = [value_weight, ring(after(value_weight, send))]
-    own, theirs = [own], [partner(after(theirs, their_half))]
-
-    offered = offer(line, keep, their_half, pairs)
+    own, theirs = [own], [partner(after(theirs, near))]
+
+    offered = offer(line, keep, near, pairs)
     every = lax.all_to_all(
         offered, "ctx", split_axis=0, concat_axis=0, axis_index_groups=lines
     )
-    far, send_far = far_states(line, every, near16)
-    ends = (far, partner(send_far), their_half)
+    far, send_far = far_states(line, every)
+    ends = (far, partner(send_far), near)
     vi, keys_too = inside(after(queries, send_far), keys, out_grad)
     theirs = [after(theirs[0], send_far)]
     mine = finish_value(factor, par, keys_too, vi, ends)
@@ -507,15 +507,18 @@
     which = jnp.asarray(order, jnp.int32)[(spot - 1 - steps) % pairs]
     offs, subs = (which // per) ^ head, which % per
 
-    def piece(dtype, step, token):
+    chains = 2
+
+    def piece(dtype, step, token, flops=1):
         at = (offs[step : step + 1], subs[step : step + 1])
-        return pieces(dtype, *at, after(mine, token), other, own, theirs)[0]
-
-    total = piece(BF16, 0, query_grad)
-    moved = ring(total)
-    other_too = across(after(other, total), 1)
-    local_part = piece(F32, 1, other_too)
-    lent.append(across(after(blocks[-1], local_part), 1))
+        vals = (after(mine, token), other, own, theirs)
+        return pieces(dtype, chains, flops, *at, *vals)
+
+    total = piece(BF16, 0, query_grad, 4 * length * cols * width)
+    moved = [ring(x) for x in total]
+    other_too = across(other, 1)
+    lent.append(across(after(blocks[-1], total[0]), 1))
+    local_part = piece(F32, 1, total[0])
 
     here = head.astype(jnp.int32).reshape(1)
     held = jnp.asarray(order, jnp.int32)[(spot - steps) % pairs]
@@ -527,24 +530,25 @@
         ]
         return sent[-1], [across(x, 2 * i + 2) for i, x in enumerate(sent)]
 
-    total = add_own(moved, local_part)
-    moved = ring(total)
     weight, borrowed = arrange(
-        per, n_head, here, held, [after(blocks[0], total)] + blocks[1:], lent
+        per, n_head, here, held, [after(blocks[0], local_part[0])] + blocks[1:], lent
     )
     token, got_other = summed_parts(other, other_too)
     token, got_mine = summed_parts(after(mine, token), mine_too)
-    for step in range(2, pairs - 1):
-        total = add_own(moved, piece(F32, step, token))
-        moved = ring(total)
-        token = total
-    local_part = piece(F32, pairs - 1, token)
+    for step in range(1, pairs - 1):
+        for i in range(chains):
+            token = add_own(moved[i], after(local_part[i], token))
+            moved[i] = ring(token)
+        local_part = piece(F32, step + 1, token)
+        token = local_part[0]
     part = head_part(
-        here, after(other, local_part), other_too, weight, borrowed, got_other
+        here, after(other, token), other_too, weight, borrowed, got_other
     )
     swapped = partner(part)
     weight_grad = finish_weight(
-        1.0 / math.sqrt(length * n_ctx), moved, after(local_part, part)
+        1.0 / math.sqrt(length * n_ctx),
+        moved,
+        [after(local_part[0], part), *local_part[1:]],
     )
     mine = after(mine, weight_grad)
     input_grad = join(

time: 136 us -> 113 us (0.83)
  waiting for transfers between devices: 54 us -> 24.3 us
  starting transfers between devices: 28.5 us -> 38.2 us
  local copies, waits for them, and re-layouts: 15.8 us -> 11.6 us
    ppermute x6 -> x9, waiting for transfers between devices: 30.9 us -> 13.5 us  [ring(): return lax.ppermute(x, 'ctx', moves)]
    ppermute x6 -> x9, starting transfers between devices: 8.64 us -> 16.9 us  [ring(): return lax.ppermute(x, 'ctx', moves)]
    all_to_all x1, waiting for transfers between devices: 14.7 us -> 6.5 us  [local(): lax.all_to_all(offered, 'ctx', split_axis=0, concat_axis=0, axis_index_gr...]
    ppermute x5, waiting for transfers between devices: 8.35 us -> 2.97 us  [partner(): return lax.ppermute(x, 'ctx', [(i, i ^ 1) for i in range(n_ctx)])]
    unnamed x40 -> x34, local copies, waits for them, and re-layouts: 13.3 us -> 9.03 us
    ppermute x14, starting transfers between devices: 6.48 us -> 8.82 us  [across(): return lax.ppermute(x, 'head', [(i, i ^ bit) for i in range(n_head)])]
    pallas_call x3, Pallas kernels: 3.27 us -> 5.34 us  [head_part(): call(part_kernel, in_specs=[SMEM] + [VMEM] * (4 + len(got)), out_specs=VM...]
  transfers between devices with their start and end apart: 26 -> 29, of which waited for: 9 -> 10; matrix products, arithmetic and copies ran while one was open for 2% -> 3% of each run, Pallas kernels for 21% -> 25%
where the time goes in v13:
time: 113 us; the launch traced here: 111 us
  starting transfers between devices  38.2 us (34%)
  Pallas kernels  35.2 us (31%)
  waiting for transfers between devices  24.3 us (22%)
  local copies, waits for them, and re-layouts  11.6 us (10%)
  between operations  1.55 us (1%)
    ppermute x9, starting transfers between devices, ring(): return lax.ppermute(x, 'ctx', moves)  16.9 us
    ppermute x9, waiting for transfers between devices, ring(): return lax.ppermute(x, 'ctx', moves)  13.5 us
    pallas_call x4, Pallas kernels, pieces(): call(functools.partial(piece_kernel, count), grid=(steps,), in_specs=[SME...  9.35 us
    unnamed x34, local copies, waits for them, and re-layouts  9.03 us
    ppermute x14, starting transfers between devices, across(): return lax.ppermute(x, 'head', [(i, i ^ bit) for i in range(n_head)])  8.82 us
    ppermute x5, starting transfers between devices, partner(): return lax.ppermute(x, 'ctx', [(i, i ^ 1) for i in range(n_ctx)])  7.46 us
    all_to_all x1, waiting for transfers between devices, local(): lax.all_to_all(offered, 'ctx', split_axis=0, concat_axis=0, axis_index_gr...  6.5 us
    pallas_call x3, Pallas kernels, head_part(): call(part_kernel, in_specs=[SMEM] + [VMEM] * (4 + len(got)), out_specs=VM...  5.34 us
  transfers between devices with their start and end apart: 29, of which 10 were waited for; matrix products, arithmetic and copies ran while one was open for 3% of the time, Pallas kernels for 25%

profile of v13, /device:TPU:0, one launch (start us, length us, event | category | flops | bytes accessed | tf_op | source)
XLA Modules:
  0.0 111.5 jit_solution(537325257567122483)
XLA Ops:
  0.7 4.0 %states.1 = (f32[2,2,128,128]{3,2,1,0:T(8,128)}, bf16[2,2,2,128,128]{4,3,2,1,0:T(8,128)(2,1)}) custom-call(s32[1]{0:T(128)} %bitcast.par_ref, bf16[512,512]{1,0:T(8,128)(2,1)} %q_ref.1, bf16[512,512]{1,0:T(8,128)(2,1)} %k_ref.1, bf16[512,512]{1,0:T(8,128)(2,1)} %v_ref, bf16[512,512]{1,0:T(8,128)(2,1)} %g_ref.1), custom_call_target="tpu_custom_call" | custom-call | flops 1 | bytes 1 | tf_op jit(solution)/shard_map/states/pallas_call | solution.py:64
  4.7 3.0 %collective-permute-start = (bf16[2,2,2,128,128]{4,3,2,1,0:T(8,128)(2,1)}, bf16[2,2,2,128,128]{4,3,2,1,0:T(8,128)(2,1)S(1)}, u32[]{:S(2)}, u32[]{:S(2)}) collective-permute-start(bf16[2,2,2,128,128]{4,3,2,1,0:T(8,128)(2,1)} %get-tuple-element.48), channel_id=1, source_target_pairs={{0,4},{4,0},{8,12},{12,8},{16,20},{20,16},{24,28},{28,24},{1,5},{5... | collective-permute-start | bytes 786440 | tf_op jit(solution)/shard_map/ppermute | solution.py:449
  7.7 2.6 %collective-permute-start.12 = (bf16[512,512]{1,0:T(8,128)(2,1)}, bf16[512,512]{1,0:T(8,128)(2,1)}, u32[]{:S(2)}, u32[]{:S(2)}) collective-permute-start(bf16[512,512]{1,0:T(8,128)(2,1)} %refs_0_.3), channel_id=1, source_target_pairs={{0,16},{4,20},{16,24},{20,28},{24,8},{28,12},{8,0},{12,4},{1,17},{... | collective-permute-start | bytes 1572872 | tf_op jit(solution)/shard_map/ppermute | solution.py:465
  11.2 3.0 %collective-permute-done.got_ref.refs_2_ = bf16[2,2,2,128,128]{4,3,2,1,0:T(8,128)(2,1)S(1)} collective-permute-done((bf16[2,2,2,128,128]{4,3,2,1,0:T(8,128)(2,1)}, bf16[2,2,2,128,128]{4,3,2,1,0:T(8,128)(2,1)S(1)}, u32[]{:S(2)}, u32[]{:S(2)}) %collective-permute-start) | collective-permute-done | bytes 262176 | tf_op jit(solution)/shard_map/ppermute | solution.py:449
  14.2 1.7 %collective-permute-start.6 = (bf16[1,512,512]{2,1,0:T(8,128)(2,1)}, bf16[1,512,512]{2,1,0:T(8,128)(2,1)S(1)}, u32[]{:S(2)}, u32[]{:S(2)}) collective-permute-start(bf16[1,512,512]{2,1,0:T(8,128)(2,1)} %get-tuple-element.61), channel_id=1, source_target_pairs={{0,4},{4,0},{8,12},{12,8},{16,20},{20,16},{24,28},{28,24},{1,5},{5... | collective-permute-start | bytes 1572872 | tf_op jit(solution)/shard_map/ppermute | solution.py:449
  16.7 5.0 %all-to-all-start = ((bf16[4,2,128,128]{3,2,1,0:T(8,128)(2,1)}), bf16[4,2,128,128]{3,2,1,0:T(8,128)(2,1)S(1)}, u32[]{:S(2)}, u32[]{:S(2)}) async-start(bf16[4,2,128,128]{3,2,1,0:T(8,128)(2,1)} %offer.1), calls=%async_computation | async-start | bytes 524288 | tf_op jit(solution)/shard_map/all_to_all | solution.py:478
  21.7 1.5 %collective-permute-start.4 = (bf16[1,512,512]{2,1,0:T(8,128)(2,1)S(1)}, bf16[1,512,512]{2,1,0:T(8,128)(2,1)S(1)}, u32[]{:S(2)}, u32[]{:S(2)}) collective-permute-start(bf16[1,512,512]{2,1,0:T(8,128)(2,1)S(1)} %get-tuple-element.59.refs_0_), channel_id=1, source_target_pairs={{0,2},{1,3},{2,0},{3,1},{4,6},{5,7},{6,4},{7,5},{8,10},{9,11},{10,... | collective-permute-start | bytes 1572872 | tf_op jit(solution)/shard_map/ppermute | solution.py:452
  23.2 6.5 %all-to-all-done.every_ref = bf16[4,2,128,128]{3,2,1,0:T(8,128)(2,1)S(1)} async-done(((bf16[4,2,128,128]{3,2,1,0:T(8,128)(2,1)}), bf16[4,2,128,128]{3,2,1,0:T(8,128)(2,1)S(1)}, u32[]{:S(2)}, u32[]{:S(2)}) %all-to-all-start) | async-done | bytes 262176 | tf_op jit(solution)/shard_map/all_to_all | solution.py:478
  31.3 1.6 %collective-permute-start.8 = (bf16[1,512,512]{2,1,0:T(8,128)(2,1)S(1)}, bf16[1,512,512]{2,1,0:T(8,128)(2,1)}, u32[]{:S(2)}, u32[]{:S(2)}) collective-permute-start(bf16[1,512,512]{2,1,0:T(8,128)(2,1)S(1)} %collective-permute-done.6.refs_4_), channel_id=1, source_target_pairs={{0,2},{1,3},{2,0},{3,1},{4,6},{5,7},{6,4},{7,5},{8,10},{9,11},{10,... | collective-permute-start | bytes 1572872 | tf_op jit(solution)/shard_map/ppermute | solution.py:452
  37.5 3.0 %inside.1 = (f32[512,512]{1,0:T(8,128)S(1)}, bf16[512,512]{1,0:T(8,128)(2,1)S(1)}) custom-call(bf16[512,512]{1,0:T(8,128)(2,1)S(1)} %copy-done, bf16[512,512]{1,0:T(8,128)(2,1)S(1)} %copy-done.2, bf16[512,512]{1,0:T(8,128)(2,1)S(1)} %copy-done.4), custom_call_target="tpu_custom_call" | custom-call | flops 1 | bytes 1 | tf_op jit(solution)/shard_map/inside/pallas_call | solution.py:144
  41.6 1.3 %collective-permute-start.2 = (bf16[512,512]{1,0:T(8,128)(2,1)S(1)}, bf16[512,512]{1,0:T(8,128)(2,1)S(1)}, u32[]{:S(2)}, u32[]{:S(2)}) collective-permute-start(bf16[512,512]{1,0:T(8,128)(2,1)S(1)} %finish_value.1.a_ref.x_ref), channel_id=1, source_target_pairs={{0,4},{4,0},{8,12},{12,8},{16,20},{20,16},{24,28},{28,24},{1,5},{5... | collective-permute-start | bytes 1572872 | tf_op jit(solution)/shard_map/ppermute | solution.py:449
  42.9 2.7 %collective-permute-start.14 = (bf16[512,512]{1,0:T(8,128)(2,1)}, bf16[512,512]{1,0:T(8,128)(2,1)}, u32[]{:S(2)}, u32[]{:S(2)}) collective-permute-start(bf16[512,512]{1,0:T(8,128)(2,1)} %collective-permute-done.13.refs_2_), channel_id=1, source_target_pairs={{0,16},{4,20},{16,24},{20,28},{24,8},{28,12},{8,0},{12,4},{1,17},{... | collective-permute-start | bytes 1572872 | tf_op jit(solution)/shard_map/ppermute | solution.py:465
  52.7 4.0 %others.1 = (bf16[512,512]{1,0:T(8,128)(2,1)}, bf16[512,512]{1,0:T(8,128)(2,1)}) custom-call(s32[1]{0:T(128)} %bitcast.par_ref, bf16[512,512]{1,0:T(8,128)(2,1)S(1)} %copy-done.1, bf16[512,512]{1,0:T(8,128)(2,1)S(1)} %copy-done.3, bf16[512,512]{1,0:T(8,128)(2,1)S(1)} %copy-done.6, bf16[512,512]{1,0:T(8,128)(2,1)S(1)} %copy-done.5, ...), custom_call_target="tpu_custom_call" | custom-call | flops 1 | bytes 1 | tf_op jit(solution)/shard_map/others/pallas_call | solution.py:243
  57.3 2.5 %pieces.4 = (bf16[256,512]{1,0:T(8,128)(2,1)S(1)}, bf16[256,512]{1,0:T(8,128)(2,1)S(1)}) custom-call(s32[1]{0:T(128)} %get-tuple-element.93.offs_ref, s32[1]{0:T(128)} %constant.84.clone.1.subs_ref, bf16[512,512]{1,0:T(8,128)(2,1)S(1)} %finish_value.1.a_ref.x_ref, bf16[512,512]{1,0:T(8,128)(2,1)S(1)} %collective-permute-done.2.b_ref.x_ref, ...), custom_call_target="tpu_custom_call" | custom-call | flops 536870912 | bytes 1 | tf_op jit(solution)/shard_map/pieces/pallas_call | solution.py:295
  63.1 2.4 %collective-permute-start.10 = (bf16[256,512]{1,0:T(8,128)(2,1)}, bf16[256,512]{1,0:T(8,128)(2,1)S(1)}, u32[]{:S(2)}, u32[]{:S(2)}) collective-permute-start(bf16[256,512]{1,0:T(8,128)(2,1)} %copy-done.14), channel_id=1, source_target_pairs={{0,16},{4,20},{16,24},{20,28},{24,8},{28,12},{8,0},{12,4},{1,17},{... | collective-permute-start | bytes 786440 | tf_op jit(solution)/shard_map/ppermute | solution.py:465
  65.5 1.6 %collective-permute-start.21 = (bf16[256,512]{1,0:T(8,128)(2,1)S(1)}, bf16[256,512]{1,0:T(8,128)(2,1)S(1)}, u32[]{:S(2)}, u32[]{:S(2)}) collective-permute-start(bf16[256,512]{1,0:T(8,128)(2,1)S(1)} %get-tuple-element.77), channel_id=1, source_target_pairs={{0,16},{4,20},{16,24},{20,28},{24,8},{28,12},{8,0},{12,4},{1,17},{... | collective-permute-start | bytes 786440 | tf_op jit(solution)/shard_map/ppermute | solution.py:465
  67.1 2.6 %pieces.5 = (f32[256,512]{1,0:T(8,128)S(1)}, f32[256,512]{1,0:T(8,128)S(1)}) custom-call(s32[1]{0:T(128)} %get-tuple-element.92.offs_ref, s32[1]{0:T(128)} %constant.84.clone.1.subs_ref, bf16[512,512]{1,0:T(8,128)(2,1)S(1)} %finish_value.1.a_ref.x_ref, bf16[512,512]{1,0:T(8,128)(2,1)S(1)} %collective-permute-done.2.b_ref.x_ref, ...), custom_call_target="tpu_custom_call" | custom-call | flops 1 | bytes 1 | tf_op jit(solution)/shard_map/pieces/pallas_call | solution.py:295
  69.7 2.2 %arrange.1 = (bf16[2,512,512]{2,1,0:T(8,128)(2,1)S(1)}, bf16[2,512,512]{2,1,0:T(8,128)(2,1)S(1)}) custom-call(s32[1]{0:T(128)} %bitcast.2.head_ref.at_ref, s32[4]{0:T(128)S(1)} %gather_fusion.1, bf16[512,512]{1,0:T(8,128)(2,1)} %refs_0_.3, bf16[512,512]{1,0:T(8,128)(2,1)} %collective-permute-done.12.refs_1_, ...), custom_call_target="tpu_custom_call" | custom-call | flops 1 | bytes 1 | tf_op jit(solution)/shard_map/arrange/pallas_call | solution.py:375
  71.9 1.8 %head_part.3 = bf16[512,512]{1,0:T(8,128)(2,1)S(1)} custom-call(s32[1]{0:T(128)S(6)} %xor.12.at_ref, bf16[512,512]{1,0:T(8,128)(2,1)S(1)} %collective-permute-done.2.b_ref.x_ref, bf16[512,512]{1,0:T(8,128)(2,1)} %collective-permute-done.11.y_ref, bf16[2,512,512]{2,1,0:T(8,128)(2,1)S(1)} %get-tuple-element.73.w_ref, ...), custom_call_target="tpu_custom_call" | custom-call | flops 1 | bytes 1 | tf_op jit(solution)/shard_map/head_part/pallas_call | solution.py:398
  73.7 1.3 %collective-permute-start.25 = (bf16[512,512]{1,0:T(8,128)(2,1)S(1)}, bf16[512,512]{1,0:T(8,128)(2,1)S(1)}, u32[]{:S(2)}, u32[]{:S(2)}) collective-permute-start(bf16[512,512]{1,0:T(8,128)(2,1)S(1)} %head_part.3), channel_id=1, source_target_pairs={{0,2},{1,3},{2,0},{3,1},{4,6},{5,7},{6,4},{7,5},{8,10},{9,11},{10,... | collective-permute-start | bytes 1572872 | tf_op jit(solution)/shard_map/ppermute | solution.py:452
  75.0 1.8 %head_part.4 = bf16[512,512]{1,0:T(8,128)(2,1)S(1)} custom-call(s32[1]{0:T(128)S(6)} %xor.12.at_ref, bf16[512,512]{1,0:T(8,128)(2,1)S(1)} %finish_value.1.a_ref.x_ref, bf16[512,512]{1,0:T(8,128)(2,1)} %collective-permute-done.19.y_ref, bf16[2,512,512]{2,1,0:T(8,128)(2,1)S(1)} %get-tuple-element.73.w_ref, bf16[2,512,512]{2,1,0:T(8,128)(2,1)S(1)} %get-tuple-element.74.wy_ref), custom_call_target="tpu_custom_call" | custom-call | flops 1 | bytes 1 | tf_op jit(solution)/shard_map/head_part/pallas_call | solution.py:398
  78.2 2.3 %collective-permute-start.23 = (bf16[256,512]{1,0:T(8,128)(2,1)S(1)}, bf16[256,512]{1,0:T(8,128)(2,1)S(1)}, u32[]{:S(2)}, u32[]{:S(2)}) collective-permute-start(bf16[256,512]{1,0:T(8,128)(2,1)S(1)} %add_own.5), channel_id=1, source_target_pairs={{0,16},{4,20},{16,24},{20,28},{24,8},{28,12},{8,0},{12,4},{1,17},{... | collective-permute-start | bytes 786440 | tf_op jit(solution)/shard_map/ppermute | solution.py:465
  80.5 2.6 %collective-permute-start.26 = (bf16[512,512]{1,0:T(8,128)(2,1)S(1)}, bf16[512,512]{1,0:T(8,128)(2,1)S(1)}, u32[]{:S(2)}, u32[]{:S(2)}) collective-permute-start(bf16[512,512]{1,0:T(8,128)(2,1)S(1)} %head_part.4), channel_id=1, source_target_pairs={{0,2},{1,3},{2,0},{3,1},{4,6},{5,7},{6,4},{7,5},{8,10},{9,11},{10,... | collective-permute-start | bytes 1572872 | tf_op jit(solution)/shard_map/ppermute | solution.py:452
  83.1 2.5 %pieces.6 = (f32[256,512]{1,0:T(8,128)S(1)}, f32[256,512]{1,0:T(8,128)S(1)}) custom-call(s32[1]{0:T(128)} %get-tuple-element.91.offs_ref, s32[1]{0:T(128)} %constant.84.clone.1.subs_ref, bf16[512,512]{1,0:T(8,128)(2,1)S(1)} %finish_value.1.a_ref.x_ref, bf16[512,512]{1,0:T(8,128)(2,1)S(1)} %collective-permute-done.2.b_ref.x_ref, ...), custom_call_target="tpu_custom_call" | custom-call | flops 1 | bytes 1 | tf_op jit(solution)/shard_map/pieces/pallas_call | solution.py:295
  85.9 3.3 %collective-permute-done.23.moved_ref = bf16[256,512]{1,0:T(8,128)(2,1)S(1)} collective-permute-done((bf16[256,512]{1,0:T(8,128)(2,1)S(1)}, bf16[256,512]{1,0:T(8,128)(2,1)S(1)}, u32[]{:S(2)}, u32[]{:S(2)}) %collective-permute-start.23) | collective-permute-done | bytes 262176 | tf_op jit(solution)/shard_map/ppermute | solution.py:465
  89.3 1.8 %pieces.7 = (f32[256,512]{1,0:T(8,128)S(1)}, f32[256,512]{1,0:T(8,128)S(1)}) custom-call(s32[1]{0:T(128)} %get-tuple-element.90.offs_ref, s32[1]{0:T(128)} %constant.84.clone.1.subs_ref, bf16[512,512]{1,0:T(8,128)(2,1)S(1)} %finish_value.1.a_ref.x_ref, bf16[512,512]{1,0:T(8,128)(2,1)S(1)} %collective-permute-done.2.b_ref.x_ref, ...), custom_call_target="tpu_custom_call" | custom-call | flops 1 | bytes 1 | tf_op jit(solution)/shard_map/pieces/pallas_call | solution.py:295
  91.1 1.8 %head_part.5 = bf16[512,512]{1,0:T(8,128)(2,1)S(1)} custom-call(s32[1]{0:T(128)} %bitcast.2.head_ref.at_ref, bf16[512,512]{1,0:T(8,128)(2,1)S(1)} %collective-permute-done.2.b_ref.x_ref, bf16[512,512]{1,0:T(8,128)(2,1)} %collective-permute-done.11.y_ref, bf16[2,512,512]{2,1,0:T(8,128)(2,1)S(1)} %get-tuple-element.73.w_ref, ...), custom_call_target="tpu_custom_call" | custom-call | flops 1 | bytes 1 | tf_op jit(solution)/shard_map/head_part/pallas_call | solution.py:398
  93.8 3.5 %collective-permute-start.24 = (bf16[256,512]{1,0:T(8,128)(2,1)S(1)}, bf16[256,512]{1,0:T(8,128)(2,1)S(1)}, u32[]{:S(2)}, u32[]{:S(2)}) collective-permute-start(bf16[256,512]{1,0:T(8,128)(2,1)S(1)} %add_own.7), channel_id=1, source_target_pairs={{0,16},{4,20},{16,24},{20,28},{24,8},{28,12},{8,0},{12,4},{1,17},{... | collective-permute-start | bytes 786440 | tf_op jit(solution)/shard_map/ppermute | solution.py:465
  97.9 6.1 %collective-permute-done.24.refs_1_ = bf16[256,512]{1,0:T(8,128)(2,1)S(1)} collective-permute-done((bf16[256,512]{1,0:T(8,128)(2,1)S(1)}, bf16[256,512]{1,0:T(8,128)(2,1)S(1)}, u32[]{:S(2)}, u32[]{:S(2)}) %collective-permute-start.24) | collective-permute-done | bytes 262176 | tf_op jit(solution)/shard_map/ppermute | solution.py:465
  104.0 3.3 %collective-permute-done.22.refs_0_ = bf16[256,512]{1,0:T(8,128)(2,1)S(1)} collective-permute-done((bf16[256,512]{1,0:T(8,128)(2,1)S(1)}, bf16[256,512]{1,0:T(8,128)(2,1)S(1)}, u32[]{:S(2)}, u32[]{:S(2)}) %collective-permute-start.22) | collective-permute-done | bytes 262176 | tf_op jit(solution)/shard_map/ppermute | solution.py:465
  107.3 1.3 %finish_weight.1 = f32[512,512]{1,0:T(8,128)} custom-call(bf16[256,512]{1,0:T(8,128)(2,1)S(1)} %collective-permute-done.22.refs_0_, bf16[256,512]{1,0:T(8,128)(2,1)S(1)} %collective-permute-done.24.refs_1_, f32[256,512]{1,0:T(8,128)S(1)} %get-tuple-element.87.refs_2_, f32[256,512]{1,0:T(8,128)S(1)} %get-tuple-element.88.refs_3_), custom_call_target="tpu_custom_call" | custom-call | flops 1 | bytes 1 | tf_op jit(solution)/shard_map/finish_weight/pallas_call | solution.py:324
  108.6 2.9 %join.1 = bf16[512,1024]{1,0:T(8,128)(2,1)} custom-call(s32[1]{0:T(128)} %bitcast.par_ref, s32[1]{0:T(128)} %bitcast.2.head_ref.at_ref, bf16[512,512]{1,0:T(8,128)(2,1)S(1)} %finish_value.1.a_ref.x_ref, bf16[512,512]{1,0:T(8,128)(2,1)} %collective-permute-done.19.y_ref, bf16[2,512,512]{2,1,0:T(8,128)(2,1)S(1)} %get-tuple-element.73.w_ref, ...), custom_call_target="tpu_custom_call" | custom-call | flops 1 | bytes 1 | tf_op jit(solution)/shard_map/join/pallas_call | solution.py:426
  (90 shorter events, 22.6 us)
Async XLA Ops:
  4.7 11.3 %copy-start.13 = (f32[2,2,128,128]{3,2,1,0:T(8,128)S(1)}, f32[2,2,128,128]{3,2,1,0:T(8,128)}, u32[]{:S(2)}) copy-start(f32[2,2,128,128]{3,2,1,0:T(8,128)} %get-tuple-element.47.keep_ref) | copy-start | bytes 786436
  4.7 9.5 %collective-permute-start = (bf16[2,2,2,128,128]{4,3,2,1,0:T(8,128)(2,1)}, bf16[2,2,2,128,128]{4,3,2,1,0:T(8,128)(2,1)S(1)}, u32[]{:S(2)}, u32[]{:S(2)}) collective-permute-start(bf16[2,2,2,128,128]{4,3,2,1,0:T(8,128)(2,1)} %get-tuple-element.48), channel_id=1, source_target_pairs={{0,4},{4,0},{8,12},{12,8},{16,20},{20,16},{24,28},{28,24},{1,5},{5... | collective-permute-start | bytes 786440 | tf_op jit(solution)/shard_map/ppermute | solution.py:449
  7.7 23.5 %collective-permute-start.12 = (bf16[512,512]{1,0:T(8,128)(2,1)}, bf16[512,512]{1,0:T(8,128)(2,1)}, u32[]{:S(2)}, u32[]{:S(2)}) collective-permute-start(bf16[512,512]{1,0:T(8,128)(2,1)} %refs_0_.3), channel_id=1, source_target_pairs={{0,16},{4,20},{16,24},{20,28},{24,8},{28,12},{8,0},{12,4},{1,17},{... | collective-permute-start | bytes 1572872 | tf_op jit(solution)/shard_map/ppermute | solution.py:465
  14.2 17.1 %collective-permute-start.6 = (bf16[1,512,512]{2,1,0:T(8,128)(2,1)}, bf16[1,512,512]{2,1,0:T(8,128)(2,1)S(1)}, u32[]{:S(2)}, u32[]{:S(2)}) collective-permute-start(bf16[1,512,512]{2,1,0:T(8,128)(2,1)} %get-tuple-element.61), channel_id=1, source_target_pairs={{0,4},{4,0},{8,12},{12,8},{16,20},{20,16},{24,28},{28,24},{1,5},{5... | collective-permute-start | bytes 1572872 | tf_op jit(solution)/shard_map/ppermute | solution.py:449
  15.9 20.5 %copy-start.2 = (bf16[512,512]{1,0:T(8,128)(2,1)S(1)}, bf16[512,512]{1,0:T(8,128)(2,1)}, u32[]{:S(2)}) copy-start(bf16[512,512]{1,0:T(8,128)(2,1)} %k_ref.1) | copy-start | bytes 1572868
  16.7 19.8 %copy-start = (bf16[512,512]{1,0:T(8,128)(2,1)S(1)}, bf16[512,512]{1,0:T(8,128)(2,1)}, u32[]{:S(2)}) copy-start(bf16[512,512]{1,0:T(8,128)(2,1)} %q_ref.1) | copy-start | bytes 1572868
  16.7 13.0 %all-to-all-start = ((bf16[4,2,128,128]{3,2,1,0:T(8,128)(2,1)}), bf16[4,2,128,128]{3,2,1,0:T(8,128)(2,1)S(1)}, u32[]{:S(2)}, u32[]{:S(2)}) async-start(bf16[4,2,128,128]{3,2,1,0:T(8,128)(2,1)} %offer.1), calls=%async_computation | async-start | bytes 524288 | tf_op jit(solution)/shard_map/all_to_all | solution.py:478
  21.7 12.3 %collective-permute-start.4 = (bf16[1,512,512]{2,1,0:T(8,128)(2,1)S(1)}, bf16[1,512,512]{2,1,0:T(8,128)(2,1)S(1)}, u32[]{:S(2)}, u32[]{:S(2)}) collective-permute-start(bf16[1,512,512]{2,1,0:T(8,128)(2,1)S(1)} %get-tuple-element.59.refs_0_), channel_id=1, source_target_pairs={{0,2},{1,3},{2,0},{3,1},{4,6},{5,7},{6,4},{7,5},{8,10},{9,11},{10,... | collective-permute-start | bytes 1572872 | tf_op jit(solution)/shard_map/ppermute | solution.py:452
  31.2 10.4 %collective-permute-start.13 = (bf16[512,512]{1,0:T(8,128)(2,1)}, bf16[512,512]{1,0:T(8,128)(2,1)}, u32[]{:S(2)}, u32[]{:S(2)}) collective-permute-start(bf16[512,512]{1,0:T(8,128)(2,1)} %collective-permute-done.12.refs_1_), channel_id=1, source_target_pairs={{0,16},{4,20},{16,24},{20,28},{24,8},{28,12},{8,0},{12,4},{1,17},{... | collective-permute-start | bytes 1572872 | tf_op jit(solution)/shard_map/ppermute | solution.py:465
  31.2 11.6 %collective-permute-start.3 = (bf16[1,512,512]{2,1,0:T(8,128)(2,1)S(1)}, bf16[1,512,512]{2,1,0:T(8,128)(2,1)S(1)}, u32[]{:S(2)}, u32[]{:S(2)}) collective-permute-start(bf16[1,512,512]{2,1,0:T(8,128)(2,1)S(1)} %get-tuple-element.59.refs_0_), channel_id=1, source_target_pairs={{0,1},{1,0},{2,3},{3,2},{4,5},{5,4},{6,7},{7,6},{8,9},{9,8},{10,11... | collective-permute-start | bytes 1572872 | tf_op jit(solution)/shard_map/ppermute | solution.py:452
  31.3 14.4 %collective-permute-start.8 = (bf16[1,512,512]{2,1,0:T(8,128)(2,1)S(1)}, bf16[1,512,512]{2,1,0:T(8,128)(2,1)}, u32[]{:S(2)}, u32[]{:S(2)}) collective-permute-start(bf16[1,512,512]{2,1,0:T(8,128)(2,1)S(1)} %collective-permute-done.6.refs_4_), channel_id=1, source_target_pairs={{0,2},{1,3},{2,0},{3,1},{4,6},{5,7},{6,4},{7,5},{8,10},{9,11},{10,... | collective-permute-start | bytes 1572872 | tf_op jit(solution)/shard_map/ppermute | solution.py:452
  34.0 12.3 %collective-permute-start.5 = (bf16[1,512,512]{2,1,0:T(8,128)(2,1)S(1)}, bf16[1,512,512]{2,1,0:T(8,128)(2,1)}, u32[]{:S(2)}, u32[]{:S(2)}) collective-permute-start(bf16[1,512,512]{2,1,0:T(8,128)(2,1)S(1)} %collective-permute-done.4.refs_2_), channel_id=1, source_target_pairs={{0,1},{1,0},{2,3},{3,2},{4,5},{5,4},{6,7},{7,6},{8,9},{9,8},{10,11... | collective-permute-start | bytes 1572872 | tf_op jit(solution)/shard_map/ppermute | solution.py:452
  34.0 6.5 %collective-permute-start.1 = (bf16[2,2,128,128]{3,2,1,0:T(8,128)(2,1)}, bf16[2,2,128,128]{3,2,1,0:T(8,128)(2,1)S(1)}, u32[]{:S(2)}, u32[]{:S(2)}) collective-permute-start(bf16[2,2,128,128]{3,2,1,0:T(8,128)(2,1)} %get-tuple-element.49), channel_id=1, source_target_pairs={{0,4},{4,0},{8,12},{12,8},{16,20},{20,16},{24,28},{28,24},{1,5},{5... | collective-permute-start | bytes 393224 | tf_op jit(solution)/shard_map/ppermute | solution.py:449
  40.5 16.2 %collective-permute-start.7 = (bf16[1,512,512]{2,1,0:T(8,128)(2,1)S(1)}, bf16[1,512,512]{2,1,0:T(8,128)(2,1)}, u32[]{:S(2)}, u32[]{:S(2)}) collective-permute-start(bf16[1,512,512]{2,1,0:T(8,128)(2,1)S(1)} %collective-permute-done.6.refs_4_), channel_id=1, source_target_pairs={{0,1},{1,0},{2,3},{3,2},{4,5},{5,4},{6,7},{7,6},{8,9},{9,8},{10,11... | collective-permute-start | bytes 1572872 | tf_op jit(solution)/shard_map/ppermute | solution.py:452
  41.6 15.2 %collective-permute-start.2 = (bf16[512,512]{1,0:T(8,128)(2,1)S(1)}, bf16[512,512]{1,0:T(8,128)(2,1)S(1)}, u32[]{:S(2)}, u32[]{:S(2)}) collective-permute-start(bf16[512,512]{1,0:T(8,128)(2,1)S(1)} %finish_value.1.a_ref.x_ref), channel_id=1, source_target_pairs={{0,4},{4,0},{8,12},{12,8},{16,20},{20,16},{24,28},{28,24},{1,5},{5... | collective-permute-start | bytes 1572872 | tf_op jit(solution)/shard_map/ppermute | solution.py:449
  42.9 17.6 %collective-permute-start.14 = (bf16[512,512]{1,0:T(8,128)(2,1)}, bf16[512,512]{1,0:T(8,128)(2,1)}, u32[]{:S(2)}, u32[]{:S(2)}) collective-permute-start(bf16[512,512]{1,0:T(8,128)(2,1)} %collective-permute-done.13.refs_2_), channel_id=1, source_target_pairs={{0,16},{4,20},{16,24},{20,28},{24,8},{28,12},{8,0},{12,4},{1,17},{... | collective-permute-start | bytes 1572872 | tf_op jit(solution)/shard_map/ppermute | solution.py:465
  45.7 11.6 %collective-permute-start.9 = (bf16[1,512,512]{2,1,0:T(8,128)(2,1)}, bf16[1,512,512]{2,1,0:T(8,128)(2,1)}, u32[]{:S(2)}, u32[]{:S(2)}) collective-permute-start(bf16[1,512,512]{2,1,0:T(8,128)(2,1)} %collective-permute-done.8.refs_6_), channel_id=1, source_target_pairs={{0,1},{1,0},{2,3},{3,2},{4,5},{5,4},{6,7},{7,6},{8,9},{9,8},{10,11... | collective-permute-start | bytes 1572872 | tf_op jit(solution)/shard_map/ppermute | solution.py:452
  46.4 14.6 %collective-permute-start.16 = (bf16[512,512]{1,0:T(8,128)(2,1)}, bf16[512,512]{1,0:T(8,128)(2,1)S(1)}, u32[]{:S(2)}, u32[]{:S(2)}) collective-permute-start(bf16[512,512]{1,0:T(8,128)(2,1)} %collective-permute-done.12.refs_1_), channel_id=1, source_target_pairs={{0,1},{1,0},{2,3},{3,2},{4,5},{5,4},{6,7},{7,6},{8,9},{9,8},{10,11... | collective-permute-start | bytes 1572872 | tf_op jit(solution)/shard_map/ppermute | solution.py:452
  56.7 6.3 %collective-permute-start.15 = (bf16[512,512]{1,0:T(8,128)(2,1)}, bf16[512,512]{1,0:T(8,128)(2,1)}, u32[]{:S(2)}, u32[]{:S(2)}) collective-permute-start(bf16[512,512]{1,0:T(8,128)(2,1)} %refs_0_.3), channel_id=1, source_target_pairs={{0,1},{1,0},{2,3},{3,2},{4,5},{5,4},{6,7},{7,6},{8,9},{9,8},{10,11... | collective-permute-start | bytes 1572872 | tf_op jit(solution)/shard_map/ppermute | solution.py:452
  56.8 8.7 %collective-permute-start.17 = (bf16[512,512]{1,0:T(8,128)(2,1)}, bf16[512,512]{1,0:T(8,128)(2,1)}, u32[]{:S(2)}, u32[]{:S(2)}) collective-permute-start(bf16[512,512]{1,0:T(8,128)(2,1)} %collective-permute-done.13.refs_2_), channel_id=1, source_target_pairs={{0,1},{1,0},{2,3},{3,2},{4,5},{5,4},{6,7},{7,6},{8,9},{9,8},{10,11... | collective-permute-start | bytes 1572872 | tf_op jit(solution)/shard_map/ppermute | solution.py:452
  60.5 9.2 %collective-permute-start.18 = (bf16[512,512]{1,0:T(8,128)(2,1)}, bf16[512,512]{1,0:T(8,128)(2,1)}, u32[]{:S(2)}, u32[]{:S(2)}) collective-permute-start(bf16[512,512]{1,0:T(8,128)(2,1)} %collective-permute-done.14.refs_3_), channel_id=1, source_target_pairs={{0,1},{1,0},{2,3},{3,2},{4,5},{5,4},{6,7},{7,6},{8,9},{9,8},{10,11... | collective-permute-start | bytes 1572872 | tf_op jit(solution)/shard_map/ppermute | solution.py:452
  60.5 11.4 %collective-permute-start.11 = (bf16[512,512]{1,0:T(8,128)(2,1)S(1)}, bf16[512,512]{1,0:T(8,128)(2,1)}, u32[]{:S(2)}, u32[]{:S(2)}) collective-permute-start(bf16[512,512]{1,0:T(8,128)(2,1)S(1)} %collective-permute-done.2.b_ref.x_ref), channel_id=1, source_target_pairs={{0,1},{1,0},{2,3},{3,2},{4,5},{5,4},{6,7},{7,6},{8,9},{9,8},{10,11... | collective-permute-start | bytes 1572872 | tf_op jit(solution)/shard_map/ppermute | solution.py:452
  61.8 13.2 %collective-permute-start.19 = (bf16[512,512]{1,0:T(8,128)(2,1)S(1)}, bf16[512,512]{1,0:T(8,128)(2,1)}, u32[]{:S(2)}, u32[]{:S(2)}) collective-permute-start(bf16[512,512]{1,0:T(8,128)(2,1)S(1)} %finish_value.1.a_ref.x_ref), channel_id=1, source_target_pairs={{0,1},{1,0},{2,3},{3,2},{4,5},{5,4},{6,7},{7,6},{8,9},{9,8},{10,11... | collective-permute-start | bytes 1572872 | tf_op jit(solution)/shard_map/ppermute | solution.py:452
  63.1 13.7 %collective-permute-start.10 = (bf16[256,512]{1,0:T(8,128)(2,1)}, bf16[256,512]{1,0:T(8,128)(2,1)S(1)}, u32[]{:S(2)}, u32[]{:S(2)}) collective-permute-start(bf16[256,512]{1,0:T(8,128)(2,1)} %copy-done.14), channel_id=1, source_target_pairs={{0,16},{4,20},{16,24},{20,28},{24,8},{28,12},{8,0},{12,4},{1,17},{... | collective-permute-start | bytes 786440 | tf_op jit(solution)/shard_map/ppermute | solution.py:465
  65.5 12.7 %collective-permute-start.21 = (bf16[256,512]{1,0:T(8,128)(2,1)S(1)}, bf16[256,512]{1,0:T(8,128)(2,1)S(1)}, u32[]{:S(2)}, u32[]{:S(2)}) collective-permute-start(bf16[256,512]{1,0:T(8,128)(2,1)S(1)} %get-tuple-element.77), channel_id=1, source_target_pairs={{0,16},{4,20},{16,24},{20,28},{24,8},{28,12},{8,0},{12,4},{1,17},{... | collective-permute-start | bytes 786440 | tf_op jit(solution)/shard_map/ppermute | solution.py:465
  73.7 17.4 %collective-permute-start.25 = (bf16[512,512]{1,0:T(8,128)(2,1)S(1)}, bf16[512,512]{1,0:T(8,128)(2,1)S(1)}, u32[]{:S(2)}, u32[]{:S(2)}) collective-permute-start(bf16[512,512]{1,0:T(8,128)(2,1)S(1)} %head_part.3), channel_id=1, source_target_pairs={{0,2},{1,3},{2,0},{3,1},{4,6},{5,7},{6,4},{7,5},{8,10},{9,11},{10,... | collective-permute-start | bytes 1572872 | tf_op jit(solution)/shard_map/ppermute | solution.py:452
  76.8 9.1 %collective-permute-start.20 = (bf16[256,512]{1,0:T(8,128)(2,1)S(1)}, bf16[256,512]{1,0:T(8,128)(2,1)S(1)}, u32[]{:S(2)}, u32[]{:S(2)}) collective-permute-start(bf16[256,512]{1,0:T(8,128)(2,1)S(1)} %add_own.4), channel_id=1, source_target_pairs={{0,16},{4,20},{16,24},{20,28},{24,8},{28,12},{8,0},{12,4},{1,17},{... | collective-permute-start | bytes 786440 | tf_op jit(solution)/shard_map/ppermute | solution.py:465
  78.2 11.0 %collective-permute-start.23 = (bf16[256,512]{1,0:T(8,128)(2,1)S(1)}, bf16[256,512]{1,0:T(8,128)(2,1)S(1)}, u32[]{:S(2)}, u32[]{:S(2)}) collective-permute-start(bf16[256,512]{1,0:T(8,128)(2,1)S(1)} %add_own.5), channel_id=1, source_target_pairs={{0,16},{4,20},{16,24},{20,28},{24,8},{28,12},{8,0},{12,4},{1,17},{... | collective-permute-start | bytes 786440 | tf_op jit(solution)/shard_map/ppermute | solution.py:465
  80.5 28.1 %collective-permute-start.26 = (bf16[512,512]{1,0:T(8,128)(2,1)S(1)}, bf16[512,512]{1,0:T(8,128)(2,1)S(1)}, u32[]{:S(2)}, u32[]{:S(2)}) collective-permute-start(bf16[512,512]{1,0:T(8,128)(2,1)S(1)} %head_part.4), channel_id=1, source_target_pairs={{0,2},{1,3},{2,0},{3,1},{4,6},{5,7},{6,4},{7,5},{8,10},{9,11},{10,... | collective-permute-start | bytes 1572872 | tf_op jit(solution)/shard_map/ppermute | solution.py:452
  92.9 15.7 %collective-permute-start.27 = (bf16[512,512]{1,0:T(8,128)(2,1)S(1)}, bf16[512,512]{1,0:T(8,128)(2,1)S(1)}, u32[]{:S(2)}, u32[]{:S(2)}) collective-permute-start(bf16[512,512]{1,0:T(8,128)(2,1)S(1)} %head_part.5), channel_id=1, source_target_pairs={{0,4},{4,0},{8,12},{12,8},{16,20},{20,16},{24,28},{28,24},{1,5},{5... | collective-permute-start | bytes 1572872 | tf_op jit(solution)/shard_map/ppermute | solution.py:449
  93.8 10.2 %collective-permute-start.24 = (bf16[256,512]{1,0:T(8,128)(2,1)S(1)}, bf16[256,512]{1,0:T(8,128)(2,1)S(1)}, u32[]{:S(2)}, u32[]{:S(2)}) collective-permute-start(bf16[256,512]{1,0:T(8,128)(2,1)S(1)} %add_own.7), channel_id=1, source_target_pairs={{0,16},{4,20},{16,24},{20,28},{24,8},{28,12},{8,0},{12,4},{1,17},{... | collective-permute-start | bytes 786440 | tf_op jit(solution)/shard_map/ppermute | solution.py:465
  97.2 10.0 %collective-permute-start.22 = (bf16[256,512]{1,0:T(8,128)(2,1)S(1)}, bf16[256,512]{1,0:T(8,128)(2,1)S(1)}, u32[]{:S(2)}, u32[]{:S(2)}) collective-permute-start(bf16[256,512]{1,0:T(8,128)(2,1)S(1)} %add_own.6), channel_id=1, source_target_pairs={{0,16},{4,20},{16,24},{20,28},{24,8},{28,12},{8,0},{12,4},{1,17},{... | collective-permute-start | bytes 786440 | tf_op jit(solution)/shard_map/ppermute | solution.py:465
  (14 other events, 29.5 us)

commit v14 on v13

--- a/solution.py
+++ b/solution.py
@@ -50,11 +50,14 @@
             @pl.when(own)
             def _():
                 keep_ref[kind, hd % half] = s
-                send_ref[1, kind, hd % half] = s.astype(BF16)
+
+            @pl.when(own & (par_ref[0] != kind))
+            def _():
+                send_ref[2, hd % half] = s.astype(BF16)
 
             @pl.when(jnp.logical_not(own))
             def _():
-                send_ref[0, kind, hd % half] = s.astype(BF16)
+                send_ref[kind, hd % half] = s.astype(BF16)
 
 
 def states(par, *arrays):
@@ -68,7 +71,7 @@
         out_specs=[VMEM] * 2,
         out_shape=[
             jax.ShapeDtypeStruct(shape, F32),
-            jax.ShapeDtypeStruct((2, *shape), BF16),
+            jax.ShapeDtypeStruct((3, *shape[1:]), BF16),
         ],
         scratch_shapes=[pltpu.VMEM((n, cols), BF16)] * 4
         + [pltpu.SemaphoreType.DMA((4, heads))],
@@ -153,7 +156,7 @@
 
 
 def offer_kernel(pair_ref, keep_ref, got_ref, out_ref):
-    sums = [(keep_ref[k] + got_ref[0, k].astype(F32)).astype(BF16) for k in range(2)]
+    sums = [(keep_ref[k] + got_ref[k].astype(F32)).astype(BF16) for k in range(2)]
     for p in range(out_ref.shape[0]):
         out_ref[p] = jnp.where(p < pair_ref[0], sums[0], sums[1])
 
@@ -193,7 +196,7 @@
     mine = par == hd // half
     i = hd % half
     outer = jnp.where(mine, far[kind, i], got[kind, i].astype(F32))
-    close = jnp.where(mine, near[0, kind, i], near[1, kind, i]).astype(F32)
+    close = jnp.where(mine, near[kind, i], near[2, i]).astype(F32)
     total = outer + jnp.where(par == kind, close, 0.0)
     hi = total.astype(BF16)
     return hi, (total - hi.astype(F32)).astype(BF16)
@@ -250,64 +253,52 @@
     )(par, q, k, v, g, *ends)
 
 
-def piece_kernel(count, offs_ref, subs_ref, a_ref, b_ref, *refs):
+def line_at(order, place):
+    place = lax.rem(place + 2 * len(order), len(order))
+    line = jnp.int32(order[0])
+    for i, p in enumerate(order[1:], 1):
+        line = jnp.where(place == i, p, line)
+    return line
+
+
+def piece_kernel(order, per, step, count, spot_ref, head_ref, a_ref, b_ref, *refs):
     own, theirs = refs[:count], refs[count : 2 * count]
     outs, (x, y, at, bt, sems) = refs[2 * count : -5], refs[-5:]
-    step, steps = pl.program_id(0), pl.num_programs(0)
-    slot = lax.rem(step, 2)
-
-    def fetch(k, to):
-        for i in range(count):
-
-            @pl.when(offs_ref[k] == i)
-            def _():
-                for j, (src, dst) in enumerate(((own, x), (theirs, y))):
-                    pltpu.make_async_copy(
-                        src[i].at[subs_ref[k]], dst.at[to], sems.at[j, to]
-                    ).start()
-
-    @pl.when(step == 0)
-    def _():
-        fetch(0, 0)
-
-    @pl.when(step + 1 < steps)
-    def _():
-        fetch(step + 1, 1 - slot)
-
-    @pl.when(step == 0)
-    def _():
-        at[...] = a_ref[...].T
-        bt[...] = b_ref[...].T
-
+    line = line_at(order, spot_ref[0] - 1 - step)
+    off, sub = lax.div(line, per) ^ head_ref[0], lax.rem(line, per)
+
+    for i in range(count):
+
+        @pl.when(off == i)
+        def _():
+            for j, (src, dst) in enumerate(((own, x), (theirs, y))):
+                pltpu.make_async_copy(src[i].at[sub], dst, sems.at[j]).start()
+
+    at[...] = a_ref[...].T
+    bt[...] = b_ref[...].T
     for j, (src, dst) in enumerate(((own, x), (theirs, y))):
-        pltpu.make_async_copy(src[0].at[0], dst.at[slot], sems.at[j, slot]).wait()
-    total = dot(at[...], x[slot], 1, 0) + dot(bt[...], y[slot], 1, 0)
+        pltpu.make_async_copy(src[0].at[0], dst, sems.at[j]).wait()
+    total = dot(at[...], x[...], 1, 0) + dot(bt[...], y[...], 1, 0)
     span = outs[0].shape[0]
     for i, out_ref in enumerate(outs):
         out_ref[...] = total[i * span : (i + 1) * span].astype(out_ref.dtype)
 
 
-def pieces(dtype, chains, flops, offs, subs, a, b, own, theirs):
-    steps = offs.shape[0]
+def pieces(dtype, chains, flops, order, per, step, spot, head, a, b, own, theirs):
     count = len(own)
     _, n, width = own[0].shape
     cols = a.shape[1]
     return call(
-        functools.partial(piece_kernel, count),
-        grid=(steps,),
+        functools.partial(piece_kernel, order, per, step, count),
+        flops=flops,
         in_specs=[SMEM] * 2 + [VMEM] * 2 + [ANY] * (2 * count),
-        flops=flops,
         out_specs=[VMEM] * chains,
         out_shape=[jax.ShapeDtypeStruct((cols // chains, width), dtype)] * chains,
-        scratch_shapes=[
-            pltpu.VMEM((2, n, width), BF16),
-            pltpu.VMEM((2, n, width), BF16),
-            pltpu.VMEM((cols, n), BF16),
-            pltpu.VMEM((cols, n), BF16),
-            pltpu.SemaphoreType.DMA((2, 2)),
-        ],
+        scratch_shapes=[pltpu.VMEM((n, width), BF16)] * 2
+        + [pltpu.VMEM((cols, n), BF16)] * 2
+        + [pltpu.SemaphoreType.DMA((2,))],
         name="pieces",
-    )(offs, subs, a, b, *own, *theirs)
+    )(spot, head, a, b, *own, *theirs)
 
 
 def weight_kernel(scale, *refs):
@@ -344,19 +335,20 @@
     )(moved, own)
 
 
-def arrange_kernel(per, head_ref, which_ref, *refs):
-    count = which_ref.shape[0]
+def arrange_kernel(order, per, head_ref, spot_ref, *refs):
+    count = len(order)
     outs, sems = refs[-3:-1], refs[-1]
     rows = refs[0].shape[0]
 
     def copies(s):
-        p = which_ref[s]
-        at = (p // per // 2, pl.ds((p % per) * rows, rows))
+        p = line_at(order, spot_ref[0] - s)
+        head, sub = lax.div(p, per), lax.rem(p, per)
+        at = (lax.div(head, 2), pl.ds(sub * rows, rows))
         pair = [
             pltpu.make_async_copy(refs[j * count + s], outs[j].at[at], sems.at[j, s])
             for j in range(2)
         ]
-        return pair, (p // per) % 2 == head_ref[0] % 2
+        return pair, lax.rem(head, 2) == lax.rem(head_ref[0], 2)
 
     for act in ("start", "wait"):
         for s in range(count):
@@ -368,18 +360,18 @@
                     getattr(c, act)()
 
 
-def arrange(per, n_head, head, which, blocks, lent):
+def arrange(order, per, n_head, head, spot, blocks, lent):
     rows, cols = blocks[0].shape
     count = len(blocks)
     out = jax.ShapeDtypeStruct((n_head // 2, per * rows, cols), BF16)
     return call(
-        functools.partial(arrange_kernel, per),
+        functools.partial(arrange_kernel, order, per),
         in_specs=[SMEM] * 2 + [ANY] * (2 * count),
         out_specs=[VMEM] * 2,
         out_shape=[out] * 2,
         scratch_shapes=[pltpu.SemaphoreType.DMA((2, count))],
         name="arrange",
-    )(head, which, *blocks, *lent)
+    )(head, spot, *blocks, *lent)
 
 
 def block_product(at_ref, x_ref, y_ref, w_ref, wy_ref):
@@ -458,8 +450,8 @@
         for i in range(pairs)
         for k in range(2)
     ]
-    spot = jnp.asarray(place, jnp.int32)[pair]
-    steps = jnp.arange(pairs, dtype=jnp.int32)
+    here = head.astype(jnp.int32).reshape(1)
+    spot = line_at(place, pair.astype(jnp.int32)).reshape(1)
 
     def ring(x):
         return lax.ppermute(x, "ctx", moves)
@@ -504,15 +496,12 @@
     own = [own[offsets.index(i)] for i in range(n_head)]
     theirs = [theirs[offsets.index(i)] for i in range(n_head)]
 
-    which = jnp.asarray(order, jnp.int32)[(spot - 1 - steps) % pairs]
-    offs, subs = (which // per) ^ head, which % per
 
     chains = 2
 
     def piece(dtype, step, token, flops=1):
-        at = (offs[step : step + 1], subs[step : step + 1])
-        vals = (after(mine, token), other, own, theirs)
-        return pieces(dtype, chains, flops, *at, *vals)
+        vals = (spot, here, after(mine, token), other, own, theirs)
+        return pieces(dtype, chains, flops, order, per, step, *vals)
 
     total = piece(BF16, 0, query_grad, 4 * length * cols * width)
     moved = [ring(x) for x in total]
@@ -520,8 +509,6 @@
     lent.append(across(after(blocks[-1], total[0]), 1))
     local_part = piece(F32, 1, total[0])
 
-    here = head.astype(jnp.int32).reshape(1)
-    held = jnp.asarray(order, jnp.int32)[(spot - steps) % pairs]
 
     def summed_parts(x, y):
         sent = [
@@ -530,26 +517,26 @@
         ]
         return sent[-1], [across(x, 2 * i + 2) for i, x in enumerate(sent)]
 
-    weight, borrowed = arrange(
-        per, n_head, here, held, [after(blocks[0], local_part[0])] + blocks[1:], lent
-    )
+    held = [after(blocks[0], local_part[0])] + blocks[1:]
+    weight, borrowed = arrange(order, per, n_head, here, spot, held, lent)
     token, got_other = summed_parts(other, other_too)
     token, got_mine = summed_parts(after(mine, token), mine_too)
+    part = None
     for step in range(1, pairs - 1):
+        if step == pairs - 2:
+            last = piece(F32, pairs - 1, token)
+            token = last[0]
         for i in range(chains):
+            if step == pairs - 2 and i == chains - 1:
+                lead = (here, after(other, token), other_too, weight, borrowed)
+                token = part = head_part(*lead, got_other)
             token = add_own(moved[i], after(local_part[i], token))
             moved[i] = ring(token)
-        local_part = piece(F32, step + 1, token)
-        token = local_part[0]
-    part = head_part(
-        here, after(other, token), other_too, weight, borrowed, got_other
-    )
+        if step < pairs - 2:
+            local_part = piece(F32, step + 1, token)
+            token = local_part[0]
     swapped = partner(part)
-    weight_grad = finish_weight(
-        1.0 / math.sqrt(length * n_ctx),
-        moved,
-        [after(local_part[0], part), *local_part[1:]],
-    )
+    weight_grad = finish_weight(1.0 / math.sqrt(length * n_ctx), moved, last)
     mine = after(mine, weight_grad)
     input_grad = join(
         par, here, per, mine, mine_too, weight, borrowed, got_mine, swapped

time: 113 us -> 103 us (0.912)
  Pallas kernels: 35.2 us -> 26.1 us
  local copies, waits for them, and re-layouts: 11.6 us -> 7.77 us
  waiting for transfers between devices: 24.3 us -> 27.9 us
  starting transfers between devices: 38.2 us -> 39.9 us
    pallas_call x5, Pallas kernels: 11.5 us -> 7.17 us  [the longest x4 5.88 us: pieces(): call(functools.partial(piece_kernel, order, per, step, count), flops=flop...]
    ppermute x14, waiting for transfers between devices: 1.35 us -> 5.52 us  [across(): return lax.ppermute(x, 'head', [(i, i ^ bit) for i in range(n_head)])]
    ppermute x9, starting transfers between devices: 16.9 us -> 20.9 us  [ring(): return lax.ppermute(x, 'ctx', moves)]
    pallas_call x3, Pallas kernels: 5.34 us -> 2.23 us  [head_part(): call(part_kernel, in_specs=[SMEM] + [VMEM] * (4 + len(got)), out_specs=VM...]
    gather x2 -> x0, local copies, waits for them, and re-layouts: 1.28 us -> none  [the longest x1 0.64 us: local(): which = jnp.asarray(order, jnp.int32)[(spot - 1 - steps) % pairs]]
    ppermute x14, starting transfers between devices: 8.82 us -> 7.54 us  [across(): return lax.ppermute(x, 'head', [(i, i ^ bit) for i in range(n_head)])]
    unnamed x34 -> x30, local copies, waits for them, and re-layouts: 9.03 us -> 7.77 us
  transfers between devices with their start and end apart: 29 -> 29, of which waited for: 10 -> 10; matrix products, arithmetic and copies ran while one was open for 3% -> 0% of each run, Pallas kernels for 25% -> 20%
where the time goes in v14:
time: 103 us
  starting transfers between devices  39.9 us (39%)
  waiting for transfers between devices  27.9 us (27%)
  Pallas kernels  26.1 us (25%)
  local copies, waits for them, and re-layouts  7.77 us (8%)
    ppermute x9, starting transfers between devices, ring(): return lax.ppermute(x, 'ctx', moves)  20.9 us
    ppermute x9, waiting for transfers between devices, ring(): return lax.ppermute(x, 'ctx', moves)  12.5 us
    unnamed x30, local copies, waits for them, and re-layouts  7.77 us
    ppermute x14, starting transfers between devices, across(): return lax.ppermute(x, 'head', [(i, i ^ bit) for i in range(n_head)])  7.54 us
    all_to_all x1, waiting for transfers between devices, local(): lax.all_to_all(offered, 'ctx', split_axis=0, concat_axis=0, axis_index_gr...  6.98 us
    ppermute x5, starting transfers between devices, partner(): return lax.ppermute(x, 'ctx', [(i, i ^ 1) for i in range(n_ctx)])  6.47 us
    pallas_call x4, Pallas kernels, pieces(): call(functools.partial(piece_kernel, order, per, step, count), flops=flop...  5.88 us
    ppermute x14, waiting for transfers between devices, across(): return lax.ppermute(x, 'head', [(i, i ^ bit) for i in range(n_head)])  5.52 us
  transfers between devices with their start and end apart: 29, of which 10 were waited for; matrix products, arithmetic and copies ran while one was open for 0% of the time, Pallas kernels for 20%

profile of v14, /device:TPU:0, one launch (start us, length us, event | category | flops | bytes accessed | tf_op | source)
XLA Modules:
  0.0 102.6 jit_solution(12105477564120040291)
XLA Ops:
  0.7 4.0 %states.1 = (f32[2,2,128,128]{3,2,1,0:T(8,128)}, bf16[3,2,128,128]{3,2,1,0:T(8,128)(2,1)}) custom-call(s32[1]{0:T(128)} %bitcast.par_ref, bf16[512,512]{1,0:T(8,128)(2,1)} %q_ref.1, bf16[512,512]{1,0:T(8,128)(2,1)} %k_ref.1, bf16[512,512]{1,0:T(8,128)(2,1)} %v_ref, bf16[512,512]{1,0:T(8,128)(2,1)} %g_ref.1), custom_call_target="tpu_custom_call" | custom-call | flops 1 | bytes 1 | tf_op jit(solution)/shard_map/states/pallas_call | solution.py:67
  4.7 3.0 %collective-permute-start = (bf16[3,2,128,128]{3,2,1,0:T(8,128)(2,1)}, bf16[3,2,128,128]{3,2,1,0:T(8,128)(2,1)S(1)}, u32[]{:S(2)}, u32[]{:S(2)}) collective-permute-start(bf16[3,2,128,128]{3,2,1,0:T(8,128)(2,1)} %get-tuple-element.48), channel_id=1, source_target_pairs={{0,4},{4,0},{8,12},{12,8},{16,20},{20,16},{24,28},{28,24},{1,5},{5... | collective-permute-start | bytes 589832 | tf_op jit(solution)/shard_map/ppermute | solution.py:441
  7.7 2.6 %collective-permute-start.12 = (bf16[512,512]{1,0:T(8,128)(2,1)}, bf16[512,512]{1,0:T(8,128)(2,1)}, u32[]{:S(2)}, u32[]{:S(2)}) collective-permute-start(bf16[512,512]{1,0:T(8,128)(2,1)} %refs_0_.3), channel_id=1, source_target_pairs={{0,16},{4,20},{16,24},{20,28},{24,8},{28,12},{8,0},{12,4},{1,17},{... | collective-permute-start | bytes 1572872 | tf_op jit(solution)/shard_map/ppermute | solution.py:457
  11.2 1.6 %collective-permute-done.got_ref.refs_2_ = bf16[3,2,128,128]{3,2,1,0:T(8,128)(2,1)S(1)} collective-permute-done((bf16[3,2,128,128]{3,2,1,0:T(8,128)(2,1)}, bf16[3,2,128,128]{3,2,1,0:T(8,128)(2,1)S(1)}, u32[]{:S(2)}, u32[]{:S(2)}) %collective-permute-start) | collective-permute-done | bytes 196640 | tf_op jit(solution)/shard_map/ppermute | solution.py:441
  12.8 1.7 %collective-permute-start.6 = (bf16[1,512,512]{2,1,0:T(8,128)(2,1)}, bf16[1,512,512]{2,1,0:T(8,128)(2,1)S(1)}, u32[]{:S(2)}, u32[]{:S(2)}) collective-permute-start(bf16[1,512,512]{2,1,0:T(8,128)(2,1)} %get-tuple-element.61), channel_id=1, source_target_pairs={{0,4},{4,0},{8,12},{12,8},{16,20},{20,16},{24,28},{28,24},{1,5},{5... | collective-permute-start | bytes 1572872 | tf_op jit(solution)/shard_map/ppermute | solution.py:441
  15.3 5.0 %all-to-all-start = ((bf16[4,2,128,128]{3,2,1,0:T(8,128)(2,1)}), bf16[4,2,128,128]{3,2,1,0:T(8,128)(2,1)S(1)}, u32[]{:S(2)}, u32[]{:S(2)}) async-start(bf16[4,2,128,128]{3,2,1,0:T(8,128)(2,1)} %offer.1), calls=%async_computation | async-start | bytes 524288 | tf_op jit(solution)/shard_map/all_to_all | solution.py:470
  20.3 1.5 %collective-permute-start.4 = (bf16[1,512,512]{2,1,0:T(8,128)(2,1)S(1)}, bf16[1,512,512]{2,1,0:T(8,128)(2,1)S(1)}, u32[]{:S(2)}, u32[]{:S(2)}) collective-permute-start(bf16[1,512,512]{2,1,0:T(8,128)(2,1)S(1)} %get-tuple-element.59.refs_0_), channel_id=1, source_target_pairs={{0,2},{1,3},{2,0},{3,1},{4,6},{5,7},{6,4},{7,5},{8,10},{9,11},{10,... | collective-permute-start | bytes 1572872 | tf_op jit(solution)/shard_map/ppermute | solution.py:444
  21.8 7.0 %all-to-all-done.every_ref = bf16[4,2,128,128]{3,2,1,0:T(8,128)(2,1)S(1)} async-done(((bf16[4,2,128,128]{3,2,1,0:T(8,128)(2,1)}), bf16[4,2,128,128]{3,2,1,0:T(8,128)(2,1)S(1)}, u32[]{:S(2)}, u32[]{:S(2)}) %all-to-all-start) | async-done | bytes 262176 | tf_op jit(solution)/shard_map/all_to_all | solution.py:470
  29.9 1.5 %collective-permute-start.8 = (bf16[1,512,512]{2,1,0:T(8,128)(2,1)S(1)}, bf16[1,512,512]{2,1,0:T(8,128)(2,1)S(1)}, u32[]{:S(2)}, u32[]{:S(2)}) collective-permute-start(bf16[1,512,512]{2,1,0:T(8,128)(2,1)S(1)} %collective-permute-done.6.refs_4_), channel_id=1, source_target_pairs={{0,2},{1,3},{2,0},{3,1},{4,6},{5,7},{6,4},{7,5},{8,10},{9,11},{10,... | collective-permute-start | bytes 1572872 | tf_op jit(solution)/shard_map/ppermute | solution.py:444
  31.4 3.8 %collective-permute-done.4.refs_2_ = bf16[1,512,512]{2,1,0:T(8,128)(2,1)S(1)} collective-permute-done((bf16[1,512,512]{2,1,0:T(8,128)(2,1)S(1)}, bf16[1,512,512]{2,1,0:T(8,128)(2,1)S(1)}, u32[]{:S(2)}, u32[]{:S(2)}) %collective-permute-start.4) | collective-permute-done | bytes 524320 | tf_op jit(solution)/shard_map/ppermute | solution.py:444
  36.8 3.0 %inside.1 = (f32[512,512]{1,0:T(8,128)S(1)}, bf16[512,512]{1,0:T(8,128)(2,1)S(1)}) custom-call(bf16[512,512]{1,0:T(8,128)(2,1)S(1)} %copy-done.4, bf16[512,512]{1,0:T(8,128)(2,1)S(1)} %copy-done.6, bf16[512,512]{1,0:T(8,128)(2,1)S(1)} %copy-done.8), custom_call_target="tpu_custom_call" | custom-call | flops 1 | bytes 1 | tf_op jit(solution)/shard_map/inside/pallas_call | solution.py:147
  39.8 1.3 %collective-permute-done.1.refs_1_ = bf16[2,2,128,128]{3,2,1,0:T(8,128)(2,1)S(1)} collective-permute-done((bf16[2,2,128,128]{3,2,1,0:T(8,128)(2,1)S(1)}, bf16[2,2,128,128]{3,2,1,0:T(8,128)(2,1)S(1)}, u32[]{:S(2)}, u32[]{:S(2)}) %collective-permute-start.1) | collective-permute-done | bytes 131104 | tf_op jit(solution)/shard_map/ppermute | solution.py:441
  42.2 1.7 %collective-permute-done.8.refs_6_ = bf16[1,512,512]{2,1,0:T(8,128)(2,1)S(1)} collective-permute-done((bf16[1,512,512]{2,1,0:T(8,128)(2,1)S(1)}, bf16[1,512,512]{2,1,0:T(8,128)(2,1)S(1)}, u32[]{:S(2)}, u32[]{:S(2)}) %collective-permute-start.8) | collective-permute-done | bytes 524320 | tf_op jit(solution)/shard_map/ppermute | solution.py:444
  44.7 2.6 %collective-permute-start.14 = (bf16[512,512]{1,0:T(8,128)(2,1)}, bf16[512,512]{1,0:T(8,128)(2,1)}, u32[]{:S(2)}, u32[]{:S(2)}) collective-permute-start(bf16[512,512]{1,0:T(8,128)(2,1)} %collective-permute-done.13.refs_2_), channel_id=1, source_target_pairs={{0,16},{4,20},{16,24},{20,28},{24,8},{28,12},{8,0},{12,4},{1,17},{... | collective-permute-start | bytes 1572872 | tf_op jit(solution)/shard_map/ppermute | solution.py:457
  53.5 4.1 %others.1 = (bf16[512,512]{1,0:T(8,128)(2,1)}, bf16[512,512]{1,0:T(8,128)(2,1)}) custom-call(s32[1]{0:T(128)} %bitcast.par_ref, bf16[512,512]{1,0:T(8,128)(2,1)S(1)} %copy-done.5, bf16[512,512]{1,0:T(8,128)(2,1)S(1)} %copy-done.7, bf16[512,512]{1,0:T(8,128)(2,1)S(1)} %copy-done.10, bf16[512,512]{1,0:T(8,128)(2,1)S(1)} %copy-done.9, ...), custom_call_target="tpu_custom_call" | custom-call | flops 1 | bytes 1 | tf_op jit(solution)/shard_map/others/pallas_call | solution.py:246
  58.1 1.8 %pieces.4 = (bf16[256,512]{1,0:T(8,128)(2,1)S(1)}, bf16[256,512]{1,0:T(8,128)(2,1)S(1)}) custom-call(s32[1]{0:T(128)} %bitcast.3.spot_ref, s32[1]{0:T(128)} %bitcast.2.head_ref.at_ref, bf16[512,512]{1,0:T(8,128)(2,1)S(1)} %finish_value.1.a_ref.x_ref, bf16[512,512]{1,0:T(8,128)(2,1)S(1)} %collective-permute-done.2.b_ref.x_ref, ...), custom_call_target="tpu_custom_call" | custom-call | flops 536870912 | bytes 1 | tf_op jit(solution)/shard_map/pieces/pallas_call | solution.py:291
  60.6 1.8 %pieces.5 = (f32[256,512]{1,0:T(8,128)S(1)}, f32[256,512]{1,0:T(8,128)S(1)}) custom-call(s32[1]{0:T(128)} %bitcast.3.spot_ref, s32[1]{0:T(128)} %bitcast.2.head_ref.at_ref, bf16[512,512]{1,0:T(8,128)(2,1)S(1)} %finish_value.1.a_ref.x_ref, bf16[512,512]{1,0:T(8,128)(2,1)S(1)} %collective-permute-done.2.b_ref.x_ref, ...), custom_call_target="tpu_custom_call" | custom-call | flops 1 | bytes 1 | tf_op jit(solution)/shard_map/pieces/pallas_call | solution.py:291
  62.4 2.9 %collective-permute-start.10 = (bf16[256,512]{1,0:T(8,128)(2,1)S(1)}, bf16[256,512]{1,0:T(8,128)(2,1)S(1)}, u32[]{:S(2)}, u32[]{:S(2)}) collective-permute-start(bf16[256,512]{1,0:T(8,128)(2,1)S(1)} %get-tuple-element.63), channel_id=1, source_target_pairs={{0,16},{4,20},{16,24},{20,28},{24,8},{28,12},{8,0},{12,4},{1,17},{... | collective-permute-start | bytes 786440 | tf_op jit(solution)/shard_map/ppermute | solution.py:457
  65.3 1.3 %arrange.1 = (bf16[2,512,512]{2,1,0:T(8,128)(2,1)S(1)}, bf16[2,512,512]{2,1,0:T(8,128)(2,1)S(1)}) custom-call(s32[1]{0:T(128)} %bitcast.2.head_ref.at_ref, s32[1]{0:T(128)} %bitcast.3.spot_ref, bf16[512,512]{1,0:T(8,128)(2,1)} %refs_0_.3, bf16[512,512]{1,0:T(8,128)(2,1)} %collective-permute-done.12.refs_1_, ...), custom_call_target="tpu_custom_call" | custom-call | flops 1 | bytes 1 | tf_op jit(solution)/shard_map/arrange/pallas_call | solution.py:367
  67.3 1.6 %collective-permute-start.24 = (bf16[512,512]{1,0:T(8,128)(2,1)S(1)}, bf16[512,512]{1,0:T(8,128)(2,1)S(1)}, u32[]{:S(2)}, u32[]{:S(2)}) collective-permute-start(bf16[512,512]{1,0:T(8,128)(2,1)S(1)} %head_part.3), channel_id=1, source_target_pairs={{0,2},{1,3},{2,0},{3,1},{4,6},{5,7},{6,4},{7,5},{8,10},{9,11},{10,... | collective-permute-start | bytes 1572872 | tf_op jit(solution)/shard_map/ppermute | solution.py:444
  70.3 1.7 %collective-permute-done.10.moved_ref = bf16[256,512]{1,0:T(8,128)(2,1)S(1)} collective-permute-done((bf16[256,512]{1,0:T(8,128)(2,1)S(1)}, bf16[256,512]{1,0:T(8,128)(2,1)S(1)}, u32[]{:S(2)}, u32[]{:S(2)}) %collective-permute-start.10) | collective-permute-done | bytes 262176 | tf_op jit(solution)/shard_map/ppermute | solution.py:457
  72.0 3.4 %collective-permute-start.20 = (bf16[256,512]{1,0:T(8,128)(2,1)S(1)}, bf16[256,512]{1,0:T(8,128)(2,1)S(1)}, u32[]{:S(2)}, u32[]{:S(2)}) collective-permute-start(bf16[256,512]{1,0:T(8,128)(2,1)S(1)} %add_own.4), channel_id=1, source_target_pairs={{0,16},{4,20},{16,24},{20,28},{24,8},{28,12},{8,0},{12,4},{1,17},{... | collective-permute-start | bytes 786440 | tf_op jit(solution)/shard_map/ppermute | solution.py:457
  75.5 2.7 %collective-permute-done.21.moved_ref = bf16[256,512]{1,0:T(8,128)(2,1)S(1)} collective-permute-done((bf16[256,512]{1,0:T(8,128)(2,1)S(1)}, bf16[256,512]{1,0:T(8,128)(2,1)S(1)}, u32[]{:S(2)}, u32[]{:S(2)}) %collective-permute-start.21) | collective-permute-done | bytes 262176 | tf_op jit(solution)/shard_map/ppermute | solution.py:457
  78.2 2.9 %collective-permute-start.23 = (bf16[256,512]{1,0:T(8,128)(2,1)S(1)}, bf16[256,512]{1,0:T(8,128)(2,1)S(1)}, u32[]{:S(2)}, u32[]{:S(2)}) collective-permute-start(bf16[256,512]{1,0:T(8,128)(2,1)S(1)} %add_own.5), channel_id=1, source_target_pairs={{0,16},{4,20},{16,24},{20,28},{24,8},{28,12},{8,0},{12,4},{1,17},{... | collective-permute-start | bytes 786440 | tf_op jit(solution)/shard_map/ppermute | solution.py:457
  81.1 1.5 %collective-permute-start.26 = (bf16[512,512]{1,0:T(8,128)(2,1)S(1)}, bf16[512,512]{1,0:T(8,128)(2,1)S(1)}, u32[]{:S(2)}, u32[]{:S(2)}) collective-permute-start(bf16[512,512]{1,0:T(8,128)(2,1)S(1)} %head_part.4), channel_id=1, source_target_pairs={{0,2},{1,3},{2,0},{3,1},{4,6},{5,7},{6,4},{7,5},{8,10},{9,11},{10,... | collective-permute-start | bytes 1572872 | tf_op jit(solution)/shard_map/ppermute | solution.py:444
  83.7 1.2 %pieces.7 = (f32[256,512]{1,0:T(8,128)S(1)}, f32[256,512]{1,0:T(8,128)S(1)}) custom-call(s32[1]{0:T(128)} %bitcast.3.spot_ref, s32[1]{0:T(128)} %bitcast.2.head_ref.at_ref, bf16[512,512]{1,0:T(8,128)(2,1)S(1)} %finish_value.1.a_ref.x_ref, bf16[512,512]{1,0:T(8,128)(2,1)S(1)} %collective-permute-done.2.b_ref.x_ref, ...), custom_call_target="tpu_custom_call" | custom-call | flops 1 | bytes 1 | tf_op jit(solution)/shard_map/pieces/pallas_call | solution.py:291
  86.3 1.7 %collective-permute-start.22 = (bf16[256,512]{1,0:T(8,128)(2,1)S(1)}, bf16[256,512]{1,0:T(8,128)(2,1)S(1)}, u32[]{:S(2)}, u32[]{:S(2)}) collective-permute-start(bf16[256,512]{1,0:T(8,128)(2,1)S(1)} %add_own.6), channel_id=1, source_target_pairs={{0,16},{4,20},{16,24},{20,28},{24,8},{28,12},{8,0},{12,4},{1,17},{... | collective-permute-start | bytes 786440 | tf_op jit(solution)/shard_map/ppermute | solution.py:457
  89.0 3.3 %collective-permute-start.25 = (bf16[256,512]{1,0:T(8,128)(2,1)S(1)}, bf16[256,512]{1,0:T(8,128)(2,1)S(1)}, u32[]{:S(2)}, u32[]{:S(2)}) collective-permute-start(bf16[256,512]{1,0:T(8,128)(2,1)S(1)} %add_own.7), channel_id=1, source_target_pairs={{0,16},{4,20},{16,24},{20,28},{24,8},{28,12},{8,0},{12,4},{1,17},{... | collective-permute-start | bytes 786440 | tf_op jit(solution)/shard_map/ppermute | solution.py:457
  92.3 3.2 %collective-permute-done.22.refs_0_ = bf16[256,512]{1,0:T(8,128)(2,1)S(1)} collective-permute-done((bf16[256,512]{1,0:T(8,128)(2,1)S(1)}, bf16[256,512]{1,0:T(8,128)(2,1)S(1)}, u32[]{:S(2)}, u32[]{:S(2)}) %collective-permute-start.22) | collective-permute-done | bytes 262176 | tf_op jit(solution)/shard_map/ppermute | solution.py:457
  95.6 3.9 %collective-permute-done.25.refs_1_ = bf16[256,512]{1,0:T(8,128)(2,1)S(1)} collective-permute-done((bf16[256,512]{1,0:T(8,128)(2,1)S(1)}, bf16[256,512]{1,0:T(8,128)(2,1)S(1)}, u32[]{:S(2)}, u32[]{:S(2)}) %collective-permute-start.25) | collective-permute-done | bytes 262176 | tf_op jit(solution)/shard_map/ppermute | solution.py:457
  99.4 1.3 %finish_weight.1 = f32[512,512]{1,0:T(8,128)} custom-call(bf16[256,512]{1,0:T(8,128)(2,1)S(1)} %collective-permute-done.22.refs_0_, bf16[256,512]{1,0:T(8,128)(2,1)S(1)} %collective-permute-done.25.refs_1_, f32[256,512]{1,0:T(8,128)S(1)} %get-tuple-element.83.refs_2_, f32[256,512]{1,0:T(8,128)S(1)} %get-tuple-element.88.refs_3_), custom_call_target="tpu_custom_call" | custom-call | flops 1 | bytes 1 | tf_op jit(solution)/shard_map/finish_weight/pallas_call | solution.py:315
  100.8 1.8 %join.1 = bf16[512,1024]{1,0:T(8,128)(2,1)} custom-call(s32[1]{0:T(128)} %bitcast.par_ref, s32[1]{0:T(128)} %bitcast.2.head_ref.at_ref, bf16[512,512]{1,0:T(8,128)(2,1)S(1)} %finish_value.1.a_ref.x_ref, bf16[512,512]{1,0:T(8,128)(2,1)S(1)} %collective-permute-done.19.y_ref, bf16[2,512,512]{2,1,0:T(8,128)(2,1)S(1)} %get-tuple-element.73.w_ref, ...), custom_call_target="tpu_custom_call" | custom-call | flops 1 | bytes 1 | tf_op jit(solution)/shard_map/join/pallas_call | solution.py:418
  (77 shorter events, 19.3 us)
Async XLA Ops:
  4.7 8.1 %collective-permute-start = (bf16[3,2,128,128]{3,2,1,0:T(8,128)(2,1)}, bf16[3,2,128,128]{3,2,1,0:T(8,128)(2,1)S(1)}, u32[]{:S(2)}, u32[]{:S(2)}) collective-permute-start(bf16[3,2,128,128]{3,2,1,0:T(8,128)(2,1)} %get-tuple-element.48), channel_id=1, source_target_pairs={{0,4},{4,0},{8,12},{12,8},{16,20},{20,16},{24,28},{28,24},{1,5},{5... | collective-permute-start | bytes 589832 | tf_op jit(solution)/shard_map/ppermute | solution.py:441
  7.7 21.2 %collective-permute-start.12 = (bf16[512,512]{1,0:T(8,128)(2,1)}, bf16[512,512]{1,0:T(8,128)(2,1)}, u32[]{:S(2)}, u32[]{:S(2)}) collective-permute-start(bf16[512,512]{1,0:T(8,128)(2,1)} %refs_0_.3), channel_id=1, source_target_pairs={{0,16},{4,20},{16,24},{20,28},{24,8},{28,12},{8,0},{12,4},{1,17},{... | collective-permute-start | bytes 1572872 | tf_op jit(solution)/shard_map/ppermute | solution.py:457
  12.8 17.1 %collective-permute-start.6 = (bf16[1,512,512]{2,1,0:T(8,128)(2,1)}, bf16[1,512,512]{2,1,0:T(8,128)(2,1)S(1)}, u32[]{:S(2)}, u32[]{:S(2)}) collective-permute-start(bf16[1,512,512]{2,1,0:T(8,128)(2,1)} %get-tuple-element.61), channel_id=1, source_target_pairs={{0,4},{4,0},{8,12},{12,8},{16,20},{20,16},{24,28},{28,24},{1,5},{5... | collective-permute-start | bytes 1572872 | tf_op jit(solution)/shard_map/ppermute | solution.py:441
  14.5 21.2 %copy-start.6 = (bf16[512,512]{1,0:T(8,128)(2,1)S(1)}, bf16[512,512]{1,0:T(8,128)(2,1)}, u32[]{:S(2)}) copy-start(bf16[512,512]{1,0:T(8,128)(2,1)} %k_ref.1) | copy-start | bytes 1572868
  15.3 20.4 %copy-start.4 = (bf16[512,512]{1,0:T(8,128)(2,1)S(1)}, bf16[512,512]{1,0:T(8,128)(2,1)}, u32[]{:S(2)}) copy-start(bf16[512,512]{1,0:T(8,128)(2,1)} %q_ref.1) | copy-start | bytes 1572868
  15.3 13.5 %all-to-all-start = ((bf16[4,2,128,128]{3,2,1,0:T(8,128)(2,1)}), bf16[4,2,128,128]{3,2,1,0:T(8,128)(2,1)S(1)}, u32[]{:S(2)}, u32[]{:S(2)}) async-start(bf16[4,2,128,128]{3,2,1,0:T(8,128)(2,1)} %offer.1), calls=%async_computation | async-start | bytes 524288 | tf_op jit(solution)/shard_map/all_to_all | solution.py:470
  20.3 14.9 %collective-permute-start.4 = (bf16[1,512,512]{2,1,0:T(8,128)(2,1)S(1)}, bf16[1,512,512]{2,1,0:T(8,128)(2,1)S(1)}, u32[]{:S(2)}, u32[]{:S(2)}) collective-permute-start(bf16[1,512,512]{2,1,0:T(8,128)(2,1)S(1)} %get-tuple-element.59.refs_0_), channel_id=1, source_target_pairs={{0,2},{1,3},{2,0},{3,1},{4,6},{5,7},{6,4},{7,5},{8,10},{9,11},{10,... | collective-permute-start | bytes 1572872 | tf_op jit(solution)/shard_map/ppermute | solution.py:444
  28.9 12.2 %copy-start.11 = (f32[2,2,128,128]{3,2,1,0:T(8,128)}, f32[2,2,128,128]{3,2,1,0:T(8,128)S(1)}, u32[]{:S(2)}) copy-start(f32[2,2,128,128]{3,2,1,0:T(8,128)S(1)} %get-tuple-element.53.refs_0_) | copy-start | bytes 786436
  28.9 12.6 %collective-permute-start.13 = (bf16[512,512]{1,0:T(8,128)(2,1)}, bf16[512,512]{1,0:T(8,128)(2,1)}, u32[]{:S(2)}, u32[]{:S(2)}) collective-permute-start(bf16[512,512]{1,0:T(8,128)(2,1)} %collective-permute-done.12.refs_1_), channel_id=1, source_target_pairs={{0,16},{4,20},{16,24},{20,28},{24,8},{28,12},{8,0},{12,4},{1,17},{... | collective-permute-start | bytes 1572872 | tf_op jit(solution)/shard_map/ppermute | solution.py:457
  29.9 14.0 %collective-permute-start.8 = (bf16[1,512,512]{2,1,0:T(8,128)(2,1)S(1)}, bf16[1,512,512]{2,1,0:T(8,128)(2,1)S(1)}, u32[]{:S(2)}, u32[]{:S(2)}) collective-permute-start(bf16[1,512,512]{2,1,0:T(8,128)(2,1)S(1)} %collective-permute-done.6.refs_4_), channel_id=1, source_target_pairs={{0,2},{1,3},{2,0},{3,1},{4,6},{5,7},{6,4},{7,5},{8,10},{9,11},{10,... | collective-permute-start | bytes 1572872 | tf_op jit(solution)/shard_map/ppermute | solution.py:444
  31.4 12.5 %collective-permute-start.3 = (bf16[1,512,512]{2,1,0:T(8,128)(2,1)S(1)}, bf16[1,512,512]{2,1,0:T(8,128)(2,1)S(1)}, u32[]{:S(2)}, u32[]{:S(2)}) collective-permute-start(bf16[1,512,512]{2,1,0:T(8,128)(2,1)S(1)} %get-tuple-element.59.refs_0_), channel_id=1, source_target_pairs={{0,1},{1,0},{2,3},{3,2},{4,5},{5,4},{6,7},{7,6},{8,9},{9,8},{10,11... | collective-permute-start | bytes 1572872 | tf_op jit(solution)/shard_map/ppermute | solution.py:444
  35.2 12.2 %collective-permute-start.5 = (bf16[1,512,512]{2,1,0:T(8,128)(2,1)S(1)}, bf16[1,512,512]{2,1,0:T(8,128)(2,1)S(1)}, u32[]{:S(2)}, u32[]{:S(2)}) collective-permute-start(bf16[1,512,512]{2,1,0:T(8,128)(2,1)S(1)} %collective-permute-done.4.refs_2_), channel_id=1, source_target_pairs={{0,1},{1,0},{2,3},{3,2},{4,5},{5,4},{6,7},{7,6},{8,9},{9,8},{10,11... | collective-permute-start | bytes 1572872 | tf_op jit(solution)/shard_map/ppermute | solution.py:444
  35.2 5.9 %collective-permute-start.1 = (bf16[2,2,128,128]{3,2,1,0:T(8,128)(2,1)S(1)}, bf16[2,2,128,128]{3,2,1,0:T(8,128)(2,1)S(1)}, u32[]{:S(2)}, u32[]{:S(2)}) collective-permute-start(bf16[2,2,128,128]{3,2,1,0:T(8,128)(2,1)S(1)} %get-tuple-element.49), channel_id=1, source_target_pairs={{0,4},{4,0},{8,12},{12,8},{16,20},{20,16},{24,28},{28,24},{1,5},{5... | collective-permute-start | bytes 393224 | tf_op jit(solution)/shard_map/ppermute | solution.py:441
  41.1 16.4 %collective-permute-start.7 = (bf16[1,512,512]{2,1,0:T(8,128)(2,1)S(1)}, bf16[1,512,512]{2,1,0:T(8,128)(2,1)}, u32[]{:S(2)}, u32[]{:S(2)}) collective-permute-start(bf16[1,512,512]{2,1,0:T(8,128)(2,1)S(1)} %collective-permute-done.6.refs_4_), channel_id=1, source_target_pairs={{0,1},{1,0},{2,3},{3,2},{4,5},{5,4},{6,7},{7,6},{8,9},{9,8},{10,11... | collective-permute-start | bytes 1572872 | tf_op jit(solution)/shard_map/ppermute | solution.py:444
  41.6 16.3 %collective-permute-start.2 = (bf16[512,512]{1,0:T(8,128)(2,1)S(1)}, bf16[512,512]{1,0:T(8,128)(2,1)S(1)}, u32[]{:S(2)}, u32[]{:S(2)}) collective-permute-start(bf16[512,512]{1,0:T(8,128)(2,1)S(1)} %finish_value.1.a_ref.x_ref), channel_id=1, source_target_pairs={{0,4},{4,0},{8,12},{12,8},{16,20},{20,16},{24,28},{28,24},{1,5},{5... | collective-permute-start | bytes 1572872 | tf_op jit(solution)/shard_map/ppermute | solution.py:441
  43.9 14.2 %collective-permute-start.9 = (bf16[1,512,512]{2,1,0:T(8,128)(2,1)S(1)}, bf16[1,512,512]{2,1,0:T(8,128)(2,1)}, u32[]{:S(2)}, u32[]{:S(2)}) collective-permute-start(bf16[1,512,512]{2,1,0:T(8,128)(2,1)S(1)} %collective-permute-done.8.refs_6_), channel_id=1, source_target_pairs={{0,1},{1,0},{2,3},{3,2},{4,5},{5,4},{6,7},{7,6},{8,9},{9,8},{10,11... | collective-permute-start | bytes 1572872 | tf_op jit(solution)/shard_map/ppermute | solution.py:444
  44.7 15.2 %collective-permute-start.14 = (bf16[512,512]{1,0:T(8,128)(2,1)}, bf16[512,512]{1,0:T(8,128)(2,1)}, u32[]{:S(2)}, u32[]{:S(2)}) collective-permute-start(bf16[512,512]{1,0:T(8,128)(2,1)} %collective-permute-done.13.refs_2_), channel_id=1, source_target_pairs={{0,16},{4,20},{16,24},{20,28},{24,8},{28,12},{8,0},{12,4},{1,17},{... | collective-permute-start | bytes 1572872 | tf_op jit(solution)/shard_map/ppermute | solution.py:457
  48.1 12.3 %collective-permute-start.16 = (bf16[512,512]{1,0:T(8,128)(2,1)}, bf16[512,512]{1,0:T(8,128)(2,1)}, u32[]{:S(2)}, u32[]{:S(2)}) collective-permute-start(bf16[512,512]{1,0:T(8,128)(2,1)} %collective-permute-done.12.refs_1_), channel_id=1, source_target_pairs={{0,1},{1,0},{2,3},{3,2},{4,5},{5,4},{6,7},{7,6},{8,9},{9,8},{10,11... | collective-permute-start | bytes 1572872 | tf_op jit(solution)/shard_map/ppermute | solution.py:444
  57.5 4.8 %collective-permute-start.15 = (bf16[512,512]{1,0:T(8,128)(2,1)}, bf16[512,512]{1,0:T(8,128)(2,1)S(1)}, u32[]{:S(2)}, u32[]{:S(2)}) collective-permute-start(bf16[512,512]{1,0:T(8,128)(2,1)} %refs_0_.3), channel_id=1, source_target_pairs={{0,1},{1,0},{2,3},{3,2},{4,5},{5,4},{6,7},{7,6},{8,9},{9,8},{10,11... | collective-permute-start | bytes 1572872 | tf_op jit(solution)/shard_map/ppermute | solution.py:444
  57.8 7.4 %collective-permute-start.17 = (bf16[512,512]{1,0:T(8,128)(2,1)}, bf16[512,512]{1,0:T(8,128)(2,1)S(1)}, u32[]{:S(2)}, u32[]{:S(2)}) collective-permute-start(bf16[512,512]{1,0:T(8,128)(2,1)} %collective-permute-done.13.refs_2_), channel_id=1, source_target_pairs={{0,1},{1,0},{2,3},{3,2},{4,5},{5,4},{6,7},{7,6},{8,9},{9,8},{10,11... | collective-permute-start | bytes 1572872 | tf_op jit(solution)/shard_map/ppermute | solution.py:444
  59.9 5.4 %collective-permute-start.18 = (bf16[512,512]{1,0:T(8,128)(2,1)}, bf16[512,512]{1,0:T(8,128)(2,1)S(1)}, u32[]{:S(2)}, u32[]{:S(2)}) collective-permute-start(bf16[512,512]{1,0:T(8,128)(2,1)} %collective-permute-done.14.refs_3_), channel_id=1, source_target_pairs={{0,1},{1,0},{2,3},{3,2},{4,5},{5,4},{6,7},{7,6},{8,9},{9,8},{10,11... | collective-permute-start | bytes 1572872 | tf_op jit(solution)/shard_map/ppermute | solution.py:444
  60.0 6.6 %collective-permute-start.11 = (bf16[512,512]{1,0:T(8,128)(2,1)S(1)}, bf16[512,512]{1,0:T(8,128)(2,1)S(1)}, u32[]{:S(2)}, u32[]{:S(2)}) collective-permute-start(bf16[512,512]{1,0:T(8,128)(2,1)S(1)} %collective-permute-done.2.b_ref.x_ref), channel_id=1, source_target_pairs={{0,1},{1,0},{2,3},{3,2},{4,5},{5,4},{6,7},{7,6},{8,9},{9,8},{10,11... | collective-permute-start | bytes 1572872 | tf_op jit(solution)/shard_map/ppermute | solution.py:444
  60.5 9.0 %collective-permute-start.19 = (bf16[512,512]{1,0:T(8,128)(2,1)S(1)}, bf16[512,512]{1,0:T(8,128)(2,1)S(1)}, u32[]{:S(2)}, u32[]{:S(2)}) collective-permute-start(bf16[512,512]{1,0:T(8,128)(2,1)S(1)} %finish_value.1.a_ref.x_ref), channel_id=1, source_target_pairs={{0,1},{1,0},{2,3},{3,2},{4,5},{5,4},{6,7},{7,6},{8,9},{9,8},{10,11... | collective-permute-start | bytes 1572872 | tf_op jit(solution)/shard_map/ppermute | solution.py:444
  62.4 9.6 %collective-permute-start.10 = (bf16[256,512]{1,0:T(8,128)(2,1)S(1)}, bf16[256,512]{1,0:T(8,128)(2,1)S(1)}, u32[]{:S(2)}, u32[]{:S(2)}) collective-permute-start(bf16[256,512]{1,0:T(8,128)(2,1)S(1)} %get-tuple-element.63), channel_id=1, source_target_pairs={{0,16},{4,20},{16,24},{20,28},{24,8},{28,12},{8,0},{12,4},{1,17},{... | collective-permute-start | bytes 786440 | tf_op jit(solution)/shard_map/ppermute | solution.py:457
  67.3 17.6 %collective-permute-start.24 = (bf16[512,512]{1,0:T(8,128)(2,1)S(1)}, bf16[512,512]{1,0:T(8,128)(2,1)S(1)}, u32[]{:S(2)}, u32[]{:S(2)}) collective-permute-start(bf16[512,512]{1,0:T(8,128)(2,1)S(1)} %head_part.3), channel_id=1, source_target_pairs={{0,2},{1,3},{2,0},{3,1},{4,6},{5,7},{6,4},{7,5},{8,10},{9,11},{10,... | collective-permute-start | bytes 1572872 | tf_op jit(solution)/shard_map/ppermute | solution.py:444
  68.9 9.2 %collective-permute-start.21 = (bf16[256,512]{1,0:T(8,128)(2,1)S(1)}, bf16[256,512]{1,0:T(8,128)(2,1)S(1)}, u32[]{:S(2)}, u32[]{:S(2)}) collective-permute-start(bf16[256,512]{1,0:T(8,128)(2,1)S(1)} %get-tuple-element.77), channel_id=1, source_target_pairs={{0,16},{4,20},{16,24},{20,28},{24,8},{28,12},{8,0},{12,4},{1,17},{... | collective-permute-start | bytes 786440 | tf_op jit(solution)/shard_map/ppermute | solution.py:457
  72.0 12.9 %collective-permute-start.20 = (bf16[256,512]{1,0:T(8,128)(2,1)S(1)}, bf16[256,512]{1,0:T(8,128)(2,1)S(1)}, u32[]{:S(2)}, u32[]{:S(2)}) collective-permute-start(bf16[256,512]{1,0:T(8,128)(2,1)S(1)} %add_own.4), channel_id=1, source_target_pairs={{0,16},{4,20},{16,24},{20,28},{24,8},{28,12},{8,0},{12,4},{1,17},{... | collective-permute-start | bytes 786440 | tf_op jit(solution)/shard_map/ppermute | solution.py:457
  78.2 10.8 %collective-permute-start.23 = (bf16[256,512]{1,0:T(8,128)(2,1)S(1)}, bf16[256,512]{1,0:T(8,128)(2,1)S(1)}, u32[]{:S(2)}, u32[]{:S(2)}) collective-permute-start(bf16[256,512]{1,0:T(8,128)(2,1)S(1)} %add_own.5), channel_id=1, source_target_pairs={{0,16},{4,20},{16,24},{20,28},{24,8},{28,12},{8,0},{12,4},{1,17},{... | collective-permute-start | bytes 786440 | tf_op jit(solution)/shard_map/ppermute | solution.py:457
  81.1 19.7 %collective-permute-start.26 = (bf16[512,512]{1,0:T(8,128)(2,1)S(1)}, bf16[512,512]{1,0:T(8,128)(2,1)S(1)}, u32[]{:S(2)}, u32[]{:S(2)}) collective-permute-start(bf16[512,512]{1,0:T(8,128)(2,1)S(1)} %head_part.4), channel_id=1, source_target_pairs={{0,2},{1,3},{2,0},{3,1},{4,6},{5,7},{6,4},{7,5},{8,10},{9,11},{10,... | collective-permute-start | bytes 1572872 | tf_op jit(solution)/shard_map/ppermute | solution.py:444
  85.7 15.0 %collective-permute-start.27 = (bf16[512,512]{1,0:T(8,128)(2,1)S(1)}, bf16[512,512]{1,0:T(8,128)(2,1)S(1)}, u32[]{:S(2)}, u32[]{:S(2)}) collective-permute-start(bf16[512,512]{1,0:T(8,128)(2,1)S(1)} %head_part.5), channel_id=1, source_target_pairs={{0,4},{4,0},{8,12},{12,8},{16,20},{20,16},{24,28},{28,24},{1,5},{5... | collective-permute-start | bytes 1572872 | tf_op jit(solution)/shard_map/ppermute | solution.py:441
  86.3 9.2 %collective-permute-start.22 = (bf16[256,512]{1,0:T(8,128)(2,1)S(1)}, bf16[256,512]{1,0:T(8,128)(2,1)S(1)}, u32[]{:S(2)}, u32[]{:S(2)}) collective-permute-start(bf16[256,512]{1,0:T(8,128)(2,1)S(1)} %add_own.6), channel_id=1, source_target_pairs={{0,16},{4,20},{16,24},{20,28},{24,8},{28,12},{8,0},{12,4},{1,17},{... | collective-permute-start | bytes 786440 | tf_op jit(solution)/shard_map/ppermute | solution.py:457
  89.0 10.4 %collective-permute-start.25 = (bf16[256,512]{1,0:T(8,128)(2,1)S(1)}, bf16[256,512]{1,0:T(8,128)(2,1)S(1)}, u32[]{:S(2)}, u32[]{:S(2)}) collective-permute-start(bf16[256,512]{1,0:T(8,128)(2,1)S(1)} %add_own.7), channel_id=1, source_target_pairs={{0,16},{4,20},{16,24},{20,28},{24,8},{28,12},{8,0},{12,4},{1,17},{... | collective-permute-start | bytes 786440 | tf_op jit(solution)/shard_map/ppermute | solution.py:457
  (12 other events, 36.4 us)

commit v15 on v14

--- a/solution.py
+++ b/solution.py
@@ -489,7 +489,7 @@
     offsets = [0]
     bit = n_head // 2
     while bit:
-        own = own + [across(r, bit) for r in own]
+        own = own + [across(after(r, mine) if len(own) > 1 else r, bit) for r in own]
         theirs = theirs + [across(r, bit) for r in theirs]
         offsets = offsets + [o ^ bit for o in offsets]
         bit //= 2
@@ -505,9 +505,9 @@
 
     total = piece(BF16, 0, query_grad, 4 * length * cols * width)
     moved = [ring(x) for x in total]
-    other_too = across(other, 1)
-    lent.append(across(after(blocks[-1], total[0]), 1))
-    local_part = piece(F32, 1, total[0])
+    other_too = across(after(other, total[0]), 1)
+    local_part = piece(F32, 1, other_too)
+    lent.append(across(after(blocks[-1], local_part[0]), 1))
 
 
     def summed_parts(x, y):
@@ -517,11 +517,7 @@
         ]
         return sent[-1], [across(x, 2 * i + 2) for i, x in enumerate(sent)]
 
-    held = [after(blocks[0], local_part[0])] + blocks[1:]
-    weight, borrowed = arrange(order, per, n_head, here, spot, held, lent)
-    token, got_other = summed_parts(other, other_too)
-    token, got_mine = summed_parts(after(mine, token), mine_too)
-    part = None
+    token = part = None
     for step in range(1, pairs - 1):
         if step == pairs - 2:
             last = piece(F32, pairs - 1, token)
@@ -530,8 +526,15 @@
             if step == pairs - 2 and i == chains - 1:
                 lead = (here, after(other, token), other_too, weight, borrowed)
                 token = part = head_part(*lead, got_other)
-            token = add_own(moved[i], after(local_part[i], token))
+            own_part = local_part[i] if token is None else after(local_part[i], token)
+            token = add_own(moved[i], own_part)
             moved[i] = ring(token)
+            if step == 1 and i == 0:
+                held = [after(blocks[0], token)] + blocks[1:]
+                weight, borrowed = arrange(order, per, n_head, here, spot, held, lent)
+                token, got_other = summed_parts(other, other_too)
+            elif step == 1 and i == chains - 1:
+                token, got_mine = summed_parts(after(mine, token), mine_too)
         if step < pairs - 2:
             local_part = piece(F32, step + 1, token)
             token = local_part[0]

time: 103 us -> 123 us (1.19)
  waiting for transfers between devices: 27.9 us -> 48.2 us
    ppermute x9, waiting for transfers between devices: 12.5 us -> 34.1 us  [ring(): return lax.ppermute(x, 'ctx', moves)]
    ppermute x14, waiting for transfers between devices: 5.52 us -> 3.49 us  [across(): return lax.ppermute(x, 'head', [(i, i ^ bit) for i in range(n_head)])]
    ppermute x9, starting transfers between devices: 20.9 us -> 22.4 us  [ring(): return lax.ppermute(x, 'ctx', moves)]
    ppermute x5, waiting for transfers between devices: 2.87 us -> 4.16 us  [partner(): return lax.ppermute(x, 'ctx', [(i, i ^ 1) for i in range(n_ctx)])]
    ppermute x14, starting transfers between devices: 7.54 us -> 6.3 us  [across(): return lax.ppermute(x, 'head', [(i, i ^ bit) for i in range(n_head)])]
    unnamed x30 -> x28, local copies, waits for them, and re-layouts: 7.77 us -> 6.98 us
  transfers between devices with their start and end apart: 29 -> 29, of which waited for: 10 -> 12; matrix products, arithmetic and copies ran while one was open for 0% -> 0% of each run, Pallas kernels for 20% -> 16%
where the time goes in v15:
time: 123 us; the launch traced here: 122 us
  waiting for transfers between devices  48.2 us (39%)
  starting transfers between devices  40.9 us (33%)
  Pallas kernels  25.2 us (20%)
  local copies, waits for them, and re-layouts  6.98 us (6%)
    ppermute x9, waiting for transfers between devices, ring(): return lax.ppermute(x, 'ctx', moves)  34.1 us
    ppermute x9, starting transfers between devices, ring(): return lax.ppermute(x, 'ctx', moves)  22.4 us
    ppermute x5, starting transfers between devices, partner(): return lax.ppermute(x, 'ctx', [(i, i ^ 1) for i in range(n_ctx)])  7.18 us
    unnamed x28, local copies, waits for them, and re-layouts  6.98 us
    all_to_all x1, waiting for transfers between devices, local(): lax.all_to_all(offered, 'ctx', split_axis=0, concat_axis=0, axis_index_gr...  6.5 us
    ppermute x14, starting transfers between devices, across(): return lax.ppermute(x, 'head', [(i, i ^ bit) for i in range(n_head)])  6.3 us
    pallas_call x4, Pallas kernels, pieces(): call(functools.partial(piece_kernel, order, per, step, count), flops=flop...  6.05 us
    all_to_all x1, starting transfers between devices, local(): lax.all_to_all(offered, 'ctx', split_axis=0, concat_axis=0, axis_index_gr...  5 us
  transfers between devices with their start and end apart: 29, of which 12 were waited for; matrix products, arithmetic and copies ran while one was open for 0% of the time, Pallas kernels for 16%

profile of v15, /device:TPU:0, one launch (start us, length us, event | category | flops | bytes accessed | tf_op | source)
XLA Modules:
  0.0 122.2 jit_solution(7590903575151579832)
XLA Ops:
  0.7 4.0 %states.1 = (f32[2,2,128,128]{3,2,1,0:T(8,128)}, bf16[3,2,128,128]{3,2,1,0:T(8,128)(2,1)}) custom-call(s32[1]{0:T(128)} %bitcast.par_ref, bf16[512,512]{1,0:T(8,128)(2,1)} %q_ref.1, bf16[512,512]{1,0:T(8,128)(2,1)} %k_ref.1, bf16[512,512]{1,0:T(8,128)(2,1)} %v_ref, bf16[512,512]{1,0:T(8,128)(2,1)} %g_ref.1), custom_call_target="tpu_custom_call" | custom-call | flops 1 | bytes 1 | tf_op jit(solution)/shard_map/states/pallas_call | solution.py:67
  4.7 3.0 %collective-permute-start = (bf16[3,2,128,128]{3,2,1,0:T(8,128)(2,1)}, bf16[3,2,128,128]{3,2,1,0:T(8,128)(2,1)S(1)}, u32[]{:S(2)}, u32[]{:S(2)}) collective-permute-start(bf16[3,2,128,128]{3,2,1,0:T(8,128)(2,1)} %get-tuple-element.50), channel_id=1, source_target_pairs={{0,4},{4,0},{8,12},{12,8},{16,20},{20,16},{24,28},{28,24},{1,5},{5... | collective-permute-start | bytes 589832 | tf_op jit(solution)/shard_map/ppermute | solution.py:441
  8.7 4.1 %collective-permute-done.got_ref.refs_2_ = bf16[3,2,128,128]{3,2,1,0:T(8,128)(2,1)S(1)} collective-permute-done((bf16[3,2,128,128]{3,2,1,0:T(8,128)(2,1)}, bf16[3,2,128,128]{3,2,1,0:T(8,128)(2,1)S(1)}, u32[]{:S(2)}, u32[]{:S(2)}) %collective-permute-start) | collective-permute-done | bytes 196640 | tf_op jit(solution)/shard_map/ppermute | solution.py:441
  12.8 1.7 %collective-permute-start.6 = (bf16[1,512,512]{2,1,0:T(8,128)(2,1)}, bf16[1,512,512]{2,1,0:T(8,128)(2,1)S(1)}, u32[]{:S(2)}, u32[]{:S(2)}) collective-permute-start(bf16[1,512,512]{2,1,0:T(8,128)(2,1)} %get-tuple-element.65), channel_id=1, source_target_pairs={{0,4},{4,0},{8,12},{12,8},{16,20},{20,16},{24,28},{28,24},{1,5},{5... | collective-permute-start | bytes 1572872 | tf_op jit(solution)/shard_map/ppermute | solution.py:441
  15.3 5.0 %all-to-all-start = ((bf16[4,2,128,128]{3,2,1,0:T(8,128)(2,1)}), bf16[4,2,128,128]{3,2,1,0:T(8,128)(2,1)S(1)}, u32[]{:S(2)}, u32[]{:S(2)}) async-start(bf16[4,2,128,128]{3,2,1,0:T(8,128)(2,1)} %offer.1), calls=%async_computation | async-start | bytes 524288 | tf_op jit(solution)/shard_map/all_to_all | solution.py:470
  20.3 1.5 %collective-permute-start.4 = (bf16[1,512,512]{2,1,0:T(8,128)(2,1)S(1)}, bf16[1,512,512]{2,1,0:T(8,128)(2,1)S(1)}, u32[]{:S(2)}, u32[]{:S(2)}) collective-permute-start(bf16[1,512,512]{2,1,0:T(8,128)(2,1)S(1)} %get-tuple-element.62.refs_0_), channel_id=1, source_target_pairs={{0,2},{1,3},{2,0},{3,1},{4,6},{5,7},{6,4},{7,5},{8,10},{9,11},{10,... | collective-permute-start | bytes 1572872 | tf_op jit(solution)/shard_map/ppermute | solution.py:444
  21.8 6.5 %all-to-all-done.every_ref = bf16[4,2,128,128]{3,2,1,0:T(8,128)(2,1)S(1)} async-done(((bf16[4,2,128,128]{3,2,1,0:T(8,128)(2,1)}), bf16[4,2,128,128]{3,2,1,0:T(8,128)(2,1)S(1)}, u32[]{:S(2)}, u32[]{:S(2)}) %all-to-all-start) | async-done | bytes 262176 | tf_op jit(solution)/shard_map/all_to_all | solution.py:470
  28.9 1.5 %collective-permute-start.8 = (bf16[1,512,512]{2,1,0:T(8,128)(2,1)S(1)}, bf16[1,512,512]{2,1,0:T(8,128)(2,1)S(1)}, u32[]{:S(2)}, u32[]{:S(2)}) collective-permute-start(bf16[1,512,512]{2,1,0:T(8,128)(2,1)S(1)} %collective-permute-done.6.refs_4_), channel_id=1, source_target_pairs={{0,2},{1,3},{2,0},{3,1},{4,6},{5,7},{6,4},{7,5},{8,10},{9,11},{10,... | collective-permute-start | bytes 1572872 | tf_op jit(solution)/shard_map/ppermute | solution.py:444
  31.5 3.0 %inside.1 = (f32[512,512]{1,0:T(8,128)S(1)}, bf16[512,512]{1,0:T(8,128)(2,1)S(1)}) custom-call(bf16[512,512]{1,0:T(8,128)(2,1)S(1)} %copy-done.2, bf16[512,512]{1,0:T(8,128)(2,1)S(1)} %copy-done.4, bf16[512,512]{1,0:T(8,128)(2,1)S(1)} %copy-done.6), custom_call_target="tpu_custom_call" | custom-call | flops 1 | bytes 1 | tf_op jit(solution)/shard_map/inside/pallas_call | solution.py:147
  35.7 3.4 %collective-permute-done.14.refs_1_ = bf16[512,512]{1,0:T(8,128)(2,1)} collective-permute-done((bf16[512,512]{1,0:T(8,128)(2,1)}, bf16[512,512]{1,0:T(8,128)(2,1)}, u32[]{:S(2)}, u32[]{:S(2)}) %collective-permute-start.14) | collective-permute-done | bytes 524320 | tf_op jit(solution)/shard_map/ppermute | solution.py:457
  39.1 1.4 %collective-permute-start.2 = (bf16[512,512]{1,0:T(8,128)(2,1)S(1)}, bf16[512,512]{1,0:T(8,128)(2,1)S(1)}, u32[]{:S(2)}, u32[]{:S(2)}) collective-permute-start(bf16[512,512]{1,0:T(8,128)(2,1)S(1)} %finish_value.1.a_ref.x_ref), channel_id=1, source_target_pairs={{0,4},{4,0},{8,12},{12,8},{16,20},{20,16},{24,28},{28,24},{1,5},{5... | collective-permute-start | bytes 1572872 | tf_op jit(solution)/shard_map/ppermute | solution.py:441
  40.5 3.3 %collective-permute-done.8.refs_6_ = bf16[1,512,512]{2,1,0:T(8,128)(2,1)S(1)} collective-permute-done((bf16[1,512,512]{2,1,0:T(8,128)(2,1)S(1)}, bf16[1,512,512]{2,1,0:T(8,128)(2,1)S(1)}, u32[]{:S(2)}, u32[]{:S(2)}) %collective-permute-start.8) | collective-permute-done | bytes 524320 | tf_op jit(solution)/shard_map/ppermute | solution.py:444
  44.6 2.6 %collective-permute-start.15 = (bf16[512,512]{1,0:T(8,128)(2,1)}, bf16[512,512]{1,0:T(8,128)(2,1)}, u32[]{:S(2)}, u32[]{:S(2)}) collective-permute-start(bf16[512,512]{1,0:T(8,128)(2,1)} %collective-permute-done.14.refs_1_), channel_id=1, source_target_pairs={{0,16},{4,20},{16,24},{20,28},{24,8},{28,12},{8,0},{12,4},{1,17},{... | collective-permute-start | bytes 1572872 | tf_op jit(solution)/shard_map/ppermute | solution.py:457
  52.3 4.0 %others.1 = (bf16[512,512]{1,0:T(8,128)(2,1)}, bf16[512,512]{1,0:T(8,128)(2,1)}) custom-call(s32[1]{0:T(128)} %bitcast.par_ref, bf16[512,512]{1,0:T(8,128)(2,1)S(1)} %copy-done.3, bf16[512,512]{1,0:T(8,128)(2,1)S(1)} %copy-done.5, bf16[512,512]{1,0:T(8,128)(2,1)S(1)} %copy-done.8, bf16[512,512]{1,0:T(8,128)(2,1)S(1)} %copy-done.7, ...), custom_call_target="tpu_custom_call" | custom-call | flops 1 | bytes 1 | tf_op jit(solution)/shard_map/others/pallas_call | solution.py:246
  56.4 2.0 %pieces.4 = (bf16[256,512]{1,0:T(8,128)(2,1)S(1)}, bf16[256,512]{1,0:T(8,128)(2,1)S(1)}) custom-call(s32[1]{0:T(128)} %bitcast.3.spot_ref, s32[1]{0:T(128)} %bitcast.2.head_ref.at_ref, bf16[512,512]{1,0:T(8,128)(2,1)S(1)} %finish_value.1.a_ref.x_ref, bf16[512,512]{1,0:T(8,128)(2,1)S(1)} %collective-permute-done.2.b_ref.x_ref, ...), custom_call_target="tpu_custom_call" | custom-call | flops 536870912 | bytes 1 | tf_op jit(solution)/shard_map/pieces/pallas_call | solution.py:291
  59.4 3.4 %collective-permute-start.16 = (bf16[512,512]{1,0:T(8,128)(2,1)}, bf16[512,512]{1,0:T(8,128)(2,1)S(1)}, u32[]{:S(2)}, u32[]{:S(2)}) collective-permute-start(bf16[512,512]{1,0:T(8,128)(2,1)} %collective-permute-done.15.refs_2_), channel_id=1, source_target_pairs={{0,16},{4,20},{16,24},{20,28},{24,8},{28,12},{8,0},{12,4},{1,17},{... | collective-permute-start | bytes 1572872 | tf_op jit(solution)/shard_map/ppermute | solution.py:457
  63.3 1.8 %pieces.5 = (f32[256,512]{1,0:T(8,128)S(1)}, f32[256,512]{1,0:T(8,128)S(1)}) custom-call(s32[1]{0:T(128)} %bitcast.3.spot_ref, s32[1]{0:T(128)} %bitcast.2.head_ref.at_ref, bf16[512,512]{1,0:T(8,128)(2,1)S(1)} %finish_value.1.a_ref.x_ref, bf16[512,512]{1,0:T(8,128)(2,1)S(1)} %collective-permute-done.2.b_ref.x_ref, ...), custom_call_target="tpu_custom_call" | custom-call | flops 1 | bytes 1 | tf_op jit(solution)/shard_map/pieces/pallas_call | solution.py:291
  65.1 9.1 %collective-permute-done.16.refs_3_ = bf16[512,512]{1,0:T(8,128)(2,1)S(1)} collective-permute-done((bf16[512,512]{1,0:T(8,128)(2,1)}, bf16[512,512]{1,0:T(8,128)(2,1)S(1)}, u32[]{:S(2)}, u32[]{:S(2)}) %collective-permute-start.16) | collective-permute-done | bytes 524320 | tf_op jit(solution)/shard_map/ppermute | solution.py:457
  74.2 3.3 %collective-permute-start.10 = (bf16[256,512]{1,0:T(8,128)(2,1)S(1)}, bf16[256,512]{1,0:T(8,128)(2,1)S(1)}, u32[]{:S(2)}, u32[]{:S(2)}) collective-permute-start(bf16[256,512]{1,0:T(8,128)(2,1)S(1)} %get-tuple-element.67), channel_id=1, source_target_pairs={{0,16},{4,20},{16,24},{20,28},{24,8},{28,12},{8,0},{12,4},{1,17},{... | collective-permute-start | bytes 786440 | tf_op jit(solution)/shard_map/ppermute | solution.py:457
  77.4 6.2 %collective-permute-done.10.moved_ref = bf16[256,512]{1,0:T(8,128)(2,1)S(1)} collective-permute-done((bf16[256,512]{1,0:T(8,128)(2,1)S(1)}, bf16[256,512]{1,0:T(8,128)(2,1)S(1)}, u32[]{:S(2)}, u32[]{:S(2)}) %collective-permute-start.10) | collective-permute-done | bytes 262176 | tf_op jit(solution)/shard_map/ppermute | solution.py:457
  84.9 1.6 %collective-permute-start.24 = (bf16[512,512]{1,0:T(8,128)(2,1)S(1)}, bf16[512,512]{1,0:T(8,128)(2,1)S(1)}, u32[]{:S(2)}, u32[]{:S(2)}) collective-permute-start(bf16[512,512]{1,0:T(8,128)(2,1)S(1)} %head_part.3), channel_id=1, source_target_pairs={{0,2},{1,3},{2,0},{3,1},{4,6},{5,7},{6,4},{7,5},{8,10},{9,11},{10,... | collective-permute-start | bytes 1572872 | tf_op jit(solution)/shard_map/ppermute | solution.py:444
  86.5 4.3 %collective-permute-start.13 = (bf16[256,512]{1,0:T(8,128)(2,1)S(1)}, bf16[256,512]{1,0:T(8,128)(2,1)S(1)}, u32[]{:S(2)}, u32[]{:S(2)}) collective-permute-start(bf16[256,512]{1,0:T(8,128)(2,1)S(1)} %get-tuple-element.71), channel_id=1, source_target_pairs={{0,16},{4,20},{16,24},{20,28},{24,8},{28,12},{8,0},{12,4},{1,17},{... | collective-permute-start | bytes 786440 | tf_op jit(solution)/shard_map/ppermute | solution.py:457
  90.8 6.6 %collective-permute-done.13.moved_ref = bf16[256,512]{1,0:T(8,128)(2,1)S(1)} collective-permute-done((bf16[256,512]{1,0:T(8,128)(2,1)S(1)}, bf16[256,512]{1,0:T(8,128)(2,1)S(1)}, u32[]{:S(2)}, u32[]{:S(2)}) %collective-permute-start.13) | collective-permute-done | bytes 262176 | tf_op jit(solution)/shard_map/ppermute | solution.py:457
  97.4 3.4 %collective-permute-start.23 = (bf16[256,512]{1,0:T(8,128)(2,1)S(1)}, bf16[256,512]{1,0:T(8,128)(2,1)S(1)}, u32[]{:S(2)}, u32[]{:S(2)}) collective-permute-start(bf16[256,512]{1,0:T(8,128)(2,1)S(1)} %add_own.5), channel_id=1, source_target_pairs={{0,16},{4,20},{16,24},{20,28},{24,8},{28,12},{8,0},{12,4},{1,17},{... | collective-permute-start | bytes 786440 | tf_op jit(solution)/shard_map/ppermute | solution.py:457
  102.2 1.1 pieces.6
  103.3 1.1 pieces.7
  105.9 1.9 %collective-permute-start.22 = (bf16[256,512]{1,0:T(8,128)(2,1)S(1)}, bf16[256,512]{1,0:T(8,128)(2,1)S(1)}, u32[]{:S(2)}, u32[]{:S(2)}) collective-permute-start(bf16[256,512]{1,0:T(8,128)(2,1)S(1)} %add_own.6), channel_id=1, source_target_pairs={{0,16},{4,20},{16,24},{20,28},{24,8},{28,12},{8,0},{12,4},{1,17},{... | collective-permute-start | bytes 786440 | tf_op jit(solution)/shard_map/ppermute | solution.py:457
  108.7 3.4 %collective-permute-start.25 = (bf16[256,512]{1,0:T(8,128)(2,1)S(1)}, bf16[256,512]{1,0:T(8,128)(2,1)S(1)}, u32[]{:S(2)}, u32[]{:S(2)}) collective-permute-start(bf16[256,512]{1,0:T(8,128)(2,1)S(1)} %add_own.7), channel_id=1, source_target_pairs={{0,16},{4,20},{16,24},{20,28},{24,8},{28,12},{8,0},{12,4},{1,17},{... | collective-permute-start | bytes 786440 | tf_op jit(solution)/shard_map/ppermute | solution.py:457
  112.1 3.0 %collective-permute-done.22.refs_0_ = bf16[256,512]{1,0:T(8,128)(2,1)S(1)} collective-permute-done((bf16[256,512]{1,0:T(8,128)(2,1)S(1)}, bf16[256,512]{1,0:T(8,128)(2,1)S(1)}, u32[]{:S(2)}, u32[]{:S(2)}) %collective-permute-start.22) | collective-permute-done | bytes 262176 | tf_op jit(solution)/shard_map/ppermute | solution.py:457
  115.1 4.0 %collective-permute-done.25.refs_1_ = bf16[256,512]{1,0:T(8,128)(2,1)S(1)} collective-permute-done((bf16[256,512]{1,0:T(8,128)(2,1)S(1)}, bf16[256,512]{1,0:T(8,128)(2,1)S(1)}, u32[]{:S(2)}, u32[]{:S(2)}) %collective-permute-start.25) | collective-permute-done | bytes 262176 | tf_op jit(solution)/shard_map/ppermute | solution.py:457
  119.1 1.3 %finish_weight.1 = f32[512,512]{1,0:T(8,128)} custom-call(bf16[256,512]{1,0:T(8,128)(2,1)S(1)} %collective-permute-done.22.refs_0_, bf16[256,512]{1,0:T(8,128)(2,1)S(1)} %collective-permute-done.25.refs_1_, f32[256,512]{1,0:T(8,128)S(1)} %get-tuple-element.87.refs_2_, f32[256,512]{1,0:T(8,128)S(1)} %get-tuple-element.92.refs_3_), custom_call_target="tpu_custom_call" | custom-call | flops 1 | bytes 1 | tf_op jit(solution)/shard_map/finish_weight/pallas_call | solution.py:315
  120.4 1.8 %join.1 = bf16[512,1024]{1,0:T(8,128)(2,1)} custom-call(s32[1]{0:T(128)} %bitcast.par_ref, s32[1]{0:T(128)} %bitcast.2.head_ref.at_ref, bf16[512,512]{1,0:T(8,128)(2,1)S(1)} %finish_value.1.a_ref.x_ref, bf16[512,512]{1,0:T(8,128)(2,1)S(1)} %collective-permute-done.21.y_ref, bf16[2,512,512]{2,1,0:T(8,128)(2,1)S(1)} %get-tuple-element.80.w_ref, ...), custom_call_target="tpu_custom_call" | custom-call | flops 1 | bytes 1 | tf_op jit(solution)/shard_map/join/pallas_call | solution.py:418
  (75 shorter events, 16.7 us)
Async XLA Ops:
  4.7 9.9 %copy-start.13 = (f32[2,2,128,128]{3,2,1,0:T(8,128)S(1)}, f32[2,2,128,128]{3,2,1,0:T(8,128)}, u32[]{:S(2)}) copy-start(f32[2,2,128,128]{3,2,1,0:T(8,128)} %get-tuple-element.49.keep_ref) | copy-start | bytes 786436
  4.7 8.1 %collective-permute-start = (bf16[3,2,128,128]{3,2,1,0:T(8,128)(2,1)}, bf16[3,2,128,128]{3,2,1,0:T(8,128)(2,1)S(1)}, u32[]{:S(2)}, u32[]{:S(2)}) collective-permute-start(bf16[3,2,128,128]{3,2,1,0:T(8,128)(2,1)} %get-tuple-element.50), channel_id=1, source_target_pairs={{0,4},{4,0},{8,12},{12,8},{16,20},{20,16},{24,28},{28,24},{1,5},{5... | collective-permute-start | bytes 589832 | tf_op jit(solution)/shard_map/ppermute | solution.py:441
  12.8 16.1 %collective-permute-start.6 = (bf16[1,512,512]{2,1,0:T(8,128)(2,1)}, bf16[1,512,512]{2,1,0:T(8,128)(2,1)S(1)}, u32[]{:S(2)}, u32[]{:S(2)}) collective-permute-start(bf16[1,512,512]{2,1,0:T(8,128)(2,1)} %get-tuple-element.65), channel_id=1, source_target_pairs={{0,4},{4,0},{8,12},{12,8},{16,20},{20,16},{24,28},{28,24},{1,5},{5... | collective-permute-start | bytes 1572872 | tf_op jit(solution)/shard_map/ppermute | solution.py:441
  14.5 15.9 %copy-start.4 = (bf16[512,512]{1,0:T(8,128)(2,1)S(1)}, bf16[512,512]{1,0:T(8,128)(2,1)}, u32[]{:S(2)}) copy-start(bf16[512,512]{1,0:T(8,128)(2,1)} %k_ref.1) | copy-start | bytes 1572868
  15.3 15.2 %copy-start.2 = (bf16[512,512]{1,0:T(8,128)(2,1)S(1)}, bf16[512,512]{1,0:T(8,128)(2,1)}, u32[]{:S(2)}) copy-start(bf16[512,512]{1,0:T(8,128)(2,1)} %q_ref.1) | copy-start | bytes 1572868
  15.3 13.0 %all-to-all-start = ((bf16[4,2,128,128]{3,2,1,0:T(8,128)(2,1)}), bf16[4,2,128,128]{3,2,1,0:T(8,128)(2,1)S(1)}, u32[]{:S(2)}, u32[]{:S(2)}) async-start(bf16[4,2,128,128]{3,2,1,0:T(8,128)(2,1)} %offer.1), calls=%async_computation | async-start | bytes 524288 | tf_op jit(solution)/shard_map/all_to_all | solution.py:470
  20.3 14.9 %collective-permute-start.4 = (bf16[1,512,512]{2,1,0:T(8,128)(2,1)S(1)}, bf16[1,512,512]{2,1,0:T(8,128)(2,1)S(1)}, u32[]{:S(2)}, u32[]{:S(2)}) collective-permute-start(bf16[1,512,512]{2,1,0:T(8,128)(2,1)S(1)} %get-tuple-element.62.refs_0_), channel_id=1, source_target_pairs={{0,2},{1,3},{2,0},{3,1},{4,6},{5,7},{6,4},{7,5},{8,10},{9,11},{10,... | collective-permute-start | bytes 1572872 | tf_op jit(solution)/shard_map/ppermute | solution.py:444
  28.5 6.1 %collective-permute-start.1 = (bf16[2,2,128,128]{3,2,1,0:T(8,128)(2,1)S(1)}, bf16[2,2,128,128]{3,2,1,0:T(8,128)(2,1)S(1)}, u32[]{:S(2)}, u32[]{:S(2)}) collective-permute-start(bf16[2,2,128,128]{3,2,1,0:T(8,128)(2,1)S(1)} %get-tuple-element.51), channel_id=1, source_target_pairs={{0,4},{4,0},{8,12},{12,8},{16,20},{20,16},{24,28},{28,24},{1,5},{5... | collective-permute-start | bytes 393224 | tf_op jit(solution)/shard_map/ppermute | solution.py:441
  28.9 10.2 %collective-permute-start.14 = (bf16[512,512]{1,0:T(8,128)(2,1)}, bf16[512,512]{1,0:T(8,128)(2,1)}, u32[]{:S(2)}, u32[]{:S(2)}) collective-permute-start(bf16[512,512]{1,0:T(8,128)(2,1)} %refs_0_.3), channel_id=1, source_target_pairs={{0,16},{4,20},{16,24},{20,28},{24,8},{28,12},{8,0},{12,4},{1,17},{... | collective-permute-start | bytes 1572872 | tf_op jit(solution)/shard_map/ppermute | solution.py:457
  28.9 14.8 %collective-permute-start.8 = (bf16[1,512,512]{2,1,0:T(8,128)(2,1)S(1)}, bf16[1,512,512]{2,1,0:T(8,128)(2,1)S(1)}, u32[]{:S(2)}, u32[]{:S(2)}) collective-permute-start(bf16[1,512,512]{2,1,0:T(8,128)(2,1)S(1)} %collective-permute-done.6.refs_4_), channel_id=1, source_target_pairs={{0,2},{1,3},{2,0},{3,1},{4,6},{5,7},{6,4},{7,5},{8,10},{9,11},{10,... | collective-permute-start | bytes 1572872 | tf_op jit(solution)/shard_map/ppermute | solution.py:444
  35.2 8.6 %collective-permute-start.5 = (bf16[1,512,512]{2,1,0:T(8,128)(2,1)S(1)}, bf16[1,512,512]{2,1,0:T(8,128)(2,1)S(1)}, u32[]{:S(2)}, u32[]{:S(2)}) collective-permute-start(bf16[1,512,512]{2,1,0:T(8,128)(2,1)S(1)} %collective-permute-done.4.refs_2_), channel_id=1, source_target_pairs={{0,1},{1,0},{2,3},{3,2},{4,5},{5,4},{6,7},{7,6},{8,9},{9,8},{10,11... | collective-permute-start | bytes 1572872 | tf_op jit(solution)/shard_map/ppermute | solution.py:444
  35.2 21.2 %collective-permute-start.7 = (bf16[1,512,512]{2,1,0:T(8,128)(2,1)S(1)}, bf16[1,512,512]{2,1,0:T(8,128)(2,1)}, u32[]{:S(2)}, u32[]{:S(2)}) collective-permute-start(bf16[1,512,512]{2,1,0:T(8,128)(2,1)S(1)} %collective-permute-done.6.refs_4_), channel_id=1, source_target_pairs={{0,1},{1,0},{2,3},{3,2},{4,5},{5,4},{6,7},{7,6},{8,9},{9,8},{10,11... | collective-permute-start | bytes 1572872 | tf_op jit(solution)/shard_map/ppermute | solution.py:444
  35.7 20.7 %collective-permute-start.3 = (bf16[1,512,512]{2,1,0:T(8,128)(2,1)S(1)}, bf16[1,512,512]{2,1,0:T(8,128)(2,1)}, u32[]{:S(2)}, u32[]{:S(2)}) collective-permute-start(bf16[1,512,512]{2,1,0:T(8,128)(2,1)S(1)} %get-tuple-element.62.refs_0_), channel_id=1, source_target_pairs={{0,1},{1,0},{2,3},{3,2},{4,5},{5,4},{6,7},{7,6},{8,9},{9,8},{10,11... | collective-permute-start | bytes 1572872 | tf_op jit(solution)/shard_map/ppermute | solution.py:444
  39.1 17.3 %collective-permute-start.2 = (bf16[512,512]{1,0:T(8,128)(2,1)S(1)}, bf16[512,512]{1,0:T(8,128)(2,1)S(1)}, u32[]{:S(2)}, u32[]{:S(2)}) collective-permute-start(bf16[512,512]{1,0:T(8,128)(2,1)S(1)} %finish_value.1.a_ref.x_ref), channel_id=1, source_target_pairs={{0,4},{4,0},{8,12},{12,8},{16,20},{20,16},{24,28},{28,24},{1,5},{5... | collective-permute-start | bytes 1572872 | tf_op jit(solution)/shard_map/ppermute | solution.py:441
  43.8 12.6 %collective-permute-start.9 = (bf16[1,512,512]{2,1,0:T(8,128)(2,1)S(1)}, bf16[1,512,512]{2,1,0:T(8,128)(2,1)}, u32[]{:S(2)}, u32[]{:S(2)}) collective-permute-start(bf16[1,512,512]{2,1,0:T(8,128)(2,1)S(1)} %collective-permute-done.8.refs_6_), channel_id=1, source_target_pairs={{0,1},{1,0},{2,3},{3,2},{4,5},{5,4},{6,7},{7,6},{8,9},{9,8},{10,11... | collective-permute-start | bytes 1572872 | tf_op jit(solution)/shard_map/ppermute | solution.py:444
  44.6 14.8 %collective-permute-start.15 = (bf16[512,512]{1,0:T(8,128)(2,1)}, bf16[512,512]{1,0:T(8,128)(2,1)}, u32[]{:S(2)}, u32[]{:S(2)}) collective-permute-start(bf16[512,512]{1,0:T(8,128)(2,1)} %collective-permute-done.14.refs_1_), channel_id=1, source_target_pairs={{0,16},{4,20},{16,24},{20,28},{24,8},{28,12},{8,0},{12,4},{1,17},{... | collective-permute-start | bytes 1572872 | tf_op jit(solution)/shard_map/ppermute | solution.py:457
  58.4 4.9 %collective-permute-start.11 = (bf16[512,512]{1,0:T(8,128)(2,1)S(1)}, bf16[512,512]{1,0:T(8,128)(2,1)S(1)}, u32[]{:S(2)}, u32[]{:S(2)}) collective-permute-start(bf16[512,512]{1,0:T(8,128)(2,1)S(1)} %collective-permute-done.2.b_ref.x_ref), channel_id=1, source_target_pairs={{0,1},{1,0},{2,3},{3,2},{4,5},{5,4},{6,7},{7,6},{8,9},{9,8},{10,11... | collective-permute-start | bytes 1572872 | tf_op jit(solution)/shard_map/ppermute | solution.py:444
  59.4 14.8 %collective-permute-start.16 = (bf16[512,512]{1,0:T(8,128)(2,1)}, bf16[512,512]{1,0:T(8,128)(2,1)S(1)}, u32[]{:S(2)}, u32[]{:S(2)}) collective-permute-start(bf16[512,512]{1,0:T(8,128)(2,1)} %collective-permute-done.15.refs_2_), channel_id=1, source_target_pairs={{0,16},{4,20},{16,24},{20,28},{24,8},{28,12},{8,0},{12,4},{1,17},{... | collective-permute-start | bytes 1572872 | tf_op jit(solution)/shard_map/ppermute | solution.py:457
  62.8 21.0 %collective-permute-start.18 = (bf16[512,512]{1,0:T(8,128)(2,1)}, bf16[512,512]{1,0:T(8,128)(2,1)S(1)}, u32[]{:S(2)}, u32[]{:S(2)}) collective-permute-start(bf16[512,512]{1,0:T(8,128)(2,1)} %collective-permute-done.14.refs_1_), channel_id=1, source_target_pairs={{0,1},{1,0},{2,3},{3,2},{4,5},{5,4},{6,7},{7,6},{8,9},{9,8},{10,11... | collective-permute-start | bytes 1572872 | tf_op jit(solution)/shard_map/ppermute | solution.py:444
  62.8 21.0 %collective-permute-start.17 = (bf16[512,512]{1,0:T(8,128)(2,1)S(1)}, bf16[512,512]{1,0:T(8,128)(2,1)S(1)}, u32[]{:S(2)}, u32[]{:S(2)}) collective-permute-start(bf16[512,512]{1,0:T(8,128)(2,1)S(1)} %copy-done.12), channel_id=1, source_target_pairs={{0,1},{1,0},{2,3},{3,2},{4,5},{5,4},{6,7},{7,6},{8,9},{9,8},{10,11... | collective-permute-start | bytes 1572872 | tf_op jit(solution)/shard_map/ppermute | solution.py:444
  63.3 20.5 %collective-permute-start.19 = (bf16[512,512]{1,0:T(8,128)(2,1)}, bf16[512,512]{1,0:T(8,128)(2,1)S(1)}, u32[]{:S(2)}, u32[]{:S(2)}) collective-permute-start(bf16[512,512]{1,0:T(8,128)(2,1)} %collective-permute-done.15.refs_2_), channel_id=1, source_target_pairs={{0,1},{1,0},{2,3},{3,2},{4,5},{5,4},{6,7},{7,6},{8,9},{9,8},{10,11... | collective-permute-start | bytes 1572872 | tf_op jit(solution)/shard_map/ppermute | solution.py:444
  74.2 9.6 %collective-permute-start.20 = (bf16[512,512]{1,0:T(8,128)(2,1)S(1)}, bf16[512,512]{1,0:T(8,128)(2,1)S(1)}, u32[]{:S(2)}, u32[]{:S(2)}) collective-permute-start(bf16[512,512]{1,0:T(8,128)(2,1)S(1)} %collective-permute-done.16.refs_3_), channel_id=1, source_target_pairs={{0,1},{1,0},{2,3},{3,2},{4,5},{5,4},{6,7},{7,6},{8,9},{9,8},{10,11... | collective-permute-start | bytes 1572872 | tf_op jit(solution)/shard_map/ppermute | solution.py:444
  74.2 9.5 %collective-permute-start.10 = (bf16[256,512]{1,0:T(8,128)(2,1)S(1)}, bf16[256,512]{1,0:T(8,128)(2,1)S(1)}, u32[]{:S(2)}, u32[]{:S(2)}) collective-permute-start(bf16[256,512]{1,0:T(8,128)(2,1)S(1)} %get-tuple-element.67), channel_id=1, source_target_pairs={{0,16},{4,20},{16,24},{20,28},{24,8},{28,12},{8,0},{12,4},{1,17},{... | collective-permute-start | bytes 786440 | tf_op jit(solution)/shard_map/ppermute | solution.py:457
  83.7 17.2 %collective-permute-start.21 = (bf16[512,512]{1,0:T(8,128)(2,1)S(1)}, bf16[512,512]{1,0:T(8,128)(2,1)S(1)}, u32[]{:S(2)}, u32[]{:S(2)}) collective-permute-start(bf16[512,512]{1,0:T(8,128)(2,1)S(1)} %finish_value.1.a_ref.x_ref), channel_id=1, source_target_pairs={{0,1},{1,0},{2,3},{3,2},{4,5},{5,4},{6,7},{7,6},{8,9},{9,8},{10,11... | collective-permute-start | bytes 1572872 | tf_op jit(solution)/shard_map/ppermute | solution.py:444
  84.9 19.7 %collective-permute-start.24 = (bf16[512,512]{1,0:T(8,128)(2,1)S(1)}, bf16[512,512]{1,0:T(8,128)(2,1)S(1)}, u32[]{:S(2)}, u32[]{:S(2)}) collective-permute-start(bf16[512,512]{1,0:T(8,128)(2,1)S(1)} %head_part.3), channel_id=1, source_target_pairs={{0,2},{1,3},{2,0},{3,1},{4,6},{5,7},{6,4},{7,5},{8,10},{9,11},{10,... | collective-permute-start | bytes 1572872 | tf_op jit(solution)/shard_map/ppermute | solution.py:444
  86.5 10.9 %collective-permute-start.13 = (bf16[256,512]{1,0:T(8,128)(2,1)S(1)}, bf16[256,512]{1,0:T(8,128)(2,1)S(1)}, u32[]{:S(2)}, u32[]{:S(2)}) collective-permute-start(bf16[256,512]{1,0:T(8,128)(2,1)S(1)} %get-tuple-element.71), channel_id=1, source_target_pairs={{0,16},{4,20},{16,24},{20,28},{24,8},{28,12},{8,0},{12,4},{1,17},{... | collective-permute-start | bytes 786440 | tf_op jit(solution)/shard_map/ppermute | solution.py:457
  90.7 13.7 %collective-permute-start.12 = (bf16[256,512]{1,0:T(8,128)(2,1)S(1)}, bf16[256,512]{1,0:T(8,128)(2,1)S(1)}, u32[]{:S(2)}, u32[]{:S(2)}) collective-permute-start(bf16[256,512]{1,0:T(8,128)(2,1)S(1)} %add_own.4), channel_id=1, source_target_pairs={{0,16},{4,20},{16,24},{20,28},{24,8},{28,12},{8,0},{12,4},{1,17},{... | collective-permute-start | bytes 786440 | tf_op jit(solution)/shard_map/ppermute | solution.py:457
  97.4 11.2 %collective-permute-start.23 = (bf16[256,512]{1,0:T(8,128)(2,1)S(1)}, bf16[256,512]{1,0:T(8,128)(2,1)S(1)}, u32[]{:S(2)}, u32[]{:S(2)}) collective-permute-start(bf16[256,512]{1,0:T(8,128)(2,1)S(1)} %add_own.5), channel_id=1, source_target_pairs={{0,16},{4,20},{16,24},{20,28},{24,8},{28,12},{8,0},{12,4},{1,17},{... | collective-permute-start | bytes 786440 | tf_op jit(solution)/shard_map/ppermute | solution.py:457
  101.6 18.8 %collective-permute-start.26 = (bf16[512,512]{1,0:T(8,128)(2,1)S(1)}, bf16[512,512]{1,0:T(8,128)(2,1)S(1)}, u32[]{:S(2)}, u32[]{:S(2)}) collective-permute-start(bf16[512,512]{1,0:T(8,128)(2,1)S(1)} %head_part.4), channel_id=1, source_target_pairs={{0,2},{1,3},{2,0},{3,1},{4,6},{5,7},{6,4},{7,5},{8,10},{9,11},{10,... | collective-permute-start | bytes 1572872 | tf_op jit(solution)/shard_map/ppermute | solution.py:444
  105.3 15.1 %collective-permute-start.27 = (bf16[512,512]{1,0:T(8,128)(2,1)S(1)}, bf16[512,512]{1,0:T(8,128)(2,1)S(1)}, u32[]{:S(2)}, u32[]{:S(2)}) collective-permute-start(bf16[512,512]{1,0:T(8,128)(2,1)S(1)} %head_part.5), channel_id=1, source_target_pairs={{0,4},{4,0},{8,12},{12,8},{16,20},{20,16},{24,28},{28,24},{1,5},{5... | collective-permute-start | bytes 1572872 | tf_op jit(solution)/shard_map/ppermute | solution.py:441
  105.9 9.2 %collective-permute-start.22 = (bf16[256,512]{1,0:T(8,128)(2,1)S(1)}, bf16[256,512]{1,0:T(8,128)(2,1)S(1)}, u32[]{:S(2)}, u32[]{:S(2)}) collective-permute-start(bf16[256,512]{1,0:T(8,128)(2,1)S(1)} %add_own.6), channel_id=1, source_target_pairs={{0,16},{4,20},{16,24},{20,28},{24,8},{28,12},{8,0},{12,4},{1,17},{... | collective-permute-start | bytes 786440 | tf_op jit(solution)/shard_map/ppermute | solution.py:457
  108.7 10.4 %collective-permute-start.25 = (bf16[256,512]{1,0:T(8,128)(2,1)S(1)}, bf16[256,512]{1,0:T(8,128)(2,1)S(1)}, u32[]{:S(2)}, u32[]{:S(2)}) collective-permute-start(bf16[256,512]{1,0:T(8,128)(2,1)S(1)} %add_own.7), channel_id=1, source_target_pairs={{0,16},{4,20},{16,24},{20,28},{24,8},{28,12},{8,0},{12,4},{1,17},{... | collective-permute-start | bytes 786440 | tf_op jit(solution)/shard_map/ppermute | solution.py:457
  (11 other events, 30.5 us)

commit v16 on v14

--- a/solution.py
+++ b/solution.py
@@ -325,12 +325,16 @@
     out_ref[...] = (moved_ref[...].astype(F32) + own_ref[...]).astype(BF16)
 
 
-def add_own(moved, own):
+def add_own(moved, part, own):
     return call(
         add_kernel,
-        in_specs=[VMEM] * 2,
-        out_specs=VMEM,
-        out_shape=jax.ShapeDtypeStruct(moved.shape, BF16),
+        grid=(1,),
+        in_specs=[
+            pl.BlockSpec(own.shape, lambda s: (part, 0)),
+            pl.BlockSpec(own.shape, lambda s: (0, 0)),
+        ],
+        out_specs=pl.BlockSpec(own.shape, lambda s: (0, 0)),
+        out_shape=jax.ShapeDtypeStruct(own.shape, BF16),
         name="add_own",
     )(moved, own)
 
@@ -489,7 +493,7 @@
     offsets = [0]
     bit = n_head // 2
     while bit:
-        own = own + [across(r, bit) for r in own]
+        own = own + [across(after(r, mine) if len(own) > 1 else r, bit) for r in own]
         theirs = theirs + [across(r, bit) for r in theirs]
         offsets = offsets + [o ^ bit for o in offsets]
         bit //= 2
@@ -499,12 +503,12 @@
 
     chains = 2
 
-    def piece(dtype, step, token, flops=1):
+    def piece(dtype, step, token, chains=chains, flops=1):
         vals = (spot, here, after(mine, token), other, own, theirs)
         return pieces(dtype, chains, flops, order, per, step, *vals)
 
-    total = piece(BF16, 0, query_grad, 4 * length * cols * width)
-    moved = [ring(x) for x in total]
+    total = piece(BF16, 0, query_grad, 1, 4 * length * cols * width)
+    moved = [ring(total[0])] * chains
     other_too = across(other, 1)
     lent.append(across(after(blocks[-1], total[0]), 1))
     local_part = piece(F32, 1, total[0])
@@ -530,7 +534,8 @@
             if step == pairs - 2 and i == chains - 1:
                 lead = (here, after(other, token), other_too, weight, borrowed)
                 token = part = head_part(*lead, got_other)
-            token = add_own(moved[i], after(local_part[i], token))
+            at = i if step == 1 else 0
+            token = add_own(moved[i], at, after(local_part[i], token))
             moved[i] = ring(token)
         if step < pairs - 2:
             local_part = piece(F32, step + 1, token)

time: 103 us -> 105 us (1.019)
  waiting for transfers between devices: 27.9 us -> 29.9 us
    ppermute x9 -> x8, waiting for transfers between devices: 12.5 us -> 20.3 us  [ring(): return lax.ppermute(x, 'ctx', moves)]
    ppermute x14, waiting for transfers between devices: 5.52 us -> 1 us  [across(): return lax.ppermute(x, 'head', [(i, i ^ bit) for i in range(n_head)])]
    ppermute x9 -> x8, starting transfers between devices: 20.9 us -> 19 us  [ring(): return lax.ppermute(x, 'ctx', moves)]
    ppermute x5, waiting for transfers between devices: 2.87 us -> 1.56 us  [partner(): return lax.ppermute(x, 'ctx', [(i, i ^ 1) for i in range(n_ctx)])]
    unnamed x30 -> x34, local copies, waits for them, and re-layouts: 7.77 us -> 8.57 us
  transfers between devices with their start and end apart: 29 -> 28, of which waited for: 10 -> 9; matrix products, arithmetic and copies ran while one was open for 0% -> 0% of each run, Pallas kernels for 20% -> 19%
where the time goes in v16:
time: 105 us; the launch traced here: 104 us
  starting transfers between devices  39.2 us (37%)
  waiting for transfers between devices  29.9 us (28%)
  Pallas kernels  25.6 us (24%)
  local copies, waits for them, and re-layouts  8.57 us (8%)
    ppermute x8, waiting for transfers between devices, ring(): return lax.ppermute(x, 'ctx', moves)  20.3 us
    ppermute x8, starting transfers between devices, ring(): return lax.ppermute(x, 'ctx', moves)  19 us
    unnamed x34, local copies, waits for them, and re-layouts  8.57 us
    ppermute x14, starting transfers between devices, across(): return lax.ppermute(x, 'head', [(i, i ^ bit) for i in range(n_head)])  7.77 us
    ppermute x5, starting transfers between devices, partner(): return lax.ppermute(x, 'ctx', [(i, i ^ 1) for i in range(n_ctx)])  7.44 us
    all_to_all x1, waiting for transfers between devices, local(): lax.all_to_all(offered, 'ctx', split_axis=0, concat_axis=0, axis_index_gr...  6.98 us
    pallas_call x4, Pallas kernels, pieces(): call(functools.partial(piece_kernel, order, per, step, count), flops=flop...  5.21 us
    all_to_all x1, starting transfers between devices, local(): lax.all_to_all(offered, 'ctx', split_axis=0, concat_axis=0, axis_index_gr...  5 us
  transfers between devices with their start and end apart: 28, of which 9 were waited for; matrix products, arithmetic and copies ran while one was open for 0% of the time, Pallas kernels for 19%

profile of v16, /device:TPU:0, one launch (start us, length us, event | category | flops | bytes accessed | tf_op | source)
XLA Modules:
  0.0 104.1 jit_solution(12538901221988258331)
XLA Ops:
  0.7 4.0 %states.1 = (f32[2,2,128,128]{3,2,1,0:T(8,128)}, bf16[3,2,128,128]{3,2,1,0:T(8,128)(2,1)}) custom-call(s32[1]{0:T(128)} %bitcast.par_ref, bf16[512,512]{1,0:T(8,128)(2,1)} %q_ref.1, bf16[512,512]{1,0:T(8,128)(2,1)} %k_ref.1, bf16[512,512]{1,0:T(8,128)(2,1)} %v_ref, bf16[512,512]{1,0:T(8,128)(2,1)} %g_ref.1), custom_call_target="tpu_custom_call" | custom-call | flops 1 | bytes 1 | tf_op jit(solution)/shard_map/states/pallas_call | solution.py:67
  4.7 3.0 %collective-permute-start = (bf16[3,2,128,128]{3,2,1,0:T(8,128)(2,1)}, bf16[3,2,128,128]{3,2,1,0:T(8,128)(2,1)S(1)}, u32[]{:S(2)}, u32[]{:S(2)}) collective-permute-start(bf16[3,2,128,128]{3,2,1,0:T(8,128)(2,1)} %get-tuple-element.48), channel_id=1, source_target_pairs={{0,4},{4,0},{8,12},{12,8},{16,20},{20,16},{24,28},{28,24},{1,5},{5... | collective-permute-start | bytes 589832 | tf_op jit(solution)/shard_map/ppermute | solution.py:445
  7.7 2.6 %collective-permute-start.12 = (bf16[512,512]{1,0:T(8,128)(2,1)}, bf16[512,512]{1,0:T(8,128)(2,1)}, u32[]{:S(2)}, u32[]{:S(2)}) collective-permute-start(bf16[512,512]{1,0:T(8,128)(2,1)} %refs_0_.3), channel_id=1, source_target_pairs={{0,16},{4,20},{16,24},{20,28},{24,8},{28,12},{8,0},{12,4},{1,17},{... | collective-permute-start | bytes 1572872 | tf_op jit(solution)/shard_map/ppermute | solution.py:461
  11.2 1.6 %collective-permute-done.got_ref.refs_2_ = bf16[3,2,128,128]{3,2,1,0:T(8,128)(2,1)S(1)} collective-permute-done((bf16[3,2,128,128]{3,2,1,0:T(8,128)(2,1)}, bf16[3,2,128,128]{3,2,1,0:T(8,128)(2,1)S(1)}, u32[]{:S(2)}, u32[]{:S(2)}) %collective-permute-start) | collective-permute-done | bytes 196640 | tf_op jit(solution)/shard_map/ppermute | solution.py:445
  12.8 1.7 %collective-permute-start.6 = (bf16[1,512,512]{2,1,0:T(8,128)(2,1)}, bf16[1,512,512]{2,1,0:T(8,128)(2,1)S(1)}, u32[]{:S(2)}, u32[]{:S(2)}) collective-permute-start(bf16[1,512,512]{2,1,0:T(8,128)(2,1)} %get-tuple-element.63), channel_id=1, source_target_pairs={{0,4},{4,0},{8,12},{12,8},{16,20},{20,16},{24,28},{28,24},{1,5},{5... | collective-permute-start | bytes 1572872 | tf_op jit(solution)/shard_map/ppermute | solution.py:445
  15.3 5.0 %all-to-all-start = ((bf16[4,2,128,128]{3,2,1,0:T(8,128)(2,1)}), bf16[4,2,128,128]{3,2,1,0:T(8,128)(2,1)S(1)}, u32[]{:S(2)}, u32[]{:S(2)}) async-start(bf16[4,2,128,128]{3,2,1,0:T(8,128)(2,1)} %offer.1), calls=%async_computation | async-start | bytes 524288 | tf_op jit(solution)/shard_map/all_to_all | solution.py:474
  20.3 1.5 %collective-permute-start.4 = (bf16[1,512,512]{2,1,0:T(8,128)(2,1)S(1)}, bf16[1,512,512]{2,1,0:T(8,128)(2,1)S(1)}, u32[]{:S(2)}, u32[]{:S(2)}) collective-permute-start(bf16[1,512,512]{2,1,0:T(8,128)(2,1)S(1)} %get-tuple-element.60.refs_0_), channel_id=1, source_target_pairs={{0,2},{1,3},{2,0},{3,1},{4,6},{5,7},{6,4},{7,5},{8,10},{9,11},{10,... | collective-permute-start | bytes 1572872 | tf_op jit(solution)/shard_map/ppermute | solution.py:448
  21.8 7.0 %all-to-all-done.every_ref = bf16[4,2,128,128]{3,2,1,0:T(8,128)(2,1)S(1)} async-done(((bf16[4,2,128,128]{3,2,1,0:T(8,128)(2,1)}), bf16[4,2,128,128]{3,2,1,0:T(8,128)(2,1)S(1)}, u32[]{:S(2)}, u32[]{:S(2)}) %all-to-all-start) | async-done | bytes 262176 | tf_op jit(solution)/shard_map/all_to_all | solution.py:474
  30.4 1.5 %collective-permute-start.8 = (bf16[1,512,512]{2,1,0:T(8,128)(2,1)S(1)}, bf16[1,512,512]{2,1,0:T(8,128)(2,1)S(1)}, u32[]{:S(2)}, u32[]{:S(2)}) collective-permute-start(bf16[1,512,512]{2,1,0:T(8,128)(2,1)S(1)} %collective-permute-done.6.refs_4_), channel_id=1, source_target_pairs={{0,2},{1,3},{2,0},{3,1},{4,6},{5,7},{6,4},{7,5},{8,10},{9,11},{10,... | collective-permute-start | bytes 1572872 | tf_op jit(solution)/shard_map/ppermute | solution.py:448
  31.9 1.0 copy-done.10
  33.0 3.0 %inside.1 = (f32[512,512]{1,0:T(8,128)S(1)}, bf16[512,512]{1,0:T(8,128)(2,1)S(1)}) custom-call(bf16[512,512]{1,0:T(8,128)(2,1)S(1)} %copy-done.6, bf16[512,512]{1,0:T(8,128)(2,1)S(1)} %copy-done.8, bf16[512,512]{1,0:T(8,128)(2,1)S(1)} %copy-done.10), custom_call_target="tpu_custom_call" | custom-call | flops 1 | bytes 1 | tf_op jit(solution)/shard_map/inside/pallas_call | solution.py:147
  37.2 4.3 %collective-permute-done.13.refs_2_ = bf16[512,512]{1,0:T(8,128)(2,1)} collective-permute-done((bf16[512,512]{1,0:T(8,128)(2,1)}, bf16[512,512]{1,0:T(8,128)(2,1)}, u32[]{:S(2)}, u32[]{:S(2)}) %collective-permute-start.13) | collective-permute-done | bytes 524320 | tf_op jit(solution)/shard_map/ppermute | solution.py:461
  41.4 1.5 %collective-permute-start.2 = (bf16[512,512]{1,0:T(8,128)(2,1)S(1)}, bf16[512,512]{1,0:T(8,128)(2,1)S(1)}, u32[]{:S(2)}, u32[]{:S(2)}) collective-permute-start(bf16[512,512]{1,0:T(8,128)(2,1)S(1)} %finish_value.1.a_ref.x_ref), channel_id=1, source_target_pairs={{0,4},{4,0},{8,12},{12,8},{16,20},{20,16},{24,28},{28,24},{1,5},{5... | collective-permute-start | bytes 1572872 | tf_op jit(solution)/shard_map/ppermute | solution.py:445
  44.7 2.6 %collective-permute-start.14 = (bf16[512,512]{1,0:T(8,128)(2,1)}, bf16[512,512]{1,0:T(8,128)(2,1)}, u32[]{:S(2)}, u32[]{:S(2)}) collective-permute-start(bf16[512,512]{1,0:T(8,128)(2,1)} %collective-permute-done.13.refs_2_), channel_id=1, source_target_pairs={{0,16},{4,20},{16,24},{20,28},{24,8},{28,12},{8,0},{12,4},{1,17},{... | collective-permute-start | bytes 1572872 | tf_op jit(solution)/shard_map/ppermute | solution.py:461
  49.4 1.0 copy-done.7
  54.6 4.1 %others.1 = (bf16[512,512]{1,0:T(8,128)(2,1)}, bf16[512,512]{1,0:T(8,128)(2,1)}) custom-call(s32[1]{0:T(128)} %bitcast.par_ref, bf16[512,512]{1,0:T(8,128)(2,1)S(1)} %copy-done.7, bf16[512,512]{1,0:T(8,128)(2,1)S(1)} %copy-done.9, bf16[512,512]{1,0:T(8,128)(2,1)S(1)} %copy-done.12, bf16[512,512]{1,0:T(8,128)(2,1)S(1)} %copy-done.11, ...), custom_call_target="tpu_custom_call" | custom-call | flops 1 | bytes 1 | tf_op jit(solution)/shard_map/others/pallas_call | solution.py:246
  58.9 1.2 %pieces.4 = bf16[512,512]{1,0:T(8,128)(2,1)S(1)} custom-call(s32[1]{0:T(128)} %bitcast.3.spot_ref, s32[1]{0:T(128)} %bitcast.2.head_ref.at_ref, bf16[512,512]{1,0:T(8,128)(2,1)S(1)} %finish_value.1.a_ref.x_ref, bf16[512,512]{1,0:T(8,128)(2,1)S(1)} %collective-permute-done.2.b_ref.x_ref, bf16[1,512,512]{2,1,0:T(8,128)(2,1)S(1)} %get-tuple-element.60.refs_0_, ...), custom_call_target="tpu_custom_call" | custom-call | flops 536870912 | bytes 1 | tf_op jit(solution)/shard_map/pieces/pallas_call | solution.py:291
  60.9 2.5 %collective-permute-start.10 = (bf16[512,512]{1,0:T(8,128)(2,1)S(1)}, bf16[512,512]{1,0:T(8,128)(2,1)S(1)}, u32[]{:S(2)}, u32[]{:S(2)}) collective-permute-start(bf16[512,512]{1,0:T(8,128)(2,1)S(1)} %pieces.4), channel_id=1, source_target_pairs={{0,16},{4,20},{16,24},{20,28},{24,8},{28,12},{8,0},{12,4},{1,17},{... | collective-permute-start | bytes 1572872 | tf_op jit(solution)/shard_map/ppermute | solution.py:461
  63.5 1.8 %pieces.5 = (f32[256,512]{1,0:T(8,128)S(1)}, f32[256,512]{1,0:T(8,128)S(1)}) custom-call(s32[1]{0:T(128)} %bitcast.3.spot_ref, s32[1]{0:T(128)} %bitcast.2.head_ref.at_ref, bf16[512,512]{1,0:T(8,128)(2,1)S(1)} %finish_value.1.a_ref.x_ref, bf16[512,512]{1,0:T(8,128)(2,1)S(1)} %collective-permute-done.2.b_ref.x_ref, ...), custom_call_target="tpu_custom_call" | custom-call | flops 1 | bytes 1 | tf_op jit(solution)/shard_map/pieces/pallas_call | solution.py:291
  65.3 1.5 %arrange.1 = (bf16[2,512,512]{2,1,0:T(8,128)(2,1)S(1)}, bf16[2,512,512]{2,1,0:T(8,128)(2,1)S(1)}) custom-call(s32[1]{0:T(128)} %bitcast.2.head_ref.at_ref, s32[1]{0:T(128)} %bitcast.3.spot_ref, bf16[512,512]{1,0:T(8,128)(2,1)} %refs_0_.3, bf16[512,512]{1,0:T(8,128)(2,1)} %collective-permute-done.12.refs_1_, ...), custom_call_target="tpu_custom_call" | custom-call | flops 1 | bytes 1 | tf_op jit(solution)/shard_map/arrange/pallas_call | solution.py:371
  69.2 6.1 %collective-permute-done.10.moved_ref = bf16[512,512]{1,0:T(8,128)(2,1)S(1)} collective-permute-done((bf16[512,512]{1,0:T(8,128)(2,1)S(1)}, bf16[512,512]{1,0:T(8,128)(2,1)S(1)}, u32[]{:S(2)}, u32[]{:S(2)}) %collective-permute-start.10) | collective-permute-done | bytes 524320 | tf_op jit(solution)/shard_map/ppermute | solution.py:461
  75.3 3.4 %collective-permute-start.20 = (bf16[256,512]{1,0:T(8,128)(2,1)S(1)}, bf16[256,512]{1,0:T(8,128)(2,1)S(1)}, u32[]{:S(2)}, u32[]{:S(2)}) collective-permute-start(bf16[256,512]{1,0:T(8,128)(2,1)S(1)} %add_own.4), channel_id=1, source_target_pairs={{0,16},{4,20},{16,24},{20,28},{24,8},{28,12},{8,0},{12,4},{1,17},{... | collective-permute-start | bytes 786440 | tf_op jit(solution)/shard_map/ppermute | solution.py:461
  78.9 1.6 %collective-permute-start.25 = (bf16[512,512]{1,0:T(8,128)(2,1)S(1)}, bf16[512,512]{1,0:T(8,128)(2,1)S(1)}, u32[]{:S(2)}, u32[]{:S(2)}) collective-permute-start(bf16[512,512]{1,0:T(8,128)(2,1)S(1)} %head_part.4), channel_id=1, source_target_pairs={{0,2},{1,3},{2,0},{3,1},{4,6},{5,7},{6,4},{7,5},{8,10},{9,11},{10,... | collective-permute-start | bytes 1572872 | tf_op jit(solution)/shard_map/ppermute | solution.py:448
  80.4 1.1 %pieces.6 = (f32[256,512]{1,0:T(8,128)S(1)}, f32[256,512]{1,0:T(8,128)S(1)}) custom-call(s32[1]{0:T(128)} %bitcast.3.spot_ref, s32[1]{0:T(128)} %bitcast.2.head_ref.at_ref, bf16[512,512]{1,0:T(8,128)(2,1)S(1)} %finish_value.1.a_ref.x_ref, bf16[512,512]{1,0:T(8,128)(2,1)S(1)} %collective-permute-done.2.b_ref.x_ref, ...), custom_call_target="tpu_custom_call" | custom-call | flops 1 | bytes 1 | tf_op jit(solution)/shard_map/pieces/pallas_call | solution.py:291
  81.6 1.1 %pieces.7 = (f32[256,512]{1,0:T(8,128)S(1)}, f32[256,512]{1,0:T(8,128)S(1)}) custom-call(s32[1]{0:T(128)} %bitcast.3.spot_ref, s32[1]{0:T(128)} %bitcast.2.head_ref.at_ref, bf16[512,512]{1,0:T(8,128)(2,1)S(1)} %finish_value.1.a_ref.x_ref, bf16[512,512]{1,0:T(8,128)(2,1)S(1)} %collective-permute-done.2.b_ref.x_ref, ...), custom_call_target="tpu_custom_call" | custom-call | flops 1 | bytes 1 | tf_op jit(solution)/shard_map/pieces/pallas_call | solution.py:291
  82.7 2.8 %collective-permute-done.20.moved_ref = bf16[256,512]{1,0:T(8,128)(2,1)S(1)} collective-permute-done((bf16[256,512]{1,0:T(8,128)(2,1)S(1)}, bf16[256,512]{1,0:T(8,128)(2,1)S(1)}, u32[]{:S(2)}, u32[]{:S(2)}) %collective-permute-start.20) | collective-permute-done | bytes 262176 | tf_op jit(solution)/shard_map/ppermute | solution.py:461
  86.9 3.4 %collective-permute-start.21 = (bf16[256,512]{1,0:T(8,128)(2,1)S(1)}, bf16[256,512]{1,0:T(8,128)(2,1)S(1)}, u32[]{:S(2)}, u32[]{:S(2)}) collective-permute-start(bf16[256,512]{1,0:T(8,128)(2,1)S(1)} %add_own.6), channel_id=1, source_target_pairs={{0,16},{4,20},{16,24},{20,28},{24,8},{28,12},{8,0},{12,4},{1,17},{... | collective-permute-start | bytes 786440 | tf_op jit(solution)/shard_map/ppermute | solution.py:461
  91.1 3.4 %collective-permute-start.24 = (bf16[256,512]{1,0:T(8,128)(2,1)S(1)}, bf16[256,512]{1,0:T(8,128)(2,1)S(1)}, u32[]{:S(2)}, u32[]{:S(2)}) collective-permute-start(bf16[256,512]{1,0:T(8,128)(2,1)S(1)} %add_own.7), channel_id=1, source_target_pairs={{0,16},{4,20},{16,24},{20,28},{24,8},{28,12},{8,0},{12,4},{1,17},{... | collective-permute-start | bytes 786440 | tf_op jit(solution)/shard_map/ppermute | solution.py:461
  94.6 2.5 %collective-permute-done.21.refs_0_ = bf16[256,512]{1,0:T(8,128)(2,1)S(1)} collective-permute-done((bf16[256,512]{1,0:T(8,128)(2,1)S(1)}, bf16[256,512]{1,0:T(8,128)(2,1)S(1)}, u32[]{:S(2)}, u32[]{:S(2)}) %collective-permute-start.21) | collective-permute-done | bytes 262176 | tf_op jit(solution)/shard_map/ppermute | solution.py:461
  97.0 3.9 %collective-permute-done.24.refs_1_ = bf16[256,512]{1,0:T(8,128)(2,1)S(1)} collective-permute-done((bf16[256,512]{1,0:T(8,128)(2,1)S(1)}, bf16[256,512]{1,0:T(8,128)(2,1)S(1)}, u32[]{:S(2)}, u32[]{:S(2)}) %collective-permute-start.24) | collective-permute-done | bytes 262176 | tf_op jit(solution)/shard_map/ppermute | solution.py:461
  101.0 1.3 %finish_weight.1 = f32[512,512]{1,0:T(8,128)} custom-call(bf16[256,512]{1,0:T(8,128)(2,1)S(1)} %collective-permute-done.21.refs_0_, bf16[256,512]{1,0:T(8,128)(2,1)S(1)} %collective-permute-done.24.refs_1_, f32[256,512]{1,0:T(8,128)S(1)} %get-tuple-element.83.refs_2_, f32[256,512]{1,0:T(8,128)S(1)} %get-tuple-element.88.refs_3_), custom_call_target="tpu_custom_call" | custom-call | flops 1 | bytes 1 | tf_op jit(solution)/shard_map/finish_weight/pallas_call | solution.py:315
  102.3 1.8 %join.1 = bf16[512,1024]{1,0:T(8,128)(2,1)} custom-call(s32[1]{0:T(128)} %bitcast.par_ref, s32[1]{0:T(128)} %bitcast.2.head_ref.at_ref, bf16[512,512]{1,0:T(8,128)(2,1)S(1)} %finish_value.1.a_ref.x_ref, bf16[512,512]{1,0:T(8,128)(2,1)S(1)} %collective-permute-done.19.y_ref, bf16[2,512,512]{2,1,0:T(8,128)(2,1)S(1)} %get-tuple-element.74.w_ref, ...), custom_call_target="tpu_custom_call" | custom-call | flops 1 | bytes 1 | tf_op jit(solution)/shard_map/join/pallas_call | solution.py:422
  (79 shorter events, 18.3 us)
Async XLA Ops:
  0.6 9.6 %copy-start.15 = (bf16[512,1024]{1,0:T(8,128)(2,1)S(1)}, bf16[512,1024]{1,0:T(8,128)(2,1)}, u32[]{:S(2)}) copy-start(bf16[512,1024]{1,0:T(8,128)(2,1)} %x_ref.1) | copy-start | bytes 3145732
  4.7 9.9 %copy-start.16 = (f32[2,2,128,128]{3,2,1,0:T(8,128)S(1)}, f32[2,2,128,128]{3,2,1,0:T(8,128)}, u32[]{:S(2)}) copy-start(f32[2,2,128,128]{3,2,1,0:T(8,128)} %get-tuple-element.47.keep_ref) | copy-start | bytes 786436
  4.7 8.1 %collective-permute-start = (bf16[3,2,128,128]{3,2,1,0:T(8,128)(2,1)}, bf16[3,2,128,128]{3,2,1,0:T(8,128)(2,1)S(1)}, u32[]{:S(2)}, u32[]{:S(2)}) collective-permute-start(bf16[3,2,128,128]{3,2,1,0:T(8,128)(2,1)} %get-tuple-element.48), channel_id=1, source_target_pairs={{0,4},{4,0},{8,12},{12,8},{16,20},{20,16},{24,28},{28,24},{1,5},{5... | collective-permute-start | bytes 589832 | tf_op jit(solution)/shard_map/ppermute | solution.py:445
  7.7 21.8 %collective-permute-start.12 = (bf16[512,512]{1,0:T(8,128)(2,1)}, bf16[512,512]{1,0:T(8,128)(2,1)}, u32[]{:S(2)}, u32[]{:S(2)}) collective-permute-start(bf16[512,512]{1,0:T(8,128)(2,1)} %refs_0_.3), channel_id=1, source_target_pairs={{0,16},{4,20},{16,24},{20,28},{24,8},{28,12},{8,0},{12,4},{1,17},{... | collective-permute-start | bytes 1572872 | tf_op jit(solution)/shard_map/ppermute | solution.py:461
  12.8 17.6 %collective-permute-start.6 = (bf16[1,512,512]{2,1,0:T(8,128)(2,1)}, bf16[1,512,512]{2,1,0:T(8,128)(2,1)S(1)}, u32[]{:S(2)}, u32[]{:S(2)}) collective-permute-start(bf16[1,512,512]{2,1,0:T(8,128)(2,1)} %get-tuple-element.63), channel_id=1, source_target_pairs={{0,4},{4,0},{8,12},{12,8},{16,20},{20,16},{24,28},{28,24},{1,5},{5... | collective-permute-start | bytes 1572872 | tf_op jit(solution)/shard_map/ppermute | solution.py:445
  14.5 17.4 %copy-start.8 = (bf16[512,512]{1,0:T(8,128)(2,1)S(1)}, bf16[512,512]{1,0:T(8,128)(2,1)}, u32[]{:S(2)}) copy-start(bf16[512,512]{1,0:T(8,128)(2,1)} %k_ref.1) | copy-start | bytes 1572868
  15.3 16.6 %copy-start.6 = (bf16[512,512]{1,0:T(8,128)(2,1)S(1)}, bf16[512,512]{1,0:T(8,128)(2,1)}, u32[]{:S(2)}) copy-start(bf16[512,512]{1,0:T(8,128)(2,1)} %q_ref.1) | copy-start | bytes 1572868
  15.3 13.5 %all-to-all-start = ((bf16[4,2,128,128]{3,2,1,0:T(8,128)(2,1)}), bf16[4,2,128,128]{3,2,1,0:T(8,128)(2,1)S(1)}, u32[]{:S(2)}, u32[]{:S(2)}) async-start(bf16[4,2,128,128]{3,2,1,0:T(8,128)(2,1)} %offer.1), calls=%async_computation | async-start | bytes 524288 | tf_op jit(solution)/shard_map/all_to_all | solution.py:474
  20.3 16.2 %collective-permute-start.4 = (bf16[1,512,512]{2,1,0:T(8,128)(2,1)S(1)}, bf16[1,512,512]{2,1,0:T(8,128)(2,1)S(1)}, u32[]{:S(2)}, u32[]{:S(2)}) collective-permute-start(bf16[1,512,512]{2,1,0:T(8,128)(2,1)S(1)} %get-tuple-element.60.refs_0_), channel_id=1, source_target_pairs={{0,2},{1,3},{2,0},{3,1},{4,6},{5,7},{6,4},{7,5},{8,10},{9,11},{10,... | collective-permute-start | bytes 1572872 | tf_op jit(solution)/shard_map/ppermute | solution.py:448
  28.9 7.1 %collective-permute-start.1 = (bf16[2,2,128,128]{3,2,1,0:T(8,128)(2,1)S(1)}, bf16[2,2,128,128]{3,2,1,0:T(8,128)(2,1)S(1)}, u32[]{:S(2)}, u32[]{:S(2)}) collective-permute-start(bf16[2,2,128,128]{3,2,1,0:T(8,128)(2,1)S(1)} %get-tuple-element.49), channel_id=1, source_target_pairs={{0,4},{4,0},{8,12},{12,8},{16,20},{20,16},{24,28},{28,24},{1,5},{5... | collective-permute-start | bytes 393224 | tf_op jit(solution)/shard_map/ppermute | solution.py:445
  29.5 11.9 %collective-permute-start.13 = (bf16[512,512]{1,0:T(8,128)(2,1)}, bf16[512,512]{1,0:T(8,128)(2,1)}, u32[]{:S(2)}, u32[]{:S(2)}) collective-permute-start(bf16[512,512]{1,0:T(8,128)(2,1)} %collective-permute-done.12.refs_1_), channel_id=1, source_target_pairs={{0,16},{4,20},{16,24},{20,28},{24,8},{28,12},{8,0},{12,4},{1,17},{... | collective-permute-start | bytes 1572872 | tf_op jit(solution)/shard_map/ppermute | solution.py:461
  30.4 13.5 %collective-permute-start.8 = (bf16[1,512,512]{2,1,0:T(8,128)(2,1)S(1)}, bf16[1,512,512]{2,1,0:T(8,128)(2,1)S(1)}, u32[]{:S(2)}, u32[]{:S(2)}) collective-permute-start(bf16[1,512,512]{2,1,0:T(8,128)(2,1)S(1)} %collective-permute-done.6.refs_4_), channel_id=1, source_target_pairs={{0,2},{1,3},{2,0},{3,1},{4,6},{5,7},{6,4},{7,5},{8,10},{9,11},{10,... | collective-permute-start | bytes 1572872 | tf_op jit(solution)/shard_map/ppermute | solution.py:448
  36.5 7.4 %collective-permute-start.5 = (bf16[1,512,512]{2,1,0:T(8,128)(2,1)S(1)}, bf16[1,512,512]{2,1,0:T(8,128)(2,1)S(1)}, u32[]{:S(2)}, u32[]{:S(2)}) collective-permute-start(bf16[1,512,512]{2,1,0:T(8,128)(2,1)S(1)} %collective-permute-done.4.refs_2_), channel_id=1, source_target_pairs={{0,1},{1,0},{2,3},{3,2},{4,5},{5,4},{6,7},{7,6},{8,9},{9,8},{10,11... | collective-permute-start | bytes 1572872 | tf_op jit(solution)/shard_map/ppermute | solution.py:448
  36.6 10.8 %collective-permute-start.3 = (bf16[1,512,512]{2,1,0:T(8,128)(2,1)S(1)}, bf16[1,512,512]{2,1,0:T(8,128)(2,1)S(1)}, u32[]{:S(2)}, u32[]{:S(2)}) collective-permute-start(bf16[1,512,512]{2,1,0:T(8,128)(2,1)S(1)} %get-tuple-element.60.refs_0_), channel_id=1, source_target_pairs={{0,1},{1,0},{2,3},{3,2},{4,5},{5,4},{6,7},{7,6},{8,9},{9,8},{10,11... | collective-permute-start | bytes 1572872 | tf_op jit(solution)/shard_map/ppermute | solution.py:448
  37.1 11.3 %collective-permute-start.7 = (bf16[1,512,512]{2,1,0:T(8,128)(2,1)S(1)}, bf16[1,512,512]{2,1,0:T(8,128)(2,1)S(1)}, u32[]{:S(2)}, u32[]{:S(2)}) collective-permute-start(bf16[1,512,512]{2,1,0:T(8,128)(2,1)S(1)} %collective-permute-done.6.refs_4_), channel_id=1, source_target_pairs={{0,1},{1,0},{2,3},{3,2},{4,5},{5,4},{6,7},{7,6},{8,9},{9,8},{10,11... | collective-permute-start | bytes 1572872 | tf_op jit(solution)/shard_map/ppermute | solution.py:448
  41.4 17.2 %collective-permute-start.2 = (bf16[512,512]{1,0:T(8,128)(2,1)S(1)}, bf16[512,512]{1,0:T(8,128)(2,1)S(1)}, u32[]{:S(2)}, u32[]{:S(2)}) collective-permute-start(bf16[512,512]{1,0:T(8,128)(2,1)S(1)} %finish_value.1.a_ref.x_ref), channel_id=1, source_target_pairs={{0,4},{4,0},{8,12},{12,8},{16,20},{20,16},{24,28},{28,24},{1,5},{5... | collective-permute-start | bytes 1572872 | tf_op jit(solution)/shard_map/ppermute | solution.py:445
  43.9 15.0 %collective-permute-start.9 = (bf16[1,512,512]{2,1,0:T(8,128)(2,1)S(1)}, bf16[1,512,512]{2,1,0:T(8,128)(2,1)}, u32[]{:S(2)}, u32[]{:S(2)}) collective-permute-start(bf16[1,512,512]{2,1,0:T(8,128)(2,1)S(1)} %collective-permute-done.8.refs_6_), channel_id=1, source_target_pairs={{0,1},{1,0},{2,3},{3,2},{4,5},{5,4},{6,7},{7,6},{8,9},{9,8},{10,11... | collective-permute-start | bytes 1572872 | tf_op jit(solution)/shard_map/ppermute | solution.py:448
  44.7 15.4 %collective-permute-start.14 = (bf16[512,512]{1,0:T(8,128)(2,1)}, bf16[512,512]{1,0:T(8,128)(2,1)}, u32[]{:S(2)}, u32[]{:S(2)}) collective-permute-start(bf16[512,512]{1,0:T(8,128)(2,1)} %collective-permute-done.13.refs_2_), channel_id=1, source_target_pairs={{0,16},{4,20},{16,24},{20,28},{24,8},{28,12},{8,0},{12,4},{1,17},{... | collective-permute-start | bytes 1572872 | tf_op jit(solution)/shard_map/ppermute | solution.py:461
  48.1 12.5 %collective-permute-start.16 = (bf16[512,512]{1,0:T(8,128)(2,1)}, bf16[512,512]{1,0:T(8,128)(2,1)}, u32[]{:S(2)}, u32[]{:S(2)}) collective-permute-start(bf16[512,512]{1,0:T(8,128)(2,1)} %collective-permute-done.12.refs_1_), channel_id=1, source_target_pairs={{0,1},{1,0},{2,3},{3,2},{4,5},{5,4},{6,7},{7,6},{8,9},{9,8},{10,11... | collective-permute-start | bytes 1572872 | tf_op jit(solution)/shard_map/ppermute | solution.py:448
  49.2 11.8 %collective-permute-start.15 = (bf16[512,512]{1,0:T(8,128)(2,1)}, bf16[512,512]{1,0:T(8,128)(2,1)}, u32[]{:S(2)}, u32[]{:S(2)}) collective-permute-start(bf16[512,512]{1,0:T(8,128)(2,1)} %refs_0_.3), channel_id=1, source_target_pairs={{0,1},{1,0},{2,3},{3,2},{4,5},{5,4},{6,7},{7,6},{8,9},{9,8},{10,11... | collective-permute-start | bytes 1572872 | tf_op jit(solution)/shard_map/ppermute | solution.py:448
  58.6 6.6 %collective-permute-start.17 = (bf16[512,512]{1,0:T(8,128)(2,1)}, bf16[512,512]{1,0:T(8,128)(2,1)S(1)}, u32[]{:S(2)}, u32[]{:S(2)}) collective-permute-start(bf16[512,512]{1,0:T(8,128)(2,1)} %collective-permute-done.13.refs_2_), channel_id=1, source_target_pairs={{0,1},{1,0},{2,3},{3,2},{4,5},{5,4},{6,7},{7,6},{8,9},{9,8},{10,11... | collective-permute-start | bytes 1572872 | tf_op jit(solution)/shard_map/ppermute | solution.py:448
  60.1 5.2 %collective-permute-start.18 = (bf16[512,512]{1,0:T(8,128)(2,1)}, bf16[512,512]{1,0:T(8,128)(2,1)S(1)}, u32[]{:S(2)}, u32[]{:S(2)}) collective-permute-start(bf16[512,512]{1,0:T(8,128)(2,1)} %collective-permute-done.14.refs_3_), channel_id=1, source_target_pairs={{0,1},{1,0},{2,3},{3,2},{4,5},{5,4},{6,7},{7,6},{8,9},{9,8},{10,11... | collective-permute-start | bytes 1572872 | tf_op jit(solution)/shard_map/ppermute | solution.py:448
  60.4 6.3 %collective-permute-start.11 = (bf16[512,512]{1,0:T(8,128)(2,1)S(1)}, bf16[512,512]{1,0:T(8,128)(2,1)S(1)}, u32[]{:S(2)}, u32[]{:S(2)}) collective-permute-start(bf16[512,512]{1,0:T(8,128)(2,1)S(1)} %collective-permute-done.2.b_ref.x_ref), channel_id=1, source_target_pairs={{0,1},{1,0},{2,3},{3,2},{4,5},{5,4},{6,7},{7,6},{8,9},{9,8},{10,11... | collective-permute-start | bytes 1572872 | tf_op jit(solution)/shard_map/ppermute | solution.py:448
  60.6 7.8 %collective-permute-start.19 = (bf16[512,512]{1,0:T(8,128)(2,1)S(1)}, bf16[512,512]{1,0:T(8,128)(2,1)S(1)}, u32[]{:S(2)}, u32[]{:S(2)}) collective-permute-start(bf16[512,512]{1,0:T(8,128)(2,1)S(1)} %finish_value.1.a_ref.x_ref), channel_id=1, source_target_pairs={{0,1},{1,0},{2,3},{3,2},{4,5},{5,4},{6,7},{7,6},{8,9},{9,8},{10,11... | collective-permute-start | bytes 1572872 | tf_op jit(solution)/shard_map/ppermute | solution.py:448
  60.9 14.3 %collective-permute-start.10 = (bf16[512,512]{1,0:T(8,128)(2,1)S(1)}, bf16[512,512]{1,0:T(8,128)(2,1)S(1)}, u32[]{:S(2)}, u32[]{:S(2)}) collective-permute-start(bf16[512,512]{1,0:T(8,128)(2,1)S(1)} %pieces.4), channel_id=1, source_target_pairs={{0,16},{4,20},{16,24},{20,28},{24,8},{28,12},{8,0},{12,4},{1,17},{... | collective-permute-start | bytes 1572872 | tf_op jit(solution)/shard_map/ppermute | solution.py:461
  67.5 18.0 %collective-permute-start.23 = (bf16[512,512]{1,0:T(8,128)(2,1)S(1)}, bf16[512,512]{1,0:T(8,128)(2,1)S(1)}, u32[]{:S(2)}, u32[]{:S(2)}) collective-permute-start(bf16[512,512]{1,0:T(8,128)(2,1)S(1)} %head_part.3), channel_id=1, source_target_pairs={{0,2},{1,3},{2,0},{3,1},{4,6},{5,7},{6,4},{7,5},{8,10},{9,11},{10,... | collective-permute-start | bytes 1572872 | tf_op jit(solution)/shard_map/ppermute | solution.py:448
  75.3 10.2 %collective-permute-start.20 = (bf16[256,512]{1,0:T(8,128)(2,1)S(1)}, bf16[256,512]{1,0:T(8,128)(2,1)S(1)}, u32[]{:S(2)}, u32[]{:S(2)}) collective-permute-start(bf16[256,512]{1,0:T(8,128)(2,1)S(1)} %add_own.4), channel_id=1, source_target_pairs={{0,16},{4,20},{16,24},{20,28},{24,8},{28,12},{8,0},{12,4},{1,17},{... | collective-permute-start | bytes 786440 | tf_op jit(solution)/shard_map/ppermute | solution.py:461
  78.8 12.3 %collective-permute-start.22 = (bf16[256,512]{1,0:T(8,128)(2,1)S(1)}, bf16[256,512]{1,0:T(8,128)(2,1)S(1)}, u32[]{:S(2)}, u32[]{:S(2)}) collective-permute-start(bf16[256,512]{1,0:T(8,128)(2,1)S(1)} %add_own.5), channel_id=1, source_target_pairs={{0,16},{4,20},{16,24},{20,28},{24,8},{28,12},{8,0},{12,4},{1,17},{... | collective-permute-start | bytes 786440 | tf_op jit(solution)/shard_map/ppermute | solution.py:461
  78.9 23.5 %collective-permute-start.25 = (bf16[512,512]{1,0:T(8,128)(2,1)S(1)}, bf16[512,512]{1,0:T(8,128)(2,1)S(1)}, u32[]{:S(2)}, u32[]{:S(2)}) collective-permute-start(bf16[512,512]{1,0:T(8,128)(2,1)S(1)} %head_part.4), channel_id=1, source_target_pairs={{0,2},{1,3},{2,0},{3,1},{4,6},{5,7},{6,4},{7,5},{8,10},{9,11},{10,... | collective-permute-start | bytes 1572872 | tf_op jit(solution)/shard_map/ppermute | solution.py:448
  86.3 16.0 %collective-permute-start.26 = (bf16[512,512]{1,0:T(8,128)(2,1)S(1)}, bf16[512,512]{1,0:T(8,128)(2,1)S(1)}, u32[]{:S(2)}, u32[]{:S(2)}) collective-permute-start(bf16[512,512]{1,0:T(8,128)(2,1)S(1)} %head_part.5), channel_id=1, source_target_pairs={{0,4},{4,0},{8,12},{12,8},{16,20},{20,16},{24,28},{28,24},{1,5},{5... | collective-permute-start | bytes 1572872 | tf_op jit(solution)/shard_map/ppermute | solution.py:445
  86.9 10.1 %collective-permute-start.21 = (bf16[256,512]{1,0:T(8,128)(2,1)S(1)}, bf16[256,512]{1,0:T(8,128)(2,1)S(1)}, u32[]{:S(2)}, u32[]{:S(2)}) collective-permute-start(bf16[256,512]{1,0:T(8,128)(2,1)S(1)} %add_own.6), channel_id=1, source_target_pairs={{0,16},{4,20},{16,24},{20,28},{24,8},{28,12},{8,0},{12,4},{1,17},{... | collective-permute-start | bytes 786440 | tf_op jit(solution)/shard_map/ppermute | solution.py:461
  91.1 9.8 %collective-permute-start.24 = (bf16[256,512]{1,0:T(8,128)(2,1)S(1)}, bf16[256,512]{1,0:T(8,128)(2,1)S(1)}, u32[]{:S(2)}, u32[]{:S(2)}) collective-permute-start(bf16[256,512]{1,0:T(8,128)(2,1)S(1)} %add_own.7), channel_id=1, source_target_pairs={{0,16},{4,20},{16,24},{20,28},{24,8},{28,12},{8,0},{12,4},{1,17},{... | collective-permute-start | bytes 786440 | tf_op jit(solution)/shard_map/ppermute | solution.py:461
  (13 other events, 28.6 us)

commit v17 on v14

--- a/solution.py
+++ b/solution.py
@@ -456,6 +456,9 @@
     def ring(x):
         return lax.ppermute(x, "ctx", moves)
 
+    def back(x):
+        return lax.ppermute(x, "ctx", [(b, a) for a, b in moves])
+
     keep, send = states(par, queries, keys, values, out_grad)
     near = partner(send)
     line = pair.astype(jnp.int32).reshape(1)
@@ -480,16 +483,21 @@
         factor, par, queries, keys, after(values, mine), out_grad, ends
     )
     token = send_far
-    for _ in range(2, pairs):
+    for _ in range(2, pairs // 2 + 1):
         blocks.append(ring(after(blocks[-1], token)))
         token = mine
-    lent = [across(after(x, mine), 1) for x in blocks[:-1]]
+    ahead = [value_weight]
+    for _ in range(pairs // 2 + 1, pairs):
+        ahead.append(back(after(ahead[-1], mine)))
+    blocks = blocks + ahead[:0:-1]
+    early = pairs // 2
+    lent = [across(after(x, mine), 1) for x in blocks[:early]]
     mine_too = across(mine, 1)
 
     offsets = [0]
     bit = n_head // 2
     while bit:
-        own = own + [across(r, bit) for r in own]
+        own = own + [across(after(r, mine) if len(own) > 1 else r, bit) for r in own]
         theirs = theirs + [across(r, bit) for r in theirs]
         offsets = offsets + [o ^ bit for o in offsets]
         bit //= 2
@@ -506,7 +514,7 @@
     total = piece(BF16, 0, query_grad, 4 * length * cols * width)
     moved = [ring(x) for x in total]
     other_too = across(other, 1)
-    lent.append(across(after(blocks[-1], total[0]), 1))
+    lent = lent + [across(after(x, total[0]), 1) for x in blocks[early:]]
     local_part = piece(F32, 1, total[0])
 
 

time: 103 us -> 114 us (1.11)
  waiting for transfers between devices: 27.9 us -> 42.2 us
  starting transfers between devices: 39.9 us -> 36.6 us
    ppermute x9 -> x8, waiting for transfers between devices: 12.5 us -> 27.8 us  [ring(): return lax.ppermute(x, 'ctx', moves)]
    ppermute x9 -> x8, starting transfers between devices: 20.9 us -> 15.1 us  [ring(): return lax.ppermute(x, 'ctx', moves)]
    ppermute x14, waiting for transfers between devices: 5.52 us -> 3.49 us  [across(): return lax.ppermute(x, 'head', [(i, i ^ bit) for i in range(n_head)])]
    ppermute x0 -> x1, starting transfers between devices: none -> 1.74 us  [back(): return lax.ppermute(x, 'ctx', [(b, a) for a, b in moves])]
    ppermute x5, waiting for transfers between devices: 2.87 us -> 4.16 us  [partner(): return lax.ppermute(x, 'ctx', [(i, i ^ 1) for i in range(n_ctx)])]
    unnamed x30 -> x34, local copies, waits for them, and re-layouts: 7.77 us -> 8.58 us
  transfers between devices with their start and end apart: 29 -> 29, of which waited for: 10 -> 12; matrix products, arithmetic and copies ran while one was open for 0% -> 0% of each run, Pallas kernels for 20% -> 17%
where the time goes in v17:
time: 114 us
  waiting for transfers between devices  42.2 us (37%)
  starting transfers between devices  36.6 us (32%)
  Pallas kernels  25.4 us (22%)
  local copies, waits for them, and re-layouts  8.58 us (8%)
    ppermute x8, waiting for transfers between devices, ring(): return lax.ppermute(x, 'ctx', moves)  27.8 us
    ppermute x8, starting transfers between devices, ring(): return lax.ppermute(x, 'ctx', moves)  15.1 us
    unnamed x34, local copies, waits for them, and re-layouts  8.58 us
    ppermute x14, starting transfers between devices, across(): return lax.ppermute(x, 'head', [(i, i ^ bit) for i in range(n_head)])  7.64 us
    ppermute x5, starting transfers between devices, partner(): return lax.ppermute(x, 'ctx', [(i, i ^ 1) for i in range(n_ctx)])  7.17 us
    all_to_all x1, waiting for transfers between devices, local(): lax.all_to_all(offered, 'ctx', split_axis=0, concat_axis=0, axis_index_gr...  6.5 us
    pallas_call x4, Pallas kernels, pieces(): call(functools.partial(piece_kernel, order, per, step, count), flops=flop...  5.21 us
    all_to_all x1, starting transfers between devices, local(): lax.all_to_all(offered, 'ctx', split_axis=0, concat_axis=0, axis_index_gr...  5 us
  transfers between devices with their start and end apart: 29, of which 12 were waited for; matrix products, arithmetic and copies ran while one was open for 0% of the time, Pallas kernels for 17%

profile of v17, /device:TPU:0, one launch (start us, length us, event | category | flops | bytes accessed | tf_op | source)
XLA Modules:
  0.0 113.7 jit_solution(8432539304450435985)
XLA Ops:
  0.7 4.0 %states.1 = (f32[2,2,128,128]{3,2,1,0:T(8,128)}, bf16[3,2,128,128]{3,2,1,0:T(8,128)(2,1)}) custom-call(s32[1]{0:T(128)} %bitcast.par_ref, bf16[512,512]{1,0:T(8,128)(2,1)} %q_ref.1, bf16[512,512]{1,0:T(8,128)(2,1)} %k_ref.1, bf16[512,512]{1,0:T(8,128)(2,1)} %v_ref, bf16[512,512]{1,0:T(8,128)(2,1)} %g_ref.1), custom_call_target="tpu_custom_call" | custom-call | flops 1 | bytes 1 | tf_op jit(solution)/shard_map/states/pallas_call | solution.py:67
  4.7 3.0 %collective-permute-start = (bf16[3,2,128,128]{3,2,1,0:T(8,128)(2,1)}, bf16[3,2,128,128]{3,2,1,0:T(8,128)(2,1)S(1)}, u32[]{:S(2)}, u32[]{:S(2)}) collective-permute-start(bf16[3,2,128,128]{3,2,1,0:T(8,128)(2,1)} %get-tuple-element.50), channel_id=1, source_target_pairs={{0,4},{4,0},{8,12},{12,8},{16,20},{20,16},{24,28},{28,24},{1,5},{5... | collective-permute-start | bytes 589832 | tf_op jit(solution)/shard_map/ppermute | solution.py:441
  8.7 4.1 %collective-permute-done.got_ref.refs_2_ = bf16[3,2,128,128]{3,2,1,0:T(8,128)(2,1)S(1)} collective-permute-done((bf16[3,2,128,128]{3,2,1,0:T(8,128)(2,1)}, bf16[3,2,128,128]{3,2,1,0:T(8,128)(2,1)S(1)}, u32[]{:S(2)}, u32[]{:S(2)}) %collective-permute-start) | collective-permute-done | bytes 196640 | tf_op jit(solution)/shard_map/ppermute | solution.py:441
  12.8 1.7 %collective-permute-start.6 = (bf16[1,512,512]{2,1,0:T(8,128)(2,1)}, bf16[1,512,512]{2,1,0:T(8,128)(2,1)S(1)}, u32[]{:S(2)}, u32[]{:S(2)}) collective-permute-start(bf16[1,512,512]{2,1,0:T(8,128)(2,1)} %get-tuple-element.65), channel_id=1, source_target_pairs={{0,4},{4,0},{8,12},{12,8},{16,20},{20,16},{24,28},{28,24},{1,5},{5... | collective-permute-start | bytes 1572872 | tf_op jit(solution)/shard_map/ppermute | solution.py:441
  15.3 5.0 %all-to-all-start = ((bf16[4,2,128,128]{3,2,1,0:T(8,128)(2,1)}), bf16[4,2,128,128]{3,2,1,0:T(8,128)(2,1)S(1)}, u32[]{:S(2)}, u32[]{:S(2)}) async-start(bf16[4,2,128,128]{3,2,1,0:T(8,128)(2,1)} %offer.1), calls=%async_computation | async-start | bytes 524288 | tf_op jit(solution)/shard_map/all_to_all | solution.py:473
  20.3 1.5 %collective-permute-start.4 = (bf16[1,512,512]{2,1,0:T(8,128)(2,1)S(1)}, bf16[1,512,512]{2,1,0:T(8,128)(2,1)S(1)}, u32[]{:S(2)}, u32[]{:S(2)}) collective-permute-start(bf16[1,512,512]{2,1,0:T(8,128)(2,1)S(1)} %get-tuple-element.62.refs_0_), channel_id=1, source_target_pairs={{0,2},{1,3},{2,0},{3,1},{4,6},{5,7},{6,4},{7,5},{8,10},{9,11},{10,... | collective-permute-start | bytes 1572872 | tf_op jit(solution)/shard_map/ppermute | solution.py:444
  21.8 6.5 %all-to-all-done.every_ref = bf16[4,2,128,128]{3,2,1,0:T(8,128)(2,1)S(1)} async-done(((bf16[4,2,128,128]{3,2,1,0:T(8,128)(2,1)}), bf16[4,2,128,128]{3,2,1,0:T(8,128)(2,1)S(1)}, u32[]{:S(2)}, u32[]{:S(2)}) %all-to-all-start) | async-done | bytes 262176 | tf_op jit(solution)/shard_map/all_to_all | solution.py:473
  28.9 1.5 %collective-permute-start.8 = (bf16[1,512,512]{2,1,0:T(8,128)(2,1)S(1)}, bf16[1,512,512]{2,1,0:T(8,128)(2,1)S(1)}, u32[]{:S(2)}, u32[]{:S(2)}) collective-permute-start(bf16[1,512,512]{2,1,0:T(8,128)(2,1)S(1)} %collective-permute-done.6.refs_4_), channel_id=1, source_target_pairs={{0,2},{1,3},{2,0},{3,1},{4,6},{5,7},{6,4},{7,5},{8,10},{9,11},{10,... | collective-permute-start | bytes 1572872 | tf_op jit(solution)/shard_map/ppermute | solution.py:444
  31.5 3.0 %inside.1 = (f32[512,512]{1,0:T(8,128)S(1)}, bf16[512,512]{1,0:T(8,128)(2,1)S(1)}) custom-call(bf16[512,512]{1,0:T(8,128)(2,1)S(1)} %copy-done.6, bf16[512,512]{1,0:T(8,128)(2,1)S(1)} %copy-done.8, bf16[512,512]{1,0:T(8,128)(2,1)S(1)} %copy-done.10), custom_call_target="tpu_custom_call" | custom-call | flops 1 | bytes 1 | tf_op jit(solution)/shard_map/inside/pallas_call | solution.py:147
  35.7 3.4 %collective-permute-done.12.refs_1_ = bf16[512,512]{1,0:T(8,128)(2,1)} collective-permute-done((bf16[512,512]{1,0:T(8,128)(2,1)}, bf16[512,512]{1,0:T(8,128)(2,1)}, u32[]{:S(2)}, u32[]{:S(2)}) %collective-permute-start.12) | collective-permute-done | bytes 524320 | tf_op jit(solution)/shard_map/ppermute | solution.py:457
  39.1 1.4 %collective-permute-start.2 = (bf16[512,512]{1,0:T(8,128)(2,1)S(1)}, bf16[512,512]{1,0:T(8,128)(2,1)S(1)}, u32[]{:S(2)}, u32[]{:S(2)}) collective-permute-start(bf16[512,512]{1,0:T(8,128)(2,1)S(1)} %finish_value.1.a_ref.x_ref), channel_id=1, source_target_pairs={{0,4},{4,0},{8,12},{12,8},{16,20},{20,16},{24,28},{28,24},{1,5},{5... | collective-permute-start | bytes 1572872 | tf_op jit(solution)/shard_map/ppermute | solution.py:441
  40.5 3.3 %collective-permute-done.8.refs_6_ = bf16[1,512,512]{2,1,0:T(8,128)(2,1)S(1)} collective-permute-done((bf16[1,512,512]{2,1,0:T(8,128)(2,1)S(1)}, bf16[1,512,512]{2,1,0:T(8,128)(2,1)S(1)}, u32[]{:S(2)}, u32[]{:S(2)}) %collective-permute-start.8) | collective-permute-done | bytes 524320 | tf_op jit(solution)/shard_map/ppermute | solution.py:444
  44.6 1.7 %collective-permute-start.14 = (bf16[512,512]{1,0:T(8,128)(2,1)}, bf16[512,512]{1,0:T(8,128)(2,1)}, u32[]{:S(2)}, u32[]{:S(2)}) collective-permute-start(bf16[512,512]{1,0:T(8,128)(2,1)} %refs_0_.3), channel_id=1, source_target_pairs={{16,0},{20,4},{24,16},{28,20},{8,24},{12,28},{0,8},{4,12},{17,1},{... | collective-permute-start | bytes 1572872 | tf_op jit(solution)/shard_map/ppermute | solution.py:460
  47.1 1.2 %collective-permute-start.13 = (bf16[512,512]{1,0:T(8,128)(2,1)}, bf16[512,512]{1,0:T(8,128)(2,1)}, u32[]{:S(2)}, u32[]{:S(2)}) collective-permute-start(bf16[512,512]{1,0:T(8,128)(2,1)} %collective-permute-done.12.refs_1_), channel_id=1, source_target_pairs={{0,16},{4,20},{16,24},{20,28},{24,8},{28,12},{8,0},{12,4},{1,17},{... | collective-permute-start | bytes 1572872 | tf_op jit(solution)/shard_map/ppermute | solution.py:457
  54.2 4.0 %others.1 = (bf16[512,512]{1,0:T(8,128)(2,1)}, bf16[512,512]{1,0:T(8,128)(2,1)}) custom-call(s32[1]{0:T(128)} %bitcast.par_ref, bf16[512,512]{1,0:T(8,128)(2,1)S(1)} %copy-done.7, bf16[512,512]{1,0:T(8,128)(2,1)S(1)} %copy-done.9, bf16[512,512]{1,0:T(8,128)(2,1)S(1)} %copy-done.12, bf16[512,512]{1,0:T(8,128)(2,1)S(1)} %copy-done.11, ...), custom_call_target="tpu_custom_call" | custom-call | flops 1 | bytes 1 | tf_op jit(solution)/shard_map/others/pallas_call | solution.py:246
  58.8 1.1 %pieces.4 = (bf16[256,512]{1,0:T(8,128)(2,1)S(1)}, bf16[256,512]{1,0:T(8,128)(2,1)S(1)}) custom-call(s32[1]{0:T(128)} %bitcast.3.spot_ref, s32[1]{0:T(128)} %bitcast.2.head_ref.at_ref, bf16[512,512]{1,0:T(8,128)(2,1)S(1)} %finish_value.1.a_ref.x_ref, bf16[512,512]{1,0:T(8,128)(2,1)S(1)} %collective-permute-done.2.b_ref.x_ref, ...), custom_call_target="tpu_custom_call" | custom-call | flops 536870912 | bytes 1 | tf_op jit(solution)/shard_map/pieces/pallas_call | solution.py:291
  60.2 11.1 %collective-permute-done.13.refs_2_ = bf16[512,512]{1,0:T(8,128)(2,1)} collective-permute-done((bf16[512,512]{1,0:T(8,128)(2,1)}, bf16[512,512]{1,0:T(8,128)(2,1)}, u32[]{:S(2)}, u32[]{:S(2)}) %collective-permute-start.13) | collective-permute-done | bytes 524320 | tf_op jit(solution)/shard_map/ppermute | solution.py:457
  72.0 1.8 %pieces.5 = (f32[256,512]{1,0:T(8,128)S(1)}, f32[256,512]{1,0:T(8,128)S(1)}) custom-call(s32[1]{0:T(128)} %bitcast.3.spot_ref, s32[1]{0:T(128)} %bitcast.2.head_ref.at_ref, bf16[512,512]{1,0:T(8,128)(2,1)S(1)} %finish_value.1.a_ref.x_ref, bf16[512,512]{1,0:T(8,128)(2,1)S(1)} %collective-permute-done.2.b_ref.x_ref, ...), custom_call_target="tpu_custom_call" | custom-call | flops 1 | bytes 1 | tf_op jit(solution)/shard_map/pieces/pallas_call | solution.py:291
  73.8 1.2 %collective-permute-start.10 = (bf16[256,512]{1,0:T(8,128)(2,1)S(1)}, bf16[256,512]{1,0:T(8,128)(2,1)S(1)}, u32[]{:S(2)}, u32[]{:S(2)}) collective-permute-start(bf16[256,512]{1,0:T(8,128)(2,1)S(1)} %get-tuple-element.67), channel_id=1, source_target_pairs={{0,16},{4,20},{16,24},{20,28},{24,8},{28,12},{8,0},{12,4},{1,17},{... | collective-permute-start | bytes 786440 | tf_op jit(solution)/shard_map/ppermute | solution.py:457
  74.9 1.3 %arrange.1 = (bf16[2,512,512]{2,1,0:T(8,128)(2,1)S(1)}, bf16[2,512,512]{2,1,0:T(8,128)(2,1)S(1)}) custom-call(s32[1]{0:T(128)} %bitcast.2.head_ref.at_ref, s32[1]{0:T(128)} %bitcast.3.spot_ref, bf16[512,512]{1,0:T(8,128)(2,1)} %refs_0_.3, bf16[512,512]{1,0:T(8,128)(2,1)} %collective-permute-done.12.refs_1_, ...), custom_call_target="tpu_custom_call" | custom-call | flops 1 | bytes 1 | tf_op jit(solution)/shard_map/arrange/pallas_call | solution.py:367
  77.0 2.3 %collective-permute-start.24 = (bf16[512,512]{1,0:T(8,128)(2,1)S(1)}, bf16[512,512]{1,0:T(8,128)(2,1)S(1)}, u32[]{:S(2)}, u32[]{:S(2)}) collective-permute-start(bf16[512,512]{1,0:T(8,128)(2,1)S(1)} %head_part.3), channel_id=1, source_target_pairs={{0,2},{1,3},{2,0},{3,1},{4,6},{5,7},{6,4},{7,5},{8,10},{9,11},{10,... | collective-permute-start | bytes 1572872 | tf_op jit(solution)/shard_map/ppermute | solution.py:444
  79.2 2.3 %collective-permute-start.21 = (bf16[256,512]{1,0:T(8,128)(2,1)S(1)}, bf16[256,512]{1,0:T(8,128)(2,1)S(1)}, u32[]{:S(2)}, u32[]{:S(2)}) collective-permute-start(bf16[256,512]{1,0:T(8,128)(2,1)S(1)} %get-tuple-element.81), channel_id=1, source_target_pairs={{0,16},{4,20},{16,24},{20,28},{24,8},{28,12},{8,0},{12,4},{1,17},{... | collective-permute-start | bytes 786440 | tf_op jit(solution)/shard_map/ppermute | solution.py:457
  83.0 1.7 %collective-permute-start.20 = (bf16[256,512]{1,0:T(8,128)(2,1)S(1)}, bf16[256,512]{1,0:T(8,128)(2,1)S(1)}, u32[]{:S(2)}, u32[]{:S(2)}) collective-permute-start(bf16[256,512]{1,0:T(8,128)(2,1)S(1)} %add_own.4), channel_id=1, source_target_pairs={{0,16},{4,20},{16,24},{20,28},{24,8},{28,12},{8,0},{12,4},{1,17},{... | collective-permute-start | bytes 786440 | tf_op jit(solution)/shard_map/ppermute | solution.py:457
  84.7 3.9 %collective-permute-done.21.moved_ref = bf16[256,512]{1,0:T(8,128)(2,1)S(1)} collective-permute-done((bf16[256,512]{1,0:T(8,128)(2,1)S(1)}, bf16[256,512]{1,0:T(8,128)(2,1)S(1)}, u32[]{:S(2)}, u32[]{:S(2)}) %collective-permute-start.21) | collective-permute-done | bytes 262176 | tf_op jit(solution)/shard_map/ppermute | solution.py:457
  88.6 3.1 %collective-permute-start.23 = (bf16[256,512]{1,0:T(8,128)(2,1)S(1)}, bf16[256,512]{1,0:T(8,128)(2,1)S(1)}, u32[]{:S(2)}, u32[]{:S(2)}) collective-permute-start(bf16[256,512]{1,0:T(8,128)(2,1)S(1)} %add_own.5), channel_id=1, source_target_pairs={{0,16},{4,20},{16,24},{20,28},{24,8},{28,12},{8,0},{12,4},{1,17},{... | collective-permute-start | bytes 786440 | tf_op jit(solution)/shard_map/ppermute | solution.py:457
  93.5 1.1 %pieces.7 = (f32[256,512]{1,0:T(8,128)S(1)}, f32[256,512]{1,0:T(8,128)S(1)}) custom-call(s32[1]{0:T(128)} %bitcast.3.spot_ref, s32[1]{0:T(128)} %bitcast.2.head_ref.at_ref, bf16[512,512]{1,0:T(8,128)(2,1)S(1)} %finish_value.1.a_ref.x_ref, bf16[512,512]{1,0:T(8,128)(2,1)S(1)} %collective-permute-done.2.b_ref.x_ref, ...), custom_call_target="tpu_custom_call" | custom-call | flops 1 | bytes 1 | tf_op jit(solution)/shard_map/pieces/pallas_call | solution.py:291
  96.1 2.5 %collective-permute-start.22 = (bf16[256,512]{1,0:T(8,128)(2,1)S(1)}, bf16[256,512]{1,0:T(8,128)(2,1)S(1)}, u32[]{:S(2)}, u32[]{:S(2)}) collective-permute-start(bf16[256,512]{1,0:T(8,128)(2,1)S(1)} %add_own.6), channel_id=1, source_target_pairs={{0,16},{4,20},{16,24},{20,28},{24,8},{28,12},{8,0},{12,4},{1,17},{... | collective-permute-start | bytes 786440 | tf_op jit(solution)/shard_map/ppermute | solution.py:457
  99.9 3.1 %collective-permute-start.25 = (bf16[256,512]{1,0:T(8,128)(2,1)S(1)}, bf16[256,512]{1,0:T(8,128)(2,1)S(1)}, u32[]{:S(2)}, u32[]{:S(2)}) collective-permute-start(bf16[256,512]{1,0:T(8,128)(2,1)S(1)} %add_own.7), channel_id=1, source_target_pairs={{0,16},{4,20},{16,24},{20,28},{24,8},{28,12},{8,0},{12,4},{1,17},{... | collective-permute-start | bytes 786440 | tf_op jit(solution)/shard_map/ppermute | solution.py:457
  103.0 2.5 %collective-permute-done.22.refs_0_ = bf16[256,512]{1,0:T(8,128)(2,1)S(1)} collective-permute-done((bf16[256,512]{1,0:T(8,128)(2,1)S(1)}, bf16[256,512]{1,0:T(8,128)(2,1)S(1)}, u32[]{:S(2)}, u32[]{:S(2)}) %collective-permute-start.22) | collective-permute-done | bytes 262176 | tf_op jit(solution)/shard_map/ppermute | solution.py:457
  105.4 5.1 %collective-permute-done.25.refs_1_ = bf16[256,512]{1,0:T(8,128)(2,1)S(1)} collective-permute-done((bf16[256,512]{1,0:T(8,128)(2,1)S(1)}, bf16[256,512]{1,0:T(8,128)(2,1)S(1)}, u32[]{:S(2)}, u32[]{:S(2)}) %collective-permute-start.25) | collective-permute-done | bytes 262176 | tf_op jit(solution)/shard_map/ppermute | solution.py:457
  110.6 1.3 %finish_weight.1 = f32[512,512]{1,0:T(8,128)} custom-call(bf16[256,512]{1,0:T(8,128)(2,1)S(1)} %collective-permute-done.22.refs_0_, bf16[256,512]{1,0:T(8,128)(2,1)S(1)} %collective-permute-done.25.refs_1_, f32[256,512]{1,0:T(8,128)S(1)} %get-tuple-element.87.refs_2_, f32[256,512]{1,0:T(8,128)S(1)} %get-tuple-element.92.refs_3_), custom_call_target="tpu_custom_call" | custom-call | flops 1 | bytes 1 | tf_op jit(solution)/shard_map/finish_weight/pallas_call | solution.py:315
  111.9 1.8 %join.1 = bf16[512,1024]{1,0:T(8,128)(2,1)} custom-call(s32[1]{0:T(128)} %bitcast.par_ref, s32[1]{0:T(128)} %bitcast.2.head_ref.at_ref, bf16[512,512]{1,0:T(8,128)(2,1)S(1)} %finish_value.1.a_ref.x_ref, bf16[512,512]{1,0:T(8,128)(2,1)S(1)} %collective-permute-done.19.y_ref, bf16[2,512,512]{2,1,0:T(8,128)(2,1)S(1)} %get-tuple-element.77.w_ref, ...), custom_call_target="tpu_custom_call" | custom-call | flops 1 | bytes 1 | tf_op jit(solution)/shard_map/join/pallas_call | solution.py:418
  (81 shorter events, 20.0 us)
Async XLA Ops:
  4.7 9.9 %copy-start.16 = (f32[2,2,128,128]{3,2,1,0:T(8,128)S(1)}, f32[2,2,128,128]{3,2,1,0:T(8,128)}, u32[]{:S(2)}) copy-start(f32[2,2,128,128]{3,2,1,0:T(8,128)} %get-tuple-element.49.keep_ref) | copy-start | bytes 786436
  4.7 8.1 %collective-permute-start = (bf16[3,2,128,128]{3,2,1,0:T(8,128)(2,1)}, bf16[3,2,128,128]{3,2,1,0:T(8,128)(2,1)S(1)}, u32[]{:S(2)}, u32[]{:S(2)}) collective-permute-start(bf16[3,2,128,128]{3,2,1,0:T(8,128)(2,1)} %get-tuple-element.50), channel_id=1, source_target_pairs={{0,4},{4,0},{8,12},{12,8},{16,20},{20,16},{24,28},{28,24},{1,5},{5... | collective-permute-start | bytes 589832 | tf_op jit(solution)/shard_map/ppermute | solution.py:441
  12.8 16.1 %collective-permute-start.6 = (bf16[1,512,512]{2,1,0:T(8,128)(2,1)}, bf16[1,512,512]{2,1,0:T(8,128)(2,1)S(1)}, u32[]{:S(2)}, u32[]{:S(2)}) collective-permute-start(bf16[1,512,512]{2,1,0:T(8,128)(2,1)} %get-tuple-element.65), channel_id=1, source_target_pairs={{0,4},{4,0},{8,12},{12,8},{16,20},{20,16},{24,28},{28,24},{1,5},{5... | collective-permute-start | bytes 1572872 | tf_op jit(solution)/shard_map/ppermute | solution.py:441
  14.5 15.9 %copy-start.8 = (bf16[512,512]{1,0:T(8,128)(2,1)S(1)}, bf16[512,512]{1,0:T(8,128)(2,1)}, u32[]{:S(2)}) copy-start(bf16[512,512]{1,0:T(8,128)(2,1)} %k_ref.1) | copy-start | bytes 1572868
  15.3 15.2 %copy-start.6 = (bf16[512,512]{1,0:T(8,128)(2,1)S(1)}, bf16[512,512]{1,0:T(8,128)(2,1)}, u32[]{:S(2)}) copy-start(bf16[512,512]{1,0:T(8,128)(2,1)} %q_ref.1) | copy-start | bytes 1572868
  15.3 13.0 %all-to-all-start = ((bf16[4,2,128,128]{3,2,1,0:T(8,128)(2,1)}), bf16[4,2,128,128]{3,2,1,0:T(8,128)(2,1)S(1)}, u32[]{:S(2)}, u32[]{:S(2)}) async-start(bf16[4,2,128,128]{3,2,1,0:T(8,128)(2,1)} %offer.1), calls=%async_computation | async-start | bytes 524288 | tf_op jit(solution)/shard_map/all_to_all | solution.py:473
  20.3 14.9 %collective-permute-start.4 = (bf16[1,512,512]{2,1,0:T(8,128)(2,1)S(1)}, bf16[1,512,512]{2,1,0:T(8,128)(2,1)S(1)}, u32[]{:S(2)}, u32[]{:S(2)}) collective-permute-start(bf16[1,512,512]{2,1,0:T(8,128)(2,1)S(1)} %get-tuple-element.62.refs_0_), channel_id=1, source_target_pairs={{0,2},{1,3},{2,0},{3,1},{4,6},{5,7},{6,4},{7,5},{8,10},{9,11},{10,... | collective-permute-start | bytes 1572872 | tf_op jit(solution)/shard_map/ppermute | solution.py:444
  28.5 6.1 %collective-permute-start.1 = (bf16[2,2,128,128]{3,2,1,0:T(8,128)(2,1)S(1)}, bf16[2,2,128,128]{3,2,1,0:T(8,128)(2,1)S(1)}, u32[]{:S(2)}, u32[]{:S(2)}) collective-permute-start(bf16[2,2,128,128]{3,2,1,0:T(8,128)(2,1)S(1)} %get-tuple-element.51), channel_id=1, source_target_pairs={{0,4},{4,0},{8,12},{12,8},{16,20},{20,16},{24,28},{28,24},{1,5},{5... | collective-permute-start | bytes 393224 | tf_op jit(solution)/shard_map/ppermute | solution.py:441
  28.9 10.2 %collective-permute-start.12 = (bf16[512,512]{1,0:T(8,128)(2,1)}, bf16[512,512]{1,0:T(8,128)(2,1)}, u32[]{:S(2)}, u32[]{:S(2)}) collective-permute-start(bf16[512,512]{1,0:T(8,128)(2,1)} %refs_0_.3), channel_id=1, source_target_pairs={{0,16},{4,20},{16,24},{20,28},{24,8},{28,12},{8,0},{12,4},{1,17},{... | collective-permute-start | bytes 1572872 | tf_op jit(solution)/shard_map/ppermute | solution.py:457
  28.9 14.8 %collective-permute-start.8 = (bf16[1,512,512]{2,1,0:T(8,128)(2,1)S(1)}, bf16[1,512,512]{2,1,0:T(8,128)(2,1)S(1)}, u32[]{:S(2)}, u32[]{:S(2)}) collective-permute-start(bf16[1,512,512]{2,1,0:T(8,128)(2,1)S(1)} %collective-permute-done.6.refs_4_), channel_id=1, source_target_pairs={{0,2},{1,3},{2,0},{3,1},{4,6},{5,7},{6,4},{7,5},{8,10},{9,11},{10,... | collective-permute-start | bytes 1572872 | tf_op jit(solution)/shard_map/ppermute | solution.py:444
  35.2 8.6 %collective-permute-start.5 = (bf16[1,512,512]{2,1,0:T(8,128)(2,1)S(1)}, bf16[1,512,512]{2,1,0:T(8,128)(2,1)S(1)}, u32[]{:S(2)}, u32[]{:S(2)}) collective-permute-start(bf16[1,512,512]{2,1,0:T(8,128)(2,1)S(1)} %collective-permute-done.4.refs_2_), channel_id=1, source_target_pairs={{0,1},{1,0},{2,3},{3,2},{4,5},{5,4},{6,7},{7,6},{8,9},{9,8},{10,11... | collective-permute-start | bytes 1572872 | tf_op jit(solution)/shard_map/ppermute | solution.py:444
  35.2 11.2 %collective-permute-start.3 = (bf16[1,512,512]{2,1,0:T(8,128)(2,1)S(1)}, bf16[1,512,512]{2,1,0:T(8,128)(2,1)S(1)}, u32[]{:S(2)}, u32[]{:S(2)}) collective-permute-start(bf16[1,512,512]{2,1,0:T(8,128)(2,1)S(1)} %get-tuple-element.62.refs_0_), channel_id=1, source_target_pairs={{0,1},{1,0},{2,3},{3,2},{4,5},{5,4},{6,7},{7,6},{8,9},{9,8},{10,11... | collective-permute-start | bytes 1572872 | tf_op jit(solution)/shard_map/ppermute | solution.py:444
  35.7 12.6 %collective-permute-start.7 = (bf16[1,512,512]{2,1,0:T(8,128)(2,1)S(1)}, bf16[1,512,512]{2,1,0:T(8,128)(2,1)S(1)}, u32[]{:S(2)}, u32[]{:S(2)}) collective-permute-start(bf16[1,512,512]{2,1,0:T(8,128)(2,1)S(1)} %collective-permute-done.6.refs_4_), channel_id=1, source_target_pairs={{0,1},{1,0},{2,3},{3,2},{4,5},{5,4},{6,7},{7,6},{8,9},{9,8},{10,11... | collective-permute-start | bytes 1572872 | tf_op jit(solution)/shard_map/ppermute | solution.py:444
  39.1 19.2 %collective-permute-start.2 = (bf16[512,512]{1,0:T(8,128)(2,1)S(1)}, bf16[512,512]{1,0:T(8,128)(2,1)S(1)}, u32[]{:S(2)}, u32[]{:S(2)}) collective-permute-start(bf16[512,512]{1,0:T(8,128)(2,1)S(1)} %finish_value.1.a_ref.x_ref), channel_id=1, source_target_pairs={{0,4},{4,0},{8,12},{12,8},{16,20},{20,16},{24,28},{28,24},{1,5},{5... | collective-permute-start | bytes 1572872 | tf_op jit(solution)/shard_map/ppermute | solution.py:441
  43.8 15.0 %collective-permute-start.9 = (bf16[1,512,512]{2,1,0:T(8,128)(2,1)S(1)}, bf16[1,512,512]{2,1,0:T(8,128)(2,1)}, u32[]{:S(2)}, u32[]{:S(2)}) collective-permute-start(bf16[1,512,512]{2,1,0:T(8,128)(2,1)S(1)} %collective-permute-done.8.refs_6_), channel_id=1, source_target_pairs={{0,1},{1,0},{2,3},{3,2},{4,5},{5,4},{6,7},{7,6},{8,9},{9,8},{10,11... | collective-permute-start | bytes 1572872 | tf_op jit(solution)/shard_map/ppermute | solution.py:444
  44.6 15.7 %collective-permute-start.14 = (bf16[512,512]{1,0:T(8,128)(2,1)}, bf16[512,512]{1,0:T(8,128)(2,1)}, u32[]{:S(2)}, u32[]{:S(2)}) collective-permute-start(bf16[512,512]{1,0:T(8,128)(2,1)} %refs_0_.3), channel_id=1, source_target_pairs={{16,0},{20,4},{24,16},{28,20},{8,24},{12,28},{0,8},{4,12},{17,1},{... | collective-permute-start | bytes 1572872 | tf_op jit(solution)/shard_map/ppermute | solution.py:460
  47.1 24.2 %collective-permute-start.13 = (bf16[512,512]{1,0:T(8,128)(2,1)}, bf16[512,512]{1,0:T(8,128)(2,1)}, u32[]{:S(2)}, u32[]{:S(2)}) collective-permute-start(bf16[512,512]{1,0:T(8,128)(2,1)} %collective-permute-done.12.refs_1_), channel_id=1, source_target_pairs={{0,16},{4,20},{16,24},{20,28},{24,8},{28,12},{8,0},{12,4},{1,17},{... | collective-permute-start | bytes 1572872 | tf_op jit(solution)/shard_map/ppermute | solution.py:457
  49.1 22.8 %collective-permute-start.16 = (bf16[512,512]{1,0:T(8,128)(2,1)}, bf16[512,512]{1,0:T(8,128)(2,1)}, u32[]{:S(2)}, u32[]{:S(2)}) collective-permute-start(bf16[512,512]{1,0:T(8,128)(2,1)} %collective-permute-done.12.refs_1_), channel_id=1, source_target_pairs={{0,1},{1,0},{2,3},{3,2},{4,5},{5,4},{6,7},{7,6},{8,9},{9,8},{10,11... | collective-permute-start | bytes 1572872 | tf_op jit(solution)/shard_map/ppermute | solution.py:444
  58.3 15.5 %collective-permute-start.15 = (bf16[512,512]{1,0:T(8,128)(2,1)}, bf16[512,512]{1,0:T(8,128)(2,1)S(1)}, u32[]{:S(2)}, u32[]{:S(2)}) collective-permute-start(bf16[512,512]{1,0:T(8,128)(2,1)} %refs_0_.3), channel_id=1, source_target_pairs={{0,1},{1,0},{2,3},{3,2},{4,5},{5,4},{6,7},{7,6},{8,9},{9,8},{10,11... | collective-permute-start | bytes 1572872 | tf_op jit(solution)/shard_map/ppermute | solution.py:444
  60.2 14.7 %collective-permute-start.18 = (bf16[512,512]{1,0:T(8,128)(2,1)}, bf16[512,512]{1,0:T(8,128)(2,1)S(1)}, u32[]{:S(2)}, u32[]{:S(2)}) collective-permute-start(bf16[512,512]{1,0:T(8,128)(2,1)} %collective-permute-done.14.refs_3_), channel_id=1, source_target_pairs={{0,1},{1,0},{2,3},{3,2},{4,5},{5,4},{6,7},{7,6},{8,9},{9,8},{10,11... | collective-permute-start | bytes 1572872 | tf_op jit(solution)/shard_map/ppermute | solution.py:444
  71.4 3.6 %collective-permute-start.17 = (bf16[512,512]{1,0:T(8,128)(2,1)}, bf16[512,512]{1,0:T(8,128)(2,1)S(1)}, u32[]{:S(2)}, u32[]{:S(2)}) collective-permute-start(bf16[512,512]{1,0:T(8,128)(2,1)} %collective-permute-done.13.refs_2_), channel_id=1, source_target_pairs={{0,1},{1,0},{2,3},{3,2},{4,5},{5,4},{6,7},{7,6},{8,9},{9,8},{10,11... | collective-permute-start | bytes 1572872 | tf_op jit(solution)/shard_map/ppermute | solution.py:444
  71.4 4.8 %collective-permute-start.11 = (bf16[512,512]{1,0:T(8,128)(2,1)S(1)}, bf16[512,512]{1,0:T(8,128)(2,1)S(1)}, u32[]{:S(2)}, u32[]{:S(2)}) collective-permute-start(bf16[512,512]{1,0:T(8,128)(2,1)S(1)} %collective-permute-done.2.b_ref.x_ref), channel_id=1, source_target_pairs={{0,1},{1,0},{2,3},{3,2},{4,5},{5,4},{6,7},{7,6},{8,9},{9,8},{10,11... | collective-permute-start | bytes 1572872 | tf_op jit(solution)/shard_map/ppermute | solution.py:444
  71.9 9.7 %collective-permute-start.19 = (bf16[512,512]{1,0:T(8,128)(2,1)S(1)}, bf16[512,512]{1,0:T(8,128)(2,1)S(1)}, u32[]{:S(2)}, u32[]{:S(2)}) collective-permute-start(bf16[512,512]{1,0:T(8,128)(2,1)S(1)} %finish_value.1.a_ref.x_ref), channel_id=1, source_target_pairs={{0,1},{1,0},{2,3},{3,2},{4,5},{5,4},{6,7},{7,6},{8,9},{9,8},{10,11... | collective-permute-start | bytes 1572872 | tf_op jit(solution)/shard_map/ppermute | solution.py:444
  73.8 9.2 %collective-permute-start.10 = (bf16[256,512]{1,0:T(8,128)(2,1)S(1)}, bf16[256,512]{1,0:T(8,128)(2,1)S(1)}, u32[]{:S(2)}, u32[]{:S(2)}) collective-permute-start(bf16[256,512]{1,0:T(8,128)(2,1)S(1)} %get-tuple-element.67), channel_id=1, source_target_pairs={{0,16},{4,20},{16,24},{20,28},{24,8},{28,12},{8,0},{12,4},{1,17},{... | collective-permute-start | bytes 786440 | tf_op jit(solution)/shard_map/ppermute | solution.py:457
  77.0 17.8 %collective-permute-start.24 = (bf16[512,512]{1,0:T(8,128)(2,1)S(1)}, bf16[512,512]{1,0:T(8,128)(2,1)S(1)}, u32[]{:S(2)}, u32[]{:S(2)}) collective-permute-start(bf16[512,512]{1,0:T(8,128)(2,1)S(1)} %head_part.3), channel_id=1, source_target_pairs={{0,2},{1,3},{2,0},{3,1},{4,6},{5,7},{6,4},{7,5},{8,10},{9,11},{10,... | collective-permute-start | bytes 1572872 | tf_op jit(solution)/shard_map/ppermute | solution.py:444
  79.2 9.3 %collective-permute-start.21 = (bf16[256,512]{1,0:T(8,128)(2,1)S(1)}, bf16[256,512]{1,0:T(8,128)(2,1)S(1)}, u32[]{:S(2)}, u32[]{:S(2)}) collective-permute-start(bf16[256,512]{1,0:T(8,128)(2,1)S(1)} %get-tuple-element.81), channel_id=1, source_target_pairs={{0,16},{4,20},{16,24},{20,28},{24,8},{28,12},{8,0},{12,4},{1,17},{... | collective-permute-start | bytes 786440 | tf_op jit(solution)/shard_map/ppermute | solution.py:457
  83.0 11.7 %collective-permute-start.20 = (bf16[256,512]{1,0:T(8,128)(2,1)S(1)}, bf16[256,512]{1,0:T(8,128)(2,1)S(1)}, u32[]{:S(2)}, u32[]{:S(2)}) collective-permute-start(bf16[256,512]{1,0:T(8,128)(2,1)S(1)} %add_own.4), channel_id=1, source_target_pairs={{0,16},{4,20},{16,24},{20,28},{24,8},{28,12},{8,0},{12,4},{1,17},{... | collective-permute-start | bytes 786440 | tf_op jit(solution)/shard_map/ppermute | solution.py:457
  88.6 11.2 %collective-permute-start.23 = (bf16[256,512]{1,0:T(8,128)(2,1)S(1)}, bf16[256,512]{1,0:T(8,128)(2,1)S(1)}, u32[]{:S(2)}, u32[]{:S(2)}) collective-permute-start(bf16[256,512]{1,0:T(8,128)(2,1)S(1)} %add_own.5), channel_id=1, source_target_pairs={{0,16},{4,20},{16,24},{20,28},{24,8},{28,12},{8,0},{12,4},{1,17},{... | collective-permute-start | bytes 786440 | tf_op jit(solution)/shard_map/ppermute | solution.py:457
  91.7 20.2 %collective-permute-start.26 = (bf16[512,512]{1,0:T(8,128)(2,1)S(1)}, bf16[512,512]{1,0:T(8,128)(2,1)S(1)}, u32[]{:S(2)}, u32[]{:S(2)}) collective-permute-start(bf16[512,512]{1,0:T(8,128)(2,1)S(1)} %head_part.4), channel_id=1, source_target_pairs={{0,2},{1,3},{2,0},{3,1},{4,6},{5,7},{6,4},{7,5},{8,10},{9,11},{10,... | collective-permute-start | bytes 1572872 | tf_op jit(solution)/shard_map/ppermute | solution.py:444
  95.5 16.4 %collective-permute-start.27 = (bf16[512,512]{1,0:T(8,128)(2,1)S(1)}, bf16[512,512]{1,0:T(8,128)(2,1)S(1)}, u32[]{:S(2)}, u32[]{:S(2)}) collective-permute-start(bf16[512,512]{1,0:T(8,128)(2,1)S(1)} %head_part.5), channel_id=1, source_target_pairs={{0,4},{4,0},{8,12},{12,8},{16,20},{20,16},{24,28},{28,24},{1,5},{5... | collective-permute-start | bytes 1572872 | tf_op jit(solution)/shard_map/ppermute | solution.py:441
  96.1 9.3 %collective-permute-start.22 = (bf16[256,512]{1,0:T(8,128)(2,1)S(1)}, bf16[256,512]{1,0:T(8,128)(2,1)S(1)}, u32[]{:S(2)}, u32[]{:S(2)}) collective-permute-start(bf16[256,512]{1,0:T(8,128)(2,1)S(1)} %add_own.6), channel_id=1, source_target_pairs={{0,16},{4,20},{16,24},{20,28},{24,8},{28,12},{8,0},{12,4},{1,17},{... | collective-permute-start | bytes 786440 | tf_op jit(solution)/shard_map/ppermute | solution.py:457
  99.9 10.7 %collective-permute-start.25 = (bf16[256,512]{1,0:T(8,128)(2,1)S(1)}, bf16[256,512]{1,0:T(8,128)(2,1)S(1)}, u32[]{:S(2)}, u32[]{:S(2)}) collective-permute-start(bf16[256,512]{1,0:T(8,128)(2,1)S(1)} %add_own.7), channel_id=1, source_target_pairs={{0,16},{4,20},{16,24},{20,28},{24,8},{28,12},{8,0},{12,4},{1,17},{... | collective-permute-start | bytes 786440 | tf_op jit(solution)/shard_map/ppermute | solution.py:457
  (14 other events, 35.5 us)

commit v18 on v17

--- a/solution.py
+++ b/solution.py
@@ -473,7 +473,7 @@
     every = lax.all_to_all(
         offered, "ctx", split_axis=0, concat_axis=0, axis_index_groups=lines
     )
-    far, send_far = far_states(line, every)
+    far, send_far = far_states(line, after(every, blocks[1]))
     ends = (far, partner(send_far), near)
     vi, keys_too = inside(after(queries, send_far), keys, out_grad)
     theirs = [after(theirs[0], send_far)]
@@ -498,7 +498,11 @@
     bit = n_head // 2
     while bit:
         own = own + [across(after(r, mine) if len(own) > 1 else r, bit) for r in own]
-        theirs = theirs + [across(r, bit) for r in theirs]
+        last = len(theirs) > 1
+        theirs = theirs + [
+            across(after(r, blocks[2]) if last and i else r, bit)
+            for i, r in enumerate(theirs)
+        ]
         offsets = offsets + [o ^ bit for o in offsets]
         bit //= 2
     own = [own[offsets.index(i)] for i in range(n_head)]
@@ -511,7 +515,8 @@
         vals = (spot, here, after(mine, token), other, own, theirs)
         return pieces(dtype, chains, flops, order, per, step, *vals)
 
-    total = piece(BF16, 0, query_grad, 4 * length * cols * width)
+    token = after(query_grad, blocks[-1])
+    total = piece(BF16, 0, token, 4 * length * cols * width)
     moved = [ring(x) for x in total]
     other_too = across(other, 1)
     lent = lent + [across(after(x, total[0]), 1) for x in blocks[early:]]

time: 114 us -> 102 us (0.89)
  waiting for transfers between devices: 42.2 us -> 30.7 us
  local copies, waits for them, and re-layouts: 8.58 us -> 4.77 us
  starting transfers between devices: 36.6 us -> 39.4 us
    ppermute x8, waiting for transfers between devices: 27.8 us -> 13.6 us  [ring(): return lax.ppermute(x, 'ctx', moves)]
    ppermute x1, waiting for transfers between devices: 0.23 us -> 4.32 us  [back(): return lax.ppermute(x, 'ctx', [(b, a) for a, b in moves])]
    unnamed x34 -> x36, local copies, waits for them, and re-layouts: 8.58 us -> 4.77 us
    ppermute x8, starting transfers between devices: 15.1 us -> 17.9 us  [ring(): return lax.ppermute(x, 'ctx', moves)]
    ppermute x14, waiting for transfers between devices: 3.49 us -> 1.11 us  [across(): return lax.ppermute(x, 'head', [(i, i ^ bit) for i in range(n_head)])]
    ppermute x5, waiting for transfers between devices: 4.16 us -> 5.79 us  [partner(): return lax.ppermute(x, 'ctx', [(i, i ^ 1) for i in range(n_ctx)])]
  transfers between devices with their start and end apart: 29 -> 29, of which waited for: 12 -> 11; matrix products, arithmetic and copies ran while one was open for 0% -> 0% of each run, Pallas kernels for 17% -> 20%
where the time goes in v18:
time: 102 us
  starting transfers between devices  39.4 us (39%)
  waiting for transfers between devices  30.7 us (30%)
  Pallas kernels  26.1 us (26%)
  local copies, waits for them, and re-layouts  4.77 us (5%)
    ppermute x8, starting transfers between devices, ring(): return lax.ppermute(x, 'ctx', moves)  17.9 us
    ppermute x8, waiting for transfers between devices, ring(): return lax.ppermute(x, 'ctx', moves)  13.6 us
    ppermute x5, starting transfers between devices, partner(): return lax.ppermute(x, 'ctx', [(i, i ^ 1) for i in range(n_ctx)])  7.43 us
    ppermute x14, starting transfers between devices, across(): return lax.ppermute(x, 'head', [(i, i ^ bit) for i in range(n_head)])  7.32 us
    pallas_call x4, Pallas kernels, pieces(): call(functools.partial(piece_kernel, order, per, step, count), flops=flop...  5.91 us
    all_to_all x1, waiting for transfers between devices, local(): lax.all_to_all(offered, 'ctx', split_axis=0, concat_axis=0, axis_index_gr...  5.85 us
    ppermute x5, waiting for transfers between devices, partner(): return lax.ppermute(x, 'ctx', [(i, i ^ 1) for i in range(n_ctx)])  5.79 us
    all_to_all x1, starting transfers between devices, local(): lax.all_to_all(offered, 'ctx', split_axis=0, concat_axis=0, axis_index_gr...  5 us
  transfers between devices with their start and end apart: 29, of which 11 were waited for; matrix products, arithmetic and copies ran while one was open for 0% of the time, Pallas kernels for 20%

profile of v18, /device:TPU:0, one launch (start us, length us, event | category | flops | bytes accessed | tf_op | source)
XLA Modules:
  0.0 101.9 jit_solution(2967537898104261934)
XLA Ops:
  0.7 4.0 %states.1 = (f32[2,2,128,128]{3,2,1,0:T(8,128)}, bf16[3,2,128,128]{3,2,1,0:T(8,128)(2,1)}) custom-call(s32[1]{0:T(128)} %bitcast.par_ref, bf16[512,512]{1,0:T(8,128)(2,1)} %q_ref.1, bf16[512,512]{1,0:T(8,128)(2,1)} %k_ref.1, bf16[512,512]{1,0:T(8,128)(2,1)} %v_ref, bf16[512,512]{1,0:T(8,128)(2,1)} %g_ref.1), custom_call_target="tpu_custom_call" | custom-call | flops 1 | bytes 1 | tf_op jit(solution)/shard_map/states/pallas_call | solution.py:67
  4.7 3.0 %collective-permute-start = (bf16[3,2,128,128]{3,2,1,0:T(8,128)(2,1)}, bf16[3,2,128,128]{3,2,1,0:T(8,128)(2,1)S(1)}, u32[]{:S(2)}, u32[]{:S(2)}) collective-permute-start(bf16[3,2,128,128]{3,2,1,0:T(8,128)(2,1)} %get-tuple-element.51), channel_id=1, source_target_pairs={{0,4},{4,0},{8,12},{12,8},{16,20},{20,16},{24,28},{28,24},{1,5},{5... | collective-permute-start | bytes 589832 | tf_op jit(solution)/shard_map/ppermute | solution.py:441
  7.7 2.6 %collective-permute-start.1 = (bf16[512,512]{1,0:T(8,128)(2,1)}, bf16[512,512]{1,0:T(8,128)(2,1)}, u32[]{:S(2)}, u32[]{:S(2)}) collective-permute-start(bf16[512,512]{1,0:T(8,128)(2,1)} %refs_0_.3), channel_id=1, source_target_pairs={{0,16},{4,20},{16,24},{20,28},{24,8},{28,12},{8,0},{12,4},{1,17},{... | collective-permute-start | bytes 1572872 | tf_op jit(solution)/shard_map/ppermute | solution.py:457
  11.2 1.6 %collective-permute-done.got_ref.refs_2_ = bf16[3,2,128,128]{3,2,1,0:T(8,128)(2,1)S(1)} collective-permute-done((bf16[3,2,128,128]{3,2,1,0:T(8,128)(2,1)}, bf16[3,2,128,128]{3,2,1,0:T(8,128)(2,1)S(1)}, u32[]{:S(2)}, u32[]{:S(2)}) %collective-permute-start) | collective-permute-done | bytes 196640 | tf_op jit(solution)/shard_map/ppermute | solution.py:441
  12.8 1.7 %collective-permute-start.7 = (bf16[1,512,512]{2,1,0:T(8,128)(2,1)}, bf16[1,512,512]{2,1,0:T(8,128)(2,1)S(1)}, u32[]{:S(2)}, u32[]{:S(2)}) collective-permute-start(bf16[1,512,512]{2,1,0:T(8,128)(2,1)} %get-tuple-element.67), channel_id=1, source_target_pairs={{0,4},{4,0},{8,12},{12,8},{16,20},{20,16},{24,28},{28,24},{1,5},{5... | collective-permute-start | bytes 1572872 | tf_op jit(solution)/shard_map/ppermute | solution.py:441
  15.3 5.0 %all-to-all-start = ((bf16[4,2,128,128]{3,2,1,0:T(8,128)(2,1)}), bf16[4,2,128,128]{3,2,1,0:T(8,128)(2,1)S(1)}, u32[]{:S(2)}, u32[]{:S(2)}) async-start(bf16[4,2,128,128]{3,2,1,0:T(8,128)(2,1)} %offer.1), calls=%async_computation | async-start | bytes 524288 | tf_op jit(solution)/shard_map/all_to_all | solution.py:473
  20.3 1.5 %collective-permute-start.5 = (bf16[1,512,512]{2,1,0:T(8,128)(2,1)S(1)}, bf16[1,512,512]{2,1,0:T(8,128)(2,1)S(1)}, u32[]{:S(2)}, u32[]{:S(2)}) collective-permute-start(bf16[1,512,512]{2,1,0:T(8,128)(2,1)S(1)} %get-tuple-element.64.refs_0_), channel_id=1, source_target_pairs={{0,2},{1,3},{2,0},{3,1},{4,6},{5,7},{6,4},{7,5},{8,10},{9,11},{10,... | collective-permute-start | bytes 1572872 | tf_op jit(solution)/shard_map/ppermute | solution.py:444
  21.8 1.1 %collective-permute-done.1.refs_1_ = bf16[512,512]{1,0:T(8,128)(2,1)} collective-permute-done((bf16[512,512]{1,0:T(8,128)(2,1)}, bf16[512,512]{1,0:T(8,128)(2,1)}, u32[]{:S(2)}, u32[]{:S(2)}) %collective-permute-start.1) | collective-permute-done | bytes 524320 | tf_op jit(solution)/shard_map/ppermute | solution.py:457
  23.0 5.8 %all-to-all-done.every_ref = bf16[4,2,128,128]{3,2,1,0:T(8,128)(2,1)S(1)} async-done(((bf16[4,2,128,128]{3,2,1,0:T(8,128)(2,1)}), bf16[4,2,128,128]{3,2,1,0:T(8,128)(2,1)S(1)}, u32[]{:S(2)}, u32[]{:S(2)}) %all-to-all-start) | async-done | bytes 262176 | tf_op jit(solution)/shard_map/all_to_all | solution.py:473
  30.4 1.5 %collective-permute-start.9 = (bf16[1,512,512]{2,1,0:T(8,128)(2,1)S(1)}, bf16[1,512,512]{2,1,0:T(8,128)(2,1)S(1)}, u32[]{:S(2)}, u32[]{:S(2)}) collective-permute-start(bf16[1,512,512]{2,1,0:T(8,128)(2,1)S(1)} %collective-permute-done.7.refs_4_), channel_id=1, source_target_pairs={{0,2},{1,3},{2,0},{3,1},{4,6},{5,7},{6,4},{7,5},{8,10},{9,11},{10,... | collective-permute-start | bytes 1572872 | tf_op jit(solution)/shard_map/ppermute | solution.py:444
  33.0 3.0 %inside.1 = (f32[512,512]{1,0:T(8,128)S(1)}, bf16[512,512]{1,0:T(8,128)(2,1)S(1)}) custom-call(bf16[512,512]{1,0:T(8,128)(2,1)S(1)} %copy-done.5, bf16[512,512]{1,0:T(8,128)(2,1)S(1)} %copy-done.7, bf16[512,512]{1,0:T(8,128)(2,1)S(1)} %copy-done.9), custom_call_target="tpu_custom_call" | custom-call | flops 1 | bytes 1 | tf_op jit(solution)/shard_map/inside/pallas_call | solution.py:147
  37.1 4.2 %collective-permute-done.10.refs_2_ = bf16[512,512]{1,0:T(8,128)(2,1)S(1)} collective-permute-done((bf16[512,512]{1,0:T(8,128)(2,1)}, bf16[512,512]{1,0:T(8,128)(2,1)S(1)}, u32[]{:S(2)}, u32[]{:S(2)}) %collective-permute-start.10) | collective-permute-done | bytes 524320 | tf_op jit(solution)/shard_map/ppermute | solution.py:457
  41.3 1.5 %collective-permute-start.3 = (bf16[512,512]{1,0:T(8,128)(2,1)S(1)}, bf16[512,512]{1,0:T(8,128)(2,1)S(1)}, u32[]{:S(2)}, u32[]{:S(2)}) collective-permute-start(bf16[512,512]{1,0:T(8,128)(2,1)S(1)} %finish_value.1.a_ref.x_ref), channel_id=1, source_target_pairs={{0,4},{4,0},{8,12},{12,8},{16,20},{20,16},{24,28},{28,24},{1,5},{5... | collective-permute-start | bytes 1572872 | tf_op jit(solution)/shard_map/ppermute | solution.py:441
  44.7 1.7 %collective-permute-start.14 = (bf16[512,512]{1,0:T(8,128)(2,1)}, bf16[512,512]{1,0:T(8,128)(2,1)}, u32[]{:S(2)}, u32[]{:S(2)}) collective-permute-start(bf16[512,512]{1,0:T(8,128)(2,1)} %refs_0_.3), channel_id=1, source_target_pairs={{16,0},{20,4},{24,16},{28,20},{8,24},{12,28},{0,8},{4,12},{17,1},{... | collective-permute-start | bytes 1572872 | tf_op jit(solution)/shard_map/ppermute | solution.py:460
  47.7 4.2 %collective-permute-done.3.b_ref.x_ref = bf16[512,512]{1,0:T(8,128)(2,1)S(1)} collective-permute-done((bf16[512,512]{1,0:T(8,128)(2,1)S(1)}, bf16[512,512]{1,0:T(8,128)(2,1)S(1)}, u32[]{:S(2)}, u32[]{:S(2)}) %collective-permute-start.3) | collective-permute-done | bytes 524320 | tf_op jit(solution)/shard_map/ppermute | solution.py:441
  54.1 1.8 %pieces.4 = (bf16[256,512]{1,0:T(8,128)(2,1)S(1)}, bf16[256,512]{1,0:T(8,128)(2,1)S(1)}) custom-call(s32[1]{0:T(128)} %bitcast.3.spot_ref, s32[1]{0:T(128)} %bitcast.2.head_ref.at_ref, bf16[512,512]{1,0:T(8,128)(2,1)S(1)} %finish_value.1.a_ref.x_ref, bf16[512,512]{1,0:T(8,128)(2,1)S(1)} %collective-permute-done.3.b_ref.x_ref, ...), custom_call_target="tpu_custom_call" | custom-call | flops 536870912 | bytes 1 | tf_op jit(solution)/shard_map/pieces/pallas_call | solution.py:291
  55.9 4.3 %collective-permute-done.14.refs_3_ = bf16[512,512]{1,0:T(8,128)(2,1)} collective-permute-done((bf16[512,512]{1,0:T(8,128)(2,1)}, bf16[512,512]{1,0:T(8,128)(2,1)}, u32[]{:S(2)}, u32[]{:S(2)}) %collective-permute-start.14) | collective-permute-done | bytes 524320 | tf_op jit(solution)/shard_map/ppermute | solution.py:460
  61.3 1.8 %pieces.5 = (f32[256,512]{1,0:T(8,128)S(1)}, f32[256,512]{1,0:T(8,128)S(1)}) custom-call(s32[1]{0:T(128)} %bitcast.3.spot_ref, s32[1]{0:T(128)} %bitcast.2.head_ref.at_ref, bf16[512,512]{1,0:T(8,128)(2,1)S(1)} %finish_value.1.a_ref.x_ref, bf16[512,512]{1,0:T(8,128)(2,1)S(1)} %collective-permute-done.3.b_ref.x_ref, ...), custom_call_target="tpu_custom_call" | custom-call | flops 1 | bytes 1 | tf_op jit(solution)/shard_map/pieces/pallas_call | solution.py:291
  63.1 1.8 %collective-permute-start.12 = (bf16[256,512]{1,0:T(8,128)(2,1)S(1)}, bf16[256,512]{1,0:T(8,128)(2,1)S(1)}, u32[]{:S(2)}, u32[]{:S(2)}) collective-permute-start(bf16[256,512]{1,0:T(8,128)(2,1)S(1)} %get-tuple-element.71), channel_id=1, source_target_pairs={{0,16},{4,20},{16,24},{20,28},{24,8},{28,12},{8,0},{12,4},{1,17},{... | collective-permute-start | bytes 786440 | tf_op jit(solution)/shard_map/ppermute | solution.py:457
  64.9 1.3 %arrange.1 = (bf16[2,512,512]{2,1,0:T(8,128)(2,1)S(1)}, bf16[2,512,512]{2,1,0:T(8,128)(2,1)S(1)}) custom-call(s32[1]{0:T(128)} %bitcast.2.head_ref.at_ref, s32[1]{0:T(128)} %bitcast.3.spot_ref, bf16[512,512]{1,0:T(8,128)(2,1)} %refs_0_.3, bf16[512,512]{1,0:T(8,128)(2,1)} %collective-permute-done.1.refs_1_, bf16[512,512]{1,0:T(8,128)(2,1)S(1)} %copy-done.16, ...), custom_call_target="tpu_custom_call" | custom-call | flops 1 | bytes 1 | tf_op jit(solution)/shard_map/arrange/pallas_call | solution.py:367
  66.9 1.6 %collective-permute-start.24 = (bf16[512,512]{1,0:T(8,128)(2,1)S(1)}, bf16[512,512]{1,0:T(8,128)(2,1)S(1)}, u32[]{:S(2)}, u32[]{:S(2)}) collective-permute-start(bf16[512,512]{1,0:T(8,128)(2,1)S(1)} %head_part.3), channel_id=1, source_target_pairs={{0,2},{1,3},{2,0},{3,1},{4,6},{5,7},{6,4},{7,5},{8,10},{9,11},{10,... | collective-permute-start | bytes 1572872 | tf_op jit(solution)/shard_map/ppermute | solution.py:444
  68.5 1.8 %collective-permute-start.21 = (bf16[256,512]{1,0:T(8,128)(2,1)S(1)}, bf16[256,512]{1,0:T(8,128)(2,1)S(1)}, u32[]{:S(2)}, u32[]{:S(2)}) collective-permute-start(bf16[256,512]{1,0:T(8,128)(2,1)S(1)} %get-tuple-element.83), channel_id=1, source_target_pairs={{0,16},{4,20},{16,24},{20,28},{24,8},{28,12},{8,0},{12,4},{1,17},{... | collective-permute-start | bytes 786440 | tf_op jit(solution)/shard_map/ppermute | solution.py:457
  71.5 2.0 %collective-permute-start.20 = (bf16[256,512]{1,0:T(8,128)(2,1)S(1)}, bf16[256,512]{1,0:T(8,128)(2,1)S(1)}, u32[]{:S(2)}, u32[]{:S(2)}) collective-permute-start(bf16[256,512]{1,0:T(8,128)(2,1)S(1)} %add_own.4), channel_id=1, source_target_pairs={{0,16},{4,20},{16,24},{20,28},{24,8},{28,12},{8,0},{12,4},{1,17},{... | collective-permute-start | bytes 786440 | tf_op jit(solution)/shard_map/ppermute | solution.py:457
  73.4 4.4 %collective-permute-done.21.moved_ref = bf16[256,512]{1,0:T(8,128)(2,1)S(1)} collective-permute-done((bf16[256,512]{1,0:T(8,128)(2,1)S(1)}, bf16[256,512]{1,0:T(8,128)(2,1)S(1)}, u32[]{:S(2)}, u32[]{:S(2)}) %collective-permute-start.21) | collective-permute-done | bytes 262176 | tf_op jit(solution)/shard_map/ppermute | solution.py:457
  77.8 2.7 %collective-permute-start.23 = (bf16[256,512]{1,0:T(8,128)(2,1)S(1)}, bf16[256,512]{1,0:T(8,128)(2,1)S(1)}, u32[]{:S(2)}, u32[]{:S(2)}) collective-permute-start(bf16[256,512]{1,0:T(8,128)(2,1)S(1)} %add_own.5), channel_id=1, source_target_pairs={{0,16},{4,20},{16,24},{20,28},{24,8},{28,12},{8,0},{12,4},{1,17},{... | collective-permute-start | bytes 786440 | tf_op jit(solution)/shard_map/ppermute | solution.py:457
  82.2 1.1 %pieces.7 = (f32[256,512]{1,0:T(8,128)S(1)}, f32[256,512]{1,0:T(8,128)S(1)}) custom-call(s32[1]{0:T(128)} %bitcast.3.spot_ref, s32[1]{0:T(128)} %bitcast.2.head_ref.at_ref, bf16[512,512]{1,0:T(8,128)(2,1)S(1)} %finish_value.1.a_ref.x_ref, bf16[512,512]{1,0:T(8,128)(2,1)S(1)} %collective-permute-done.3.b_ref.x_ref, ...), custom_call_target="tpu_custom_call" | custom-call | flops 1 | bytes 1 | tf_op jit(solution)/shard_map/pieces/pallas_call | solution.py:291
  84.8 2.7 %collective-permute-start.22 = (bf16[256,512]{1,0:T(8,128)(2,1)S(1)}, bf16[256,512]{1,0:T(8,128)(2,1)S(1)}, u32[]{:S(2)}, u32[]{:S(2)}) collective-permute-start(bf16[256,512]{1,0:T(8,128)(2,1)S(1)} %add_own.6), channel_id=1, source_target_pairs={{0,16},{4,20},{16,24},{20,28},{24,8},{28,12},{8,0},{12,4},{1,17},{... | collective-permute-start | bytes 786440 | tf_op jit(solution)/shard_map/ppermute | solution.py:457
  88.2 3.4 %collective-permute-start.25 = (bf16[256,512]{1,0:T(8,128)(2,1)S(1)}, bf16[256,512]{1,0:T(8,128)(2,1)S(1)}, u32[]{:S(2)}, u32[]{:S(2)}) collective-permute-start(bf16[256,512]{1,0:T(8,128)(2,1)S(1)} %add_own.7), channel_id=1, source_target_pairs={{0,16},{4,20},{16,24},{20,28},{24,8},{28,12},{8,0},{12,4},{1,17},{... | collective-permute-start | bytes 786440 | tf_op jit(solution)/shard_map/ppermute | solution.py:457
  91.6 4.1 %others.1 = (bf16[512,512]{1,0:T(8,128)(2,1)}, bf16[512,512]{1,0:T(8,128)(2,1)}) custom-call(s32[1]{0:T(128)} %bitcast.par_ref, bf16[512,512]{1,0:T(8,128)(2,1)S(1)} %copy-done.6, bf16[512,512]{1,0:T(8,128)(2,1)S(1)} %copy-done.8, bf16[512,512]{1,0:T(8,128)(2,1)S(1)} %copy-done.11, bf16[512,512]{1,0:T(8,128)(2,1)S(1)} %copy-done.10, ...), custom_call_target="tpu_custom_call" | custom-call | flops 1 | bytes 1 | tf_op jit(solution)/shard_map/others/pallas_call | solution.py:246
  95.7 3.0 %collective-permute-done.25.refs_1_ = bf16[256,512]{1,0:T(8,128)(2,1)S(1)} collective-permute-done((bf16[256,512]{1,0:T(8,128)(2,1)S(1)}, bf16[256,512]{1,0:T(8,128)(2,1)S(1)}, u32[]{:S(2)}, u32[]{:S(2)}) %collective-permute-start.25) | collective-permute-done | bytes 262176 | tf_op jit(solution)/shard_map/ppermute | solution.py:457
  98.8 1.3 %finish_weight.1 = f32[512,512]{1,0:T(8,128)} custom-call(bf16[256,512]{1,0:T(8,128)(2,1)S(1)} %collective-permute-done.22.refs_0_, bf16[256,512]{1,0:T(8,128)(2,1)S(1)} %collective-permute-done.25.refs_1_, f32[256,512]{1,0:T(8,128)S(1)} %get-tuple-element.89.refs_2_, f32[256,512]{1,0:T(8,128)S(1)} %get-tuple-element.94.refs_3_), custom_call_target="tpu_custom_call" | custom-call | flops 1 | bytes 1 | tf_op jit(solution)/shard_map/finish_weight/pallas_call | solution.py:315
  100.1 1.8 %join.1 = bf16[512,1024]{1,0:T(8,128)(2,1)} custom-call(s32[1]{0:T(128)} %bitcast.par_ref, s32[1]{0:T(128)} %bitcast.2.head_ref.at_ref, bf16[512,512]{1,0:T(8,128)(2,1)S(1)} %finish_value.1.a_ref.x_ref, bf16[512,512]{1,0:T(8,128)(2,1)S(1)} %collective-permute-done.19.y_ref, bf16[2,512,512]{2,1,0:T(8,128)(2,1)S(1)} %get-tuple-element.79.w_ref, ...), custom_call_target="tpu_custom_call" | custom-call | flops 1 | bytes 1 | tf_op jit(solution)/shard_map/join/pallas_call | solution.py:418
  (83 shorter events, 17.4 us)
Async XLA Ops:
  4.7 9.9 %copy-start.17 = (f32[2,2,128,128]{3,2,1,0:T(8,128)S(1)}, f32[2,2,128,128]{3,2,1,0:T(8,128)}, u32[]{:S(2)}) copy-start(f32[2,2,128,128]{3,2,1,0:T(8,128)} %get-tuple-element.50.keep_ref) | copy-start | bytes 786436
  4.7 8.1 %collective-permute-start = (bf16[3,2,128,128]{3,2,1,0:T(8,128)(2,1)}, bf16[3,2,128,128]{3,2,1,0:T(8,128)(2,1)S(1)}, u32[]{:S(2)}, u32[]{:S(2)}) collective-permute-start(bf16[3,2,128,128]{3,2,1,0:T(8,128)(2,1)} %get-tuple-element.51), channel_id=1, source_target_pairs={{0,4},{4,0},{8,12},{12,8},{16,20},{20,16},{24,28},{28,24},{1,5},{5... | collective-permute-start | bytes 589832 | tf_op jit(solution)/shard_map/ppermute | solution.py:441
  7.7 15.3 %collective-permute-start.1 = (bf16[512,512]{1,0:T(8,128)(2,1)}, bf16[512,512]{1,0:T(8,128)(2,1)}, u32[]{:S(2)}, u32[]{:S(2)}) collective-permute-start(bf16[512,512]{1,0:T(8,128)(2,1)} %refs_0_.3), channel_id=1, source_target_pairs={{0,16},{4,20},{16,24},{20,28},{24,8},{28,12},{8,0},{12,4},{1,17},{... | collective-permute-start | bytes 1572872 | tf_op jit(solution)/shard_map/ppermute | solution.py:457
  12.8 17.6 %collective-permute-start.7 = (bf16[1,512,512]{2,1,0:T(8,128)(2,1)}, bf16[1,512,512]{2,1,0:T(8,128)(2,1)S(1)}, u32[]{:S(2)}, u32[]{:S(2)}) collective-permute-start(bf16[1,512,512]{2,1,0:T(8,128)(2,1)} %get-tuple-element.67), channel_id=1, source_target_pairs={{0,4},{4,0},{8,12},{12,8},{16,20},{20,16},{24,28},{28,24},{1,5},{5... | collective-permute-start | bytes 1572872 | tf_op jit(solution)/shard_map/ppermute | solution.py:441
  14.5 17.4 %copy-start.7 = (bf16[512,512]{1,0:T(8,128)(2,1)S(1)}, bf16[512,512]{1,0:T(8,128)(2,1)}, u32[]{:S(2)}) copy-start(bf16[512,512]{1,0:T(8,128)(2,1)} %k_ref.1) | copy-start | bytes 1572868
  15.3 16.6 %copy-start.5 = (bf16[512,512]{1,0:T(8,128)(2,1)S(1)}, bf16[512,512]{1,0:T(8,128)(2,1)}, u32[]{:S(2)}) copy-start(bf16[512,512]{1,0:T(8,128)(2,1)} %q_ref.1) | copy-start | bytes 1572868
  15.3 13.5 %all-to-all-start = ((bf16[4,2,128,128]{3,2,1,0:T(8,128)(2,1)}), bf16[4,2,128,128]{3,2,1,0:T(8,128)(2,1)S(1)}, u32[]{:S(2)}, u32[]{:S(2)}) async-start(bf16[4,2,128,128]{3,2,1,0:T(8,128)(2,1)} %offer.1), calls=%async_computation | async-start | bytes 524288 | tf_op jit(solution)/shard_map/all_to_all | solution.py:473
  20.3 16.2 %collective-permute-start.5 = (bf16[1,512,512]{2,1,0:T(8,128)(2,1)S(1)}, bf16[1,512,512]{2,1,0:T(8,128)(2,1)S(1)}, u32[]{:S(2)}, u32[]{:S(2)}) collective-permute-start(bf16[1,512,512]{2,1,0:T(8,128)(2,1)S(1)} %get-tuple-element.64.refs_0_), channel_id=1, source_target_pairs={{0,2},{1,3},{2,0},{3,1},{4,6},{5,7},{6,4},{7,5},{8,10},{9,11},{10,... | collective-permute-start | bytes 1572872 | tf_op jit(solution)/shard_map/ppermute | solution.py:444
  28.9 7.1 %collective-permute-start.2 = (bf16[2,2,128,128]{3,2,1,0:T(8,128)(2,1)S(1)}, bf16[2,2,128,128]{3,2,1,0:T(8,128)(2,1)S(1)}, u32[]{:S(2)}, u32[]{:S(2)}) collective-permute-start(bf16[2,2,128,128]{3,2,1,0:T(8,128)(2,1)S(1)} %get-tuple-element.54), channel_id=1, source_target_pairs={{0,4},{4,0},{8,12},{12,8},{16,20},{20,16},{24,28},{28,24},{1,5},{5... | collective-permute-start | bytes 393224 | tf_op jit(solution)/shard_map/ppermute | solution.py:441
  29.5 11.8 %collective-permute-start.10 = (bf16[512,512]{1,0:T(8,128)(2,1)}, bf16[512,512]{1,0:T(8,128)(2,1)S(1)}, u32[]{:S(2)}, u32[]{:S(2)}) collective-permute-start(bf16[512,512]{1,0:T(8,128)(2,1)} %collective-permute-done.1.refs_1_), channel_id=1, source_target_pairs={{0,16},{4,20},{16,24},{20,28},{24,8},{28,12},{8,0},{12,4},{1,17},{... | collective-permute-start | bytes 1572872 | tf_op jit(solution)/shard_map/ppermute | solution.py:457
  30.4 13.5 %collective-permute-start.9 = (bf16[1,512,512]{2,1,0:T(8,128)(2,1)S(1)}, bf16[1,512,512]{2,1,0:T(8,128)(2,1)S(1)}, u32[]{:S(2)}, u32[]{:S(2)}) collective-permute-start(bf16[1,512,512]{2,1,0:T(8,128)(2,1)S(1)} %collective-permute-done.7.refs_4_), channel_id=1, source_target_pairs={{0,2},{1,3},{2,0},{3,1},{4,6},{5,7},{6,4},{7,5},{8,10},{9,11},{10,... | collective-permute-start | bytes 1572872 | tf_op jit(solution)/shard_map/ppermute | solution.py:444
  36.5 7.4 %collective-permute-start.6 = (bf16[1,512,512]{2,1,0:T(8,128)(2,1)S(1)}, bf16[1,512,512]{2,1,0:T(8,128)(2,1)S(1)}, u32[]{:S(2)}, u32[]{:S(2)}) collective-permute-start(bf16[1,512,512]{2,1,0:T(8,128)(2,1)S(1)} %collective-permute-done.5.refs_2_), channel_id=1, source_target_pairs={{0,1},{1,0},{2,3},{3,2},{4,5},{5,4},{6,7},{7,6},{8,9},{9,8},{10,11... | collective-permute-start | bytes 1572872 | tf_op jit(solution)/shard_map/ppermute | solution.py:444
  36.6 9.9 %collective-permute-start.4 = (bf16[1,512,512]{2,1,0:T(8,128)(2,1)S(1)}, bf16[1,512,512]{2,1,0:T(8,128)(2,1)S(1)}, u32[]{:S(2)}, u32[]{:S(2)}) collective-permute-start(bf16[1,512,512]{2,1,0:T(8,128)(2,1)S(1)} %get-tuple-element.64.refs_0_), channel_id=1, source_target_pairs={{0,1},{1,0},{2,3},{3,2},{4,5},{5,4},{6,7},{7,6},{8,9},{9,8},{10,11... | collective-permute-start | bytes 1572872 | tf_op jit(solution)/shard_map/ppermute | solution.py:444
  37.1 10.4 %collective-permute-start.8 = (bf16[1,512,512]{2,1,0:T(8,128)(2,1)S(1)}, bf16[1,512,512]{2,1,0:T(8,128)(2,1)}, u32[]{:S(2)}, u32[]{:S(2)}) collective-permute-start(bf16[1,512,512]{2,1,0:T(8,128)(2,1)S(1)} %collective-permute-done.7.refs_4_), channel_id=1, source_target_pairs={{0,1},{1,0},{2,3},{3,2},{4,5},{5,4},{6,7},{7,6},{8,9},{9,8},{10,11... | collective-permute-start | bytes 1572872 | tf_op jit(solution)/shard_map/ppermute | solution.py:444
  41.3 10.7 %collective-permute-start.3 = (bf16[512,512]{1,0:T(8,128)(2,1)S(1)}, bf16[512,512]{1,0:T(8,128)(2,1)S(1)}, u32[]{:S(2)}, u32[]{:S(2)}) collective-permute-start(bf16[512,512]{1,0:T(8,128)(2,1)S(1)} %finish_value.1.a_ref.x_ref), channel_id=1, source_target_pairs={{0,4},{4,0},{8,12},{12,8},{16,20},{20,16},{24,28},{28,24},{1,5},{5... | collective-permute-start | bytes 1572872 | tf_op jit(solution)/shard_map/ppermute | solution.py:441
  43.9 8.1 %collective-permute-start.11 = (bf16[1,512,512]{2,1,0:T(8,128)(2,1)S(1)}, bf16[1,512,512]{2,1,0:T(8,128)(2,1)}, u32[]{:S(2)}, u32[]{:S(2)}) collective-permute-start(bf16[1,512,512]{2,1,0:T(8,128)(2,1)S(1)} %collective-permute-done.9.refs_6_), channel_id=1, source_target_pairs={{0,1},{1,0},{2,3},{3,2},{4,5},{5,4},{6,7},{7,6},{8,9},{9,8},{10,11... | collective-permute-start | bytes 1572872 | tf_op jit(solution)/shard_map/ppermute | solution.py:444
  44.7 15.6 %collective-permute-start.14 = (bf16[512,512]{1,0:T(8,128)(2,1)}, bf16[512,512]{1,0:T(8,128)(2,1)}, u32[]{:S(2)}, u32[]{:S(2)}) collective-permute-start(bf16[512,512]{1,0:T(8,128)(2,1)} %refs_0_.3), channel_id=1, source_target_pairs={{16,0},{20,4},{24,16},{28,20},{8,24},{12,28},{0,8},{4,12},{17,1},{... | collective-permute-start | bytes 1572872 | tf_op jit(solution)/shard_map/ppermute | solution.py:460
  47.2 13.5 %collective-permute-start.16 = (bf16[512,512]{1,0:T(8,128)(2,1)}, bf16[512,512]{1,0:T(8,128)(2,1)}, u32[]{:S(2)}, u32[]{:S(2)}) collective-permute-start(bf16[512,512]{1,0:T(8,128)(2,1)} %collective-permute-done.1.refs_1_), channel_id=1, source_target_pairs={{0,1},{1,0},{2,3},{3,2},{4,5},{5,4},{6,7},{7,6},{8,9},{9,8},{10,11... | collective-permute-start | bytes 1572872 | tf_op jit(solution)/shard_map/ppermute | solution.py:444
  47.5 15.6 %collective-permute-start.15 = (bf16[512,512]{1,0:T(8,128)(2,1)}, bf16[512,512]{1,0:T(8,128)(2,1)S(1)}, u32[]{:S(2)}, u32[]{:S(2)}) collective-permute-start(bf16[512,512]{1,0:T(8,128)(2,1)} %refs_0_.3), channel_id=1, source_target_pairs={{0,1},{1,0},{2,3},{3,2},{4,5},{5,4},{6,7},{7,6},{8,9},{9,8},{10,11... | collective-permute-start | bytes 1572872 | tf_op jit(solution)/shard_map/ppermute | solution.py:444
  60.2 4.6 %collective-permute-start.18 = (bf16[512,512]{1,0:T(8,128)(2,1)}, bf16[512,512]{1,0:T(8,128)(2,1)S(1)}, u32[]{:S(2)}, u32[]{:S(2)}) collective-permute-start(bf16[512,512]{1,0:T(8,128)(2,1)} %collective-permute-done.14.refs_3_), channel_id=1, source_target_pairs={{0,1},{1,0},{2,3},{3,2},{4,5},{5,4},{6,7},{7,6},{8,9},{9,8},{10,11... | collective-permute-start | bytes 1572872 | tf_op jit(solution)/shard_map/ppermute | solution.py:444
  60.2 4.6 %collective-permute-start.17 = (bf16[512,512]{1,0:T(8,128)(2,1)S(1)}, bf16[512,512]{1,0:T(8,128)(2,1)S(1)}, u32[]{:S(2)}, u32[]{:S(2)}) collective-permute-start(bf16[512,512]{1,0:T(8,128)(2,1)S(1)} %copy-done.16), channel_id=1, source_target_pairs={{0,1},{1,0},{2,3},{3,2},{4,5},{5,4},{6,7},{7,6},{8,9},{9,8},{10,11... | collective-permute-start | bytes 1572872 | tf_op jit(solution)/shard_map/ppermute | solution.py:444
  60.7 5.4 %collective-permute-start.13 = (bf16[512,512]{1,0:T(8,128)(2,1)S(1)}, bf16[512,512]{1,0:T(8,128)(2,1)S(1)}, u32[]{:S(2)}, u32[]{:S(2)}) collective-permute-start(bf16[512,512]{1,0:T(8,128)(2,1)S(1)} %collective-permute-done.3.b_ref.x_ref), channel_id=1, source_target_pairs={{0,1},{1,0},{2,3},{3,2},{4,5},{5,4},{6,7},{7,6},{8,9},{9,8},{10,11... | collective-permute-start | bytes 1572872 | tf_op jit(solution)/shard_map/ppermute | solution.py:444
  60.8 9.6 %collective-permute-start.19 = (bf16[512,512]{1,0:T(8,128)(2,1)S(1)}, bf16[512,512]{1,0:T(8,128)(2,1)S(1)}, u32[]{:S(2)}, u32[]{:S(2)}) collective-permute-start(bf16[512,512]{1,0:T(8,128)(2,1)S(1)} %finish_value.1.a_ref.x_ref), channel_id=1, source_target_pairs={{0,1},{1,0},{2,3},{3,2},{4,5},{5,4},{6,7},{7,6},{8,9},{9,8},{10,11... | collective-permute-start | bytes 1572872 | tf_op jit(solution)/shard_map/ppermute | solution.py:444
  63.1 8.3 %collective-permute-start.12 = (bf16[256,512]{1,0:T(8,128)(2,1)S(1)}, bf16[256,512]{1,0:T(8,128)(2,1)S(1)}, u32[]{:S(2)}, u32[]{:S(2)}) collective-permute-start(bf16[256,512]{1,0:T(8,128)(2,1)S(1)} %get-tuple-element.71), channel_id=1, source_target_pairs={{0,16},{4,20},{16,24},{20,28},{24,8},{28,12},{8,0},{12,4},{1,17},{... | collective-permute-start | bytes 786440 | tf_op jit(solution)/shard_map/ppermute | solution.py:457
  66.9 16.5 %collective-permute-start.24 = (bf16[512,512]{1,0:T(8,128)(2,1)S(1)}, bf16[512,512]{1,0:T(8,128)(2,1)S(1)}, u32[]{:S(2)}, u32[]{:S(2)}) collective-permute-start(bf16[512,512]{1,0:T(8,128)(2,1)S(1)} %head_part.3), channel_id=1, source_target_pairs={{0,2},{1,3},{2,0},{3,1},{4,6},{5,7},{6,4},{7,5},{8,10},{9,11},{10,... | collective-permute-start | bytes 1572872 | tf_op jit(solution)/shard_map/ppermute | solution.py:444
  68.5 9.2 %collective-permute-start.21 = (bf16[256,512]{1,0:T(8,128)(2,1)S(1)}, bf16[256,512]{1,0:T(8,128)(2,1)S(1)}, u32[]{:S(2)}, u32[]{:S(2)}) collective-permute-start(bf16[256,512]{1,0:T(8,128)(2,1)S(1)} %get-tuple-element.83), channel_id=1, source_target_pairs={{0,16},{4,20},{16,24},{20,28},{24,8},{28,12},{8,0},{12,4},{1,17},{... | collective-permute-start | bytes 786440 | tf_op jit(solution)/shard_map/ppermute | solution.py:457
  71.5 11.9 %collective-permute-start.20 = (bf16[256,512]{1,0:T(8,128)(2,1)S(1)}, bf16[256,512]{1,0:T(8,128)(2,1)S(1)}, u32[]{:S(2)}, u32[]{:S(2)}) collective-permute-start(bf16[256,512]{1,0:T(8,128)(2,1)S(1)} %add_own.4), channel_id=1, source_target_pairs={{0,16},{4,20},{16,24},{20,28},{24,8},{28,12},{8,0},{12,4},{1,17},{... | collective-permute-start | bytes 786440 | tf_op jit(solution)/shard_map/ppermute | solution.py:457
  77.8 10.3 %collective-permute-start.23 = (bf16[256,512]{1,0:T(8,128)(2,1)S(1)}, bf16[256,512]{1,0:T(8,128)(2,1)S(1)}, u32[]{:S(2)}, u32[]{:S(2)}) collective-permute-start(bf16[256,512]{1,0:T(8,128)(2,1)S(1)} %add_own.5), channel_id=1, source_target_pairs={{0,16},{4,20},{16,24},{20,28},{24,8},{28,12},{8,0},{12,4},{1,17},{... | collective-permute-start | bytes 786440 | tf_op jit(solution)/shard_map/ppermute | solution.py:457
  80.6 19.5 %collective-permute-start.26 = (bf16[512,512]{1,0:T(8,128)(2,1)S(1)}, bf16[512,512]{1,0:T(8,128)(2,1)S(1)}, u32[]{:S(2)}, u32[]{:S(2)}) collective-permute-start(bf16[512,512]{1,0:T(8,128)(2,1)S(1)} %head_part.4), channel_id=1, source_target_pairs={{0,2},{1,3},{2,0},{3,1},{4,6},{5,7},{6,4},{7,5},{8,10},{9,11},{10,... | collective-permute-start | bytes 1572872 | tf_op jit(solution)/shard_map/ppermute | solution.py:444
  84.2 15.9 %collective-permute-start.27 = (bf16[512,512]{1,0:T(8,128)(2,1)S(1)}, bf16[512,512]{1,0:T(8,128)(2,1)S(1)}, u32[]{:S(2)}, u32[]{:S(2)}) collective-permute-start(bf16[512,512]{1,0:T(8,128)(2,1)S(1)} %head_part.5), channel_id=1, source_target_pairs={{0,4},{4,0},{8,12},{12,8},{16,20},{20,16},{24,28},{28,24},{1,5},{5... | collective-permute-start | bytes 1572872 | tf_op jit(solution)/shard_map/ppermute | solution.py:441
  84.8 10.9 %collective-permute-start.22 = (bf16[256,512]{1,0:T(8,128)(2,1)S(1)}, bf16[256,512]{1,0:T(8,128)(2,1)S(1)}, u32[]{:S(2)}, u32[]{:S(2)}) collective-permute-start(bf16[256,512]{1,0:T(8,128)(2,1)S(1)} %add_own.6), channel_id=1, source_target_pairs={{0,16},{4,20},{16,24},{20,28},{24,8},{28,12},{8,0},{12,4},{1,17},{... | collective-permute-start | bytes 786440 | tf_op jit(solution)/shard_map/ppermute | solution.py:457
  88.2 10.6 %collective-permute-start.25 = (bf16[256,512]{1,0:T(8,128)(2,1)S(1)}, bf16[256,512]{1,0:T(8,128)(2,1)S(1)}, u32[]{:S(2)}, u32[]{:S(2)}) collective-permute-start(bf16[256,512]{1,0:T(8,128)(2,1)S(1)} %add_own.7), channel_id=1, source_target_pairs={{0,16},{4,20},{16,24},{20,28},{24,8},{28,12},{8,0},{12,4},{1,17},{... | collective-permute-start | bytes 786440 | tf_op jit(solution)/shard_map/ppermute | solution.py:457
  (15 other events, 73.0 us)

commit v19 on v18

--- a/solution.py
+++ b/solution.py
@@ -543,17 +543,19 @@
             if step == pairs - 2 and i == chains - 1:
                 lead = (here, after(other, token), other_too, weight, borrowed)
                 token = part = head_part(*lead, got_other)
-            token = add_own(moved[i], after(local_part[i], token))
+            ready = [token] + (moved[i + 1 :] if step == 1 else [])
+            own_part = after(local_part[i], *ready)
+            token = add_own(moved[i], own_part)
             moved[i] = ring(token)
         if step < pairs - 2:
             local_part = piece(F32, step + 1, token)
             token = local_part[0]
     swapped = partner(part)
-    weight_grad = finish_weight(1.0 / math.sqrt(length * n_ctx), moved, last)
-    mine = after(mine, weight_grad)
     input_grad = join(
         par, here, per, mine, mine_too, weight, borrowed, got_mine, swapped
     )
+    last = [after(last[0], input_grad), *last[1:]]
+    weight_grad = finish_weight(1.0 / math.sqrt(length * n_ctx), moved, last)
     return (query_grad, key_grad, input_grad, weight_grad)
 
 

time: 102 us -> 109 us (1.069)
  waiting for transfers between devices: 30.7 us -> 38 us
  starting transfers between devices: 39.4 us -> 37.3 us
    ppermute x8, waiting for transfers between devices: 13.6 us -> 20.9 us  [ring(): return lax.ppermute(x, 'ctx', moves)]
    ppermute x8, starting transfers between devices: 17.9 us -> 14.8 us  [ring(): return lax.ppermute(x, 'ctx', moves)]
  transfers between devices with their start and end apart: 29 -> 29, of which waited for: 11 -> 12; matrix products, arithmetic and copies ran while one was open for 0% -> 0% of each run, Pallas kernels for 20% -> 19%
where the time goes in v19:
time: 109 us; the launch traced here: 108 us
  waiting for transfers between devices  38 us (35%)
  starting transfers between devices  37.3 us (34%)
  Pallas kernels  26.1 us (24%)
  local copies, waits for them, and re-layouts  5.76 us (5%)
    ppermute x8, waiting for transfers between devices, ring(): return lax.ppermute(x, 'ctx', moves)  20.9 us
    ppermute x8, starting transfers between devices, ring(): return lax.ppermute(x, 'ctx', moves)  14.8 us
    ppermute x14, starting transfers between devices, across(): return lax.ppermute(x, 'head', [(i, i ^ bit) for i in range(n_head)])  8.27 us
    ppermute x5, starting transfers between devices, partner(): return lax.ppermute(x, 'ctx', [(i, i ^ 1) for i in range(n_ctx)])  7.43 us
    pallas_call x4, Pallas kernels, pieces(): call(functools.partial(piece_kernel, order, per, step, count), flops=flop...  5.92 us
    all_to_all x1, waiting for transfers between devices, local(): lax.all_to_all(offered, 'ctx', split_axis=0, concat_axis=0, axis_index_gr...  5.85 us
    ppermute x5, waiting for transfers between devices, partner(): return lax.ppermute(x, 'ctx', [(i, i ^ 1) for i in range(n_ctx)])  5.79 us
    unnamed x36, local copies, waits for them, and re-layouts  5.76 us
  transfers between devices with their start and end apart: 29, of which 12 were waited for; matrix products, arithmetic and copies ran while one was open for 0% of the time, Pallas kernels for 19%

profile of v19, /device:TPU:0, one launch (start us, length us, event | category | flops | bytes accessed | tf_op | source)
XLA Modules:
  0.0 108.1 jit_solution(15227028527325500431)
XLA Ops:
  0.7 4.0 %states.1 = (f32[2,2,128,128]{3,2,1,0:T(8,128)}, bf16[3,2,128,128]{3,2,1,0:T(8,128)(2,1)}) custom-call(s32[1]{0:T(128)} %bitcast.par_ref, bf16[512,512]{1,0:T(8,128)(2,1)} %q_ref.1, bf16[512,512]{1,0:T(8,128)(2,1)} %k_ref.1, bf16[512,512]{1,0:T(8,128)(2,1)} %v_ref, bf16[512,512]{1,0:T(8,128)(2,1)} %g_ref.1), custom_call_target="tpu_custom_call" | custom-call | flops 1 | bytes 1 | tf_op jit(solution)/shard_map/states/pallas_call | solution.py:67
  4.7 3.0 %collective-permute-start = (bf16[3,2,128,128]{3,2,1,0:T(8,128)(2,1)}, bf16[3,2,128,128]{3,2,1,0:T(8,128)(2,1)S(1)}, u32[]{:S(2)}, u32[]{:S(2)}) collective-permute-start(bf16[3,2,128,128]{3,2,1,0:T(8,128)(2,1)} %get-tuple-element.51), channel_id=1, source_target_pairs={{0,4},{4,0},{8,12},{12,8},{16,20},{20,16},{24,28},{28,24},{1,5},{5... | collective-permute-start | bytes 589832 | tf_op jit(solution)/shard_map/ppermute | solution.py:441
  7.7 2.6 %collective-permute-start.1 = (bf16[512,512]{1,0:T(8,128)(2,1)}, bf16[512,512]{1,0:T(8,128)(2,1)}, u32[]{:S(2)}, u32[]{:S(2)}) collective-permute-start(bf16[512,512]{1,0:T(8,128)(2,1)} %refs_0_.3), channel_id=1, source_target_pairs={{0,16},{4,20},{16,24},{20,28},{24,8},{28,12},{8,0},{12,4},{1,17},{... | collective-permute-start | bytes 1572872 | tf_op jit(solution)/shard_map/ppermute | solution.py:457
  11.2 1.6 %collective-permute-done.got_ref.refs_2_ = bf16[3,2,128,128]{3,2,1,0:T(8,128)(2,1)S(1)} collective-permute-done((bf16[3,2,128,128]{3,2,1,0:T(8,128)(2,1)}, bf16[3,2,128,128]{3,2,1,0:T(8,128)(2,1)S(1)}, u32[]{:S(2)}, u32[]{:S(2)}) %collective-permute-start) | collective-permute-done | bytes 196640 | tf_op jit(solution)/shard_map/ppermute | solution.py:441
  12.8 1.7 %collective-permute-start.8 = (bf16[1,512,512]{2,1,0:T(8,128)(2,1)}, bf16[1,512,512]{2,1,0:T(8,128)(2,1)S(1)}, u32[]{:S(2)}, u32[]{:S(2)}) collective-permute-start(bf16[1,512,512]{2,1,0:T(8,128)(2,1)} %get-tuple-element.67), channel_id=1, source_target_pairs={{0,4},{4,0},{8,12},{12,8},{16,20},{20,16},{24,28},{28,24},{1,5},{5... | collective-permute-start | bytes 1572872 | tf_op jit(solution)/shard_map/ppermute | solution.py:441
  15.3 5.0 %all-to-all-start = ((bf16[4,2,128,128]{3,2,1,0:T(8,128)(2,1)}), bf16[4,2,128,128]{3,2,1,0:T(8,128)(2,1)S(1)}, u32[]{:S(2)}, u32[]{:S(2)}) async-start(bf16[4,2,128,128]{3,2,1,0:T(8,128)(2,1)} %offer.1), calls=%async_computation | async-start | bytes 524288 | tf_op jit(solution)/shard_map/all_to_all | solution.py:473
  20.3 1.5 %collective-permute-start.6 = (bf16[1,512,512]{2,1,0:T(8,128)(2,1)S(1)}, bf16[1,512,512]{2,1,0:T(8,128)(2,1)S(1)}, u32[]{:S(2)}, u32[]{:S(2)}) collective-permute-start(bf16[1,512,512]{2,1,0:T(8,128)(2,1)S(1)} %get-tuple-element.64.refs_0_), channel_id=1, source_target_pairs={{0,2},{1,3},{2,0},{3,1},{4,6},{5,7},{6,4},{7,5},{8,10},{9,11},{10,... | collective-permute-start | bytes 1572872 | tf_op jit(solution)/shard_map/ppermute | solution.py:444
  23.0 5.8 %all-to-all-done.every_ref = bf16[4,2,128,128]{3,2,1,0:T(8,128)(2,1)S(1)} async-done(((bf16[4,2,128,128]{3,2,1,0:T(8,128)(2,1)}), bf16[4,2,128,128]{3,2,1,0:T(8,128)(2,1)S(1)}, u32[]{:S(2)}, u32[]{:S(2)}) %all-to-all-start) | async-done | bytes 262176 | tf_op jit(solution)/shard_map/all_to_all | solution.py:473
  30.4 1.5 %collective-permute-start.10 = (bf16[1,512,512]{2,1,0:T(8,128)(2,1)S(1)}, bf16[1,512,512]{2,1,0:T(8,128)(2,1)S(1)}, u32[]{:S(2)}, u32[]{:S(2)}) collective-permute-start(bf16[1,512,512]{2,1,0:T(8,128)(2,1)S(1)} %collective-permute-done.8.refs_4_), channel_id=1, source_target_pairs={{0,2},{1,3},{2,0},{3,1},{4,6},{5,7},{6,4},{7,5},{8,10},{9,11},{10,... | collective-permute-start | bytes 1572872 | tf_op jit(solution)/shard_map/ppermute | solution.py:444
  33.0 3.0 %inside.1 = (f32[512,512]{1,0:T(8,128)S(1)}, bf16[512,512]{1,0:T(8,128)(2,1)S(1)}) custom-call(bf16[512,512]{1,0:T(8,128)(2,1)S(1)} %copy-done.5, bf16[512,512]{1,0:T(8,128)(2,1)S(1)} %copy-done.7, bf16[512,512]{1,0:T(8,128)(2,1)S(1)} %copy-done.9), custom_call_target="tpu_custom_call" | custom-call | flops 1 | bytes 1 | tf_op jit(solution)/shard_map/inside/pallas_call | solution.py:147
  37.1 4.2 %collective-permute-done.11.refs_2_ = bf16[512,512]{1,0:T(8,128)(2,1)S(1)} collective-permute-done((bf16[512,512]{1,0:T(8,128)(2,1)}, bf16[512,512]{1,0:T(8,128)(2,1)S(1)}, u32[]{:S(2)}, u32[]{:S(2)}) %collective-permute-start.11) | collective-permute-done | bytes 524320 | tf_op jit(solution)/shard_map/ppermute | solution.py:457
  41.3 1.5 %collective-permute-start.4 = (bf16[512,512]{1,0:T(8,128)(2,1)S(1)}, bf16[512,512]{1,0:T(8,128)(2,1)S(1)}, u32[]{:S(2)}, u32[]{:S(2)}) collective-permute-start(bf16[512,512]{1,0:T(8,128)(2,1)S(1)} %finish_value.1.a_ref.x_ref), channel_id=1, source_target_pairs={{0,4},{4,0},{8,12},{12,8},{16,20},{20,16},{24,28},{28,24},{1,5},{5... | collective-permute-start | bytes 1572872 | tf_op jit(solution)/shard_map/ppermute | solution.py:441
  44.7 1.7 %collective-permute-start.13 = (bf16[512,512]{1,0:T(8,128)(2,1)}, bf16[512,512]{1,0:T(8,128)(2,1)}, u32[]{:S(2)}, u32[]{:S(2)}) collective-permute-start(bf16[512,512]{1,0:T(8,128)(2,1)} %refs_0_.3), channel_id=1, source_target_pairs={{16,0},{20,4},{24,16},{28,20},{8,24},{12,28},{0,8},{4,12},{17,1},{... | collective-permute-start | bytes 1572872 | tf_op jit(solution)/shard_map/ppermute | solution.py:460
  47.7 4.2 %collective-permute-done.4.b_ref.x_ref = bf16[512,512]{1,0:T(8,128)(2,1)S(1)} collective-permute-done((bf16[512,512]{1,0:T(8,128)(2,1)S(1)}, bf16[512,512]{1,0:T(8,128)(2,1)S(1)}, u32[]{:S(2)}, u32[]{:S(2)}) %collective-permute-start.4) | collective-permute-done | bytes 524320 | tf_op jit(solution)/shard_map/ppermute | solution.py:441
  54.1 1.8 %pieces.4 = (bf16[256,512]{1,0:T(8,128)(2,1)S(1)}, bf16[256,512]{1,0:T(8,128)(2,1)S(1)}) custom-call(s32[1]{0:T(128)} %bitcast.3.spot_ref, s32[1]{0:T(128)} %bitcast.2.head_ref.at_ref, bf16[512,512]{1,0:T(8,128)(2,1)S(1)} %finish_value.1.a_ref.x_ref, bf16[512,512]{1,0:T(8,128)(2,1)S(1)} %collective-permute-done.4.b_ref.x_ref, ...), custom_call_target="tpu_custom_call" | custom-call | flops 536870912 | bytes 1 | tf_op jit(solution)/shard_map/pieces/pallas_call | solution.py:291
  55.9 4.3 %collective-permute-done.13.refs_3_ = bf16[512,512]{1,0:T(8,128)(2,1)} collective-permute-done((bf16[512,512]{1,0:T(8,128)(2,1)}, bf16[512,512]{1,0:T(8,128)(2,1)}, u32[]{:S(2)}, u32[]{:S(2)}) %collective-permute-start.13) | collective-permute-done | bytes 524320 | tf_op jit(solution)/shard_map/ppermute | solution.py:460
  61.3 1.8 %pieces.5 = (f32[256,512]{1,0:T(8,128)S(1)}, f32[256,512]{1,0:T(8,128)S(1)}) custom-call(s32[1]{0:T(128)} %bitcast.3.spot_ref, s32[1]{0:T(128)} %bitcast.2.head_ref.at_ref, bf16[512,512]{1,0:T(8,128)(2,1)S(1)} %finish_value.1.a_ref.x_ref, bf16[512,512]{1,0:T(8,128)(2,1)S(1)} %collective-permute-done.4.b_ref.x_ref, ...), custom_call_target="tpu_custom_call" | custom-call | flops 1 | bytes 1 | tf_op jit(solution)/shard_map/pieces/pallas_call | solution.py:291
  63.1 1.8 %collective-permute-start.21 = (bf16[256,512]{1,0:T(8,128)(2,1)S(1)}, bf16[256,512]{1,0:T(8,128)(2,1)S(1)}, u32[]{:S(2)}, u32[]{:S(2)}) collective-permute-start(bf16[256,512]{1,0:T(8,128)(2,1)S(1)} %get-tuple-element.82), channel_id=1, source_target_pairs={{0,16},{4,20},{16,24},{20,28},{24,8},{28,12},{8,0},{12,4},{1,17},{... | collective-permute-start | bytes 786440 | tf_op jit(solution)/shard_map/ppermute | solution.py:457
  64.9 1.7 %collective-permute-start.20 = (bf16[256,512]{1,0:T(8,128)(2,1)S(1)}, bf16[256,512]{1,0:T(8,128)(2,1)S(1)}, u32[]{:S(2)}, u32[]{:S(2)}) collective-permute-start(bf16[256,512]{1,0:T(8,128)(2,1)S(1)} %get-tuple-element.71), channel_id=1, source_target_pairs={{0,16},{4,20},{16,24},{20,28},{24,8},{28,12},{8,0},{12,4},{1,17},{... | collective-permute-start | bytes 786440 | tf_op jit(solution)/shard_map/ppermute | solution.py:457
  68.7 1.5 %collective-permute-start.23 = (bf16[512,512]{1,0:T(8,128)(2,1)S(1)}, bf16[512,512]{1,0:T(8,128)(2,1)S(1)}, u32[]{:S(2)}, u32[]{:S(2)}) collective-permute-start(bf16[512,512]{1,0:T(8,128)(2,1)S(1)} %head_part.3), channel_id=1, source_target_pairs={{0,2},{1,3},{2,0},{3,1},{4,6},{5,7},{6,4},{7,5},{8,10},{9,11},{10,... | collective-permute-start | bytes 1572872 | tf_op jit(solution)/shard_map/ppermute | solution.py:444
  71.0 1.4 %collective-permute-done.21.moved_ref = bf16[256,512]{1,0:T(8,128)(2,1)S(1)} collective-permute-done((bf16[256,512]{1,0:T(8,128)(2,1)S(1)}, bf16[256,512]{1,0:T(8,128)(2,1)S(1)}, u32[]{:S(2)}, u32[]{:S(2)}) %collective-permute-start.21) | collective-permute-done | bytes 262176 | tf_op jit(solution)/shard_map/ppermute | solution.py:457
  72.4 3.9 %collective-permute-done.20.moved_ref = bf16[256,512]{1,0:T(8,128)(2,1)S(1)} collective-permute-done((bf16[256,512]{1,0:T(8,128)(2,1)S(1)}, bf16[256,512]{1,0:T(8,128)(2,1)S(1)}, u32[]{:S(2)}, u32[]{:S(2)}) %collective-permute-start.20) | collective-permute-done | bytes 262176 | tf_op jit(solution)/shard_map/ppermute | solution.py:457
  76.3 2.7 %collective-permute-start.22 = (bf16[256,512]{1,0:T(8,128)(2,1)S(1)}, bf16[256,512]{1,0:T(8,128)(2,1)S(1)}, u32[]{:S(2)}, u32[]{:S(2)}) collective-permute-start(bf16[256,512]{1,0:T(8,128)(2,1)S(1)} %add_own.4), channel_id=1, source_target_pairs={{0,16},{4,20},{16,24},{20,28},{24,8},{28,12},{8,0},{12,4},{1,17},{... | collective-permute-start | bytes 786440 | tf_op jit(solution)/shard_map/ppermute | solution.py:457
  79.0 1.5 %collective-permute-start.19 = (bf16[512,512]{1,0:T(8,128)(2,1)S(1)}, bf16[512,512]{1,0:T(8,128)(2,1)S(1)}, u32[]{:S(2)}, u32[]{:S(2)}) collective-permute-start(bf16[512,512]{1,0:T(8,128)(2,1)S(1)} %head_part.4), channel_id=1, source_target_pairs={{0,2},{1,3},{2,0},{3,1},{4,6},{5,7},{6,4},{7,5},{8,10},{9,11},{10,... | collective-permute-start | bytes 1572872 | tf_op jit(solution)/shard_map/ppermute | solution.py:444
  83.9 2.1 %collective-permute-done.22.moved_ref = bf16[256,512]{1,0:T(8,128)(2,1)S(1)} collective-permute-done((bf16[256,512]{1,0:T(8,128)(2,1)S(1)}, bf16[256,512]{1,0:T(8,128)(2,1)S(1)}, u32[]{:S(2)}, u32[]{:S(2)}) %collective-permute-start.22) | collective-permute-done | bytes 262176 | tf_op jit(solution)/shard_map/ppermute | solution.py:457
  87.4 1.6 %collective-permute-start.26 = (bf16[256,512]{1,0:T(8,128)(2,1)S(1)}, bf16[256,512]{1,0:T(8,128)(2,1)S(1)}, u32[]{:S(2)}, u32[]{:S(2)}) collective-permute-start(bf16[256,512]{1,0:T(8,128)(2,1)S(1)} %add_own.5), channel_id=1, source_target_pairs={{0,16},{4,20},{16,24},{20,28},{24,8},{28,12},{8,0},{12,4},{1,17},{... | collective-permute-start | bytes 786440 | tf_op jit(solution)/shard_map/ppermute | solution.py:457
  89.1 1.6 %collective-permute-start.25 = (bf16[256,512]{1,0:T(8,128)(2,1)S(1)}, bf16[256,512]{1,0:T(8,128)(2,1)S(1)}, u32[]{:S(2)}, u32[]{:S(2)}) collective-permute-start(bf16[256,512]{1,0:T(8,128)(2,1)S(1)} %add_own.6), channel_id=1, source_target_pairs={{0,16},{4,20},{16,24},{20,28},{24,8},{28,12},{8,0},{12,4},{1,17},{... | collective-permute-start | bytes 786440 | tf_op jit(solution)/shard_map/ppermute | solution.py:457
  90.6 6.7 %collective-permute-done.26.moved_ref = bf16[256,512]{1,0:T(8,128)(2,1)S(1)} collective-permute-done((bf16[256,512]{1,0:T(8,128)(2,1)S(1)}, bf16[256,512]{1,0:T(8,128)(2,1)S(1)}, u32[]{:S(2)}, u32[]{:S(2)}) %collective-permute-start.26) | collective-permute-done | bytes 262176 | tf_op jit(solution)/shard_map/ppermute | solution.py:457
  97.4 2.0 %collective-permute-start.27 = (bf16[256,512]{1,0:T(8,128)(2,1)S(1)}, bf16[256,512]{1,0:T(8,128)(2,1)S(1)}, u32[]{:S(2)}, u32[]{:S(2)}) collective-permute-start(bf16[256,512]{1,0:T(8,128)(2,1)S(1)} %add_own.7), channel_id=1, source_target_pairs={{0,16},{4,20},{16,24},{20,28},{24,8},{28,12},{8,0},{12,4},{1,17},{... | collective-permute-start | bytes 786440 | tf_op jit(solution)/shard_map/ppermute | solution.py:457
  99.3 4.1 %others.1 = (bf16[512,512]{1,0:T(8,128)(2,1)}, bf16[512,512]{1,0:T(8,128)(2,1)}) custom-call(s32[1]{0:T(128)} %bitcast.par_ref, bf16[512,512]{1,0:T(8,128)(2,1)S(1)} %copy-done.6, bf16[512,512]{1,0:T(8,128)(2,1)S(1)} %copy-done.8, bf16[512,512]{1,0:T(8,128)(2,1)S(1)} %copy-done.11, bf16[512,512]{1,0:T(8,128)(2,1)S(1)} %copy-done.10, ...), custom_call_target="tpu_custom_call" | custom-call | flops 1 | bytes 1 | tf_op jit(solution)/shard_map/others/pallas_call | solution.py:246
  103.4 1.8 %join.1 = bf16[512,1024]{1,0:T(8,128)(2,1)} custom-call(s32[1]{0:T(128)} %bitcast.par_ref, s32[1]{0:T(128)} %bitcast.2.head_ref.at_ref, bf16[512,512]{1,0:T(8,128)(2,1)S(1)} %finish_value.1.a_ref.x_ref, bf16[512,512]{1,0:T(8,128)(2,1)S(1)} %collective-permute-done.3.y_ref, bf16[2,512,512]{2,1,0:T(8,128)(2,1)S(1)} %get-tuple-element.79.w_ref, ...), custom_call_target="tpu_custom_call" | custom-call | flops 1 | bytes 1 | tf_op jit(solution)/shard_map/join/pallas_call | solution.py:418
  105.2 1.5 %collective-permute-done.27.refs_1_ = bf16[256,512]{1,0:T(8,128)(2,1)S(1)} collective-permute-done((bf16[256,512]{1,0:T(8,128)(2,1)S(1)}, bf16[256,512]{1,0:T(8,128)(2,1)S(1)}, u32[]{:S(2)}, u32[]{:S(2)}) %collective-permute-start.27) | collective-permute-done | bytes 262176 | tf_op jit(solution)/shard_map/ppermute | solution.py:457
  (83 shorter events, 21.8 us)
Async XLA Ops:
  4.7 8.1 %collective-permute-start = (bf16[3,2,128,128]{3,2,1,0:T(8,128)(2,1)}, bf16[3,2,128,128]{3,2,1,0:T(8,128)(2,1)S(1)}, u32[]{:S(2)}, u32[]{:S(2)}) collective-permute-start(bf16[3,2,128,128]{3,2,1,0:T(8,128)(2,1)} %get-tuple-element.51), channel_id=1, source_target_pairs={{0,4},{4,0},{8,12},{12,8},{16,20},{20,16},{24,28},{28,24},{1,5},{5... | collective-permute-start | bytes 589832 | tf_op jit(solution)/shard_map/ppermute | solution.py:441
  7.7 15.3 %collective-permute-start.1 = (bf16[512,512]{1,0:T(8,128)(2,1)}, bf16[512,512]{1,0:T(8,128)(2,1)}, u32[]{:S(2)}, u32[]{:S(2)}) collective-permute-start(bf16[512,512]{1,0:T(8,128)(2,1)} %refs_0_.3), channel_id=1, source_target_pairs={{0,16},{4,20},{16,24},{20,28},{24,8},{28,12},{8,0},{12,4},{1,17},{... | collective-permute-start | bytes 1572872 | tf_op jit(solution)/shard_map/ppermute | solution.py:457
  12.8 17.6 %collective-permute-start.8 = (bf16[1,512,512]{2,1,0:T(8,128)(2,1)}, bf16[1,512,512]{2,1,0:T(8,128)(2,1)S(1)}, u32[]{:S(2)}, u32[]{:S(2)}) collective-permute-start(bf16[1,512,512]{2,1,0:T(8,128)(2,1)} %get-tuple-element.67), channel_id=1, source_target_pairs={{0,4},{4,0},{8,12},{12,8},{16,20},{20,16},{24,28},{28,24},{1,5},{5... | collective-permute-start | bytes 1572872 | tf_op jit(solution)/shard_map/ppermute | solution.py:441
  14.5 17.4 %copy-start.7 = (bf16[512,512]{1,0:T(8,128)(2,1)S(1)}, bf16[512,512]{1,0:T(8,128)(2,1)}, u32[]{:S(2)}) copy-start(bf16[512,512]{1,0:T(8,128)(2,1)} %k_ref.1) | copy-start | bytes 1572868
  15.3 16.6 %copy-start.5 = (bf16[512,512]{1,0:T(8,128)(2,1)S(1)}, bf16[512,512]{1,0:T(8,128)(2,1)}, u32[]{:S(2)}) copy-start(bf16[512,512]{1,0:T(8,128)(2,1)} %q_ref.1) | copy-start | bytes 1572868
  15.3 13.5 %all-to-all-start = ((bf16[4,2,128,128]{3,2,1,0:T(8,128)(2,1)}), bf16[4,2,128,128]{3,2,1,0:T(8,128)(2,1)S(1)}, u32[]{:S(2)}, u32[]{:S(2)}) async-start(bf16[4,2,128,128]{3,2,1,0:T(8,128)(2,1)} %offer.1), calls=%async_computation | async-start | bytes 524288 | tf_op jit(solution)/shard_map/all_to_all | solution.py:473
  20.3 16.2 %collective-permute-start.6 = (bf16[1,512,512]{2,1,0:T(8,128)(2,1)S(1)}, bf16[1,512,512]{2,1,0:T(8,128)(2,1)S(1)}, u32[]{:S(2)}, u32[]{:S(2)}) collective-permute-start(bf16[1,512,512]{2,1,0:T(8,128)(2,1)S(1)} %get-tuple-element.64.refs_0_), channel_id=1, source_target_pairs={{0,2},{1,3},{2,0},{3,1},{4,6},{5,7},{6,4},{7,5},{8,10},{9,11},{10,... | collective-permute-start | bytes 1572872 | tf_op jit(solution)/shard_map/ppermute | solution.py:444
  28.9 7.1 %collective-permute-start.2 = (bf16[2,2,128,128]{3,2,1,0:T(8,128)(2,1)S(1)}, bf16[2,2,128,128]{3,2,1,0:T(8,128)(2,1)S(1)}, u32[]{:S(2)}, u32[]{:S(2)}) collective-permute-start(bf16[2,2,128,128]{3,2,1,0:T(8,128)(2,1)S(1)} %get-tuple-element.54), channel_id=1, source_target_pairs={{0,4},{4,0},{8,12},{12,8},{16,20},{20,16},{24,28},{28,24},{1,5},{5... | collective-permute-start | bytes 393224 | tf_op jit(solution)/shard_map/ppermute | solution.py:441
  29.5 11.8 %collective-permute-start.11 = (bf16[512,512]{1,0:T(8,128)(2,1)}, bf16[512,512]{1,0:T(8,128)(2,1)S(1)}, u32[]{:S(2)}, u32[]{:S(2)}) collective-permute-start(bf16[512,512]{1,0:T(8,128)(2,1)} %collective-permute-done.1.refs_1_), channel_id=1, source_target_pairs={{0,16},{4,20},{16,24},{20,28},{24,8},{28,12},{8,0},{12,4},{1,17},{... | collective-permute-start | bytes 1572872 | tf_op jit(solution)/shard_map/ppermute | solution.py:457
  30.4 13.5 %collective-permute-start.10 = (bf16[1,512,512]{2,1,0:T(8,128)(2,1)S(1)}, bf16[1,512,512]{2,1,0:T(8,128)(2,1)S(1)}, u32[]{:S(2)}, u32[]{:S(2)}) collective-permute-start(bf16[1,512,512]{2,1,0:T(8,128)(2,1)S(1)} %collective-permute-done.8.refs_4_), channel_id=1, source_target_pairs={{0,2},{1,3},{2,0},{3,1},{4,6},{5,7},{6,4},{7,5},{8,10},{9,11},{10,... | collective-permute-start | bytes 1572872 | tf_op jit(solution)/shard_map/ppermute | solution.py:444
  36.5 7.4 %collective-permute-start.7 = (bf16[1,512,512]{2,1,0:T(8,128)(2,1)S(1)}, bf16[1,512,512]{2,1,0:T(8,128)(2,1)S(1)}, u32[]{:S(2)}, u32[]{:S(2)}) collective-permute-start(bf16[1,512,512]{2,1,0:T(8,128)(2,1)S(1)} %collective-permute-done.6.refs_2_), channel_id=1, source_target_pairs={{0,1},{1,0},{2,3},{3,2},{4,5},{5,4},{6,7},{7,6},{8,9},{9,8},{10,11... | collective-permute-start | bytes 1572872 | tf_op jit(solution)/shard_map/ppermute | solution.py:444
  36.6 9.9 %collective-permute-start.5 = (bf16[1,512,512]{2,1,0:T(8,128)(2,1)S(1)}, bf16[1,512,512]{2,1,0:T(8,128)(2,1)S(1)}, u32[]{:S(2)}, u32[]{:S(2)}) collective-permute-start(bf16[1,512,512]{2,1,0:T(8,128)(2,1)S(1)} %get-tuple-element.64.refs_0_), channel_id=1, source_target_pairs={{0,1},{1,0},{2,3},{3,2},{4,5},{5,4},{6,7},{7,6},{8,9},{9,8},{10,11... | collective-permute-start | bytes 1572872 | tf_op jit(solution)/shard_map/ppermute | solution.py:444
  37.1 10.4 %collective-permute-start.9 = (bf16[1,512,512]{2,1,0:T(8,128)(2,1)S(1)}, bf16[1,512,512]{2,1,0:T(8,128)(2,1)}, u32[]{:S(2)}, u32[]{:S(2)}) collective-permute-start(bf16[1,512,512]{2,1,0:T(8,128)(2,1)S(1)} %collective-permute-done.8.refs_4_), channel_id=1, source_target_pairs={{0,1},{1,0},{2,3},{3,2},{4,5},{5,4},{6,7},{7,6},{8,9},{9,8},{10,11... | collective-permute-start | bytes 1572872 | tf_op jit(solution)/shard_map/ppermute | solution.py:444
  41.3 10.7 %collective-permute-start.4 = (bf16[512,512]{1,0:T(8,128)(2,1)S(1)}, bf16[512,512]{1,0:T(8,128)(2,1)S(1)}, u32[]{:S(2)}, u32[]{:S(2)}) collective-permute-start(bf16[512,512]{1,0:T(8,128)(2,1)S(1)} %finish_value.1.a_ref.x_ref), channel_id=1, source_target_pairs={{0,4},{4,0},{8,12},{12,8},{16,20},{20,16},{24,28},{28,24},{1,5},{5... | collective-permute-start | bytes 1572872 | tf_op jit(solution)/shard_map/ppermute | solution.py:441
  43.9 8.1 %collective-permute-start.12 = (bf16[1,512,512]{2,1,0:T(8,128)(2,1)S(1)}, bf16[1,512,512]{2,1,0:T(8,128)(2,1)}, u32[]{:S(2)}, u32[]{:S(2)}) collective-permute-start(bf16[1,512,512]{2,1,0:T(8,128)(2,1)S(1)} %collective-permute-done.10.refs_6_), channel_id=1, source_target_pairs={{0,1},{1,0},{2,3},{3,2},{4,5},{5,4},{6,7},{7,6},{8,9},{9,8},{10,11... | collective-permute-start | bytes 1572872 | tf_op jit(solution)/shard_map/ppermute | solution.py:444
  44.7 15.6 %collective-permute-start.13 = (bf16[512,512]{1,0:T(8,128)(2,1)}, bf16[512,512]{1,0:T(8,128)(2,1)}, u32[]{:S(2)}, u32[]{:S(2)}) collective-permute-start(bf16[512,512]{1,0:T(8,128)(2,1)} %refs_0_.3), channel_id=1, source_target_pairs={{16,0},{20,4},{24,16},{28,20},{8,24},{12,28},{0,8},{4,12},{17,1},{... | collective-permute-start | bytes 1572872 | tf_op jit(solution)/shard_map/ppermute | solution.py:460
  47.2 13.5 %collective-permute-start.15 = (bf16[512,512]{1,0:T(8,128)(2,1)}, bf16[512,512]{1,0:T(8,128)(2,1)}, u32[]{:S(2)}, u32[]{:S(2)}) collective-permute-start(bf16[512,512]{1,0:T(8,128)(2,1)} %collective-permute-done.1.refs_1_), channel_id=1, source_target_pairs={{0,1},{1,0},{2,3},{3,2},{4,5},{5,4},{6,7},{7,6},{8,9},{9,8},{10,11... | collective-permute-start | bytes 1572872 | tf_op jit(solution)/shard_map/ppermute | solution.py:444
  47.5 15.6 %collective-permute-start.14 = (bf16[512,512]{1,0:T(8,128)(2,1)}, bf16[512,512]{1,0:T(8,128)(2,1)S(1)}, u32[]{:S(2)}, u32[]{:S(2)}) collective-permute-start(bf16[512,512]{1,0:T(8,128)(2,1)} %refs_0_.3), channel_id=1, source_target_pairs={{0,1},{1,0},{2,3},{3,2},{4,5},{5,4},{6,7},{7,6},{8,9},{9,8},{10,11... | collective-permute-start | bytes 1572872 | tf_op jit(solution)/shard_map/ppermute | solution.py:444
  60.2 4.6 %collective-permute-start.17 = (bf16[512,512]{1,0:T(8,128)(2,1)}, bf16[512,512]{1,0:T(8,128)(2,1)S(1)}, u32[]{:S(2)}, u32[]{:S(2)}) collective-permute-start(bf16[512,512]{1,0:T(8,128)(2,1)} %collective-permute-done.13.refs_3_), channel_id=1, source_target_pairs={{0,1},{1,0},{2,3},{3,2},{4,5},{5,4},{6,7},{7,6},{8,9},{9,8},{10,11... | collective-permute-start | bytes 1572872 | tf_op jit(solution)/shard_map/ppermute | solution.py:444
  60.2 6.4 %collective-permute-start.16 = (bf16[512,512]{1,0:T(8,128)(2,1)S(1)}, bf16[512,512]{1,0:T(8,128)(2,1)S(1)}, u32[]{:S(2)}, u32[]{:S(2)}) collective-permute-start(bf16[512,512]{1,0:T(8,128)(2,1)S(1)} %copy-done.16), channel_id=1, source_target_pairs={{0,1},{1,0},{2,3},{3,2},{4,5},{5,4},{6,7},{7,6},{8,9},{9,8},{10,11... | collective-permute-start | bytes 1572872 | tf_op jit(solution)/shard_map/ppermute | solution.py:444
  60.7 7.2 %collective-permute-start.18 = (bf16[512,512]{1,0:T(8,128)(2,1)S(1)}, bf16[512,512]{1,0:T(8,128)(2,1)S(1)}, u32[]{:S(2)}, u32[]{:S(2)}) collective-permute-start(bf16[512,512]{1,0:T(8,128)(2,1)S(1)} %collective-permute-done.4.b_ref.x_ref), channel_id=1, source_target_pairs={{0,1},{1,0},{2,3},{3,2},{4,5},{5,4},{6,7},{7,6},{8,9},{9,8},{10,11... | collective-permute-start | bytes 1572872 | tf_op jit(solution)/shard_map/ppermute | solution.py:444
  60.8 9.5 %collective-permute-start.3 = (bf16[512,512]{1,0:T(8,128)(2,1)S(1)}, bf16[512,512]{1,0:T(8,128)(2,1)S(1)}, u32[]{:S(2)}, u32[]{:S(2)}) collective-permute-start(bf16[512,512]{1,0:T(8,128)(2,1)S(1)} %finish_value.1.a_ref.x_ref), channel_id=1, source_target_pairs={{0,1},{1,0},{2,3},{3,2},{4,5},{5,4},{6,7},{7,6},{8,9},{9,8},{10,11... | collective-permute-start | bytes 1572872 | tf_op jit(solution)/shard_map/ppermute | solution.py:444
  63.1 9.3 %collective-permute-start.21 = (bf16[256,512]{1,0:T(8,128)(2,1)S(1)}, bf16[256,512]{1,0:T(8,128)(2,1)S(1)}, u32[]{:S(2)}, u32[]{:S(2)}) collective-permute-start(bf16[256,512]{1,0:T(8,128)(2,1)S(1)} %get-tuple-element.82), channel_id=1, source_target_pairs={{0,16},{4,20},{16,24},{20,28},{24,8},{28,12},{8,0},{12,4},{1,17},{... | collective-permute-start | bytes 786440 | tf_op jit(solution)/shard_map/ppermute | solution.py:457
  64.9 11.4 %collective-permute-start.20 = (bf16[256,512]{1,0:T(8,128)(2,1)S(1)}, bf16[256,512]{1,0:T(8,128)(2,1)S(1)}, u32[]{:S(2)}, u32[]{:S(2)}) collective-permute-start(bf16[256,512]{1,0:T(8,128)(2,1)S(1)} %get-tuple-element.71), channel_id=1, source_target_pairs={{0,16},{4,20},{16,24},{20,28},{24,8},{28,12},{8,0},{12,4},{1,17},{... | collective-permute-start | bytes 786440 | tf_op jit(solution)/shard_map/ppermute | solution.py:457
  68.7 17.4 %collective-permute-start.23 = (bf16[512,512]{1,0:T(8,128)(2,1)S(1)}, bf16[512,512]{1,0:T(8,128)(2,1)S(1)}, u32[]{:S(2)}, u32[]{:S(2)}) collective-permute-start(bf16[512,512]{1,0:T(8,128)(2,1)S(1)} %head_part.3), channel_id=1, source_target_pairs={{0,2},{1,3},{2,0},{3,1},{4,6},{5,7},{6,4},{7,5},{8,10},{9,11},{10,... | collective-permute-start | bytes 1572872 | tf_op jit(solution)/shard_map/ppermute | solution.py:444
  76.3 9.7 %collective-permute-start.22 = (bf16[256,512]{1,0:T(8,128)(2,1)S(1)}, bf16[256,512]{1,0:T(8,128)(2,1)S(1)}, u32[]{:S(2)}, u32[]{:S(2)}) collective-permute-start(bf16[256,512]{1,0:T(8,128)(2,1)S(1)} %add_own.4), channel_id=1, source_target_pairs={{0,16},{4,20},{16,24},{20,28},{24,8},{28,12},{8,0},{12,4},{1,17},{... | collective-permute-start | bytes 786440 | tf_op jit(solution)/shard_map/ppermute | solution.py:457
  79.0 24.4 %collective-permute-start.19 = (bf16[512,512]{1,0:T(8,128)(2,1)S(1)}, bf16[512,512]{1,0:T(8,128)(2,1)S(1)}, u32[]{:S(2)}, u32[]{:S(2)}) collective-permute-start(bf16[512,512]{1,0:T(8,128)(2,1)S(1)} %head_part.4), channel_id=1, source_target_pairs={{0,2},{1,3},{2,0},{3,1},{4,6},{5,7},{6,4},{7,5},{8,10},{9,11},{10,... | collective-permute-start | bytes 1572872 | tf_op jit(solution)/shard_map/ppermute | solution.py:444
  86.1 13.3 %copy-start.10 = (bf16[512,512]{1,0:T(8,128)(2,1)S(1)}, bf16[512,512]{1,0:T(8,128)(2,1)}, u32[]{:S(2)}) copy-start(bf16[512,512]{1,0:T(8,128)(2,1)} %g_ref.1) | copy-start | bytes 1572868
  86.8 16.6 %collective-permute-start.24 = (bf16[512,512]{1,0:T(8,128)(2,1)S(1)}, bf16[512,512]{1,0:T(8,128)(2,1)S(1)}, u32[]{:S(2)}, u32[]{:S(2)}) collective-permute-start(bf16[512,512]{1,0:T(8,128)(2,1)S(1)} %head_part.5), channel_id=1, source_target_pairs={{0,4},{4,0},{8,12},{12,8},{16,20},{20,16},{24,28},{28,24},{1,5},{5... | collective-permute-start | bytes 1572872 | tf_op jit(solution)/shard_map/ppermute | solution.py:441
  87.4 9.9 %collective-permute-start.26 = (bf16[256,512]{1,0:T(8,128)(2,1)S(1)}, bf16[256,512]{1,0:T(8,128)(2,1)S(1)}, u32[]{:S(2)}, u32[]{:S(2)}) collective-permute-start(bf16[256,512]{1,0:T(8,128)(2,1)S(1)} %add_own.5), channel_id=1, source_target_pairs={{0,16},{4,20},{16,24},{20,28},{24,8},{28,12},{8,0},{12,4},{1,17},{... | collective-permute-start | bytes 786440 | tf_op jit(solution)/shard_map/ppermute | solution.py:457
  89.1 16.2 %collective-permute-start.25 = (bf16[256,512]{1,0:T(8,128)(2,1)S(1)}, bf16[256,512]{1,0:T(8,128)(2,1)S(1)}, u32[]{:S(2)}, u32[]{:S(2)}) collective-permute-start(bf16[256,512]{1,0:T(8,128)(2,1)S(1)} %add_own.6), channel_id=1, source_target_pairs={{0,16},{4,20},{16,24},{20,28},{24,8},{28,12},{8,0},{12,4},{1,17},{... | collective-permute-start | bytes 786440 | tf_op jit(solution)/shard_map/ppermute | solution.py:457
  97.4 9.4 %collective-permute-start.27 = (bf16[256,512]{1,0:T(8,128)(2,1)S(1)}, bf16[256,512]{1,0:T(8,128)(2,1)S(1)}, u32[]{:S(2)}, u32[]{:S(2)}) collective-permute-start(bf16[256,512]{1,0:T(8,128)(2,1)S(1)} %add_own.7), channel_id=1, source_target_pairs={{0,16},{4,20},{16,24},{20,28},{24,8},{28,12},{8,0},{12,4},{1,17},{... | collective-permute-start | bytes 786440 | tf_op jit(solution)/shard_map/ppermute | solution.py:457
  (15 other events, 87.5 us)

commit v20 on v19

--- a/solution.py
+++ b/solution.py
@@ -543,9 +543,7 @@
             if step == pairs - 2 and i == chains - 1:
                 lead = (here, after(other, token), other_too, weight, borrowed)
                 token = part = head_part(*lead, got_other)
-            ready = [token] + (moved[i + 1 :] if step == 1 else [])
-            own_part = after(local_part[i], *ready)
-            token = add_own(moved[i], own_part)
+            token = add_own(moved[i], after(local_part[i], token))
             moved[i] = ring(token)
         if step < pairs - 2:
             local_part = piece(F32, step + 1, token)

time: 109 us -> 106 us (0.972)
  waiting for transfers between devices: 38 us -> 33.4 us
  starting transfers between devices: 37.3 us -> 39.9 us
    ppermute x8, waiting for transfers between devices: 20.9 us -> 16.4 us  [ring(): return lax.ppermute(x, 'ctx', moves)]
    ppermute x8, starting transfers between devices: 14.8 us -> 16.9 us  [ring(): return lax.ppermute(x, 'ctx', moves)]
  transfers between devices with their start and end apart: 29 -> 29, of which waited for: 12 -> 12; matrix products, arithmetic and copies ran while one was open for 0% -> 0% of each run, Pallas kernels for 19% -> 20%
where the time goes in v20:
time: 106 us; the launch traced here: 105 us
  starting transfers between devices  39.9 us (38%)
  waiting for transfers between devices  33.4 us (32%)
  Pallas kernels  26.1 us (25%)
  local copies, waits for them, and re-layouts  4.77 us (4%)
    ppermute x8, starting transfers between devices, ring(): return lax.ppermute(x, 'ctx', moves)  16.9 us
    ppermute x8, waiting for transfers between devices, ring(): return lax.ppermute(x, 'ctx', moves)  16.4 us
    ppermute x14, starting transfers between devices, across(): return lax.ppermute(x, 'head', [(i, i ^ bit) for i in range(n_head)])  8.83 us
    ppermute x5, starting transfers between devices, partner(): return lax.ppermute(x, 'ctx', [(i, i ^ 1) for i in range(n_ctx)])  7.43 us
    pallas_call x4, Pallas kernels, pieces(): call(functools.partial(piece_kernel, order, per, step, count), flops=flop...  5.94 us
    all_to_all x1, waiting for transfers between devices, local(): lax.all_to_all(offered, 'ctx', split_axis=0, concat_axis=0, axis_index_gr...  5.85 us
    ppermute x5, waiting for transfers between devices, partner(): return lax.ppermute(x, 'ctx', [(i, i ^ 1) for i in range(n_ctx)])  5.79 us
    all_to_all x1, starting transfers between devices, local(): lax.all_to_all(offered, 'ctx', split_axis=0, concat_axis=0, axis_index_gr...  5 us
  transfers between devices with their start and end apart: 29, of which 12 were waited for; matrix products, arithmetic and copies ran while one was open for 0% of the time, Pallas kernels for 20%

profile of v20, /device:TPU:0, one launch (start us, length us, event | category | flops | bytes accessed | tf_op | source)
XLA Modules:
  0.0 105.2 jit_solution(1324224744169336000)
XLA Ops:
  0.7 4.0 %states.1 = (f32[2,2,128,128]{3,2,1,0:T(8,128)}, bf16[3,2,128,128]{3,2,1,0:T(8,128)(2,1)}) custom-call(s32[1]{0:T(128)} %bitcast.par_ref, bf16[512,512]{1,0:T(8,128)(2,1)} %q_ref.1, bf16[512,512]{1,0:T(8,128)(2,1)} %k_ref.1, bf16[512,512]{1,0:T(8,128)(2,1)} %v_ref, bf16[512,512]{1,0:T(8,128)(2,1)} %g_ref.1), custom_call_target="tpu_custom_call" | custom-call | flops 1 | bytes 1 | tf_op jit(solution)/shard_map/states/pallas_call | solution.py:67
  4.7 3.0 %collective-permute-start = (bf16[3,2,128,128]{3,2,1,0:T(8,128)(2,1)}, bf16[3,2,128,128]{3,2,1,0:T(8,128)(2,1)S(1)}, u32[]{:S(2)}, u32[]{:S(2)}) collective-permute-start(bf16[3,2,128,128]{3,2,1,0:T(8,128)(2,1)} %get-tuple-element.51), channel_id=1, source_target_pairs={{0,4},{4,0},{8,12},{12,8},{16,20},{20,16},{24,28},{28,24},{1,5},{5... | collective-permute-start | bytes 589832 | tf_op jit(solution)/shard_map/ppermute | solution.py:441
  7.7 2.6 %collective-permute-start.1 = (bf16[512,512]{1,0:T(8,128)(2,1)}, bf16[512,512]{1,0:T(8,128)(2,1)}, u32[]{:S(2)}, u32[]{:S(2)}) collective-permute-start(bf16[512,512]{1,0:T(8,128)(2,1)} %refs_0_.3), channel_id=1, source_target_pairs={{0,16},{4,20},{16,24},{20,28},{24,8},{28,12},{8,0},{12,4},{1,17},{... | collective-permute-start | bytes 1572872 | tf_op jit(solution)/shard_map/ppermute | solution.py:457
  11.2 1.6 %collective-permute-done.got_ref.refs_2_ = bf16[3,2,128,128]{3,2,1,0:T(8,128)(2,1)S(1)} collective-permute-done((bf16[3,2,128,128]{3,2,1,0:T(8,128)(2,1)}, bf16[3,2,128,128]{3,2,1,0:T(8,128)(2,1)S(1)}, u32[]{:S(2)}, u32[]{:S(2)}) %collective-permute-start) | collective-permute-done | bytes 196640 | tf_op jit(solution)/shard_map/ppermute | solution.py:441
  12.8 1.7 %collective-permute-start.8 = (bf16[1,512,512]{2,1,0:T(8,128)(2,1)}, bf16[1,512,512]{2,1,0:T(8,128)(2,1)S(1)}, u32[]{:S(2)}, u32[]{:S(2)}) collective-permute-start(bf16[1,512,512]{2,1,0:T(8,128)(2,1)} %get-tuple-element.67), channel_id=1, source_target_pairs={{0,4},{4,0},{8,12},{12,8},{16,20},{20,16},{24,28},{28,24},{1,5},{5... | collective-permute-start | bytes 1572872 | tf_op jit(solution)/shard_map/ppermute | solution.py:441
  15.3 5.0 %all-to-all-start = ((bf16[4,2,128,128]{3,2,1,0:T(8,128)(2,1)}), bf16[4,2,128,128]{3,2,1,0:T(8,128)(2,1)S(1)}, u32[]{:S(2)}, u32[]{:S(2)}) async-start(bf16[4,2,128,128]{3,2,1,0:T(8,128)(2,1)} %offer.1), calls=%async_computation | async-start | bytes 524288 | tf_op jit(solution)/shard_map/all_to_all | solution.py:473
  20.3 1.5 %collective-permute-start.6 = (bf16[1,512,512]{2,1,0:T(8,128)(2,1)S(1)}, bf16[1,512,512]{2,1,0:T(8,128)(2,1)S(1)}, u32[]{:S(2)}, u32[]{:S(2)}) collective-permute-start(bf16[1,512,512]{2,1,0:T(8,128)(2,1)S(1)} %get-tuple-element.64.refs_0_), channel_id=1, source_target_pairs={{0,2},{1,3},{2,0},{3,1},{4,6},{5,7},{6,4},{7,5},{8,10},{9,11},{10,... | collective-permute-start | bytes 1572872 | tf_op jit(solution)/shard_map/ppermute | solution.py:444
  23.0 5.8 %all-to-all-done.every_ref = bf16[4,2,128,128]{3,2,1,0:T(8,128)(2,1)S(1)} async-done(((bf16[4,2,128,128]{3,2,1,0:T(8,128)(2,1)}), bf16[4,2,128,128]{3,2,1,0:T(8,128)(2,1)S(1)}, u32[]{:S(2)}, u32[]{:S(2)}) %all-to-all-start) | async-done | bytes 262176 | tf_op jit(solution)/shard_map/all_to_all | solution.py:473
  30.4 1.5 %collective-permute-start.10 = (bf16[1,512,512]{2,1,0:T(8,128)(2,1)S(1)}, bf16[1,512,512]{2,1,0:T(8,128)(2,1)S(1)}, u32[]{:S(2)}, u32[]{:S(2)}) collective-permute-start(bf16[1,512,512]{2,1,0:T(8,128)(2,1)S(1)} %collective-permute-done.8.refs_4_), channel_id=1, source_target_pairs={{0,2},{1,3},{2,0},{3,1},{4,6},{5,7},{6,4},{7,5},{8,10},{9,11},{10,... | collective-permute-start | bytes 1572872 | tf_op jit(solution)/shard_map/ppermute | solution.py:444
  33.0 3.0 %inside.1 = (f32[512,512]{1,0:T(8,128)S(1)}, bf16[512,512]{1,0:T(8,128)(2,1)S(1)}) custom-call(bf16[512,512]{1,0:T(8,128)(2,1)S(1)} %copy-done.5, bf16[512,512]{1,0:T(8,128)(2,1)S(1)} %copy-done.7, bf16[512,512]{1,0:T(8,128)(2,1)S(1)} %copy-done.9), custom_call_target="tpu_custom_call" | custom-call | flops 1 | bytes 1 | tf_op jit(solution)/shard_map/inside/pallas_call | solution.py:147
  37.1 4.2 %collective-permute-done.11.refs_2_ = bf16[512,512]{1,0:T(8,128)(2,1)S(1)} collective-permute-done((bf16[512,512]{1,0:T(8,128)(2,1)}, bf16[512,512]{1,0:T(8,128)(2,1)S(1)}, u32[]{:S(2)}, u32[]{:S(2)}) %collective-permute-start.11) | collective-permute-done | bytes 524320 | tf_op jit(solution)/shard_map/ppermute | solution.py:457
  41.3 1.5 %collective-permute-start.4 = (bf16[512,512]{1,0:T(8,128)(2,1)S(1)}, bf16[512,512]{1,0:T(8,128)(2,1)S(1)}, u32[]{:S(2)}, u32[]{:S(2)}) collective-permute-start(bf16[512,512]{1,0:T(8,128)(2,1)S(1)} %finish_value.1.a_ref.x_ref), channel_id=1, source_target_pairs={{0,4},{4,0},{8,12},{12,8},{16,20},{20,16},{24,28},{28,24},{1,5},{5... | collective-permute-start | bytes 1572872 | tf_op jit(solution)/shard_map/ppermute | solution.py:441
  44.7 1.7 %collective-permute-start.13 = (bf16[512,512]{1,0:T(8,128)(2,1)}, bf16[512,512]{1,0:T(8,128)(2,1)}, u32[]{:S(2)}, u32[]{:S(2)}) collective-permute-start(bf16[512,512]{1,0:T(8,128)(2,1)} %refs_0_.3), channel_id=1, source_target_pairs={{16,0},{20,4},{24,16},{28,20},{8,24},{12,28},{0,8},{4,12},{17,1},{... | collective-permute-start | bytes 1572872 | tf_op jit(solution)/shard_map/ppermute | solution.py:460
  47.7 4.2 %collective-permute-done.4.b_ref.x_ref = bf16[512,512]{1,0:T(8,128)(2,1)S(1)} collective-permute-done((bf16[512,512]{1,0:T(8,128)(2,1)S(1)}, bf16[512,512]{1,0:T(8,128)(2,1)S(1)}, u32[]{:S(2)}, u32[]{:S(2)}) %collective-permute-start.4) | collective-permute-done | bytes 524320 | tf_op jit(solution)/shard_map/ppermute | solution.py:441
  54.1 1.8 %pieces.4 = (bf16[256,512]{1,0:T(8,128)(2,1)S(1)}, bf16[256,512]{1,0:T(8,128)(2,1)S(1)}) custom-call(s32[1]{0:T(128)} %bitcast.3.spot_ref, s32[1]{0:T(128)} %bitcast.2.head_ref.at_ref, bf16[512,512]{1,0:T(8,128)(2,1)S(1)} %finish_value.1.a_ref.x_ref, bf16[512,512]{1,0:T(8,128)(2,1)S(1)} %collective-permute-done.4.b_ref.x_ref, ...), custom_call_target="tpu_custom_call" | custom-call | flops 536870912 | bytes 1 | tf_op jit(solution)/shard_map/pieces/pallas_call | solution.py:291
  55.9 4.3 %collective-permute-done.13.refs_3_ = bf16[512,512]{1,0:T(8,128)(2,1)} collective-permute-done((bf16[512,512]{1,0:T(8,128)(2,1)}, bf16[512,512]{1,0:T(8,128)(2,1)}, u32[]{:S(2)}, u32[]{:S(2)}) %collective-permute-start.13) | collective-permute-done | bytes 524320 | tf_op jit(solution)/shard_map/ppermute | solution.py:460
  61.3 1.8 %pieces.5 = (f32[256,512]{1,0:T(8,128)S(1)}, f32[256,512]{1,0:T(8,128)S(1)}) custom-call(s32[1]{0:T(128)} %bitcast.3.spot_ref, s32[1]{0:T(128)} %bitcast.2.head_ref.at_ref, bf16[512,512]{1,0:T(8,128)(2,1)S(1)} %finish_value.1.a_ref.x_ref, bf16[512,512]{1,0:T(8,128)(2,1)S(1)} %collective-permute-done.4.b_ref.x_ref, ...), custom_call_target="tpu_custom_call" | custom-call | flops 1 | bytes 1 | tf_op jit(solution)/shard_map/pieces/pallas_call | solution.py:291
  63.1 1.8 %collective-permute-start.20 = (bf16[256,512]{1,0:T(8,128)(2,1)S(1)}, bf16[256,512]{1,0:T(8,128)(2,1)S(1)}, u32[]{:S(2)}, u32[]{:S(2)}) collective-permute-start(bf16[256,512]{1,0:T(8,128)(2,1)S(1)} %get-tuple-element.71), channel_id=1, source_target_pairs={{0,16},{4,20},{16,24},{20,28},{24,8},{28,12},{8,0},{12,4},{1,17},{... | collective-permute-start | bytes 786440 | tf_op jit(solution)/shard_map/ppermute | solution.py:457
  66.9 1.6 %collective-permute-start.23 = (bf16[512,512]{1,0:T(8,128)(2,1)S(1)}, bf16[512,512]{1,0:T(8,128)(2,1)S(1)}, u32[]{:S(2)}, u32[]{:S(2)}) collective-permute-start(bf16[512,512]{1,0:T(8,128)(2,1)S(1)} %head_part.3), channel_id=1, source_target_pairs={{0,2},{1,3},{2,0},{3,1},{4,6},{5,7},{6,4},{7,5},{8,10},{9,11},{10,... | collective-permute-start | bytes 1572872 | tf_op jit(solution)/shard_map/ppermute | solution.py:444
  68.5 1.8 %collective-permute-start.22 = (bf16[256,512]{1,0:T(8,128)(2,1)S(1)}, bf16[256,512]{1,0:T(8,128)(2,1)S(1)}, u32[]{:S(2)}, u32[]{:S(2)}) collective-permute-start(bf16[256,512]{1,0:T(8,128)(2,1)S(1)} %get-tuple-element.83), channel_id=1, source_target_pairs={{0,16},{4,20},{16,24},{20,28},{24,8},{28,12},{8,0},{12,4},{1,17},{... | collective-permute-start | bytes 786440 | tf_op jit(solution)/shard_map/ppermute | solution.py:457
  71.5 2.0 %collective-permute-start.21 = (bf16[256,512]{1,0:T(8,128)(2,1)S(1)}, bf16[256,512]{1,0:T(8,128)(2,1)S(1)}, u32[]{:S(2)}, u32[]{:S(2)}) collective-permute-start(bf16[256,512]{1,0:T(8,128)(2,1)S(1)} %add_own.4), channel_id=1, source_target_pairs={{0,16},{4,20},{16,24},{20,28},{24,8},{28,12},{8,0},{12,4},{1,17},{... | collective-permute-start | bytes 786440 | tf_op jit(solution)/shard_map/ppermute | solution.py:457
  73.4 2.0 %collective-permute-start.19 = (bf16[512,512]{1,0:T(8,128)(2,1)S(1)}, bf16[512,512]{1,0:T(8,128)(2,1)S(1)}, u32[]{:S(2)}, u32[]{:S(2)}) collective-permute-start(bf16[512,512]{1,0:T(8,128)(2,1)S(1)} %head_part.4), channel_id=1, source_target_pairs={{0,2},{1,3},{2,0},{3,1},{4,6},{5,7},{6,4},{7,5},{8,10},{9,11},{10,... | collective-permute-start | bytes 1572872 | tf_op jit(solution)/shard_map/ppermute | solution.py:444
  75.4 2.3 %collective-permute-done.22.moved_ref = bf16[256,512]{1,0:T(8,128)(2,1)S(1)} collective-permute-done((bf16[256,512]{1,0:T(8,128)(2,1)S(1)}, bf16[256,512]{1,0:T(8,128)(2,1)S(1)}, u32[]{:S(2)}, u32[]{:S(2)}) %collective-permute-start.22) | collective-permute-done | bytes 262176 | tf_op jit(solution)/shard_map/ppermute | solution.py:457
  80.2 1.8 %collective-permute-done.21.moved_ref = bf16[256,512]{1,0:T(8,128)(2,1)S(1)} collective-permute-done((bf16[256,512]{1,0:T(8,128)(2,1)S(1)}, bf16[256,512]{1,0:T(8,128)(2,1)S(1)}, u32[]{:S(2)}, u32[]{:S(2)}) %collective-permute-start.21) | collective-permute-done | bytes 262176 | tf_op jit(solution)/shard_map/ppermute | solution.py:457
  83.4 3.1 %collective-permute-start.26 = (bf16[256,512]{1,0:T(8,128)(2,1)S(1)}, bf16[256,512]{1,0:T(8,128)(2,1)S(1)}, u32[]{:S(2)}, u32[]{:S(2)}) collective-permute-start(bf16[256,512]{1,0:T(8,128)(2,1)S(1)} %add_own.5), channel_id=1, source_target_pairs={{0,16},{4,20},{16,24},{20,28},{24,8},{28,12},{8,0},{12,4},{1,17},{... | collective-permute-start | bytes 786440 | tf_op jit(solution)/shard_map/ppermute | solution.py:457
  86.4 1.7 %collective-permute-start.25 = (bf16[256,512]{1,0:T(8,128)(2,1)S(1)}, bf16[256,512]{1,0:T(8,128)(2,1)S(1)}, u32[]{:S(2)}, u32[]{:S(2)}) collective-permute-start(bf16[256,512]{1,0:T(8,128)(2,1)S(1)} %add_own.6), channel_id=1, source_target_pairs={{0,16},{4,20},{16,24},{20,28},{24,8},{28,12},{8,0},{12,4},{1,17},{... | collective-permute-start | bytes 786440 | tf_op jit(solution)/shard_map/ppermute | solution.py:457
  88.1 5.4 %collective-permute-done.26.moved_ref = bf16[256,512]{1,0:T(8,128)(2,1)S(1)} collective-permute-done((bf16[256,512]{1,0:T(8,128)(2,1)S(1)}, bf16[256,512]{1,0:T(8,128)(2,1)S(1)}, u32[]{:S(2)}, u32[]{:S(2)}) %collective-permute-start.26) | collective-permute-done | bytes 262176 | tf_op jit(solution)/shard_map/ppermute | solution.py:457
  93.6 3.1 %collective-permute-start.27 = (bf16[256,512]{1,0:T(8,128)(2,1)S(1)}, bf16[256,512]{1,0:T(8,128)(2,1)S(1)}, u32[]{:S(2)}, u32[]{:S(2)}) collective-permute-start(bf16[256,512]{1,0:T(8,128)(2,1)S(1)} %add_own.7), channel_id=1, source_target_pairs={{0,16},{4,20},{16,24},{20,28},{24,8},{28,12},{8,0},{12,4},{1,17},{... | collective-permute-start | bytes 786440 | tf_op jit(solution)/shard_map/ppermute | solution.py:457
  96.7 4.1 %others.1 = (bf16[512,512]{1,0:T(8,128)(2,1)}, bf16[512,512]{1,0:T(8,128)(2,1)}) custom-call(s32[1]{0:T(128)} %bitcast.par_ref, bf16[512,512]{1,0:T(8,128)(2,1)S(1)} %copy-done.6, bf16[512,512]{1,0:T(8,128)(2,1)S(1)} %copy-done.8, bf16[512,512]{1,0:T(8,128)(2,1)S(1)} %copy-done.11, bf16[512,512]{1,0:T(8,128)(2,1)S(1)} %copy-done.10, ...), custom_call_target="tpu_custom_call" | custom-call | flops 1 | bytes 1 | tf_op jit(solution)/shard_map/others/pallas_call | solution.py:246
  100.8 1.8 %join.1 = bf16[512,1024]{1,0:T(8,128)(2,1)} custom-call(s32[1]{0:T(128)} %bitcast.par_ref, s32[1]{0:T(128)} %bitcast.2.head_ref.at_ref, bf16[512,512]{1,0:T(8,128)(2,1)S(1)} %finish_value.1.a_ref.x_ref, bf16[512,512]{1,0:T(8,128)(2,1)S(1)} %collective-permute-done.3.y_ref, bf16[2,512,512]{2,1,0:T(8,128)(2,1)S(1)} %get-tuple-element.79.w_ref, ...), custom_call_target="tpu_custom_call" | custom-call | flops 1 | bytes 1 | tf_op jit(solution)/shard_map/join/pallas_call | solution.py:418
  102.6 1.3 %collective-permute-done.27.refs_1_ = bf16[256,512]{1,0:T(8,128)(2,1)S(1)} collective-permute-done((bf16[256,512]{1,0:T(8,128)(2,1)S(1)}, bf16[256,512]{1,0:T(8,128)(2,1)S(1)}, u32[]{:S(2)}, u32[]{:S(2)}) %collective-permute-start.27) | collective-permute-done | bytes 262176 | tf_op jit(solution)/shard_map/ppermute | solution.py:457
  103.9 1.3 %finish_weight.1 = f32[512,512]{1,0:T(8,128)} custom-call(bf16[256,512]{1,0:T(8,128)(2,1)S(1)} %collective-permute-done.25.refs_0_, bf16[256,512]{1,0:T(8,128)(2,1)S(1)} %collective-permute-done.27.refs_1_, f32[256,512]{1,0:T(8,128)S(1)} %get-tuple-element.94.refs_2_, f32[256,512]{1,0:T(8,128)S(1)} %get-tuple-element.95.refs_3_), custom_call_target="tpu_custom_call" | custom-call | flops 1 | bytes 1 | tf_op jit(solution)/shard_map/finish_weight/pallas_call | solution.py:315
  (83 shorter events, 19.8 us)
Async XLA Ops:
  4.7 8.1 %collective-permute-start = (bf16[3,2,128,128]{3,2,1,0:T(8,128)(2,1)}, bf16[3,2,128,128]{3,2,1,0:T(8,128)(2,1)S(1)}, u32[]{:S(2)}, u32[]{:S(2)}) collective-permute-start(bf16[3,2,128,128]{3,2,1,0:T(8,128)(2,1)} %get-tuple-element.51), channel_id=1, source_target_pairs={{0,4},{4,0},{8,12},{12,8},{16,20},{20,16},{24,28},{28,24},{1,5},{5... | collective-permute-start | bytes 589832 | tf_op jit(solution)/shard_map/ppermute | solution.py:441
  7.7 15.3 %collective-permute-start.1 = (bf16[512,512]{1,0:T(8,128)(2,1)}, bf16[512,512]{1,0:T(8,128)(2,1)}, u32[]{:S(2)}, u32[]{:S(2)}) collective-permute-start(bf16[512,512]{1,0:T(8,128)(2,1)} %refs_0_.3), channel_id=1, source_target_pairs={{0,16},{4,20},{16,24},{20,28},{24,8},{28,12},{8,0},{12,4},{1,17},{... | collective-permute-start | bytes 1572872 | tf_op jit(solution)/shard_map/ppermute | solution.py:457
  12.8 17.6 %collective-permute-start.8 = (bf16[1,512,512]{2,1,0:T(8,128)(2,1)}, bf16[1,512,512]{2,1,0:T(8,128)(2,1)S(1)}, u32[]{:S(2)}, u32[]{:S(2)}) collective-permute-start(bf16[1,512,512]{2,1,0:T(8,128)(2,1)} %get-tuple-element.67), channel_id=1, source_target_pairs={{0,4},{4,0},{8,12},{12,8},{16,20},{20,16},{24,28},{28,24},{1,5},{5... | collective-permute-start | bytes 1572872 | tf_op jit(solution)/shard_map/ppermute | solution.py:441
  14.5 17.4 %copy-start.7 = (bf16[512,512]{1,0:T(8,128)(2,1)S(1)}, bf16[512,512]{1,0:T(8,128)(2,1)}, u32[]{:S(2)}) copy-start(bf16[512,512]{1,0:T(8,128)(2,1)} %k_ref.1) | copy-start | bytes 1572868
  15.3 16.6 %copy-start.5 = (bf16[512,512]{1,0:T(8,128)(2,1)S(1)}, bf16[512,512]{1,0:T(8,128)(2,1)}, u32[]{:S(2)}) copy-start(bf16[512,512]{1,0:T(8,128)(2,1)} %q_ref.1) | copy-start | bytes 1572868
  15.3 13.5 %all-to-all-start = ((bf16[4,2,128,128]{3,2,1,0:T(8,128)(2,1)}), bf16[4,2,128,128]{3,2,1,0:T(8,128)(2,1)S(1)}, u32[]{:S(2)}, u32[]{:S(2)}) async-start(bf16[4,2,128,128]{3,2,1,0:T(8,128)(2,1)} %offer.1), calls=%async_computation | async-start | bytes 524288 | tf_op jit(solution)/shard_map/all_to_all | solution.py:473
  20.3 16.2 %collective-permute-start.6 = (bf16[1,512,512]{2,1,0:T(8,128)(2,1)S(1)}, bf16[1,512,512]{2,1,0:T(8,128)(2,1)S(1)}, u32[]{:S(2)}, u32[]{:S(2)}) collective-permute-start(bf16[1,512,512]{2,1,0:T(8,128)(2,1)S(1)} %get-tuple-element.64.refs_0_), channel_id=1, source_target_pairs={{0,2},{1,3},{2,0},{3,1},{4,6},{5,7},{6,4},{7,5},{8,10},{9,11},{10,... | collective-permute-start | bytes 1572872 | tf_op jit(solution)/shard_map/ppermute | solution.py:444
  28.9 7.1 %collective-permute-start.2 = (bf16[2,2,128,128]{3,2,1,0:T(8,128)(2,1)S(1)}, bf16[2,2,128,128]{3,2,1,0:T(8,128)(2,1)S(1)}, u32[]{:S(2)}, u32[]{:S(2)}) collective-permute-start(bf16[2,2,128,128]{3,2,1,0:T(8,128)(2,1)S(1)} %get-tuple-element.54), channel_id=1, source_target_pairs={{0,4},{4,0},{8,12},{12,8},{16,20},{20,16},{24,28},{28,24},{1,5},{5... | collective-permute-start | bytes 393224 | tf_op jit(solution)/shard_map/ppermute | solution.py:441
  29.5 11.8 %collective-permute-start.11 = (bf16[512,512]{1,0:T(8,128)(2,1)}, bf16[512,512]{1,0:T(8,128)(2,1)S(1)}, u32[]{:S(2)}, u32[]{:S(2)}) collective-permute-start(bf16[512,512]{1,0:T(8,128)(2,1)} %collective-permute-done.1.refs_1_), channel_id=1, source_target_pairs={{0,16},{4,20},{16,24},{20,28},{24,8},{28,12},{8,0},{12,4},{1,17},{... | collective-permute-start | bytes 1572872 | tf_op jit(solution)/shard_map/ppermute | solution.py:457
  30.4 13.5 %collective-permute-start.10 = (bf16[1,512,512]{2,1,0:T(8,128)(2,1)S(1)}, bf16[1,512,512]{2,1,0:T(8,128)(2,1)S(1)}, u32[]{:S(2)}, u32[]{:S(2)}) collective-permute-start(bf16[1,512,512]{2,1,0:T(8,128)(2,1)S(1)} %collective-permute-done.8.refs_4_), channel_id=1, source_target_pairs={{0,2},{1,3},{2,0},{3,1},{4,6},{5,7},{6,4},{7,5},{8,10},{9,11},{10,... | collective-permute-start | bytes 1572872 | tf_op jit(solution)/shard_map/ppermute | solution.py:444
  36.5 7.4 %collective-permute-start.7 = (bf16[1,512,512]{2,1,0:T(8,128)(2,1)S(1)}, bf16[1,512,512]{2,1,0:T(8,128)(2,1)S(1)}, u32[]{:S(2)}, u32[]{:S(2)}) collective-permute-start(bf16[1,512,512]{2,1,0:T(8,128)(2,1)S(1)} %collective-permute-done.6.refs_2_), channel_id=1, source_target_pairs={{0,1},{1,0},{2,3},{3,2},{4,5},{5,4},{6,7},{7,6},{8,9},{9,8},{10,11... | collective-permute-start | bytes 1572872 | tf_op jit(solution)/shard_map/ppermute | solution.py:444
  36.6 9.9 %collective-permute-start.5 = (bf16[1,512,512]{2,1,0:T(8,128)(2,1)S(1)}, bf16[1,512,512]{2,1,0:T(8,128)(2,1)S(1)}, u32[]{:S(2)}, u32[]{:S(2)}) collective-permute-start(bf16[1,512,512]{2,1,0:T(8,128)(2,1)S(1)} %get-tuple-element.64.refs_0_), channel_id=1, source_target_pairs={{0,1},{1,0},{2,3},{3,2},{4,5},{5,4},{6,7},{7,6},{8,9},{9,8},{10,11... | collective-permute-start | bytes 1572872 | tf_op jit(solution)/shard_map/ppermute | solution.py:444
  37.1 10.4 %collective-permute-start.9 = (bf16[1,512,512]{2,1,0:T(8,128)(2,1)S(1)}, bf16[1,512,512]{2,1,0:T(8,128)(2,1)}, u32[]{:S(2)}, u32[]{:S(2)}) collective-permute-start(bf16[1,512,512]{2,1,0:T(8,128)(2,1)S(1)} %collective-permute-done.8.refs_4_), channel_id=1, source_target_pairs={{0,1},{1,0},{2,3},{3,2},{4,5},{5,4},{6,7},{7,6},{8,9},{9,8},{10,11... | collective-permute-start | bytes 1572872 | tf_op jit(solution)/shard_map/ppermute | solution.py:444
  41.3 10.7 %collective-permute-start.4 = (bf16[512,512]{1,0:T(8,128)(2,1)S(1)}, bf16[512,512]{1,0:T(8,128)(2,1)S(1)}, u32[]{:S(2)}, u32[]{:S(2)}) collective-permute-start(bf16[512,512]{1,0:T(8,128)(2,1)S(1)} %finish_value.1.a_ref.x_ref), channel_id=1, source_target_pairs={{0,4},{4,0},{8,12},{12,8},{16,20},{20,16},{24,28},{28,24},{1,5},{5... | collective-permute-start | bytes 1572872 | tf_op jit(solution)/shard_map/ppermute | solution.py:441
  43.9 8.1 %collective-permute-start.12 = (bf16[1,512,512]{2,1,0:T(8,128)(2,1)S(1)}, bf16[1,512,512]{2,1,0:T(8,128)(2,1)}, u32[]{:S(2)}, u32[]{:S(2)}) collective-permute-start(bf16[1,512,512]{2,1,0:T(8,128)(2,1)S(1)} %collective-permute-done.10.refs_6_), channel_id=1, source_target_pairs={{0,1},{1,0},{2,3},{3,2},{4,5},{5,4},{6,7},{7,6},{8,9},{9,8},{10,11... | collective-permute-start | bytes 1572872 | tf_op jit(solution)/shard_map/ppermute | solution.py:444
  44.7 15.6 %collective-permute-start.13 = (bf16[512,512]{1,0:T(8,128)(2,1)}, bf16[512,512]{1,0:T(8,128)(2,1)}, u32[]{:S(2)}, u32[]{:S(2)}) collective-permute-start(bf16[512,512]{1,0:T(8,128)(2,1)} %refs_0_.3), channel_id=1, source_target_pairs={{16,0},{20,4},{24,16},{28,20},{8,24},{12,28},{0,8},{4,12},{17,1},{... | collective-permute-start | bytes 1572872 | tf_op jit(solution)/shard_map/ppermute | solution.py:460
  47.2 13.5 %collective-permute-start.15 = (bf16[512,512]{1,0:T(8,128)(2,1)}, bf16[512,512]{1,0:T(8,128)(2,1)}, u32[]{:S(2)}, u32[]{:S(2)}) collective-permute-start(bf16[512,512]{1,0:T(8,128)(2,1)} %collective-permute-done.1.refs_1_), channel_id=1, source_target_pairs={{0,1},{1,0},{2,3},{3,2},{4,5},{5,4},{6,7},{7,6},{8,9},{9,8},{10,11... | collective-permute-start | bytes 1572872 | tf_op jit(solution)/shard_map/ppermute | solution.py:444
  47.5 15.6 %collective-permute-start.14 = (bf16[512,512]{1,0:T(8,128)(2,1)}, bf16[512,512]{1,0:T(8,128)(2,1)S(1)}, u32[]{:S(2)}, u32[]{:S(2)}) collective-permute-start(bf16[512,512]{1,0:T(8,128)(2,1)} %refs_0_.3), channel_id=1, source_target_pairs={{0,1},{1,0},{2,3},{3,2},{4,5},{5,4},{6,7},{7,6},{8,9},{9,8},{10,11... | collective-permute-start | bytes 1572872 | tf_op jit(solution)/shard_map/ppermute | solution.py:444
  60.2 4.6 %collective-permute-start.17 = (bf16[512,512]{1,0:T(8,128)(2,1)}, bf16[512,512]{1,0:T(8,128)(2,1)S(1)}, u32[]{:S(2)}, u32[]{:S(2)}) collective-permute-start(bf16[512,512]{1,0:T(8,128)(2,1)} %collective-permute-done.13.refs_3_), channel_id=1, source_target_pairs={{0,1},{1,0},{2,3},{3,2},{4,5},{5,4},{6,7},{7,6},{8,9},{9,8},{10,11... | collective-permute-start | bytes 1572872 | tf_op jit(solution)/shard_map/ppermute | solution.py:444
  60.2 4.6 %collective-permute-start.16 = (bf16[512,512]{1,0:T(8,128)(2,1)S(1)}, bf16[512,512]{1,0:T(8,128)(2,1)S(1)}, u32[]{:S(2)}, u32[]{:S(2)}) collective-permute-start(bf16[512,512]{1,0:T(8,128)(2,1)S(1)} %copy-done.16), channel_id=1, source_target_pairs={{0,1},{1,0},{2,3},{3,2},{4,5},{5,4},{6,7},{7,6},{8,9},{9,8},{10,11... | collective-permute-start | bytes 1572872 | tf_op jit(solution)/shard_map/ppermute | solution.py:444
  60.7 5.4 %collective-permute-start.18 = (bf16[512,512]{1,0:T(8,128)(2,1)S(1)}, bf16[512,512]{1,0:T(8,128)(2,1)S(1)}, u32[]{:S(2)}, u32[]{:S(2)}) collective-permute-start(bf16[512,512]{1,0:T(8,128)(2,1)S(1)} %collective-permute-done.4.b_ref.x_ref), channel_id=1, source_target_pairs={{0,1},{1,0},{2,3},{3,2},{4,5},{5,4},{6,7},{7,6},{8,9},{9,8},{10,11... | collective-permute-start | bytes 1572872 | tf_op jit(solution)/shard_map/ppermute | solution.py:444
  60.8 9.6 %collective-permute-start.3 = (bf16[512,512]{1,0:T(8,128)(2,1)S(1)}, bf16[512,512]{1,0:T(8,128)(2,1)S(1)}, u32[]{:S(2)}, u32[]{:S(2)}) collective-permute-start(bf16[512,512]{1,0:T(8,128)(2,1)S(1)} %finish_value.1.a_ref.x_ref), channel_id=1, source_target_pairs={{0,1},{1,0},{2,3},{3,2},{4,5},{5,4},{6,7},{7,6},{8,9},{9,8},{10,11... | collective-permute-start | bytes 1572872 | tf_op jit(solution)/shard_map/ppermute | solution.py:444
  63.1 8.3 %collective-permute-start.20 = (bf16[256,512]{1,0:T(8,128)(2,1)S(1)}, bf16[256,512]{1,0:T(8,128)(2,1)S(1)}, u32[]{:S(2)}, u32[]{:S(2)}) collective-permute-start(bf16[256,512]{1,0:T(8,128)(2,1)S(1)} %get-tuple-element.71), channel_id=1, source_target_pairs={{0,16},{4,20},{16,24},{20,28},{24,8},{28,12},{8,0},{12,4},{1,17},{... | collective-permute-start | bytes 786440 | tf_op jit(solution)/shard_map/ppermute | solution.py:457
  66.9 15.0 %collective-permute-start.23 = (bf16[512,512]{1,0:T(8,128)(2,1)S(1)}, bf16[512,512]{1,0:T(8,128)(2,1)S(1)}, u32[]{:S(2)}, u32[]{:S(2)}) collective-permute-start(bf16[512,512]{1,0:T(8,128)(2,1)S(1)} %head_part.3), channel_id=1, source_target_pairs={{0,2},{1,3},{2,0},{3,1},{4,6},{5,7},{6,4},{7,5},{8,10},{9,11},{10,... | collective-permute-start | bytes 1572872 | tf_op jit(solution)/shard_map/ppermute | solution.py:444
  68.5 9.2 %collective-permute-start.22 = (bf16[256,512]{1,0:T(8,128)(2,1)S(1)}, bf16[256,512]{1,0:T(8,128)(2,1)S(1)}, u32[]{:S(2)}, u32[]{:S(2)}) collective-permute-start(bf16[256,512]{1,0:T(8,128)(2,1)S(1)} %get-tuple-element.83), channel_id=1, source_target_pairs={{0,16},{4,20},{16,24},{20,28},{24,8},{28,12},{8,0},{12,4},{1,17},{... | collective-permute-start | bytes 786440 | tf_op jit(solution)/shard_map/ppermute | solution.py:457
  71.5 10.5 %collective-permute-start.21 = (bf16[256,512]{1,0:T(8,128)(2,1)S(1)}, bf16[256,512]{1,0:T(8,128)(2,1)S(1)}, u32[]{:S(2)}, u32[]{:S(2)}) collective-permute-start(bf16[256,512]{1,0:T(8,128)(2,1)S(1)} %add_own.4), channel_id=1, source_target_pairs={{0,16},{4,20},{16,24},{20,28},{24,8},{28,12},{8,0},{12,4},{1,17},{... | collective-permute-start | bytes 786440 | tf_op jit(solution)/shard_map/ppermute | solution.py:457
  73.4 27.4 %collective-permute-start.19 = (bf16[512,512]{1,0:T(8,128)(2,1)S(1)}, bf16[512,512]{1,0:T(8,128)(2,1)S(1)}, u32[]{:S(2)}, u32[]{:S(2)}) collective-permute-start(bf16[512,512]{1,0:T(8,128)(2,1)S(1)} %head_part.4), channel_id=1, source_target_pairs={{0,2},{1,3},{2,0},{3,1},{4,6},{5,7},{6,4},{7,5},{8,10},{9,11},{10,... | collective-permute-start | bytes 1572872 | tf_op jit(solution)/shard_map/ppermute | solution.py:444
  82.0 14.7 %copy-start.10 = (bf16[512,512]{1,0:T(8,128)(2,1)S(1)}, bf16[512,512]{1,0:T(8,128)(2,1)}, u32[]{:S(2)}) copy-start(bf16[512,512]{1,0:T(8,128)(2,1)} %g_ref.1) | copy-start | bytes 1572868
  82.8 18.0 %collective-permute-start.24 = (bf16[512,512]{1,0:T(8,128)(2,1)S(1)}, bf16[512,512]{1,0:T(8,128)(2,1)S(1)}, u32[]{:S(2)}, u32[]{:S(2)}) collective-permute-start(bf16[512,512]{1,0:T(8,128)(2,1)S(1)} %head_part.5), channel_id=1, source_target_pairs={{0,4},{4,0},{8,12},{12,8},{16,20},{20,16},{24,28},{28,24},{1,5},{5... | collective-permute-start | bytes 1572872 | tf_op jit(solution)/shard_map/ppermute | solution.py:441
  83.4 10.2 %collective-permute-start.26 = (bf16[256,512]{1,0:T(8,128)(2,1)S(1)}, bf16[256,512]{1,0:T(8,128)(2,1)S(1)}, u32[]{:S(2)}, u32[]{:S(2)}) collective-permute-start(bf16[256,512]{1,0:T(8,128)(2,1)S(1)} %add_own.5), channel_id=1, source_target_pairs={{0,16},{4,20},{16,24},{20,28},{24,8},{28,12},{8,0},{12,4},{1,17},{... | collective-permute-start | bytes 786440 | tf_op jit(solution)/shard_map/ppermute | solution.py:457
  86.4 16.2 %collective-permute-start.25 = (bf16[256,512]{1,0:T(8,128)(2,1)S(1)}, bf16[256,512]{1,0:T(8,128)(2,1)S(1)}, u32[]{:S(2)}, u32[]{:S(2)}) collective-permute-start(bf16[256,512]{1,0:T(8,128)(2,1)S(1)} %add_own.6), channel_id=1, source_target_pairs={{0,16},{4,20},{16,24},{20,28},{24,8},{28,12},{8,0},{12,4},{1,17},{... | collective-permute-start | bytes 786440 | tf_op jit(solution)/shard_map/ppermute | solution.py:457
  93.6 10.3 %collective-permute-start.27 = (bf16[256,512]{1,0:T(8,128)(2,1)S(1)}, bf16[256,512]{1,0:T(8,128)(2,1)S(1)}, u32[]{:S(2)}, u32[]{:S(2)}) collective-permute-start(bf16[256,512]{1,0:T(8,128)(2,1)S(1)} %add_own.7), channel_id=1, source_target_pairs={{0,16},{4,20},{16,24},{20,28},{24,8},{28,12},{8,0},{12,4},{1,17},{... | collective-permute-start | bytes 786440 | tf_op jit(solution)/shard_map/ppermute | solution.py:457
  (15 other events, 91.4 us)

commit v21 on v18

--- a/solution.py
+++ b/solution.py
@@ -520,7 +520,7 @@
     moved = [ring(x) for x in total]
     other_too = across(other, 1)
     lent = lent + [across(after(x, total[0]), 1) for x in blocks[early:]]
-    local_part = piece(F32, 1, total[0])
+    local_part = piece(F32, 1, lent[-1])
 
 
     def summed_parts(x, y):

time: 102 us -> 105 us (1.029)
  waiting for transfers between devices: 30.7 us -> 34.8 us
  local copies, waits for them, and re-layouts: 4.77 us -> 2.93 us
    ppermute x14, waiting for transfers between devices: 1.11 us -> 4.74 us  [across(): return lax.ppermute(x, 'head', [(i, i ^ bit) for i in range(n_head)])]
    ppermute x1, waiting for transfers between devices: 4.32 us -> 6.23 us  [back(): return lax.ppermute(x, 'ctx', [(b, a) for a, b in moves])]
    unnamed x36 -> x32, local copies, waits for them, and re-layouts: 4.77 us -> 2.93 us
    ppermute x8, waiting for transfers between devices: 13.6 us -> 11.9 us  [ring(): return lax.ppermute(x, 'ctx', moves)]
  transfers between devices with their start and end apart: 29 -> 29, of which waited for: 11 -> 13; matrix products, arithmetic and copies ran while one was open for 0% -> 0% of each run, Pallas kernels for 20% -> 20%
where the time goes in v21:
time: 105 us
  starting transfers between devices  40 us (38%)
  waiting for transfers between devices  34.8 us (33%)
  Pallas kernels  26.3 us (25%)
  local copies, waits for them, and re-layouts  2.93 us (3%)
    ppermute x8, starting transfers between devices, ring(): return lax.ppermute(x, 'ctx', moves)  18.4 us
    ppermute x8, waiting for transfers between devices, ring(): return lax.ppermute(x, 'ctx', moves)  11.9 us
    ppermute x5, starting transfers between devices, partner(): return lax.ppermute(x, 'ctx', [(i, i ^ 1) for i in range(n_ctx)])  7.43 us
    ppermute x14, starting transfers between devices, across(): return lax.ppermute(x, 'head', [(i, i ^ bit) for i in range(n_head)])  7.39 us
    ppermute x1, waiting for transfers between devices, back(): return lax.ppermute(x, 'ctx', [(b, a) for a, b in moves])  6.23 us
    ppermute x5, waiting for transfers between devices, partner(): return lax.ppermute(x, 'ctx', [(i, i ^ 1) for i in range(n_ctx)])  6.1 us
    pallas_call x4, Pallas kernels, pieces(): call(functools.partial(piece_kernel, order, per, step, count), flops=flop...  6.04 us
    all_to_all x1, waiting for transfers between devices, local(): lax.all_to_all(offered, 'ctx', split_axis=0, concat_axis=0, axis_index_gr...  5.85 us
  transfers between devices with their start and end apart: 29, of which 13 were waited for; matrix products, arithmetic and copies ran while one was open for 0% of the time, Pallas kernels for 20%

profile of v21, /device:TPU:0, one launch (start us, length us, event | category | flops | bytes accessed | tf_op | source)
XLA Modules:
  0.0 104.9 jit_solution(16101609865961677623)
XLA Ops:
  0.7 4.0 %states.1 = (f32[2,2,128,128]{3,2,1,0:T(8,128)}, bf16[3,2,128,128]{3,2,1,0:T(8,128)(2,1)}) custom-call(s32[1]{0:T(128)} %bitcast.par_ref, bf16[512,512]{1,0:T(8,128)(2,1)} %q_ref.1, bf16[512,512]{1,0:T(8,128)(2,1)} %k_ref.1, bf16[512,512]{1,0:T(8,128)(2,1)} %v_ref, bf16[512,512]{1,0:T(8,128)(2,1)} %g_ref.1), custom_call_target="tpu_custom_call" | custom-call | flops 1 | bytes 1 | tf_op jit(solution)/shard_map/states/pallas_call | solution.py:67
  4.7 3.0 %collective-permute-start = (bf16[3,2,128,128]{3,2,1,0:T(8,128)(2,1)}, bf16[3,2,128,128]{3,2,1,0:T(8,128)(2,1)S(1)}, u32[]{:S(2)}, u32[]{:S(2)}) collective-permute-start(bf16[3,2,128,128]{3,2,1,0:T(8,128)(2,1)} %get-tuple-element.51), channel_id=1, source_target_pairs={{0,4},{4,0},{8,12},{12,8},{16,20},{20,16},{24,28},{28,24},{1,5},{5... | collective-permute-start | bytes 589832 | tf_op jit(solution)/shard_map/ppermute | solution.py:441
  7.7 2.6 %collective-permute-start.1 = (bf16[512,512]{1,0:T(8,128)(2,1)}, bf16[512,512]{1,0:T(8,128)(2,1)}, u32[]{:S(2)}, u32[]{:S(2)}) collective-permute-start(bf16[512,512]{1,0:T(8,128)(2,1)} %refs_0_.3), channel_id=1, source_target_pairs={{0,16},{4,20},{16,24},{20,28},{24,8},{28,12},{8,0},{12,4},{1,17},{... | collective-permute-start | bytes 1572872 | tf_op jit(solution)/shard_map/ppermute | solution.py:457
  11.2 1.6 %collective-permute-done.got_ref.refs_2_ = bf16[3,2,128,128]{3,2,1,0:T(8,128)(2,1)S(1)} collective-permute-done((bf16[3,2,128,128]{3,2,1,0:T(8,128)(2,1)}, bf16[3,2,128,128]{3,2,1,0:T(8,128)(2,1)S(1)}, u32[]{:S(2)}, u32[]{:S(2)}) %collective-permute-start) | collective-permute-done | bytes 196640 | tf_op jit(solution)/shard_map/ppermute | solution.py:441
  12.8 1.7 %collective-permute-start.7 = (bf16[1,512,512]{2,1,0:T(8,128)(2,1)}, bf16[1,512,512]{2,1,0:T(8,128)(2,1)S(1)}, u32[]{:S(2)}, u32[]{:S(2)}) collective-permute-start(bf16[1,512,512]{2,1,0:T(8,128)(2,1)} %get-tuple-element.67), channel_id=1, source_target_pairs={{0,4},{4,0},{8,12},{12,8},{16,20},{20,16},{24,28},{28,24},{1,5},{5... | collective-permute-start | bytes 1572872 | tf_op jit(solution)/shard_map/ppermute | solution.py:441
  15.3 5.0 %all-to-all-start = ((bf16[4,2,128,128]{3,2,1,0:T(8,128)(2,1)}), bf16[4,2,128,128]{3,2,1,0:T(8,128)(2,1)S(1)}, u32[]{:S(2)}, u32[]{:S(2)}) async-start(bf16[4,2,128,128]{3,2,1,0:T(8,128)(2,1)} %offer.1), calls=%async_computation | async-start | bytes 524288 | tf_op jit(solution)/shard_map/all_to_all | solution.py:473
  20.3 1.5 %collective-permute-start.5 = (bf16[1,512,512]{2,1,0:T(8,128)(2,1)S(1)}, bf16[1,512,512]{2,1,0:T(8,128)(2,1)S(1)}, u32[]{:S(2)}, u32[]{:S(2)}) collective-permute-start(bf16[1,512,512]{2,1,0:T(8,128)(2,1)S(1)} %get-tuple-element.64.refs_0_), channel_id=1, source_target_pairs={{0,2},{1,3},{2,0},{3,1},{4,6},{5,7},{6,4},{7,5},{8,10},{9,11},{10,... | collective-permute-start | bytes 1572872 | tf_op jit(solution)/shard_map/ppermute | solution.py:444
  23.0 5.8 %all-to-all-done.every_ref = bf16[4,2,128,128]{3,2,1,0:T(8,128)(2,1)S(1)} async-done(((bf16[4,2,128,128]{3,2,1,0:T(8,128)(2,1)}), bf16[4,2,128,128]{3,2,1,0:T(8,128)(2,1)S(1)}, u32[]{:S(2)}, u32[]{:S(2)}) %all-to-all-start) | async-done | bytes 262176 | tf_op jit(solution)/shard_map/all_to_all | solution.py:473
  30.4 1.5 %collective-permute-start.9 = (bf16[1,512,512]{2,1,0:T(8,128)(2,1)S(1)}, bf16[1,512,512]{2,1,0:T(8,128)(2,1)S(1)}, u32[]{:S(2)}, u32[]{:S(2)}) collective-permute-start(bf16[1,512,512]{2,1,0:T(8,128)(2,1)S(1)} %collective-permute-done.7.refs_4_), channel_id=1, source_target_pairs={{0,2},{1,3},{2,0},{3,1},{4,6},{5,7},{6,4},{7,5},{8,10},{9,11},{10,... | collective-permute-start | bytes 1572872 | tf_op jit(solution)/shard_map/ppermute | solution.py:444
  33.0 3.0 %inside.1 = (f32[512,512]{1,0:T(8,128)S(1)}, bf16[512,512]{1,0:T(8,128)(2,1)S(1)}) custom-call(bf16[512,512]{1,0:T(8,128)(2,1)S(1)} %copy-done.3, bf16[512,512]{1,0:T(8,128)(2,1)S(1)} %copy-done.5, bf16[512,512]{1,0:T(8,128)(2,1)S(1)} %copy-done.7), custom_call_target="tpu_custom_call" | custom-call | flops 1 | bytes 1 | tf_op jit(solution)/shard_map/inside/pallas_call | solution.py:147
  37.1 1.5 %collective-permute-start.3 = (bf16[512,512]{1,0:T(8,128)(2,1)S(1)}, bf16[512,512]{1,0:T(8,128)(2,1)S(1)}, u32[]{:S(2)}, u32[]{:S(2)}) collective-permute-start(bf16[512,512]{1,0:T(8,128)(2,1)S(1)} %finish_value.1.a_ref.x_ref), channel_id=1, source_target_pairs={{0,4},{4,0},{8,12},{12,8},{16,20},{20,16},{24,28},{28,24},{1,5},{5... | collective-permute-start | bytes 1572872 | tf_op jit(solution)/shard_map/ppermute | solution.py:441
  38.6 2.7 %collective-permute-done.10.refs_2_ = bf16[512,512]{1,0:T(8,128)(2,1)S(1)} collective-permute-done((bf16[512,512]{1,0:T(8,128)(2,1)}, bf16[512,512]{1,0:T(8,128)(2,1)S(1)}, u32[]{:S(2)}, u32[]{:S(2)}) %collective-permute-start.10) | collective-permute-done | bytes 524320 | tf_op jit(solution)/shard_map/ppermute | solution.py:457
  41.3 2.6 %collective-permute-done.9.refs_6_ = bf16[1,512,512]{2,1,0:T(8,128)(2,1)S(1)} collective-permute-done((bf16[1,512,512]{2,1,0:T(8,128)(2,1)S(1)}, bf16[1,512,512]{2,1,0:T(8,128)(2,1)S(1)}, u32[]{:S(2)}, u32[]{:S(2)}) %collective-permute-start.9) | collective-permute-done | bytes 524320 | tf_op jit(solution)/shard_map/ppermute | solution.py:444
  44.7 1.7 %collective-permute-start.13 = (bf16[512,512]{1,0:T(8,128)(2,1)}, bf16[512,512]{1,0:T(8,128)(2,1)}, u32[]{:S(2)}, u32[]{:S(2)}) collective-permute-start(bf16[512,512]{1,0:T(8,128)(2,1)} %refs_0_.3), channel_id=1, source_target_pairs={{16,0},{20,4},{24,16},{28,20},{8,24},{12,28},{0,8},{4,12},{17,1},{... | collective-permute-start | bytes 1572872 | tf_op jit(solution)/shard_map/ppermute | solution.py:460
  46.4 4.5 %collective-permute-done.3.b_ref.x_ref = bf16[512,512]{1,0:T(8,128)(2,1)S(1)} collective-permute-done((bf16[512,512]{1,0:T(8,128)(2,1)S(1)}, bf16[512,512]{1,0:T(8,128)(2,1)S(1)}, u32[]{:S(2)}, u32[]{:S(2)}) %collective-permute-start.3) | collective-permute-done | bytes 524320 | tf_op jit(solution)/shard_map/ppermute | solution.py:441
  52.0 2.0 %pieces.4 = (bf16[256,512]{1,0:T(8,128)(2,1)S(1)}, bf16[256,512]{1,0:T(8,128)(2,1)S(1)}) custom-call(s32[1]{0:T(128)} %bitcast.3.spot_ref, s32[1]{0:T(128)} %bitcast.2.head_ref.at_ref, bf16[512,512]{1,0:T(8,128)(2,1)S(1)} %finish_value.1.a_ref.x_ref, bf16[512,512]{1,0:T(8,128)(2,1)S(1)} %collective-permute-done.3.b_ref.x_ref, ...), custom_call_target="tpu_custom_call" | custom-call | flops 536870912 | bytes 1 | tf_op jit(solution)/shard_map/pieces/pallas_call | solution.py:291
  54.0 6.2 %collective-permute-done.13.refs_3_ = bf16[512,512]{1,0:T(8,128)(2,1)} collective-permute-done((bf16[512,512]{1,0:T(8,128)(2,1)}, bf16[512,512]{1,0:T(8,128)(2,1)}, u32[]{:S(2)}, u32[]{:S(2)}) %collective-permute-start.13) | collective-permute-done | bytes 524320 | tf_op jit(solution)/shard_map/ppermute | solution.py:460
  62.5 1.8 %pieces.5 = (f32[256,512]{1,0:T(8,128)S(1)}, f32[256,512]{1,0:T(8,128)S(1)}) custom-call(s32[1]{0:T(128)} %bitcast.3.spot_ref, s32[1]{0:T(128)} %bitcast.2.head_ref.at_ref, bf16[512,512]{1,0:T(8,128)(2,1)S(1)} %finish_value.1.a_ref.x_ref, bf16[512,512]{1,0:T(8,128)(2,1)S(1)} %collective-permute-done.3.b_ref.x_ref, ...), custom_call_target="tpu_custom_call" | custom-call | flops 1 | bytes 1 | tf_op jit(solution)/shard_map/pieces/pallas_call | solution.py:291
  65.4 1.7 %collective-permute-start.12 = (bf16[256,512]{1,0:T(8,128)(2,1)S(1)}, bf16[256,512]{1,0:T(8,128)(2,1)S(1)}, u32[]{:S(2)}, u32[]{:S(2)}) collective-permute-start(bf16[256,512]{1,0:T(8,128)(2,1)S(1)} %get-tuple-element.71), channel_id=1, source_target_pairs={{0,16},{4,20},{16,24},{20,28},{24,8},{28,12},{8,0},{12,4},{1,17},{... | collective-permute-start | bytes 786440 | tf_op jit(solution)/shard_map/ppermute | solution.py:457
  67.1 1.3 %arrange.1 = (bf16[2,512,512]{2,1,0:T(8,128)(2,1)S(1)}, bf16[2,512,512]{2,1,0:T(8,128)(2,1)S(1)}) custom-call(s32[1]{0:T(128)} %bitcast.2.head_ref.at_ref, s32[1]{0:T(128)} %bitcast.3.spot_ref, bf16[512,512]{1,0:T(8,128)(2,1)} %refs_0_.3, bf16[512,512]{1,0:T(8,128)(2,1)} %collective-permute-done.1.refs_1_, bf16[512,512]{1,0:T(8,128)(2,1)S(1)} %copy-done.14, ...), custom_call_target="tpu_custom_call" | custom-call | flops 1 | bytes 1 | tf_op jit(solution)/shard_map/arrange/pallas_call | solution.py:367
  69.2 1.6 %collective-permute-start.24 = (bf16[512,512]{1,0:T(8,128)(2,1)S(1)}, bf16[512,512]{1,0:T(8,128)(2,1)S(1)}, u32[]{:S(2)}, u32[]{:S(2)}) collective-permute-start(bf16[512,512]{1,0:T(8,128)(2,1)S(1)} %head_part.3), channel_id=1, source_target_pairs={{0,2},{1,3},{2,0},{3,1},{4,6},{5,7},{6,4},{7,5},{8,10},{9,11},{10,... | collective-permute-start | bytes 1572872 | tf_op jit(solution)/shard_map/ppermute | solution.py:444
  70.8 2.4 %collective-permute-start.21 = (bf16[256,512]{1,0:T(8,128)(2,1)S(1)}, bf16[256,512]{1,0:T(8,128)(2,1)S(1)}, u32[]{:S(2)}, u32[]{:S(2)}) collective-permute-start(bf16[256,512]{1,0:T(8,128)(2,1)S(1)} %get-tuple-element.83), channel_id=1, source_target_pairs={{0,16},{4,20},{16,24},{20,28},{24,8},{28,12},{8,0},{12,4},{1,17},{... | collective-permute-start | bytes 786440 | tf_op jit(solution)/shard_map/ppermute | solution.py:457
  74.6 2.1 %collective-permute-start.20 = (bf16[256,512]{1,0:T(8,128)(2,1)S(1)}, bf16[256,512]{1,0:T(8,128)(2,1)S(1)}, u32[]{:S(2)}, u32[]{:S(2)}) collective-permute-start(bf16[256,512]{1,0:T(8,128)(2,1)S(1)} %add_own.4), channel_id=1, source_target_pairs={{0,16},{4,20},{16,24},{20,28},{24,8},{28,12},{8,0},{12,4},{1,17},{... | collective-permute-start | bytes 786440 | tf_op jit(solution)/shard_map/ppermute | solution.py:457
  76.6 3.5 %collective-permute-done.21.moved_ref = bf16[256,512]{1,0:T(8,128)(2,1)S(1)} collective-permute-done((bf16[256,512]{1,0:T(8,128)(2,1)S(1)}, bf16[256,512]{1,0:T(8,128)(2,1)S(1)}, u32[]{:S(2)}, u32[]{:S(2)}) %collective-permute-start.21) | collective-permute-done | bytes 262176 | tf_op jit(solution)/shard_map/ppermute | solution.py:457
  80.2 3.2 %collective-permute-start.23 = (bf16[256,512]{1,0:T(8,128)(2,1)S(1)}, bf16[256,512]{1,0:T(8,128)(2,1)S(1)}, u32[]{:S(2)}, u32[]{:S(2)}) collective-permute-start(bf16[256,512]{1,0:T(8,128)(2,1)S(1)} %add_own.5), channel_id=1, source_target_pairs={{0,16},{4,20},{16,24},{20,28},{24,8},{28,12},{8,0},{12,4},{1,17},{... | collective-permute-start | bytes 786440 | tf_op jit(solution)/shard_map/ppermute | solution.py:457
  85.5 1.1 %pieces.7 = (f32[256,512]{1,0:T(8,128)S(1)}, f32[256,512]{1,0:T(8,128)S(1)}) custom-call(s32[1]{0:T(128)} %bitcast.3.spot_ref, s32[1]{0:T(128)} %bitcast.2.head_ref.at_ref, bf16[512,512]{1,0:T(8,128)(2,1)S(1)} %finish_value.1.a_ref.x_ref, bf16[512,512]{1,0:T(8,128)(2,1)S(1)} %collective-permute-done.3.b_ref.x_ref, ...), custom_call_target="tpu_custom_call" | custom-call | flops 1 | bytes 1 | tf_op jit(solution)/shard_map/pieces/pallas_call | solution.py:291
  88.2 2.2 %collective-permute-start.22 = (bf16[256,512]{1,0:T(8,128)(2,1)S(1)}, bf16[256,512]{1,0:T(8,128)(2,1)S(1)}, u32[]{:S(2)}, u32[]{:S(2)}) collective-permute-start(bf16[256,512]{1,0:T(8,128)(2,1)S(1)} %add_own.6), channel_id=1, source_target_pairs={{0,16},{4,20},{16,24},{20,28},{24,8},{28,12},{8,0},{12,4},{1,17},{... | collective-permute-start | bytes 786440 | tf_op jit(solution)/shard_map/ppermute | solution.py:457
  91.2 3.4 %collective-permute-start.25 = (bf16[256,512]{1,0:T(8,128)(2,1)S(1)}, bf16[256,512]{1,0:T(8,128)(2,1)S(1)}, u32[]{:S(2)}, u32[]{:S(2)}) collective-permute-start(bf16[256,512]{1,0:T(8,128)(2,1)S(1)} %add_own.7), channel_id=1, source_target_pairs={{0,16},{4,20},{16,24},{20,28},{24,8},{28,12},{8,0},{12,4},{1,17},{... | collective-permute-start | bytes 786440 | tf_op jit(solution)/shard_map/ppermute | solution.py:457
  94.6 4.1 %others.1 = (bf16[512,512]{1,0:T(8,128)(2,1)}, bf16[512,512]{1,0:T(8,128)(2,1)}) custom-call(s32[1]{0:T(128)} %bitcast.par_ref, bf16[512,512]{1,0:T(8,128)(2,1)S(1)} %copy-done.4, bf16[512,512]{1,0:T(8,128)(2,1)S(1)} %copy-done.6, bf16[512,512]{1,0:T(8,128)(2,1)S(1)} %copy-done.9, bf16[512,512]{1,0:T(8,128)(2,1)S(1)} %copy-done.8, ...), custom_call_target="tpu_custom_call" | custom-call | flops 1 | bytes 1 | tf_op jit(solution)/shard_map/others/pallas_call | solution.py:246
  98.7 3.1 %collective-permute-done.25.refs_1_ = bf16[256,512]{1,0:T(8,128)(2,1)S(1)} collective-permute-done((bf16[256,512]{1,0:T(8,128)(2,1)S(1)}, bf16[256,512]{1,0:T(8,128)(2,1)S(1)}, u32[]{:S(2)}, u32[]{:S(2)}) %collective-permute-start.25) | collective-permute-done | bytes 262176 | tf_op jit(solution)/shard_map/ppermute | solution.py:457
  101.8 1.3 %finish_weight.1 = f32[512,512]{1,0:T(8,128)} custom-call(bf16[256,512]{1,0:T(8,128)(2,1)S(1)} %collective-permute-done.22.refs_0_, bf16[256,512]{1,0:T(8,128)(2,1)S(1)} %collective-permute-done.25.refs_1_, f32[256,512]{1,0:T(8,128)S(1)} %get-tuple-element.89.refs_2_, f32[256,512]{1,0:T(8,128)S(1)} %get-tuple-element.94.refs_3_), custom_call_target="tpu_custom_call" | custom-call | flops 1 | bytes 1 | tf_op jit(solution)/shard_map/finish_weight/pallas_call | solution.py:315
  103.1 1.8 %join.1 = bf16[512,1024]{1,0:T(8,128)(2,1)} custom-call(s32[1]{0:T(128)} %bitcast.par_ref, s32[1]{0:T(128)} %bitcast.2.head_ref.at_ref, bf16[512,512]{1,0:T(8,128)(2,1)S(1)} %finish_value.1.a_ref.x_ref, bf16[512,512]{1,0:T(8,128)(2,1)S(1)} %collective-permute-done.19.y_ref, bf16[2,512,512]{2,1,0:T(8,128)(2,1)S(1)} %get-tuple-element.79.w_ref, ...), custom_call_target="tpu_custom_call" | custom-call | flops 1 | bytes 1 | tf_op jit(solution)/shard_map/join/pallas_call | solution.py:418
  (79 shorter events, 18.4 us)
Async XLA Ops:
  4.7 9.9 %copy-start.15 = (f32[2,2,128,128]{3,2,1,0:T(8,128)S(1)}, f32[2,2,128,128]{3,2,1,0:T(8,128)}, u32[]{:S(2)}) copy-start(f32[2,2,128,128]{3,2,1,0:T(8,128)} %get-tuple-element.50.keep_ref) | copy-start | bytes 786436
  4.7 8.1 %collective-permute-start = (bf16[3,2,128,128]{3,2,1,0:T(8,128)(2,1)}, bf16[3,2,128,128]{3,2,1,0:T(8,128)(2,1)S(1)}, u32[]{:S(2)}, u32[]{:S(2)}) collective-permute-start(bf16[3,2,128,128]{3,2,1,0:T(8,128)(2,1)} %get-tuple-element.51), channel_id=1, source_target_pairs={{0,4},{4,0},{8,12},{12,8},{16,20},{20,16},{24,28},{28,24},{1,5},{5... | collective-permute-start | bytes 589832 | tf_op jit(solution)/shard_map/ppermute | solution.py:441
  7.7 15.3 %collective-permute-start.1 = (bf16[512,512]{1,0:T(8,128)(2,1)}, bf16[512,512]{1,0:T(8,128)(2,1)}, u32[]{:S(2)}, u32[]{:S(2)}) collective-permute-start(bf16[512,512]{1,0:T(8,128)(2,1)} %refs_0_.3), channel_id=1, source_target_pairs={{0,16},{4,20},{16,24},{20,28},{24,8},{28,12},{8,0},{12,4},{1,17},{... | collective-permute-start | bytes 1572872 | tf_op jit(solution)/shard_map/ppermute | solution.py:457
  12.8 17.6 %collective-permute-start.7 = (bf16[1,512,512]{2,1,0:T(8,128)(2,1)}, bf16[1,512,512]{2,1,0:T(8,128)(2,1)S(1)}, u32[]{:S(2)}, u32[]{:S(2)}) collective-permute-start(bf16[1,512,512]{2,1,0:T(8,128)(2,1)} %get-tuple-element.67), channel_id=1, source_target_pairs={{0,4},{4,0},{8,12},{12,8},{16,20},{20,16},{24,28},{28,24},{1,5},{5... | collective-permute-start | bytes 1572872 | tf_op jit(solution)/shard_map/ppermute | solution.py:441
  14.5 17.4 %copy-start.5 = (bf16[512,512]{1,0:T(8,128)(2,1)S(1)}, bf16[512,512]{1,0:T(8,128)(2,1)}, u32[]{:S(2)}) copy-start(bf16[512,512]{1,0:T(8,128)(2,1)} %k_ref.1) | copy-start | bytes 1572868
  15.3 16.6 %copy-start.3 = (bf16[512,512]{1,0:T(8,128)(2,1)S(1)}, bf16[512,512]{1,0:T(8,128)(2,1)}, u32[]{:S(2)}) copy-start(bf16[512,512]{1,0:T(8,128)(2,1)} %q_ref.1) | copy-start | bytes 1572868
  15.3 13.5 %all-to-all-start = ((bf16[4,2,128,128]{3,2,1,0:T(8,128)(2,1)}), bf16[4,2,128,128]{3,2,1,0:T(8,128)(2,1)S(1)}, u32[]{:S(2)}, u32[]{:S(2)}) async-start(bf16[4,2,128,128]{3,2,1,0:T(8,128)(2,1)} %offer.1), calls=%async_computation | async-start | bytes 524288 | tf_op jit(solution)/shard_map/all_to_all | solution.py:473
  20.3 16.2 %collective-permute-start.5 = (bf16[1,512,512]{2,1,0:T(8,128)(2,1)S(1)}, bf16[1,512,512]{2,1,0:T(8,128)(2,1)S(1)}, u32[]{:S(2)}, u32[]{:S(2)}) collective-permute-start(bf16[1,512,512]{2,1,0:T(8,128)(2,1)S(1)} %get-tuple-element.64.refs_0_), channel_id=1, source_target_pairs={{0,2},{1,3},{2,0},{3,1},{4,6},{5,7},{6,4},{7,5},{8,10},{9,11},{10,... | collective-permute-start | bytes 1572872 | tf_op jit(solution)/shard_map/ppermute | solution.py:444
  28.9 7.1 %collective-permute-start.2 = (bf16[2,2,128,128]{3,2,1,0:T(8,128)(2,1)S(1)}, bf16[2,2,128,128]{3,2,1,0:T(8,128)(2,1)S(1)}, u32[]{:S(2)}, u32[]{:S(2)}) collective-permute-start(bf16[2,2,128,128]{3,2,1,0:T(8,128)(2,1)S(1)} %get-tuple-element.54), channel_id=1, source_target_pairs={{0,4},{4,0},{8,12},{12,8},{16,20},{20,16},{24,28},{28,24},{1,5},{5... | collective-permute-start | bytes 393224 | tf_op jit(solution)/shard_map/ppermute | solution.py:441
  29.5 11.8 %collective-permute-start.10 = (bf16[512,512]{1,0:T(8,128)(2,1)}, bf16[512,512]{1,0:T(8,128)(2,1)S(1)}, u32[]{:S(2)}, u32[]{:S(2)}) collective-permute-start(bf16[512,512]{1,0:T(8,128)(2,1)} %collective-permute-done.1.refs_1_), channel_id=1, source_target_pairs={{0,16},{4,20},{16,24},{20,28},{24,8},{28,12},{8,0},{12,4},{1,17},{... | collective-permute-start | bytes 1572872 | tf_op jit(solution)/shard_map/ppermute | solution.py:457
  30.4 13.5 %collective-permute-start.9 = (bf16[1,512,512]{2,1,0:T(8,128)(2,1)S(1)}, bf16[1,512,512]{2,1,0:T(8,128)(2,1)S(1)}, u32[]{:S(2)}, u32[]{:S(2)}) collective-permute-start(bf16[1,512,512]{2,1,0:T(8,128)(2,1)S(1)} %collective-permute-done.7.refs_4_), channel_id=1, source_target_pairs={{0,2},{1,3},{2,0},{3,1},{4,6},{5,7},{6,4},{7,5},{8,10},{9,11},{10,... | collective-permute-start | bytes 1572872 | tf_op jit(solution)/shard_map/ppermute | solution.py:444
  36.5 7.4 %collective-permute-start.6 = (bf16[1,512,512]{2,1,0:T(8,128)(2,1)S(1)}, bf16[1,512,512]{2,1,0:T(8,128)(2,1)S(1)}, u32[]{:S(2)}, u32[]{:S(2)}) collective-permute-start(bf16[1,512,512]{2,1,0:T(8,128)(2,1)S(1)} %collective-permute-done.5.refs_2_), channel_id=1, source_target_pairs={{0,1},{1,0},{2,3},{3,2},{4,5},{5,4},{6,7},{7,6},{8,9},{9,8},{10,11... | collective-permute-start | bytes 1572872 | tf_op jit(solution)/shard_map/ppermute | solution.py:444
  36.6 9.9 %collective-permute-start.8 = (bf16[1,512,512]{2,1,0:T(8,128)(2,1)S(1)}, bf16[1,512,512]{2,1,0:T(8,128)(2,1)}, u32[]{:S(2)}, u32[]{:S(2)}) collective-permute-start(bf16[1,512,512]{2,1,0:T(8,128)(2,1)S(1)} %collective-permute-done.7.refs_4_), channel_id=1, source_target_pairs={{0,1},{1,0},{2,3},{3,2},{4,5},{5,4},{6,7},{7,6},{8,9},{9,8},{10,11... | collective-permute-start | bytes 1572872 | tf_op jit(solution)/shard_map/ppermute | solution.py:444
  37.1 13.9 %collective-permute-start.3 = (bf16[512,512]{1,0:T(8,128)(2,1)S(1)}, bf16[512,512]{1,0:T(8,128)(2,1)S(1)}, u32[]{:S(2)}, u32[]{:S(2)}) collective-permute-start(bf16[512,512]{1,0:T(8,128)(2,1)S(1)} %finish_value.1.a_ref.x_ref), channel_id=1, source_target_pairs={{0,4},{4,0},{8,12},{12,8},{16,20},{20,16},{24,28},{28,24},{1,5},{5... | collective-permute-start | bytes 1572872 | tf_op jit(solution)/shard_map/ppermute | solution.py:441
  41.3 5.1 %collective-permute-start.4 = (bf16[1,512,512]{2,1,0:T(8,128)(2,1)S(1)}, bf16[1,512,512]{2,1,0:T(8,128)(2,1)}, u32[]{:S(2)}, u32[]{:S(2)}) collective-permute-start(bf16[1,512,512]{2,1,0:T(8,128)(2,1)S(1)} %get-tuple-element.64.refs_0_), channel_id=1, source_target_pairs={{0,1},{1,0},{2,3},{3,2},{4,5},{5,4},{6,7},{7,6},{8,9},{9,8},{10,11... | collective-permute-start | bytes 1572872 | tf_op jit(solution)/shard_map/ppermute | solution.py:444
  43.9 7.1 %collective-permute-start.11 = (bf16[1,512,512]{2,1,0:T(8,128)(2,1)S(1)}, bf16[1,512,512]{2,1,0:T(8,128)(2,1)}, u32[]{:S(2)}, u32[]{:S(2)}) collective-permute-start(bf16[1,512,512]{2,1,0:T(8,128)(2,1)S(1)} %collective-permute-done.9.refs_6_), channel_id=1, source_target_pairs={{0,1},{1,0},{2,3},{3,2},{4,5},{5,4},{6,7},{7,6},{8,9},{9,8},{10,11... | collective-permute-start | bytes 1572872 | tf_op jit(solution)/shard_map/ppermute | solution.py:444
  44.7 15.5 %collective-permute-start.13 = (bf16[512,512]{1,0:T(8,128)(2,1)}, bf16[512,512]{1,0:T(8,128)(2,1)}, u32[]{:S(2)}, u32[]{:S(2)}) collective-permute-start(bf16[512,512]{1,0:T(8,128)(2,1)} %refs_0_.3), channel_id=1, source_target_pairs={{16,0},{20,4},{24,16},{28,20},{8,24},{12,28},{0,8},{4,12},{17,1},{... | collective-permute-start | bytes 1572872 | tf_op jit(solution)/shard_map/ppermute | solution.py:460
  60.2 2.1 %collective-permute-start.14 = (bf16[512,512]{1,0:T(8,128)(2,1)}, bf16[512,512]{1,0:T(8,128)(2,1)S(1)}, u32[]{:S(2)}, u32[]{:S(2)}) collective-permute-start(bf16[512,512]{1,0:T(8,128)(2,1)} %collective-permute-done.13.refs_3_), channel_id=1, source_target_pairs={{0,1},{1,0},{2,3},{3,2},{4,5},{5,4},{6,7},{7,6},{8,9},{9,8},{10,11... | collective-permute-start | bytes 1572872 | tf_op jit(solution)/shard_map/ppermute | solution.py:444
  60.2 6.9 %collective-permute-start.16 = (bf16[512,512]{1,0:T(8,128)(2,1)}, bf16[512,512]{1,0:T(8,128)(2,1)S(1)}, u32[]{:S(2)}, u32[]{:S(2)}) collective-permute-start(bf16[512,512]{1,0:T(8,128)(2,1)} %refs_0_.3), channel_id=1, source_target_pairs={{0,1},{1,0},{2,3},{3,2},{4,5},{5,4},{6,7},{7,6},{8,9},{9,8},{10,11... | collective-permute-start | bytes 1572872 | tf_op jit(solution)/shard_map/ppermute | solution.py:444
  60.7 4.6 %collective-permute-start.17 = (bf16[512,512]{1,0:T(8,128)(2,1)}, bf16[512,512]{1,0:T(8,128)(2,1)S(1)}, u32[]{:S(2)}, u32[]{:S(2)}) collective-permute-start(bf16[512,512]{1,0:T(8,128)(2,1)} %collective-permute-done.1.refs_1_), channel_id=1, source_target_pairs={{0,1},{1,0},{2,3},{3,2},{4,5},{5,4},{6,7},{7,6},{8,9},{9,8},{10,11... | collective-permute-start | bytes 1572872 | tf_op jit(solution)/shard_map/ppermute | solution.py:444
  60.8 6.4 %collective-permute-start.18 = (bf16[512,512]{1,0:T(8,128)(2,1)S(1)}, bf16[512,512]{1,0:T(8,128)(2,1)S(1)}, u32[]{:S(2)}, u32[]{:S(2)}) collective-permute-start(bf16[512,512]{1,0:T(8,128)(2,1)S(1)} %copy-done.14), channel_id=1, source_target_pairs={{0,1},{1,0},{2,3},{3,2},{4,5},{5,4},{6,7},{7,6},{8,9},{9,8},{10,11... | collective-permute-start | bytes 1572872 | tf_op jit(solution)/shard_map/ppermute | solution.py:444
  61.3 7.1 %collective-permute-start.15 = (bf16[512,512]{1,0:T(8,128)(2,1)S(1)}, bf16[512,512]{1,0:T(8,128)(2,1)S(1)}, u32[]{:S(2)}, u32[]{:S(2)}) collective-permute-start(bf16[512,512]{1,0:T(8,128)(2,1)S(1)} %collective-permute-done.3.b_ref.x_ref), channel_id=1, source_target_pairs={{0,1},{1,0},{2,3},{3,2},{4,5},{5,4},{6,7},{7,6},{8,9},{9,8},{10,11... | collective-permute-start | bytes 1572872 | tf_op jit(solution)/shard_map/ppermute | solution.py:444
  62.4 10.8 %collective-permute-start.19 = (bf16[512,512]{1,0:T(8,128)(2,1)S(1)}, bf16[512,512]{1,0:T(8,128)(2,1)S(1)}, u32[]{:S(2)}, u32[]{:S(2)}) collective-permute-start(bf16[512,512]{1,0:T(8,128)(2,1)S(1)} %finish_value.1.a_ref.x_ref), channel_id=1, source_target_pairs={{0,1},{1,0},{2,3},{3,2},{4,5},{5,4},{6,7},{7,6},{8,9},{9,8},{10,11... | collective-permute-start | bytes 1572872 | tf_op jit(solution)/shard_map/ppermute | solution.py:444
  65.4 9.1 %collective-permute-start.12 = (bf16[256,512]{1,0:T(8,128)(2,1)S(1)}, bf16[256,512]{1,0:T(8,128)(2,1)S(1)}, u32[]{:S(2)}, u32[]{:S(2)}) collective-permute-start(bf16[256,512]{1,0:T(8,128)(2,1)S(1)} %get-tuple-element.71), channel_id=1, source_target_pairs={{0,16},{4,20},{16,24},{20,28},{24,8},{28,12},{8,0},{12,4},{1,17},{... | collective-permute-start | bytes 786440 | tf_op jit(solution)/shard_map/ppermute | solution.py:457
  69.2 17.6 %collective-permute-start.24 = (bf16[512,512]{1,0:T(8,128)(2,1)S(1)}, bf16[512,512]{1,0:T(8,128)(2,1)S(1)}, u32[]{:S(2)}, u32[]{:S(2)}) collective-permute-start(bf16[512,512]{1,0:T(8,128)(2,1)S(1)} %head_part.3), channel_id=1, source_target_pairs={{0,2},{1,3},{2,0},{3,1},{4,6},{5,7},{6,4},{7,5},{8,10},{9,11},{10,... | collective-permute-start | bytes 1572872 | tf_op jit(solution)/shard_map/ppermute | solution.py:444
  70.8 9.4 %collective-permute-start.21 = (bf16[256,512]{1,0:T(8,128)(2,1)S(1)}, bf16[256,512]{1,0:T(8,128)(2,1)S(1)}, u32[]{:S(2)}, u32[]{:S(2)}) collective-permute-start(bf16[256,512]{1,0:T(8,128)(2,1)S(1)} %get-tuple-element.83), channel_id=1, source_target_pairs={{0,16},{4,20},{16,24},{20,28},{24,8},{28,12},{8,0},{12,4},{1,17},{... | collective-permute-start | bytes 786440 | tf_op jit(solution)/shard_map/ppermute | solution.py:457
  74.6 12.1 %collective-permute-start.20 = (bf16[256,512]{1,0:T(8,128)(2,1)S(1)}, bf16[256,512]{1,0:T(8,128)(2,1)S(1)}, u32[]{:S(2)}, u32[]{:S(2)}) collective-permute-start(bf16[256,512]{1,0:T(8,128)(2,1)S(1)} %add_own.4), channel_id=1, source_target_pairs={{0,16},{4,20},{16,24},{20,28},{24,8},{28,12},{8,0},{12,4},{1,17},{... | collective-permute-start | bytes 786440 | tf_op jit(solution)/shard_map/ppermute | solution.py:457
  80.2 11.0 %collective-permute-start.23 = (bf16[256,512]{1,0:T(8,128)(2,1)S(1)}, bf16[256,512]{1,0:T(8,128)(2,1)S(1)}, u32[]{:S(2)}, u32[]{:S(2)}) collective-permute-start(bf16[256,512]{1,0:T(8,128)(2,1)S(1)} %add_own.5), channel_id=1, source_target_pairs={{0,16},{4,20},{16,24},{20,28},{24,8},{28,12},{8,0},{12,4},{1,17},{... | collective-permute-start | bytes 786440 | tf_op jit(solution)/shard_map/ppermute | solution.py:457
  83.4 19.8 %collective-permute-start.26 = (bf16[512,512]{1,0:T(8,128)(2,1)S(1)}, bf16[512,512]{1,0:T(8,128)(2,1)S(1)}, u32[]{:S(2)}, u32[]{:S(2)}) collective-permute-start(bf16[512,512]{1,0:T(8,128)(2,1)S(1)} %head_part.4), channel_id=1, source_target_pairs={{0,2},{1,3},{2,0},{3,1},{4,6},{5,7},{6,4},{7,5},{8,10},{9,11},{10,... | collective-permute-start | bytes 1572872 | tf_op jit(solution)/shard_map/ppermute | solution.py:444
  87.6 15.6 %collective-permute-start.27 = (bf16[512,512]{1,0:T(8,128)(2,1)S(1)}, bf16[512,512]{1,0:T(8,128)(2,1)S(1)}, u32[]{:S(2)}, u32[]{:S(2)}) collective-permute-start(bf16[512,512]{1,0:T(8,128)(2,1)S(1)} %head_part.5), channel_id=1, source_target_pairs={{0,4},{4,0},{8,12},{12,8},{16,20},{20,16},{24,28},{28,24},{1,5},{5... | collective-permute-start | bytes 1572872 | tf_op jit(solution)/shard_map/ppermute | solution.py:441
  88.2 10.6 %collective-permute-start.22 = (bf16[256,512]{1,0:T(8,128)(2,1)S(1)}, bf16[256,512]{1,0:T(8,128)(2,1)S(1)}, u32[]{:S(2)}, u32[]{:S(2)}) collective-permute-start(bf16[256,512]{1,0:T(8,128)(2,1)S(1)} %add_own.6), channel_id=1, source_target_pairs={{0,16},{4,20},{16,24},{20,28},{24,8},{28,12},{8,0},{12,4},{1,17},{... | collective-permute-start | bytes 786440 | tf_op jit(solution)/shard_map/ppermute | solution.py:457
  91.2 10.6 %collective-permute-start.25 = (bf16[256,512]{1,0:T(8,128)(2,1)S(1)}, bf16[256,512]{1,0:T(8,128)(2,1)S(1)}, u32[]{:S(2)}, u32[]{:S(2)}) collective-permute-start(bf16[256,512]{1,0:T(8,128)(2,1)S(1)} %add_own.7), channel_id=1, source_target_pairs={{0,16},{4,20},{16,24},{20,28},{24,8},{28,12},{8,0},{12,4},{1,17},{... | collective-permute-start | bytes 786440 | tf_op jit(solution)/shard_map/ppermute | solution.py:457
  (13 other events, 70.7 us)
